TPU v7x, 32 devices: a whole 2x2x4 slice. The times are simulated.
32 devices in a mesh: grp: 2 (over y), row: 4 (over z), inner: 4 (over x, core).
Axes of the slice: x: 2, y: 2, z: 4, core: 2. Of those that a mesh axis runs over, the one named last changes fastest.
Arguments:
- density: bfloat16 [128, 8, 128, 128], P(('grp', 'row', 'inner')), parts along dimension 0
- inverse_start: bfloat16 [128, 8, 128, 128], P(('grp', 'row', 'inner')), parts along dimension 0
- block_cols: int32 [128, 8], P(('grp', 'row', 'inner')), parts along dimension 0, may hold values from 0 to 63, as said below
Outputs:
- density_next: bfloat16 [128, 8, 128, 128], P(('grp', 'row', 'inner')), parts along dimension 0
- inverse_next: bfloat16 [128, 8, 128, 128], P(('grp', 'row', 'inner')), parts along dimension 0
There are 2 independent parts, one for each index of `grp`. A program takes and returns all parts, laid end to end along the dimension named above; each array names one. Nothing has to cross between parts.
Inputs may be any that keep to these rules, and one draw needn't show every extreme that they name: `block_cols`: row i holds 8 distinct block-columns (i + d) mod 64 with d from -4 to 4, in increasing d; d = 0 is always among them.
All inputs are finite; a program needn't handle non-finite values.
Results may differ from a plain program's by a relative error of at most 0.0071.
Values may be sent and summed in bfloat16 or wider, within the bound.
No kernel may reach another device: no remote copies, remote signals or barrier semaphores. Data moves between devices by JAX's collectives and lax.ppermute only.
A program may use at most 64 MiB of HBM per device.

v0:
```python
import jax
import jax.numpy as jnp
from jax import lax
from jax.sharding import PartitionSpec as P

SWEEPS = 2


def shifted_2(x, axis, by):
    size = lax.axis_size(axis)
    return lax.ppermute(x, axis, [(i, (i + by) % size) for i in range(size)])


def rim_rows(blocks):
    below = shifted_2(blocks, ("row", "inner"), 1)
    above = shifted_2(blocks, ("row", "inner"), -1)
    return jnp.concatenate([below, blocks, above], axis=0)


def pattern_rows(columns):
    below_parts = []
    below_parts.insert(0, shifted_2(columns, ("row", "inner"), 1))
    above_parts = [shifted_2(columns, ("row", "inner"), -1)]
    return jnp.concatenate(below_parts + [columns] + above_parts, axis=0)


def missing_slot(columns, start_row, total_rows):
    row_count = columns.shape[0]
    per_row = columns.shape[1]
    row_ids = start_row + jnp.arange(row_count, dtype=jnp.int32)
    positions = jnp.mod(columns - row_ids[:, None] + per_row // 2, total_rows)
    return per_row * (per_row + 1) // 2 - jnp.sum(positions, axis=1)


def to_band(blocks, dropped):
    zero_slot = jnp.zeros_like(blocks[:, :1])
    left_copy = jnp.concatenate([blocks, zero_slot], axis=1)
    right_copy = jnp.concatenate([zero_slot, blocks], axis=1)
    slot_index = jnp.arange(blocks.shape[1] + 1, dtype=jnp.int32)[None, :]
    take_left = (slot_index < dropped[:, None])[:, :, None, None]
    take_right = (slot_index > dropped[:, None])[:, :, None, None]
    empty = jnp.zeros((), blocks.dtype)
    return jnp.where(take_left, left_copy, jnp.where(take_right, right_copy, empty))


def from_band(band_blocks, dropped):
    per_row = band_blocks.shape[1] - 1
    slot_index = jnp.arange(per_row, dtype=jnp.int32)[None, :]
    keep_low = (slot_index < dropped[:, None])[:, :, None, None]
    return jnp.where(keep_low, band_blocks[:, :per_row], band_blocks[:, 1:])


def band_product(left_band, left_dropped, right_band):
    row_count = left_band.shape[0]
    width = left_band.shape[1]
    half_band = (width - 1) // 2
    padded = jnp.pad(right_band, ((0, 0), (half_band, half_band), (0, 0), (0, 0)))
    total = jnp.zeros(left_band.shape, jnp.float32)
    for slot_left in range(width):
        offset = slot_left - half_band
        aligned = padded[
            slot_left : slot_left + row_count, half_band - offset : half_band - offset + width
        ]
        total = total + jnp.einsum(
            "rab,rqbc->rqac", left_band[:, slot_left], aligned, preferred_element_type=jnp.float32
        )
    return from_band(total, left_dropped)


def on_device(density, inverse_start, block_cols):
    row_count = density.shape[0]
    per_row = density.shape[1]
    block_order = density.shape[2]
    half_band = per_row // 2
    total_rows = row_count * lax.axis_size(("row", "inner"))
    first_row = lax.axis_index(("row", "inner")) * row_count
    own_ids = first_row + jnp.arange(row_count, dtype=jnp.int32)
    unit_block = jnp.eye(block_order, dtype=jnp.float32)
    diagonal = (block_cols == own_ids[:, None]).astype(jnp.float32)[:, :, None, None] * unit_block
    near_cols = pattern_rows(block_cols)
    rim_start = first_row - half_band
    own_gap = missing_slot(block_cols, first_row, total_rows)
    rim_gap = missing_slot(near_cols, rim_start, total_rows)
    square_sum = band_product(
        to_band(density, own_gap), own_gap, to_band(rim_rows(density), rim_gap)
    )
    square = square_sum.astype(jnp.bfloat16)
    shifted = (2.0 * square_sum - 2.0 * density.astype(jnp.float32) + diagonal).astype(jnp.bfloat16)
    inverse = inverse_start
    shifted_band = to_band(shifted, own_gap)
    for sweep_index in range(SWEEPS):
        correction = band_product(
            shifted_band, own_gap, to_band(rim_rows(inverse), rim_gap)
        ).astype(jnp.bfloat16)
        update = band_product(
            to_band(inverse, own_gap), own_gap, to_band(rim_rows(correction), rim_gap)
        )
        inverse = (2.0 * inverse.astype(jnp.float32) - update).astype(jnp.bfloat16)
    density_next = band_product(
        to_band(square, own_gap), own_gap, to_band(rim_rows(inverse), rim_gap)
    ).astype(jnp.bfloat16)
    return (density_next, inverse)


def solution(mesh):
    in_specs = (
        P(("grp", "row", "inner"), None, None, None),
        P(("grp", "row", "inner"), None, None, None),
        P(("grp", "row", "inner"), None),
    )
    out_specs = (
        P(("grp", "row", "inner"), None, None, None),
        P(("grp", "row", "inner"), None, None, None),
    )
    return jax.shard_map(
        on_device, mesh=mesh, in_specs=in_specs, out_specs=out_specs, check_vma=False
    )
```

profile of v0, /device:TPU:1, one launch (start us, length us, event | category | flops | bytes accessed | tf_op | source)
XLA Modules:
  0.0 194.8 jit_solution(862185762813969399)
XLA Ops:
  0.6 2.7 %collective-permute-start = (s32[4,8]{1,0:T(4,128)}, s32[4,8]{1,0:T(4,128)S(1)}, u32[]{:S(2)}, u32[]{:S(2)}) collective-permute-start(s32[4,8]{1,0:T(4,128)} %param.5), channel_id=1, source_target_pairs={{0,1},{1,2},{2,3},{3,4},{4,5},{5,6},{6,7},{7,8},{8,9},{9,10},{10,1... | collective-permute-start | bytes 392 | tf_op jit(solution)/shard_map/ppermute | solution.py:11
  3.3 2.3 %copy.5 = bf16[4,8,128,128]{3,2,0,1:T(8,128)(2,1)} copy(bf16[4,8,128,128]{3,2,1,0:T(8,128)(2,1)} %param.4) | data formatting | bytes 2097152 | tf_op args[1]
  5.6 1.7 collective-permute-start.2
  11.0 3.9 %collective-permute-start.5 = (bf16[4,8,128,128]{3,2,0,1:T(8,128)(2,1)}, bf16[4,8,128,128]{3,2,0,1:T(8,128)(2,1)S(1)}, u32[]{:S(2)}, u32[]{:S(2)}) collective-permute-start(bf16[4,8,128,128]{3,2,0,1:T(8,128)(2,1)} %copy.9), channel_id=1, source_target_pairs={{0,15},{1,0},{2,1},{3,2},{4,3},{5,4},{6,5},{7,6},{8,7},{9,8},{10,9... | collective-permute-start | bytes 3145736 | tf_op jit(solution)/shard_map/ppermute | solution.py:11
  15.1 26.8 %collective-permute-done.2 = bf16[4,8,128,128]{3,2,0,1:T(8,128)(2,1)} collective-permute-done((bf16[4,8,128,128]{3,2,0,1:T(8,128)(2,1)}, bf16[4,8,128,128]{3,2,0,1:T(8,128)(2,1)}, u32[]{:S(2)}, u32[]{:S(2)}) %collective-permute-start.2) | collective-permute-done | bytes 1048608 | tf_op jit(solution)/shard_map/ppermute | solution.py:11
  41.9 1.3 constant_dynamic-update-slice_fusion.5
  43.2 9.9 %collective-permute-done.4 = bf16[4,8,128,128]{3,2,0,1:T(8,128)(2,1)} collective-permute-done((bf16[4,8,128,128]{3,2,0,1:T(8,128)(2,1)}, bf16[4,8,128,128]{3,2,0,1:T(8,128)(2,1)}, u32[]{:S(2)}, u32[]{:S(2)}) %collective-permute-start.4) | collective-permute-done | bytes 1048608 | tf_op jit(solution)/shard_map/ppermute | solution.py:11
  53.1 1.3 constant_dynamic-update-slice_fusion.2
  54.6 1.4 constant_dynamic-update-slice_fusion.3
  60.9 1.4 add_bitcast_fusion.5
  63.1 1.6 select_select_fusion.6
  68.2 1.2 add_bitcast_fusion.4
  69.5 2.5 %collective-permute-start.6 = (bf16[4,8,128,128]{3,2,0,1:T(8,128)(2,1)S(1)}, bf16[4,8,128,128]{3,2,0,1:T(8,128)(2,1)S(1)}, u32[]{:S(2)}, u32[]{:S(2)}) collective-permute-start(bf16[4,8,128,128]{3,2,0,1:T(8,128)(2,1)S(1)} %fusion.6), channel_id=1, source_target_pairs={{0,1},{1,2},{2,3},{3,4},{4,5},{5,6},{6,7},{7,8},{8,9},{9,10},{10,1... | collective-permute-start | bytes 3145736 | tf_op jit(solution)/shard_map/ppermute | solution.py:11
  72.1 23.0 %collective-permute-done.6 = bf16[4,8,128,128]{3,2,0,1:T(8,128)(2,1)S(1)} collective-permute-done((bf16[4,8,128,128]{3,2,0,1:T(8,128)(2,1)S(1)}, bf16[4,8,128,128]{3,2,0,1:T(8,128)(2,1)S(1)}, u32[]{:S(2)}, u32[]{:S(2)}) %collective-permute-start.6) | collective-permute-done | bytes 1048608 | tf_op jit(solution)/shard_map/ppermute | solution.py:11
  99.5 1.3 add_bitcast_fusion.3
  101.3 2.5 %collective-permute-start.8 = (bf16[4,8,128,128]{3,2,0,1:T(8,128)(2,1)S(1)}, bf16[4,8,128,128]{3,2,0,1:T(8,128)(2,1)S(1)}, u32[]{:S(2)}, u32[]{:S(2)}) collective-permute-start(bf16[4,8,128,128]{3,2,0,1:T(8,128)(2,1)S(1)} %fusion.5), channel_id=1, source_target_pairs={{0,1},{1,2},{2,3},{3,4},{4,5},{5,6},{6,7},{7,8},{8,9},{9,10},{10,1... | collective-permute-start | bytes 3145736 | tf_op jit(solution)/shard_map/ppermute | solution.py:11
  103.9 23.0 %collective-permute-done.8 = bf16[4,8,128,128]{3,2,0,1:T(8,128)(2,1)S(1)} collective-permute-done((bf16[4,8,128,128]{3,2,0,1:T(8,128)(2,1)S(1)}, bf16[4,8,128,128]{3,2,0,1:T(8,128)(2,1)S(1)}, u32[]{:S(2)}, u32[]{:S(2)}) %collective-permute-start.8) | collective-permute-done | bytes 1048608 | tf_op jit(solution)/shard_map/ppermute | solution.py:11
  131.3 1.2 add_bitcast_fusion.2
  132.6 2.5 %collective-permute-start.10 = (bf16[4,8,128,128]{3,2,0,1:T(8,128)(2,1)S(1)}, bf16[4,8,128,128]{3,2,0,1:T(8,128)(2,1)S(1)}, u32[]{:S(2)}, u32[]{:S(2)}) collective-permute-start(bf16[4,8,128,128]{3,2,0,1:T(8,128)(2,1)S(1)} %fusion.3), channel_id=1, source_target_pairs={{0,1},{1,2},{2,3},{3,4},{4,5},{5,6},{6,7},{7,8},{8,9},{9,10},{10,1... | collective-permute-start | bytes 3145736 | tf_op jit(solution)/shard_map/ppermute | solution.py:11
  135.4 22.8 %collective-permute-done.10 = bf16[4,8,128,128]{3,2,0,1:T(8,128)(2,1)S(1)} collective-permute-done((bf16[4,8,128,128]{3,2,0,1:T(8,128)(2,1)S(1)}, bf16[4,8,128,128]{3,2,0,1:T(8,128)(2,1)S(1)}, u32[]{:S(2)}, u32[]{:S(2)}) %collective-permute-start.10) | collective-permute-done | bytes 1048608 | tf_op jit(solution)/shard_map/ppermute | solution.py:11
  162.6 1.3 add_bitcast_fusion.1
  164.4 2.5 %collective-permute-start.12 = (bf16[4,8,128,128]{3,2,0,1:T(8,128)(2,1)S(1)}, bf16[4,8,128,128]{3,2,0,1:T(8,128)(2,1)S(1)}, u32[]{:S(2)}, u32[]{:S(2)}) collective-permute-start(bf16[4,8,128,128]{3,2,0,1:T(8,128)(2,1)S(1)} %fusion.2), channel_id=1, source_target_pairs={{0,1},{1,2},{2,3},{3,4},{4,5},{5,6},{6,7},{7,8},{8,9},{9,10},{10,1... | collective-permute-start | bytes 3145736 | tf_op jit(solution)/shard_map/ppermute | solution.py:11
  168.0 20.0 %collective-permute-done.12 = bf16[4,8,128,128]{3,2,0,1:T(8,128)(2,1)S(1)} collective-permute-done((bf16[4,8,128,128]{3,2,0,1:T(8,128)(2,1)S(1)}, bf16[4,8,128,128]{3,2,0,1:T(8,128)(2,1)S(1)}, u32[]{:S(2)}, u32[]{:S(2)}) %collective-permute-start.12) | collective-permute-done | bytes 1048608 | tf_op jit(solution)/shard_map/ppermute | solution.py:11
  192.4 1.2 add_bitcast_fusion
  (105 shorter events, 34.2 us)
Async XLA Ops:
  0.6 9.5 %copy-start.2 = (s32[4,8]{1,0:T(4,128)S(1)}, s32[4,8]{1,0:T(4,128)}, u32[]{:S(2)}) copy-start(s32[4,8]{1,0:T(4,128)} %param.5) | copy-start | bytes 388
  0.6 7.9 %copy-start = (bf16[4,8,128,128]{3,2,1,0:T(8,128)(2,1)S(1)}, bf16[4,8,128,128]{3,2,1,0:T(8,128)(2,1)}, u32[]{:S(2)}) copy-start(bf16[4,8,128,128]{3,2,1,0:T(8,128)(2,1)} %param.3) | copy-start | bytes 3145732
  0.6 10.4 %collective-permute-start = (s32[4,8]{1,0:T(4,128)}, s32[4,8]{1,0:T(4,128)S(1)}, u32[]{:S(2)}, u32[]{:S(2)}) collective-permute-start(s32[4,8]{1,0:T(4,128)} %param.5), channel_id=1, source_target_pairs={{0,1},{1,2},{2,3},{3,4},{4,5},{5,6},{6,7},{7,8},{8,9},{9,10},{10,1... | collective-permute-start | bytes 392 | tf_op jit(solution)/shard_map/ppermute | solution.py:11
  3.3 11.6 %collective-permute-start.1 = (s32[4,8]{1,0:T(4,128)}, s32[4,8]{1,0:T(4,128)S(1)}, u32[]{:S(2)}, u32[]{:S(2)}) collective-permute-start(s32[4,8]{1,0:T(4,128)} %param.5), channel_id=1, source_target_pairs={{0,15},{1,0},{2,1},{3,2},{4,3},{5,4},{6,5},{7,6},{8,7},{9,8},{10,9... | collective-permute-start | bytes 392 | tf_op jit(solution)/shard_map/ppermute | solution.py:11
  5.6 36.3 %collective-permute-start.2 = (bf16[4,8,128,128]{3,2,0,1:T(8,128)(2,1)}, bf16[4,8,128,128]{3,2,0,1:T(8,128)(2,1)}, u32[]{:S(2)}, u32[]{:S(2)}) collective-permute-start(bf16[4,8,128,128]{3,2,0,1:T(8,128)(2,1)} %copy.5), channel_id=1, source_target_pairs={{0,1},{1,2},{2,3},{3,4},{4,5},{5,6},{6,7},{7,8},{8,9},{9,10},{10,1... | collective-permute-start | bytes 3145736 | tf_op jit(solution)/shard_map/ppermute | solution.py:11
  7.4 47.2 %collective-permute-start.3 = (bf16[4,8,128,128]{3,2,0,1:T(8,128)(2,1)}, bf16[4,8,128,128]{3,2,0,1:T(8,128)(2,1)}, u32[]{:S(2)}, u32[]{:S(2)}) collective-permute-start(bf16[4,8,128,128]{3,2,0,1:T(8,128)(2,1)} %copy.5), channel_id=1, source_target_pairs={{0,15},{1,0},{2,1},{3,2},{4,3},{5,4},{6,5},{7,6},{8,7},{9,8},{10,9... | collective-permute-start | bytes 3145736 | tf_op jit(solution)/shard_map/ppermute | solution.py:11
  9.6 43.5 %collective-permute-start.4 = (bf16[4,8,128,128]{3,2,0,1:T(8,128)(2,1)}, bf16[4,8,128,128]{3,2,0,1:T(8,128)(2,1)}, u32[]{:S(2)}, u32[]{:S(2)}) collective-permute-start(bf16[4,8,128,128]{3,2,0,1:T(8,128)(2,1)} %copy.9), channel_id=1, source_target_pairs={{0,1},{1,2},{2,3},{3,4},{4,5},{5,6},{6,7},{7,8},{8,9},{9,10},{10,1... | collective-permute-start | bytes 3145736 | tf_op jit(solution)/shard_map/ppermute | solution.py:11
  10.8 43.6 %copy-start.1 = (bf16[4,8,128,128]{3,2,1,0:T(8,128)(2,1)S(1)}, bf16[4,8,128,128]{3,2,1,0:T(8,128)(2,1)}, u32[]{:S(2)}) copy-start(bf16[4,8,128,128]{3,2,1,0:T(8,128)(2,1)} %param.4) | copy-start | bytes 3145732
  11.0 45.1 %collective-permute-start.5 = (bf16[4,8,128,128]{3,2,0,1:T(8,128)(2,1)}, bf16[4,8,128,128]{3,2,0,1:T(8,128)(2,1)S(1)}, u32[]{:S(2)}, u32[]{:S(2)}) collective-permute-start(bf16[4,8,128,128]{3,2,0,1:T(8,128)(2,1)} %copy.9), channel_id=1, source_target_pairs={{0,15},{1,0},{2,1},{3,2},{4,3},{5,4},{6,5},{7,6},{8,7},{9,8},{10,9... | collective-permute-start | bytes 3145736 | tf_op jit(solution)/shard_map/ppermute | solution.py:11
  69.5 25.5 %collective-permute-start.6 = (bf16[4,8,128,128]{3,2,0,1:T(8,128)(2,1)S(1)}, bf16[4,8,128,128]{3,2,0,1:T(8,128)(2,1)S(1)}, u32[]{:S(2)}, u32[]{:S(2)}) collective-permute-start(bf16[4,8,128,128]{3,2,0,1:T(8,128)(2,1)S(1)} %fusion.6), channel_id=1, source_target_pairs={{0,1},{1,2},{2,3},{3,4},{4,5},{5,6},{6,7},{7,8},{8,9},{9,10},{10,1... | collective-permute-start | bytes 3145736 | tf_op jit(solution)/shard_map/ppermute | solution.py:11
  72.1 23.0 %collective-permute-start.7 = (bf16[4,8,128,128]{3,2,0,1:T(8,128)(2,1)S(1)}, bf16[4,8,128,128]{3,2,0,1:T(8,128)(2,1)S(1)}, u32[]{:S(2)}, u32[]{:S(2)}) collective-permute-start(bf16[4,8,128,128]{3,2,0,1:T(8,128)(2,1)S(1)} %fusion.6), channel_id=1, source_target_pairs={{0,15},{1,0},{2,1},{3,2},{4,3},{5,4},{6,5},{7,6},{8,7},{9,8},{10,9... | collective-permute-start | bytes 3145736 | tf_op jit(solution)/shard_map/ppermute | solution.py:11
  101.3 25.5 %collective-permute-start.8 = (bf16[4,8,128,128]{3,2,0,1:T(8,128)(2,1)S(1)}, bf16[4,8,128,128]{3,2,0,1:T(8,128)(2,1)S(1)}, u32[]{:S(2)}, u32[]{:S(2)}) collective-permute-start(bf16[4,8,128,128]{3,2,0,1:T(8,128)(2,1)S(1)} %fusion.5), channel_id=1, source_target_pairs={{0,1},{1,2},{2,3},{3,4},{4,5},{5,6},{6,7},{7,8},{8,9},{9,10},{10,1... | collective-permute-start | bytes 3145736 | tf_op jit(solution)/shard_map/ppermute | solution.py:11
  103.9 23.0 %collective-permute-start.9 = (bf16[4,8,128,128]{3,2,0,1:T(8,128)(2,1)S(1)}, bf16[4,8,128,128]{3,2,0,1:T(8,128)(2,1)S(1)}, u32[]{:S(2)}, u32[]{:S(2)}) collective-permute-start(bf16[4,8,128,128]{3,2,0,1:T(8,128)(2,1)S(1)} %fusion.5), channel_id=1, source_target_pairs={{0,15},{1,0},{2,1},{3,2},{4,3},{5,4},{6,5},{7,6},{8,7},{9,8},{10,9... | collective-permute-start | bytes 3145736 | tf_op jit(solution)/shard_map/ppermute | solution.py:11
  132.6 25.5 %collective-permute-start.10 = (bf16[4,8,128,128]{3,2,0,1:T(8,128)(2,1)S(1)}, bf16[4,8,128,128]{3,2,0,1:T(8,128)(2,1)S(1)}, u32[]{:S(2)}, u32[]{:S(2)}) collective-permute-start(bf16[4,8,128,128]{3,2,0,1:T(8,128)(2,1)S(1)} %fusion.3), channel_id=1, source_target_pairs={{0,1},{1,2},{2,3},{3,4},{4,5},{5,6},{6,7},{7,8},{8,9},{9,10},{10,1... | collective-permute-start | bytes 3145736 | tf_op jit(solution)/shard_map/ppermute | solution.py:11
  135.2 23.0 %collective-permute-start.11 = (bf16[4,8,128,128]{3,2,0,1:T(8,128)(2,1)S(1)}, bf16[4,8,128,128]{3,2,0,1:T(8,128)(2,1)S(1)}, u32[]{:S(2)}, u32[]{:S(2)}) collective-permute-start(bf16[4,8,128,128]{3,2,0,1:T(8,128)(2,1)S(1)} %fusion.3), channel_id=1, source_target_pairs={{0,15},{1,0},{2,1},{3,2},{4,3},{5,4},{6,5},{7,6},{8,7},{9,8},{10,9... | collective-permute-start | bytes 3145736 | tf_op jit(solution)/shard_map/ppermute | solution.py:11
  164.4 23.6 %collective-permute-start.12 = (bf16[4,8,128,128]{3,2,0,1:T(8,128)(2,1)S(1)}, bf16[4,8,128,128]{3,2,0,1:T(8,128)(2,1)S(1)}, u32[]{:S(2)}, u32[]{:S(2)}) collective-permute-start(bf16[4,8,128,128]{3,2,0,1:T(8,128)(2,1)S(1)} %fusion.2), channel_id=1, source_target_pairs={{0,1},{1,2},{2,3},{3,4},{4,5},{5,6},{6,7},{7,8},{8,9},{9,10},{10,1... | collective-permute-start | bytes 3145736 | tf_op jit(solution)/shard_map/ppermute | solution.py:11
  166.9 21.1 %collective-permute-start.13 = (bf16[4,8,128,128]{3,2,0,1:T(8,128)(2,1)S(1)}, bf16[4,8,128,128]{3,2,0,1:T(8,128)(2,1)S(1)}, u32[]{:S(2)}, u32[]{:S(2)}) collective-permute-start(bf16[4,8,128,128]{3,2,0,1:T(8,128)(2,1)S(1)} %fusion.2), channel_id=1, source_target_pairs={{0,15},{1,0},{2,1},{3,2},{4,3},{5,4},{6,5},{7,6},{8,7},{9,8},{10,9... | collective-permute-start | bytes 3145736 | tf_op jit(solution)/shard_map/ppermute | solution.py:11
where the time goes:
time: 196 us; the launch traced here: 195 us
  waiting for transfers between devices  125 us (64%)
  matrix products  28.2 us (14%)
  starting transfers between devices  20.2 us (10%)
  other arithmetic  9.96 us (5%)
  local copies, waits for them, and re-layouts  9.93 us (5%)
    ppermute x14, waiting for transfers between devices, shifted_2(): return lax.ppermute(x, axis, [(i, (i + by) % size) for i in range(size)])  125 us
    dot_general x54, matrix products, band_product(): jnp.einsum('rab,rqbc->rqac', left_band[:, slot_left], aligned, preferred_...  28.2 us
    ppermute x14, starting transfers between devices, shifted_2(): return lax.ppermute(x, axis, [(i, (i + by) % size) for i in range(size)])  20.2 us
    unnamed x14, local copies, waits for them, and re-layouts  8.31 us
    select_n x8, other arithmetic, to_band(): jnp.where(take_left, left_copy, jnp.where(take_right, right_copy, empty))  5.84 us
  transfers between devices with their start and end apart: 14, of which 6 were waited for; matrix products, arithmetic and copies ran while one was open for 5% of the time, Pallas kernels for 0%

commit v1 on v0

v1 whole, which is shorter than its diff:
```python
import functools

import jax
import jax.numpy as jnp
from jax import lax
from jax.experimental import pallas as pl
from jax.experimental.pallas import tpu as pltpu
from jax.sharding import PartitionSpec as P

SWEEPS = 2
RING = ("row", "inner")
VMEM_BYTES = 48 * 1024 * 1024


def shifted_by(x, by):
    size = lax.axis_size(RING)
    return lax.ppermute(x, RING, [(i, (i + by) % size) for i in range(size)])


class Frame:
    def __init__(self, half, order):
        self.h = half
        self.b = order
        self.k = 2 * half
        self.rows = 3 * half
        self.pairs = self.rows // 2
        self.reach = half // 2
        self.own_pairs = range(half // 2, half)

    def tiles(self, columns):
        for col in columns:
            for row in range(max(0, col - self.reach), min(self.pairs, col + self.reach + 1)):
                yield row, col

    def inner(self, row, col):
        return max(row, col) - self.reach, min(row, col) + self.reach + 1


def starts(counts):
    out = [0]
    for c in counts:
        out.append(out[-1] + c)
    return out


def near_below_counts(h):
    return [h + 1 + k for k in range(h)]


def near_above_counts(h):
    return [2 * h - k for k in range(h)]


def far_below_counts(h):
    return [k + 1 for k in range(h)]


def far_above_counts(h):
    return [h - k for k in range(h)]


def last_slots(rows, counts):
    width = rows.shape[1]
    return jnp.concatenate([rows[k, width - c :] for k, c in enumerate(counts)], axis=0)


def first_slots(rows, counts):
    return jnp.concatenate([rows[k, :c] for k, c in enumerate(counts)], axis=0)


def block_at(slots_of, offset, dropped, slot_limit):
    slot = jnp.minimum(offset - (offset > dropped).astype(jnp.int32), slot_limit)
    value = slots_of(slot)
    return jnp.where(offset == dropped, jnp.zeros_like(value), value)


def fill_row(f, dest, row, row_shift, slots_of, dropped, lo_col, hi_col):
    b = f.b
    first = 2 * (row // 2) - 2 * f.reach
    for col in range(max(lo_col, first), min(hi_col, first + 4 * f.reach + 2)):
        offset = col - row + f.h
        place = (
            pl.ds((row + row_shift) * b, b),
            pl.ds((col + row_shift) * b, b),
        )
        if 0 <= offset <= f.k:
            dest[place] = block_at(slots_of, offset, dropped, f.k - 1)
        else:
            dest[place] = jnp.zeros((b, b), dest.dtype)


def masked(f, tile, row, col, drop_ref):
    b = f.b
    parts = []
    for i in range(2):
        r = 2 * row + i
        line = []
        for j in range(2):
            offset = 2 * col + j - r + f.h
            piece = tile[i * b : (i + 1) * b, j * b : (j + 1) * b]
            if 0 <= offset <= f.k:
                piece = jnp.where(drop_ref[r + f.h] == offset, 0.0, piece)
            else:
                piece = jnp.zeros_like(piece)
            line.append(piece)
        parts.append(jnp.concatenate(line, axis=1))
    return jnp.concatenate(parts, axis=0)


def band_place(f, row, lo, hi):
    t = 2 * f.b
    return pl.ds(row * t, t), pl.ds((lo - row + f.reach) * t, (hi - lo) * t)


def dense_place(f, row_lo, row_hi, col_lo, col_hi):
    t = 2 * f.b
    return pl.ds(row_lo * t, (row_hi - row_lo) * t), pl.ds(col_lo * t, (col_hi - col_lo) * t)


def dot(a, b):
    return jnp.dot(a, b, preferred_element_type=jnp.float32)


def square_kernel(f, drop_ref, own, below, above, far_below, far_above, square, shifted, wide):
    h, k = f.h, f.k
    for r in range(h):
        for source, row in ((below, r), (own, h + r), (above, 2 * h + r)):
            fill_row(
                f, wide, row, h, lambda s, source=source, r=r: source[r, s], drop_ref[row + h], -h, 4 * h
            )
    low, high = starts(far_below_counts(h)), starts(far_above_counts(h))
    for r in range(h):
        base = low[r] - (k - (r + 1))
        fill_row(
            f, wide, r - h, h,
            lambda s, base=base, lo=k - (r + 1): far_below[base + jnp.maximum(s, lo)],
            drop_ref[r], 0, r + 1,
        )
        for col in range(r + 1, 2 * (r // 2) + 2):
            wide[pl.ds(r * f.b, f.b), pl.ds((col + h) * f.b, f.b)] = jnp.zeros((f.b, f.b), wide.dtype)
        fill_row(
            f, wide, 3 * h + r, h,
            lambda s, base=high[r], hi=h - r - 1: far_above[base + jnp.minimum(s, hi)],
            drop_ref[4 * h + r], 2 * h + r, 3 * h,
        )
        for col in range(2 * h + 2 * (r // 2), 2 * h + r):
            wide[pl.ds((4 * h + r) * f.b, f.b), pl.ds((col + h) * f.b, f.b)] = jnp.zeros(
                (f.b, f.b), wide.dtype
            )
    t = 2 * f.b
    shift = h // 2
    unit = (
        lax.broadcasted_iota(jnp.int32, (t, t), 0) == lax.broadcasted_iota(jnp.int32, (t, t), 1)
    ).astype(jnp.float32)
    for row, col in f.tiles(range(f.pairs)):
        lo, hi = f.inner(row, col)
        lo, hi = lo + shift, hi + shift
        total = dot(
            wide[dense_place(f, row + shift, row + shift + 1, lo, hi)],
            wide[dense_place(f, lo, hi, col + shift, col + shift + 1)],
        )
        total = masked(f, total, row, col, drop_ref)
        here = wide[dense_place(f, row + shift, row + shift + 1, col + shift, col + shift + 1)]
        moved = 2.0 * total - 2.0 * here.astype(jnp.float32)
        if row == col:
            moved = moved + unit
        place = band_place(f, row, col, col + 1)
        square[place] = total.astype(square.dtype)
        shifted[place] = moved.astype(shifted.dtype)


def clipped(f, row, col):
    lo, hi = f.inner(row, col)
    return max(lo, 0), min(hi, f.pairs)


def local(f, col):
    return col - f.h // 2


def own_place(f, lo, hi, col):
    return dense_place(f, lo, hi, local(f, col), local(f, col) + 1)


def sweep_kernel(f, drop_ref, shifted, own, below, above, fresh, to_next, to_prev, wide, correction):
    h, k, b = f.h, f.k, f.b
    low, high = starts(near_below_counts(h)), starts(near_above_counts(h))
    for r in range(h):
        lo = k - near_below_counts(h)[r]
        fill_row(
            f, wide, r, 0,
            lambda s, base=low[r] - lo, lo=lo: below[base + jnp.maximum(s, lo)],
            drop_ref[r + h], 0, 3 * h,
        )
        fill_row(f, wide, h + r, 0, lambda s, r=r: own[r, s], drop_ref[r + 2 * h], 0, 3 * h)
        fill_row(
            f, wide, 2 * h + r, 0,
            lambda s, base=high[r], hi=near_above_counts(h)[r] - 1: above[base + jnp.minimum(s, hi)],
            drop_ref[r + 3 * h], 0, 3 * h,
        )
    for row, col in f.tiles(f.own_pairs):
        lo, hi = clipped(f, row, col)
        total = dot(shifted[band_place(f, row, lo, hi)], wide[dense_place(f, lo, hi, col, col + 1)])
        correction[own_place(f, row, row + 1, col)] = masked(f, total, row, col, drop_ref).astype(
            correction.dtype
        )
    for row, col in f.tiles(f.own_pairs):
        lo, hi = clipped(f, row, col)
        total = dot(wide[dense_place(f, row, row + 1, lo, hi)], correction[own_place(f, lo, hi, col)])
        total = masked(f, total, row, col, drop_ref)
        here = wide[dense_place(f, row, row + 1, col, col + 1)].astype(jnp.float32)
        fresh[own_place(f, row, row + 1, col)] = (2.0 * here - total).astype(fresh.dtype)
    at = 0
    for c in range(h):
        for r in range(h, h + h + 1 + c):
            to_next[at] = fresh[pl.ds(r * b, b), pl.ds(c * b, b)]
            at += 1
    at = 0
    for c in range(h):
        for r in range(c, 2 * h):
            to_prev[at] = fresh[pl.ds(r * b, b), pl.ds(c * b, b)]
            at += 1


def right_kernel(f, drop_ref, left, right, out):
    for row, col in f.tiles(f.own_pairs):
        lo, hi = clipped(f, row, col)
        total = dot(left[band_place(f, row, lo, hi)], right[own_place(f, lo, hi, col)])
        out[own_place(f, row, row + 1, col)] = masked(f, total, row, col, drop_ref).astype(out.dtype)


def edge_blocks(f, matrix, to_next, to_prev):
    h, b = f.h, f.b
    at = 0
    for c in range(h):
        for r in range(2 * h, 2 * h + c + 1):
            to_next[at] = matrix[pl.ds(r * b, b), pl.ds(c * b, b)]
            at += 1
    at = 0
    for c in range(h):
        for r in range(c, h):
            to_prev[at] = matrix[pl.ds(r * b, b), pl.ds(c * b, b)]
            at += 1


def last_sweep_kernel(f, drop_ref, own, below, above, correction, fresh, to_next, to_prev, low, high):
    h, b = f.h, f.b
    zero = jnp.zeros((b, b), low.dtype)
    at = 0
    for c in range(h):
        for r in range(h + 1 + c):
            low[pl.ds(r * b, b), pl.ds(c * b, b)] = below[at]
            at += 1
        for r in range(h + 1 + c, 2 * (c // 2) + h + 2):
            low[pl.ds(r * b, b), pl.ds(c * b, b)] = zero
    at = 0
    for c in range(h):
        for r in range(2 * (c // 2), c):
            high[pl.ds(r * b, b), pl.ds(c * b, b)] = zero
        for r in range(c, 2 * h):
            high[pl.ds(r * b, b), pl.ds(c * b, b)] = above[at]
            at += 1
    s = h // 2
    for row, col in f.tiles(f.own_pairs):
        lo, hi = clipped(f, row, col)
        total = None
        for source, first, last, row_shift in ((low, 0, s, 0), (own, s, 2 * s, 0), (high, 2 * s, 3 * s, s)):
            a, z = max(lo, first), min(hi, last)
            if a >= z:
                continue
            part = dot(
                source[dense_place(f, row - row_shift, row - row_shift + 1, a - first, z - first)],
                correction[own_place(f, a, z, col)],
            )
            total = part if total is None else total + part
        total = masked(f, total, row, col, drop_ref)
        here = own[own_place(f, row, row + 1, col)].astype(jnp.float32)
        fresh[own_place(f, row, row + 1, col)] = (2.0 * here - total).astype(fresh.dtype)
    edge_blocks(f, fresh, to_next, to_prev)


def density_kernel(f, drop_ref, square, inverse, out, to_next, to_prev):
    right_kernel(f, drop_ref, square, inverse, out)
    edge_blocks(f, out, to_next, to_prev)


def rows_kernel(f, drop_ref, *refs):
    h, k, b = f.h, f.k, f.b
    low = starts([h - c for c in range(h)])
    low = starts([c + 1 for c in range(h)])
    high = starts([h - c for c in range(h)])
    half = len(refs) // 2
    outs = refs[-2:]
    for which in range(2):
        own, below, above = refs[3 * which : 3 * which + 3]
        out = outs[which]
        for r in range(h):
            dropped = drop_ref[r + 2 * h]

            def at_offset(offset, r=r, own=own, below=below, above=above):
                col = r + offset
                if col < h:
                    return below[low[col] + r]
                if col < 2 * h:
                    return own[pl.ds((h + r) * b, b), pl.ds((col - h) * b, b)]
                return above[high[col - 2 * h] + r - (col - 2 * h)]

            for s in range(k):
                out[r, s] = jnp.where(dropped <= s, at_offset(s + 1), at_offset(s))


def call(kernel, out_shapes, scratch, flops, drop, *args):
    vmem = pl.BlockSpec(memory_space=pltpu.VMEM)
    moved = sum(a.size * a.dtype.itemsize for a in args)
    moved += sum(s.size * s.dtype.itemsize for s in out_shapes)
    return pl.pallas_call(
        kernel,
        out_shape=out_shapes,
        in_specs=[pl.BlockSpec(memory_space=pltpu.SMEM)] + [vmem] * len(args),
        out_specs=[vmem] * len(out_shapes),
        scratch_shapes=scratch,
        compiler_params=pltpu.CompilerParams(vmem_limit_bytes=VMEM_BYTES),
        cost_estimate=pl.CostEstimate(flops=flops, bytes_accessed=moved, transcendentals=0),
    )(drop, *args)


def on_device(density, inverse_start, block_cols):
    rows, width, order, _ = density.shape
    half = width // 2
    assert rows == half and half % 2 == 0
    f = Frame(half, order)
    total_rows = rows * lax.axis_size(RING)
    kind = density.dtype

    below = shifted_by(density, 1)
    above = shifted_by(density, -1)
    inverse_below = shifted_by(last_slots(inverse_start, near_below_counts(half)), 1)
    inverse_above = shifted_by(first_slots(inverse_start, near_above_counts(half)), -1)

    own_ids = lax.axis_index(RING) * rows + jnp.arange(rows, dtype=jnp.int32)
    positions = jnp.mod(block_cols - own_ids[:, None] + half, total_rows)
    dropped = width * (width + 1) // 2 - jnp.sum(positions, axis=1)
    drop = jnp.concatenate(
        [shifted_by(dropped, 2), shifted_by(dropped, 1), dropped, shifted_by(dropped, -1), shifted_by(dropped, -2)]
    )

    far_below = shifted_by(last_slots(below, far_below_counts(half)), 1)
    far_above = shifted_by(first_slots(above, far_above_counts(half)), -1)

    tile_flops = 2 * (2 * order) ** 3
    span = f.rows * order
    band = jax.ShapeDtypeStruct((span, (2 * f.reach + 1) * 2 * order), kind)
    columns = jax.ShapeDtypeStruct((span, half * order), kind)
    near = jax.ShapeDtypeStruct((sum(near_below_counts(half)), order, order), kind)
    edge = jax.ShapeDtypeStruct((sum(far_below_counts(half)), order, order), kind)
    square, shifted = call(
        functools.partial(square_kernel, f),
        [band, band],
        [pltpu.VMEM((5 * half * order, 5 * half * order), kind)],
        94 * tile_flops,
        drop, density, below, above, far_below, far_above,
    )
    inverse, to_next, to_prev = call(
        functools.partial(sweep_kernel, f),
        [columns, near, near],
        [pltpu.VMEM((span, span), kind), pltpu.VMEM((span, half * order), kind)],
        76 * tile_flops,
        drop, shifted, inverse_start, inverse_below, inverse_above,
    )
    inverse_below = shifted_by(to_next, 1)
    inverse_above = shifted_by(to_prev, -1)
    (correction,) = call(
        functools.partial(right_kernel, f), [columns], [], 38 * tile_flops, drop, shifted, inverse
    )
    inverse, to_next, to_prev = call(
        functools.partial(last_sweep_kernel, f),
        [columns, edge, edge],
        [pltpu.VMEM((2 * half * order, half * order), kind), pltpu.VMEM((2 * half * order, half * order), kind)],
        38 * tile_flops,
        drop, inverse, inverse_below, inverse_above, correction,
    )
    inverse_parts = (inverse, shifted_by(to_next, 1), shifted_by(to_prev, -1))
    density_columns, to_next, to_prev = call(
        functools.partial(density_kernel, f), [columns, edge, edge], [], 38 * tile_flops, drop, square, inverse
    )
    density_parts = (density_columns, shifted_by(to_next, 1), shifted_by(to_prev, -1))
    out = jax.ShapeDtypeStruct(density.shape, kind)
    return tuple(
        call(functools.partial(rows_kernel, f), [out, out], [], 0, drop, *density_parts, *inverse_parts)
    )


def solution(mesh):
    blocks = P(("grp", "row", "inner"), None, None, None)
    return jax.shard_map(
        on_device,
        mesh=mesh,
        in_specs=(blocks, blocks, P(("grp", "row", "inner"), None)),
        out_specs=(blocks, blocks),
        check_vma=False,
    )
```

time: 196 us -> 123 us (0.63)
  waiting for transfers between devices: 125 us -> 57.7 us
  matrix products: 28.2 us -> 0 us
  Pallas kernels: 0 us -> 26.4 us
  starting transfers between devices: 20.2 us -> 29.3 us
  other arithmetic: 9.96 us -> 3.75 us
  local copies, waits for them, and re-layouts: 9.93 us -> 4.67 us
    ppermute x14 -> x16, waiting for transfers between devices: 125 us -> 57.7 us  [shifted_by(): return lax.ppermute(x, RING, [(i, (i + by) % size) for i in range(size)])]
    dot_general x54 -> x0, matrix products: 28.2 us -> none  [band_product(): jnp.einsum('rab,rqbc->rqac', left_band[:, slot_left], aligned, preferred_...]
    pallas_call x0 -> x6, Pallas kernels: none -> 26.4 us  [call(): pl.pallas_call(kernel, out_shape=out_shapes, in_specs=[pl.BlockSpec(memor...]
    ppermute x14 -> x16, starting transfers between devices: 20.2 us -> 29.3 us  [shifted_by(): return lax.ppermute(x, RING, [(i, (i + by) % size) for i in range(size)])]
    unnamed x14 -> x8, local copies, waits for them, and re-layouts: 8.31 us -> 2.4 us
    select_n x8 -> x0, other arithmetic: 5.84 us -> none  [to_band(): jnp.where(take_left, left_copy, jnp.where(take_right, right_copy, empty))]
    convert_element_type x9 -> x0, other arithmetic: 2.24 us -> none  [the longest x2 0.92 us: on_device(): inverse = (2.0 * inverse.astype(jnp.float32) - update).astype(jnp.bfloat16)]
    squeeze x0 -> x12, local copies, waits for them, and re-layouts: none -> 2.19 us  [the longest x8 2.16 us: first_slots(): return jnp.concatenate([rows[k, :c] for k, c in enumerate(counts)], axis=0)]
  transfers between devices with their start and end apart: 14 -> 16, of which waited for: 6 -> 11; matrix products, arithmetic and copies ran while one was open for 5% -> 5% of each run, Pallas kernels for 0% -> 12%
where the time goes in v1:
time: 123 us
  waiting for transfers between devices  57.7 us (47%)
  starting transfers between devices  29.3 us (24%)
  Pallas kernels  26.4 us (21%)
  local copies, waits for them, and re-layouts  4.67 us (4%)
  other arithmetic  3.75 us (3%)
    ppermute x16, waiting for transfers between devices, shifted_by(): return lax.ppermute(x, RING, [(i, (i + by) % size) for i in range(size)])  57.7 us
    ppermute x16, starting transfers between devices, shifted_by(): return lax.ppermute(x, RING, [(i, (i + by) % size) for i in range(size)])  29.3 us
    pallas_call x6, Pallas kernels, call(): pl.pallas_call(kernel, out_shape=out_shapes, in_specs=[pl.BlockSpec(memor...  26.4 us
  transfers between devices with their start and end apart: 16, of which 11 were waited for; matrix products, arithmetic and copies ran while one was open for 5% of the time, Pallas kernels for 12%

profile of v1, /device:TPU:1, one launch (start us, length us, event | category | flops | bytes accessed | tf_op | source)
XLA Modules:
  0.0 122.6 jit_solution(2104375907416974505)
XLA Ops:
  0.6 2.7 %collective-permute-start.4 = (bf16[4,8,128,128]{3,2,1,0:T(8,128)(2,1)}, bf16[4,8,128,128]{3,2,1,0:T(8,128)(2,1)S(1)}, u32[]{:S(2)}, u32[]{:S(2)}) collective-permute-start(bf16[4,8,128,128]{3,2,1,0:T(8,128)(2,1)} %own.2), channel_id=1, source_target_pairs={{0,1},{1,2},{2,3},{3,4},{4,5},{5,6},{6,7},{7,8},{8,9},{9,10},{10,1... | collective-permute-start | bytes 3145736 | tf_op jit(solution)/shard_map/ppermute | solution.py:17
  6.5 1.7 %collective-permute-start.8 = (bf16[26,128,128]{2,1,0:T(8,128)(2,1)}, bf16[26,128,128]{2,1,0:T(8,128)(2,1)}, u32[]{:S(2)}, u32[]{:S(2)}) collective-permute-start(bf16[26,128,128]{2,1,0:T(8,128)(2,1)} %pad_maximum_fusion), channel_id=1, source_target_pairs={{0,1},{1,2},{2,3},{3,4},{4,5},{5,6},{6,7},{7,8},{8,9},{9,10},{10,1... | collective-permute-start | bytes 2555912 | tf_op jit(solution)/shard_map/ppermute | solution.py:17
  10.4 25.3 %collective-permute-done.4.below = bf16[4,8,128,128]{3,2,1,0:T(8,128)(2,1)S(1)} collective-permute-done((bf16[4,8,128,128]{3,2,1,0:T(8,128)(2,1)}, bf16[4,8,128,128]{3,2,1,0:T(8,128)(2,1)S(1)}, u32[]{:S(2)}, u32[]{:S(2)}) %collective-permute-start.4) | collective-permute-done | bytes 1048608 | tf_op jit(solution)/shard_map/ppermute | solution.py:17
  36.5 2.4 %collective-permute-start.6 = (bf16[10,128,128]{2,1,0:T(8,128)(2,1)}, bf16[10,128,128]{2,1,0:T(8,128)(2,1)S(1)}, u32[]{:S(2)}, u32[]{:S(2)}) collective-permute-start(bf16[10,128,128]{2,1,0:T(8,128)(2,1)} %pad_maximum_fusion.2), channel_id=1, source_target_pairs={{0,1},{1,2},{2,3},{3,4},{4,5},{5,6},{6,7},{7,8},{8,9},{9,10},{10,1... | collective-permute-start | bytes 983048 | tf_op jit(solution)/shard_map/ppermute | solution.py:17
  38.9 2.7 %collective-permute-done.5.above = bf16[4,8,128,128]{3,2,1,0:T(8,128)(2,1)S(1)} collective-permute-done((bf16[4,8,128,128]{3,2,1,0:T(8,128)(2,1)}, bf16[4,8,128,128]{3,2,1,0:T(8,128)(2,1)S(1)}, u32[]{:S(2)}, u32[]{:S(2)}) %collective-permute-start.5) | collective-permute-done | bytes 1048608 | tf_op jit(solution)/shard_map/ppermute | solution.py:17
  42.6 2.3 %collective-permute-start.3 = (s32[4]{0:T(128)S(1)}, s32[4]{0:T(128)S(1)}, u32[]{:S(2)}, u32[]{:S(2)}) collective-permute-start(s32[4]{0:T(128)S(1)} %broadcast_subtract_fusion), channel_id=1, source_target_pairs={{0,14},{1,15},{2,0},{3,1},{4,2},{5,3},{6,4},{7,5},{8,6},{9,7},{10,... | collective-permute-start | bytes 56 | tf_op jit(solution)/shard_map/ppermute | solution.py:17
  45.6 9.3 %collective-permute-start.2 = (s32[4]{0:T(128)S(1)}, s32[4]{0:T(128)S(1)}, u32[]{:S(2)}, u32[]{:S(2)}) collective-permute-start(s32[4]{0:T(128)S(1)} %broadcast_subtract_fusion), channel_id=1, source_target_pairs={{0,15},{1,0},{2,1},{3,2},{4,3},{5,4},{6,5},{7,6},{8,7},{9,8},{10,9... | collective-permute-start | bytes 56 | tf_op jit(solution)/shard_map/ppermute | solution.py:17
  56.9 1.9 %collective-permute-start = (s32[4]{0:T(128)S(1)}, s32[4]{0:T(128)S(1)}, u32[]{:S(2)}, u32[]{:S(2)}) collective-permute-start(s32[4]{0:T(128)S(1)} %broadcast_subtract_fusion), channel_id=1, source_target_pairs={{0,2},{1,3},{2,4},{3,5},{4,6},{5,7},{6,8},{7,9},{8,10},{9,11},{10,... | collective-permute-start | bytes 56 | tf_op jit(solution)/shard_map/ppermute | solution.py:17
  58.7 3.5 %collective-permute-done = s32[4]{0:T(128)S(1)} collective-permute-done((s32[4]{0:T(128)S(1)}, s32[4]{0:T(128)S(1)}, u32[]{:S(2)}, u32[]{:S(2)}) %collective-permute-start) | collective-permute-done | bytes 48 | tf_op jit(solution)/shard_map/ppermute | solution.py:17
  62.3 1.2 copy-done.2
  63.6 7.9 %shard_map.50 = (bf16[1536,1280]{1,0:T(8,128)(2,1)}, bf16[1536,1280]{1,0:T(8,128)(2,1)}) custom-call(s32[20]{0:T(128)S(1)} %concatenate.15.drop_ref, bf16[4,8,128,128]{3,2,1,0:T(8,128)(2,1)S(1)} %copy-done.2, bf16[4,8,128,128]{3,2,1,0:T(8,128)(2,1)S(1)} %collective-permute-done.4.below, bf16[4,8,128,128]{3,2,1,0:T(8,128)(2,1)S(1)} %collective-permute-done.5.above, ...), custom_call_target="tpu_custom_call" | custom-call | flops 3154116608 | bytes 11665408 | tf_op jit(solution)/shard_map/pallas_call | solution.py:316
  71.5 5.8 %shard_map.51 = (bf16[1536,512]{1,0:T(8,128)(2,1)S(1)}, bf16[26,128,128]{2,1,0:T(8,128)(2,1)S(1)}, bf16[26,128,128]{2,1,0:T(8,128)(2,1)S(1)}) custom-call(s32[20]{0:T(128)S(1)} %concatenate.15.drop_ref, bf16[1536,1280]{1,0:T(8,128)(2,1)} %get-tuple-element.14.shifted.left, bf16[4,8,128,128]{3,2,1,0:T(8,128)(2,1)S(1)} %copy-done.1, ...), custom_call_target="tpu_custom_call" | custom-call | flops 2550136832 | bytes 9961472 | tf_op jit(solution)/shard_map/pallas_call | solution.py:316
  77.3 2.8 %collective-permute-start.10 = (bf16[26,128,128]{2,1,0:T(8,128)(2,1)S(1)}, bf16[26,128,128]{2,1,0:T(8,128)(2,1)S(1)}, u32[]{:S(2)}, u32[]{:S(2)}) collective-permute-start(bf16[26,128,128]{2,1,0:T(8,128)(2,1)S(1)} %get-tuple-element.16), channel_id=1, source_target_pairs={{0,1},{1,2},{2,3},{3,4},{4,5},{5,6},{6,7},{7,8},{8,9},{9,10},{10,1... | collective-permute-start | bytes 2555912 | tf_op jit(solution)/shard_map/ppermute | solution.py:17
  80.1 3.1 %collective-permute-start.11 = (bf16[26,128,128]{2,1,0:T(8,128)(2,1)S(1)}, bf16[26,128,128]{2,1,0:T(8,128)(2,1)S(1)}, u32[]{:S(2)}, u32[]{:S(2)}) collective-permute-start(bf16[26,128,128]{2,1,0:T(8,128)(2,1)S(1)} %get-tuple-element.17), channel_id=1, source_target_pairs={{0,15},{1,0},{2,1},{3,2},{4,3},{5,4},{6,5},{7,6},{8,7},{9,8},{10,9... | collective-permute-start | bytes 2555912 | tf_op jit(solution)/shard_map/ppermute | solution.py:17
  83.3 3.6 %shard_map.52.correction = bf16[1536,512]{1,0:T(8,128)(2,1)S(1)} custom-call(s32[20]{0:T(128)S(1)} %concatenate.15.drop_ref, bf16[1536,1280]{1,0:T(8,128)(2,1)} %get-tuple-element.14.shifted.left, bf16[1536,512]{1,0:T(8,128)(2,1)S(1)} %get-tuple-element.15.right.own), custom_call_target="tpu_custom_call" | custom-call | flops 1275068416 | bytes 7077888 | tf_op jit(solution)/shard_map/pallas_call | solution.py:316
  88.0 10.9 %collective-permute-done.10.below = bf16[26,128,128]{2,1,0:T(8,128)(2,1)S(1)} collective-permute-done((bf16[26,128,128]{2,1,0:T(8,128)(2,1)S(1)}, bf16[26,128,128]{2,1,0:T(8,128)(2,1)S(1)}, u32[]{:S(2)}, u32[]{:S(2)}) %collective-permute-start.10) | collective-permute-done | bytes 852000 | tf_op jit(solution)/shard_map/ppermute | solution.py:17
  98.9 2.5 %collective-permute-done.11.above = bf16[26,128,128]{2,1,0:T(8,128)(2,1)S(1)} collective-permute-done((bf16[26,128,128]{2,1,0:T(8,128)(2,1)S(1)}, bf16[26,128,128]{2,1,0:T(8,128)(2,1)S(1)}, u32[]{:S(2)}, u32[]{:S(2)}) %collective-permute-start.11) | collective-permute-done | bytes 852000 | tf_op jit(solution)/shard_map/ppermute | solution.py:17
  101.4 3.1 %shard_map.53 = (bf16[1536,512]{1,0:T(8,128)(2,1)S(1)}, bf16[10,128,128]{2,1,0:T(8,128)(2,1)S(1)}, bf16[10,128,128]{2,1,0:T(8,128)(2,1)S(1)}) custom-call(s32[20]{0:T(128)S(1)} %concatenate.15.drop_ref, bf16[1536,512]{1,0:T(8,128)(2,1)S(1)} %get-tuple-element.15.right.own, bf16[26,128,128]{2,1,0:T(8,128)(2,1)S(1)} %collective-permute-done.10.below, ...), custom_call_target="tpu_custom_call" | custom-call | flops 1275068416 | bytes 7077888 | tf_op jit(solution)/shard_map/pallas_call | solution.py:316
  105.1 3.7 %shard_map.54 = (bf16[1536,512]{1,0:T(8,128)(2,1)S(1)}, bf16[10,128,128]{2,1,0:T(8,128)(2,1)S(1)}, bf16[10,128,128]{2,1,0:T(8,128)(2,1)S(1)}) custom-call(s32[20]{0:T(128)S(1)} %concatenate.15.drop_ref, bf16[1536,1280]{1,0:T(8,128)(2,1)} %get-tuple-element.13.square, bf16[1536,512]{1,0:T(8,128)(2,1)S(1)} %get-tuple-element.18.inverse.refs_3_), custom_call_target="tpu_custom_call" | custom-call | flops 1275068416 | bytes 7733248 | tf_op jit(solution)/shard_map/pallas_call | solution.py:316
  108.8 1.4 %collective-permute-start.12 = (bf16[10,128,128]{2,1,0:T(8,128)(2,1)S(1)}, bf16[10,128,128]{2,1,0:T(8,128)(2,1)S(1)}, u32[]{:S(2)}, u32[]{:S(2)}) collective-permute-start(bf16[10,128,128]{2,1,0:T(8,128)(2,1)S(1)} %get-tuple-element.20), channel_id=1, source_target_pairs={{0,1},{1,2},{2,3},{3,4},{4,5},{5,6},{6,7},{7,8},{8,9},{9,10},{10,1... | collective-permute-start | bytes 983048 | tf_op jit(solution)/shard_map/ppermute | solution.py:17
  110.1 3.2 %collective-permute-done.15.refs_5_ = bf16[10,128,128]{2,1,0:T(8,128)(2,1)S(1)} collective-permute-done((bf16[10,128,128]{2,1,0:T(8,128)(2,1)S(1)}, bf16[10,128,128]{2,1,0:T(8,128)(2,1)S(1)}, u32[]{:S(2)}, u32[]{:S(2)}) %collective-permute-start.15) | collective-permute-done | bytes 327712 | tf_op jit(solution)/shard_map/ppermute | solution.py:17
  113.4 5.8 %collective-permute-done.12.refs_1_ = bf16[10,128,128]{2,1,0:T(8,128)(2,1)S(1)} collective-permute-done((bf16[10,128,128]{2,1,0:T(8,128)(2,1)S(1)}, bf16[10,128,128]{2,1,0:T(8,128)(2,1)S(1)}, u32[]{:S(2)}, u32[]{:S(2)}) %collective-permute-start.12) | collective-permute-done | bytes 327712 | tf_op jit(solution)/shard_map/ppermute | solution.py:17
  119.1 1.2 %collective-permute-done.13.refs_2_ = bf16[10,128,128]{2,1,0:T(8,128)(2,1)S(1)} collective-permute-done((bf16[10,128,128]{2,1,0:T(8,128)(2,1)S(1)}, bf16[10,128,128]{2,1,0:T(8,128)(2,1)S(1)}, u32[]{:S(2)}, u32[]{:S(2)}) %collective-permute-start.13) | collective-permute-done | bytes 327712 | tf_op jit(solution)/shard_map/ppermute | solution.py:17
  120.4 2.3 %shard_map.55 = (bf16[4,8,128,128]{3,2,1,0:T(8,128)(2,1)}, bf16[4,8,128,128]{3,2,1,0:T(8,128)(2,1)}) custom-call(s32[20]{0:T(128)S(1)} %concatenate.15.drop_ref, bf16[1536,512]{1,0:T(8,128)(2,1)S(1)} %get-tuple-element.19.refs_0_, bf16[10,128,128]{2,1,0:T(8,128)(2,1)S(1)} %collective-permute-done.12.refs_1_, ...), custom_call_target="tpu_custom_call" | custom-call | bytes 6553600 | tf_op jit(solution)/shard_map/pallas_call | solution.py:316
  (42 shorter events, 11.6 us)
Async XLA Ops:
  0.6 4.7 %copy-start.1 = (bf16[4,8,128,128]{3,2,1,0:T(8,128)(2,1)S(1)}, bf16[4,8,128,128]{3,2,1,0:T(8,128)(2,1)}, u32[]{:S(2)}) copy-start(bf16[4,8,128,128]{3,2,1,0:T(8,128)(2,1)} %own.3) | copy-start | bytes 3145732
  0.6 35.1 %collective-permute-start.4 = (bf16[4,8,128,128]{3,2,1,0:T(8,128)(2,1)}, bf16[4,8,128,128]{3,2,1,0:T(8,128)(2,1)S(1)}, u32[]{:S(2)}, u32[]{:S(2)}) collective-permute-start(bf16[4,8,128,128]{3,2,1,0:T(8,128)(2,1)} %own.2), channel_id=1, source_target_pairs={{0,1},{1,2},{2,3},{3,4},{4,5},{5,6},{6,7},{7,8},{8,9},{9,10},{10,1... | collective-permute-start | bytes 3145736 | tf_op jit(solution)/shard_map/ppermute | solution.py:17
  3.3 38.3 %collective-permute-start.5 = (bf16[4,8,128,128]{3,2,1,0:T(8,128)(2,1)}, bf16[4,8,128,128]{3,2,1,0:T(8,128)(2,1)S(1)}, u32[]{:S(2)}, u32[]{:S(2)}) collective-permute-start(bf16[4,8,128,128]{3,2,1,0:T(8,128)(2,1)} %own.2), channel_id=1, source_target_pairs={{0,15},{1,0},{2,1},{3,2},{4,3},{5,4},{6,5},{7,6},{8,7},{9,8},{10,9... | collective-permute-start | bytes 3145736 | tf_op jit(solution)/shard_map/ppermute | solution.py:17
  6.5 65.0 %collective-permute-start.8 = (bf16[26,128,128]{2,1,0:T(8,128)(2,1)}, bf16[26,128,128]{2,1,0:T(8,128)(2,1)}, u32[]{:S(2)}, u32[]{:S(2)}) collective-permute-start(bf16[26,128,128]{2,1,0:T(8,128)(2,1)} %pad_maximum_fusion), channel_id=1, source_target_pairs={{0,1},{1,2},{2,3},{3,4},{4,5},{5,6},{6,7},{7,8},{8,9},{9,10},{10,1... | collective-permute-start | bytes 2555912 | tf_op jit(solution)/shard_map/ppermute | solution.py:17
  9.2 33.2 %copy-start.3 = (s32[4,8]{1,0:T(4,128)S(1)}, s32[4,8]{1,0:T(4,128)}, u32[]{:S(2)}) copy-start(s32[4,8]{1,0:T(4,128)} %param.5) | copy-start | bytes 388
  9.2 62.2 %collective-permute-start.9 = (bf16[26,128,128]{2,1,0:T(8,128)(2,1)}, bf16[26,128,128]{2,1,0:T(8,128)(2,1)}, u32[]{:S(2)}, u32[]{:S(2)}) collective-permute-start(bf16[26,128,128]{2,1,0:T(8,128)(2,1)} %pad_maximum_fusion.1), channel_id=1, source_target_pairs={{0,15},{1,0},{2,1},{3,2},{4,3},{5,4},{6,5},{7,6},{8,7},{9,8},{10,9... | collective-permute-start | bytes 2555912 | tf_op jit(solution)/shard_map/ppermute | solution.py:17
  36.5 25.8 %collective-permute-start.6 = (bf16[10,128,128]{2,1,0:T(8,128)(2,1)}, bf16[10,128,128]{2,1,0:T(8,128)(2,1)S(1)}, u32[]{:S(2)}, u32[]{:S(2)}) collective-permute-start(bf16[10,128,128]{2,1,0:T(8,128)(2,1)} %pad_maximum_fusion.2), channel_id=1, source_target_pairs={{0,1},{1,2},{2,3},{3,4},{4,5},{5,6},{6,7},{7,8},{8,9},{9,10},{10,1... | collective-permute-start | bytes 983048 | tf_op jit(solution)/shard_map/ppermute | solution.py:17
  42.4 19.9 %collective-permute-start.7 = (bf16[10,128,128]{2,1,0:T(8,128)(2,1)}, bf16[10,128,128]{2,1,0:T(8,128)(2,1)}, u32[]{:S(2)}, u32[]{:S(2)}) collective-permute-start(bf16[10,128,128]{2,1,0:T(8,128)(2,1)} %pad_maximum_fusion.3), channel_id=1, source_target_pairs={{0,15},{1,0},{2,1},{3,2},{4,3},{5,4},{6,5},{7,6},{8,7},{9,8},{10,9... | collective-permute-start | bytes 983048 | tf_op jit(solution)/shard_map/ppermute | solution.py:17
  42.6 3.0 %collective-permute-start.3 = (s32[4]{0:T(128)S(1)}, s32[4]{0:T(128)S(1)}, u32[]{:S(2)}, u32[]{:S(2)}) collective-permute-start(s32[4]{0:T(128)S(1)} %broadcast_subtract_fusion), channel_id=1, source_target_pairs={{0,14},{1,15},{2,0},{3,1},{4,2},{5,3},{6,4},{7,5},{8,6},{9,7},{10,... | collective-permute-start | bytes 56 | tf_op jit(solution)/shard_map/ppermute | solution.py:17
  45.6 10.1 %collective-permute-start.2 = (s32[4]{0:T(128)S(1)}, s32[4]{0:T(128)S(1)}, u32[]{:S(2)}, u32[]{:S(2)}) collective-permute-start(s32[4]{0:T(128)S(1)} %broadcast_subtract_fusion), channel_id=1, source_target_pairs={{0,15},{1,0},{2,1},{3,2},{4,3},{5,4},{6,5},{7,6},{8,7},{9,8},{10,9... | collective-permute-start | bytes 56 | tf_op jit(solution)/shard_map/ppermute | solution.py:17
  55.7 1.1 collective-permute-start.1
  56.9 5.4 %collective-permute-start = (s32[4]{0:T(128)S(1)}, s32[4]{0:T(128)S(1)}, u32[]{:S(2)}, u32[]{:S(2)}) collective-permute-start(s32[4]{0:T(128)S(1)} %broadcast_subtract_fusion), channel_id=1, source_target_pairs={{0,2},{1,3},{2,4},{3,5},{4,6},{5,7},{6,8},{7,9},{8,10},{9,11},{10,... | collective-permute-start | bytes 56 | tf_op jit(solution)/shard_map/ppermute | solution.py:17
  62.3 1.2 %copy-start.2 = (bf16[4,8,128,128]{3,2,1,0:T(8,128)(2,1)S(1)}, bf16[4,8,128,128]{3,2,1,0:T(8,128)(2,1)}, u32[]{:S(2)}) copy-start(bf16[4,8,128,128]{3,2,1,0:T(8,128)(2,1)} %own.2) | copy-start | bytes 3145732
  77.3 21.6 %collective-permute-start.10 = (bf16[26,128,128]{2,1,0:T(8,128)(2,1)S(1)}, bf16[26,128,128]{2,1,0:T(8,128)(2,1)S(1)}, u32[]{:S(2)}, u32[]{:S(2)}) collective-permute-start(bf16[26,128,128]{2,1,0:T(8,128)(2,1)S(1)} %get-tuple-element.16), channel_id=1, source_target_pairs={{0,1},{1,2},{2,3},{3,4},{4,5},{5,6},{6,7},{7,8},{8,9},{9,10},{10,1... | collective-permute-start | bytes 2555912 | tf_op jit(solution)/shard_map/ppermute | solution.py:17
  80.1 21.2 %collective-permute-start.11 = (bf16[26,128,128]{2,1,0:T(8,128)(2,1)S(1)}, bf16[26,128,128]{2,1,0:T(8,128)(2,1)S(1)}, u32[]{:S(2)}, u32[]{:S(2)}) collective-permute-start(bf16[26,128,128]{2,1,0:T(8,128)(2,1)S(1)} %get-tuple-element.17), channel_id=1, source_target_pairs={{0,15},{1,0},{2,1},{3,2},{4,3},{5,4},{6,5},{7,6},{8,7},{9,8},{10,9... | collective-permute-start | bytes 2555912 | tf_op jit(solution)/shard_map/ppermute | solution.py:17
  86.8 1.2 copy-start
  104.5 5.6 %collective-permute-start.14 = (bf16[10,128,128]{2,1,0:T(8,128)(2,1)S(1)}, bf16[10,128,128]{2,1,0:T(8,128)(2,1)S(1)}, u32[]{:S(2)}, u32[]{:S(2)}) collective-permute-start(bf16[10,128,128]{2,1,0:T(8,128)(2,1)S(1)} %get-tuple-element.22), channel_id=1, source_target_pairs={{0,1},{1,2},{2,3},{3,4},{4,5},{5,6},{6,7},{7,8},{8,9},{9,10},{10,1... | collective-permute-start | bytes 983048 | tf_op jit(solution)/shard_map/ppermute | solution.py:17
  104.6 8.8 %collective-permute-start.15 = (bf16[10,128,128]{2,1,0:T(8,128)(2,1)S(1)}, bf16[10,128,128]{2,1,0:T(8,128)(2,1)S(1)}, u32[]{:S(2)}, u32[]{:S(2)}) collective-permute-start(bf16[10,128,128]{2,1,0:T(8,128)(2,1)S(1)} %get-tuple-element.23), channel_id=1, source_target_pairs={{0,15},{1,0},{2,1},{3,2},{4,3},{5,4},{6,5},{7,6},{8,7},{9,8},{10,9... | collective-permute-start | bytes 983048 | tf_op jit(solution)/shard_map/ppermute | solution.py:17
  108.8 10.3 %collective-permute-start.12 = (bf16[10,128,128]{2,1,0:T(8,128)(2,1)S(1)}, bf16[10,128,128]{2,1,0:T(8,128)(2,1)S(1)}, u32[]{:S(2)}, u32[]{:S(2)}) collective-permute-start(bf16[10,128,128]{2,1,0:T(8,128)(2,1)S(1)} %get-tuple-element.20), channel_id=1, source_target_pairs={{0,1},{1,2},{2,3},{3,4},{4,5},{5,6},{6,7},{7,8},{8,9},{9,10},{10,1... | collective-permute-start | bytes 983048 | tf_op jit(solution)/shard_map/ppermute | solution.py:17
  110.1 10.2 %collective-permute-start.13 = (bf16[10,128,128]{2,1,0:T(8,128)(2,1)S(1)}, bf16[10,128,128]{2,1,0:T(8,128)(2,1)S(1)}, u32[]{:S(2)}, u32[]{:S(2)}) collective-permute-start(bf16[10,128,128]{2,1,0:T(8,128)(2,1)S(1)} %get-tuple-element.21), channel_id=1, source_target_pairs={{0,15},{1,0},{2,1},{3,2},{4,3},{5,4},{6,5},{7,6},{8,7},{9,8},{10,9... | collective-permute-start | bytes 983048 | tf_op jit(solution)/shard_map/ppermute | solution.py:17

commit v2 on v0

v2 whole, which is shorter than its diff:
```python
import functools

import jax
import jax.numpy as jnp
from jax import lax
from jax.experimental import pallas as pl
from jax.experimental.pallas import tpu as pltpu
from jax.sharding import PartitionSpec as P

RING = ("row", "inner")
MIB = 1024 * 1024


class Frame:
    def __init__(self, half, order):
        self.h = half
        self.b = order
        self.k = 2 * half
        self.p = half // 2
        self.t = 2 * order
        self.group = half * order
        self.pairs = 3 * self.p
        self.own_pairs = range(self.p, 2 * self.p)
        self.edge_rows = [*range(self.p), *range(2 * self.p, 3 * self.p)]

    def tiles(self, columns):
        for col in columns:
            for row in range(max(0, col - self.p), min(self.pairs, col + self.p + 1)):
                yield row, col

    def inner(self, row, col):
        return max(row, col) - self.p, min(row, col) + self.p + 1

    def clipped(self, row, col):
        lo, hi = self.inner(row, col)
        return max(lo, 0), min(hi, self.pairs)

    def split(self, row, col):
        lo, hi = self.clipped(row, col)
        for g in range(3):
            a, z = max(lo, g * self.p), min(hi, (g + 1) * self.p)
            if a < z:
                yield g, a - g * self.p, z - g * self.p


def under(h):
    return [(r, c) for r in range(h) for c in range(r + 1)]


def over(h):
    return [(r, c) for r in range(h) for c in range(r, h)]


def at(f, row_lo, row_hi, col_lo, col_hi):
    t = f.t
    return pl.ds(row_lo * t, (row_hi - row_lo) * t), pl.ds(col_lo * t, (col_hi - col_lo) * t)


def block(f, r, c):
    return pl.ds(r * f.b, f.b), pl.ds(c * f.b, f.b)


def banded(f, row, lo, hi):
    return at(f, row, row + 1, lo - row + f.p, hi - row + f.p)


def dot(a, b):
    return jnp.dot(a, b, preferred_element_type=jnp.float32)


def stored(rows, r, offset, dropped):
    slot = jnp.minimum(offset - (offset > dropped).astype(jnp.int32), rows.shape[1] - 1)
    value = rows[r, slot]
    return jnp.where(offset == dropped, jnp.zeros_like(value), value)


def spread(f, dest, row, col, packed, places):
    index = {place: i for i, place in enumerate(places)}
    for r in range(f.h):
        for c in range(f.h):
            i = index.get((r, c))
            value = jnp.zeros((f.b, f.b), dest.dtype) if i is None else packed[i]
            dest[block(f, row + r, col + c)] = value


def pack(f, source, row, packed, places):
    for i, (r, c) in enumerate(places):
        packed[i] = source[block(f, row + r, c)]


def masked(f, tile, row, col, drop_ref):
    b = f.b
    parts = []
    for i in range(2):
        r = 2 * row + i
        line = []
        for j in range(2):
            offset = 2 * col + j - r + f.h
            piece = tile[i * b : (i + 1) * b, j * b : (j + 1) * b]
            if 0 <= offset <= f.k:
                piece = jnp.where(drop_ref[r] == offset, 0.0, piece)
            else:
                piece = jnp.zeros_like(piece)
            line.append(piece)
        parts.append(jnp.concatenate(line, axis=1))
    return jnp.concatenate(parts, axis=0)


def slabs_kernel(f, drop_ref, own, corner, up, down):
    h = f.h
    for r in range(h):
        for c in range(h):
            corner[block(f, r, c)] = stored(own, r, c - r + h, drop_ref[r])
    for i, (r, c) in enumerate(under(h)):
        up[i] = stored(own, r, 2 * h + c - r, drop_ref[r])
    for i, (r, c) in enumerate(over(h)):
        down[i] = stored(own, r, c - r, drop_ref[r])


def forward_kernel(f, drop_ref, below, above, *refs):
    h = f.h
    far_up, far_down = refs[3:5]
    odd = drop_ref[3 * h] == 1

    def send(rows, first):
        for i, (r, c) in enumerate(under(h)):
            far_up[i] = stored(rows, r, 2 * h + c - r, drop_ref[first + r])
        for i, (r, c) in enumerate(over(h)):
            far_down[i] = stored(rows, r, c - r, drop_ref[first + r])

    @pl.when(odd)
    def _():
        send(above, 2 * h)

    @pl.when(jnp.logical_not(odd))
    def _():
        send(below, 0)


def square_kernel(f, drop_ref, own, below, above, far_below, far_above, square, shifted, wide):
    h, p = f.h, f.p
    for g, source in enumerate((below, own, above)):
        for r in range(h):
            row = g * h + r
            first = 2 * (row // 2) - h
            for col in range(first, first + 2 * h + 2):
                offset = col - row + h
                if 0 <= offset <= f.k:
                    value = stored(source, r, offset, drop_ref[row])
                else:
                    value = jnp.zeros((f.b, f.b), wide.dtype)
                wide[block(f, row + h, col + h)] = value
    spread(f, wide, 0, h, far_below, under(h))
    spread(f, wide, 4 * h, 3 * h, far_above, over(h))
    unit = (
        lax.broadcasted_iota(jnp.int32, (f.t, f.t), 0) == lax.broadcasted_iota(jnp.int32, (f.t, f.t), 1)
    ).astype(jnp.float32)
    for row, col in f.tiles(range(f.pairs)):
        lo, hi = f.inner(row, col)
        lo, hi = lo + p, hi + p
        total = dot(
            wide[at(f, row + p, row + p + 1, lo, hi)], wide[at(f, lo, hi, col + p, col + p + 1)]
        )
        total = masked(f, total, row, col, drop_ref)
        here = wide[at(f, row + p, row + p + 1, col + p, col + p + 1)]
        moved = 2.0 * total - 2.0 * here.astype(jnp.float32)
        if row == col:
            moved = moved + unit
        place = banded(f, row, col, col + 1)
        square[place] = total.astype(square.dtype)
        shifted[place] = moved.astype(shifted.dtype)


def right_tile(f, left, right, row, col):
    lo, hi = f.clipped(row, col)
    return dot(left[banded(f, row, lo, hi)], right[at(f, lo, hi, col - f.p, col - f.p + 1)])


def first_sweep_kernel(
    f, drop_ref, shifted, corner, up, down, from_below, from_above, correction, fresh, partial, whole, before, after
):
    h, p = f.h, f.p
    spread(f, whole, 0, 0, from_below, under(h))
    for i in range(h):
        rows = pl.ds(i * f.b, f.b)
        whole[pl.ds((h + i) * f.b, f.b), :] = corner[rows, :]
    spread(f, whole, 2 * h, 0, from_above, over(h))
    spread(f, before, 0, 0, down, over(h))
    spread(f, after, 0, 0, up, under(h))
    for row, col in f.tiles(f.own_pairs):
        total = masked(f, right_tile(f, shifted, whole, row, col), row, col, drop_ref)
        correction[at(f, row, row + 1, col - p, col - p + 1)] = total.astype(correction.dtype)
    for row, col in f.tiles(f.own_pairs):
        c = col - p
        own_row = row in f.own_pairs
        total = 2.0 * whole[at(f, row, row + 1, c, c + 1)].astype(jnp.float32)
        for g, a, z in f.split(row, col):
            if g == 1:
                left = whole[at(f, row, row + 1, a, z)]
            elif own_row:
                left = (before, None, after)[g][at(f, row - p, row - p + 1, a, z)]
            else:
                continue
            total = total - dot(left, correction[at(f, g * p + a, g * p + z, c, c + 1)])
        if own_row:
            total = masked(f, total, row, col, drop_ref)
            fresh[at(f, row - p, row - p + 1, c, c + 1)] = total.astype(fresh.dtype)
        else:
            place = row if row < p else row - p
            partial[at(f, place, place + 1, c, c + 1)] = total


def edges(f, drop_ref, corner_below, corner_above, correction, start, low, high):
    p = f.p
    for row, col in f.tiles(f.own_pairs):
        if row in f.own_pairs:
            continue
        c = col - p
        side = 0 if row < p else 2
        corner, dest = ((corner_below, low), None, (corner_above, high))[side]
        local = row - side * p
        total = start(row, col)
        for g, a, z in f.split(row, col):
            if g == side:
                total = total - dot(
                    corner[at(f, local, local + 1, a, z)], correction[at(f, g * p + a, g * p + z, c, c + 1)]
                )
        total = masked(f, total, row, col, drop_ref)
        dest[at(f, local, local + 1, c, c + 1)] = total.astype(dest.dtype)


def first_edges_kernel(f, drop_ref, corner_below, corner_above, correction, partial, low, high, to_prev, to_next):
    p = f.p

    def start(row, col):
        place = row if row < p else row - p
        return partial[at(f, place, place + 1, col - p, col - p + 1)]

    edges(f, drop_ref, corner_below, corner_above, correction, start, low, high)
    pack(f, low, 0, to_prev, under(f.h))
    pack(f, high, 0, to_next, over(f.h))


def gather(f, whole, low, own, high):
    for g, source in enumerate((low, own, high)):
        for i in range(f.h):
            whole[pl.ds(g * f.group + i * f.b, f.b), :] = source[pl.ds(i * f.b, f.b), :]


def correction_kernel(f, drop_ref, shifted, low, own, high, correction, whole):
    p = f.p
    gather(f, whole, low, own, high)
    for row, col in f.tiles(f.own_pairs):
        total = masked(f, right_tile(f, shifted, whole, row, col), row, col, drop_ref)
        correction[at(f, row, row + 1, col - p, col - p + 1)] = total.astype(correction.dtype)


def second_edges_kernel(
    f, drop_ref, corner_below, corner_above, correction, low, high, new_low, new_high, to_prev, to_next
):
    p = f.p

    def start(row, col):
        c = col - p
        source, local = (low, row) if row < p else (high, row - 2 * p)
        total = 2.0 * source[at(f, local, local + 1, c, c + 1)].astype(jnp.float32)
        for g, a, z in f.split(row, col):
            if g == 1:
                total = total - dot(
                    source[at(f, local, local + 1, a, z)], correction[at(f, p + a, p + z, c, c + 1)]
                )
        return total

    edges(f, drop_ref, corner_below, corner_above, correction, start, new_low, new_high)
    pack(f, new_low, 0, to_prev, under(f.h))
    pack(f, new_high, 0, to_next, over(f.h))


def density_edges_kernel(
    f, drop_ref, own, from_below, from_above, correction, new_low, new_high, square, whole, to_prev, to_next,
    before, after, low, high,
):
    h, p = f.h, f.p
    spread(f, before, 0, 0, from_below, over(h))
    spread(f, after, 0, 0, from_above, under(h))
    for row, col in f.tiles(f.own_pairs):
        if row not in f.own_pairs:
            continue
        c, local = col - p, row - p
        total = 2.0 * own[at(f, local, local + 1, c, c + 1)].astype(jnp.float32)
        for g, a, z in f.split(row, col):
            left = (before, own, after)[g][at(f, local, local + 1, a, z)]
            total = total - dot(left, correction[at(f, g * p + a, g * p + z, c, c + 1)])
        total = masked(f, total, row, col, drop_ref)
        whole[at(f, row, row + 1, c, c + 1)] = total.astype(whole.dtype)
    for i in range(h):
        rows = pl.ds(i * f.b, f.b)
        whole[pl.ds(i * f.b, f.b), :] = new_low[rows, :]
        whole[pl.ds(2 * f.group + i * f.b, f.b), :] = new_high[rows, :]
    for row, col in f.tiles(f.own_pairs):
        if row in f.own_pairs:
            continue
        total = masked(f, right_tile(f, square, whole, row, col), row, col, drop_ref)
        dest, local = (low, row) if row < p else (high, row - 2 * p)
        dest[at(f, local, local + 1, col - p, col - p + 1)] = total.astype(dest.dtype)
    pack(f, low, 0, to_prev, under(h))
    pack(f, high, 0, to_next, over(h))


def density_own_kernel(f, drop_ref, square, whole, out):
    p = f.p
    for row, col in f.tiles(f.own_pairs):
        if row in f.own_pairs:
            total = masked(f, right_tile(f, square, whole, row, col), row, col, drop_ref)
            out[at(f, row - p, row - p + 1, col - p, col - p + 1)] = total.astype(out.dtype)


def rows_kernel(f, first, drop_ref, own, from_below, from_above, out):
    h = f.h
    over_index = {place: i for i, place in enumerate(over(h))}
    under_index = {place: i for i, place in enumerate(under(h))}
    for r in range(h):
        dropped = drop_ref[h + r]

        def at_offset(offset, r=r):
            col = r + offset
            if col < h:
                return from_below[over_index[r, col]]
            if col < 2 * h:
                return own[block(f, first + r, col - h)]
            return from_above[under_index[r, col - 2 * h]]

        for s in range(f.k):
            out[r, s] = jnp.where(dropped <= s, at_offset(s + 1), at_offset(s))


VMEM = pl.BlockSpec(memory_space=pltpu.VMEM)
SMEM = pl.BlockSpec(memory_space=pltpu.SMEM)
ANY = pl.BlockSpec(memory_space=pl.ANY)


def call(kernel, outs, scratch, flops, limit, drop, *args, passed=()):
    moved = sum(a.size * a.dtype.itemsize for a in args) + sum(s.size * s.dtype.itemsize for s in outs)
    n = len(args)
    return pl.pallas_call(
        kernel,
        out_shape=[*outs, *[jax.ShapeDtypeStruct(a.shape, a.dtype) for a in passed]],
        in_specs=[SMEM] + [VMEM] * n + [ANY] * len(passed),
        out_specs=[VMEM] * len(outs) + [ANY] * len(passed),
        scratch_shapes=scratch,
        input_output_aliases={1 + n + i: len(outs) + i for i in range(len(passed))},
        compiler_params=pltpu.CompilerParams(vmem_limit_bytes=limit * MIB),
        cost_estimate=pl.CostEstimate(flops=flops, bytes_accessed=moved, transcendentals=0),
    )(drop, *args, *passed)


def permuted(x, step):
    size = lax.axis_size(RING)
    return lax.ppermute(x, RING, [(i, (i + step(i)) % size) for i in range(size)])


def to_next(x):
    return permuted(x, lambda i: 1)


def to_prev(x):
    return permuted(x, lambda i: -1)


def on_device(density, inverse_start, block_cols):
    rows, width, order, _ = density.shape
    half = width // 2
    ring = lax.axis_size(RING)
    assert rows == half and half % 2 == 0 and ring % 2 == 0
    f = Frame(half, order)
    kind = density.dtype
    me = lax.axis_index(RING)

    def absent(columns, first):
        ids = first + jnp.arange(columns.shape[0], dtype=jnp.int32)
        positions = jnp.mod(columns - ids[:, None] + half, rows * ring)
        return width * (width + 1) // 2 - jnp.sum(positions, axis=1)

    below, above = to_next(density), to_prev(density)
    near_cols = jnp.concatenate([to_next(block_cols), block_cols, to_prev(block_cols)], axis=0)
    drop = jnp.concatenate([absent(near_cols, (me - 1) * rows), jnp.reshape(me % 2, (1,))])
    own_drop = absent(block_cols, me * rows)

    unit = 2 * f.t**3
    square_group = jax.ShapeDtypeStruct((f.group, f.group), kind)
    columns = jax.ShapeDtypeStruct((3 * f.group, f.group), kind)
    band = jax.ShapeDtypeStruct((3 * f.group, (2 * f.p + 1) * f.t), kind)
    triangle = jax.ShapeDtypeStruct((half * (half + 1) // 2, order, order), kind)
    partial_sums = jax.ShapeDtypeStruct((2 * f.group, f.group), jnp.float32)
    group_scratch = pltpu.VMEM((f.group, f.group), kind)
    whole_scratch = pltpu.VMEM((3 * f.group, f.group), kind)

    def run(kernel, outs, scratch, tiles, limit, *args, **kw):
        return call(functools.partial(kernel, f), outs, scratch, tiles * unit, limit, *args, **kw)

    corner, up, down = run(
        slabs_kernel, [square_group, triangle, triangle], [], 0, 8, own_drop, inverse_start
    )
    far_up, far_down, corner, up, down = run(
        forward_kernel, [triangle, triangle], [], 0, 8, drop, below, above, passed=(corner, up, down)
    )
    far_below = permuted(far_up, lambda i: 1 + 2 * (i % 2))
    far_above = permuted(far_down, lambda i: -3 + 2 * (i % 2))
    from_below, from_above = to_next(up), to_prev(down)
    corner_below, corner_above = to_next(corner), to_prev(corner)

    square, shifted = run(
        square_kernel,
        [band, band],
        [pltpu.VMEM((5 * f.group, 5 * f.group), kind)],
        94, 28, drop, density, below, above, far_below, far_above,
    )
    correction, own, partial = run(
        first_sweep_kernel,
        [columns, square_group, partial_sums],
        [whole_scratch, group_scratch, group_scratch],
        66, 20, drop, shifted, corner, up, down, from_below, from_above,
    )
    next_corner_below, next_corner_above = to_next(own), to_prev(own)
    low, high, back, forth = run(
        first_edges_kernel,
        [square_group, square_group, triangle, triangle],
        [],
        10, 12, drop, corner_below, corner_above, correction, partial,
    )
    from_above, from_below = to_prev(back), to_next(forth)
    (correction,) = run(
        correction_kernel, [columns], [whole_scratch], 38, 16, drop, shifted, low, own, high
    )
    new_low, new_high, back, forth = run(
        second_edges_kernel,
        [square_group, square_group, triangle, triangle],
        [],
        20, 12, drop, next_corner_below, next_corner_above, correction, low, high,
    )
    inverse_above, inverse_below = to_prev(back), to_next(forth)
    whole, back, forth = run(
        density_edges_kernel,
        [columns, triangle, triangle],
        [group_scratch] * 4,
        38, 20, drop, own, from_below, from_above, correction, new_low, new_high, square,
    )
    density_above, density_below = to_prev(back), to_next(forth)
    (density_own,) = run(density_own_kernel, [square_group], [], 18, 12, drop, square, whole)
    out = jax.ShapeDtypeStruct(density.shape, kind)

    def assembled(own, first, from_below, from_above):
        kernel = functools.partial(rows_kernel, f, first)
        return call(kernel, [out], [], 0, 8, drop, own, from_below, from_above)[0]

    inverse_next = assembled(whole, half, inverse_below, inverse_above)
    density_next = assembled(density_own, 0, density_below, density_above)
    return density_next, inverse_next


def solution(mesh):
    blocks = P(("grp", "row", "inner"), None, None, None)
    return jax.shard_map(
        on_device,
        mesh=mesh,
        in_specs=(blocks, blocks, P(("grp", "row", "inner"), None)),
        out_specs=(blocks, blocks),
        check_vma=False,
    )
```

time: 196 us -> 91 us (0.46)
  waiting for transfers between devices: 125 us -> 45.1 us
  matrix products: 28.2 us -> 0 us
  Pallas kernels: 0 us -> 20.7 us
  local copies, waits for them, and re-layouts: 9.93 us -> 1.22 us
  other arithmetic: 9.96 us -> 1.86 us
    ppermute x14 -> x18, waiting for transfers between devices: 125 us -> 45.1 us  [permuted(): lax.ppermute(x, RING, [(i, (i + step(i)) % size) for i in range(size)])]
    dot_general x54 -> x0, matrix products: 28.2 us -> none  [band_product(): jnp.einsum('rab,rqbc->rqac', left_band[:, slot_left], aligned, preferred_...]
    pallas_call x0 -> x11, Pallas kernels: none -> 20.7 us  [call(): pl.pallas_call(kernel, out_shape=[*outs, *[jax.ShapeDtypeStruct(a.shape,...]
    unnamed x14 -> x4, local copies, waits for them, and re-layouts: 8.31 us -> 1.22 us
    select_n x8 -> x0, other arithmetic: 5.84 us -> none  [to_band(): jnp.where(take_left, left_copy, jnp.where(take_right, right_copy, empty))]
    convert_element_type x9 -> x0, other arithmetic: 2.24 us -> none  [the longest x2 0.92 us: on_device(): inverse = (2.0 * inverse.astype(jnp.float32) - update).astype(jnp.bfloat16)]
    ppermute x14 -> x18, starting transfers between devices: 20.2 us -> 21.1 us  [permuted(): lax.ppermute(x, RING, [(i, (i + step(i)) % size) for i in range(size)])]
  transfers between devices with their start and end apart: 14 -> 18, of which waited for: 6 -> 8; matrix products, arithmetic and copies ran while one was open for 5% -> 2% of each run, Pallas kernels for 0% -> 20%
where the time goes in v2:
time: 91 us; the launch traced here: 90.8 us
  waiting for transfers between devices  45.1 us (50%)
  starting transfers between devices  21.1 us (23%)
  Pallas kernels  20.7 us (23%)
  other arithmetic  1.86 us (2%)
  local copies, waits for them, and re-layouts  1.22 us (1%)
    ppermute x18, waiting for transfers between devices, permuted(): lax.ppermute(x, RING, [(i, (i + step(i)) % size) for i in range(size)])  45.1 us
    ppermute x18, starting transfers between devices, permuted(): lax.ppermute(x, RING, [(i, (i + step(i)) % size) for i in range(size)])  21.1 us
    pallas_call x11, Pallas kernels, call(): pl.pallas_call(kernel, out_shape=[*outs, *[jax.ShapeDtypeStruct(a.shape,...  20.7 us
  transfers between devices with their start and end apart: 18, of which 8 were waited for; matrix products, arithmetic and copies ran while one was open for 2% of the time, Pallas kernels for 20%

profile of v2, /device:TPU:1, one launch (start us, length us, event | category | flops | bytes accessed | tf_op | source)
XLA Modules:
  0.0 90.8 jit_solution(17102113291445494386)
XLA Ops:
  0.6 2.7 %collective-permute-start.2 = (bf16[4,8,128,128]{3,2,1,0:T(8,128)(2,1)}, bf16[4,8,128,128]{3,2,1,0:T(8,128)(2,1)S(1)}, u32[]{:S(2)}, u32[]{:S(2)}) collective-permute-start(bf16[4,8,128,128]{3,2,1,0:T(8,128)(2,1)} %own.3), channel_id=1, source_target_pairs={{0,1},{1,2},{2,3},{3,4},{4,5},{5,6},{6,7},{7,8},{8,9},{9,10},{10,1... | collective-permute-start | bytes 3145736 | tf_op jit(solution)/shard_map/ppermute | solution.py:359
  3.3 2.9 %collective-permute-start.1 = (s32[4,8]{1,0:T(4,128)}, s32[4,8]{1,0:T(4,128)S(1)}, u32[]{:S(2)}, u32[]{:S(2)}) collective-permute-start(s32[4,8]{1,0:T(4,128)} %param.5), channel_id=1, source_target_pairs={{0,15},{1,0},{2,1},{3,2},{4,3},{5,4},{6,5},{7,6},{8,7},{9,8},{10,9... | collective-permute-start | bytes 392 | tf_op jit(solution)/shard_map/ppermute | solution.py:359
  7.1 1.2 %copy-done = bf16[4,8,128,128]{3,2,1,0:T(8,128)(2,1)S(1)} copy-done((bf16[4,8,128,128]{3,2,1,0:T(8,128)(2,1)S(1)}, bf16[4,8,128,128]{3,2,1,0:T(8,128)(2,1)}, u32[]{:S(2)}) %copy-start) | copy-done | bytes 1048600
  9.2 19.8 %collective-permute-done.1 = s32[4,8]{1,0:T(4,128)S(1)} collective-permute-done((s32[4,8]{1,0:T(4,128)}, s32[4,8]{1,0:T(4,128)S(1)}, u32[]{:S(2)}, u32[]{:S(2)}) %collective-permute-start.1) | collective-permute-done | bytes 160 | tf_op jit(solution)/shard_map/ppermute | solution.py:359
  31.3 3.0 %collective-permute-start.6 = (bf16[10,128,128]{2,1,0:T(8,128)(2,1)S(1)}, bf16[10,128,128]{2,1,0:T(8,128)(2,1)S(1)}, u32[]{:S(2)}, u32[]{:S(2)}) collective-permute-start(bf16[10,128,128]{2,1,0:T(8,128)(2,1)S(1)} %get-tuple-element.34.up), channel_id=1, source_target_pairs={{0,1},{1,2},{2,3},{3,4},{4,5},{5,6},{6,7},{7,8},{8,9},{9,10},{10,1... | collective-permute-start | bytes 983048 | tf_op jit(solution)/shard_map/ppermute | solution.py:359
  34.3 1.7 %collective-permute-start.8 = (bf16[512,512]{1,0:T(8,128)(2,1)S(1)}, bf16[512,512]{1,0:T(8,128)(2,1)S(1)}, u32[]{:S(2)}, u32[]{:S(2)}) collective-permute-start(bf16[512,512]{1,0:T(8,128)(2,1)S(1)} %get-tuple-element.33.corner), channel_id=1, source_target_pairs={{0,1},{1,2},{2,3},{3,4},{4,5},{5,6},{6,7},{7,8},{8,9},{9,10},{10,1... | collective-permute-start | bytes 1572872 | tf_op jit(solution)/shard_map/ppermute | solution.py:359
  36.0 5.0 %collective-permute-start.9 = (bf16[512,512]{1,0:T(8,128)(2,1)S(1)}, bf16[512,512]{1,0:T(8,128)(2,1)S(1)}, u32[]{:S(2)}, u32[]{:S(2)}) collective-permute-start(bf16[512,512]{1,0:T(8,128)(2,1)S(1)} %get-tuple-element.33.corner), channel_id=1, source_target_pairs={{0,15},{1,0},{2,1},{3,2},{4,3},{5,4},{6,5},{7,6},{8,7},{9,8},{10,9... | collective-permute-start | bytes 1572872 | tf_op jit(solution)/shard_map/ppermute | solution.py:359
  41.1 4.3 %shard_map.52 = (bf16[1536,1280]{1,0:T(8,128)(2,1)S(1)}, bf16[1536,1280]{1,0:T(8,128)(2,1)S(1)}) custom-call(s32[13]{0:T(128)S(1)} %pad_add_fusion.drop_ref, bf16[4,8,128,128]{3,2,1,0:T(8,128)(2,1)S(1)} %copy-done.1, bf16[4,8,128,128]{3,2,1,0:T(8,128)(2,1)S(1)} %collective-permute-done.2.below, bf16[4,8,128,128]{3,2,1,0:T(8,128)(2,1)S(1)} %collective-permute-done.3.above, ...), custom_call_target="tpu_custom_call" | custom-call | flops 3154116608 | bytes 11665408 | tf_op jit(solution)/shard_map/pallas_call | solution.py:345
  45.5 3.1 %shard_map.53 = (bf16[1536,512]{1,0:T(8,128)(2,1)S(1)}, bf16[512,512]{1,0:T(8,128)(2,1)S(1)}, f32[1024,512]{1,0:T(8,128)S(1)}) custom-call(s32[13]{0:T(128)S(1)} %pad_add_fusion.drop_ref, bf16[1536,1280]{1,0:T(8,128)(2,1)S(1)} %get-tuple-element.32.shifted, bf16[512,512]{1,0:T(8,128)(2,1)S(1)} %get-tuple-element.33.corner, ...), custom_call_target="tpu_custom_call" | custom-call | flops 2214592512 | bytes 9961472 | tf_op jit(solution)/shard_map/pallas_call | solution.py:345
  48.6 1.4 %collective-permute-start.12 = (bf16[512,512]{1,0:T(8,128)(2,1)S(1)}, bf16[512,512]{1,0:T(8,128)(2,1)S(1)}, u32[]{:S(2)}, u32[]{:S(2)}) collective-permute-start(bf16[512,512]{1,0:T(8,128)(2,1)S(1)} %get-tuple-element.36.own), channel_id=1, source_target_pairs={{0,1},{1,2},{2,3},{3,4},{4,5},{5,6},{6,7},{7,8},{8,9},{9,10},{10,1... | collective-permute-start | bytes 1572872 | tf_op jit(solution)/shard_map/ppermute | solution.py:359
  50.1 2.9 %collective-permute-done.8.corner_below = bf16[512,512]{1,0:T(8,128)(2,1)S(1)} collective-permute-done((bf16[512,512]{1,0:T(8,128)(2,1)S(1)}, bf16[512,512]{1,0:T(8,128)(2,1)S(1)}, u32[]{:S(2)}, u32[]{:S(2)}) %collective-permute-start.8) | collective-permute-done | bytes 524320 | tf_op jit(solution)/shard_map/ppermute | solution.py:359
  53.1 11.6 %collective-permute-done.9.corner_above = bf16[512,512]{1,0:T(8,128)(2,1)S(1)} collective-permute-done((bf16[512,512]{1,0:T(8,128)(2,1)S(1)}, bf16[512,512]{1,0:T(8,128)(2,1)S(1)}, u32[]{:S(2)}, u32[]{:S(2)}) %collective-permute-start.9) | collective-permute-done | bytes 524320 | tf_op jit(solution)/shard_map/ppermute | solution.py:359
  64.7 1.1 %shard_map.54 = (bf16[512,512]{1,0:T(8,128)(2,1)S(1)}, bf16[512,512]{1,0:T(8,128)(2,1)S(1)}, bf16[10,128,128]{2,1,0:T(8,128)(2,1)S(1)}, bf16[10,128,128]{2,1,0:T(8,128)(2,1)S(1)}) custom-call(s32[13]{0:T(128)S(1)} %pad_add_fusion.drop_ref, bf16[512,512]{1,0:T(8,128)(2,1)S(1)} %collective-permute-done.8.corner_below, ...), custom_call_target="tpu_custom_call" | custom-call | flops 335544320 | bytes 6422528 | tf_op jit(solution)/shard_map/pallas_call | solution.py:345
  66.4 2.0 %shard_map.55.correction = bf16[1536,512]{1,0:T(8,128)(2,1)S(1)} custom-call(s32[13]{0:T(128)S(1)} %pad_add_fusion.drop_ref, bf16[1536,1280]{1,0:T(8,128)(2,1)S(1)} %get-tuple-element.32.shifted, bf16[512,512]{1,0:T(8,128)(2,1)S(1)} %get-tuple-element.41.low, bf16[512,512]{1,0:T(8,128)(2,1)S(1)} %get-tuple-element.36.own, ...), custom_call_target="tpu_custom_call" | custom-call | flops 1275068416 | bytes 7077888 | tf_op jit(solution)/shard_map/pallas_call | solution.py:345
  68.4 1.9 %collective-permute-done.13.corner_above = bf16[512,512]{1,0:T(8,128)(2,1)S(1)} collective-permute-done((bf16[512,512]{1,0:T(8,128)(2,1)S(1)}, bf16[512,512]{1,0:T(8,128)(2,1)S(1)}, u32[]{:S(2)}, u32[]{:S(2)}) %collective-permute-start.13) | collective-permute-done | bytes 524320 | tf_op jit(solution)/shard_map/ppermute | solution.py:359
  70.3 1.5 %shard_map.56 = (bf16[512,512]{1,0:T(8,128)(2,1)S(1)}, bf16[512,512]{1,0:T(8,128)(2,1)S(1)}, bf16[10,128,128]{2,1,0:T(8,128)(2,1)S(1)}, bf16[10,128,128]{2,1,0:T(8,128)(2,1)S(1)}) custom-call(s32[13]{0:T(128)S(1)} %pad_add_fusion.drop_ref, bf16[512,512]{1,0:T(8,128)(2,1)S(1)} %collective-permute-done.12.corner_below, ...), custom_call_target="tpu_custom_call" | custom-call | flops 671088640 | bytes 5373952 | tf_op jit(solution)/shard_map/pallas_call | solution.py:345
  72.4 4.4 %collective-permute-done.10.from_below = bf16[10,128,128]{2,1,0:T(8,128)(2,1)S(1)} collective-permute-done((bf16[10,128,128]{2,1,0:T(8,128)(2,1)S(1)}, bf16[10,128,128]{2,1,0:T(8,128)(2,1)S(1)}, u32[]{:S(2)}, u32[]{:S(2)}) %collective-permute-start.10) | collective-permute-done | bytes 327712 | tf_op jit(solution)/shard_map/ppermute | solution.py:359
  76.8 2.2 %shard_map.57 = (bf16[1536,512]{1,0:T(8,128)(2,1)S(1)}, bf16[10,128,128]{2,1,0:T(8,128)(2,1)S(1)}, bf16[10,128,128]{2,1,0:T(8,128)(2,1)S(1)}) custom-call(s32[13]{0:T(128)S(1)} %pad_add_fusion.drop_ref, bf16[512,512]{1,0:T(8,128)(2,1)S(1)} %get-tuple-element.36.own, bf16[10,128,128]{2,1,0:T(8,128)(2,1)S(1)} %collective-permute-done.10.from_below, ...), custom_call_target="tpu_custom_call" | custom-call | flops 1275068416 | bytes 9961472 | tf_op jit(solution)/shard_map/pallas_call | solution.py:345
  79.1 2.5 %collective-permute-start.14 = (bf16[10,128,128]{2,1,0:T(8,128)(2,1)S(1)}, bf16[10,128,128]{2,1,0:T(8,128)(2,1)S(1)}, u32[]{:S(2)}, u32[]{:S(2)}) collective-permute-start(bf16[10,128,128]{2,1,0:T(8,128)(2,1)S(1)} %get-tuple-element.46), channel_id=1, source_target_pairs={{0,1},{1,2},{2,3},{3,4},{4,5},{5,6},{6,7},{7,8},{8,9},{9,10},{10,1... | collective-permute-start | bytes 983048 | tf_op jit(solution)/shard_map/ppermute | solution.py:359
  81.6 1.3 %shard_map.58.own = bf16[512,512]{1,0:T(8,128)(2,1)S(1)} custom-call(s32[13]{0:T(128)S(1)} %pad_add_fusion.drop_ref, bf16[1536,1280]{1,0:T(8,128)(2,1)S(1)} %get-tuple-element.31.square, bf16[1536,512]{1,0:T(8,128)(2,1)S(1)} %get-tuple-element.45.whole.own), custom_call_target="tpu_custom_call" | custom-call | flops 603979776 | bytes 6029312 | tf_op jit(solution)/shard_map/pallas_call | solution.py:345
  82.9 2.6 %collective-permute-done.17.from_above = bf16[10,128,128]{2,1,0:T(8,128)(2,1)S(1)} collective-permute-done((bf16[10,128,128]{2,1,0:T(8,128)(2,1)S(1)}, bf16[10,128,128]{2,1,0:T(8,128)(2,1)S(1)}, u32[]{:S(2)}, u32[]{:S(2)}) %collective-permute-start.17) | collective-permute-done | bytes 327712 | tf_op jit(solution)/shard_map/ppermute | solution.py:359
  85.5 1.7 %shard_map.60 = bf16[4,8,128,128]{3,2,1,0:T(8,128)(2,1)} custom-call(s32[13]{0:T(128)S(1)} %pad_add_fusion.drop_ref, bf16[1536,512]{1,0:T(8,128)(2,1)S(1)} %get-tuple-element.45.whole.own, bf16[10,128,128]{2,1,0:T(8,128)(2,1)S(1)} %collective-permute-done.16.from_below, bf16[10,128,128]{2,1,0:T(8,128)(2,1)S(1)} %collective-permute-done.17.from_above), custom_call_target="tpu_custom_call" | custom-call | bytes 3276800 | tf_op jit(solution)/shard_map/pallas_call | solution.py:345
  87.3 1.7 %collective-permute-done.15.from_above = bf16[10,128,128]{2,1,0:T(8,128)(2,1)S(1)} collective-permute-done((bf16[10,128,128]{2,1,0:T(8,128)(2,1)S(1)}, bf16[10,128,128]{2,1,0:T(8,128)(2,1)S(1)}, u32[]{:S(2)}, u32[]{:S(2)}) %collective-permute-start.15) | collective-permute-done | bytes 327712 | tf_op jit(solution)/shard_map/ppermute | solution.py:359
  89.0 1.7 %shard_map.59 = bf16[4,8,128,128]{3,2,1,0:T(8,128)(2,1)} custom-call(s32[13]{0:T(128)S(1)} %pad_add_fusion.drop_ref, bf16[512,512]{1,0:T(8,128)(2,1)S(1)} %shard_map.58.own, bf16[10,128,128]{2,1,0:T(8,128)(2,1)S(1)} %collective-permute-done.14.from_below, bf16[10,128,128]{2,1,0:T(8,128)(2,1)S(1)} %collective-permute-done.15.from_above), custom_call_target="tpu_custom_call" | custom-call | bytes 2228224 | tf_op jit(solution)/shard_map/pallas_call | solution.py:345
  (34 shorter events, 5.4 us)
Async XLA Ops:
  0.6 29.3 %collective-permute-start.2 = (bf16[4,8,128,128]{3,2,1,0:T(8,128)(2,1)}, bf16[4,8,128,128]{3,2,1,0:T(8,128)(2,1)S(1)}, u32[]{:S(2)}, u32[]{:S(2)}) collective-permute-start(bf16[4,8,128,128]{3,2,1,0:T(8,128)(2,1)} %own.3), channel_id=1, source_target_pairs={{0,1},{1,2},{2,3},{3,4},{4,5},{5,6},{6,7},{7,8},{8,9},{9,10},{10,1... | collective-permute-start | bytes 3145736 | tf_op jit(solution)/shard_map/ppermute | solution.py:359
  3.3 26.7 %collective-permute-start.3 = (bf16[4,8,128,128]{3,2,1,0:T(8,128)(2,1)}, bf16[4,8,128,128]{3,2,1,0:T(8,128)(2,1)S(1)}, u32[]{:S(2)}, u32[]{:S(2)}) collective-permute-start(bf16[4,8,128,128]{3,2,1,0:T(8,128)(2,1)} %own.3), channel_id=1, source_target_pairs={{0,15},{1,0},{2,1},{3,2},{4,3},{5,4},{6,5},{7,6},{8,7},{9,8},{10,9... | collective-permute-start | bytes 3145736 | tf_op jit(solution)/shard_map/ppermute | solution.py:359
  3.3 25.7 %collective-permute-start.1 = (s32[4,8]{1,0:T(4,128)}, s32[4,8]{1,0:T(4,128)S(1)}, u32[]{:S(2)}, u32[]{:S(2)}) collective-permute-start(s32[4,8]{1,0:T(4,128)} %param.5), channel_id=1, source_target_pairs={{0,15},{1,0},{2,1},{3,2},{4,3},{5,4},{6,5},{7,6},{8,7},{9,8},{10,9... | collective-permute-start | bytes 392 | tf_op jit(solution)/shard_map/ppermute | solution.py:359
  6.2 22.8 %collective-permute-start = (s32[4,8]{1,0:T(4,128)}, s32[4,8]{1,0:T(4,128)S(1)}, u32[]{:S(2)}, u32[]{:S(2)}) collective-permute-start(s32[4,8]{1,0:T(4,128)} %param.5), channel_id=1, source_target_pairs={{0,1},{1,2},{2,3},{3,4},{4,5},{5,6},{6,7},{7,8},{8,9},{9,10},{10,1... | collective-permute-start | bytes 392 | tf_op jit(solution)/shard_map/ppermute | solution.py:359
  7.1 1.2 %copy-start = (bf16[4,8,128,128]{3,2,1,0:T(8,128)(2,1)S(1)}, bf16[4,8,128,128]{3,2,1,0:T(8,128)(2,1)}, u32[]{:S(2)}) copy-start(bf16[4,8,128,128]{3,2,1,0:T(8,128)(2,1)} %own.2) | copy-start | bytes 3145732
  8.4 32.8 %copy-start.1 = (bf16[4,8,128,128]{3,2,1,0:T(8,128)(2,1)S(1)}, bf16[4,8,128,128]{3,2,1,0:T(8,128)(2,1)}, u32[]{:S(2)}) copy-start(bf16[4,8,128,128]{3,2,1,0:T(8,128)(2,1)} %own.3) | copy-start | bytes 3145732
  30.7 5.3 %collective-permute-start.4 = (bf16[10,128,128]{2,1,0:T(8,128)(2,1)S(1)}, bf16[10,128,128]{2,1,0:T(8,128)(2,1)S(1)}, u32[]{:S(2)}, u32[]{:S(2)}) collective-permute-start(bf16[10,128,128]{2,1,0:T(8,128)(2,1)S(1)} %get-tuple-element.29), channel_id=1, source_target_pairs={{0,1},{1,4},{2,3},{3,6},{4,5},{5,8},{6,7},{7,10},{8,9},{9,12},{10,... | collective-permute-start | bytes 983048 | tf_op jit(solution)/shard_map/ppermute | solution.py:359
  30.8 10.4 %collective-permute-start.5 = (bf16[10,128,128]{2,1,0:T(8,128)(2,1)S(1)}, bf16[10,128,128]{2,1,0:T(8,128)(2,1)S(1)}, u32[]{:S(2)}, u32[]{:S(2)}) collective-permute-start(bf16[10,128,128]{2,1,0:T(8,128)(2,1)S(1)} %get-tuple-element.30), channel_id=1, source_target_pairs={{0,13},{1,0},{2,15},{3,2},{4,1},{5,4},{6,3},{7,6},{8,5},{9,8},{10,... | collective-permute-start | bytes 983048 | tf_op jit(solution)/shard_map/ppermute | solution.py:359
  31.3 14.2 %collective-permute-start.6 = (bf16[10,128,128]{2,1,0:T(8,128)(2,1)S(1)}, bf16[10,128,128]{2,1,0:T(8,128)(2,1)S(1)}, u32[]{:S(2)}, u32[]{:S(2)}) collective-permute-start(bf16[10,128,128]{2,1,0:T(8,128)(2,1)S(1)} %get-tuple-element.34.up), channel_id=1, source_target_pairs={{0,1},{1,2},{2,3},{3,4},{4,5},{5,6},{6,7},{7,8},{8,9},{9,10},{10,1... | collective-permute-start | bytes 983048 | tf_op jit(solution)/shard_map/ppermute | solution.py:359
  34.3 11.2 %collective-permute-start.7 = (bf16[10,128,128]{2,1,0:T(8,128)(2,1)S(1)}, bf16[10,128,128]{2,1,0:T(8,128)(2,1)S(1)}, u32[]{:S(2)}, u32[]{:S(2)}) collective-permute-start(bf16[10,128,128]{2,1,0:T(8,128)(2,1)S(1)} %get-tuple-element.35.down), channel_id=1, source_target_pairs={{0,15},{1,0},{2,1},{3,2},{4,3},{5,4},{6,5},{7,6},{8,7},{9,8},{10,9... | collective-permute-start | bytes 983048 | tf_op jit(solution)/shard_map/ppermute | solution.py:359
  34.3 18.8 %collective-permute-start.8 = (bf16[512,512]{1,0:T(8,128)(2,1)S(1)}, bf16[512,512]{1,0:T(8,128)(2,1)S(1)}, u32[]{:S(2)}, u32[]{:S(2)}) collective-permute-start(bf16[512,512]{1,0:T(8,128)(2,1)S(1)} %get-tuple-element.33.corner), channel_id=1, source_target_pairs={{0,1},{1,2},{2,3},{3,4},{4,5},{5,6},{6,7},{7,8},{8,9},{9,10},{10,1... | collective-permute-start | bytes 1572872 | tf_op jit(solution)/shard_map/ppermute | solution.py:359
  36.0 28.6 %collective-permute-start.9 = (bf16[512,512]{1,0:T(8,128)(2,1)S(1)}, bf16[512,512]{1,0:T(8,128)(2,1)S(1)}, u32[]{:S(2)}, u32[]{:S(2)}) collective-permute-start(bf16[512,512]{1,0:T(8,128)(2,1)S(1)} %get-tuple-element.33.corner), channel_id=1, source_target_pairs={{0,15},{1,0},{2,1},{3,2},{4,3},{5,4},{6,5},{7,6},{8,7},{9,8},{10,9... | collective-permute-start | bytes 1572872 | tf_op jit(solution)/shard_map/ppermute | solution.py:359
  48.6 19.8 %collective-permute-start.12 = (bf16[512,512]{1,0:T(8,128)(2,1)S(1)}, bf16[512,512]{1,0:T(8,128)(2,1)S(1)}, u32[]{:S(2)}, u32[]{:S(2)}) collective-permute-start(bf16[512,512]{1,0:T(8,128)(2,1)S(1)} %get-tuple-element.36.own), channel_id=1, source_target_pairs={{0,1},{1,2},{2,3},{3,4},{4,5},{5,6},{6,7},{7,8},{8,9},{9,10},{10,1... | collective-permute-start | bytes 1572872 | tf_op jit(solution)/shard_map/ppermute | solution.py:359
  50.0 20.3 %collective-permute-start.13 = (bf16[512,512]{1,0:T(8,128)(2,1)S(1)}, bf16[512,512]{1,0:T(8,128)(2,1)S(1)}, u32[]{:S(2)}, u32[]{:S(2)}) collective-permute-start(bf16[512,512]{1,0:T(8,128)(2,1)S(1)} %get-tuple-element.36.own), channel_id=1, source_target_pairs={{0,15},{1,0},{2,1},{3,2},{4,3},{5,4},{6,5},{7,6},{8,7},{9,8},{10,9... | collective-permute-start | bytes 1572872 | tf_op jit(solution)/shard_map/ppermute | solution.py:359
  65.8 11.0 %collective-permute-start.10 = (bf16[10,128,128]{2,1,0:T(8,128)(2,1)S(1)}, bf16[10,128,128]{2,1,0:T(8,128)(2,1)S(1)}, u32[]{:S(2)}, u32[]{:S(2)}) collective-permute-start(bf16[10,128,128]{2,1,0:T(8,128)(2,1)S(1)} %get-tuple-element.39), channel_id=1, source_target_pairs={{0,1},{1,2},{2,3},{3,4},{4,5},{5,6},{6,7},{7,8},{8,9},{9,10},{10,1... | collective-permute-start | bytes 983048 | tf_op jit(solution)/shard_map/ppermute | solution.py:359
  65.9 10.9 %collective-permute-start.11 = (bf16[10,128,128]{2,1,0:T(8,128)(2,1)S(1)}, bf16[10,128,128]{2,1,0:T(8,128)(2,1)S(1)}, u32[]{:S(2)}, u32[]{:S(2)}) collective-permute-start(bf16[10,128,128]{2,1,0:T(8,128)(2,1)S(1)} %get-tuple-element.40), channel_id=1, source_target_pairs={{0,15},{1,0},{2,1},{3,2},{4,3},{5,4},{6,5},{7,6},{8,7},{9,8},{10,9... | collective-permute-start | bytes 983048 | tf_op jit(solution)/shard_map/ppermute | solution.py:359
  71.8 11.1 %collective-permute-start.16 = (bf16[10,128,128]{2,1,0:T(8,128)(2,1)S(1)}, bf16[10,128,128]{2,1,0:T(8,128)(2,1)S(1)}, u32[]{:S(2)}, u32[]{:S(2)}) collective-permute-start(bf16[10,128,128]{2,1,0:T(8,128)(2,1)S(1)} %get-tuple-element.48), channel_id=1, source_target_pairs={{0,1},{1,2},{2,3},{3,4},{4,5},{5,6},{6,7},{7,8},{8,9},{9,10},{10,1... | collective-permute-start | bytes 983048 | tf_op jit(solution)/shard_map/ppermute | solution.py:359
  71.9 13.6 %collective-permute-start.17 = (bf16[10,128,128]{2,1,0:T(8,128)(2,1)S(1)}, bf16[10,128,128]{2,1,0:T(8,128)(2,1)S(1)}, u32[]{:S(2)}, u32[]{:S(2)}) collective-permute-start(bf16[10,128,128]{2,1,0:T(8,128)(2,1)S(1)} %get-tuple-element.49), channel_id=1, source_target_pairs={{0,15},{1,0},{2,1},{3,2},{4,3},{5,4},{6,5},{7,6},{8,7},{9,8},{10,9... | collective-permute-start | bytes 983048 | tf_op jit(solution)/shard_map/ppermute | solution.py:359
  79.1 8.3 %collective-permute-start.14 = (bf16[10,128,128]{2,1,0:T(8,128)(2,1)S(1)}, bf16[10,128,128]{2,1,0:T(8,128)(2,1)S(1)}, u32[]{:S(2)}, u32[]{:S(2)}) collective-permute-start(bf16[10,128,128]{2,1,0:T(8,128)(2,1)S(1)} %get-tuple-element.46), channel_id=1, source_target_pairs={{0,1},{1,2},{2,3},{3,4},{4,5},{5,6},{6,7},{7,8},{8,9},{9,10},{10,1... | collective-permute-start | bytes 983048 | tf_op jit(solution)/shard_map/ppermute | solution.py:359
  81.6 7.5 %collective-permute-start.15 = (bf16[10,128,128]{2,1,0:T(8,128)(2,1)S(1)}, bf16[10,128,128]{2,1,0:T(8,128)(2,1)S(1)}, u32[]{:S(2)}, u32[]{:S(2)}) collective-permute-start(bf16[10,128,128]{2,1,0:T(8,128)(2,1)S(1)} %get-tuple-element.47), channel_id=1, source_target_pairs={{0,15},{1,0},{2,1},{3,2},{4,3},{5,4},{6,5},{7,6},{8,7},{9,8},{10,9... | collective-permute-start | bytes 983048 | tf_op jit(solution)/shard_map/ppermute | solution.py:359

commit v3 on v2

--- a/solution.py
+++ b/solution.py
@@ -9,6 +9,7 @@
 
 RING = ("row", "inner")
 MIB = 1024 * 1024
+NOTE = 16
 
 
 class Frame:
@@ -79,13 +80,13 @@
     for r in range(f.h):
         for c in range(f.h):
             i = index.get((r, c))
-            value = jnp.zeros((f.b, f.b), dest.dtype) if i is None else packed[i]
+            value = jnp.zeros((f.b, f.b), dest.dtype) if i is None else packed[block(f, i, 0)]
             dest[block(f, row + r, col + c)] = value
 
 
 def pack(f, source, row, packed, places):
     for i, (r, c) in enumerate(places):
-        packed[i] = source[block(f, row + r, c)]
+        packed[block(f, i, 0)] = source[block(f, row + r, c)]
 
 
 def masked(f, tile, row, col, drop_ref):
@@ -112,21 +113,26 @@
         for c in range(h):
             corner[block(f, r, c)] = stored(own, r, c - r + h, drop_ref[r])
     for i, (r, c) in enumerate(under(h)):
-        up[i] = stored(own, r, 2 * h + c - r, drop_ref[r])
+        up[block(f, i, 0)] = stored(own, r, 2 * h + c - r, drop_ref[r])
     for i, (r, c) in enumerate(over(h)):
-        down[i] = stored(own, r, c - r, drop_ref[r])
-
-
-def forward_kernel(f, drop_ref, below, above, *refs):
+        down[block(f, i, 0)] = stored(own, r, c - r, drop_ref[r])
+    line = lax.broadcasted_iota(jnp.int32, (NOTE, f.b), 0)
+    note = jnp.zeros((NOTE, f.b), jnp.float32)
+    for r in range(h):
+        note = jnp.where(line == r, drop_ref[r].astype(jnp.float32), note)
+    for packed, places in ((up, under(h)), (down, over(h))):
+        packed[pl.ds(len(places) * f.b, NOTE), :] = note.astype(packed.dtype)
+
+
+def forward_kernel(f, drop_ref, below, above, unused_in, far_up, far_down, unused_out):
     h = f.h
-    far_up, far_down = refs[3:5]
     odd = drop_ref[3 * h] == 1
 
     def send(rows, first):
         for i, (r, c) in enumerate(under(h)):
-            far_up[i] = stored(rows, r, 2 * h + c - r, drop_ref[first + r])
+            far_up[block(f, i, 0)] = stored(rows, r, 2 * h + c - r, drop_ref[first + r])
         for i, (r, c) in enumerate(over(h)):
-            far_down[i] = stored(rows, r, c - r, drop_ref[first + r])
+            far_down[block(f, i, 0)] = stored(rows, r, c - r, drop_ref[first + r])
 
     @pl.when(odd)
     def _():
@@ -325,10 +331,10 @@
         def at_offset(offset, r=r):
             col = r + offset
             if col < h:
-                return from_below[over_index[r, col]]
+                return from_below[block(f, over_index[r, col], 0)]
             if col < 2 * h:
                 return own[block(f, first + r, col - h)]
-            return from_above[under_index[r, col - 2 * h]]
+            return from_above[block(f, under_index[r, col - 2 * h], 0)]
 
         for s in range(f.k):
             out[r, s] = jnp.where(dropped <= s, at_offset(s + 1), at_offset(s))
@@ -375,22 +381,24 @@
     f = Frame(half, order)
     kind = density.dtype
     me = lax.axis_index(RING)
+    total = rows * ring
 
     def absent(columns, first):
         ids = first + jnp.arange(columns.shape[0], dtype=jnp.int32)
-        positions = jnp.mod(columns - ids[:, None] + half, rows * ring)
+        positions = columns - ids[:, None] + half
+        positions = positions + jnp.where(positions < 0, total, jnp.where(positions >= total, -total, 0))
         return width * (width + 1) // 2 - jnp.sum(positions, axis=1)
 
     below, above = to_next(density), to_prev(density)
-    near_cols = jnp.concatenate([to_next(block_cols), block_cols, to_prev(block_cols)], axis=0)
-    drop = jnp.concatenate([absent(near_cols, (me - 1) * rows), jnp.reshape(me % 2, (1,))])
     own_drop = absent(block_cols, me * rows)
 
     unit = 2 * f.t**3
     square_group = jax.ShapeDtypeStruct((f.group, f.group), kind)
     columns = jax.ShapeDtypeStruct((3 * f.group, f.group), kind)
     band = jax.ShapeDtypeStruct((3 * f.group, (2 * f.p + 1) * f.t), kind)
-    triangle = jax.ShapeDtypeStruct((half * (half + 1) // 2, order, order), kind)
+    triangle_rows = half * (half + 1) // 2 * order
+    triangle = jax.ShapeDtypeStruct((triangle_rows, order), kind)
+    noted = jax.ShapeDtypeStruct((triangle_rows + NOTE, order), kind)
     partial_sums = jax.ShapeDtypeStruct((2 * f.group, f.group), jnp.float32)
     group_scratch = pltpu.VMEM((f.group, f.group), kind)
     whole_scratch = pltpu.VMEM((3 * f.group, f.group), kind)
@@ -398,16 +406,20 @@
     def run(kernel, outs, scratch, tiles, limit, *args, **kw):
         return call(functools.partial(kernel, f), outs, scratch, tiles * unit, limit, *args, **kw)
 
-    corner, up, down = run(
-        slabs_kernel, [square_group, triangle, triangle], [], 0, 8, own_drop, inverse_start
-    )
-    far_up, far_down, corner, up, down = run(
-        forward_kernel, [triangle, triangle], [], 0, 8, drop, below, above, passed=(corner, up, down)
-    )
+    corner, up, down = run(slabs_kernel, [square_group, noted, noted], [], 0, 8, own_drop, inverse_start)
+    from_below, from_above = to_next(up), to_prev(down)
+
+    def note(slab):
+        return slab[triangle_rows : triangle_rows + rows, 0].astype(jnp.int32)
+
+    odd = jnp.reshape(me & 1, (1,))
+    drop = jnp.concatenate([note(from_below), own_drop, note(from_above), odd])
+    far_up, far_down, corner = run(
+        forward_kernel, [triangle, triangle], [], 0, 8, drop, below, above, passed=(corner,)
+    )
+    corner_below, corner_above = to_next(corner), to_prev(corner)
     far_below = permuted(far_up, lambda i: 1 + 2 * (i % 2))
     far_above = permuted(far_down, lambda i: -3 + 2 * (i % 2))
-    from_below, from_above = to_next(up), to_prev(down)
-    corner_below, corner_above = to_next(corner), to_prev(corner)
 
     square, shifted = run(
         square_kernel,

time: 91 us -> 95.4 us (1.048)
  waiting for transfers between devices: 45.1 us -> 54.4 us
  starting transfers between devices: 21.1 us -> 14.9 us
    ppermute x18 -> x16, waiting for transfers between devices: 45.1 us -> 54.4 us  [permuted(): lax.ppermute(x, RING, [(i, (i + step(i)) % size) for i in range(size)])]
    ppermute x18 -> x16, starting transfers between devices: 21.1 us -> 14.9 us  [permuted(): lax.ppermute(x, RING, [(i, (i + step(i)) % size) for i in range(size)])]
    convert_element_type x0 -> x2, other arithmetic: none -> 1.57 us  [note(): return slab[triangle_rows:triangle_rows + rows, 0].astype(jnp.int32)]
  transfers between devices with their start and end apart: 18 -> 16, of which waited for: 8 -> 9; matrix products, arithmetic and copies ran while one was open for 2% -> 3% of each run, Pallas kernels for 20% -> 20%
where the time goes in v3:
time: 95.4 us; the launch traced here: 95.1 us
  waiting for transfers between devices  54.4 us (57%)
  Pallas kernels  21.2 us (22%)
  starting transfers between devices  14.9 us (16%)
  other arithmetic  2.53 us (3%)
  local copies, waits for them, and re-layouts  1.22 us (1%)
    ppermute x16, waiting for transfers between devices, permuted(): lax.ppermute(x, RING, [(i, (i + step(i)) % size) for i in range(size)])  54.4 us
    pallas_call x11, Pallas kernels, call(): pl.pallas_call(kernel, out_shape=[*outs, *[jax.ShapeDtypeStruct(a.shape,...  21.2 us
    ppermute x16, starting transfers between devices, permuted(): lax.ppermute(x, RING, [(i, (i + step(i)) % size) for i in range(size)])  14.9 us
  transfers between devices with their start and end apart: 16, of which 9 were waited for; matrix products, arithmetic and copies ran while one was open for 3% of the time, Pallas kernels for 20%

profile of v3, /device:TPU:1, one launch (start us, length us, event | category | flops | bytes accessed | tf_op | source)
XLA Modules:
  0.0 95.1 jit_solution(11625980416910003630)
XLA Ops:
  0.6 2.7 %collective-permute-start.2 = (bf16[4,8,128,128]{3,2,1,0:T(8,128)(2,1)}, bf16[4,8,128,128]{3,2,1,0:T(8,128)(2,1)S(1)}, u32[]{:S(2)}, u32[]{:S(2)}) collective-permute-start(bf16[4,8,128,128]{3,2,1,0:T(8,128)(2,1)} %own.3), channel_id=1, source_target_pairs={{0,1},{1,2},{2,3},{3,4},{4,5},{5,6},{6,7},{7,8},{8,9},{9,10},{10,1... | collective-permute-start | bytes 3145736 | tf_op jit(solution)/shard_map/ppermute | solution.py:365
  4.2 1.2 %copy-done = bf16[4,8,128,128]{3,2,1,0:T(8,128)(2,1)S(1)} copy-done((bf16[4,8,128,128]{3,2,1,0:T(8,128)(2,1)S(1)}, bf16[4,8,128,128]{3,2,1,0:T(8,128)(2,1)}, u32[]{:S(2)}) %copy-start) | copy-done | bytes 1048600
  6.2 3.0 %collective-permute-start.1 = (bf16[1296,128]{1,0:T(8,128)(2,1)S(1)}, bf16[1296,128]{1,0:T(8,128)(2,1)}, u32[]{:S(2)}, u32[]{:S(2)}) collective-permute-start(bf16[1296,128]{1,0:T(8,128)(2,1)S(1)} %get-tuple-element.25.down), channel_id=1, source_target_pairs={{0,15},{1,0},{2,1},{3,2},{4,3},{5,4},{6,5},{7,6},{8,7},{9,8},{10,9... | collective-permute-start | bytes 995336 | tf_op jit(solution)/shard_map/ppermute | solution.py:365
  9.2 26.9 %collective-permute-done.1.from_above = bf16[1296,128]{1,0:T(8,128)(2,1)} collective-permute-done((bf16[1296,128]{1,0:T(8,128)(2,1)S(1)}, bf16[1296,128]{1,0:T(8,128)(2,1)}, u32[]{:S(2)}, u32[]{:S(2)}) %collective-permute-start.1) | collective-permute-done | bytes 331808 | tf_op jit(solution)/shard_map/ppermute | solution.py:365
  39.1 2.8 %collective-permute-start.6 = (bf16[512,512]{1,0:T(8,128)(2,1)S(1)}, bf16[512,512]{1,0:T(8,128)(2,1)S(1)}, u32[]{:S(2)}, u32[]{:S(2)}) collective-permute-start(bf16[512,512]{1,0:T(8,128)(2,1)S(1)} %get-tuple-element.31.corner), channel_id=1, source_target_pairs={{0,1},{1,2},{2,3},{3,4},{4,5},{5,6},{6,7},{7,8},{8,9},{9,10},{10,1... | collective-permute-start | bytes 1572872 | tf_op jit(solution)/shard_map/ppermute | solution.py:365
  41.9 1.1 %collective-permute-done.4.far_below = bf16[1280,128]{1,0:T(8,128)(2,1)S(1)} collective-permute-done((bf16[1280,128]{1,0:T(8,128)(2,1)S(1)}, bf16[1280,128]{1,0:T(8,128)(2,1)S(1)}, u32[]{:S(2)}, u32[]{:S(2)}) %collective-permute-start.4) | collective-permute-done | bytes 327712 | tf_op jit(solution)/shard_map/ppermute | solution.py:365
  43.0 6.0 %collective-permute-done.5.far_above = bf16[1280,128]{1,0:T(8,128)(2,1)S(1)} collective-permute-done((bf16[1280,128]{1,0:T(8,128)(2,1)S(1)}, bf16[1280,128]{1,0:T(8,128)(2,1)S(1)}, u32[]{:S(2)}, u32[]{:S(2)}) %collective-permute-start.5) | collective-permute-done | bytes 327712 | tf_op jit(solution)/shard_map/ppermute | solution.py:365
  49.0 4.3 %shard_map.52 = (bf16[1536,1280]{1,0:T(8,128)(2,1)S(1)}, bf16[1536,1280]{1,0:T(8,128)(2,1)S(1)}) custom-call(s32[13]{0:T(128)S(1)} %pad_add_fusion.drop_ref, bf16[4,8,128,128]{3,2,1,0:T(8,128)(2,1)S(1)} %copy-done.1, bf16[4,8,128,128]{3,2,1,0:T(8,128)(2,1)S(1)} %collective-permute-done.2.below, bf16[4,8,128,128]{3,2,1,0:T(8,128)(2,1)S(1)} %collective-permute-done.3.above, ...), custom_call_target="tpu_custom_call" | custom-call | flops 3154116608 | bytes 11665408 | tf_op jit(solution)/shard_map/pallas_call | solution.py:351
  53.3 3.6 %shard_map.53 = (bf16[1536,512]{1,0:T(8,128)(2,1)S(1)}, bf16[512,512]{1,0:T(8,128)(2,1)S(1)}, f32[1024,512]{1,0:T(8,128)S(1)}) custom-call(s32[13]{0:T(128)S(1)} %pad_add_fusion.drop_ref, bf16[1536,1280]{1,0:T(8,128)(2,1)S(1)} %get-tuple-element.30.shifted, bf16[512,512]{1,0:T(8,128)(2,1)S(1)} %get-tuple-element.31.corner, ...), custom_call_target="tpu_custom_call" | custom-call | flops 2214592512 | bytes 9977856 | tf_op jit(solution)/shard_map/pallas_call | solution.py:351
  57.0 1.1 %collective-permute-start.10 = (bf16[512,512]{1,0:T(8,128)(2,1)S(1)}, bf16[512,512]{1,0:T(8,128)(2,1)S(1)}, u32[]{:S(2)}, u32[]{:S(2)}) collective-permute-start(bf16[512,512]{1,0:T(8,128)(2,1)S(1)} %get-tuple-element.32.own), channel_id=1, source_target_pairs={{0,1},{1,2},{2,3},{3,4},{4,5},{5,6},{6,7},{7,8},{8,9},{9,10},{10,1... | collective-permute-start | bytes 1572872 | tf_op jit(solution)/shard_map/ppermute | solution.py:365
  58.1 1.1 %shard_map.54 = (bf16[512,512]{1,0:T(8,128)(2,1)S(1)}, bf16[512,512]{1,0:T(8,128)(2,1)S(1)}, bf16[1280,128]{1,0:T(8,128)(2,1)S(1)}, bf16[1280,128]{1,0:T(8,128)(2,1)S(1)}) custom-call(s32[13]{0:T(128)S(1)} %pad_add_fusion.drop_ref, bf16[512,512]{1,0:T(8,128)(2,1)S(1)} %collective-permute-done.6.corner_below, ...), custom_call_target="tpu_custom_call" | custom-call | flops 335544320 | bytes 6422528 | tf_op jit(solution)/shard_map/pallas_call | solution.py:351
  59.2 1.8 %collective-permute-start.8 = (bf16[1280,128]{1,0:T(8,128)(2,1)S(1)}, bf16[1280,128]{1,0:T(8,128)(2,1)S(1)}, u32[]{:S(2)}, u32[]{:S(2)}) collective-permute-start(bf16[1280,128]{1,0:T(8,128)(2,1)S(1)} %get-tuple-element.35), channel_id=1, source_target_pairs={{0,1},{1,2},{2,3},{3,4},{4,5},{5,6},{6,7},{7,8},{8,9},{9,10},{10,1... | collective-permute-start | bytes 983048 | tf_op jit(solution)/shard_map/ppermute | solution.py:365
  61.0 1.9 %collective-permute-start.9 = (bf16[1280,128]{1,0:T(8,128)(2,1)S(1)}, bf16[1280,128]{1,0:T(8,128)(2,1)S(1)}, u32[]{:S(2)}, u32[]{:S(2)}) collective-permute-start(bf16[1280,128]{1,0:T(8,128)(2,1)S(1)} %get-tuple-element.36), channel_id=1, source_target_pairs={{0,15},{1,0},{2,1},{3,2},{4,3},{5,4},{6,5},{7,6},{8,7},{9,8},{10,9... | collective-permute-start | bytes 983048 | tf_op jit(solution)/shard_map/ppermute | solution.py:365
  63.0 2.0 %shard_map.55.correction = bf16[1536,512]{1,0:T(8,128)(2,1)S(1)} custom-call(s32[13]{0:T(128)S(1)} %pad_add_fusion.drop_ref, bf16[1536,1280]{1,0:T(8,128)(2,1)S(1)} %get-tuple-element.30.shifted, bf16[512,512]{1,0:T(8,128)(2,1)S(1)} %get-tuple-element.37.low, bf16[512,512]{1,0:T(8,128)(2,1)S(1)} %get-tuple-element.32.own, ...), custom_call_target="tpu_custom_call" | custom-call | flops 1275068416 | bytes 7077888 | tf_op jit(solution)/shard_map/pallas_call | solution.py:351
  65.0 8.4 %collective-permute-done.10.corner_below = bf16[512,512]{1,0:T(8,128)(2,1)S(1)} collective-permute-done((bf16[512,512]{1,0:T(8,128)(2,1)S(1)}, bf16[512,512]{1,0:T(8,128)(2,1)S(1)}, u32[]{:S(2)}, u32[]{:S(2)}) %collective-permute-start.10) | collective-permute-done | bytes 524320 | tf_op jit(solution)/shard_map/ppermute | solution.py:365
  73.3 2.5 %collective-permute-done.11.corner_above = bf16[512,512]{1,0:T(8,128)(2,1)S(1)} collective-permute-done((bf16[512,512]{1,0:T(8,128)(2,1)S(1)}, bf16[512,512]{1,0:T(8,128)(2,1)S(1)}, u32[]{:S(2)}, u32[]{:S(2)}) %collective-permute-start.11) | collective-permute-done | bytes 524320 | tf_op jit(solution)/shard_map/ppermute | solution.py:365
  75.8 1.6 %shard_map.56 = (bf16[512,512]{1,0:T(8,128)(2,1)S(1)}, bf16[512,512]{1,0:T(8,128)(2,1)S(1)}, bf16[1280,128]{1,0:T(8,128)(2,1)S(1)}, bf16[1280,128]{1,0:T(8,128)(2,1)S(1)}) custom-call(s32[13]{0:T(128)S(1)} %pad_add_fusion.drop_ref, bf16[512,512]{1,0:T(8,128)(2,1)S(1)} %collective-permute-done.10.corner_below, ...), custom_call_target="tpu_custom_call" | custom-call | flops 671088640 | bytes 5373952 | tf_op jit(solution)/shard_map/pallas_call | solution.py:351
  77.9 4.9 %collective-permute-done.9.from_above = bf16[1280,128]{1,0:T(8,128)(2,1)S(1)} collective-permute-done((bf16[1280,128]{1,0:T(8,128)(2,1)S(1)}, bf16[1280,128]{1,0:T(8,128)(2,1)S(1)}, u32[]{:S(2)}, u32[]{:S(2)}) %collective-permute-start.9) | collective-permute-done | bytes 327712 | tf_op jit(solution)/shard_map/ppermute | solution.py:365
  82.9 2.3 %shard_map.57 = (bf16[1536,512]{1,0:T(8,128)(2,1)S(1)}, bf16[1280,128]{1,0:T(8,128)(2,1)S(1)}, bf16[1280,128]{1,0:T(8,128)(2,1)S(1)}) custom-call(s32[13]{0:T(128)S(1)} %pad_add_fusion.drop_ref, bf16[512,512]{1,0:T(8,128)(2,1)S(1)} %get-tuple-element.32.own, bf16[1280,128]{1,0:T(8,128)(2,1)S(1)} %collective-permute-done.8.from_below, ...), custom_call_target="tpu_custom_call" | custom-call | flops 1275068416 | bytes 9961472 | tf_op jit(solution)/shard_map/pallas_call | solution.py:351
  85.7 1.3 %shard_map.58.own = bf16[512,512]{1,0:T(8,128)(2,1)S(1)} custom-call(s32[13]{0:T(128)S(1)} %pad_add_fusion.drop_ref, bf16[1536,1280]{1,0:T(8,128)(2,1)S(1)} %get-tuple-element.29.square, bf16[1536,512]{1,0:T(8,128)(2,1)S(1)} %get-tuple-element.41.whole.own), custom_call_target="tpu_custom_call" | custom-call | flops 603979776 | bytes 6029312 | tf_op jit(solution)/shard_map/pallas_call | solution.py:351
  87.0 2.9 %collective-permute-done.15.from_above = bf16[1280,128]{1,0:T(8,128)(2,1)S(1)} collective-permute-done((bf16[1280,128]{1,0:T(8,128)(2,1)S(1)}, bf16[1280,128]{1,0:T(8,128)(2,1)S(1)}, u32[]{:S(2)}, u32[]{:S(2)}) %collective-permute-start.15) | collective-permute-done | bytes 327712 | tf_op jit(solution)/shard_map/ppermute | solution.py:365
  89.9 1.7 %shard_map.60 = bf16[4,8,128,128]{3,2,1,0:T(8,128)(2,1)} custom-call(s32[13]{0:T(128)S(1)} %pad_add_fusion.drop_ref, bf16[1536,512]{1,0:T(8,128)(2,1)S(1)} %get-tuple-element.41.whole.own, bf16[1280,128]{1,0:T(8,128)(2,1)S(1)} %collective-permute-done.14.from_below, bf16[1280,128]{1,0:T(8,128)(2,1)S(1)} %collective-permute-done.15.from_above), custom_call_target="tpu_custom_call" | custom-call | bytes 3276800 | tf_op jit(solution)/shard_map/pallas_call | solution.py:351
  91.6 1.1 %collective-permute-done.12.from_below = bf16[1280,128]{1,0:T(8,128)(2,1)S(1)} collective-permute-done((bf16[1280,128]{1,0:T(8,128)(2,1)S(1)}, bf16[1280,128]{1,0:T(8,128)(2,1)S(1)}, u32[]{:S(2)}, u32[]{:S(2)}) %collective-permute-start.12) | collective-permute-done | bytes 327712 | tf_op jit(solution)/shard_map/ppermute | solution.py:365
  93.4 1.7 %shard_map.59 = bf16[4,8,128,128]{3,2,1,0:T(8,128)(2,1)} custom-call(s32[13]{0:T(128)S(1)} %pad_add_fusion.drop_ref, bf16[512,512]{1,0:T(8,128)(2,1)S(1)} %shard_map.58.own, bf16[1280,128]{1,0:T(8,128)(2,1)S(1)} %collective-permute-done.12.from_below, bf16[1280,128]{1,0:T(8,128)(2,1)S(1)} %collective-permute-done.13.from_above), custom_call_target="tpu_custom_call" | custom-call | bytes 2228224 | tf_op jit(solution)/shard_map/pallas_call | solution.py:351
  (29 shorter events, 6.5 us)
Async XLA Ops:
  0.6 37.2 %collective-permute-start.2 = (bf16[4,8,128,128]{3,2,1,0:T(8,128)(2,1)}, bf16[4,8,128,128]{3,2,1,0:T(8,128)(2,1)S(1)}, u32[]{:S(2)}, u32[]{:S(2)}) collective-permute-start(bf16[4,8,128,128]{3,2,1,0:T(8,128)(2,1)} %own.3), channel_id=1, source_target_pairs={{0,1},{1,2},{2,3},{3,4},{4,5},{5,6},{6,7},{7,8},{8,9},{9,10},{10,1... | collective-permute-start | bytes 3145736 | tf_op jit(solution)/shard_map/ppermute | solution.py:365
  3.3 34.5 %collective-permute-start.3 = (bf16[4,8,128,128]{3,2,1,0:T(8,128)(2,1)}, bf16[4,8,128,128]{3,2,1,0:T(8,128)(2,1)S(1)}, u32[]{:S(2)}, u32[]{:S(2)}) collective-permute-start(bf16[4,8,128,128]{3,2,1,0:T(8,128)(2,1)} %own.3), channel_id=1, source_target_pairs={{0,15},{1,0},{2,1},{3,2},{4,3},{5,4},{6,5},{7,6},{8,7},{9,8},{10,9... | collective-permute-start | bytes 3145736 | tf_op jit(solution)/shard_map/ppermute | solution.py:365
  4.2 1.2 %copy-start = (bf16[4,8,128,128]{3,2,1,0:T(8,128)(2,1)S(1)}, bf16[4,8,128,128]{3,2,1,0:T(8,128)(2,1)}, u32[]{:S(2)}) copy-start(bf16[4,8,128,128]{3,2,1,0:T(8,128)(2,1)} %own.2) | copy-start | bytes 3145732
  6.2 29.9 %collective-permute-start.1 = (bf16[1296,128]{1,0:T(8,128)(2,1)S(1)}, bf16[1296,128]{1,0:T(8,128)(2,1)}, u32[]{:S(2)}, u32[]{:S(2)}) collective-permute-start(bf16[1296,128]{1,0:T(8,128)(2,1)S(1)} %get-tuple-element.25.down), channel_id=1, source_target_pairs={{0,15},{1,0},{2,1},{3,2},{4,3},{5,4},{6,5},{7,6},{8,7},{9,8},{10,9... | collective-permute-start | bytes 995336 | tf_op jit(solution)/shard_map/ppermute | solution.py:365
  9.2 27.7 %collective-permute-start = (bf16[1296,128]{1,0:T(8,128)(2,1)S(1)}, bf16[1296,128]{1,0:T(8,128)(2,1)}, u32[]{:S(2)}, u32[]{:S(2)}) collective-permute-start(bf16[1296,128]{1,0:T(8,128)(2,1)S(1)} %get-tuple-element.24.up), channel_id=1, source_target_pairs={{0,1},{1,2},{2,3},{3,4},{4,5},{5,6},{6,7},{7,8},{8,9},{9,10},{10,1... | collective-permute-start | bytes 995336 | tf_op jit(solution)/shard_map/ppermute | solution.py:365
  9.2 39.7 %copy-start.1 = (bf16[4,8,128,128]{3,2,1,0:T(8,128)(2,1)S(1)}, bf16[4,8,128,128]{3,2,1,0:T(8,128)(2,1)}, u32[]{:S(2)}) copy-start(bf16[4,8,128,128]{3,2,1,0:T(8,128)(2,1)} %own.3) | copy-start | bytes 3145732
  38.6 4.5 %collective-permute-start.4 = (bf16[1280,128]{1,0:T(8,128)(2,1)S(1)}, bf16[1280,128]{1,0:T(8,128)(2,1)S(1)}, u32[]{:S(2)}, u32[]{:S(2)}) collective-permute-start(bf16[1280,128]{1,0:T(8,128)(2,1)S(1)} %get-tuple-element.27), channel_id=1, source_target_pairs={{0,1},{1,4},{2,3},{3,6},{4,5},{5,8},{6,7},{7,10},{8,9},{9,12},{10,... | collective-permute-start | bytes 983048 | tf_op jit(solution)/shard_map/ppermute | solution.py:365
  38.6 10.4 %collective-permute-start.5 = (bf16[1280,128]{1,0:T(8,128)(2,1)S(1)}, bf16[1280,128]{1,0:T(8,128)(2,1)S(1)}, u32[]{:S(2)}, u32[]{:S(2)}) collective-permute-start(bf16[1280,128]{1,0:T(8,128)(2,1)S(1)} %get-tuple-element.28), channel_id=1, source_target_pairs={{0,13},{1,0},{2,15},{3,2},{4,1},{5,4},{6,3},{7,6},{8,5},{9,8},{10,... | collective-permute-start | bytes 983048 | tf_op jit(solution)/shard_map/ppermute | solution.py:365
  39.1 19.0 %collective-permute-start.6 = (bf16[512,512]{1,0:T(8,128)(2,1)S(1)}, bf16[512,512]{1,0:T(8,128)(2,1)S(1)}, u32[]{:S(2)}, u32[]{:S(2)}) collective-permute-start(bf16[512,512]{1,0:T(8,128)(2,1)S(1)} %get-tuple-element.31.corner), channel_id=1, source_target_pairs={{0,1},{1,2},{2,3},{3,4},{4,5},{5,6},{6,7},{7,8},{8,9},{9,10},{10,1... | collective-permute-start | bytes 1572872 | tf_op jit(solution)/shard_map/ppermute | solution.py:365
  41.9 16.2 %collective-permute-start.7 = (bf16[512,512]{1,0:T(8,128)(2,1)S(1)}, bf16[512,512]{1,0:T(8,128)(2,1)S(1)}, u32[]{:S(2)}, u32[]{:S(2)}) collective-permute-start(bf16[512,512]{1,0:T(8,128)(2,1)S(1)} %get-tuple-element.31.corner), channel_id=1, source_target_pairs={{0,15},{1,0},{2,1},{3,2},{4,3},{5,4},{6,5},{7,6},{8,7},{9,8},{10,9... | collective-permute-start | bytes 1572872 | tf_op jit(solution)/shard_map/ppermute | solution.py:365
  57.0 16.4 %collective-permute-start.10 = (bf16[512,512]{1,0:T(8,128)(2,1)S(1)}, bf16[512,512]{1,0:T(8,128)(2,1)S(1)}, u32[]{:S(2)}, u32[]{:S(2)}) collective-permute-start(bf16[512,512]{1,0:T(8,128)(2,1)S(1)} %get-tuple-element.32.own), channel_id=1, source_target_pairs={{0,1},{1,2},{2,3},{3,4},{4,5},{5,6},{6,7},{7,8},{8,9},{9,10},{10,1... | collective-permute-start | bytes 1572872 | tf_op jit(solution)/shard_map/ppermute | solution.py:365
  58.1 17.7 %collective-permute-start.11 = (bf16[512,512]{1,0:T(8,128)(2,1)S(1)}, bf16[512,512]{1,0:T(8,128)(2,1)S(1)}, u32[]{:S(2)}, u32[]{:S(2)}) collective-permute-start(bf16[512,512]{1,0:T(8,128)(2,1)S(1)} %get-tuple-element.32.own), channel_id=1, source_target_pairs={{0,15},{1,0},{2,1},{3,2},{4,3},{5,4},{6,5},{7,6},{8,7},{9,8},{10,9... | collective-permute-start | bytes 1572872 | tf_op jit(solution)/shard_map/ppermute | solution.py:365
  59.2 18.7 %collective-permute-start.8 = (bf16[1280,128]{1,0:T(8,128)(2,1)S(1)}, bf16[1280,128]{1,0:T(8,128)(2,1)S(1)}, u32[]{:S(2)}, u32[]{:S(2)}) collective-permute-start(bf16[1280,128]{1,0:T(8,128)(2,1)S(1)} %get-tuple-element.35), channel_id=1, source_target_pairs={{0,1},{1,2},{2,3},{3,4},{4,5},{5,6},{6,7},{7,8},{8,9},{9,10},{10,1... | collective-permute-start | bytes 983048 | tf_op jit(solution)/shard_map/ppermute | solution.py:365
  61.0 21.8 %collective-permute-start.9 = (bf16[1280,128]{1,0:T(8,128)(2,1)S(1)}, bf16[1280,128]{1,0:T(8,128)(2,1)S(1)}, u32[]{:S(2)}, u32[]{:S(2)}) collective-permute-start(bf16[1280,128]{1,0:T(8,128)(2,1)S(1)} %get-tuple-element.36), channel_id=1, source_target_pairs={{0,15},{1,0},{2,1},{3,2},{4,3},{5,4},{6,5},{7,6},{8,7},{9,8},{10,9... | collective-permute-start | bytes 983048 | tf_op jit(solution)/shard_map/ppermute | solution.py:365
  77.4 9.6 %collective-permute-start.14 = (bf16[1280,128]{1,0:T(8,128)(2,1)S(1)}, bf16[1280,128]{1,0:T(8,128)(2,1)S(1)}, u32[]{:S(2)}, u32[]{:S(2)}) collective-permute-start(bf16[1280,128]{1,0:T(8,128)(2,1)S(1)} %get-tuple-element.44), channel_id=1, source_target_pairs={{0,1},{1,2},{2,3},{3,4},{4,5},{5,6},{6,7},{7,8},{8,9},{9,10},{10,1... | collective-permute-start | bytes 983048 | tf_op jit(solution)/shard_map/ppermute | solution.py:365
  77.4 12.4 %collective-permute-start.15 = (bf16[1280,128]{1,0:T(8,128)(2,1)S(1)}, bf16[1280,128]{1,0:T(8,128)(2,1)S(1)}, u32[]{:S(2)}, u32[]{:S(2)}) collective-permute-start(bf16[1280,128]{1,0:T(8,128)(2,1)S(1)} %get-tuple-element.45), channel_id=1, source_target_pairs={{0,15},{1,0},{2,1},{3,2},{4,3},{5,4},{6,5},{7,6},{8,7},{9,8},{10,9... | collective-permute-start | bytes 983048 | tf_op jit(solution)/shard_map/ppermute | solution.py:365
  85.1 7.6 %collective-permute-start.12 = (bf16[1280,128]{1,0:T(8,128)(2,1)S(1)}, bf16[1280,128]{1,0:T(8,128)(2,1)S(1)}, u32[]{:S(2)}, u32[]{:S(2)}) collective-permute-start(bf16[1280,128]{1,0:T(8,128)(2,1)S(1)} %get-tuple-element.42), channel_id=1, source_target_pairs={{0,1},{1,2},{2,3},{3,4},{4,5},{5,6},{6,7},{7,8},{8,9},{9,10},{10,1... | collective-permute-start | bytes 983048 | tf_op jit(solution)/shard_map/ppermute | solution.py:365
  85.2 8.2 %collective-permute-start.13 = (bf16[1280,128]{1,0:T(8,128)(2,1)S(1)}, bf16[1280,128]{1,0:T(8,128)(2,1)S(1)}, u32[]{:S(2)}, u32[]{:S(2)}) collective-permute-start(bf16[1280,128]{1,0:T(8,128)(2,1)S(1)} %get-tuple-element.43), channel_id=1, source_target_pairs={{0,15},{1,0},{2,1},{3,2},{4,3},{5,4},{6,5},{7,6},{8,7},{9,8},{10,9... | collective-permute-start | bytes 983048 | tf_op jit(solution)/shard_map/ppermute | solution.py:365

commit v4 on v2

--- a/solution.py
+++ b/solution.py
@@ -51,6 +51,10 @@
     return [(r, c) for r in range(h) for c in range(r, h)]
 
 
+def full(h):
+    return [(r, c) for r in range(h) for c in range(h)]
+
+
 def at(f, row_lo, row_hi, col_lo, col_hi):
     t = f.t
     return pl.ds(row_lo * t, (row_hi - row_lo) * t), pl.ds(col_lo * t, (col_hi - col_lo) * t)
@@ -68,24 +72,11 @@
     return jnp.dot(a, b, preferred_element_type=jnp.float32)
 
 
-def stored(rows, r, offset, dropped):
-    slot = jnp.minimum(offset - (offset > dropped).astype(jnp.int32), rows.shape[1] - 1)
-    value = rows[r, slot]
+def stored(rows, r, offset, dropped, slots=None):
+    last = (rows.shape[1] if slots is None else slots) - 1
+    slot = jnp.minimum(offset - (offset > dropped).astype(jnp.int32), last)
+    value = rows[r, slot] if slots is None else rows((r, slot))
     return jnp.where(offset == dropped, jnp.zeros_like(value), value)
-
-
-def spread(f, dest, row, col, packed, places):
-    index = {place: i for i, place in enumerate(places)}
-    for r in range(f.h):
-        for c in range(f.h):
-            i = index.get((r, c))
-            value = jnp.zeros((f.b, f.b), dest.dtype) if i is None else packed[i]
-            dest[block(f, row + r, col + c)] = value
-
-
-def pack(f, source, row, packed, places):
-    for i, (r, c) in enumerate(places):
-        packed[i] = source[block(f, row + r, c)]
 
 
 def masked(f, tile, row, col, drop_ref):
@@ -106,50 +97,90 @@
     return jnp.concatenate(parts, axis=0)
 
 
-def slabs_kernel(f, drop_ref, own, corner, up, down):
+def odd_place(f, drop_ref):
+    return drop_ref[3 * f.h] == 1
+
+
+def indexed(f, ref, first=0):
+    return lambda i: ref[block(f, first + i, 0)]
+
+
+def plain(ref):
+    return lambda place: ref[place]
+
+
+def sides(f, drop_ref, mate, cross):
+    odd = odd_place(f, drop_ref)
+
+    def below(key):
+        return jnp.where(odd, mate(key), cross(key))
+
+    def above(key):
+        return jnp.where(odd, cross(key), mate(key))
+
+    return below, above
+
+
+def spread(f, dest, row, col, read, places):
+    index = {place: i for i, place in enumerate(places)}
+    for r in range(f.h):
+        for c in range(f.h):
+            i = index.get((r, c))
+            dest[block(f, row + r, col + c)] = jnp.zeros((f.b, f.b), dest.dtype) if i is None else read(i)
+
+
+def pack_edges(f, drop_ref, low, high, to_mate, to_cross):
+    odd = odd_place(f, drop_ref)
+    for i, (lower, upper) in enumerate(zip(under(f.h), over(f.h))):
+        back, forth = low[block(f, *lower)], high[block(f, *upper)]
+        to_mate[block(f, i, 0)] = jnp.where(odd, back, forth)
+        to_cross[block(f, i, 0)] = jnp.where(odd, forth, back)
+
+
+def slabs_kernel(f, drop_ref, own, corner, to_mate, to_cross):
     h = f.h
-    for r in range(h):
-        for c in range(h):
-            corner[block(f, r, c)] = stored(own, r, c - r + h, drop_ref[r])
-    for i, (r, c) in enumerate(under(h)):
-        up[i] = stored(own, r, 2 * h + c - r, drop_ref[r])
-    for i, (r, c) in enumerate(over(h)):
-        down[i] = stored(own, r, c - r, drop_ref[r])
-
-
-def forward_kernel(f, drop_ref, below, above, *refs):
+    odd = odd_place(f, drop_ref)
+    n = len(under(h))
+    for i, (lower, upper) in enumerate(zip(under(h), over(h))):
+        (r, c), (s, d) = lower, upper
+        forth = stored(own, r, 2 * h + c - r, drop_ref[h + r])
+        back = stored(own, s, d - s, drop_ref[h + s])
+        to_mate[block(f, i, 0)] = jnp.where(odd, back, forth)
+        to_cross[block(f, i, 0)] = jnp.where(odd, forth, back)
+    for i, (r, c) in enumerate(full(h)):
+        value = stored(own, r, c - r + h, drop_ref[h + r])
+        corner[block(f, i, 0)] = value
+        to_mate[block(f, n + i, 0)] = value
+        to_cross[block(f, n + i, 0)] = value
+
+
+def forward_kernel(f, drop_ref, cross, *refs):
     h = f.h
-    far_up, far_down = refs[3:5]
-    odd = drop_ref[3 * h] == 1
-
-    def send(rows, first):
-        for i, (r, c) in enumerate(under(h)):
-            far_up[i] = stored(rows, r, 2 * h + c - r, drop_ref[first + r])
-        for i, (r, c) in enumerate(over(h)):
-            far_down[i] = stored(rows, r, c - r, drop_ref[first + r])
-
-    @pl.when(odd)
-    def _():
-        send(above, 2 * h)
-
-    @pl.when(jnp.logical_not(odd))
-    def _():
-        send(below, 0)
-
-
-def square_kernel(f, drop_ref, own, below, above, far_below, far_above, square, shifted, wide):
+    odd = odd_place(f, drop_ref)
+    to_mate, to_far = refs[-2:]
+    for i, (lower, upper) in enumerate(zip(under(h), over(h))):
+        (r, c), (s, d) = lower, upper
+        forth = stored(cross, r, 2 * h + c - r, jnp.where(odd, drop_ref[2 * h + r], drop_ref[r]))
+        back = stored(cross, s, d - s, jnp.where(odd, drop_ref[2 * h + s], drop_ref[s]))
+        to_mate[block(f, i, 0)] = jnp.where(odd, back, forth)
+        to_far[block(f, i, 0)] = jnp.where(odd, forth, back)
+
+
+def square_kernel(f, drop_ref, own, mate, cross, far_mate, far_far, square, shifted, wide):
     h, p = f.h, f.p
-    for g, source in enumerate((below, own, above)):
+    below, above = sides(f, drop_ref, plain(mate), plain(cross))
+    for g, read in enumerate((below, plain(own), above)):
         for r in range(h):
             row = g * h + r
             first = 2 * (row // 2) - h
             for col in range(first, first + 2 * h + 2):
                 offset = col - row + h
                 if 0 <= offset <= f.k:
-                    value = stored(source, r, offset, drop_ref[row])
+                    value = stored(read, r, offset, drop_ref[row], f.k)
                 else:
                     value = jnp.zeros((f.b, f.b), wide.dtype)
                 wide[block(f, row + h, col + h)] = value
+    far_below, far_above = sides(f, drop_ref, indexed(f, far_mate), indexed(f, far_far))
     spread(f, wide, 0, h, far_below, under(h))
     spread(f, wide, 4 * h, 3 * h, far_above, over(h))
     unit = (
@@ -177,13 +208,14 @@
 
 
 def first_sweep_kernel(
-    f, drop_ref, shifted, corner, up, down, from_below, from_above, correction, fresh, partial, whole, before, after
+    f, drop_ref, shifted, corner, sent_mate, sent_cross, mate, cross,
+    correction, fresh, partial, whole, before, after,
 ):
     h, p = f.h, f.p
+    from_below, from_above = sides(f, drop_ref, indexed(f, mate), indexed(f, cross))
+    down, up = sides(f, drop_ref, indexed(f, sent_mate), indexed(f, sent_cross))
     spread(f, whole, 0, 0, from_below, under(h))
-    for i in range(h):
-        rows = pl.ds(i * f.b, f.b)
-        whole[pl.ds((h + i) * f.b, f.b), :] = corner[rows, :]
+    spread(f, whole, h, 0, indexed(f, corner), full(h))
     spread(f, whole, 2 * h, 0, from_above, over(h))
     spread(f, before, 0, 0, down, over(h))
     spread(f, after, 0, 0, up, under(h))
@@ -223,22 +255,27 @@
         for g, a, z in f.split(row, col):
             if g == side:
                 total = total - dot(
-                    corner[at(f, local, local + 1, a, z)], correction[at(f, g * p + a, g * p + z, c, c + 1)]
+                    corner(at(f, local, local + 1, a, z)), correction[at(f, g * p + a, g * p + z, c, c + 1)]
                 )
         total = masked(f, total, row, col, drop_ref)
         dest[at(f, local, local + 1, c, c + 1)] = total.astype(dest.dtype)
 
 
-def first_edges_kernel(f, drop_ref, corner_below, corner_above, correction, partial, low, high, to_prev, to_next):
+def first_edges_kernel(
+    f, drop_ref, mate, cross, correction, partial, low, high, to_mate, to_cross, before, after
+):
     p = f.p
+    n = len(under(f.h))
+    below, above = sides(f, drop_ref, indexed(f, mate, n), indexed(f, cross, n))
+    spread(f, before, 0, 0, below, full(f.h))
+    spread(f, after, 0, 0, above, full(f.h))
 
     def start(row, col):
         place = row if row < p else row - p
         return partial[at(f, place, place + 1, col - p, col - p + 1)]
 
-    edges(f, drop_ref, corner_below, corner_above, correction, start, low, high)
-    pack(f, low, 0, to_prev, under(f.h))
-    pack(f, high, 0, to_next, over(f.h))
+    edges(f, drop_ref, plain(before), plain(after), correction, start, low, high)
+    pack_edges(f, drop_ref, low, high, to_mate, to_cross)
 
 
 def gather(f, whole, low, own, high):
@@ -256,7 +293,7 @@
 
 
 def second_edges_kernel(
-    f, drop_ref, corner_below, corner_above, correction, low, high, new_low, new_high, to_prev, to_next
+    f, drop_ref, mate, cross, correction, low, high, new_low, new_high, to_mate, to_cross
 ):
     p = f.p
 
@@ -271,18 +308,19 @@
                 )
         return total
 
-    edges(f, drop_ref, corner_below, corner_above, correction, start, new_low, new_high)
-    pack(f, new_low, 0, to_prev, under(f.h))
-    pack(f, new_high, 0, to_next, over(f.h))
+    below, above = sides(f, drop_ref, plain(mate), plain(cross))
+    edges(f, drop_ref, below, above, correction, start, new_low, new_high)
+    pack_edges(f, drop_ref, new_low, new_high, to_mate, to_cross)
 
 
 def density_edges_kernel(
-    f, drop_ref, own, from_below, from_above, correction, new_low, new_high, square, whole, to_prev, to_next,
+    f, drop_ref, own, mate, cross, correction, new_low, new_high, square, whole, to_mate, to_cross,
     before, after, low, high,
 ):
     h, p = f.h, f.p
-    spread(f, before, 0, 0, from_below, over(h))
-    spread(f, after, 0, 0, from_above, under(h))
+    below, above = sides(f, drop_ref, indexed(f, mate), indexed(f, cross))
+    spread(f, before, 0, 0, below, over(h))
+    spread(f, after, 0, 0, above, under(h))
     for row, col in f.tiles(f.own_pairs):
         if row not in f.own_pairs:
             continue
@@ -303,8 +341,7 @@
         total = masked(f, right_tile(f, square, whole, row, col), row, col, drop_ref)
         dest, local = (low, row) if row < p else (high, row - 2 * p)
         dest[at(f, local, local + 1, col - p, col - p + 1)] = total.astype(dest.dtype)
-    pack(f, low, 0, to_prev, under(h))
-    pack(f, high, 0, to_next, over(h))
+    pack_edges(f, drop_ref, low, high, to_mate, to_cross)
 
 
 def density_own_kernel(f, drop_ref, square, whole, out):
@@ -315,8 +352,9 @@
             out[at(f, row - p, row - p + 1, col - p, col - p + 1)] = total.astype(out.dtype)
 
 
-def rows_kernel(f, first, drop_ref, own, from_below, from_above, out):
+def rows_kernel(f, first, drop_ref, own, mate, cross, out):
     h = f.h
+    below, above = sides(f, drop_ref, indexed(f, mate), indexed(f, cross))
     over_index = {place: i for i, place in enumerate(over(h))}
     under_index = {place: i for i, place in enumerate(under(h))}
     for r in range(h):
@@ -325,10 +363,10 @@
         def at_offset(offset, r=r):
             col = r + offset
             if col < h:
-                return from_below[over_index[r, col]]
+                return below(over_index[r, col])
             if col < 2 * h:
                 return own[block(f, first + r, col - h)]
-            return from_above[under_index[r, col - 2 * h]]
+            return above(under_index[r, col - 2 * h])
 
         for s in range(f.k):
             out[r, s] = jnp.where(dropped <= s, at_offset(s + 1), at_offset(s))
@@ -339,58 +377,72 @@
 ANY = pl.BlockSpec(memory_space=pl.ANY)
 
 
-def call(kernel, outs, scratch, flops, limit, drop, *args, passed=()):
+def call(kernel, outs, scratch, flops, limit, drop, *args, passed=(), after=()):
     moved = sum(a.size * a.dtype.itemsize for a in args) + sum(s.size * s.dtype.itemsize for s in outs)
     n = len(args)
     return pl.pallas_call(
         kernel,
         out_shape=[*outs, *[jax.ShapeDtypeStruct(a.shape, a.dtype) for a in passed]],
-        in_specs=[SMEM] + [VMEM] * n + [ANY] * len(passed),
+        in_specs=[SMEM] + [VMEM] * n + [ANY] * (len(passed) + len(after)),
         out_specs=[VMEM] * len(outs) + [ANY] * len(passed),
         scratch_shapes=scratch,
         input_output_aliases={1 + n + i: len(outs) + i for i in range(len(passed))},
         compiler_params=pltpu.CompilerParams(vmem_limit_bytes=limit * MIB),
         cost_estimate=pl.CostEstimate(flops=flops, bytes_accessed=moved, transcendentals=0),
-    )(drop, *args, *passed)
-
-
-def permuted(x, step):
+    )(drop, *args, *passed, *after)
+
+
+def routed(x, step):
     size = lax.axis_size(RING)
-    return lax.ppermute(x, RING, [(i, (i + step(i)) % size) for i in range(size)])
-
-
-def to_next(x):
-    return permuted(x, lambda i: 1)
-
-
-def to_prev(x):
-    return permuted(x, lambda i: -1)
+    return lax.ppermute(x, RING, [(i, (i + step(i)) % size) for i in range(size) if step(i)])
 
 
 def on_device(density, inverse_start, block_cols):
     rows, width, order, _ = density.shape
     half = width // 2
     ring = lax.axis_size(RING)
+    total = rows * ring
     assert rows == half and half % 2 == 0 and ring % 2 == 0
     f = Frame(half, order)
     kind = density.dtype
     me = lax.axis_index(RING)
+    odd = (me & 1) == 1
+
+    def mate_step(i):
+        return 1 - 2 * (i % 2)
+
+    def cross_step(i):
+        return 2 * (i % 2) - 1
+
+    def to_mate(x):
+        return routed(x, mate_step)
+
+    def to_cross(x):
+        return routed(x, cross_step)
 
     def absent(columns, first):
         ids = first + jnp.arange(columns.shape[0], dtype=jnp.int32)
-        positions = jnp.mod(columns - ids[:, None] + half, rows * ring)
+        positions = columns - ids[:, None] + half
+        positions = positions + jnp.where(positions < 0, total, jnp.where(positions >= total, -total, 0))
         return width * (width + 1) // 2 - jnp.sum(positions, axis=1)
 
-    below, above = to_next(density), to_prev(density)
-    near_cols = jnp.concatenate([to_next(block_cols), block_cols, to_prev(block_cols)], axis=0)
-    drop = jnp.concatenate([absent(near_cols, (me - 1) * rows), jnp.reshape(me % 2, (1,))])
-    own_drop = absent(block_cols, me * rows)
+    mate_cols, cross_cols = to_mate(block_cols), to_cross(block_cols)
+    density_mate, density_cross = to_mate(density), to_cross(density)
+
+    marks = jnp.reshape(me & 1, (1,))
+    near_cols = jnp.concatenate(
+        [jnp.where(odd, mate_cols, cross_cols), block_cols, jnp.where(odd, cross_cols, mate_cols)], axis=0
+    )
+    drop = jnp.concatenate([absent(near_cols, (me - 1) * rows), marks])
 
     unit = 2 * f.t**3
+    count = half * (half + 1) // 2
     square_group = jax.ShapeDtypeStruct((f.group, f.group), kind)
     columns = jax.ShapeDtypeStruct((3 * f.group, f.group), kind)
     band = jax.ShapeDtypeStruct((3 * f.group, (2 * f.p + 1) * f.t), kind)
-    triangle = jax.ShapeDtypeStruct((half * (half + 1) // 2, order, order), kind)
+    triangle = jax.ShapeDtypeStruct((count * order, order), kind)
+    listed = jax.ShapeDtypeStruct((half * half * order, order), kind)
+    both = jax.ShapeDtypeStruct(((count + half * half) * order, order), kind)
     partial_sums = jax.ShapeDtypeStruct((2 * f.group, f.group), jnp.float32)
     group_scratch = pltpu.VMEM((f.group, f.group), kind)
     whole_scratch = pltpu.VMEM((3 * f.group, f.group), kind)
@@ -398,63 +450,61 @@
     def run(kernel, outs, scratch, tiles, limit, *args, **kw):
         return call(functools.partial(kernel, f), outs, scratch, tiles * unit, limit, *args, **kw)
 
-    corner, up, down = run(
-        slabs_kernel, [square_group, triangle, triangle], [], 0, 8, own_drop, inverse_start
-    )
-    far_up, far_down, corner, up, down = run(
-        forward_kernel, [triangle, triangle], [], 0, 8, drop, below, above, passed=(corner, up, down)
-    )
-    far_below = permuted(far_up, lambda i: 1 + 2 * (i % 2))
-    far_above = permuted(far_down, lambda i: -3 + 2 * (i % 2))
-    from_below, from_above = to_next(up), to_prev(down)
-    corner_below, corner_above = to_next(corner), to_prev(corner)
+    corner, slab_mate, slab_cross = run(
+        slabs_kernel, [listed, both, both], [], 0, 12, drop, inverse_start
+    )
+    from_mate, from_cross = to_mate(slab_mate), to_cross(slab_cross)
+    forward_mate, forward_far = run(
+        forward_kernel, [triangle, triangle], [], 0, 8, drop, density_cross, after=(density_mate, from_mate)
+    )
+    far_mate = to_mate(forward_mate)
+    far_far = routed(forward_far, lambda i: 3 * cross_step(i))
 
     square, shifted = run(
         square_kernel,
         [band, band],
         [pltpu.VMEM((5 * f.group, 5 * f.group), kind)],
-        94, 28, drop, density, below, above, far_below, far_above,
+        94, 28, drop, density, density_mate, density_cross, far_mate, far_far,
     )
     correction, own, partial = run(
         first_sweep_kernel,
         [columns, square_group, partial_sums],
         [whole_scratch, group_scratch, group_scratch],
-        66, 20, drop, shifted, corner, up, down, from_below, from_above,
-    )
-    next_corner_below, next_corner_above = to_next(own), to_prev(own)
-    low, high, back, forth = run(
+        66, 24, drop, shifted, corner, slab_mate, slab_cross, from_mate, from_cross,
+    )
+    corner_mate, corner_cross = to_mate(own), to_cross(own)
+    low, high, edge_mate, edge_cross = run(
         first_edges_kernel,
         [square_group, square_group, triangle, triangle],
-        [],
-        10, 12, drop, corner_below, corner_above, correction, partial,
-    )
-    from_above, from_below = to_prev(back), to_next(forth)
+        [group_scratch] * 2,
+        10, 16, drop, from_mate, from_cross, correction, partial,
+    )
+    edge_mate, edge_cross = to_mate(edge_mate), to_cross(edge_cross)
     (correction,) = run(
         correction_kernel, [columns], [whole_scratch], 38, 16, drop, shifted, low, own, high
     )
-    new_low, new_high, back, forth = run(
+    new_low, new_high, inverse_mate, inverse_cross = run(
         second_edges_kernel,
         [square_group, square_group, triangle, triangle],
         [],
-        20, 12, drop, next_corner_below, next_corner_above, correction, low, high,
-    )
-    inverse_above, inverse_below = to_prev(back), to_next(forth)
-    whole, back, forth = run(
+        20, 12, drop, corner_mate, corner_cross, correction, low, high,
+    )
+    inverse_mate, inverse_cross = to_mate(inverse_mate), to_cross(inverse_cross)
+    whole, rim_mate, rim_cross = run(
         density_edges_kernel,
         [columns, triangle, triangle],
         [group_scratch] * 4,
-        38, 20, drop, own, from_below, from_above, correction, new_low, new_high, square,
-    )
-    density_above, density_below = to_prev(back), to_next(forth)
+        38, 20, drop, own, edge_mate, edge_cross, correction, new_low, new_high, square,
+    )
+    rim_mate, rim_cross = to_mate(rim_mate), to_cross(rim_cross)
     (density_own,) = run(density_own_kernel, [square_group], [], 18, 12, drop, square, whole)
     out = jax.ShapeDtypeStruct(density.shape, kind)
 
-    def assembled(own, first, from_below, from_above):
-        kernel = functools.partial(rows_kernel, f, first)
-        return call(kernel, [out], [], 0, 8, drop, own, from_below, from_above)[0]
-
-    inverse_next = assembled(whole, half, inverse_below, inverse_above)
-    density_next = assembled(density_own, 0, density_below, density_above)
+    def assembled(own, first, mate, cross):
+        return call(functools.partial(rows_kernel, f, first), [out], [], 0, 8, drop, own, mate, cross)[0]
+
+    inverse_next = assembled(whole, half, inverse_mate, inverse_cross)
+    density_next = assembled(density_own, 0, rim_mate, rim_cross)
     return density_next, inverse_next
 
 

time: 91 us -> 98.8 us (1.086)
  waiting for transfers between devices: 45.1 us -> 62.2 us
  starting transfers between devices: 21.1 us -> 12.1 us
    ppermute x18 -> x16, waiting for transfers between devices: 45.1 us -> 62.2 us  [routed(): lax.ppermute(x, RING, [(i, (i + step(i)) % size) for i in range(size) if...]
    ppermute x18 -> x16, starting transfers between devices: 21.1 us -> 12.1 us  [routed(): lax.ppermute(x, RING, [(i, (i + step(i)) % size) for i in range(size) if...]
  transfers between devices with their start and end apart: 18 -> 16, of which waited for: 8 -> 8; matrix products, arithmetic and copies ran while one was open for 2% -> 1% of each run, Pallas kernels for 20% -> 17%
where the time goes in v4:
time: 98.8 us; the launch traced here: 98.6 us
  waiting for transfers between devices  62.2 us (63%)
  Pallas kernels  21.4 us (22%)
  starting transfers between devices  12.1 us (12%)
  local copies, waits for them, and re-layouts  1.23 us (1%)
    ppermute x16, waiting for transfers between devices, routed(): lax.ppermute(x, RING, [(i, (i + step(i)) % size) for i in range(size) if...  62.2 us
    pallas_call x11, Pallas kernels, call(): pl.pallas_call(kernel, out_shape=[*outs, *[jax.ShapeDtypeStruct(a.shape,...  21.4 us
    ppermute x16, starting transfers between devices, routed(): lax.ppermute(x, RING, [(i, (i + step(i)) % size) for i in range(size) if...  12.1 us
  transfers between devices with their start and end apart: 16, of which 8 were waited for; matrix products, arithmetic and copies ran while one was open for 1% of the time, Pallas kernels for 17%

profile of v4, /device:TPU:1, one launch (start us, length us, event | category | flops | bytes accessed | tf_op | source)
XLA Modules:
  0.0 98.6 jit_solution(92553846297885603)
XLA Ops:
  0.8 2.6 %collective-permute-start.1 = (s32[4,8]{1,0:T(4,128)}, s32[4,8]{1,0:T(4,128)S(1)}, u32[]{:S(2)}, u32[]{:S(2)}) collective-permute-start(s32[4,8]{1,0:T(4,128)} %param.5), channel_id=1, source_target_pairs={{0,15},{1,2},{2,1},{3,4},{4,3},{5,6},{6,5},{7,8},{8,7},{9,10},{10,... | collective-permute-start | bytes 392 | tf_op jit(solution)/shard_map/ppermute | solution.py:397
  3.4 3.5 %collective-permute-start.2 = (bf16[4,8,128,128]{3,2,1,0:T(8,128)(2,1)}, bf16[4,8,128,128]{3,2,1,0:T(8,128)(2,1)S(1)}, u32[]{:S(2)}, u32[]{:S(2)}) collective-permute-start(bf16[4,8,128,128]{3,2,1,0:T(8,128)(2,1)} %own.3), channel_id=1, source_target_pairs={{0,1},{1,0},{2,3},{3,2},{4,5},{5,4},{6,7},{7,6},{8,9},{9,8},{10,11... | collective-permute-start | bytes 3145736 | tf_op jit(solution)/shard_map/ppermute | solution.py:397
  7.8 1.2 %copy-done = bf16[4,8,128,128]{3,2,1,0:T(8,128)(2,1)S(1)} copy-done((bf16[4,8,128,128]{3,2,1,0:T(8,128)(2,1)S(1)}, bf16[4,8,128,128]{3,2,1,0:T(8,128)(2,1)}, u32[]{:S(2)}) %copy-start) | copy-done | bytes 1048600
  9.1 0.9 shard_map.50
  10.0 1.6 %collective-permute-start.4 = (bf16[3328,128]{1,0:T(8,128)(2,1)S(1)}, bf16[3328,128]{1,0:T(8,128)(2,1)S(1)}, u32[]{:S(2)}, u32[]{:S(2)}) collective-permute-start(bf16[3328,128]{1,0:T(8,128)(2,1)S(1)} %get-tuple-element.23.sent_mate), channel_id=1, source_target_pairs={{0,1},{1,0},{2,3},{3,2},{4,5},{5,4},{6,7},{7,6},{8,9},{9,8},{10,11... | collective-permute-start | bytes 2555912 | tf_op jit(solution)/shard_map/ppermute | solution.py:397
  11.9 1.7 %collective-permute-done.4.refs_1_.mate = bf16[3328,128]{1,0:T(8,128)(2,1)S(1)} collective-permute-done((bf16[3328,128]{1,0:T(8,128)(2,1)S(1)}, bf16[3328,128]{1,0:T(8,128)(2,1)S(1)}, u32[]{:S(2)}, u32[]{:S(2)}) %collective-permute-start.4) | collective-permute-done | bytes 852000 | tf_op jit(solution)/shard_map/ppermute | solution.py:397
  13.6 28.1 %collective-permute-done.3.cross = bf16[4,8,128,128]{3,2,1,0:T(8,128)(2,1)S(1)} collective-permute-done((bf16[4,8,128,128]{3,2,1,0:T(8,128)(2,1)}, bf16[4,8,128,128]{3,2,1,0:T(8,128)(2,1)S(1)}, u32[]{:S(2)}, u32[]{:S(2)}) %collective-permute-start.3) | collective-permute-done | bytes 1048608 | tf_op jit(solution)/shard_map/ppermute | solution.py:397
  42.5 1.5 %collective-permute-done.5.far_mate = bf16[1280,128]{1,0:T(8,128)(2,1)S(1)} collective-permute-done((bf16[1280,128]{1,0:T(8,128)(2,1)S(1)}, bf16[1280,128]{1,0:T(8,128)(2,1)S(1)}, u32[]{:S(2)}, u32[]{:S(2)}) %collective-permute-start.5) | collective-permute-done | bytes 327712 | tf_op jit(solution)/shard_map/ppermute | solution.py:397
  44.1 8.5 %collective-permute-done.6.far_far = bf16[1280,128]{1,0:T(8,128)(2,1)S(1)} collective-permute-done((bf16[1280,128]{1,0:T(8,128)(2,1)S(1)}, bf16[1280,128]{1,0:T(8,128)(2,1)S(1)}, u32[]{:S(2)}, u32[]{:S(2)}) %collective-permute-start.6) | collective-permute-done | bytes 327712 | tf_op jit(solution)/shard_map/ppermute | solution.py:397
  52.5 4.6 %shard_map.52 = (bf16[1536,1280]{1,0:T(8,128)(2,1)S(1)}, bf16[1536,1280]{1,0:T(8,128)(2,1)S(1)}) custom-call(s32[13]{0:T(128)S(1)} %pad_add_fusion.drop_ref, bf16[4,8,128,128]{3,2,1,0:T(8,128)(2,1)S(1)} %copy-done.1, bf16[4,8,128,128]{3,2,1,0:T(8,128)(2,1)S(1)} %collective-permute-done.2.refs_0_.mate, ...), custom_call_target="tpu_custom_call" | custom-call | flops 3154116608 | bytes 11665408 | tf_op jit(solution)/shard_map/pallas_call | solution.py:383
  57.2 3.2 %shard_map.53 = (bf16[1536,512]{1,0:T(8,128)(2,1)S(1)}, bf16[512,512]{1,0:T(8,128)(2,1)S(1)}, f32[1024,512]{1,0:T(8,128)S(1)}) custom-call(s32[13]{0:T(128)S(1)} %pad_add_fusion.drop_ref, bf16[1536,1280]{1,0:T(8,128)(2,1)S(1)} %get-tuple-element.27.shifted, bf16[2048,128]{1,0:T(8,128)(2,1)S(1)} %get-tuple-element.28.corner, ...), custom_call_target="tpu_custom_call" | custom-call | flops 2214592512 | bytes 12058624 | tf_op jit(solution)/shard_map/pallas_call | solution.py:383
  60.3 0.9 collective-permute-start.11
  61.7 1.3 %shard_map.54 = (bf16[512,512]{1,0:T(8,128)(2,1)S(1)}, bf16[512,512]{1,0:T(8,128)(2,1)S(1)}, bf16[1280,128]{1,0:T(8,128)(2,1)S(1)}, bf16[1280,128]{1,0:T(8,128)(2,1)S(1)}) custom-call(s32[13]{0:T(128)S(1)} %pad_add_fusion.drop_ref, bf16[3328,128]{1,0:T(8,128)(2,1)S(1)} %collective-permute-done.4.refs_1_.mate, ...), custom_call_target="tpu_custom_call" | custom-call | flops 335544320 | bytes 7077888 | tf_op jit(solution)/shard_map/pallas_call | solution.py:383
  63.1 0.9 collective-permute-start.9
  64.1 2.0 %shard_map.55.correction = bf16[1536,512]{1,0:T(8,128)(2,1)S(1)} custom-call(s32[13]{0:T(128)S(1)} %pad_add_fusion.drop_ref, bf16[1536,1280]{1,0:T(8,128)(2,1)S(1)} %get-tuple-element.27.shifted, bf16[512,512]{1,0:T(8,128)(2,1)S(1)} %get-tuple-element.35.low, bf16[512,512]{1,0:T(8,128)(2,1)S(1)} %get-tuple-element.30.own, ...), custom_call_target="tpu_custom_call" | custom-call | flops 1275068416 | bytes 7077888 | tf_op jit(solution)/shard_map/pallas_call | solution.py:383
  66.1 12.1 %collective-permute-done.11.cross = bf16[512,512]{1,0:T(8,128)(2,1)S(1)} collective-permute-done((bf16[512,512]{1,0:T(8,128)(2,1)S(1)}, bf16[512,512]{1,0:T(8,128)(2,1)S(1)}, u32[]{:S(2)}, u32[]{:S(2)}) %collective-permute-start.11) | collective-permute-done | bytes 524320 | tf_op jit(solution)/shard_map/ppermute | solution.py:397
  78.1 1.5 %shard_map.56 = (bf16[512,512]{1,0:T(8,128)(2,1)S(1)}, bf16[512,512]{1,0:T(8,128)(2,1)S(1)}, bf16[1280,128]{1,0:T(8,128)(2,1)S(1)}, bf16[1280,128]{1,0:T(8,128)(2,1)S(1)}) custom-call(s32[13]{0:T(128)S(1)} %pad_add_fusion.drop_ref, bf16[512,512]{1,0:T(8,128)(2,1)S(1)} %collective-permute-done.10.mate, bf16[512,512]{1,0:T(8,128)(2,1)S(1)} %collective-permute-done.11.cross, ...), custom_call_target="tpu_custom_call" | custom-call | flops 671088640 | bytes 5373952 | tf_op jit(solution)/shard_map/pallas_call | solution.py:383
  80.4 1.3 %collective-permute-done.9.cross = bf16[1280,128]{1,0:T(8,128)(2,1)S(1)} collective-permute-done((bf16[1280,128]{1,0:T(8,128)(2,1)S(1)}, bf16[1280,128]{1,0:T(8,128)(2,1)S(1)}, u32[]{:S(2)}, u32[]{:S(2)}) %collective-permute-start.9) | collective-permute-done | bytes 327712 | tf_op jit(solution)/shard_map/ppermute | solution.py:397
  81.6 2.3 %shard_map.57 = (bf16[1536,512]{1,0:T(8,128)(2,1)S(1)}, bf16[1280,128]{1,0:T(8,128)(2,1)S(1)}, bf16[1280,128]{1,0:T(8,128)(2,1)S(1)}) custom-call(s32[13]{0:T(128)S(1)} %pad_add_fusion.drop_ref, bf16[512,512]{1,0:T(8,128)(2,1)S(1)} %get-tuple-element.30.own, bf16[1280,128]{1,0:T(8,128)(2,1)S(1)} %collective-permute-done.8.mate, ...), custom_call_target="tpu_custom_call" | custom-call | flops 1275068416 | bytes 9961472 | tf_op jit(solution)/shard_map/pallas_call | solution.py:383
  84.6 1.3 %shard_map.58.own = bf16[512,512]{1,0:T(8,128)(2,1)S(1)} custom-call(s32[13]{0:T(128)S(1)} %pad_add_fusion.drop_ref, bf16[1536,1280]{1,0:T(8,128)(2,1)S(1)} %get-tuple-element.26.square, bf16[1536,512]{1,0:T(8,128)(2,1)S(1)} %get-tuple-element.39.whole.own), custom_call_target="tpu_custom_call" | custom-call | flops 603979776 | bytes 6029312 | tf_op jit(solution)/shard_map/pallas_call | solution.py:383
  86.0 7.3 %collective-permute-done.15.cross = bf16[1280,128]{1,0:T(8,128)(2,1)S(1)} collective-permute-done((bf16[1280,128]{1,0:T(8,128)(2,1)S(1)}, bf16[1280,128]{1,0:T(8,128)(2,1)S(1)}, u32[]{:S(2)}, u32[]{:S(2)}) %collective-permute-start.15) | collective-permute-done | bytes 327712 | tf_op jit(solution)/shard_map/ppermute | solution.py:397
  93.3 1.8 %shard_map.60 = bf16[4,8,128,128]{3,2,1,0:T(8,128)(2,1)} custom-call(s32[13]{0:T(128)S(1)} %pad_add_fusion.drop_ref, bf16[1536,512]{1,0:T(8,128)(2,1)S(1)} %get-tuple-element.39.whole.own, bf16[1280,128]{1,0:T(8,128)(2,1)S(1)} %collective-permute-done.14.mate, bf16[1280,128]{1,0:T(8,128)(2,1)S(1)} %collective-permute-done.15.cross), custom_call_target="tpu_custom_call" | custom-call | bytes 3276800 | tf_op jit(solution)/shard_map/pallas_call | solution.py:383
  95.1 1.7 %collective-permute-done.13.cross = bf16[1280,128]{1,0:T(8,128)(2,1)S(1)} collective-permute-done((bf16[1280,128]{1,0:T(8,128)(2,1)S(1)}, bf16[1280,128]{1,0:T(8,128)(2,1)S(1)}, u32[]{:S(2)}, u32[]{:S(2)}) %collective-permute-start.13) | collective-permute-done | bytes 327712 | tf_op jit(solution)/shard_map/ppermute | solution.py:397
  96.8 1.8 %shard_map.59 = bf16[4,8,128,128]{3,2,1,0:T(8,128)(2,1)} custom-call(s32[13]{0:T(128)S(1)} %pad_add_fusion.drop_ref, bf16[512,512]{1,0:T(8,128)(2,1)S(1)} %shard_map.58.own, bf16[1280,128]{1,0:T(8,128)(2,1)S(1)} %collective-permute-done.12.mate, bf16[1280,128]{1,0:T(8,128)(2,1)S(1)} %collective-permute-done.13.cross), custom_call_target="tpu_custom_call" | custom-call | bytes 2228224 | tf_op jit(solution)/shard_map/pallas_call | solution.py:383
  (28 shorter events, 4.3 us)
Async XLA Ops:
  0.6 6.2 %collective-permute-start = (s32[4,8]{1,0:T(4,128)}, s32[4,8]{1,0:T(4,128)S(1)}, u32[]{:S(2)}, u32[]{:S(2)}) collective-permute-start(s32[4,8]{1,0:T(4,128)} %param.5), channel_id=1, source_target_pairs={{0,1},{1,0},{2,3},{3,2},{4,5},{5,4},{6,7},{7,6},{8,9},{9,8},{10,11... | collective-permute-start | bytes 392 | tf_op jit(solution)/shard_map/ppermute | solution.py:397
  0.8 6.1 %collective-permute-start.1 = (s32[4,8]{1,0:T(4,128)}, s32[4,8]{1,0:T(4,128)S(1)}, u32[]{:S(2)}, u32[]{:S(2)}) collective-permute-start(s32[4,8]{1,0:T(4,128)} %param.5), channel_id=1, source_target_pairs={{0,15},{1,2},{2,1},{3,4},{4,3},{5,6},{6,5},{7,8},{8,7},{9,10},{10,... | collective-permute-start | bytes 392 | tf_op jit(solution)/shard_map/ppermute | solution.py:397
  3.4 10.2 %collective-permute-start.2 = (bf16[4,8,128,128]{3,2,1,0:T(8,128)(2,1)}, bf16[4,8,128,128]{3,2,1,0:T(8,128)(2,1)S(1)}, u32[]{:S(2)}, u32[]{:S(2)}) collective-permute-start(bf16[4,8,128,128]{3,2,1,0:T(8,128)(2,1)} %own.3), channel_id=1, source_target_pairs={{0,1},{1,0},{2,3},{3,2},{4,5},{5,4},{6,7},{7,6},{8,9},{9,8},{10,11... | collective-permute-start | bytes 3145736 | tf_op jit(solution)/shard_map/ppermute | solution.py:397
  6.8 34.8 %collective-permute-start.3 = (bf16[4,8,128,128]{3,2,1,0:T(8,128)(2,1)}, bf16[4,8,128,128]{3,2,1,0:T(8,128)(2,1)S(1)}, u32[]{:S(2)}, u32[]{:S(2)}) collective-permute-start(bf16[4,8,128,128]{3,2,1,0:T(8,128)(2,1)} %own.3), channel_id=1, source_target_pairs={{0,15},{1,2},{2,1},{3,4},{4,3},{5,6},{6,5},{7,8},{8,7},{9,10},{10,... | collective-permute-start | bytes 3145736 | tf_op jit(solution)/shard_map/ppermute | solution.py:397
  7.8 1.2 %copy-start = (bf16[4,8,128,128]{3,2,1,0:T(8,128)(2,1)S(1)}, bf16[4,8,128,128]{3,2,1,0:T(8,128)(2,1)}, u32[]{:S(2)}) copy-start(bf16[4,8,128,128]{3,2,1,0:T(8,128)(2,1)} %own.2) | copy-start | bytes 3145732
  9.1 43.5 %copy-start.1 = (bf16[4,8,128,128]{3,2,1,0:T(8,128)(2,1)S(1)}, bf16[4,8,128,128]{3,2,1,0:T(8,128)(2,1)}, u32[]{:S(2)}) copy-start(bf16[4,8,128,128]{3,2,1,0:T(8,128)(2,1)} %own.3) | copy-start | bytes 3145732
  10.0 3.6 %collective-permute-start.4 = (bf16[3328,128]{1,0:T(8,128)(2,1)S(1)}, bf16[3328,128]{1,0:T(8,128)(2,1)S(1)}, u32[]{:S(2)}, u32[]{:S(2)}) collective-permute-start(bf16[3328,128]{1,0:T(8,128)(2,1)S(1)} %get-tuple-element.23.sent_mate), channel_id=1, source_target_pairs={{0,1},{1,0},{2,3},{3,2},{4,5},{5,4},{6,7},{7,6},{8,9},{9,8},{10,11... | collective-permute-start | bytes 2555912 | tf_op jit(solution)/shard_map/ppermute | solution.py:397
  11.6 45.6 %collective-permute-start.7 = (bf16[3328,128]{1,0:T(8,128)(2,1)S(1)}, bf16[3328,128]{1,0:T(8,128)(2,1)S(1)}, u32[]{:S(2)}, u32[]{:S(2)}) collective-permute-start(bf16[3328,128]{1,0:T(8,128)(2,1)S(1)} %get-tuple-element.29.sent_cross), channel_id=1, source_target_pairs={{0,15},{1,2},{2,1},{3,4},{4,3},{5,6},{6,5},{7,8},{8,7},{9,10},{10,... | collective-permute-start | bytes 2555912 | tf_op jit(solution)/shard_map/ppermute | solution.py:397
  42.4 1.7 %collective-permute-start.5 = (bf16[1280,128]{1,0:T(8,128)(2,1)S(1)}, bf16[1280,128]{1,0:T(8,128)(2,1)S(1)}, u32[]{:S(2)}, u32[]{:S(2)}) collective-permute-start(bf16[1280,128]{1,0:T(8,128)(2,1)S(1)} %get-tuple-element.24), channel_id=1, source_target_pairs={{0,1},{1,0},{2,3},{3,2},{4,5},{5,4},{6,7},{7,6},{8,9},{9,8},{10,11... | collective-permute-start | bytes 983048 | tf_op jit(solution)/shard_map/ppermute | solution.py:397
  42.4 10.1 %collective-permute-start.6 = (bf16[1280,128]{1,0:T(8,128)(2,1)S(1)}, bf16[1280,128]{1,0:T(8,128)(2,1)S(1)}, u32[]{:S(2)}, u32[]{:S(2)}) collective-permute-start(bf16[1280,128]{1,0:T(8,128)(2,1)S(1)} %get-tuple-element.25), channel_id=1, source_target_pairs={{0,13},{1,4},{2,15},{3,6},{4,1},{5,8},{6,3},{7,10},{8,5},{9,12},{1... | collective-permute-start | bytes 983048 | tf_op jit(solution)/shard_map/ppermute | solution.py:397
  60.3 17.8 %collective-permute-start.11 = (bf16[512,512]{1,0:T(8,128)(2,1)S(1)}, bf16[512,512]{1,0:T(8,128)(2,1)S(1)}, u32[]{:S(2)}, u32[]{:S(2)}) collective-permute-start(bf16[512,512]{1,0:T(8,128)(2,1)S(1)} %get-tuple-element.30.own), channel_id=1, source_target_pairs={{0,15},{1,2},{2,1},{3,4},{4,3},{5,6},{6,5},{7,8},{8,7},{9,10},{10,... | collective-permute-start | bytes 1572872 | tf_op jit(solution)/shard_map/ppermute | solution.py:397
  61.2 16.9 %collective-permute-start.10 = (bf16[512,512]{1,0:T(8,128)(2,1)S(1)}, bf16[512,512]{1,0:T(8,128)(2,1)S(1)}, u32[]{:S(2)}, u32[]{:S(2)}) collective-permute-start(bf16[512,512]{1,0:T(8,128)(2,1)S(1)} %get-tuple-element.30.own), channel_id=1, source_target_pairs={{0,1},{1,0},{2,3},{3,2},{4,5},{5,4},{6,7},{7,6},{8,9},{9,8},{10,11... | collective-permute-start | bytes 1572872 | tf_op jit(solution)/shard_map/ppermute | solution.py:397
  63.0 17.3 %collective-permute-start.8 = (bf16[1280,128]{1,0:T(8,128)(2,1)S(1)}, bf16[1280,128]{1,0:T(8,128)(2,1)S(1)}, u32[]{:S(2)}, u32[]{:S(2)}) collective-permute-start(bf16[1280,128]{1,0:T(8,128)(2,1)S(1)} %get-tuple-element.33), channel_id=1, source_target_pairs={{0,1},{1,0},{2,3},{3,2},{4,5},{5,4},{6,7},{7,6},{8,9},{9,8},{10,11... | collective-permute-start | bytes 983048 | tf_op jit(solution)/shard_map/ppermute | solution.py:397
  63.1 18.5 %collective-permute-start.9 = (bf16[1280,128]{1,0:T(8,128)(2,1)S(1)}, bf16[1280,128]{1,0:T(8,128)(2,1)S(1)}, u32[]{:S(2)}, u32[]{:S(2)}) collective-permute-start(bf16[1280,128]{1,0:T(8,128)(2,1)S(1)} %get-tuple-element.34), channel_id=1, source_target_pairs={{0,15},{1,2},{2,1},{3,4},{4,3},{5,6},{6,5},{7,8},{8,7},{9,10},{10,... | collective-permute-start | bytes 983048 | tf_op jit(solution)/shard_map/ppermute | solution.py:397
  79.6 6.3 %collective-permute-start.14 = (bf16[1280,128]{1,0:T(8,128)(2,1)S(1)}, bf16[1280,128]{1,0:T(8,128)(2,1)S(1)}, u32[]{:S(2)}, u32[]{:S(2)}) collective-permute-start(bf16[1280,128]{1,0:T(8,128)(2,1)S(1)} %get-tuple-element.42), channel_id=1, source_target_pairs={{0,1},{1,0},{2,3},{3,2},{4,5},{5,4},{6,7},{7,6},{8,9},{9,8},{10,11... | collective-permute-start | bytes 983048 | tf_op jit(solution)/shard_map/ppermute | solution.py:397
  79.7 13.6 %collective-permute-start.15 = (bf16[1280,128]{1,0:T(8,128)(2,1)S(1)}, bf16[1280,128]{1,0:T(8,128)(2,1)S(1)}, u32[]{:S(2)}, u32[]{:S(2)}) collective-permute-start(bf16[1280,128]{1,0:T(8,128)(2,1)S(1)} %get-tuple-element.43), channel_id=1, source_target_pairs={{0,15},{1,2},{2,1},{3,4},{4,3},{5,6},{6,5},{7,8},{8,7},{9,10},{10,... | collective-permute-start | bytes 983048 | tf_op jit(solution)/shard_map/ppermute | solution.py:397
  83.9 11.2 %collective-permute-start.12 = (bf16[1280,128]{1,0:T(8,128)(2,1)S(1)}, bf16[1280,128]{1,0:T(8,128)(2,1)S(1)}, u32[]{:S(2)}, u32[]{:S(2)}) collective-permute-start(bf16[1280,128]{1,0:T(8,128)(2,1)S(1)} %get-tuple-element.40), channel_id=1, source_target_pairs={{0,1},{1,0},{2,3},{3,2},{4,5},{5,4},{6,7},{7,6},{8,9},{9,8},{10,11... | collective-permute-start | bytes 983048 | tf_op jit(solution)/shard_map/ppermute | solution.py:397
  84.0 12.8 %collective-permute-start.13 = (bf16[1280,128]{1,0:T(8,128)(2,1)S(1)}, bf16[1280,128]{1,0:T(8,128)(2,1)S(1)}, u32[]{:S(2)}, u32[]{:S(2)}) collective-permute-start(bf16[1280,128]{1,0:T(8,128)(2,1)S(1)} %get-tuple-element.41), channel_id=1, source_target_pairs={{0,15},{1,2},{2,1},{3,4},{4,3},{5,6},{6,5},{7,8},{8,7},{9,10},{10,... | collective-permute-start | bytes 983048 | tf_op jit(solution)/shard_map/ppermute | solution.py:397

commit v5 on v4

--- a/solution.py
+++ b/solution.py
@@ -139,25 +139,24 @@
 
 def slabs_kernel(f, drop_ref, own, corner, to_mate, to_cross):
     h = f.h
-    odd = odd_place(f, drop_ref)
+    odd = drop_ref[h] == 1
     n = len(under(h))
     for i, (lower, upper) in enumerate(zip(under(h), over(h))):
         (r, c), (s, d) = lower, upper
-        forth = stored(own, r, 2 * h + c - r, drop_ref[h + r])
-        back = stored(own, s, d - s, drop_ref[h + s])
+        forth = stored(own, r, 2 * h + c - r, drop_ref[r])
+        back = stored(own, s, d - s, drop_ref[s])
         to_mate[block(f, i, 0)] = jnp.where(odd, back, forth)
         to_cross[block(f, i, 0)] = jnp.where(odd, forth, back)
     for i, (r, c) in enumerate(full(h)):
-        value = stored(own, r, c - r + h, drop_ref[h + r])
+        value = stored(own, r, c - r + h, drop_ref[r])
         corner[block(f, i, 0)] = value
         to_mate[block(f, n + i, 0)] = value
-        to_cross[block(f, n + i, 0)] = value
 
 
 def forward_kernel(f, drop_ref, cross, *refs):
     h = f.h
     odd = odd_place(f, drop_ref)
-    to_mate, to_far = refs[-2:]
+    to_mate, to_far = refs[-4:-2]
     for i, (lower, upper) in enumerate(zip(under(h), over(h))):
         (r, c), (s, d) = lower, upper
         forth = stored(cross, r, 2 * h + c - r, jnp.where(odd, drop_ref[2 * h + r], drop_ref[r]))
@@ -266,7 +265,7 @@
 ):
     p = f.p
     n = len(under(f.h))
-    below, above = sides(f, drop_ref, indexed(f, mate, n), indexed(f, cross, n))
+    below, above = sides(f, drop_ref, indexed(f, mate, n), indexed(f, cross))
     spread(f, before, 0, 0, below, full(f.h))
     spread(f, after, 0, 0, above, full(f.h))
 
@@ -420,20 +419,17 @@
     def to_cross(x):
         return routed(x, cross_step)
 
-    def absent(columns, first):
-        ids = first + jnp.arange(columns.shape[0], dtype=jnp.int32)
-        positions = columns - ids[:, None] + half
-        positions = positions + jnp.where(positions < 0, total, jnp.where(positions >= total, -total, 0))
-        return width * (width + 1) // 2 - jnp.sum(positions, axis=1)
-
-    mate_cols, cross_cols = to_mate(block_cols), to_cross(block_cols)
+    positions = block_cols - (me * rows + jnp.arange(rows, dtype=jnp.int32))[:, None] + half
+    positions = positions + jnp.where(positions < 0, total, jnp.where(positions >= total, -total, 0))
+    own_drop = width * (width + 1) // 2 - jnp.sum(positions, axis=1)
+
     density_mate, density_cross = to_mate(density), to_cross(density)
-
-    marks = jnp.reshape(me & 1, (1,))
-    near_cols = jnp.concatenate(
-        [jnp.where(odd, mate_cols, cross_cols), block_cols, jnp.where(odd, cross_cols, mate_cols)], axis=0
-    )
-    drop = jnp.concatenate([absent(near_cols, (me - 1) * rows), marks])
+    mate_drop, cross_drop = to_mate(own_drop), to_cross(own_drop)
+    mark = jnp.reshape(me & 1, (1,))
+    start_drop = jnp.concatenate([own_drop, mark])
+    drop = jnp.concatenate(
+        [jnp.where(odd, mate_drop, cross_drop), own_drop, jnp.where(odd, cross_drop, mate_drop), mark]
+    )
 
     unit = 2 * f.t**3
     count = half * (half + 1) // 2
@@ -450,15 +446,17 @@
     def run(kernel, outs, scratch, tiles, limit, *args, **kw):
         return call(functools.partial(kernel, f), outs, scratch, tiles * unit, limit, *args, **kw)
 
-    corner, slab_mate, slab_cross = run(
-        slabs_kernel, [listed, both, both], [], 0, 12, drop, inverse_start
-    )
-    from_mate, from_cross = to_mate(slab_mate), to_cross(slab_cross)
-    forward_mate, forward_far = run(
-        forward_kernel, [triangle, triangle], [], 0, 8, drop, density_cross, after=(density_mate, from_mate)
+    corner, slab_mate, triangle_cross = run(
+        slabs_kernel, [listed, both, triangle], [], 0, 12, start_drop, inverse_start
+    )
+    from_mate = to_mate(slab_mate)
+    forward_mate, forward_far, triangle_cross, corner = run(
+        forward_kernel, [triangle, triangle], [], 0, 8, drop, density_cross,
+        passed=(triangle_cross, corner), after=(density_mate,),
     )
     far_mate = to_mate(forward_mate)
     far_far = routed(forward_far, lambda i: 3 * cross_step(i))
+    cross_triangle, cross_corner = to_cross(triangle_cross), to_cross(corner)
 
     square, shifted = run(
         square_kernel,
@@ -470,14 +468,14 @@
         first_sweep_kernel,
         [columns, square_group, partial_sums],
         [whole_scratch, group_scratch, group_scratch],
-        66, 24, drop, shifted, corner, slab_mate, slab_cross, from_mate, from_cross,
+        66, 24, drop, shifted, corner, slab_mate, triangle_cross, from_mate, cross_triangle,
     )
     corner_mate, corner_cross = to_mate(own), to_cross(own)
     low, high, edge_mate, edge_cross = run(
         first_edges_kernel,
         [square_group, square_group, triangle, triangle],
         [group_scratch] * 2,
-        10, 16, drop, from_mate, from_cross, correction, partial,
+        10, 16, drop, from_mate, cross_corner, correction, partial,
     )
     edge_mate, edge_cross = to_mate(edge_mate), to_cross(edge_cross)
     (correction,) = run(

time: 98.8 us -> 94.6 us (0.957)
  waiting for transfers between devices: 62.2 us -> 39.7 us
  starting transfers between devices: 12.1 us -> 28.1 us
  Pallas kernels: 21.4 us -> 23.1 us
    ppermute x16 -> x17, waiting for transfers between devices: 62.2 us -> 39.7 us  [routed(): lax.ppermute(x, RING, [(i, (i + step(i)) % size) for i in range(size) if...]
    ppermute x16 -> x17, starting transfers between devices: 12.1 us -> 28.1 us  [routed(): lax.ppermute(x, RING, [(i, (i + step(i)) % size) for i in range(size) if...]
    pallas_call x11, Pallas kernels: 21.4 us -> 23.1 us  [call(): pl.pallas_call(kernel, out_shape=[*outs, *[jax.ShapeDtypeStruct(a.shape,...]
  transfers between devices with their start and end apart: 16 -> 17, of which waited for: 8 -> 6; matrix products, arithmetic and copies ran while one was open for 1% -> 1% of each run, Pallas kernels for 17% -> 23%
where the time goes in v5:
time: 94.6 us; the launch traced here: 93.9 us
  waiting for transfers between devices  39.7 us (42%)
  starting transfers between devices  28.1 us (30%)
  Pallas kernels  23.1 us (24%)
  local copies, waits for them, and re-layouts  1.23 us (1%)
  other arithmetic  1.03 us (1%)
    ppermute x17, waiting for transfers between devices, routed(): lax.ppermute(x, RING, [(i, (i + step(i)) % size) for i in range(size) if...  39.7 us
    ppermute x17, starting transfers between devices, routed(): lax.ppermute(x, RING, [(i, (i + step(i)) % size) for i in range(size) if...  28.1 us
    pallas_call x11, Pallas kernels, call(): pl.pallas_call(kernel, out_shape=[*outs, *[jax.ShapeDtypeStruct(a.shape,...  23.1 us
  transfers between devices with their start and end apart: 17, of which 6 were waited for; matrix products, arithmetic and copies ran while one was open for 1% of the time, Pallas kernels for 23%

profile of v5, /device:TPU:1, one launch (start us, length us, event | category | flops | bytes accessed | tf_op | source)
XLA Modules:
  0.0 93.9 jit_solution(17451295081597453511)
XLA Ops:
  0.8 2.6 %collective-permute-start.3 = (bf16[4,8,128,128]{3,2,1,0:T(8,128)(2,1)}, bf16[4,8,128,128]{3,2,1,0:T(8,128)(2,1)S(1)}, u32[]{:S(2)}, u32[]{:S(2)}) collective-permute-start(bf16[4,8,128,128]{3,2,1,0:T(8,128)(2,1)} %own.3), channel_id=1, source_target_pairs={{0,15},{1,2},{2,1},{3,4},{4,3},{5,6},{6,5},{7,8},{8,7},{9,10},{10,... | collective-permute-start | bytes 3145736 | tf_op jit(solution)/shard_map/ppermute | solution.py:396
  4.3 3.5 %collective-permute-start = (s32[4]{0:T(128)S(1)}, s32[4]{0:T(128)S(1)}, u32[]{:S(2)}, u32[]{:S(2)}) collective-permute-start(s32[4]{0:T(128)S(1)} %broadcast_subtract_fusion), channel_id=1, source_target_pairs={{0,1},{1,0},{2,3},{3,2},{4,5},{5,4},{6,7},{7,6},{8,9},{9,8},{10,11... | collective-permute-start | bytes 56 | tf_op jit(solution)/shard_map/ppermute | solution.py:396
  7.9 1.2 %copy-done = bf16[4,8,128,128]{3,2,1,0:T(8,128)(2,1)S(1)} copy-done((bf16[4,8,128,128]{3,2,1,0:T(8,128)(2,1)S(1)}, bf16[4,8,128,128]{3,2,1,0:T(8,128)(2,1)}, u32[]{:S(2)}) %copy-start) | copy-done | bytes 1048600
  9.1 1.9 %shard_map.50 = (bf16[2048,128]{1,0:T(8,128)(2,1)S(1)}, bf16[3328,128]{1,0:T(8,128)(2,1)}, bf16[1280,128]{1,0:T(8,128)(2,1)}) custom-call(s32[5]{0:T(128)S(1)} %pad_add_fusion.1.drop_ref, bf16[4,8,128,128]{3,2,1,0:T(8,128)(2,1)S(1)} %copy-done), custom_call_target="tpu_custom_call" | custom-call | bytes 2752512 | tf_op jit(solution)/shard_map/pallas_call | solution.py:382
  11.6 15.7 %collective-permute-done.1 = s32[4]{0:T(128)S(1)} collective-permute-done((s32[4]{0:T(128)S(1)}, s32[4]{0:T(128)S(1)}, u32[]{:S(2)}, u32[]{:S(2)}) %collective-permute-start.1) | collective-permute-done | bytes 48 | tf_op jit(solution)/shard_map/ppermute | solution.py:396
  28.3 2.2 %collective-permute-start.5 = (bf16[1280,128]{1,0:T(8,128)(2,1)S(1)}, bf16[1280,128]{1,0:T(8,128)(2,1)S(1)}, u32[]{:S(2)}, u32[]{:S(2)}) collective-permute-start(bf16[1280,128]{1,0:T(8,128)(2,1)S(1)} %get-tuple-element.28), channel_id=1, source_target_pairs={{0,13},{1,4},{2,15},{3,6},{4,1},{5,8},{6,3},{7,10},{8,5},{9,12},{1... | collective-permute-start | bytes 983048 | tf_op jit(solution)/shard_map/ppermute | solution.py:396
  30.5 3.2 %collective-permute-start.7 = (bf16[1280,128]{1,0:T(8,128)(2,1)}, bf16[1280,128]{1,0:T(8,128)(2,1)S(1)}, u32[]{:S(2)}, u32[]{:S(2)}) collective-permute-start(bf16[1280,128]{1,0:T(8,128)(2,1)} %get-tuple-element.33.sent_cross), channel_id=1, source_target_pairs={{0,15},{1,2},{2,1},{3,4},{4,3},{5,6},{6,5},{7,8},{8,7},{9,10},{10,... | collective-permute-start | bytes 983048 | tf_op jit(solution)/shard_map/ppermute | solution.py:396
  33.7 4.6 %collective-permute-done.5.far_far = bf16[1280,128]{1,0:T(8,128)(2,1)S(1)} collective-permute-done((bf16[1280,128]{1,0:T(8,128)(2,1)S(1)}, bf16[1280,128]{1,0:T(8,128)(2,1)S(1)}, u32[]{:S(2)}, u32[]{:S(2)}) %collective-permute-start.5) | collective-permute-done | bytes 327712 | tf_op jit(solution)/shard_map/ppermute | solution.py:396
  38.4 4.7 %shard_map.52 = (bf16[1536,1280]{1,0:T(8,128)(2,1)S(1)}, bf16[1536,1280]{1,0:T(8,128)(2,1)S(1)}) custom-call(s32[13]{0:T(128)S(1)} %pad_add_fusion.drop_ref, bf16[4,8,128,128]{3,2,1,0:T(8,128)(2,1)S(1)} %copy-done.1, bf16[4,8,128,128]{3,2,1,0:T(8,128)(2,1)S(1)} %collective-permute-done.2.refs_2_.mate, ...), custom_call_target="tpu_custom_call" | custom-call | flops 3154116608 | bytes 11665408 | tf_op jit(solution)/shard_map/pallas_call | solution.py:382
  43.1 3.8 %shard_map.53 = (bf16[1536,512]{1,0:T(8,128)(2,1)S(1)}, bf16[512,512]{1,0:T(8,128)(2,1)S(1)}, f32[1024,512]{1,0:T(8,128)S(1)}) custom-call(s32[13]{0:T(128)S(1)} %pad_add_fusion.drop_ref, bf16[1536,1280]{1,0:T(8,128)(2,1)S(1)} %get-tuple-element.30.shifted, bf16[2048,128]{1,0:T(8,128)(2,1)S(1)} %get-tuple-element.31.corner, ...), custom_call_target="tpu_custom_call" | custom-call | flops 2214592512 | bytes 11010048 | tf_op jit(solution)/shard_map/pallas_call | solution.py:382
  46.9 2.4 %collective-permute-start.11 = (bf16[512,512]{1,0:T(8,128)(2,1)S(1)}, bf16[512,512]{1,0:T(8,128)(2,1)S(1)}, u32[]{:S(2)}, u32[]{:S(2)}) collective-permute-start(bf16[512,512]{1,0:T(8,128)(2,1)S(1)} %get-tuple-element.34.own), channel_id=1, source_target_pairs={{0,1},{1,0},{2,3},{3,2},{4,5},{5,4},{6,7},{7,6},{8,9},{9,8},{10,11... | collective-permute-start | bytes 1572872 | tf_op jit(solution)/shard_map/ppermute | solution.py:396
  49.3 1.2 %collective-permute-start.12 = (bf16[512,512]{1,0:T(8,128)(2,1)S(1)}, bf16[512,512]{1,0:T(8,128)(2,1)S(1)}, u32[]{:S(2)}, u32[]{:S(2)}) collective-permute-start(bf16[512,512]{1,0:T(8,128)(2,1)S(1)} %get-tuple-element.34.own), channel_id=1, source_target_pairs={{0,15},{1,2},{2,1},{3,4},{4,3},{5,6},{6,5},{7,8},{8,7},{9,10},{10,... | collective-permute-start | bytes 1572872 | tf_op jit(solution)/shard_map/ppermute | solution.py:396
  50.6 2.9 %collective-permute-done.8.cross = bf16[2048,128]{1,0:T(8,128)(2,1)S(1)} collective-permute-done((bf16[2048,128]{1,0:T(8,128)(2,1)S(1)}, bf16[2048,128]{1,0:T(8,128)(2,1)S(1)}, u32[]{:S(2)}, u32[]{:S(2)}) %collective-permute-start.8) | collective-permute-done | bytes 524320 | tf_op jit(solution)/shard_map/ppermute | solution.py:396
  53.4 1.3 %shard_map.54 = (bf16[512,512]{1,0:T(8,128)(2,1)S(1)}, bf16[512,512]{1,0:T(8,128)(2,1)S(1)}, bf16[1280,128]{1,0:T(8,128)(2,1)S(1)}, bf16[1280,128]{1,0:T(8,128)(2,1)S(1)}) custom-call(s32[13]{0:T(128)S(1)} %pad_add_fusion.drop_ref, bf16[3328,128]{1,0:T(8,128)(2,1)S(1)} %collective-permute-done.6.mate, bf16[2048,128]{1,0:T(8,128)(2,1)S(1)} %collective-permute-done.8.cross, ...), custom_call_target="tpu_custom_call" | custom-call | flops 335544320 | bytes 6750208 | tf_op jit(solution)/shard_map/pallas_call | solution.py:382
  56.7 2.0 %shard_map.55.correction = bf16[1536,512]{1,0:T(8,128)(2,1)S(1)} custom-call(s32[13]{0:T(128)S(1)} %pad_add_fusion.drop_ref, bf16[1536,1280]{1,0:T(8,128)(2,1)S(1)} %get-tuple-element.30.shifted, bf16[512,512]{1,0:T(8,128)(2,1)S(1)} %get-tuple-element.39.low, bf16[512,512]{1,0:T(8,128)(2,1)S(1)} %get-tuple-element.34.own, ...), custom_call_target="tpu_custom_call" | custom-call | flops 1275068416 | bytes 7077888 | tf_op jit(solution)/shard_map/pallas_call | solution.py:382
  58.7 9.5 %collective-permute-done.12.cross = bf16[512,512]{1,0:T(8,128)(2,1)S(1)} collective-permute-done((bf16[512,512]{1,0:T(8,128)(2,1)S(1)}, bf16[512,512]{1,0:T(8,128)(2,1)S(1)}, u32[]{:S(2)}, u32[]{:S(2)}) %collective-permute-start.12) | collective-permute-done | bytes 524320 | tf_op jit(solution)/shard_map/ppermute | solution.py:396
  68.2 1.5 %shard_map.56 = (bf16[512,512]{1,0:T(8,128)(2,1)S(1)}, bf16[512,512]{1,0:T(8,128)(2,1)S(1)}, bf16[1280,128]{1,0:T(8,128)(2,1)S(1)}, bf16[1280,128]{1,0:T(8,128)(2,1)S(1)}) custom-call(s32[13]{0:T(128)S(1)} %pad_add_fusion.drop_ref, bf16[512,512]{1,0:T(8,128)(2,1)S(1)} %collective-permute-done.11.mate, bf16[512,512]{1,0:T(8,128)(2,1)S(1)} %collective-permute-done.12.cross, ...), custom_call_target="tpu_custom_call" | custom-call | flops 671088640 | bytes 5373952 | tf_op jit(solution)/shard_map/pallas_call | solution.py:382
  69.8 1.8 %collective-permute-start.16 = (bf16[1280,128]{1,0:T(8,128)(2,1)S(1)}, bf16[1280,128]{1,0:T(8,128)(2,1)S(1)}, u32[]{:S(2)}, u32[]{:S(2)}) collective-permute-start(bf16[1280,128]{1,0:T(8,128)(2,1)S(1)} %get-tuple-element.47), channel_id=1, source_target_pairs={{0,15},{1,2},{2,1},{3,4},{4,3},{5,6},{6,5},{7,8},{8,7},{9,10},{10,... | collective-permute-start | bytes 983048 | tf_op jit(solution)/shard_map/ppermute | solution.py:396
  71.7 2.3 %shard_map.57 = (bf16[1536,512]{1,0:T(8,128)(2,1)S(1)}, bf16[1280,128]{1,0:T(8,128)(2,1)S(1)}, bf16[1280,128]{1,0:T(8,128)(2,1)S(1)}) custom-call(s32[13]{0:T(128)S(1)} %pad_add_fusion.drop_ref, bf16[512,512]{1,0:T(8,128)(2,1)S(1)} %get-tuple-element.34.own, bf16[1280,128]{1,0:T(8,128)(2,1)S(1)} %collective-permute-done.9.mate, ...), custom_call_target="tpu_custom_call" | custom-call | flops 1275068416 | bytes 9961472 | tf_op jit(solution)/shard_map/pallas_call | solution.py:382
  74.0 8.2 %collective-permute-start.13 = (bf16[1280,128]{1,0:T(8,128)(2,1)S(1)}, bf16[1280,128]{1,0:T(8,128)(2,1)S(1)}, u32[]{:S(2)}, u32[]{:S(2)}) collective-permute-start(bf16[1280,128]{1,0:T(8,128)(2,1)S(1)} %get-tuple-element.44), channel_id=1, source_target_pairs={{0,1},{1,0},{2,3},{3,2},{4,5},{5,4},{6,7},{7,6},{8,9},{9,8},{10,11... | collective-permute-start | bytes 983048 | tf_op jit(solution)/shard_map/ppermute | solution.py:396
  82.1 1.3 %shard_map.58.own = bf16[512,512]{1,0:T(8,128)(2,1)S(1)} custom-call(s32[13]{0:T(128)S(1)} %pad_add_fusion.drop_ref, bf16[1536,1280]{1,0:T(8,128)(2,1)S(1)} %get-tuple-element.29.square, bf16[1536,512]{1,0:T(8,128)(2,1)S(1)} %get-tuple-element.43.whole.own), custom_call_target="tpu_custom_call" | custom-call | flops 603979776 | bytes 6029312 | tf_op jit(solution)/shard_map/pallas_call | solution.py:382
  83.5 1.8 %shard_map.60 = bf16[4,8,128,128]{3,2,1,0:T(8,128)(2,1)} custom-call(s32[13]{0:T(128)S(1)} %pad_add_fusion.drop_ref, bf16[1536,512]{1,0:T(8,128)(2,1)S(1)} %get-tuple-element.43.whole.own, bf16[1280,128]{1,0:T(8,128)(2,1)S(1)} %collective-permute-done.15.mate, bf16[1280,128]{1,0:T(8,128)(2,1)S(1)} %collective-permute-done.16.cross), custom_call_target="tpu_custom_call" | custom-call | bytes 3276800 | tf_op jit(solution)/shard_map/pallas_call | solution.py:382
  85.2 6.9 %collective-permute-done.14.cross = bf16[1280,128]{1,0:T(8,128)(2,1)S(1)} collective-permute-done((bf16[1280,128]{1,0:T(8,128)(2,1)S(1)}, bf16[1280,128]{1,0:T(8,128)(2,1)S(1)}, u32[]{:S(2)}, u32[]{:S(2)}) %collective-permute-start.14) | collective-permute-done | bytes 327712 | tf_op jit(solution)/shard_map/ppermute | solution.py:396
  92.1 1.8 %shard_map.59 = bf16[4,8,128,128]{3,2,1,0:T(8,128)(2,1)} custom-call(s32[13]{0:T(128)S(1)} %pad_add_fusion.drop_ref, bf16[512,512]{1,0:T(8,128)(2,1)S(1)} %shard_map.58.own, bf16[1280,128]{1,0:T(8,128)(2,1)S(1)} %collective-permute-done.13.mate, bf16[1280,128]{1,0:T(8,128)(2,1)S(1)} %collective-permute-done.14.cross), custom_call_target="tpu_custom_call" | custom-call | bytes 2228224 | tf_op jit(solution)/shard_map/pallas_call | solution.py:382
  (31 shorter events, 4.8 us)
Async XLA Ops:
  0.6 26.8 %collective-permute-start.2 = (bf16[4,8,128,128]{3,2,1,0:T(8,128)(2,1)}, bf16[4,8,128,128]{3,2,1,0:T(8,128)(2,1)S(1)}, u32[]{:S(2)}, u32[]{:S(2)}) collective-permute-start(bf16[4,8,128,128]{3,2,1,0:T(8,128)(2,1)} %own.3), channel_id=1, source_target_pairs={{0,1},{1,0},{2,3},{3,2},{4,5},{5,4},{6,7},{7,6},{8,9},{9,8},{10,11... | collective-permute-start | bytes 3145736 | tf_op jit(solution)/shard_map/ppermute | solution.py:396
  0.8 26.7 %collective-permute-start.3 = (bf16[4,8,128,128]{3,2,1,0:T(8,128)(2,1)}, bf16[4,8,128,128]{3,2,1,0:T(8,128)(2,1)S(1)}, u32[]{:S(2)}, u32[]{:S(2)}) collective-permute-start(bf16[4,8,128,128]{3,2,1,0:T(8,128)(2,1)} %own.3), channel_id=1, source_target_pairs={{0,15},{1,2},{2,1},{3,4},{4,3},{5,6},{6,5},{7,8},{8,7},{9,10},{10,... | collective-permute-start | bytes 3145736 | tf_op jit(solution)/shard_map/ppermute | solution.py:396
  4.3 7.4 %collective-permute-start = (s32[4]{0:T(128)S(1)}, s32[4]{0:T(128)S(1)}, u32[]{:S(2)}, u32[]{:S(2)}) collective-permute-start(s32[4]{0:T(128)S(1)} %broadcast_subtract_fusion), channel_id=1, source_target_pairs={{0,1},{1,0},{2,3},{3,2},{4,5},{5,4},{6,7},{7,6},{8,9},{9,8},{10,11... | collective-permute-start | bytes 56 | tf_op jit(solution)/shard_map/ppermute | solution.py:396
  7.8 19.6 %collective-permute-start.1 = (s32[4]{0:T(128)S(1)}, s32[4]{0:T(128)S(1)}, u32[]{:S(2)}, u32[]{:S(2)}) collective-permute-start(s32[4]{0:T(128)S(1)} %broadcast_subtract_fusion), channel_id=1, source_target_pairs={{0,15},{1,2},{2,1},{3,4},{4,3},{5,6},{6,5},{7,8},{8,7},{9,10},{10,... | collective-permute-start | bytes 56 | tf_op jit(solution)/shard_map/ppermute | solution.py:396
  7.9 1.2 %copy-start = (bf16[4,8,128,128]{3,2,1,0:T(8,128)(2,1)S(1)}, bf16[4,8,128,128]{3,2,1,0:T(8,128)(2,1)}, u32[]{:S(2)}) copy-start(bf16[4,8,128,128]{3,2,1,0:T(8,128)(2,1)} %own.2) | copy-start | bytes 3145732
  11.0 32.1 %collective-permute-start.6 = (bf16[3328,128]{1,0:T(8,128)(2,1)}, bf16[3328,128]{1,0:T(8,128)(2,1)S(1)}, u32[]{:S(2)}, u32[]{:S(2)}) collective-permute-start(bf16[3328,128]{1,0:T(8,128)(2,1)} %get-tuple-element.32.sent_mate), channel_id=1, source_target_pairs={{0,1},{1,0},{2,3},{3,2},{4,5},{5,4},{6,7},{7,6},{8,9},{9,8},{10,11... | collective-permute-start | bytes 2555912 | tf_op jit(solution)/shard_map/ppermute | solution.py:396
  11.6 26.7 %copy-start.1 = (bf16[4,8,128,128]{3,2,1,0:T(8,128)(2,1)S(1)}, bf16[4,8,128,128]{3,2,1,0:T(8,128)(2,1)}, u32[]{:S(2)}) copy-start(bf16[4,8,128,128]{3,2,1,0:T(8,128)(2,1)} %own.3) | copy-start | bytes 3145732
  28.2 5.6 %collective-permute-start.4 = (bf16[1280,128]{1,0:T(8,128)(2,1)S(1)}, bf16[1280,128]{1,0:T(8,128)(2,1)S(1)}, u32[]{:S(2)}, u32[]{:S(2)}) collective-permute-start(bf16[1280,128]{1,0:T(8,128)(2,1)S(1)} %get-tuple-element.27), channel_id=1, source_target_pairs={{0,1},{1,0},{2,3},{3,2},{4,5},{5,4},{6,7},{7,6},{8,9},{9,8},{10,11... | collective-permute-start | bytes 983048 | tf_op jit(solution)/shard_map/ppermute | solution.py:396
  28.3 10.1 %collective-permute-start.5 = (bf16[1280,128]{1,0:T(8,128)(2,1)S(1)}, bf16[1280,128]{1,0:T(8,128)(2,1)S(1)}, u32[]{:S(2)}, u32[]{:S(2)}) collective-permute-start(bf16[1280,128]{1,0:T(8,128)(2,1)S(1)} %get-tuple-element.28), channel_id=1, source_target_pairs={{0,13},{1,4},{2,15},{3,6},{4,1},{5,8},{6,3},{7,10},{8,5},{9,12},{1... | collective-permute-start | bytes 983048 | tf_op jit(solution)/shard_map/ppermute | solution.py:396
  30.5 12.5 %collective-permute-start.7 = (bf16[1280,128]{1,0:T(8,128)(2,1)}, bf16[1280,128]{1,0:T(8,128)(2,1)S(1)}, u32[]{:S(2)}, u32[]{:S(2)}) collective-permute-start(bf16[1280,128]{1,0:T(8,128)(2,1)} %get-tuple-element.33.sent_cross), channel_id=1, source_target_pairs={{0,15},{1,2},{2,1},{3,4},{4,3},{5,6},{6,5},{7,8},{8,7},{9,10},{10,... | collective-permute-start | bytes 983048 | tf_op jit(solution)/shard_map/ppermute | solution.py:396
  33.7 19.7 %collective-permute-start.8 = (bf16[2048,128]{1,0:T(8,128)(2,1)S(1)}, bf16[2048,128]{1,0:T(8,128)(2,1)S(1)}, u32[]{:S(2)}, u32[]{:S(2)}) collective-permute-start(bf16[2048,128]{1,0:T(8,128)(2,1)S(1)} %get-tuple-element.31.corner), channel_id=1, source_target_pairs={{0,15},{1,2},{2,1},{3,4},{4,3},{5,6},{6,5},{7,8},{8,7},{9,10},{10,... | collective-permute-start | bytes 1572872 | tf_op jit(solution)/shard_map/ppermute | solution.py:396
  46.9 11.8 %collective-permute-start.11 = (bf16[512,512]{1,0:T(8,128)(2,1)S(1)}, bf16[512,512]{1,0:T(8,128)(2,1)S(1)}, u32[]{:S(2)}, u32[]{:S(2)}) collective-permute-start(bf16[512,512]{1,0:T(8,128)(2,1)S(1)} %get-tuple-element.34.own), channel_id=1, source_target_pairs={{0,1},{1,0},{2,3},{3,2},{4,5},{5,4},{6,7},{7,6},{8,9},{9,8},{10,11... | collective-permute-start | bytes 1572872 | tf_op jit(solution)/shard_map/ppermute | solution.py:396
  49.3 18.8 %collective-permute-start.12 = (bf16[512,512]{1,0:T(8,128)(2,1)S(1)}, bf16[512,512]{1,0:T(8,128)(2,1)S(1)}, u32[]{:S(2)}, u32[]{:S(2)}) collective-permute-start(bf16[512,512]{1,0:T(8,128)(2,1)S(1)} %get-tuple-element.34.own), channel_id=1, source_target_pairs={{0,15},{1,2},{2,1},{3,4},{4,3},{5,6},{6,5},{7,8},{8,7},{9,10},{10,... | collective-permute-start | bytes 1572872 | tf_op jit(solution)/shard_map/ppermute | solution.py:396
  54.8 16.8 %collective-permute-start.9 = (bf16[1280,128]{1,0:T(8,128)(2,1)S(1)}, bf16[1280,128]{1,0:T(8,128)(2,1)S(1)}, u32[]{:S(2)}, u32[]{:S(2)}) collective-permute-start(bf16[1280,128]{1,0:T(8,128)(2,1)S(1)} %get-tuple-element.37), channel_id=1, source_target_pairs={{0,1},{1,0},{2,3},{3,2},{4,5},{5,4},{6,7},{7,6},{8,9},{9,8},{10,11... | collective-permute-start | bytes 983048 | tf_op jit(solution)/shard_map/ppermute | solution.py:396
  55.5 16.1 %collective-permute-start.10 = (bf16[1280,128]{1,0:T(8,128)(2,1)S(1)}, bf16[1280,128]{1,0:T(8,128)(2,1)S(1)}, u32[]{:S(2)}, u32[]{:S(2)}) collective-permute-start(bf16[1280,128]{1,0:T(8,128)(2,1)S(1)} %get-tuple-element.38), channel_id=1, source_target_pairs={{0,15},{1,2},{2,1},{3,4},{4,3},{5,6},{6,5},{7,8},{8,7},{9,10},{10,... | collective-permute-start | bytes 983048 | tf_op jit(solution)/shard_map/ppermute | solution.py:396
  69.7 13.8 %collective-permute-start.15 = (bf16[1280,128]{1,0:T(8,128)(2,1)S(1)}, bf16[1280,128]{1,0:T(8,128)(2,1)S(1)}, u32[]{:S(2)}, u32[]{:S(2)}) collective-permute-start(bf16[1280,128]{1,0:T(8,128)(2,1)S(1)} %get-tuple-element.46), channel_id=1, source_target_pairs={{0,1},{1,0},{2,3},{3,2},{4,5},{5,4},{6,7},{7,6},{8,9},{9,8},{10,11... | collective-permute-start | bytes 983048 | tf_op jit(solution)/shard_map/ppermute | solution.py:396
  69.8 13.7 %collective-permute-start.16 = (bf16[1280,128]{1,0:T(8,128)(2,1)S(1)}, bf16[1280,128]{1,0:T(8,128)(2,1)S(1)}, u32[]{:S(2)}, u32[]{:S(2)}) collective-permute-start(bf16[1280,128]{1,0:T(8,128)(2,1)S(1)} %get-tuple-element.47), channel_id=1, source_target_pairs={{0,15},{1,2},{2,1},{3,4},{4,3},{5,6},{6,5},{7,8},{8,7},{9,10},{10,... | collective-permute-start | bytes 983048 | tf_op jit(solution)/shard_map/ppermute | solution.py:396
  74.0 11.3 %collective-permute-start.13 = (bf16[1280,128]{1,0:T(8,128)(2,1)S(1)}, bf16[1280,128]{1,0:T(8,128)(2,1)S(1)}, u32[]{:S(2)}, u32[]{:S(2)}) collective-permute-start(bf16[1280,128]{1,0:T(8,128)(2,1)S(1)} %get-tuple-element.44), channel_id=1, source_target_pairs={{0,1},{1,0},{2,3},{3,2},{4,5},{5,4},{6,7},{7,6},{8,9},{9,8},{10,11... | collective-permute-start | bytes 983048 | tf_op jit(solution)/shard_map/ppermute | solution.py:396
  82.1 10.0 %collective-permute-start.14 = (bf16[1280,128]{1,0:T(8,128)(2,1)S(1)}, bf16[1280,128]{1,0:T(8,128)(2,1)S(1)}, u32[]{:S(2)}, u32[]{:S(2)}) collective-permute-start(bf16[1280,128]{1,0:T(8,128)(2,1)S(1)} %get-tuple-element.45), channel_id=1, source_target_pairs={{0,15},{1,2},{2,1},{3,4},{4,3},{5,6},{6,5},{7,8},{8,7},{9,10},{10,... | collective-permute-start | bytes 983048 | tf_op jit(solution)/shard_map/ppermute | solution.py:396

commit v6 on v2

--- a/solution.py
+++ b/solution.py
@@ -307,31 +307,45 @@
     pack(f, high, 0, to_next, over(h))
 
 
-def density_own_kernel(f, drop_ref, square, whole, out):
+def own_outputs_kernel(f, drop_ref, square, whole, density_out, inverse_out, scratch):
     p = f.p
     for row, col in f.tiles(f.own_pairs):
         if row in f.own_pairs:
             total = masked(f, right_tile(f, square, whole, row, col), row, col, drop_ref)
-            out[at(f, row - p, row - p + 1, col - p, col - p + 1)] = total.astype(out.dtype)
-
-
-def rows_kernel(f, first, drop_ref, own, from_below, from_above, out):
+            scratch[at(f, row - p, row - p + 1, col - p, col - p + 1)] = total.astype(scratch.dtype)
+    own_slots(f, drop_ref, lambda r, c: scratch[block(f, r, c)], density_out)
+    own_slots(f, drop_ref, lambda r, c: whole[block(f, f.h + r, c)], inverse_out)
+
+
+def own_slots(f, drop_ref, read, out):
     h = f.h
-    over_index = {place: i for i, place in enumerate(over(h))}
-    under_index = {place: i for i, place in enumerate(under(h))}
     for r in range(h):
         dropped = drop_ref[h + r]
-
-        def at_offset(offset, r=r):
-            col = r + offset
-            if col < h:
-                return from_below[over_index[r, col]]
-            if col < 2 * h:
-                return own[block(f, first + r, col - h)]
-            return from_above[under_index[r, col - 2 * h]]
-
-        for s in range(f.k):
-            out[r, s] = jnp.where(dropped <= s, at_offset(s + 1), at_offset(s))
+        for c in range(h):
+            offset = c - r + h
+            slot = jnp.minimum(offset - (offset > dropped).astype(jnp.int32), f.k - 1)
+
+            @pl.when(offset != dropped)
+            def _(r=r, c=c, slot=slot):
+                out[r, slot] = read(r, c)
+
+
+def side_slots_kernel(f, drop_ref, from_below, from_above, *refs):
+    h = f.h
+    token, out, sems = refs[-3:]
+    token[...] = jnp.zeros_like(token)
+    copies = []
+    for g, (source, places) in enumerate(((from_below, over(h)), (from_above, under(h)))):
+        for i, (r, c) in enumerate(places):
+            offset = c - r + 2 * h * g
+            dropped = drop_ref[h + r]
+            slot = jnp.minimum(offset - (offset > dropped).astype(jnp.int32), f.k - 1)
+            copy = pltpu.make_async_copy(source.at[i], out.at[r, slot], sems.at[len(copies)])
+            copies.append((offset != dropped, copy))
+    for present, copy in copies:
+        pl.when(present)(copy.start)
+    for present, copy in copies:
+        pl.when(present)(copy.wait)
 
 
 VMEM = pl.BlockSpec(memory_space=pltpu.VMEM)
@@ -339,19 +353,18 @@
 ANY = pl.BlockSpec(memory_space=pl.ANY)
 
 
-def call(kernel, outs, scratch, flops, limit, drop, *args, passed=()):
-    moved = sum(a.size * a.dtype.itemsize for a in args) + sum(s.size * s.dtype.itemsize for s in outs)
+def call(kernel, outs, scratch, flops, limit, drop, *args, passed=(), after=()):
     n = len(args)
     return pl.pallas_call(
         kernel,
         out_shape=[*outs, *[jax.ShapeDtypeStruct(a.shape, a.dtype) for a in passed]],
-        in_specs=[SMEM] + [VMEM] * n + [ANY] * len(passed),
+        in_specs=[SMEM] + [VMEM] * n + [ANY] * (len(passed) + len(after)),
         out_specs=[VMEM] * len(outs) + [ANY] * len(passed),
         scratch_shapes=scratch,
         input_output_aliases={1 + n + i: len(outs) + i for i in range(len(passed))},
         compiler_params=pltpu.CompilerParams(vmem_limit_bytes=limit * MIB),
-        cost_estimate=pl.CostEstimate(flops=flops, bytes_accessed=moved, transcendentals=0),
-    )(drop, *args, *passed)
+        cost_estimate=pl.CostEstimate(flops=flops, bytes_accessed=0, transcendentals=0),
+    )(drop, *args, *passed, *after)
 
 
 def permuted(x, step):
@@ -375,16 +388,15 @@
     f = Frame(half, order)
     kind = density.dtype
     me = lax.axis_index(RING)
-
-    def absent(columns, first):
-        ids = first + jnp.arange(columns.shape[0], dtype=jnp.int32)
-        positions = jnp.mod(columns - ids[:, None] + half, rows * ring)
-        return width * (width + 1) // 2 - jnp.sum(positions, axis=1)
+    total = rows * ring
+
+    positions = block_cols - (me * rows + jnp.arange(rows, dtype=jnp.int32))[:, None] + half
+    positions = positions + jnp.where(positions < 0, total, jnp.where(positions >= total, -total, 0))
+    own_drop = width * (width + 1) // 2 - jnp.sum(positions, axis=1)
 
     below, above = to_next(density), to_prev(density)
-    near_cols = jnp.concatenate([to_next(block_cols), block_cols, to_prev(block_cols)], axis=0)
-    drop = jnp.concatenate([absent(near_cols, (me - 1) * rows), jnp.reshape(me % 2, (1,))])
-    own_drop = absent(block_cols, me * rows)
+    odd = jnp.reshape(me & 1, (1,))
+    drop = jnp.concatenate([to_next(own_drop), own_drop, to_prev(own_drop), odd])
 
     unit = 2 * f.t**3
     square_group = jax.ShapeDtypeStruct((f.group, f.group), kind)
@@ -439,22 +451,25 @@
         20, 12, drop, next_corner_below, next_corner_above, correction, low, high,
     )
     inverse_above, inverse_below = to_prev(back), to_next(forth)
+    out = jax.ShapeDtypeStruct(density.shape, kind)
     whole, back, forth = run(
         density_edges_kernel,
         [columns, triangle, triangle],
         [group_scratch] * 4,
-        38, 20, drop, own, from_below, from_above, correction, new_low, new_high, square,
+        38, 24, drop, own, from_below, from_above, correction, new_low, new_high, square,
     )
     density_above, density_below = to_prev(back), to_next(forth)
-    (density_own,) = run(density_own_kernel, [square_group], [], 18, 12, drop, square, whole)
-    out = jax.ShapeDtypeStruct(density.shape, kind)
-
-    def assembled(own, first, from_below, from_above):
-        kernel = functools.partial(rows_kernel, f, first)
-        return call(kernel, [out], [], 0, 8, drop, own, from_below, from_above)[0]
-
-    inverse_next = assembled(whole, half, inverse_below, inverse_above)
-    density_next = assembled(density_own, 0, density_below, density_above)
+    density_own, inverse_own = run(own_outputs_kernel, [out, out], [group_scratch], 18, 16, drop, square, whole)
+
+    def completed(own, from_below, from_above, after=()):
+        sems = pltpu.SemaphoreType.DMA((2 * triangle.shape[0],))
+        token = jax.ShapeDtypeStruct((8, order), jnp.float32)
+        return run(
+            side_slots_kernel, [token], [sems], 0, 8, drop, from_below, from_above, passed=(own,), after=after
+        )
+
+    token, inverse_next = completed(inverse_own, inverse_below, inverse_above)
+    _, density_next = completed(density_own, density_below, density_above, after=(token,))
     return density_next, inverse_next
 
 

time: 91 us -> 90.6 us (level)
  Pallas kernels: 20.7 us -> 22.4 us
  waiting for transfers between devices: 45.1 us -> 43.7 us
  other arithmetic: 1.86 us -> 0.95 us
    pallas_call x11, Pallas kernels: 20.7 us -> 22.4 us  [call(): pl.pallas_call(kernel, out_shape=[*outs, *[jax.ShapeDtypeStruct(a.shape,...]
    ppermute x18, waiting for transfers between devices: 45.1 us -> 43.7 us  [permuted(): lax.ppermute(x, RING, [(i, (i + step(i)) % size) for i in range(size)])]
  transfers between devices with their start and end apart: 18 -> 18, of which waited for: 8 -> 8; matrix products, arithmetic and copies ran while one was open for 2% -> 1% of each run, Pallas kernels for 20% -> 22%
where the time goes in v6:
time: 90.6 us; the launch traced here: 90.4 us
  waiting for transfers between devices  43.7 us (48%)
  Pallas kernels  22.4 us (25%)
  starting transfers between devices  21.2 us (23%)
  local copies, waits for them, and re-layouts  1.23 us (1%)
  other arithmetic  0.95 us (1%)
  between operations  0.92 us (1%)
    ppermute x18, waiting for transfers between devices, permuted(): lax.ppermute(x, RING, [(i, (i + step(i)) % size) for i in range(size)])  43.7 us
    pallas_call x11, Pallas kernels, call(): pl.pallas_call(kernel, out_shape=[*outs, *[jax.ShapeDtypeStruct(a.shape,...  22.4 us
    ppermute x18, starting transfers between devices, permuted(): lax.ppermute(x, RING, [(i, (i + step(i)) % size) for i in range(size)])  21.2 us
  transfers between devices with their start and end apart: 18, of which 8 were waited for; matrix products, arithmetic and copies ran while one was open for 1% of the time, Pallas kernels for 22%

profile of v6, /device:TPU:1, one launch (start us, length us, event | category | flops | bytes accessed | tf_op | source)
XLA Modules:
  0.0 90.4 jit_solution(18442875465338513990)
XLA Ops:
  0.6 2.7 %collective-permute-start.2 = (bf16[4,8,128,128]{3,2,1,0:T(8,128)(2,1)}, bf16[4,8,128,128]{3,2,1,0:T(8,128)(2,1)S(1)}, u32[]{:S(2)}, u32[]{:S(2)}) collective-permute-start(bf16[4,8,128,128]{3,2,1,0:T(8,128)(2,1)} %own.3), channel_id=1, source_target_pairs={{0,1},{1,2},{2,3},{3,4},{4,5},{5,6},{6,7},{7,8},{8,9},{9,10},{10,1... | collective-permute-start | bytes 3145736 | tf_op jit(solution)/shard_map/ppermute | solution.py:372
  4.2 3.0 %collective-permute-start.1 = (s32[4]{0:T(128)S(1)}, s32[4]{0:T(128)S(1)}, u32[]{:S(2)}, u32[]{:S(2)}) collective-permute-start(s32[4]{0:T(128)S(1)} %broadcast_subtract_fusion.drop_ref), channel_id=1, source_target_pairs={{0,15},{1,0},{2,1},{3,2},{4,3},{5,4},{6,5},{7,6},{8,7},{9,8},{10,9... | collective-permute-start | bytes 56 | tf_op jit(solution)/shard_map/ppermute | solution.py:372
  7.2 1.2 %copy-done = bf16[4,8,128,128]{3,2,1,0:T(8,128)(2,1)S(1)} copy-done((bf16[4,8,128,128]{3,2,1,0:T(8,128)(2,1)S(1)}, bf16[4,8,128,128]{3,2,1,0:T(8,128)(2,1)}, u32[]{:S(2)}) %copy-start) | copy-done | bytes 1048600
  9.2 19.8 %collective-permute-done.1 = s32[4]{0:T(128)S(1)} collective-permute-done((s32[4]{0:T(128)S(1)}, s32[4]{0:T(128)S(1)}, u32[]{:S(2)}, u32[]{:S(2)}) %collective-permute-start.1) | collective-permute-done | bytes 48 | tf_op jit(solution)/shard_map/ppermute | solution.py:372
  30.4 3.0 %collective-permute-start.6 = (bf16[10,128,128]{2,1,0:T(8,128)(2,1)S(1)}, bf16[10,128,128]{2,1,0:T(8,128)(2,1)S(1)}, u32[]{:S(2)}, u32[]{:S(2)}) collective-permute-start(bf16[10,128,128]{2,1,0:T(8,128)(2,1)S(1)} %get-tuple-element.38.up), channel_id=1, source_target_pairs={{0,1},{1,2},{2,3},{3,4},{4,5},{5,6},{6,7},{7,8},{8,9},{9,10},{10,1... | collective-permute-start | bytes 983048 | tf_op jit(solution)/shard_map/ppermute | solution.py:372
  33.4 1.7 %collective-permute-start.8 = (bf16[512,512]{1,0:T(8,128)(2,1)S(1)}, bf16[512,512]{1,0:T(8,128)(2,1)S(1)}, u32[]{:S(2)}, u32[]{:S(2)}) collective-permute-start(bf16[512,512]{1,0:T(8,128)(2,1)S(1)} %get-tuple-element.37.corner), channel_id=1, source_target_pairs={{0,1},{1,2},{2,3},{3,4},{4,5},{5,6},{6,7},{7,8},{8,9},{9,10},{10,1... | collective-permute-start | bytes 1572872 | tf_op jit(solution)/shard_map/ppermute | solution.py:372
  35.2 5.0 %collective-permute-start.9 = (bf16[512,512]{1,0:T(8,128)(2,1)S(1)}, bf16[512,512]{1,0:T(8,128)(2,1)S(1)}, u32[]{:S(2)}, u32[]{:S(2)}) collective-permute-start(bf16[512,512]{1,0:T(8,128)(2,1)S(1)} %get-tuple-element.37.corner), channel_id=1, source_target_pairs={{0,15},{1,0},{2,1},{3,2},{4,3},{5,4},{6,5},{7,6},{8,7},{9,8},{10,9... | collective-permute-start | bytes 1572872 | tf_op jit(solution)/shard_map/ppermute | solution.py:372
  40.3 4.4 %shard_map.52 = (bf16[1536,1280]{1,0:T(8,128)(2,1)S(1)}, bf16[1536,1280]{1,0:T(8,128)(2,1)S(1)}) custom-call(s32[13]{0:T(128)S(1)} %pad_add_fusion.drop_ref, bf16[4,8,128,128]{3,2,1,0:T(8,128)(2,1)S(1)} %copy-done.1, bf16[4,8,128,128]{3,2,1,0:T(8,128)(2,1)S(1)} %collective-permute-done.2.below, bf16[4,8,128,128]{3,2,1,0:T(8,128)(2,1)S(1)} %collective-permute-done.3.above, ...), custom_call_target="tpu_custom_call" | custom-call | flops 3154116608 | tf_op jit(solution)/shard_map/pallas_call | solution.py:358
  44.7 3.1 %shard_map.53 = (bf16[1536,512]{1,0:T(8,128)(2,1)S(1)}, bf16[512,512]{1,0:T(8,128)(2,1)S(1)}, f32[1024,512]{1,0:T(8,128)S(1)}) custom-call(s32[13]{0:T(128)S(1)} %pad_add_fusion.drop_ref, bf16[1536,1280]{1,0:T(8,128)(2,1)S(1)} %get-tuple-element.36.shifted, bf16[512,512]{1,0:T(8,128)(2,1)S(1)} %get-tuple-element.37.corner, ...), custom_call_target="tpu_custom_call" | custom-call | flops 2214592512 | tf_op jit(solution)/shard_map/pallas_call | solution.py:358
  47.7 1.4 %collective-permute-start.12 = (bf16[512,512]{1,0:T(8,128)(2,1)S(1)}, bf16[512,512]{1,0:T(8,128)(2,1)S(1)}, u32[]{:S(2)}, u32[]{:S(2)}) collective-permute-start(bf16[512,512]{1,0:T(8,128)(2,1)S(1)} %get-tuple-element.40.own), channel_id=1, source_target_pairs={{0,1},{1,2},{2,3},{3,4},{4,5},{5,6},{6,7},{7,8},{8,9},{9,10},{10,1... | collective-permute-start | bytes 1572872 | tf_op jit(solution)/shard_map/ppermute | solution.py:372
  49.3 2.9 %collective-permute-done.8.corner_below = bf16[512,512]{1,0:T(8,128)(2,1)S(1)} collective-permute-done((bf16[512,512]{1,0:T(8,128)(2,1)S(1)}, bf16[512,512]{1,0:T(8,128)(2,1)S(1)}, u32[]{:S(2)}, u32[]{:S(2)}) %collective-permute-start.8) | collective-permute-done | bytes 524320 | tf_op jit(solution)/shard_map/ppermute | solution.py:372
  52.2 11.6 %collective-permute-done.9.corner_above = bf16[512,512]{1,0:T(8,128)(2,1)S(1)} collective-permute-done((bf16[512,512]{1,0:T(8,128)(2,1)S(1)}, bf16[512,512]{1,0:T(8,128)(2,1)S(1)}, u32[]{:S(2)}, u32[]{:S(2)}) %collective-permute-start.9) | collective-permute-done | bytes 524320 | tf_op jit(solution)/shard_map/ppermute | solution.py:372
  63.8 1.1 %shard_map.54 = (bf16[512,512]{1,0:T(8,128)(2,1)S(1)}, bf16[512,512]{1,0:T(8,128)(2,1)S(1)}, bf16[10,128,128]{2,1,0:T(8,128)(2,1)S(1)}, bf16[10,128,128]{2,1,0:T(8,128)(2,1)S(1)}) custom-call(s32[13]{0:T(128)S(1)} %pad_add_fusion.drop_ref, bf16[512,512]{1,0:T(8,128)(2,1)S(1)} %collective-permute-done.8.corner_below, ...), custom_call_target="tpu_custom_call" | custom-call | flops 335544320 | tf_op jit(solution)/shard_map/pallas_call | solution.py:358
  65.5 2.0 %shard_map.55.correction = bf16[1536,512]{1,0:T(8,128)(2,1)S(1)} custom-call(s32[13]{0:T(128)S(1)} %pad_add_fusion.drop_ref, bf16[1536,1280]{1,0:T(8,128)(2,1)S(1)} %get-tuple-element.36.shifted, bf16[512,512]{1,0:T(8,128)(2,1)S(1)} %get-tuple-element.45.low, bf16[512,512]{1,0:T(8,128)(2,1)S(1)} %get-tuple-element.40.own, ...), custom_call_target="tpu_custom_call" | custom-call | flops 1275068416 | tf_op jit(solution)/shard_map/pallas_call | solution.py:358
  67.5 1.9 %collective-permute-done.13.corner_above = bf16[512,512]{1,0:T(8,128)(2,1)S(1)} collective-permute-done((bf16[512,512]{1,0:T(8,128)(2,1)S(1)}, bf16[512,512]{1,0:T(8,128)(2,1)S(1)}, u32[]{:S(2)}, u32[]{:S(2)}) %collective-permute-start.13) | collective-permute-done | bytes 524320 | tf_op jit(solution)/shard_map/ppermute | solution.py:372
  69.4 1.5 %shard_map.56 = (bf16[512,512]{1,0:T(8,128)(2,1)S(1)}, bf16[512,512]{1,0:T(8,128)(2,1)S(1)}, bf16[10,128,128]{2,1,0:T(8,128)(2,1)S(1)}, bf16[10,128,128]{2,1,0:T(8,128)(2,1)S(1)}) custom-call(s32[13]{0:T(128)S(1)} %pad_add_fusion.drop_ref, bf16[512,512]{1,0:T(8,128)(2,1)S(1)} %collective-permute-done.12.corner_below, ...), custom_call_target="tpu_custom_call" | custom-call | flops 671088640 | tf_op jit(solution)/shard_map/pallas_call | solution.py:358
  71.5 4.4 %collective-permute-done.10.from_below = bf16[10,128,128]{2,1,0:T(8,128)(2,1)S(1)} collective-permute-done((bf16[10,128,128]{2,1,0:T(8,128)(2,1)S(1)}, bf16[10,128,128]{2,1,0:T(8,128)(2,1)S(1)}, u32[]{:S(2)}, u32[]{:S(2)}) %collective-permute-start.10) | collective-permute-done | bytes 327712 | tf_op jit(solution)/shard_map/ppermute | solution.py:372
  76.0 2.2 %shard_map.57 = (bf16[1536,512]{1,0:T(8,128)(2,1)S(1)}, bf16[10,128,128]{2,1,0:T(8,128)(2,1)S(1)}, bf16[10,128,128]{2,1,0:T(8,128)(2,1)S(1)}) custom-call(s32[13]{0:T(128)S(1)} %pad_add_fusion.drop_ref, bf16[512,512]{1,0:T(8,128)(2,1)S(1)} %get-tuple-element.40.own, bf16[10,128,128]{2,1,0:T(8,128)(2,1)S(1)} %collective-permute-done.10.from_below, ...), custom_call_target="tpu_custom_call" | custom-call | flops 1275068416 | tf_op jit(solution)/shard_map/pallas_call | solution.py:358
  78.2 2.5 %collective-permute-start.14 = (bf16[10,128,128]{2,1,0:T(8,128)(2,1)S(1)}, bf16[10,128,128]{2,1,0:T(8,128)(2,1)S(1)}, u32[]{:S(2)}, u32[]{:S(2)}) collective-permute-start(bf16[10,128,128]{2,1,0:T(8,128)(2,1)S(1)} %get-tuple-element.50), channel_id=1, source_target_pairs={{0,1},{1,2},{2,3},{3,4},{4,5},{5,6},{6,7},{7,8},{8,9},{9,10},{10,1... | collective-permute-start | bytes 983048 | tf_op jit(solution)/shard_map/ppermute | solution.py:372
  80.7 2.9 %shard_map.58 = (bf16[4,8,128,128]{3,2,1,0:T(8,128)(2,1)}, bf16[4,8,128,128]{3,2,1,0:T(8,128)(2,1)}) custom-call(s32[13]{0:T(128)S(1)} %pad_add_fusion.drop_ref, bf16[1536,1280]{1,0:T(8,128)(2,1)S(1)} %get-tuple-element.49.square, bf16[1536,512]{1,0:T(8,128)(2,1)S(1)} %get-tuple-element.52.whole), custom_call_target="tpu_custom_call" | custom-call | flops 603979776 | tf_op jit(solution)/shard_map/pallas_call | solution.py:358
  83.6 1.0 %collective-permute-done.17.from_above = bf16[10,128,128]{2,1,0:T(8,128)(2,1)S(1)} collective-permute-done((bf16[10,128,128]{2,1,0:T(8,128)(2,1)S(1)}, bf16[10,128,128]{2,1,0:T(8,128)(2,1)S(1)}, u32[]{:S(2)}, u32[]{:S(2)}) %collective-permute-start.17) | collective-permute-done | bytes 327712 | tf_op jit(solution)/shard_map/ppermute | solution.py:372
  84.7 1.5 %shard_map.59 = (f32[8,128]{1,0:T(8,128)S(1)}, bf16[4,8,128,128]{3,2,1,0:T(8,128)(2,1)}) custom-call(s32[13]{0:T(128)S(1)} %pad_add_fusion.drop_ref, bf16[10,128,128]{2,1,0:T(8,128)(2,1)S(1)} %collective-permute-done.16.from_below, bf16[10,128,128]{2,1,0:T(8,128)(2,1)S(1)} %collective-permute-done.17.from_above, ...), custom_call_target="tpu_custom_call", output_to_operand_aliasing={{1}: (3, {})} | custom-call | tf_op jit(solution)/shard_map/pallas_call | solution.py:358
  86.5 1.7 %collective-permute-done.15.from_above = bf16[10,128,128]{2,1,0:T(8,128)(2,1)S(1)} collective-permute-done((bf16[10,128,128]{2,1,0:T(8,128)(2,1)S(1)}, bf16[10,128,128]{2,1,0:T(8,128)(2,1)S(1)}, u32[]{:S(2)}, u32[]{:S(2)}) %collective-permute-start.15) | collective-permute-done | bytes 327712 | tf_op jit(solution)/shard_map/ppermute | solution.py:372
  88.2 2.1 %shard_map.60 = (f32[8,128]{1,0:T(8,128)}, bf16[4,8,128,128]{3,2,1,0:T(8,128)(2,1)}) custom-call(s32[13]{0:T(128)S(1)} %pad_add_fusion.drop_ref, bf16[10,128,128]{2,1,0:T(8,128)(2,1)S(1)} %collective-permute-done.14.from_below, bf16[10,128,128]{2,1,0:T(8,128)(2,1)S(1)} %collective-permute-done.15.from_above, ...), custom_call_target="tpu_custom_call", output_to_operand_aliasing={{1}: (3, {})} | custom-call | tf_op jit(solution)/shard_map/pallas_call | solution.py:358
  (31 shorter events, 4.7 us)
Async XLA Ops:
  0.6 28.5 %collective-permute-start.2 = (bf16[4,8,128,128]{3,2,1,0:T(8,128)(2,1)}, bf16[4,8,128,128]{3,2,1,0:T(8,128)(2,1)S(1)}, u32[]{:S(2)}, u32[]{:S(2)}) collective-permute-start(bf16[4,8,128,128]{3,2,1,0:T(8,128)(2,1)} %own.3), channel_id=1, source_target_pairs={{0,1},{1,2},{2,3},{3,4},{4,5},{5,6},{6,7},{7,8},{8,9},{9,10},{10,1... | collective-permute-start | bytes 3145736 | tf_op jit(solution)/shard_map/ppermute | solution.py:372
  3.3 25.8 %collective-permute-start.3 = (bf16[4,8,128,128]{3,2,1,0:T(8,128)(2,1)}, bf16[4,8,128,128]{3,2,1,0:T(8,128)(2,1)S(1)}, u32[]{:S(2)}, u32[]{:S(2)}) collective-permute-start(bf16[4,8,128,128]{3,2,1,0:T(8,128)(2,1)} %own.3), channel_id=1, source_target_pairs={{0,15},{1,0},{2,1},{3,2},{4,3},{5,4},{6,5},{7,6},{8,7},{9,8},{10,9... | collective-permute-start | bytes 3145736 | tf_op jit(solution)/shard_map/ppermute | solution.py:372
  4.2 24.9 %collective-permute-start.1 = (s32[4]{0:T(128)S(1)}, s32[4]{0:T(128)S(1)}, u32[]{:S(2)}, u32[]{:S(2)}) collective-permute-start(s32[4]{0:T(128)S(1)} %broadcast_subtract_fusion.drop_ref), channel_id=1, source_target_pairs={{0,15},{1,0},{2,1},{3,2},{4,3},{5,4},{6,5},{7,6},{8,7},{9,8},{10,9... | collective-permute-start | bytes 56 | tf_op jit(solution)/shard_map/ppermute | solution.py:372
  7.1 21.9 %collective-permute-start = (s32[4]{0:T(128)S(1)}, s32[4]{0:T(128)S(1)}, u32[]{:S(2)}, u32[]{:S(2)}) collective-permute-start(s32[4]{0:T(128)S(1)} %broadcast_subtract_fusion.drop_ref), channel_id=1, source_target_pairs={{0,1},{1,2},{2,3},{3,4},{4,5},{5,6},{6,7},{7,8},{8,9},{9,10},{10,1... | collective-permute-start | bytes 56 | tf_op jit(solution)/shard_map/ppermute | solution.py:372
  7.2 1.2 %copy-start = (bf16[4,8,128,128]{3,2,1,0:T(8,128)(2,1)S(1)}, bf16[4,8,128,128]{3,2,1,0:T(8,128)(2,1)}, u32[]{:S(2)}) copy-start(bf16[4,8,128,128]{3,2,1,0:T(8,128)(2,1)} %own.2) | copy-start | bytes 3145732
  8.4 31.9 %copy-start.1 = (bf16[4,8,128,128]{3,2,1,0:T(8,128)(2,1)S(1)}, bf16[4,8,128,128]{3,2,1,0:T(8,128)(2,1)}, u32[]{:S(2)}) copy-start(bf16[4,8,128,128]{3,2,1,0:T(8,128)(2,1)} %own.3) | copy-start | bytes 3145732
  29.8 5.3 %collective-permute-start.4 = (bf16[10,128,128]{2,1,0:T(8,128)(2,1)S(1)}, bf16[10,128,128]{2,1,0:T(8,128)(2,1)S(1)}, u32[]{:S(2)}, u32[]{:S(2)}) collective-permute-start(bf16[10,128,128]{2,1,0:T(8,128)(2,1)S(1)} %get-tuple-element.34), channel_id=1, source_target_pairs={{0,1},{1,4},{2,3},{3,6},{4,5},{5,8},{6,7},{7,10},{8,9},{9,12},{10,... | collective-permute-start | bytes 983048 | tf_op jit(solution)/shard_map/ppermute | solution.py:372
  29.9 10.4 %collective-permute-start.5 = (bf16[10,128,128]{2,1,0:T(8,128)(2,1)S(1)}, bf16[10,128,128]{2,1,0:T(8,128)(2,1)S(1)}, u32[]{:S(2)}, u32[]{:S(2)}) collective-permute-start(bf16[10,128,128]{2,1,0:T(8,128)(2,1)S(1)} %get-tuple-element.35), channel_id=1, source_target_pairs={{0,13},{1,0},{2,15},{3,2},{4,1},{5,4},{6,3},{7,6},{8,5},{9,8},{10,... | collective-permute-start | bytes 983048 | tf_op jit(solution)/shard_map/ppermute | solution.py:372
  30.4 14.2 %collective-permute-start.6 = (bf16[10,128,128]{2,1,0:T(8,128)(2,1)S(1)}, bf16[10,128,128]{2,1,0:T(8,128)(2,1)S(1)}, u32[]{:S(2)}, u32[]{:S(2)}) collective-permute-start(bf16[10,128,128]{2,1,0:T(8,128)(2,1)S(1)} %get-tuple-element.38.up), channel_id=1, source_target_pairs={{0,1},{1,2},{2,3},{3,4},{4,5},{5,6},{6,7},{7,8},{8,9},{9,10},{10,1... | collective-permute-start | bytes 983048 | tf_op jit(solution)/shard_map/ppermute | solution.py:372
  33.4 11.2 %collective-permute-start.7 = (bf16[10,128,128]{2,1,0:T(8,128)(2,1)S(1)}, bf16[10,128,128]{2,1,0:T(8,128)(2,1)S(1)}, u32[]{:S(2)}, u32[]{:S(2)}) collective-permute-start(bf16[10,128,128]{2,1,0:T(8,128)(2,1)S(1)} %get-tuple-element.39.down), channel_id=1, source_target_pairs={{0,15},{1,0},{2,1},{3,2},{4,3},{5,4},{6,5},{7,6},{8,7},{9,8},{10,9... | collective-permute-start | bytes 983048 | tf_op jit(solution)/shard_map/ppermute | solution.py:372
  33.4 18.8 %collective-permute-start.8 = (bf16[512,512]{1,0:T(8,128)(2,1)S(1)}, bf16[512,512]{1,0:T(8,128)(2,1)S(1)}, u32[]{:S(2)}, u32[]{:S(2)}) collective-permute-start(bf16[512,512]{1,0:T(8,128)(2,1)S(1)} %get-tuple-element.37.corner), channel_id=1, source_target_pairs={{0,1},{1,2},{2,3},{3,4},{4,5},{5,6},{6,7},{7,8},{8,9},{9,10},{10,1... | collective-permute-start | bytes 1572872 | tf_op jit(solution)/shard_map/ppermute | solution.py:372
  35.2 28.6 %collective-permute-start.9 = (bf16[512,512]{1,0:T(8,128)(2,1)S(1)}, bf16[512,512]{1,0:T(8,128)(2,1)S(1)}, u32[]{:S(2)}, u32[]{:S(2)}) collective-permute-start(bf16[512,512]{1,0:T(8,128)(2,1)S(1)} %get-tuple-element.37.corner), channel_id=1, source_target_pairs={{0,15},{1,0},{2,1},{3,2},{4,3},{5,4},{6,5},{7,6},{8,7},{9,8},{10,9... | collective-permute-start | bytes 1572872 | tf_op jit(solution)/shard_map/ppermute | solution.py:372
  47.7 19.8 %collective-permute-start.12 = (bf16[512,512]{1,0:T(8,128)(2,1)S(1)}, bf16[512,512]{1,0:T(8,128)(2,1)S(1)}, u32[]{:S(2)}, u32[]{:S(2)}) collective-permute-start(bf16[512,512]{1,0:T(8,128)(2,1)S(1)} %get-tuple-element.40.own), channel_id=1, source_target_pairs={{0,1},{1,2},{2,3},{3,4},{4,5},{5,6},{6,7},{7,8},{8,9},{9,10},{10,1... | collective-permute-start | bytes 1572872 | tf_op jit(solution)/shard_map/ppermute | solution.py:372
  49.1 20.3 %collective-permute-start.13 = (bf16[512,512]{1,0:T(8,128)(2,1)S(1)}, bf16[512,512]{1,0:T(8,128)(2,1)S(1)}, u32[]{:S(2)}, u32[]{:S(2)}) collective-permute-start(bf16[512,512]{1,0:T(8,128)(2,1)S(1)} %get-tuple-element.40.own), channel_id=1, source_target_pairs={{0,15},{1,0},{2,1},{3,2},{4,3},{5,4},{6,5},{7,6},{8,7},{9,8},{10,9... | collective-permute-start | bytes 1572872 | tf_op jit(solution)/shard_map/ppermute | solution.py:372
  64.9 11.0 %collective-permute-start.10 = (bf16[10,128,128]{2,1,0:T(8,128)(2,1)S(1)}, bf16[10,128,128]{2,1,0:T(8,128)(2,1)S(1)}, u32[]{:S(2)}, u32[]{:S(2)}) collective-permute-start(bf16[10,128,128]{2,1,0:T(8,128)(2,1)S(1)} %get-tuple-element.43), channel_id=1, source_target_pairs={{0,1},{1,2},{2,3},{3,4},{4,5},{5,6},{6,7},{7,8},{8,9},{9,10},{10,1... | collective-permute-start | bytes 983048 | tf_op jit(solution)/shard_map/ppermute | solution.py:372
  65.0 10.9 %collective-permute-start.11 = (bf16[10,128,128]{2,1,0:T(8,128)(2,1)S(1)}, bf16[10,128,128]{2,1,0:T(8,128)(2,1)S(1)}, u32[]{:S(2)}, u32[]{:S(2)}) collective-permute-start(bf16[10,128,128]{2,1,0:T(8,128)(2,1)S(1)} %get-tuple-element.44), channel_id=1, source_target_pairs={{0,15},{1,0},{2,1},{3,2},{4,3},{5,4},{6,5},{7,6},{8,7},{9,8},{10,9... | collective-permute-start | bytes 983048 | tf_op jit(solution)/shard_map/ppermute | solution.py:372
  71.0 12.7 %collective-permute-start.16 = (bf16[10,128,128]{2,1,0:T(8,128)(2,1)S(1)}, bf16[10,128,128]{2,1,0:T(8,128)(2,1)S(1)}, u32[]{:S(2)}, u32[]{:S(2)}) collective-permute-start(bf16[10,128,128]{2,1,0:T(8,128)(2,1)S(1)} %get-tuple-element.54), channel_id=1, source_target_pairs={{0,1},{1,2},{2,3},{3,4},{4,5},{5,6},{6,7},{7,8},{8,9},{9,10},{10,1... | collective-permute-start | bytes 983048 | tf_op jit(solution)/shard_map/ppermute | solution.py:372
  71.0 13.7 %collective-permute-start.17 = (bf16[10,128,128]{2,1,0:T(8,128)(2,1)S(1)}, bf16[10,128,128]{2,1,0:T(8,128)(2,1)S(1)}, u32[]{:S(2)}, u32[]{:S(2)}) collective-permute-start(bf16[10,128,128]{2,1,0:T(8,128)(2,1)S(1)} %get-tuple-element.55), channel_id=1, source_target_pairs={{0,15},{1,0},{2,1},{3,2},{4,3},{5,4},{6,5},{7,6},{8,7},{9,8},{10,9... | collective-permute-start | bytes 983048 | tf_op jit(solution)/shard_map/ppermute | solution.py:372
  78.2 8.3 %collective-permute-start.14 = (bf16[10,128,128]{2,1,0:T(8,128)(2,1)S(1)}, bf16[10,128,128]{2,1,0:T(8,128)(2,1)S(1)}, u32[]{:S(2)}, u32[]{:S(2)}) collective-permute-start(bf16[10,128,128]{2,1,0:T(8,128)(2,1)S(1)} %get-tuple-element.50), channel_id=1, source_target_pairs={{0,1},{1,2},{2,3},{3,4},{4,5},{5,6},{6,7},{7,8},{8,9},{9,10},{10,1... | collective-permute-start | bytes 983048 | tf_op jit(solution)/shard_map/ppermute | solution.py:372
  80.7 7.5 %collective-permute-start.15 = (bf16[10,128,128]{2,1,0:T(8,128)(2,1)S(1)}, bf16[10,128,128]{2,1,0:T(8,128)(2,1)S(1)}, u32[]{:S(2)}, u32[]{:S(2)}) collective-permute-start(bf16[10,128,128]{2,1,0:T(8,128)(2,1)S(1)} %get-tuple-element.51), channel_id=1, source_target_pairs={{0,15},{1,0},{2,1},{3,2},{4,3},{5,4},{6,5},{7,6},{8,7},{9,8},{10,9... | collective-permute-start | bytes 983048 | tf_op jit(solution)/shard_map/ppermute | solution.py:372

commit v7 on v4

--- a/solution.py
+++ b/solution.py
@@ -129,15 +129,12 @@
             dest[block(f, row + r, col + c)] = jnp.zeros((f.b, f.b), dest.dtype) if i is None else read(i)
 
 
-def pack_edges(f, drop_ref, low, high, to_mate, to_cross):
-    odd = odd_place(f, drop_ref)
-    for i, (lower, upper) in enumerate(zip(under(f.h), over(f.h))):
-        back, forth = low[block(f, *lower)], high[block(f, *upper)]
-        to_mate[block(f, i, 0)] = jnp.where(odd, back, forth)
-        to_cross[block(f, i, 0)] = jnp.where(odd, forth, back)
-
-
-def slabs_kernel(f, drop_ref, own, corner, to_mate, to_cross):
+def pack(f, source, packed, places):
+    for i, (r, c) in enumerate(places):
+        packed[block(f, i, 0)] = source[block(f, r, c)]
+
+
+def slabs_kernel(f, drop_ref, own, corner, corner_again, to_mate, to_cross):
     h = f.h
     odd = odd_place(f, drop_ref)
     n = len(under(h))
@@ -150,14 +147,14 @@
     for i, (r, c) in enumerate(full(h)):
         value = stored(own, r, c - r + h, drop_ref[h + r])
         corner[block(f, i, 0)] = value
+        corner_again[block(f, i, 0)] = value
         to_mate[block(f, n + i, 0)] = value
-        to_cross[block(f, n + i, 0)] = value
 
 
 def forward_kernel(f, drop_ref, cross, *refs):
     h = f.h
     odd = odd_place(f, drop_ref)
-    to_mate, to_far = refs[-2:]
+    to_mate, to_far = refs[-4:-2]
     for i, (lower, upper) in enumerate(zip(under(h), over(h))):
         (r, c), (s, d) = lower, upper
         forth = stored(cross, r, 2 * h + c - r, jnp.where(odd, drop_ref[2 * h + r], drop_ref[r]))
@@ -166,7 +163,7 @@
         to_far[block(f, i, 0)] = jnp.where(odd, forth, back)
 
 
-def square_kernel(f, drop_ref, own, mate, cross, far_mate, far_far, square, shifted, wide):
+def square_kernel(f, drop_ref, own, cross, mate, far_far, far_mate, square, shifted, wide):
     h, p = f.h, f.p
     below, above = sides(f, drop_ref, plain(mate), plain(cross))
     for g, read in enumerate((below, plain(own), above)):
@@ -208,7 +205,7 @@
 
 
 def first_sweep_kernel(
-    f, drop_ref, shifted, corner, sent_mate, sent_cross, mate, cross,
+    f, drop_ref, shifted, corner, sent_mate, sent_cross, mate, cross, unused,
     correction, fresh, partial, whole, before, after,
 ):
     h, p = f.h, f.p
@@ -262,11 +259,16 @@
 
 
 def first_edges_kernel(
-    f, drop_ref, mate, cross, correction, partial, low, high, to_mate, to_cross, before, after
+    f, drop_ref, mate, direct, turned, correction, partial, low, high, to_prev, to_next, before, after
 ):
     p = f.p
-    n = len(under(f.h))
-    below, above = sides(f, drop_ref, indexed(f, mate, n), indexed(f, cross, n))
+    turning = drop_ref[3 * f.h + 1] == 1
+    direct_corner, turned_corner = indexed(f, direct), indexed(f, turned)
+
+    def cross(i):
+        return jnp.where(turning, turned_corner(i), direct_corner(i))
+
+    below, above = sides(f, drop_ref, indexed(f, mate, len(under(f.h))), cross)
     spread(f, before, 0, 0, below, full(f.h))
     spread(f, after, 0, 0, above, full(f.h))
 
@@ -275,7 +277,8 @@
         return partial[at(f, place, place + 1, col - p, col - p + 1)]
 
     edges(f, drop_ref, plain(before), plain(after), correction, start, low, high)
-    pack_edges(f, drop_ref, low, high, to_mate, to_cross)
+    pack(f, low, to_prev, under(f.h))
+    pack(f, high, to_next, over(f.h))
 
 
 def gather(f, whole, low, own, high):
@@ -293,7 +296,7 @@
 
 
 def second_edges_kernel(
-    f, drop_ref, mate, cross, correction, low, high, new_low, new_high, to_mate, to_cross
+    f, drop_ref, corner_below, corner_above, correction, low, high, new_low, new_high, to_prev, to_next
 ):
     p = f.p
 
@@ -308,19 +311,18 @@
                 )
         return total
 
-    below, above = sides(f, drop_ref, plain(mate), plain(cross))
-    edges(f, drop_ref, below, above, correction, start, new_low, new_high)
-    pack_edges(f, drop_ref, new_low, new_high, to_mate, to_cross)
+    edges(f, drop_ref, plain(corner_below), plain(corner_above), correction, start, new_low, new_high)
+    pack(f, new_low, to_prev, under(f.h))
+    pack(f, new_high, to_next, over(f.h))
 
 
 def density_edges_kernel(
-    f, drop_ref, own, mate, cross, correction, new_low, new_high, square, whole, to_mate, to_cross,
+    f, drop_ref, own, from_below, from_above, correction, new_low, new_high, square, whole, to_prev, to_next,
     before, after, low, high,
 ):
     h, p = f.h, f.p
-    below, above = sides(f, drop_ref, indexed(f, mate), indexed(f, cross))
-    spread(f, before, 0, 0, below, over(h))
-    spread(f, after, 0, 0, above, under(h))
+    spread(f, before, 0, 0, indexed(f, from_below), over(h))
+    spread(f, after, 0, 0, indexed(f, from_above), under(h))
     for row, col in f.tiles(f.own_pairs):
         if row not in f.own_pairs:
             continue
@@ -341,7 +343,8 @@
         total = masked(f, right_tile(f, square, whole, row, col), row, col, drop_ref)
         dest, local = (low, row) if row < p else (high, row - 2 * p)
         dest[at(f, local, local + 1, col - p, col - p + 1)] = total.astype(dest.dtype)
-    pack_edges(f, drop_ref, low, high, to_mate, to_cross)
+    pack(f, low, to_prev, under(f.h))
+    pack(f, high, to_next, over(f.h))
 
 
 def density_own_kernel(f, drop_ref, square, whole, out):
@@ -352,9 +355,9 @@
             out[at(f, row - p, row - p + 1, col - p, col - p + 1)] = total.astype(out.dtype)
 
 
-def rows_kernel(f, first, drop_ref, own, mate, cross, out):
+def rows_kernel(f, first, drop_ref, own, from_below, from_above, out):
     h = f.h
-    below, above = sides(f, drop_ref, indexed(f, mate), indexed(f, cross))
+    below, above = indexed(f, from_below), indexed(f, from_above)
     over_index = {place: i for i, place in enumerate(over(h))}
     under_index = {place: i for i, place in enumerate(under(h))}
     for r in range(h):
@@ -377,19 +380,21 @@
 ANY = pl.BlockSpec(memory_space=pl.ANY)
 
 
-def call(kernel, outs, scratch, flops, limit, drop, *args, passed=(), after=()):
+def call(kernel, outs, scratch, flops, limit, drop, *args, passed=(), light=False):
     moved = sum(a.size * a.dtype.itemsize for a in args) + sum(s.size * s.dtype.itemsize for s in outs)
+    if light:
+        flops = moved = 0
     n = len(args)
     return pl.pallas_call(
         kernel,
         out_shape=[*outs, *[jax.ShapeDtypeStruct(a.shape, a.dtype) for a in passed]],
-        in_specs=[SMEM] + [VMEM] * n + [ANY] * (len(passed) + len(after)),
+        in_specs=[SMEM] + [VMEM] * n + [ANY] * len(passed),
         out_specs=[VMEM] * len(outs) + [ANY] * len(passed),
         scratch_shapes=scratch,
         input_output_aliases={1 + n + i: len(outs) + i for i in range(len(passed))},
         compiler_params=pltpu.CompilerParams(vmem_limit_bytes=limit * MIB),
         cost_estimate=pl.CostEstimate(flops=flops, bytes_accessed=moved, transcendentals=0),
-    )(drop, *args, *passed, *after)
+    )(drop, *args, *passed)
 
 
 def routed(x, step):
@@ -400,13 +405,12 @@
 def on_device(density, inverse_start, block_cols):
     rows, width, order, _ = density.shape
     half = width // 2
-    ring = lax.axis_size(RING)
+    ring, inner = lax.axis_size(RING), lax.axis_size(RING[1])
     total = rows * ring
-    assert rows == half and half % 2 == 0 and ring % 2 == 0
+    assert rows == half and half % 2 == 0 and inner % 2 == 0
     f = Frame(half, order)
     kind = density.dtype
     me = lax.axis_index(RING)
-    odd = (me & 1) == 1
 
     def mate_step(i):
         return 1 - 2 * (i % 2)
@@ -420,20 +424,31 @@
     def to_cross(x):
         return routed(x, cross_step)
 
-    def absent(columns, first):
-        ids = first + jnp.arange(columns.shape[0], dtype=jnp.int32)
-        positions = columns - ids[:, None] + half
-        positions = positions + jnp.where(positions < 0, total, jnp.where(positions >= total, -total, 0))
-        return width * (width + 1) // 2 - jnp.sum(positions, axis=1)
-
-    mate_cols, cross_cols = to_mate(block_cols), to_cross(block_cols)
-    density_mate, density_cross = to_mate(density), to_cross(density)
-
-    marks = jnp.reshape(me & 1, (1,))
+    def to_next(x):
+        return routed(x, lambda i: 1)
+
+    def to_prev(x):
+        return routed(x, lambda i: -1)
+
+    def turns(i):
+        return i % inner in (0, inner - 1)
+
+    cross_cols = to_cross(block_cols)
+    density_cross = to_cross(density)
+    mate_cols = to_mate(block_cols)
+    density_mate = to_mate(density)
+
+    even = (me & 1) == 0
     near_cols = jnp.concatenate(
-        [jnp.where(odd, mate_cols, cross_cols), block_cols, jnp.where(odd, cross_cols, mate_cols)], axis=0
-    )
-    drop = jnp.concatenate([absent(near_cols, (me - 1) * rows), marks])
+        [jnp.where(even, cross_cols, mate_cols), block_cols, jnp.where(even, mate_cols, cross_cols)], axis=0
+    )
+    ids = (me - 1) * rows + jnp.arange(3 * rows, dtype=jnp.int32)
+    positions = near_cols - ids[:, None] + half
+    positions = positions + jnp.where(positions < 0, total, jnp.where(positions >= total, -total, 0))
+    absent = width * (width + 1) // 2 - jnp.sum(positions, axis=1)
+    place = lax.axis_index(RING[1])
+    marks = jnp.stack([~even, (place == 0) | (place == inner - 1)]).astype(jnp.int32)
+    drop = jnp.concatenate([absent, marks])
 
     unit = 2 * f.t**3
     count = half * (half + 1) // 2
@@ -450,61 +465,66 @@
     def run(kernel, outs, scratch, tiles, limit, *args, **kw):
         return call(functools.partial(kernel, f), outs, scratch, tiles * unit, limit, *args, **kw)
 
-    corner, slab_mate, slab_cross = run(
-        slabs_kernel, [listed, both, both], [], 0, 12, drop, inverse_start
-    )
-    from_mate, from_cross = to_mate(slab_mate), to_cross(slab_cross)
-    forward_mate, forward_far = run(
-        forward_kernel, [triangle, triangle], [], 0, 8, drop, density_cross, after=(density_mate, from_mate)
+    corner, corner_turning, slab_mate, triangle_cross = run(
+        slabs_kernel, [listed, listed, both, triangle], [], 0, 12, drop, inverse_start
+    )
+    from_mate = to_mate(slab_mate)
+    direct = routed(corner, lambda i: 0 if turns(i) else cross_step(i))
+    forward_mate, forward_far, triangle_cross, corner_turning = run(
+        forward_kernel, [triangle, triangle], [], 0, 12, drop, density_cross, density_mate, from_mate,
+        passed=(triangle_cross, corner_turning),
     )
     far_mate = to_mate(forward_mate)
     far_far = routed(forward_far, lambda i: 3 * cross_step(i))
+    cross_triangle = to_cross(triangle_cross)
+    turned = routed(corner_turning, lambda i: cross_step(i) if turns(i) else 0)
 
     square, shifted = run(
         square_kernel,
         [band, band],
         [pltpu.VMEM((5 * f.group, 5 * f.group), kind)],
-        94, 28, drop, density, density_mate, density_cross, far_mate, far_far,
+        94, 28, drop, density, density_cross, density_mate, far_far, far_mate, light=True,
     )
     correction, own, partial = run(
         first_sweep_kernel,
         [columns, square_group, partial_sums],
         [whole_scratch, group_scratch, group_scratch],
-        66, 24, drop, shifted, corner, slab_mate, slab_cross, from_mate, from_cross,
-    )
-    corner_mate, corner_cross = to_mate(own), to_cross(own)
-    low, high, edge_mate, edge_cross = run(
+        66, 24, drop, shifted, corner, slab_mate, triangle_cross, from_mate, cross_triangle, direct,
+    )
+    next_corner_below, next_corner_above = to_next(own), to_prev(own)
+    low, high, back, forth = run(
         first_edges_kernel,
         [square_group, square_group, triangle, triangle],
         [group_scratch] * 2,
-        10, 16, drop, from_mate, from_cross, correction, partial,
-    )
-    edge_mate, edge_cross = to_mate(edge_mate), to_cross(edge_cross)
+        10, 16, drop, from_mate, direct, turned, correction, partial,
+    )
+    from_above, from_below = to_prev(back), to_next(forth)
     (correction,) = run(
         correction_kernel, [columns], [whole_scratch], 38, 16, drop, shifted, low, own, high
     )
-    new_low, new_high, inverse_mate, inverse_cross = run(
+    new_low, new_high, back, forth = run(
         second_edges_kernel,
         [square_group, square_group, triangle, triangle],
         [],
-        20, 12, drop, corner_mate, corner_cross, correction, low, high,
-    )
-    inverse_mate, inverse_cross = to_mate(inverse_mate), to_cross(inverse_cross)
-    whole, rim_mate, rim_cross = run(
+        20, 12, drop, next_corner_below, next_corner_above, correction, low, high,
+    )
+    inverse_above, inverse_below = to_prev(back), to_next(forth)
+    whole, back, forth = run(
         density_edges_kernel,
         [columns, triangle, triangle],
         [group_scratch] * 4,
-        38, 20, drop, own, edge_mate, edge_cross, correction, new_low, new_high, square,
-    )
-    rim_mate, rim_cross = to_mate(rim_mate), to_cross(rim_cross)
+        38, 20, drop, own, from_below, from_above, correction, new_low, new_high, square,
+    )
+    density_above, density_below = to_prev(back), to_next(forth)
     (density_own,) = run(density_own_kernel, [square_group], [], 18, 12, drop, square, whole)
     out = jax.ShapeDtypeStruct(density.shape, kind)
 
-    def assembled(own, first, mate, cross):
-        return call(functools.partial(rows_kernel, f, first), [out], [], 0, 8, drop, own, mate, cross)[0]
-
-    inverse_next = assembled(whole, half, inverse_mate, inverse_cross)
-    density_next = assembled(density_own, 0, rim_mate, rim_cross)
+    def assembled(own, first, from_below, from_above):
+        kernel = functools.partial(rows_kernel, f, first)
+        return call(kernel, [out], [], 0, 8, drop, own, from_below, from_above)[0]
+
+    inverse_next = assembled(whole, half, inverse_below, inverse_above)
+    density_next = assembled(density_own, 0, density_below, density_above)
     return density_next, inverse_next
 
 

time: 98.8 us -> 91.3 us (0.924)
  the two profiles are of different devices: /device:TPU:1 before, /device:TPU:17 now
where the time goes in v7:
time: 91.3 us; the launch traced here: 91 us
  waiting for transfers between devices  43.6 us (48%)
  starting transfers between devices  22.9 us (25%)
  Pallas kernels  21.5 us (24%)
  local copies, waits for them, and re-layouts  1.23 us (1%)
  other arithmetic  1.03 us (1%)
    ppermute x18, waiting for transfers between devices, routed(): lax.ppermute(x, RING, [(i, (i + step(i)) % size) for i in range(size) if...  43.6 us
    ppermute x18, starting transfers between devices, routed(): lax.ppermute(x, RING, [(i, (i + step(i)) % size) for i in range(size) if...  22.9 us
    pallas_call x11, Pallas kernels, call(): pl.pallas_call(kernel, out_shape=[*outs, *[jax.ShapeDtypeStruct(a.shape,...  21.5 us
  transfers between devices with their start and end apart: 18, of which 6 were waited for; matrix products, arithmetic and copies ran while one was open for 1% of the time, Pallas kernels for 22%

profile of v7, /device:TPU:17, one launch (start us, length us, event | category | flops | bytes accessed | tf_op | source)
XLA Modules:
  0.0 91.0 jit_solution(9924437203773470775)
XLA Ops:
  0.6 1.8 %collective-permute-start = (s32[4,8]{1,0:T(4,128)}, s32[4,8]{1,0:T(4,128)S(1)}, u32[]{:S(2)}, u32[]{:S(2)}) collective-permute-start(s32[4,8]{1,0:T(4,128)} %param.5), channel_id=1, source_target_pairs={{0,15},{1,2},{2,1},{3,4},{4,3},{5,6},{6,5},{7,8},{8,7},{9,10},{10,... | collective-permute-start | bytes 392 | tf_op jit(solution)/shard_map/ppermute | solution.py:402
  2.5 1.7 %collective-permute-start.2 = (bf16[4,8,128,128]{3,2,1,0:T(8,128)(2,1)}, bf16[4,8,128,128]{3,2,1,0:T(8,128)(2,1)S(1)}, u32[]{:S(2)}, u32[]{:S(2)}) collective-permute-start(bf16[4,8,128,128]{3,2,1,0:T(8,128)(2,1)} %own.3), channel_id=1, source_target_pairs={{0,15},{1,2},{2,1},{3,4},{4,3},{5,6},{6,5},{7,8},{8,7},{9,10},{10,... | collective-permute-start | bytes 3145736 | tf_op jit(solution)/shard_map/ppermute | solution.py:402
  5.2 1.2 %copy-done = bf16[4,8,128,128]{3,2,1,0:T(8,128)(2,1)S(1)} copy-done((bf16[4,8,128,128]{3,2,1,0:T(8,128)(2,1)S(1)}, bf16[4,8,128,128]{3,2,1,0:T(8,128)(2,1)}, u32[]{:S(2)}) %copy-start) | copy-done | bytes 1048600
  7.4 1.3 %collective-permute-start.4 = (bf16[3328,128]{1,0:T(8,128)(2,1)S(1)}, bf16[3328,128]{1,0:T(8,128)(2,1)S(1)}, u32[]{:S(2)}, u32[]{:S(2)}) collective-permute-start(bf16[3328,128]{1,0:T(8,128)(2,1)S(1)} %get-tuple-element.26.sent_mate), channel_id=1, source_target_pairs={{0,1},{1,0},{2,3},{3,2},{4,5},{5,4},{6,7},{7,6},{8,9},{9,8},{10,11... | collective-permute-start | bytes 2555912 | tf_op jit(solution)/shard_map/ppermute | solution.py:402
  8.7 2.8 %collective-permute-start.8 = (bf16[2048,128]{1,0:T(8,128)(2,1)S(1)}, bf16[2048,128]{1,0:T(8,128)(2,1)S(1)}, u32[]{:S(2)}, u32[]{:S(2)}) collective-permute-start(bf16[2048,128]{1,0:T(8,128)(2,1)S(1)} %get-tuple-element.33.corner), channel_id=1, source_target_pairs={{1,2},{2,1},{5,6},{6,5},{9,10},{10,9},{13,14},{14,13},{17,18},{18,... | collective-permute-start | bytes 1572872 | tf_op jit(solution)/shard_map/ppermute | solution.py:402
  11.5 16.6 %collective-permute-done.2.cross = bf16[4,8,128,128]{3,2,1,0:T(8,128)(2,1)S(1)} collective-permute-done((bf16[4,8,128,128]{3,2,1,0:T(8,128)(2,1)}, bf16[4,8,128,128]{3,2,1,0:T(8,128)(2,1)S(1)}, u32[]{:S(2)}, u32[]{:S(2)}) %collective-permute-start.2) | collective-permute-done | bytes 1048608 | tf_op jit(solution)/shard_map/ppermute | solution.py:402
  29.5 1.3 %collective-permute-start.7 = (bf16[1280,128]{1,0:T(8,128)(2,1)S(1)}, bf16[1280,128]{1,0:T(8,128)(2,1)S(1)}, u32[]{:S(2)}, u32[]{:S(2)}) collective-permute-start(bf16[1280,128]{1,0:T(8,128)(2,1)S(1)} %get-tuple-element.34.sent_cross), channel_id=1, source_target_pairs={{0,15},{1,2},{2,1},{3,4},{4,3},{5,6},{6,5},{7,8},{8,7},{9,10},{10,... | collective-permute-start | bytes 983048 | tf_op jit(solution)/shard_map/ppermute | solution.py:402
  31.5 6.7 %collective-permute-done.5.far_far = bf16[1280,128]{1,0:T(8,128)(2,1)S(1)} collective-permute-done((bf16[1280,128]{1,0:T(8,128)(2,1)S(1)}, bf16[1280,128]{1,0:T(8,128)(2,1)S(1)}, u32[]{:S(2)}, u32[]{:S(2)}) %collective-permute-start.5) | collective-permute-done | bytes 327712 | tf_op jit(solution)/shard_map/ppermute | solution.py:402
  38.2 4.7 %shard_map.52 = (bf16[1536,1280]{1,0:T(8,128)(2,1)S(1)}, bf16[1536,1280]{1,0:T(8,128)(2,1)S(1)}) custom-call(s32[14]{0:T(128)S(1)} %pad_add_fusion.drop_ref, bf16[4,8,128,128]{3,2,1,0:T(8,128)(2,1)S(1)} %copy-done.1, bf16[4,8,128,128]{3,2,1,0:T(8,128)(2,1)S(1)} %collective-permute-done.2.cross, ...), custom_call_target="tpu_custom_call" | custom-call | tf_op jit(solution)/shard_map/pallas_call | solution.py:388
  42.9 3.1 %shard_map.53 = (bf16[1536,512]{1,0:T(8,128)(2,1)S(1)}, bf16[512,512]{1,0:T(8,128)(2,1)S(1)}, f32[1024,512]{1,0:T(8,128)S(1)}) custom-call(s32[14]{0:T(128)S(1)} %pad_add_fusion.drop_ref, bf16[1536,1280]{1,0:T(8,128)(2,1)S(1)} %get-tuple-element.32.shifted, bf16[2048,128]{1,0:T(8,128)(2,1)S(1)} %get-tuple-element.33.corner, ...), custom_call_target="tpu_custom_call" | custom-call | flops 2214592512 | bytes 11534336 | tf_op jit(solution)/shard_map/pallas_call | solution.py:388
  46.1 1.1 %collective-permute-start.13 = (bf16[512,512]{1,0:T(8,128)(2,1)S(1)}, bf16[512,512]{1,0:T(8,128)(2,1)S(1)}, u32[]{:S(2)}, u32[]{:S(2)}) collective-permute-start(bf16[512,512]{1,0:T(8,128)(2,1)S(1)} %get-tuple-element.35.own), channel_id=1, source_target_pairs={{0,15},{1,0},{2,1},{3,2},{4,3},{5,4},{6,5},{7,6},{8,7},{9,8},{10,9... | collective-permute-start | bytes 1572872 | tf_op jit(solution)/shard_map/ppermute | solution.py:402
  47.1 8.7 %collective-permute-start.12 = (bf16[512,512]{1,0:T(8,128)(2,1)S(1)}, bf16[512,512]{1,0:T(8,128)(2,1)S(1)}, u32[]{:S(2)}, u32[]{:S(2)}) collective-permute-start(bf16[512,512]{1,0:T(8,128)(2,1)S(1)} %get-tuple-element.35.own), channel_id=1, source_target_pairs={{0,1},{1,2},{2,3},{3,4},{4,5},{5,6},{6,7},{7,8},{8,9},{9,10},{10,1... | collective-permute-start | bytes 1572872 | tf_op jit(solution)/shard_map/ppermute | solution.py:402
  55.8 1.5 %shard_map.54 = (bf16[512,512]{1,0:T(8,128)(2,1)S(1)}, bf16[512,512]{1,0:T(8,128)(2,1)S(1)}, bf16[1280,128]{1,0:T(8,128)(2,1)S(1)}, bf16[1280,128]{1,0:T(8,128)(2,1)S(1)}) custom-call(s32[14]{0:T(128)S(1)} %pad_add_fusion.drop_ref, bf16[3328,128]{1,0:T(8,128)(2,1)S(1)} %collective-permute-done.4.refs_1_.mate, ...), custom_call_target="tpu_custom_call" | custom-call | flops 335544320 | bytes 7274496 | tf_op jit(solution)/shard_map/pallas_call | solution.py:388
  57.8 1.3 %collective-permute-start.11 = (bf16[1280,128]{1,0:T(8,128)(2,1)S(1)}, bf16[1280,128]{1,0:T(8,128)(2,1)S(1)}, u32[]{:S(2)}, u32[]{:S(2)}) collective-permute-start(bf16[1280,128]{1,0:T(8,128)(2,1)S(1)} %get-tuple-element.40), channel_id=1, source_target_pairs={{0,15},{1,0},{2,1},{3,2},{4,3},{5,4},{6,5},{7,6},{8,7},{9,8},{10,9... | collective-permute-start | bytes 983048 | tf_op jit(solution)/shard_map/ppermute | solution.py:402
  59.1 2.0 %shard_map.55.correction = bf16[1536,512]{1,0:T(8,128)(2,1)S(1)} custom-call(s32[14]{0:T(128)S(1)} %pad_add_fusion.drop_ref, bf16[1536,1280]{1,0:T(8,128)(2,1)S(1)} %get-tuple-element.32.shifted, bf16[512,512]{1,0:T(8,128)(2,1)S(1)} %get-tuple-element.41.low, bf16[512,512]{1,0:T(8,128)(2,1)S(1)} %get-tuple-element.35.own, ...), custom_call_target="tpu_custom_call" | custom-call | flops 1275068416 | bytes 7077888 | tf_op jit(solution)/shard_map/pallas_call | solution.py:388
  61.1 10.7 %collective-permute-done.13.corner_above = bf16[512,512]{1,0:T(8,128)(2,1)S(1)} collective-permute-done((bf16[512,512]{1,0:T(8,128)(2,1)S(1)}, bf16[512,512]{1,0:T(8,128)(2,1)S(1)}, u32[]{:S(2)}, u32[]{:S(2)}) %collective-permute-start.13) | collective-permute-done | bytes 524320 | tf_op jit(solution)/shard_map/ppermute | solution.py:402
  71.8 1.5 %shard_map.56 = (bf16[512,512]{1,0:T(8,128)(2,1)S(1)}, bf16[512,512]{1,0:T(8,128)(2,1)S(1)}, bf16[1280,128]{1,0:T(8,128)(2,1)S(1)}, bf16[1280,128]{1,0:T(8,128)(2,1)S(1)}) custom-call(s32[14]{0:T(128)S(1)} %pad_add_fusion.drop_ref, bf16[512,512]{1,0:T(8,128)(2,1)S(1)} %collective-permute-done.12.corner_below, ...), custom_call_target="tpu_custom_call" | custom-call | flops 671088640 | bytes 5373952 | tf_op jit(solution)/shard_map/pallas_call | solution.py:388
  73.9 4.9 %collective-permute-done.11.from_above = bf16[1280,128]{1,0:T(8,128)(2,1)S(1)} collective-permute-done((bf16[1280,128]{1,0:T(8,128)(2,1)S(1)}, bf16[1280,128]{1,0:T(8,128)(2,1)S(1)}, u32[]{:S(2)}, u32[]{:S(2)}) %collective-permute-start.11) | collective-permute-done | bytes 327712 | tf_op jit(solution)/shard_map/ppermute | solution.py:402
  78.8 2.2 %shard_map.57 = (bf16[1536,512]{1,0:T(8,128)(2,1)S(1)}, bf16[1280,128]{1,0:T(8,128)(2,1)S(1)}, bf16[1280,128]{1,0:T(8,128)(2,1)S(1)}) custom-call(s32[14]{0:T(128)S(1)} %pad_add_fusion.drop_ref, bf16[512,512]{1,0:T(8,128)(2,1)S(1)} %get-tuple-element.35.own, bf16[1280,128]{1,0:T(8,128)(2,1)S(1)} %collective-permute-done.10.from_below, ...), custom_call_target="tpu_custom_call" | custom-call | flops 1275068416 | bytes 9961472 | tf_op jit(solution)/shard_map/pallas_call | solution.py:388
  81.6 1.3 %shard_map.58.own = bf16[512,512]{1,0:T(8,128)(2,1)S(1)} custom-call(s32[14]{0:T(128)S(1)} %pad_add_fusion.drop_ref, bf16[1536,1280]{1,0:T(8,128)(2,1)S(1)} %get-tuple-element.31.square, bf16[1536,512]{1,0:T(8,128)(2,1)S(1)} %get-tuple-element.45.whole.own), custom_call_target="tpu_custom_call" | custom-call | flops 603979776 | bytes 6029312 | tf_op jit(solution)/shard_map/pallas_call | solution.py:388
  82.9 2.9 %collective-permute-done.17.from_above = bf16[1280,128]{1,0:T(8,128)(2,1)S(1)} collective-permute-done((bf16[1280,128]{1,0:T(8,128)(2,1)S(1)}, bf16[1280,128]{1,0:T(8,128)(2,1)S(1)}, u32[]{:S(2)}, u32[]{:S(2)}) %collective-permute-start.17) | collective-permute-done | bytes 327712 | tf_op jit(solution)/shard_map/ppermute | solution.py:402
  85.8 1.7 %shard_map.60 = bf16[4,8,128,128]{3,2,1,0:T(8,128)(2,1)} custom-call(s32[14]{0:T(128)S(1)} %pad_add_fusion.drop_ref, bf16[1536,512]{1,0:T(8,128)(2,1)S(1)} %get-tuple-element.45.whole.own, bf16[1280,128]{1,0:T(8,128)(2,1)S(1)} %collective-permute-done.16.from_below, bf16[1280,128]{1,0:T(8,128)(2,1)S(1)} %collective-permute-done.17.from_above), custom_call_target="tpu_custom_call" | custom-call | bytes 3276800 | tf_op jit(solution)/shard_map/pallas_call | solution.py:388
  87.5 1.8 %collective-permute-done.15.from_above = bf16[1280,128]{1,0:T(8,128)(2,1)S(1)} collective-permute-done((bf16[1280,128]{1,0:T(8,128)(2,1)S(1)}, bf16[1280,128]{1,0:T(8,128)(2,1)S(1)}, u32[]{:S(2)}, u32[]{:S(2)}) %collective-permute-start.15) | collective-permute-done | bytes 327712 | tf_op jit(solution)/shard_map/ppermute | solution.py:402
  89.3 1.7 %shard_map.59 = bf16[4,8,128,128]{3,2,1,0:T(8,128)(2,1)} custom-call(s32[14]{0:T(128)S(1)} %pad_add_fusion.drop_ref, bf16[512,512]{1,0:T(8,128)(2,1)S(1)} %shard_map.58.own, bf16[1280,128]{1,0:T(8,128)(2,1)S(1)} %collective-permute-done.14.from_below, bf16[1280,128]{1,0:T(8,128)(2,1)S(1)} %collective-permute-done.15.from_above), custom_call_target="tpu_custom_call" | custom-call | bytes 2228224 | tf_op jit(solution)/shard_map/pallas_call | solution.py:388
  (33 shorter events, 5.6 us)
Async XLA Ops:
  0.6 3.6 %collective-permute-start = (s32[4,8]{1,0:T(4,128)}, s32[4,8]{1,0:T(4,128)S(1)}, u32[]{:S(2)}, u32[]{:S(2)}) collective-permute-start(s32[4,8]{1,0:T(4,128)} %param.5), channel_id=1, source_target_pairs={{0,15},{1,2},{2,1},{3,4},{4,3},{5,6},{6,5},{7,8},{8,7},{9,10},{10,... | collective-permute-start | bytes 392 | tf_op jit(solution)/shard_map/ppermute | solution.py:402
  2.5 1.8 %collective-permute-start.1 = (s32[4,8]{1,0:T(4,128)}, s32[4,8]{1,0:T(4,128)S(1)}, u32[]{:S(2)}, u32[]{:S(2)}) collective-permute-start(s32[4,8]{1,0:T(4,128)} %param.5), channel_id=1, source_target_pairs={{0,1},{1,0},{2,3},{3,2},{4,5},{5,4},{6,7},{7,6},{8,9},{9,8},{10,11... | collective-permute-start | bytes 392 | tf_op jit(solution)/shard_map/ppermute | solution.py:402
  2.5 25.7 %collective-permute-start.2 = (bf16[4,8,128,128]{3,2,1,0:T(8,128)(2,1)}, bf16[4,8,128,128]{3,2,1,0:T(8,128)(2,1)S(1)}, u32[]{:S(2)}, u32[]{:S(2)}) collective-permute-start(bf16[4,8,128,128]{3,2,1,0:T(8,128)(2,1)} %own.3), channel_id=1, source_target_pairs={{0,15},{1,2},{2,1},{3,4},{4,3},{5,6},{6,5},{7,8},{8,7},{9,10},{10,... | collective-permute-start | bytes 3145736 | tf_op jit(solution)/shard_map/ppermute | solution.py:402
  4.1 24.0 %collective-permute-start.3 = (bf16[4,8,128,128]{3,2,1,0:T(8,128)(2,1)}, bf16[4,8,128,128]{3,2,1,0:T(8,128)(2,1)S(1)}, u32[]{:S(2)}, u32[]{:S(2)}) collective-permute-start(bf16[4,8,128,128]{3,2,1,0:T(8,128)(2,1)} %own.3), channel_id=1, source_target_pairs={{0,1},{1,0},{2,3},{3,2},{4,5},{5,4},{6,7},{7,6},{8,9},{9,8},{10,11... | collective-permute-start | bytes 3145736 | tf_op jit(solution)/shard_map/ppermute | solution.py:402
  5.2 1.2 %copy-start = (bf16[4,8,128,128]{3,2,1,0:T(8,128)(2,1)S(1)}, bf16[4,8,128,128]{3,2,1,0:T(8,128)(2,1)}, u32[]{:S(2)}) copy-start(bf16[4,8,128,128]{3,2,1,0:T(8,128)(2,1)} %own.2) | copy-start | bytes 3145732
  7.3 30.9 %copy-start.1 = (bf16[4,8,128,128]{3,2,1,0:T(8,128)(2,1)S(1)}, bf16[4,8,128,128]{3,2,1,0:T(8,128)(2,1)}, u32[]{:S(2)}) copy-start(bf16[4,8,128,128]{3,2,1,0:T(8,128)(2,1)} %own.3) | copy-start | bytes 3145732
  7.4 4.2 %collective-permute-start.4 = (bf16[3328,128]{1,0:T(8,128)(2,1)S(1)}, bf16[3328,128]{1,0:T(8,128)(2,1)S(1)}, u32[]{:S(2)}, u32[]{:S(2)}) collective-permute-start(bf16[3328,128]{1,0:T(8,128)(2,1)S(1)} %get-tuple-element.26.sent_mate), channel_id=1, source_target_pairs={{0,1},{1,0},{2,3},{3,2},{4,5},{5,4},{6,7},{7,6},{8,9},{9,8},{10,11... | collective-permute-start | bytes 2555912 | tf_op jit(solution)/shard_map/ppermute | solution.py:402
  8.7 34.2 %collective-permute-start.8 = (bf16[2048,128]{1,0:T(8,128)(2,1)S(1)}, bf16[2048,128]{1,0:T(8,128)(2,1)S(1)}, u32[]{:S(2)}, u32[]{:S(2)}) collective-permute-start(bf16[2048,128]{1,0:T(8,128)(2,1)S(1)} %get-tuple-element.33.corner), channel_id=1, source_target_pairs={{1,2},{2,1},{5,6},{6,5},{9,10},{10,9},{13,14},{14,13},{17,18},{18,... | collective-permute-start | bytes 1572872 | tf_op jit(solution)/shard_map/ppermute | solution.py:402
  28.9 9.3 %collective-permute-start.5 = (bf16[1280,128]{1,0:T(8,128)(2,1)S(1)}, bf16[1280,128]{1,0:T(8,128)(2,1)S(1)}, u32[]{:S(2)}, u32[]{:S(2)}) collective-permute-start(bf16[1280,128]{1,0:T(8,128)(2,1)S(1)} %get-tuple-element.29), channel_id=1, source_target_pairs={{0,13},{1,4},{2,15},{3,6},{4,1},{5,8},{6,3},{7,10},{8,5},{9,12},{1... | collective-permute-start | bytes 983048 | tf_op jit(solution)/shard_map/ppermute | solution.py:402
  28.9 9.3 %collective-permute-start.6 = (bf16[1280,128]{1,0:T(8,128)(2,1)S(1)}, bf16[1280,128]{1,0:T(8,128)(2,1)S(1)}, u32[]{:S(2)}, u32[]{:S(2)}) collective-permute-start(bf16[1280,128]{1,0:T(8,128)(2,1)S(1)} %get-tuple-element.30), channel_id=1, source_target_pairs={{0,1},{1,0},{2,3},{3,2},{4,5},{5,4},{6,7},{7,6},{8,9},{9,8},{10,11... | collective-permute-start | bytes 983048 | tf_op jit(solution)/shard_map/ppermute | solution.py:402
  29.5 13.4 %collective-permute-start.7 = (bf16[1280,128]{1,0:T(8,128)(2,1)S(1)}, bf16[1280,128]{1,0:T(8,128)(2,1)S(1)}, u32[]{:S(2)}, u32[]{:S(2)}) collective-permute-start(bf16[1280,128]{1,0:T(8,128)(2,1)S(1)} %get-tuple-element.34.sent_cross), channel_id=1, source_target_pairs={{0,15},{1,2},{2,1},{3,4},{4,3},{5,6},{6,5},{7,8},{8,7},{9,10},{10,... | collective-permute-start | bytes 983048 | tf_op jit(solution)/shard_map/ppermute | solution.py:402
  30.8 25.0 %collective-permute-start.9 = (bf16[2048,128]{1,0:T(8,128)(2,1)S(1)}, bf16[2048,128]{1,0:T(8,128)(2,1)S(1)}, u32[]{:S(2)}, u32[]{:S(2)}) collective-permute-start(bf16[2048,128]{1,0:T(8,128)(2,1)S(1)} %get-tuple-element.36), channel_id=1, source_target_pairs={{0,15},{3,4},{4,3},{7,8},{8,7},{11,12},{12,11},{15,0},{16,31},{19,... | collective-permute-start | bytes 1572872 | tf_op jit(solution)/shard_map/ppermute | solution.py:402
  46.1 25.7 %collective-permute-start.13 = (bf16[512,512]{1,0:T(8,128)(2,1)S(1)}, bf16[512,512]{1,0:T(8,128)(2,1)S(1)}, u32[]{:S(2)}, u32[]{:S(2)}) collective-permute-start(bf16[512,512]{1,0:T(8,128)(2,1)S(1)} %get-tuple-element.35.own), channel_id=1, source_target_pairs={{0,15},{1,0},{2,1},{3,2},{4,3},{5,4},{6,5},{7,6},{8,7},{9,8},{10,9... | collective-permute-start | bytes 1572872 | tf_op jit(solution)/shard_map/ppermute | solution.py:402
  47.1 24.6 %collective-permute-start.12 = (bf16[512,512]{1,0:T(8,128)(2,1)S(1)}, bf16[512,512]{1,0:T(8,128)(2,1)S(1)}, u32[]{:S(2)}, u32[]{:S(2)}) collective-permute-start(bf16[512,512]{1,0:T(8,128)(2,1)S(1)} %get-tuple-element.35.own), channel_id=1, source_target_pairs={{0,1},{1,2},{2,3},{3,4},{4,5},{5,6},{6,7},{7,8},{8,9},{9,10},{10,1... | collective-permute-start | bytes 1572872 | tf_op jit(solution)/shard_map/ppermute | solution.py:402
  57.3 16.6 %collective-permute-start.10 = (bf16[1280,128]{1,0:T(8,128)(2,1)S(1)}, bf16[1280,128]{1,0:T(8,128)(2,1)S(1)}, u32[]{:S(2)}, u32[]{:S(2)}) collective-permute-start(bf16[1280,128]{1,0:T(8,128)(2,1)S(1)} %get-tuple-element.39), channel_id=1, source_target_pairs={{0,1},{1,2},{2,3},{3,4},{4,5},{5,6},{6,7},{7,8},{8,9},{9,10},{10,1... | collective-permute-start | bytes 983048 | tf_op jit(solution)/shard_map/ppermute | solution.py:402
  57.8 21.0 %collective-permute-start.11 = (bf16[1280,128]{1,0:T(8,128)(2,1)S(1)}, bf16[1280,128]{1,0:T(8,128)(2,1)S(1)}, u32[]{:S(2)}, u32[]{:S(2)}) collective-permute-start(bf16[1280,128]{1,0:T(8,128)(2,1)S(1)} %get-tuple-element.40), channel_id=1, source_target_pairs={{0,15},{1,0},{2,1},{3,2},{4,3},{5,4},{6,5},{7,6},{8,7},{9,8},{10,9... | collective-permute-start | bytes 983048 | tf_op jit(solution)/shard_map/ppermute | solution.py:402
  73.3 9.6 %collective-permute-start.16 = (bf16[1280,128]{1,0:T(8,128)(2,1)S(1)}, bf16[1280,128]{1,0:T(8,128)(2,1)S(1)}, u32[]{:S(2)}, u32[]{:S(2)}) collective-permute-start(bf16[1280,128]{1,0:T(8,128)(2,1)S(1)} %get-tuple-element.48), channel_id=1, source_target_pairs={{0,1},{1,2},{2,3},{3,4},{4,5},{5,6},{6,7},{7,8},{8,9},{9,10},{10,1... | collective-permute-start | bytes 983048 | tf_op jit(solution)/shard_map/ppermute | solution.py:402
  73.4 12.4 %collective-permute-start.17 = (bf16[1280,128]{1,0:T(8,128)(2,1)S(1)}, bf16[1280,128]{1,0:T(8,128)(2,1)S(1)}, u32[]{:S(2)}, u32[]{:S(2)}) collective-permute-start(bf16[1280,128]{1,0:T(8,128)(2,1)S(1)} %get-tuple-element.49), channel_id=1, source_target_pairs={{0,15},{1,0},{2,1},{3,2},{4,3},{5,4},{6,5},{7,6},{8,7},{9,8},{10,9... | collective-permute-start | bytes 983048 | tf_op jit(solution)/shard_map/ppermute | solution.py:402
  81.0 6.5 %collective-permute-start.14 = (bf16[1280,128]{1,0:T(8,128)(2,1)S(1)}, bf16[1280,128]{1,0:T(8,128)(2,1)S(1)}, u32[]{:S(2)}, u32[]{:S(2)}) collective-permute-start(bf16[1280,128]{1,0:T(8,128)(2,1)S(1)} %get-tuple-element.46), channel_id=1, source_target_pairs={{0,1},{1,2},{2,3},{3,4},{4,5},{5,6},{6,7},{7,8},{8,9},{9,10},{10,1... | collective-permute-start | bytes 983048 | tf_op jit(solution)/shard_map/ppermute | solution.py:402
  81.1 8.2 %collective-permute-start.15 = (bf16[1280,128]{1,0:T(8,128)(2,1)S(1)}, bf16[1280,128]{1,0:T(8,128)(2,1)S(1)}, u32[]{:S(2)}, u32[]{:S(2)}) collective-permute-start(bf16[1280,128]{1,0:T(8,128)(2,1)S(1)} %get-tuple-element.47), channel_id=1, source_target_pairs={{0,15},{1,0},{2,1},{3,2},{4,3},{5,4},{6,5},{7,6},{8,7},{9,8},{10,9... | collective-permute-start | bytes 983048 | tf_op jit(solution)/shard_map/ppermute | solution.py:402

commit v8 on v7

--- a/solution.py
+++ b/solution.py
@@ -136,16 +136,16 @@
 
 def slabs_kernel(f, drop_ref, own, corner, corner_again, to_mate, to_cross):
     h = f.h
-    odd = odd_place(f, drop_ref)
+    odd = drop_ref[h] == 1
     n = len(under(h))
     for i, (lower, upper) in enumerate(zip(under(h), over(h))):
         (r, c), (s, d) = lower, upper
-        forth = stored(own, r, 2 * h + c - r, drop_ref[h + r])
-        back = stored(own, s, d - s, drop_ref[h + s])
+        forth = stored(own, r, 2 * h + c - r, drop_ref[r])
+        back = stored(own, s, d - s, drop_ref[s])
         to_mate[block(f, i, 0)] = jnp.where(odd, back, forth)
         to_cross[block(f, i, 0)] = jnp.where(odd, forth, back)
     for i, (r, c) in enumerate(full(h)):
-        value = stored(own, r, c - r + h, drop_ref[h + r])
+        value = stored(own, r, c - r + h, drop_ref[r])
         corner[block(f, i, 0)] = value
         corner_again[block(f, i, 0)] = value
         to_mate[block(f, n + i, 0)] = value
@@ -205,7 +205,7 @@
 
 
 def first_sweep_kernel(
-    f, drop_ref, shifted, corner, sent_mate, sent_cross, mate, cross, unused,
+    f, drop_ref, shifted, corner, sent_mate, sent_cross, mate, cross,
     correction, fresh, partial, whole, before, after,
 ):
     h, p = f.h, f.p
@@ -259,16 +259,10 @@
 
 
 def first_edges_kernel(
-    f, drop_ref, mate, direct, turned, correction, partial, low, high, to_prev, to_next, before, after
+    f, drop_ref, mate, cross, correction, partial, low, high, to_prev, to_next, before, after
 ):
     p = f.p
-    turning = drop_ref[3 * f.h + 1] == 1
-    direct_corner, turned_corner = indexed(f, direct), indexed(f, turned)
-
-    def cross(i):
-        return jnp.where(turning, turned_corner(i), direct_corner(i))
-
-    below, above = sides(f, drop_ref, indexed(f, mate, len(under(f.h))), cross)
+    below, above = sides(f, drop_ref, indexed(f, mate, len(under(f.h))), indexed(f, cross))
     spread(f, before, 0, 0, below, full(f.h))
     spread(f, after, 0, 0, above, full(f.h))
 
@@ -405,9 +399,9 @@
 def on_device(density, inverse_start, block_cols):
     rows, width, order, _ = density.shape
     half = width // 2
-    ring, inner = lax.axis_size(RING), lax.axis_size(RING[1])
+    ring = lax.axis_size(RING)
     total = rows * ring
-    assert rows == half and half % 2 == 0 and inner % 2 == 0
+    assert rows == half and half % 2 == 0 and ring % 2 == 0
     f = Frame(half, order)
     kind = density.dtype
     me = lax.axis_index(RING)
@@ -430,25 +424,18 @@
     def to_prev(x):
         return routed(x, lambda i: -1)
 
-    def turns(i):
-        return i % inner in (0, inner - 1)
-
-    cross_cols = to_cross(block_cols)
-    density_cross = to_cross(density)
-    mate_cols = to_mate(block_cols)
-    density_mate = to_mate(density)
-
+    positions = block_cols - (me * rows + jnp.arange(rows, dtype=jnp.int32))[:, None] + half
+    positions = positions + jnp.where(positions < 0, total, jnp.where(positions >= total, -total, 0))
+    own_drop = width * (width + 1) // 2 - jnp.sum(positions, axis=1)
+
+    density_cross, density_mate = to_cross(density), to_mate(density)
+    cross_drop, mate_drop = to_cross(own_drop), to_mate(own_drop)
     even = (me & 1) == 0
-    near_cols = jnp.concatenate(
-        [jnp.where(even, cross_cols, mate_cols), block_cols, jnp.where(even, mate_cols, cross_cols)], axis=0
-    )
-    ids = (me - 1) * rows + jnp.arange(3 * rows, dtype=jnp.int32)
-    positions = near_cols - ids[:, None] + half
-    positions = positions + jnp.where(positions < 0, total, jnp.where(positions >= total, -total, 0))
-    absent = width * (width + 1) // 2 - jnp.sum(positions, axis=1)
-    place = lax.axis_index(RING[1])
-    marks = jnp.stack([~even, (place == 0) | (place == inner - 1)]).astype(jnp.int32)
-    drop = jnp.concatenate([absent, marks])
+    mark = jnp.reshape(me & 1, (1,))
+    start_drop = jnp.concatenate([own_drop, mark])
+    drop = jnp.concatenate(
+        [jnp.where(even, cross_drop, mate_drop), own_drop, jnp.where(even, mate_drop, cross_drop), mark]
+    )
 
     unit = 2 * f.t**3
     count = half * (half + 1) // 2
@@ -465,19 +452,18 @@
     def run(kernel, outs, scratch, tiles, limit, *args, **kw):
         return call(functools.partial(kernel, f), outs, scratch, tiles * unit, limit, *args, **kw)
 
-    corner, corner_turning, slab_mate, triangle_cross = run(
-        slabs_kernel, [listed, listed, both, triangle], [], 0, 12, drop, inverse_start
+    corner, corner_cross, slab_mate, triangle_cross = run(
+        slabs_kernel, [listed, listed, both, triangle], [], 0, 12, start_drop, inverse_start
     )
     from_mate = to_mate(slab_mate)
-    direct = routed(corner, lambda i: 0 if turns(i) else cross_step(i))
-    forward_mate, forward_far, triangle_cross, corner_turning = run(
+    forward_mate, forward_far, triangle_cross, corner_cross = run(
         forward_kernel, [triangle, triangle], [], 0, 12, drop, density_cross, density_mate, from_mate,
-        passed=(triangle_cross, corner_turning),
+        passed=(triangle_cross, corner_cross),
     )
     far_mate = to_mate(forward_mate)
     far_far = routed(forward_far, lambda i: 3 * cross_step(i))
     cross_triangle = to_cross(triangle_cross)
-    turned = routed(corner_turning, lambda i: cross_step(i) if turns(i) else 0)
+    cross_corner = to_cross(corner_cross)
 
     square, shifted = run(
         square_kernel,
@@ -489,14 +475,14 @@
         first_sweep_kernel,
         [columns, square_group, partial_sums],
         [whole_scratch, group_scratch, group_scratch],
-        66, 24, drop, shifted, corner, slab_mate, triangle_cross, from_mate, cross_triangle, direct,
+        66, 24, drop, shifted, corner, slab_mate, triangle_cross, from_mate, cross_triangle,
     )
     next_corner_below, next_corner_above = to_next(own), to_prev(own)
     low, high, back, forth = run(
         first_edges_kernel,
         [square_group, square_group, triangle, triangle],
         [group_scratch] * 2,
-        10, 16, drop, from_mate, direct, turned, correction, partial,
+        10, 16, drop, from_mate, cross_corner, correction, partial,
     )
     from_above, from_below = to_prev(back), to_next(forth)
     (correction,) = run(

time: 91.3 us -> 89.5 us (0.980)
  the two profiles are of different devices: /device:TPU:17 before, /device:TPU:1 now
where the time goes in v8:
time: 89.5 us; the launch traced here: 89.3 us
  waiting for transfers between devices  43.5 us (49%)
  Pallas kernels  23.1 us (26%)
  starting transfers between devices  18.9 us (21%)
  local copies, waits for them, and re-layouts  2.03 us (2%)
  other arithmetic  1.04 us (1%)
    ppermute x17, waiting for transfers between devices, routed(): lax.ppermute(x, RING, [(i, (i + step(i)) % size) for i in range(size) if...  43.5 us
    pallas_call x11, Pallas kernels, call(): pl.pallas_call(kernel, out_shape=[*outs, *[jax.ShapeDtypeStruct(a.shape,...  23.1 us
    ppermute x17, starting transfers between devices, routed(): lax.ppermute(x, RING, [(i, (i + step(i)) % size) for i in range(size) if...  18.9 us
    unnamed x8, local copies, waits for them, and re-layouts  2.03 us
  transfers between devices with their start and end apart: 17, of which 9 were waited for; matrix products, arithmetic and copies ran while one was open for 1% of the time, Pallas kernels for 23%

profile of v8, /device:TPU:1, one launch (start us, length us, event | category | flops | bytes accessed | tf_op | source)
XLA Modules:
  0.0 89.3 jit_solution(13226127457073150665)
XLA Ops:
  0.6 2.7 %collective-permute-start.2 = (bf16[4,8,128,128]{3,2,1,0:T(8,128)(2,1)}, bf16[4,8,128,128]{3,2,1,0:T(8,128)(2,1)S(1)}, u32[]{:S(2)}, u32[]{:S(2)}) collective-permute-start(bf16[4,8,128,128]{3,2,1,0:T(8,128)(2,1)} %own.3), channel_id=1, source_target_pairs={{0,15},{1,2},{2,1},{3,4},{4,3},{5,6},{6,5},{7,8},{8,7},{9,10},{10,... | collective-permute-start | bytes 3145736 | tf_op jit(solution)/shard_map/ppermute | solution.py:396
  3.3 2.9 %collective-permute-start.3 = (bf16[4,8,128,128]{3,2,1,0:T(8,128)(2,1)}, bf16[4,8,128,128]{3,2,1,0:T(8,128)(2,1)S(1)}, u32[]{:S(2)}, u32[]{:S(2)}) collective-permute-start(bf16[4,8,128,128]{3,2,1,0:T(8,128)(2,1)} %own.3), channel_id=1, source_target_pairs={{0,1},{1,0},{2,3},{3,2},{4,5},{5,4},{6,7},{7,6},{8,9},{9,8},{10,11... | collective-permute-start | bytes 3145736 | tf_op jit(solution)/shard_map/ppermute | solution.py:396
  8.4 1.9 %shard_map.50 = (bf16[2048,128]{1,0:T(8,128)(2,1)S(1)}, bf16[2048,128]{1,0:T(8,128)(2,1)S(1)}, bf16[3328,128]{1,0:T(8,128)(2,1)}, bf16[1280,128]{1,0:T(8,128)(2,1)}) custom-call(s32[5]{0:T(128)S(1)} %pad_add_fusion.1.drop_ref, bf16[4,8,128,128]{3,2,1,0:T(8,128)(2,1)S(1)} %copy-done), custom_call_target="tpu_custom_call" | custom-call | bytes 3276800 | tf_op jit(solution)/shard_map/pallas_call | solution.py:382
  11.6 1.5 %collective-permute-done.1 = s32[4]{0:T(128)S(1)} collective-permute-done((s32[4]{0:T(128)S(1)}, s32[4]{0:T(128)S(1)}, u32[]{:S(2)}, u32[]{:S(2)}) %collective-permute-start.1) | collective-permute-done | bytes 48 | tf_op jit(solution)/shard_map/ppermute | solution.py:396
  13.1 14.2 %collective-permute-done = s32[4]{0:T(128)S(1)} collective-permute-done((s32[4]{0:T(128)S(1)}, s32[4]{0:T(128)S(1)}, u32[]{:S(2)}, u32[]{:S(2)}) %collective-permute-start) | collective-permute-done | bytes 48 | tf_op jit(solution)/shard_map/ppermute | solution.py:396
  28.2 3.7 %collective-permute-start.6 = (bf16[1280,128]{1,0:T(8,128)(2,1)S(1)}, bf16[1280,128]{1,0:T(8,128)(2,1)S(1)}, u32[]{:S(2)}, u32[]{:S(2)}) collective-permute-start(bf16[1280,128]{1,0:T(8,128)(2,1)S(1)} %get-tuple-element.30), channel_id=1, source_target_pairs={{0,1},{1,0},{2,3},{3,2},{4,5},{5,4},{6,7},{7,6},{8,9},{9,8},{10,11... | collective-permute-start | bytes 983048 | tf_op jit(solution)/shard_map/ppermute | solution.py:396
  31.9 1.7 %collective-permute-start.8 = (bf16[2048,128]{1,0:T(8,128)(2,1)S(1)}, bf16[2048,128]{1,0:T(8,128)(2,1)S(1)}, u32[]{:S(2)}, u32[]{:S(2)}) collective-permute-start(bf16[2048,128]{1,0:T(8,128)(2,1)S(1)} %get-tuple-element.36), channel_id=1, source_target_pairs={{0,15},{1,2},{2,1},{3,4},{4,3},{5,6},{6,5},{7,8},{8,7},{9,10},{10,... | collective-permute-start | bytes 1572872 | tf_op jit(solution)/shard_map/ppermute | solution.py:396
  33.7 4.2 %collective-permute-done.5.far_far = bf16[1280,128]{1,0:T(8,128)(2,1)S(1)} collective-permute-done((bf16[1280,128]{1,0:T(8,128)(2,1)S(1)}, bf16[1280,128]{1,0:T(8,128)(2,1)S(1)}, u32[]{:S(2)}, u32[]{:S(2)}) %collective-permute-start.5) | collective-permute-done | bytes 327712 | tf_op jit(solution)/shard_map/ppermute | solution.py:396
  37.9 4.7 %shard_map.52 = (bf16[1536,1280]{1,0:T(8,128)(2,1)S(1)}, bf16[1536,1280]{1,0:T(8,128)(2,1)S(1)}) custom-call(s32[13]{0:T(128)S(1)} %pad_add_fusion.drop_ref, bf16[4,8,128,128]{3,2,1,0:T(8,128)(2,1)S(1)} %copy-done.1, bf16[4,8,128,128]{3,2,1,0:T(8,128)(2,1)S(1)} %collective-permute-done.2.cross, ...), custom_call_target="tpu_custom_call" | custom-call | tf_op jit(solution)/shard_map/pallas_call | solution.py:382
  42.6 3.8 %shard_map.53 = (bf16[1536,512]{1,0:T(8,128)(2,1)S(1)}, bf16[512,512]{1,0:T(8,128)(2,1)S(1)}, f32[1024,512]{1,0:T(8,128)S(1)}) custom-call(s32[13]{0:T(128)S(1)} %pad_add_fusion.drop_ref, bf16[1536,1280]{1,0:T(8,128)(2,1)S(1)} %get-tuple-element.32.shifted, bf16[2048,128]{1,0:T(8,128)(2,1)S(1)} %copy-done.3, bf16[3328,128]{1,0:T(8,128)(2,1)} %get-tuple-element.26.sent_mate, ...), custom_call_target="tpu_custom_call" | custom-call | flops 2214592512 | bytes 11010048 | tf_op jit(solution)/shard_map/pallas_call | solution.py:382
  46.5 2.6 %collective-permute-start.12 = (bf16[512,512]{1,0:T(8,128)(2,1)S(1)}, bf16[512,512]{1,0:T(8,128)(2,1)S(1)}, u32[]{:S(2)}, u32[]{:S(2)}) collective-permute-start(bf16[512,512]{1,0:T(8,128)(2,1)S(1)} %get-tuple-element.35.own), channel_id=1, source_target_pairs={{0,15},{1,0},{2,1},{3,2},{4,3},{5,4},{6,5},{7,6},{8,7},{9,8},{10,9... | collective-permute-start | bytes 1572872 | tf_op jit(solution)/shard_map/ppermute | solution.py:396
  50.1 6.4 %collective-permute-done.8.cross = bf16[2048,128]{1,0:T(8,128)(2,1)S(1)} collective-permute-done((bf16[2048,128]{1,0:T(8,128)(2,1)S(1)}, bf16[2048,128]{1,0:T(8,128)(2,1)S(1)}, u32[]{:S(2)}, u32[]{:S(2)}) %collective-permute-start.8) | collective-permute-done | bytes 524320 | tf_op jit(solution)/shard_map/ppermute | solution.py:396
  56.5 1.3 %shard_map.54 = (bf16[512,512]{1,0:T(8,128)(2,1)S(1)}, bf16[512,512]{1,0:T(8,128)(2,1)S(1)}, bf16[1280,128]{1,0:T(8,128)(2,1)S(1)}, bf16[1280,128]{1,0:T(8,128)(2,1)S(1)}) custom-call(s32[13]{0:T(128)S(1)} %pad_add_fusion.drop_ref, bf16[3328,128]{1,0:T(8,128)(2,1)S(1)} %collective-permute-done.4.refs_1_.mate, ...), custom_call_target="tpu_custom_call" | custom-call | flops 335544320 | bytes 6750208 | tf_op jit(solution)/shard_map/pallas_call | solution.py:382
  57.9 2.5 %collective-permute-start.9 = (bf16[1280,128]{1,0:T(8,128)(2,1)S(1)}, bf16[1280,128]{1,0:T(8,128)(2,1)S(1)}, u32[]{:S(2)}, u32[]{:S(2)}) collective-permute-start(bf16[1280,128]{1,0:T(8,128)(2,1)S(1)} %get-tuple-element.39), channel_id=1, source_target_pairs={{0,1},{1,2},{2,3},{3,4},{4,5},{5,6},{6,7},{7,8},{8,9},{9,10},{10,1... | collective-permute-start | bytes 983048 | tf_op jit(solution)/shard_map/ppermute | solution.py:396
  60.4 2.0 %shard_map.55.correction = bf16[1536,512]{1,0:T(8,128)(2,1)S(1)} custom-call(s32[13]{0:T(128)S(1)} %pad_add_fusion.drop_ref, bf16[1536,1280]{1,0:T(8,128)(2,1)S(1)} %get-tuple-element.32.shifted, bf16[512,512]{1,0:T(8,128)(2,1)S(1)} %get-tuple-element.41.low, bf16[512,512]{1,0:T(8,128)(2,1)S(1)} %get-tuple-element.35.own, ...), custom_call_target="tpu_custom_call" | custom-call | flops 1275068416 | bytes 7077888 | tf_op jit(solution)/shard_map/pallas_call | solution.py:382
  62.4 9.2 %collective-permute-done.12.corner_above = bf16[512,512]{1,0:T(8,128)(2,1)S(1)} collective-permute-done((bf16[512,512]{1,0:T(8,128)(2,1)S(1)}, bf16[512,512]{1,0:T(8,128)(2,1)S(1)}, u32[]{:S(2)}, u32[]{:S(2)}) %collective-permute-start.12) | collective-permute-done | bytes 524320 | tf_op jit(solution)/shard_map/ppermute | solution.py:396
  71.6 1.5 %shard_map.56 = (bf16[512,512]{1,0:T(8,128)(2,1)S(1)}, bf16[512,512]{1,0:T(8,128)(2,1)S(1)}, bf16[1280,128]{1,0:T(8,128)(2,1)S(1)}, bf16[1280,128]{1,0:T(8,128)(2,1)S(1)}) custom-call(s32[13]{0:T(128)S(1)} %pad_add_fusion.drop_ref, bf16[512,512]{1,0:T(8,128)(2,1)S(1)} %collective-permute-done.11.corner_below, ...), custom_call_target="tpu_custom_call" | custom-call | flops 671088640 | bytes 5373952 | tf_op jit(solution)/shard_map/pallas_call | solution.py:382
  73.7 1.4 %collective-permute-done.10.from_above = bf16[1280,128]{1,0:T(8,128)(2,1)S(1)} collective-permute-done((bf16[1280,128]{1,0:T(8,128)(2,1)S(1)}, bf16[1280,128]{1,0:T(8,128)(2,1)S(1)}, u32[]{:S(2)}, u32[]{:S(2)}) %collective-permute-start.10) | collective-permute-done | bytes 327712 | tf_op jit(solution)/shard_map/ppermute | solution.py:396
  75.1 2.2 %shard_map.57 = (bf16[1536,512]{1,0:T(8,128)(2,1)S(1)}, bf16[1280,128]{1,0:T(8,128)(2,1)S(1)}, bf16[1280,128]{1,0:T(8,128)(2,1)S(1)}) custom-call(s32[13]{0:T(128)S(1)} %pad_add_fusion.drop_ref, bf16[512,512]{1,0:T(8,128)(2,1)S(1)} %get-tuple-element.35.own, bf16[1280,128]{1,0:T(8,128)(2,1)S(1)} %collective-permute-done.9.from_below, ...), custom_call_target="tpu_custom_call" | custom-call | flops 1275068416 | bytes 9961472 | tf_op jit(solution)/shard_map/pallas_call | solution.py:382
  77.9 1.3 %shard_map.58.own = bf16[512,512]{1,0:T(8,128)(2,1)S(1)} custom-call(s32[13]{0:T(128)S(1)} %pad_add_fusion.drop_ref, bf16[1536,1280]{1,0:T(8,128)(2,1)S(1)} %get-tuple-element.31.square, bf16[1536,512]{1,0:T(8,128)(2,1)S(1)} %get-tuple-element.45.whole.own), custom_call_target="tpu_custom_call" | custom-call | flops 603979776 | bytes 6029312 | tf_op jit(solution)/shard_map/pallas_call | solution.py:382
  80.0 1.7 %shard_map.60 = bf16[4,8,128,128]{3,2,1,0:T(8,128)(2,1)} custom-call(s32[13]{0:T(128)S(1)} %pad_add_fusion.drop_ref, bf16[1536,512]{1,0:T(8,128)(2,1)S(1)} %get-tuple-element.45.whole.own, bf16[1280,128]{1,0:T(8,128)(2,1)S(1)} %collective-permute-done.15.from_below, bf16[1280,128]{1,0:T(8,128)(2,1)S(1)} %collective-permute-done.16.from_above), custom_call_target="tpu_custom_call" | custom-call | bytes 3276800 | tf_op jit(solution)/shard_map/pallas_call | solution.py:382
  81.7 3.4 %collective-permute-done.13.from_below = bf16[1280,128]{1,0:T(8,128)(2,1)S(1)} collective-permute-done((bf16[1280,128]{1,0:T(8,128)(2,1)S(1)}, bf16[1280,128]{1,0:T(8,128)(2,1)S(1)}, u32[]{:S(2)}, u32[]{:S(2)}) %collective-permute-start.13) | collective-permute-done | bytes 327712 | tf_op jit(solution)/shard_map/ppermute | solution.py:396
  85.1 2.5 %collective-permute-done.14.from_above = bf16[1280,128]{1,0:T(8,128)(2,1)S(1)} collective-permute-done((bf16[1280,128]{1,0:T(8,128)(2,1)S(1)}, bf16[1280,128]{1,0:T(8,128)(2,1)S(1)}, u32[]{:S(2)}, u32[]{:S(2)}) %collective-permute-start.14) | collective-permute-done | bytes 327712 | tf_op jit(solution)/shard_map/ppermute | solution.py:396
  87.5 1.7 %shard_map.59 = bf16[4,8,128,128]{3,2,1,0:T(8,128)(2,1)} custom-call(s32[13]{0:T(128)S(1)} %pad_add_fusion.drop_ref, bf16[512,512]{1,0:T(8,128)(2,1)S(1)} %shard_map.58.own, bf16[1280,128]{1,0:T(8,128)(2,1)S(1)} %collective-permute-done.13.from_below, bf16[1280,128]{1,0:T(8,128)(2,1)S(1)} %collective-permute-done.14.from_above), custom_call_target="tpu_custom_call" | custom-call | bytes 2228224 | tf_op jit(solution)/shard_map/pallas_call | solution.py:382
  (35 shorter events, 7.3 us)
Async XLA Ops:
  0.6 26.8 %collective-permute-start.2 = (bf16[4,8,128,128]{3,2,1,0:T(8,128)(2,1)}, bf16[4,8,128,128]{3,2,1,0:T(8,128)(2,1)S(1)}, u32[]{:S(2)}, u32[]{:S(2)}) collective-permute-start(bf16[4,8,128,128]{3,2,1,0:T(8,128)(2,1)} %own.3), channel_id=1, source_target_pairs={{0,15},{1,2},{2,1},{3,4},{4,3},{5,6},{6,5},{7,8},{8,7},{9,10},{10,... | collective-permute-start | bytes 3145736 | tf_op jit(solution)/shard_map/ppermute | solution.py:396
  3.3 24.1 %collective-permute-start.3 = (bf16[4,8,128,128]{3,2,1,0:T(8,128)(2,1)}, bf16[4,8,128,128]{3,2,1,0:T(8,128)(2,1)S(1)}, u32[]{:S(2)}, u32[]{:S(2)}) collective-permute-start(bf16[4,8,128,128]{3,2,1,0:T(8,128)(2,1)} %own.3), channel_id=1, source_target_pairs={{0,1},{1,0},{2,3},{3,2},{4,5},{5,4},{6,7},{7,6},{8,9},{9,8},{10,11... | collective-permute-start | bytes 3145736 | tf_op jit(solution)/shard_map/ppermute | solution.py:396
  7.1 1.2 %copy-start = (bf16[4,8,128,128]{3,2,1,0:T(8,128)(2,1)S(1)}, bf16[4,8,128,128]{3,2,1,0:T(8,128)(2,1)}, u32[]{:S(2)}) copy-start(bf16[4,8,128,128]{3,2,1,0:T(8,128)(2,1)} %own.2) | copy-start | bytes 3145732
  10.3 0.8 copy-start.2
  11.1 16.3 %collective-permute-start.4 = (bf16[3328,128]{1,0:T(8,128)(2,1)}, bf16[3328,128]{1,0:T(8,128)(2,1)S(1)}, u32[]{:S(2)}, u32[]{:S(2)}) collective-permute-start(bf16[3328,128]{1,0:T(8,128)(2,1)} %get-tuple-element.26.sent_mate), channel_id=1, source_target_pairs={{0,1},{1,0},{2,3},{3,2},{4,5},{5,4},{6,7},{7,6},{8,9},{9,8},{10,11... | collective-permute-start | bytes 2555912 | tf_op jit(solution)/shard_map/ppermute | solution.py:396
  11.1 2.0 %collective-permute-start.1 = (s32[4]{0:T(128)S(1)}, s32[4]{0:T(128)S(1)}, u32[]{:S(2)}, u32[]{:S(2)}) collective-permute-start(s32[4]{0:T(128)S(1)} %broadcast_subtract_fusion), channel_id=1, source_target_pairs={{0,1},{1,0},{2,3},{3,2},{4,5},{5,4},{6,7},{7,6},{8,9},{9,8},{10,11... | collective-permute-start | bytes 56 | tf_op jit(solution)/shard_map/ppermute | solution.py:396
  11.6 15.7 %collective-permute-start = (s32[4]{0:T(128)S(1)}, s32[4]{0:T(128)S(1)}, u32[]{:S(2)}, u32[]{:S(2)}) collective-permute-start(s32[4]{0:T(128)S(1)} %broadcast_subtract_fusion), channel_id=1, source_target_pairs={{0,15},{1,2},{2,1},{3,4},{4,3},{5,6},{6,5},{7,8},{8,7},{9,10},{10,... | collective-permute-start | bytes 56 | tf_op jit(solution)/shard_map/ppermute | solution.py:396
  11.6 26.3 %copy-start.1 = (bf16[4,8,128,128]{3,2,1,0:T(8,128)(2,1)S(1)}, bf16[4,8,128,128]{3,2,1,0:T(8,128)(2,1)}, u32[]{:S(2)}) copy-start(bf16[4,8,128,128]{3,2,1,0:T(8,128)(2,1)} %own.3) | copy-start | bytes 3145732
  28.1 14.5 %copy-start.3 = (bf16[2048,128]{1,0:T(8,128)(2,1)S(1)}, bf16[2048,128]{1,0:T(8,128)(2,1)}, u32[]{:S(2)}) copy-start(bf16[2048,128]{1,0:T(8,128)(2,1)} %copy-done.2) | copy-start | bytes 1572868
  28.1 9.8 %collective-permute-start.5 = (bf16[1280,128]{1,0:T(8,128)(2,1)S(1)}, bf16[1280,128]{1,0:T(8,128)(2,1)S(1)}, u32[]{:S(2)}, u32[]{:S(2)}) collective-permute-start(bf16[1280,128]{1,0:T(8,128)(2,1)S(1)} %get-tuple-element.29), channel_id=1, source_target_pairs={{0,13},{1,4},{2,15},{3,6},{4,1},{5,8},{6,3},{7,10},{8,5},{9,12},{1... | collective-permute-start | bytes 983048 | tf_op jit(solution)/shard_map/ppermute | solution.py:396
  28.2 9.7 %collective-permute-start.6 = (bf16[1280,128]{1,0:T(8,128)(2,1)S(1)}, bf16[1280,128]{1,0:T(8,128)(2,1)S(1)}, u32[]{:S(2)}, u32[]{:S(2)}) collective-permute-start(bf16[1280,128]{1,0:T(8,128)(2,1)S(1)} %get-tuple-element.30), channel_id=1, source_target_pairs={{0,1},{1,0},{2,3},{3,2},{4,5},{5,4},{6,7},{7,6},{8,9},{9,8},{10,11... | collective-permute-start | bytes 983048 | tf_op jit(solution)/shard_map/ppermute | solution.py:396
  31.9 10.7 %collective-permute-start.7 = (bf16[1280,128]{1,0:T(8,128)(2,1)}, bf16[1280,128]{1,0:T(8,128)(2,1)S(1)}, u32[]{:S(2)}, u32[]{:S(2)}) collective-permute-start(bf16[1280,128]{1,0:T(8,128)(2,1)} %get-tuple-element.34.sent_cross), channel_id=1, source_target_pairs={{0,15},{1,2},{2,1},{3,4},{4,3},{5,6},{6,5},{7,8},{8,7},{9,10},{10,... | collective-permute-start | bytes 983048 | tf_op jit(solution)/shard_map/ppermute | solution.py:396
  31.9 24.6 %collective-permute-start.8 = (bf16[2048,128]{1,0:T(8,128)(2,1)S(1)}, bf16[2048,128]{1,0:T(8,128)(2,1)S(1)}, u32[]{:S(2)}, u32[]{:S(2)}) collective-permute-start(bf16[2048,128]{1,0:T(8,128)(2,1)S(1)} %get-tuple-element.36), channel_id=1, source_target_pairs={{0,15},{1,2},{2,1},{3,4},{4,3},{5,6},{6,5},{7,8},{8,7},{9,10},{10,... | collective-permute-start | bytes 1572872 | tf_op jit(solution)/shard_map/ppermute | solution.py:396
  46.5 25.2 %collective-permute-start.12 = (bf16[512,512]{1,0:T(8,128)(2,1)S(1)}, bf16[512,512]{1,0:T(8,128)(2,1)S(1)}, u32[]{:S(2)}, u32[]{:S(2)}) collective-permute-start(bf16[512,512]{1,0:T(8,128)(2,1)S(1)} %get-tuple-element.35.own), channel_id=1, source_target_pairs={{0,15},{1,0},{2,1},{3,2},{4,3},{5,4},{6,5},{7,6},{8,7},{9,8},{10,9... | collective-permute-start | bytes 1572872 | tf_op jit(solution)/shard_map/ppermute | solution.py:396
  49.1 22.5 %collective-permute-start.11 = (bf16[512,512]{1,0:T(8,128)(2,1)S(1)}, bf16[512,512]{1,0:T(8,128)(2,1)S(1)}, u32[]{:S(2)}, u32[]{:S(2)}) collective-permute-start(bf16[512,512]{1,0:T(8,128)(2,1)S(1)} %get-tuple-element.35.own), channel_id=1, source_target_pairs={{0,1},{1,2},{2,3},{3,4},{4,5},{5,6},{6,7},{7,8},{8,9},{9,10},{10,1... | collective-permute-start | bytes 1572872 | tf_op jit(solution)/shard_map/ppermute | solution.py:396
  57.9 15.9 %collective-permute-start.9 = (bf16[1280,128]{1,0:T(8,128)(2,1)S(1)}, bf16[1280,128]{1,0:T(8,128)(2,1)S(1)}, u32[]{:S(2)}, u32[]{:S(2)}) collective-permute-start(bf16[1280,128]{1,0:T(8,128)(2,1)S(1)} %get-tuple-element.39), channel_id=1, source_target_pairs={{0,1},{1,2},{2,3},{3,4},{4,5},{5,6},{6,7},{7,8},{8,9},{9,10},{10,1... | collective-permute-start | bytes 983048 | tf_op jit(solution)/shard_map/ppermute | solution.py:396
  60.4 14.7 %collective-permute-start.10 = (bf16[1280,128]{1,0:T(8,128)(2,1)S(1)}, bf16[1280,128]{1,0:T(8,128)(2,1)S(1)}, u32[]{:S(2)}, u32[]{:S(2)}) collective-permute-start(bf16[1280,128]{1,0:T(8,128)(2,1)S(1)} %get-tuple-element.40), channel_id=1, source_target_pairs={{0,15},{1,0},{2,1},{3,2},{4,3},{5,4},{6,5},{7,6},{8,7},{9,8},{10,9... | collective-permute-start | bytes 983048 | tf_op jit(solution)/shard_map/ppermute | solution.py:396
  73.2 6.1 %collective-permute-start.15 = (bf16[1280,128]{1,0:T(8,128)(2,1)S(1)}, bf16[1280,128]{1,0:T(8,128)(2,1)S(1)}, u32[]{:S(2)}, u32[]{:S(2)}) collective-permute-start(bf16[1280,128]{1,0:T(8,128)(2,1)S(1)} %get-tuple-element.48), channel_id=1, source_target_pairs={{0,1},{1,2},{2,3},{3,4},{4,5},{5,6},{6,7},{7,8},{8,9},{9,10},{10,1... | collective-permute-start | bytes 983048 | tf_op jit(solution)/shard_map/ppermute | solution.py:396
  73.2 6.7 %collective-permute-start.16 = (bf16[1280,128]{1,0:T(8,128)(2,1)S(1)}, bf16[1280,128]{1,0:T(8,128)(2,1)S(1)}, u32[]{:S(2)}, u32[]{:S(2)}) collective-permute-start(bf16[1280,128]{1,0:T(8,128)(2,1)S(1)} %get-tuple-element.49), channel_id=1, source_target_pairs={{0,15},{1,0},{2,1},{3,2},{4,3},{5,4},{6,5},{7,6},{8,7},{9,8},{10,9... | collective-permute-start | bytes 983048 | tf_op jit(solution)/shard_map/ppermute | solution.py:396
  77.4 7.7 %collective-permute-start.13 = (bf16[1280,128]{1,0:T(8,128)(2,1)S(1)}, bf16[1280,128]{1,0:T(8,128)(2,1)S(1)}, u32[]{:S(2)}, u32[]{:S(2)}) collective-permute-start(bf16[1280,128]{1,0:T(8,128)(2,1)S(1)} %get-tuple-element.46), channel_id=1, source_target_pairs={{0,1},{1,2},{2,3},{3,4},{4,5},{5,6},{6,7},{7,8},{8,9},{9,10},{10,1... | collective-permute-start | bytes 983048 | tf_op jit(solution)/shard_map/ppermute | solution.py:396
  77.5 10.0 %collective-permute-start.14 = (bf16[1280,128]{1,0:T(8,128)(2,1)S(1)}, bf16[1280,128]{1,0:T(8,128)(2,1)S(1)}, u32[]{:S(2)}, u32[]{:S(2)}) collective-permute-start(bf16[1280,128]{1,0:T(8,128)(2,1)S(1)} %get-tuple-element.47), channel_id=1, source_target_pairs={{0,15},{1,0},{2,1},{3,2},{4,3},{5,4},{6,5},{7,6},{8,7},{9,8},{10,9... | collective-permute-start | bytes 983048 | tf_op jit(solution)/shard_map/ppermute | solution.py:396

commit v9 on v8

--- a/solution.py
+++ b/solution.py
@@ -154,16 +154,17 @@
 def forward_kernel(f, drop_ref, cross, *refs):
     h = f.h
     odd = odd_place(f, drop_ref)
-    to_mate, to_far = refs[-4:-2]
+    to_mate, to_far = refs[-5:-3], refs[-3]
     for i, (lower, upper) in enumerate(zip(under(h), over(h))):
         (r, c), (s, d) = lower, upper
         forth = stored(cross, r, 2 * h + c - r, jnp.where(odd, drop_ref[2 * h + r], drop_ref[r]))
         back = stored(cross, s, d - s, jnp.where(odd, drop_ref[2 * h + s], drop_ref[s]))
-        to_mate[block(f, i, 0)] = jnp.where(odd, back, forth)
+        part, place = i % 2, i // 2
+        to_mate[part][block(f, place, 0)] = jnp.where(odd, back, forth)
         to_far[block(f, i, 0)] = jnp.where(odd, forth, back)
 
 
-def square_kernel(f, drop_ref, own, cross, mate, far_far, far_mate, square, shifted, wide):
+def square_kernel(f, drop_ref, own, cross, mate, far_far, far_mate, far_mate_too, square, shifted, wide):
     h, p = f.h, f.p
     below, above = sides(f, drop_ref, plain(mate), plain(cross))
     for g, read in enumerate((below, plain(own), above)):
@@ -177,7 +178,8 @@
                 else:
                     value = jnp.zeros((f.b, f.b), wide.dtype)
                 wide[block(f, row + h, col + h)] = value
-    far_below, far_above = sides(f, drop_ref, indexed(f, far_mate), indexed(f, far_far))
+    far_mates = [indexed(f, far_mate), indexed(f, far_mate_too)]
+    far_below, far_above = sides(f, drop_ref, lambda i: far_mates[i % 2](i // 2), indexed(f, far_far))
     spread(f, wide, 0, h, far_below, under(h))
     spread(f, wide, 4 * h, 3 * h, far_above, over(h))
     unit = (
@@ -443,6 +445,7 @@
     columns = jax.ShapeDtypeStruct((3 * f.group, f.group), kind)
     band = jax.ShapeDtypeStruct((3 * f.group, (2 * f.p + 1) * f.t), kind)
     triangle = jax.ShapeDtypeStruct((count * order, order), kind)
+    half_triangle = jax.ShapeDtypeStruct((count // 2 * order, order), kind)
     listed = jax.ShapeDtypeStruct((half * half * order, order), kind)
     both = jax.ShapeDtypeStruct(((count + half * half) * order, order), kind)
     partial_sums = jax.ShapeDtypeStruct((2 * f.group, f.group), jnp.float32)
@@ -456,11 +459,11 @@
         slabs_kernel, [listed, listed, both, triangle], [], 0, 12, start_drop, inverse_start
     )
     from_mate = to_mate(slab_mate)
-    forward_mate, forward_far, triangle_cross, corner_cross = run(
-        forward_kernel, [triangle, triangle], [], 0, 12, drop, density_cross, density_mate, from_mate,
+    forward_mate, forward_mate_too, forward_far, triangle_cross, corner_cross = run(
+        forward_kernel, [half_triangle, half_triangle, triangle], [], 0, 12, drop, density_cross, density_mate, from_mate,
         passed=(triangle_cross, corner_cross),
     )
-    far_mate = to_mate(forward_mate)
+    far_mate, far_mate_too = to_mate(forward_mate), to_mate(forward_mate_too)
     far_far = routed(forward_far, lambda i: 3 * cross_step(i))
     cross_triangle = to_cross(triangle_cross)
     cross_corner = to_cross(corner_cross)
@@ -469,13 +472,13 @@
         square_kernel,
         [band, band],
         [pltpu.VMEM((5 * f.group, 5 * f.group), kind)],
-        94, 28, drop, density, density_cross, density_mate, far_far, far_mate, light=True,
+        94, 28, drop, density, density_cross, density_mate, far_far, far_mate, far_mate_too, light=True,
     )
     correction, own, partial = run(
         first_sweep_kernel,
         [columns, square_group, partial_sums],
         [whole_scratch, group_scratch, group_scratch],
-        66, 24, drop, shifted, corner, slab_mate, triangle_cross, from_mate, cross_triangle,
+        66, 24, drop, shifted, corner, slab_mate, triangle_cross, from_mate, cross_triangle, light=True,
     )
     next_corner_below, next_corner_above = to_next(own), to_prev(own)
     low, high, back, forth = run(

time: 89.5 us -> 86.3 us (0.964)
  waiting for transfers between devices: 43.5 us -> 38 us
  starting transfers between devices: 18.9 us -> 20.3 us
    ppermute x17 -> x18, waiting for transfers between devices: 43.5 us -> 38 us  [routed(): lax.ppermute(x, RING, [(i, (i + step(i)) % size) for i in range(size) if...]
    ppermute x17 -> x18, starting transfers between devices: 18.9 us -> 20.3 us  [routed(): lax.ppermute(x, RING, [(i, (i + step(i)) % size) for i in range(size) if...]
  transfers between devices with their start and end apart: 17 -> 18, of which waited for: 9 -> 10; matrix products, arithmetic and copies ran while one was open for 1% -> 1% of each run, Pallas kernels for 23% -> 24%
where the time goes in v9:
time: 86.3 us; the launch traced here: 85.3 us
  waiting for transfers between devices  38 us (44%)
  Pallas kernels  23.1 us (27%)
  starting transfers between devices  20.3 us (24%)
  local copies, waits for them, and re-layouts  2.05 us (2%)
  other arithmetic  1.04 us (1%)
    ppermute x18, waiting for transfers between devices, routed(): lax.ppermute(x, RING, [(i, (i + step(i)) % size) for i in range(size) if...  38 us
    pallas_call x11, Pallas kernels, call(): pl.pallas_call(kernel, out_shape=[*outs, *[jax.ShapeDtypeStruct(a.shape,...  23.1 us
    ppermute x18, starting transfers between devices, routed(): lax.ppermute(x, RING, [(i, (i + step(i)) % size) for i in range(size) if...  20.3 us
    unnamed x8, local copies, waits for them, and re-layouts  2.05 us
  transfers between devices with their start and end apart: 18, of which 10 were waited for; matrix products, arithmetic and copies ran while one was open for 1% of the time, Pallas kernels for 24%

profile of v9, /device:TPU:1, one launch (start us, length us, event | category | flops | bytes accessed | tf_op | source)
XLA Modules:
  0.0 85.3 jit_solution(11358779871039621159)
XLA Ops:
  0.6 2.7 %collective-permute-start.2 = (bf16[4,8,128,128]{3,2,1,0:T(8,128)(2,1)}, bf16[4,8,128,128]{3,2,1,0:T(8,128)(2,1)S(1)}, u32[]{:S(2)}, u32[]{:S(2)}) collective-permute-start(bf16[4,8,128,128]{3,2,1,0:T(8,128)(2,1)} %own.3), channel_id=1, source_target_pairs={{0,15},{1,2},{2,1},{3,4},{4,3},{5,6},{6,5},{7,8},{8,7},{9,10},{10,... | collective-permute-start | bytes 3145736 | tf_op jit(solution)/shard_map/ppermute | solution.py:398
  3.3 2.9 %collective-permute-start.3 = (bf16[4,8,128,128]{3,2,1,0:T(8,128)(2,1)}, bf16[4,8,128,128]{3,2,1,0:T(8,128)(2,1)S(1)}, u32[]{:S(2)}, u32[]{:S(2)}) collective-permute-start(bf16[4,8,128,128]{3,2,1,0:T(8,128)(2,1)} %own.3), channel_id=1, source_target_pairs={{0,1},{1,0},{2,3},{3,2},{4,5},{5,4},{6,7},{7,6},{8,9},{9,8},{10,11... | collective-permute-start | bytes 3145736 | tf_op jit(solution)/shard_map/ppermute | solution.py:398
  7.1 1.2 %copy-done = bf16[4,8,128,128]{3,2,1,0:T(8,128)(2,1)S(1)} copy-done((bf16[4,8,128,128]{3,2,1,0:T(8,128)(2,1)S(1)}, bf16[4,8,128,128]{3,2,1,0:T(8,128)(2,1)}, u32[]{:S(2)}) %copy-start) | copy-done | bytes 1048600
  8.4 2.1 %shard_map.50 = (bf16[2048,128]{1,0:T(8,128)(2,1)S(1)}, bf16[2048,128]{1,0:T(8,128)(2,1)}, bf16[3328,128]{1,0:T(8,128)(2,1)}, bf16[1280,128]{1,0:T(8,128)(2,1)S(1)}) custom-call(s32[5]{0:T(128)S(1)} %pad_add_fusion.1.drop_ref, bf16[4,8,128,128]{3,2,1,0:T(8,128)(2,1)S(1)} %copy-done), custom_call_target="tpu_custom_call" | custom-call | bytes 3276800 | tf_op jit(solution)/shard_map/pallas_call | solution.py:384
  11.7 1.5 %collective-permute-done.1 = s32[4]{0:T(128)S(1)} collective-permute-done((s32[4]{0:T(128)S(1)}, s32[4]{0:T(128)S(1)}, u32[]{:S(2)}, u32[]{:S(2)}) %collective-permute-start.1) | collective-permute-done | bytes 48 | tf_op jit(solution)/shard_map/ppermute | solution.py:398
  13.2 14.1 %collective-permute-done = s32[4]{0:T(128)S(1)} collective-permute-done((s32[4]{0:T(128)S(1)}, s32[4]{0:T(128)S(1)}, u32[]{:S(2)}, u32[]{:S(2)}) %collective-permute-start) | collective-permute-done | bytes 48 | tf_op jit(solution)/shard_map/ppermute | solution.py:398
  28.2 1.8 %collective-permute-start.8 = (bf16[1280,128]{1,0:T(8,128)(2,1)S(1)}, bf16[1280,128]{1,0:T(8,128)(2,1)S(1)}, u32[]{:S(2)}, u32[]{:S(2)}) collective-permute-start(bf16[1280,128]{1,0:T(8,128)(2,1)S(1)} %get-tuple-element.36.sent_cross), channel_id=1, source_target_pairs={{0,15},{1,2},{2,1},{3,4},{4,3},{5,6},{6,5},{7,8},{8,7},{9,10},{10,... | collective-permute-start | bytes 983048 | tf_op jit(solution)/shard_map/ppermute | solution.py:398
  30.1 6.3 %collective-permute-start.6 = (bf16[640,128]{1,0:T(8,128)(2,1)S(1)}, bf16[640,128]{1,0:T(8,128)(2,1)S(1)}, u32[]{:S(2)}, u32[]{:S(2)}) collective-permute-start(bf16[640,128]{1,0:T(8,128)(2,1)S(1)} %get-tuple-element.31), channel_id=1, source_target_pairs={{0,1},{1,0},{2,3},{3,2},{4,5},{5,4},{6,7},{7,6},{8,9},{9,8},{10,11... | collective-permute-start | bytes 491528 | tf_op jit(solution)/shard_map/ppermute | solution.py:398
  37.9 4.7 %shard_map.52 = (bf16[1536,1280]{1,0:T(8,128)(2,1)S(1)}, bf16[1536,1280]{1,0:T(8,128)(2,1)S(1)}) custom-call(s32[13]{0:T(128)S(1)} %pad_add_fusion.drop_ref, bf16[4,8,128,128]{3,2,1,0:T(8,128)(2,1)S(1)} %copy-done.1, bf16[4,8,128,128]{3,2,1,0:T(8,128)(2,1)S(1)} %collective-permute-done.2.cross, ...), custom_call_target="tpu_custom_call" | custom-call | tf_op jit(solution)/shard_map/pallas_call | solution.py:384
  42.6 3.8 %shard_map.53 = (bf16[1536,512]{1,0:T(8,128)(2,1)S(1)}, bf16[512,512]{1,0:T(8,128)(2,1)S(1)}, f32[1024,512]{1,0:T(8,128)S(1)}) custom-call(s32[13]{0:T(128)S(1)} %pad_add_fusion.drop_ref, bf16[1536,1280]{1,0:T(8,128)(2,1)S(1)} %get-tuple-element.34.shifted, bf16[2048,128]{1,0:T(8,128)(2,1)S(1)} %copy-done.3, bf16[3328,128]{1,0:T(8,128)(2,1)} %get-tuple-element.27.sent_mate, ...), custom_call_target="tpu_custom_call" | custom-call | tf_op jit(solution)/shard_map/pallas_call | solution.py:384
  46.4 2.5 %collective-permute-start.13 = (bf16[512,512]{1,0:T(8,128)(2,1)S(1)}, bf16[512,512]{1,0:T(8,128)(2,1)S(1)}, u32[]{:S(2)}, u32[]{:S(2)}) collective-permute-start(bf16[512,512]{1,0:T(8,128)(2,1)S(1)} %get-tuple-element.37.own), channel_id=1, source_target_pairs={{0,15},{1,0},{2,1},{3,2},{4,3},{5,4},{6,5},{7,6},{8,7},{9,8},{10,9... | collective-permute-start | bytes 1572872 | tf_op jit(solution)/shard_map/ppermute | solution.py:398
  48.9 1.2 %collective-permute-start.12 = (bf16[512,512]{1,0:T(8,128)(2,1)S(1)}, bf16[512,512]{1,0:T(8,128)(2,1)S(1)}, u32[]{:S(2)}, u32[]{:S(2)}) collective-permute-start(bf16[512,512]{1,0:T(8,128)(2,1)S(1)} %get-tuple-element.37.own), channel_id=1, source_target_pairs={{0,1},{1,2},{2,3},{3,4},{4,5},{5,6},{6,7},{7,8},{8,9},{9,10},{10,1... | collective-permute-start | bytes 1572872 | tf_op jit(solution)/shard_map/ppermute | solution.py:398
  50.1 1.3 %shard_map.54 = (bf16[512,512]{1,0:T(8,128)(2,1)S(1)}, bf16[512,512]{1,0:T(8,128)(2,1)S(1)}, bf16[1280,128]{1,0:T(8,128)(2,1)S(1)}, bf16[1280,128]{1,0:T(8,128)(2,1)S(1)}) custom-call(s32[13]{0:T(128)S(1)} %pad_add_fusion.drop_ref, bf16[3328,128]{1,0:T(8,128)(2,1)S(1)} %collective-permute-done.4.refs_1_.mate, ...), custom_call_target="tpu_custom_call" | custom-call | flops 335544320 | bytes 6750208 | tf_op jit(solution)/shard_map/pallas_call | solution.py:384
  51.4 1.2 %collective-permute-start.10 = (bf16[1280,128]{1,0:T(8,128)(2,1)S(1)}, bf16[1280,128]{1,0:T(8,128)(2,1)S(1)}, u32[]{:S(2)}, u32[]{:S(2)}) collective-permute-start(bf16[1280,128]{1,0:T(8,128)(2,1)S(1)} %get-tuple-element.41), channel_id=1, source_target_pairs={{0,1},{1,2},{2,3},{3,4},{4,5},{5,6},{6,7},{7,8},{8,9},{9,10},{10,1... | collective-permute-start | bytes 983048 | tf_op jit(solution)/shard_map/ppermute | solution.py:398
  52.7 2.0 %shard_map.55.correction = bf16[1536,512]{1,0:T(8,128)(2,1)S(1)} custom-call(s32[13]{0:T(128)S(1)} %pad_add_fusion.drop_ref, bf16[1536,1280]{1,0:T(8,128)(2,1)S(1)} %get-tuple-element.34.shifted, bf16[512,512]{1,0:T(8,128)(2,1)S(1)} %get-tuple-element.43.low, bf16[512,512]{1,0:T(8,128)(2,1)S(1)} %get-tuple-element.37.own, ...), custom_call_target="tpu_custom_call" | custom-call | flops 1275068416 | bytes 7077888 | tf_op jit(solution)/shard_map/pallas_call | solution.py:384
  54.7 11.3 %collective-permute-done.13.corner_above = bf16[512,512]{1,0:T(8,128)(2,1)S(1)} collective-permute-done((bf16[512,512]{1,0:T(8,128)(2,1)S(1)}, bf16[512,512]{1,0:T(8,128)(2,1)S(1)}, u32[]{:S(2)}, u32[]{:S(2)}) %collective-permute-start.13) | collective-permute-done | bytes 524320 | tf_op jit(solution)/shard_map/ppermute | solution.py:398
  66.0 1.5 %shard_map.56 = (bf16[512,512]{1,0:T(8,128)(2,1)S(1)}, bf16[512,512]{1,0:T(8,128)(2,1)S(1)}, bf16[1280,128]{1,0:T(8,128)(2,1)S(1)}, bf16[1280,128]{1,0:T(8,128)(2,1)S(1)}) custom-call(s32[13]{0:T(128)S(1)} %pad_add_fusion.drop_ref, bf16[512,512]{1,0:T(8,128)(2,1)S(1)} %collective-permute-done.12.corner_below, ...), custom_call_target="tpu_custom_call" | custom-call | flops 671088640 | bytes 5373952 | tf_op jit(solution)/shard_map/pallas_call | solution.py:384
  68.1 4.9 %collective-permute-done.11.from_above = bf16[1280,128]{1,0:T(8,128)(2,1)S(1)} collective-permute-done((bf16[1280,128]{1,0:T(8,128)(2,1)S(1)}, bf16[1280,128]{1,0:T(8,128)(2,1)S(1)}, u32[]{:S(2)}, u32[]{:S(2)}) %collective-permute-start.11) | collective-permute-done | bytes 327712 | tf_op jit(solution)/shard_map/ppermute | solution.py:398
  73.0 2.2 %shard_map.57 = (bf16[1536,512]{1,0:T(8,128)(2,1)S(1)}, bf16[1280,128]{1,0:T(8,128)(2,1)S(1)}, bf16[1280,128]{1,0:T(8,128)(2,1)S(1)}) custom-call(s32[13]{0:T(128)S(1)} %pad_add_fusion.drop_ref, bf16[512,512]{1,0:T(8,128)(2,1)S(1)} %get-tuple-element.37.own, bf16[1280,128]{1,0:T(8,128)(2,1)S(1)} %collective-permute-done.10.from_below, ...), custom_call_target="tpu_custom_call" | custom-call | flops 1275068416 | bytes 9961472 | tf_op jit(solution)/shard_map/pallas_call | solution.py:384
  75.8 1.3 %shard_map.58.own = bf16[512,512]{1,0:T(8,128)(2,1)S(1)} custom-call(s32[13]{0:T(128)S(1)} %pad_add_fusion.drop_ref, bf16[1536,1280]{1,0:T(8,128)(2,1)S(1)} %get-tuple-element.33.square, bf16[1536,512]{1,0:T(8,128)(2,1)S(1)} %get-tuple-element.47.whole.own), custom_call_target="tpu_custom_call" | custom-call | flops 603979776 | bytes 6029312 | tf_op jit(solution)/shard_map/pallas_call | solution.py:384
  77.2 2.9 %collective-permute-done.17.from_above = bf16[1280,128]{1,0:T(8,128)(2,1)S(1)} collective-permute-done((bf16[1280,128]{1,0:T(8,128)(2,1)S(1)}, bf16[1280,128]{1,0:T(8,128)(2,1)S(1)}, u32[]{:S(2)}, u32[]{:S(2)}) %collective-permute-start.17) | collective-permute-done | bytes 327712 | tf_op jit(solution)/shard_map/ppermute | solution.py:398
  80.1 1.7 %shard_map.60 = bf16[4,8,128,128]{3,2,1,0:T(8,128)(2,1)} custom-call(s32[13]{0:T(128)S(1)} %pad_add_fusion.drop_ref, bf16[1536,512]{1,0:T(8,128)(2,1)S(1)} %get-tuple-element.47.whole.own, bf16[1280,128]{1,0:T(8,128)(2,1)S(1)} %collective-permute-done.16.from_below, bf16[1280,128]{1,0:T(8,128)(2,1)S(1)} %collective-permute-done.17.from_above), custom_call_target="tpu_custom_call" | custom-call | bytes 3276800 | tf_op jit(solution)/shard_map/pallas_call | solution.py:384
  81.8 1.1 %collective-permute-done.14.from_below = bf16[1280,128]{1,0:T(8,128)(2,1)S(1)} collective-permute-done((bf16[1280,128]{1,0:T(8,128)(2,1)S(1)}, bf16[1280,128]{1,0:T(8,128)(2,1)S(1)}, u32[]{:S(2)}, u32[]{:S(2)}) %collective-permute-start.14) | collective-permute-done | bytes 327712 | tf_op jit(solution)/shard_map/ppermute | solution.py:398
  83.6 1.7 %shard_map.59 = bf16[4,8,128,128]{3,2,1,0:T(8,128)(2,1)} custom-call(s32[13]{0:T(128)S(1)} %pad_add_fusion.drop_ref, bf16[512,512]{1,0:T(8,128)(2,1)S(1)} %shard_map.58.own, bf16[1280,128]{1,0:T(8,128)(2,1)S(1)} %collective-permute-done.14.from_below, bf16[1280,128]{1,0:T(8,128)(2,1)S(1)} %collective-permute-done.15.from_above), custom_call_target="tpu_custom_call" | custom-call | bytes 2228224 | tf_op jit(solution)/shard_map/pallas_call | solution.py:384
  (37 shorter events, 6.6 us)
Async XLA Ops:
  0.6 26.8 %collective-permute-start.2 = (bf16[4,8,128,128]{3,2,1,0:T(8,128)(2,1)}, bf16[4,8,128,128]{3,2,1,0:T(8,128)(2,1)S(1)}, u32[]{:S(2)}, u32[]{:S(2)}) collective-permute-start(bf16[4,8,128,128]{3,2,1,0:T(8,128)(2,1)} %own.3), channel_id=1, source_target_pairs={{0,15},{1,2},{2,1},{3,4},{4,3},{5,6},{6,5},{7,8},{8,7},{9,10},{10,... | collective-permute-start | bytes 3145736 | tf_op jit(solution)/shard_map/ppermute | solution.py:398
  3.3 24.1 %collective-permute-start.3 = (bf16[4,8,128,128]{3,2,1,0:T(8,128)(2,1)}, bf16[4,8,128,128]{3,2,1,0:T(8,128)(2,1)S(1)}, u32[]{:S(2)}, u32[]{:S(2)}) collective-permute-start(bf16[4,8,128,128]{3,2,1,0:T(8,128)(2,1)} %own.3), channel_id=1, source_target_pairs={{0,1},{1,0},{2,3},{3,2},{4,5},{5,4},{6,7},{7,6},{8,9},{9,8},{10,11... | collective-permute-start | bytes 3145736 | tf_op jit(solution)/shard_map/ppermute | solution.py:398
  7.1 1.2 %copy-start = (bf16[4,8,128,128]{3,2,1,0:T(8,128)(2,1)S(1)}, bf16[4,8,128,128]{3,2,1,0:T(8,128)(2,1)}, u32[]{:S(2)}) copy-start(bf16[4,8,128,128]{3,2,1,0:T(8,128)(2,1)} %own.2) | copy-start | bytes 3145732
  10.4 0.8 copy-start.2
  11.2 16.2 %collective-permute-start.4 = (bf16[3328,128]{1,0:T(8,128)(2,1)}, bf16[3328,128]{1,0:T(8,128)(2,1)S(1)}, u32[]{:S(2)}, u32[]{:S(2)}) collective-permute-start(bf16[3328,128]{1,0:T(8,128)(2,1)} %get-tuple-element.27.sent_mate), channel_id=1, source_target_pairs={{0,1},{1,0},{2,3},{3,2},{4,5},{5,4},{6,7},{7,6},{8,9},{9,8},{10,11... | collective-permute-start | bytes 2555912 | tf_op jit(solution)/shard_map/ppermute | solution.py:398
  11.2 2.0 %collective-permute-start.1 = (s32[4]{0:T(128)S(1)}, s32[4]{0:T(128)S(1)}, u32[]{:S(2)}, u32[]{:S(2)}) collective-permute-start(s32[4]{0:T(128)S(1)} %broadcast_subtract_fusion), channel_id=1, source_target_pairs={{0,1},{1,0},{2,3},{3,2},{4,5},{5,4},{6,7},{7,6},{8,9},{9,8},{10,11... | collective-permute-start | bytes 56 | tf_op jit(solution)/shard_map/ppermute | solution.py:398
  11.7 15.6 %collective-permute-start = (s32[4]{0:T(128)S(1)}, s32[4]{0:T(128)S(1)}, u32[]{:S(2)}, u32[]{:S(2)}) collective-permute-start(s32[4]{0:T(128)S(1)} %broadcast_subtract_fusion), channel_id=1, source_target_pairs={{0,15},{1,2},{2,1},{3,4},{4,3},{5,6},{6,5},{7,8},{8,7},{9,10},{10,... | collective-permute-start | bytes 56 | tf_op jit(solution)/shard_map/ppermute | solution.py:398
  11.7 26.2 %copy-start.1 = (bf16[4,8,128,128]{3,2,1,0:T(8,128)(2,1)S(1)}, bf16[4,8,128,128]{3,2,1,0:T(8,128)(2,1)}, u32[]{:S(2)}) copy-start(bf16[4,8,128,128]{3,2,1,0:T(8,128)(2,1)} %own.3) | copy-start | bytes 3145732
  28.1 14.5 %copy-start.3 = (bf16[2048,128]{1,0:T(8,128)(2,1)S(1)}, bf16[2048,128]{1,0:T(8,128)(2,1)}, u32[]{:S(2)}) copy-start(bf16[2048,128]{1,0:T(8,128)(2,1)} %copy-done.2) | copy-start | bytes 1572868
  28.1 9.8 %collective-permute-start.5 = (bf16[1280,128]{1,0:T(8,128)(2,1)S(1)}, bf16[1280,128]{1,0:T(8,128)(2,1)S(1)}, u32[]{:S(2)}, u32[]{:S(2)}) collective-permute-start(bf16[1280,128]{1,0:T(8,128)(2,1)S(1)} %get-tuple-element.30), channel_id=1, source_target_pairs={{0,13},{1,4},{2,15},{3,6},{4,1},{5,8},{6,3},{7,10},{8,5},{9,12},{1... | collective-permute-start | bytes 983048 | tf_op jit(solution)/shard_map/ppermute | solution.py:398
  28.2 14.4 %collective-permute-start.8 = (bf16[1280,128]{1,0:T(8,128)(2,1)S(1)}, bf16[1280,128]{1,0:T(8,128)(2,1)S(1)}, u32[]{:S(2)}, u32[]{:S(2)}) collective-permute-start(bf16[1280,128]{1,0:T(8,128)(2,1)S(1)} %get-tuple-element.36.sent_cross), channel_id=1, source_target_pairs={{0,15},{1,2},{2,1},{3,4},{4,3},{5,6},{6,5},{7,8},{8,7},{9,10},{10,... | collective-permute-start | bytes 983048 | tf_op jit(solution)/shard_map/ppermute | solution.py:398
  30.0 20.1 %collective-permute-start.9 = (bf16[2048,128]{1,0:T(8,128)(2,1)}, bf16[2048,128]{1,0:T(8,128)(2,1)S(1)}, u32[]{:S(2)}, u32[]{:S(2)}) collective-permute-start(bf16[2048,128]{1,0:T(8,128)(2,1)} %get-tuple-element.38), channel_id=1, source_target_pairs={{0,15},{1,2},{2,1},{3,4},{4,3},{5,6},{6,5},{7,8},{8,7},{9,10},{10,... | collective-permute-start | bytes 1572872 | tf_op jit(solution)/shard_map/ppermute | solution.py:398
  30.1 7.3 %collective-permute-start.6 = (bf16[640,128]{1,0:T(8,128)(2,1)S(1)}, bf16[640,128]{1,0:T(8,128)(2,1)S(1)}, u32[]{:S(2)}, u32[]{:S(2)}) collective-permute-start(bf16[640,128]{1,0:T(8,128)(2,1)S(1)} %get-tuple-element.31), channel_id=1, source_target_pairs={{0,1},{1,0},{2,3},{3,2},{4,5},{5,4},{6,7},{7,6},{8,9},{9,8},{10,11... | collective-permute-start | bytes 491528 | tf_op jit(solution)/shard_map/ppermute | solution.py:398
  36.4 1.4 %collective-permute-start.7 = (bf16[640,128]{1,0:T(8,128)(2,1)S(1)}, bf16[640,128]{1,0:T(8,128)(2,1)S(1)}, u32[]{:S(2)}, u32[]{:S(2)}) collective-permute-start(bf16[640,128]{1,0:T(8,128)(2,1)S(1)} %get-tuple-element.32), channel_id=1, source_target_pairs={{0,1},{1,0},{2,3},{3,2},{4,5},{5,4},{6,7},{7,6},{8,9},{9,8},{10,11... | collective-permute-start | bytes 491528 | tf_op jit(solution)/shard_map/ppermute | solution.py:398
  46.4 19.6 %collective-permute-start.13 = (bf16[512,512]{1,0:T(8,128)(2,1)S(1)}, bf16[512,512]{1,0:T(8,128)(2,1)S(1)}, u32[]{:S(2)}, u32[]{:S(2)}) collective-permute-start(bf16[512,512]{1,0:T(8,128)(2,1)S(1)} %get-tuple-element.37.own), channel_id=1, source_target_pairs={{0,15},{1,0},{2,1},{3,2},{4,3},{5,4},{6,5},{7,6},{8,7},{9,8},{10,9... | collective-permute-start | bytes 1572872 | tf_op jit(solution)/shard_map/ppermute | solution.py:398
  48.9 17.1 %collective-permute-start.12 = (bf16[512,512]{1,0:T(8,128)(2,1)S(1)}, bf16[512,512]{1,0:T(8,128)(2,1)S(1)}, u32[]{:S(2)}, u32[]{:S(2)}) collective-permute-start(bf16[512,512]{1,0:T(8,128)(2,1)S(1)} %get-tuple-element.37.own), channel_id=1, source_target_pairs={{0,1},{1,2},{2,3},{3,4},{4,5},{5,6},{6,7},{7,8},{8,9},{9,10},{10,1... | collective-permute-start | bytes 1572872 | tf_op jit(solution)/shard_map/ppermute | solution.py:398
  51.4 16.7 %collective-permute-start.10 = (bf16[1280,128]{1,0:T(8,128)(2,1)S(1)}, bf16[1280,128]{1,0:T(8,128)(2,1)S(1)}, u32[]{:S(2)}, u32[]{:S(2)}) collective-permute-start(bf16[1280,128]{1,0:T(8,128)(2,1)S(1)} %get-tuple-element.41), channel_id=1, source_target_pairs={{0,1},{1,2},{2,3},{3,4},{4,5},{5,6},{6,7},{7,8},{8,9},{9,10},{10,1... | collective-permute-start | bytes 983048 | tf_op jit(solution)/shard_map/ppermute | solution.py:398
  52.7 20.4 %collective-permute-start.11 = (bf16[1280,128]{1,0:T(8,128)(2,1)S(1)}, bf16[1280,128]{1,0:T(8,128)(2,1)S(1)}, u32[]{:S(2)}, u32[]{:S(2)}) collective-permute-start(bf16[1280,128]{1,0:T(8,128)(2,1)S(1)} %get-tuple-element.42), channel_id=1, source_target_pairs={{0,15},{1,0},{2,1},{3,2},{4,3},{5,4},{6,5},{7,6},{8,7},{9,8},{10,9... | collective-permute-start | bytes 983048 | tf_op jit(solution)/shard_map/ppermute | solution.py:398
  67.6 9.6 %collective-permute-start.16 = (bf16[1280,128]{1,0:T(8,128)(2,1)S(1)}, bf16[1280,128]{1,0:T(8,128)(2,1)S(1)}, u32[]{:S(2)}, u32[]{:S(2)}) collective-permute-start(bf16[1280,128]{1,0:T(8,128)(2,1)S(1)} %get-tuple-element.50), channel_id=1, source_target_pairs={{0,1},{1,2},{2,3},{3,4},{4,5},{5,6},{6,7},{7,8},{8,9},{9,10},{10,1... | collective-permute-start | bytes 983048 | tf_op jit(solution)/shard_map/ppermute | solution.py:398
  67.7 12.3 %collective-permute-start.17 = (bf16[1280,128]{1,0:T(8,128)(2,1)S(1)}, bf16[1280,128]{1,0:T(8,128)(2,1)S(1)}, u32[]{:S(2)}, u32[]{:S(2)}) collective-permute-start(bf16[1280,128]{1,0:T(8,128)(2,1)S(1)} %get-tuple-element.51), channel_id=1, source_target_pairs={{0,15},{1,0},{2,1},{3,2},{4,3},{5,4},{6,5},{7,6},{8,7},{9,8},{10,9... | collective-permute-start | bytes 983048 | tf_op jit(solution)/shard_map/ppermute | solution.py:398
  75.3 7.6 %collective-permute-start.14 = (bf16[1280,128]{1,0:T(8,128)(2,1)S(1)}, bf16[1280,128]{1,0:T(8,128)(2,1)S(1)}, u32[]{:S(2)}, u32[]{:S(2)}) collective-permute-start(bf16[1280,128]{1,0:T(8,128)(2,1)S(1)} %get-tuple-element.48), channel_id=1, source_target_pairs={{0,1},{1,2},{2,3},{3,4},{4,5},{5,6},{6,7},{7,8},{8,9},{9,10},{10,1... | collective-permute-start | bytes 983048 | tf_op jit(solution)/shard_map/ppermute | solution.py:398
  75.3 8.2 %collective-permute-start.15 = (bf16[1280,128]{1,0:T(8,128)(2,1)S(1)}, bf16[1280,128]{1,0:T(8,128)(2,1)S(1)}, u32[]{:S(2)}, u32[]{:S(2)}) collective-permute-start(bf16[1280,128]{1,0:T(8,128)(2,1)S(1)} %get-tuple-element.49), channel_id=1, source_target_pairs={{0,15},{1,0},{2,1},{3,2},{4,3},{5,4},{6,5},{7,6},{8,7},{9,8},{10,9... | collective-permute-start | bytes 983048 | tf_op jit(solution)/shard_map/ppermute | solution.py:398

commit v10 on v9

--- a/solution.py
+++ b/solution.py
@@ -129,9 +129,12 @@
             dest[block(f, row + r, col + c)] = jnp.zeros((f.b, f.b), dest.dtype) if i is None else read(i)
 
 
-def pack(f, source, packed, places):
-    for i, (r, c) in enumerate(places):
-        packed[block(f, i, 0)] = source[block(f, r, c)]
+def pack_edges(f, drop_ref, low, high, to_cross, to_mate):
+    odd = odd_place(f, drop_ref)
+    for i, (lower, upper) in enumerate(zip(under(f.h), over(f.h))):
+        back, forth = low[block(f, *lower)], high[block(f, *upper)]
+        to_cross[block(f, i, 0)] = jnp.where(odd, forth, back)
+        to_mate[block(f, i, 0)] = jnp.where(odd, back, forth)
 
 
 def slabs_kernel(f, drop_ref, own, corner, corner_again, to_mate, to_cross):
@@ -261,7 +264,7 @@
 
 
 def first_edges_kernel(
-    f, drop_ref, mate, cross, correction, partial, low, high, to_prev, to_next, before, after
+    f, drop_ref, mate, cross, correction, partial, low, high, to_cross, to_mate, before, after
 ):
     p = f.p
     below, above = sides(f, drop_ref, indexed(f, mate, len(under(f.h))), indexed(f, cross))
@@ -273,8 +276,7 @@
         return partial[at(f, place, place + 1, col - p, col - p + 1)]
 
     edges(f, drop_ref, plain(before), plain(after), correction, start, low, high)
-    pack(f, low, to_prev, under(f.h))
-    pack(f, high, to_next, over(f.h))
+    pack_edges(f, drop_ref, low, high, to_cross, to_mate)
 
 
 def gather(f, whole, low, own, high):
@@ -292,7 +294,7 @@
 
 
 def second_edges_kernel(
-    f, drop_ref, corner_below, corner_above, correction, low, high, new_low, new_high, to_prev, to_next
+    f, drop_ref, mate, cross, correction, low, high, new_low, new_high, to_cross, to_mate
 ):
     p = f.p
 
@@ -307,18 +309,19 @@
                 )
         return total
 
-    edges(f, drop_ref, plain(corner_below), plain(corner_above), correction, start, new_low, new_high)
-    pack(f, new_low, to_prev, under(f.h))
-    pack(f, new_high, to_next, over(f.h))
+    below, above = sides(f, drop_ref, plain(mate), plain(cross))
+    edges(f, drop_ref, below, above, correction, start, new_low, new_high)
+    pack_edges(f, drop_ref, new_low, new_high, to_cross, to_mate)
 
 
 def density_edges_kernel(
-    f, drop_ref, own, from_below, from_above, correction, new_low, new_high, square, whole, to_prev, to_next,
+    f, drop_ref, own, cross, mate, correction, new_low, new_high, square, whole, to_cross, to_mate,
     before, after, low, high,
 ):
     h, p = f.h, f.p
-    spread(f, before, 0, 0, indexed(f, from_below), over(h))
-    spread(f, after, 0, 0, indexed(f, from_above), under(h))
+    below, above = sides(f, drop_ref, indexed(f, mate), indexed(f, cross))
+    spread(f, before, 0, 0, below, over(h))
+    spread(f, after, 0, 0, above, under(h))
     for row, col in f.tiles(f.own_pairs):
         if row not in f.own_pairs:
             continue
@@ -339,8 +342,7 @@
         total = masked(f, right_tile(f, square, whole, row, col), row, col, drop_ref)
         dest, local = (low, row) if row < p else (high, row - 2 * p)
         dest[at(f, local, local + 1, col - p, col - p + 1)] = total.astype(dest.dtype)
-    pack(f, low, to_prev, under(f.h))
-    pack(f, high, to_next, over(f.h))
+    pack_edges(f, drop_ref, low, high, to_cross, to_mate)
 
 
 def density_own_kernel(f, drop_ref, square, whole, out):
@@ -351,9 +353,9 @@
             out[at(f, row - p, row - p + 1, col - p, col - p + 1)] = total.astype(out.dtype)
 
 
-def rows_kernel(f, first, drop_ref, own, from_below, from_above, out):
+def rows_kernel(f, first, drop_ref, own, cross, mate, out):
     h = f.h
-    below, above = indexed(f, from_below), indexed(f, from_above)
+    below, above = sides(f, drop_ref, indexed(f, mate), indexed(f, cross))
     over_index = {place: i for i, place in enumerate(over(h))}
     under_index = {place: i for i, place in enumerate(under(h))}
     for r in range(h):
@@ -420,12 +422,6 @@
     def to_cross(x):
         return routed(x, cross_step)
 
-    def to_next(x):
-        return routed(x, lambda i: 1)
-
-    def to_prev(x):
-        return routed(x, lambda i: -1)
-
     positions = block_cols - (me * rows + jnp.arange(rows, dtype=jnp.int32))[:, None] + half
     positions = positions + jnp.where(positions < 0, total, jnp.where(positions >= total, -total, 0))
     own_drop = width * (width + 1) // 2 - jnp.sum(positions, axis=1)
@@ -480,40 +476,39 @@
         [whole_scratch, group_scratch, group_scratch],
         66, 24, drop, shifted, corner, slab_mate, triangle_cross, from_mate, cross_triangle, light=True,
     )
-    next_corner_below, next_corner_above = to_next(own), to_prev(own)
-    low, high, back, forth = run(
+    corner_cross, corner_mate = to_cross(own), to_mate(own)
+    low, high, edge_cross, edge_mate = run(
         first_edges_kernel,
         [square_group, square_group, triangle, triangle],
         [group_scratch] * 2,
         10, 16, drop, from_mate, cross_corner, correction, partial,
     )
-    from_above, from_below = to_prev(back), to_next(forth)
+    edge_cross, edge_mate = to_cross(edge_cross), to_mate(edge_mate)
     (correction,) = run(
         correction_kernel, [columns], [whole_scratch], 38, 16, drop, shifted, low, own, high
     )
-    new_low, new_high, back, forth = run(
+    new_low, new_high, inverse_cross, inverse_mate = run(
         second_edges_kernel,
         [square_group, square_group, triangle, triangle],
         [],
-        20, 12, drop, next_corner_below, next_corner_above, correction, low, high,
-    )
-    inverse_above, inverse_below = to_prev(back), to_next(forth)
-    whole, back, forth = run(
+        20, 12, drop, corner_mate, corner_cross, correction, low, high,
+    )
+    inverse_cross, inverse_mate = to_cross(inverse_cross), to_mate(inverse_mate)
+    whole, rim_cross, rim_mate = run(
         density_edges_kernel,
         [columns, triangle, triangle],
         [group_scratch] * 4,
-        38, 20, drop, own, from_below, from_above, correction, new_low, new_high, square,
-    )
-    density_above, density_below = to_prev(back), to_next(forth)
+        38, 20, drop, own, edge_cross, edge_mate, correction, new_low, new_high, square,
+    )
+    rim_cross, rim_mate = to_cross(rim_cross), to_mate(rim_mate)
     (density_own,) = run(density_own_kernel, [square_group], [], 18, 12, drop, square, whole)
     out = jax.ShapeDtypeStruct(density.shape, kind)
 
-    def assembled(own, first, from_below, from_above):
-        kernel = functools.partial(rows_kernel, f, first)
-        return call(kernel, [out], [], 0, 8, drop, own, from_below, from_above)[0]
-
-    inverse_next = assembled(whole, half, inverse_below, inverse_above)
-    density_next = assembled(density_own, 0, density_below, density_above)
+    def assembled(own, first, cross, mate):
+        return call(functools.partial(rows_kernel, f, first), [out], [], 0, 8, drop, own, cross, mate)[0]
+
+    inverse_next = assembled(whole, half, inverse_cross, inverse_mate)
+    density_next = assembled(density_own, 0, rim_cross, rim_mate)
     return density_next, inverse_next
 
 

time: 86.3 us -> 85.8 us (level)
  starting transfers between devices: 20.3 us -> 25.9 us
  waiting for transfers between devices: 38 us -> 32.7 us
    ppermute x18, starting transfers between devices: 20.3 us -> 25.9 us  [routed(): lax.ppermute(x, RING, [(i, (i + step(i)) % size) for i in range(size) if...]
    ppermute x18, waiting for transfers between devices: 38 us -> 32.7 us  [routed(): lax.ppermute(x, RING, [(i, (i + step(i)) % size) for i in range(size) if...]
  transfers between devices with their start and end apart: 18 -> 18, of which waited for: 10 -> 7; matrix products, arithmetic and copies ran while one was open for 1% -> 1% of each run, Pallas kernels for 24% -> 24%
where the time goes in v10:
time: 85.8 us; the launch traced here: 85.5 us
  waiting for transfers between devices  32.7 us (38%)
  starting transfers between devices  25.9 us (30%)
  Pallas kernels  23.2 us (27%)
  local copies, waits for them, and re-layouts  2.05 us (2%)
  other arithmetic  1.04 us (1%)
    ppermute x18, waiting for transfers between devices, routed(): lax.ppermute(x, RING, [(i, (i + step(i)) % size) for i in range(size) if...  32.7 us
    ppermute x18, starting transfers between devices, routed(): lax.ppermute(x, RING, [(i, (i + step(i)) % size) for i in range(size) if...  25.9 us
    pallas_call x11, Pallas kernels, call(): pl.pallas_call(kernel, out_shape=[*outs, *[jax.ShapeDtypeStruct(a.shape,...  23.2 us
    unnamed x8, local copies, waits for them, and re-layouts  2.05 us
  transfers between devices with their start and end apart: 18, of which 7 were waited for; matrix products, arithmetic and copies ran while one was open for 1% of the time, Pallas kernels for 24%

profile of v10, /device:TPU:1, one launch (start us, length us, event | category | flops | bytes accessed | tf_op | source)
XLA Modules:
  0.0 85.5 jit_solution(7260325093364812975)
XLA Ops:
  0.6 2.7 %collective-permute-start.2 = (bf16[4,8,128,128]{3,2,1,0:T(8,128)(2,1)}, bf16[4,8,128,128]{3,2,1,0:T(8,128)(2,1)S(1)}, u32[]{:S(2)}, u32[]{:S(2)}) collective-permute-start(bf16[4,8,128,128]{3,2,1,0:T(8,128)(2,1)} %own.3), channel_id=1, source_target_pairs={{0,15},{1,2},{2,1},{3,4},{4,3},{5,6},{6,5},{7,8},{8,7},{9,10},{10,... | collective-permute-start | bytes 3145736 | tf_op jit(solution)/shard_map/ppermute | solution.py:400
  3.3 2.9 %collective-permute-start.3 = (bf16[4,8,128,128]{3,2,1,0:T(8,128)(2,1)}, bf16[4,8,128,128]{3,2,1,0:T(8,128)(2,1)S(1)}, u32[]{:S(2)}, u32[]{:S(2)}) collective-permute-start(bf16[4,8,128,128]{3,2,1,0:T(8,128)(2,1)} %own.3), channel_id=1, source_target_pairs={{0,1},{1,0},{2,3},{3,2},{4,5},{5,4},{6,7},{7,6},{8,9},{9,8},{10,11... | collective-permute-start | bytes 3145736 | tf_op jit(solution)/shard_map/ppermute | solution.py:400
  7.1 1.2 %copy-done = bf16[4,8,128,128]{3,2,1,0:T(8,128)(2,1)S(1)} copy-done((bf16[4,8,128,128]{3,2,1,0:T(8,128)(2,1)S(1)}, bf16[4,8,128,128]{3,2,1,0:T(8,128)(2,1)}, u32[]{:S(2)}) %copy-start) | copy-done | bytes 1048600
  8.4 2.1 %shard_map.50 = (bf16[2048,128]{1,0:T(8,128)(2,1)S(1)}, bf16[2048,128]{1,0:T(8,128)(2,1)}, bf16[3328,128]{1,0:T(8,128)(2,1)}, bf16[1280,128]{1,0:T(8,128)(2,1)S(1)}) custom-call(s32[5]{0:T(128)S(1)} %pad_add_fusion.1.drop_ref, bf16[4,8,128,128]{3,2,1,0:T(8,128)(2,1)S(1)} %copy-done), custom_call_target="tpu_custom_call" | custom-call | bytes 3276800 | tf_op jit(solution)/shard_map/pallas_call | solution.py:386
  11.7 1.5 %collective-permute-done.1 = s32[4]{0:T(128)S(1)} collective-permute-done((s32[4]{0:T(128)S(1)}, s32[4]{0:T(128)S(1)}, u32[]{:S(2)}, u32[]{:S(2)}) %collective-permute-start.1) | collective-permute-done | bytes 48 | tf_op jit(solution)/shard_map/ppermute | solution.py:400
  13.2 14.1 %collective-permute-done = s32[4]{0:T(128)S(1)} collective-permute-done((s32[4]{0:T(128)S(1)}, s32[4]{0:T(128)S(1)}, u32[]{:S(2)}, u32[]{:S(2)}) %collective-permute-start) | collective-permute-done | bytes 48 | tf_op jit(solution)/shard_map/ppermute | solution.py:400
  28.2 1.8 %collective-permute-start.8 = (bf16[1280,128]{1,0:T(8,128)(2,1)S(1)}, bf16[1280,128]{1,0:T(8,128)(2,1)S(1)}, u32[]{:S(2)}, u32[]{:S(2)}) collective-permute-start(bf16[1280,128]{1,0:T(8,128)(2,1)S(1)} %get-tuple-element.36.sent_cross), channel_id=1, source_target_pairs={{0,15},{1,2},{2,1},{3,4},{4,3},{5,6},{6,5},{7,8},{8,7},{9,10},{10,... | collective-permute-start | bytes 983048 | tf_op jit(solution)/shard_map/ppermute | solution.py:400
  30.1 6.3 %collective-permute-start.6 = (bf16[640,128]{1,0:T(8,128)(2,1)S(1)}, bf16[640,128]{1,0:T(8,128)(2,1)S(1)}, u32[]{:S(2)}, u32[]{:S(2)}) collective-permute-start(bf16[640,128]{1,0:T(8,128)(2,1)S(1)} %get-tuple-element.31), channel_id=1, source_target_pairs={{0,1},{1,0},{2,3},{3,2},{4,5},{5,4},{6,7},{7,6},{8,9},{9,8},{10,11... | collective-permute-start | bytes 491528 | tf_op jit(solution)/shard_map/ppermute | solution.py:400
  37.9 4.7 %shard_map.52 = (bf16[1536,1280]{1,0:T(8,128)(2,1)S(1)}, bf16[1536,1280]{1,0:T(8,128)(2,1)S(1)}) custom-call(s32[13]{0:T(128)S(1)} %pad_add_fusion.drop_ref, bf16[4,8,128,128]{3,2,1,0:T(8,128)(2,1)S(1)} %copy-done.1, bf16[4,8,128,128]{3,2,1,0:T(8,128)(2,1)S(1)} %collective-permute-done.2.cross, ...), custom_call_target="tpu_custom_call" | custom-call | tf_op jit(solution)/shard_map/pallas_call | solution.py:386
  42.6 3.8 %shard_map.53 = (bf16[1536,512]{1,0:T(8,128)(2,1)S(1)}, bf16[512,512]{1,0:T(8,128)(2,1)S(1)}, f32[1024,512]{1,0:T(8,128)S(1)}) custom-call(s32[13]{0:T(128)S(1)} %pad_add_fusion.drop_ref, bf16[1536,1280]{1,0:T(8,128)(2,1)S(1)} %get-tuple-element.34.shifted, bf16[2048,128]{1,0:T(8,128)(2,1)S(1)} %copy-done.3, bf16[3328,128]{1,0:T(8,128)(2,1)} %get-tuple-element.27.sent_mate, ...), custom_call_target="tpu_custom_call" | custom-call | tf_op jit(solution)/shard_map/pallas_call | solution.py:386
  46.4 3.6 %collective-permute-start.13 = (bf16[512,512]{1,0:T(8,128)(2,1)S(1)}, bf16[512,512]{1,0:T(8,128)(2,1)S(1)}, u32[]{:S(2)}, u32[]{:S(2)}) collective-permute-start(bf16[512,512]{1,0:T(8,128)(2,1)S(1)} %get-tuple-element.37.own), channel_id=1, source_target_pairs={{0,15},{1,2},{2,1},{3,4},{4,3},{5,6},{6,5},{7,8},{8,7},{9,10},{10,... | collective-permute-start | bytes 1572872 | tf_op jit(solution)/shard_map/ppermute | solution.py:400
  50.0 1.3 %shard_map.54 = (bf16[512,512]{1,0:T(8,128)(2,1)S(1)}, bf16[512,512]{1,0:T(8,128)(2,1)S(1)}, bf16[1280,128]{1,0:T(8,128)(2,1)S(1)}, bf16[1280,128]{1,0:T(8,128)(2,1)S(1)}) custom-call(s32[13]{0:T(128)S(1)} %pad_add_fusion.drop_ref, bf16[3328,128]{1,0:T(8,128)(2,1)S(1)} %collective-permute-done.4.refs_1_.mate, ...), custom_call_target="tpu_custom_call" | custom-call | flops 335544320 | bytes 6750208 | tf_op jit(solution)/shard_map/pallas_call | solution.py:386
  51.4 1.3 %collective-permute-start.10 = (bf16[1280,128]{1,0:T(8,128)(2,1)S(1)}, bf16[1280,128]{1,0:T(8,128)(2,1)S(1)}, u32[]{:S(2)}, u32[]{:S(2)}) collective-permute-start(bf16[1280,128]{1,0:T(8,128)(2,1)S(1)} %get-tuple-element.41), channel_id=1, source_target_pairs={{0,15},{1,2},{2,1},{3,4},{4,3},{5,6},{6,5},{7,8},{8,7},{9,10},{10,... | collective-permute-start | bytes 983048 | tf_op jit(solution)/shard_map/ppermute | solution.py:400
  52.7 2.1 %collective-permute-start.11 = (bf16[1280,128]{1,0:T(8,128)(2,1)S(1)}, bf16[1280,128]{1,0:T(8,128)(2,1)S(1)}, u32[]{:S(2)}, u32[]{:S(2)}) collective-permute-start(bf16[1280,128]{1,0:T(8,128)(2,1)S(1)} %get-tuple-element.42), channel_id=1, source_target_pairs={{0,1},{1,0},{2,3},{3,2},{4,5},{5,4},{6,7},{7,6},{8,9},{9,8},{10,11... | collective-permute-start | bytes 983048 | tf_op jit(solution)/shard_map/ppermute | solution.py:400
  54.8 2.0 %shard_map.55.correction = bf16[1536,512]{1,0:T(8,128)(2,1)S(1)} custom-call(s32[13]{0:T(128)S(1)} %pad_add_fusion.drop_ref, bf16[1536,1280]{1,0:T(8,128)(2,1)S(1)} %get-tuple-element.34.shifted, bf16[512,512]{1,0:T(8,128)(2,1)S(1)} %get-tuple-element.43.low, bf16[512,512]{1,0:T(8,128)(2,1)S(1)} %get-tuple-element.37.own, ...), custom_call_target="tpu_custom_call" | custom-call | flops 1275068416 | bytes 7077888 | tf_op jit(solution)/shard_map/pallas_call | solution.py:386
  56.8 10.4 %collective-permute-done.13.cross = bf16[512,512]{1,0:T(8,128)(2,1)S(1)} collective-permute-done((bf16[512,512]{1,0:T(8,128)(2,1)S(1)}, bf16[512,512]{1,0:T(8,128)(2,1)S(1)}, u32[]{:S(2)}, u32[]{:S(2)}) %collective-permute-start.13) | collective-permute-done | bytes 524320 | tf_op jit(solution)/shard_map/ppermute | solution.py:400
  67.2 1.5 %shard_map.56 = (bf16[512,512]{1,0:T(8,128)(2,1)S(1)}, bf16[512,512]{1,0:T(8,128)(2,1)S(1)}, bf16[1280,128]{1,0:T(8,128)(2,1)S(1)}, bf16[1280,128]{1,0:T(8,128)(2,1)S(1)}) custom-call(s32[13]{0:T(128)S(1)} %pad_add_fusion.drop_ref, bf16[512,512]{1,0:T(8,128)(2,1)S(1)} %collective-permute-done.12.mate, bf16[512,512]{1,0:T(8,128)(2,1)S(1)} %collective-permute-done.13.cross, ...), custom_call_target="tpu_custom_call" | custom-call | flops 671088640 | bytes 5373952 | tf_op jit(solution)/shard_map/pallas_call | solution.py:386
  68.7 2.5 %collective-permute-start.16 = (bf16[1280,128]{1,0:T(8,128)(2,1)S(1)}, bf16[1280,128]{1,0:T(8,128)(2,1)S(1)}, u32[]{:S(2)}, u32[]{:S(2)}) collective-permute-start(bf16[1280,128]{1,0:T(8,128)(2,1)S(1)} %get-tuple-element.50), channel_id=1, source_target_pairs={{0,15},{1,2},{2,1},{3,4},{4,3},{5,6},{6,5},{7,8},{8,7},{9,10},{10,... | collective-permute-start | bytes 983048 | tf_op jit(solution)/shard_map/ppermute | solution.py:400
  71.2 2.3 %shard_map.57 = (bf16[1536,512]{1,0:T(8,128)(2,1)S(1)}, bf16[1280,128]{1,0:T(8,128)(2,1)S(1)}, bf16[1280,128]{1,0:T(8,128)(2,1)S(1)}) custom-call(s32[13]{0:T(128)S(1)} %pad_add_fusion.drop_ref, bf16[512,512]{1,0:T(8,128)(2,1)S(1)} %get-tuple-element.37.own, bf16[1280,128]{1,0:T(8,128)(2,1)S(1)} %collective-permute-done.10.cross, ...), custom_call_target="tpu_custom_call" | custom-call | flops 1275068416 | bytes 9961472 | tf_op jit(solution)/shard_map/pallas_call | solution.py:386
  73.5 2.0 %collective-permute-start.14 = (bf16[1280,128]{1,0:T(8,128)(2,1)S(1)}, bf16[1280,128]{1,0:T(8,128)(2,1)S(1)}, u32[]{:S(2)}, u32[]{:S(2)}) collective-permute-start(bf16[1280,128]{1,0:T(8,128)(2,1)S(1)} %get-tuple-element.48), channel_id=1, source_target_pairs={{0,15},{1,2},{2,1},{3,4},{4,3},{5,6},{6,5},{7,8},{8,7},{9,10},{10,... | collective-permute-start | bytes 983048 | tf_op jit(solution)/shard_map/ppermute | solution.py:400
  75.5 1.3 %shard_map.58.own = bf16[512,512]{1,0:T(8,128)(2,1)S(1)} custom-call(s32[13]{0:T(128)S(1)} %pad_add_fusion.drop_ref, bf16[1536,1280]{1,0:T(8,128)(2,1)S(1)} %get-tuple-element.33.square, bf16[1536,512]{1,0:T(8,128)(2,1)S(1)} %get-tuple-element.47.whole.own), custom_call_target="tpu_custom_call" | custom-call | flops 603979776 | bytes 6029312 | tf_op jit(solution)/shard_map/pallas_call | solution.py:386
  76.9 1.8 %shard_map.60 = bf16[4,8,128,128]{3,2,1,0:T(8,128)(2,1)} custom-call(s32[13]{0:T(128)S(1)} %pad_add_fusion.drop_ref, bf16[1536,512]{1,0:T(8,128)(2,1)S(1)} %get-tuple-element.47.whole.own, bf16[1280,128]{1,0:T(8,128)(2,1)S(1)} %collective-permute-done.16.cross, bf16[1280,128]{1,0:T(8,128)(2,1)S(1)} %collective-permute-done.17.mate), custom_call_target="tpu_custom_call" | custom-call | bytes 3276800 | tf_op jit(solution)/shard_map/pallas_call | solution.py:386
  78.6 5.1 %collective-permute-done.14.cross = bf16[1280,128]{1,0:T(8,128)(2,1)S(1)} collective-permute-done((bf16[1280,128]{1,0:T(8,128)(2,1)S(1)}, bf16[1280,128]{1,0:T(8,128)(2,1)S(1)}, u32[]{:S(2)}, u32[]{:S(2)}) %collective-permute-start.14) | collective-permute-done | bytes 327712 | tf_op jit(solution)/shard_map/ppermute | solution.py:400
  83.8 1.8 %shard_map.59 = bf16[4,8,128,128]{3,2,1,0:T(8,128)(2,1)} custom-call(s32[13]{0:T(128)S(1)} %pad_add_fusion.drop_ref, bf16[512,512]{1,0:T(8,128)(2,1)S(1)} %shard_map.58.own, bf16[1280,128]{1,0:T(8,128)(2,1)S(1)} %collective-permute-done.14.cross, bf16[1280,128]{1,0:T(8,128)(2,1)S(1)} %collective-permute-done.15.mate), custom_call_target="tpu_custom_call" | custom-call | bytes 2228224 | tf_op jit(solution)/shard_map/pallas_call | solution.py:386
  (37 shorter events, 4.8 us)
Async XLA Ops:
  0.6 26.8 %collective-permute-start.2 = (bf16[4,8,128,128]{3,2,1,0:T(8,128)(2,1)}, bf16[4,8,128,128]{3,2,1,0:T(8,128)(2,1)S(1)}, u32[]{:S(2)}, u32[]{:S(2)}) collective-permute-start(bf16[4,8,128,128]{3,2,1,0:T(8,128)(2,1)} %own.3), channel_id=1, source_target_pairs={{0,15},{1,2},{2,1},{3,4},{4,3},{5,6},{6,5},{7,8},{8,7},{9,10},{10,... | collective-permute-start | bytes 3145736 | tf_op jit(solution)/shard_map/ppermute | solution.py:400
  3.3 24.1 %collective-permute-start.3 = (bf16[4,8,128,128]{3,2,1,0:T(8,128)(2,1)}, bf16[4,8,128,128]{3,2,1,0:T(8,128)(2,1)S(1)}, u32[]{:S(2)}, u32[]{:S(2)}) collective-permute-start(bf16[4,8,128,128]{3,2,1,0:T(8,128)(2,1)} %own.3), channel_id=1, source_target_pairs={{0,1},{1,0},{2,3},{3,2},{4,5},{5,4},{6,7},{7,6},{8,9},{9,8},{10,11... | collective-permute-start | bytes 3145736 | tf_op jit(solution)/shard_map/ppermute | solution.py:400
  7.1 1.2 %copy-start = (bf16[4,8,128,128]{3,2,1,0:T(8,128)(2,1)S(1)}, bf16[4,8,128,128]{3,2,1,0:T(8,128)(2,1)}, u32[]{:S(2)}) copy-start(bf16[4,8,128,128]{3,2,1,0:T(8,128)(2,1)} %own.2) | copy-start | bytes 3145732
  10.4 0.8 copy-start.2
  11.2 16.2 %collective-permute-start.4 = (bf16[3328,128]{1,0:T(8,128)(2,1)}, bf16[3328,128]{1,0:T(8,128)(2,1)S(1)}, u32[]{:S(2)}, u32[]{:S(2)}) collective-permute-start(bf16[3328,128]{1,0:T(8,128)(2,1)} %get-tuple-element.27.sent_mate), channel_id=1, source_target_pairs={{0,1},{1,0},{2,3},{3,2},{4,5},{5,4},{6,7},{7,6},{8,9},{9,8},{10,11... | collective-permute-start | bytes 2555912 | tf_op jit(solution)/shard_map/ppermute | solution.py:400
  11.2 2.0 %collective-permute-start.1 = (s32[4]{0:T(128)S(1)}, s32[4]{0:T(128)S(1)}, u32[]{:S(2)}, u32[]{:S(2)}) collective-permute-start(s32[4]{0:T(128)S(1)} %broadcast_subtract_fusion), channel_id=1, source_target_pairs={{0,1},{1,0},{2,3},{3,2},{4,5},{5,4},{6,7},{7,6},{8,9},{9,8},{10,11... | collective-permute-start | bytes 56 | tf_op jit(solution)/shard_map/ppermute | solution.py:400
  11.7 15.6 %collective-permute-start = (s32[4]{0:T(128)S(1)}, s32[4]{0:T(128)S(1)}, u32[]{:S(2)}, u32[]{:S(2)}) collective-permute-start(s32[4]{0:T(128)S(1)} %broadcast_subtract_fusion), channel_id=1, source_target_pairs={{0,15},{1,2},{2,1},{3,4},{4,3},{5,6},{6,5},{7,8},{8,7},{9,10},{10,... | collective-permute-start | bytes 56 | tf_op jit(solution)/shard_map/ppermute | solution.py:400
  11.7 26.2 %copy-start.1 = (bf16[4,8,128,128]{3,2,1,0:T(8,128)(2,1)S(1)}, bf16[4,8,128,128]{3,2,1,0:T(8,128)(2,1)}, u32[]{:S(2)}) copy-start(bf16[4,8,128,128]{3,2,1,0:T(8,128)(2,1)} %own.3) | copy-start | bytes 3145732
  28.1 14.5 %copy-start.3 = (bf16[2048,128]{1,0:T(8,128)(2,1)S(1)}, bf16[2048,128]{1,0:T(8,128)(2,1)}, u32[]{:S(2)}) copy-start(bf16[2048,128]{1,0:T(8,128)(2,1)} %copy-done.2) | copy-start | bytes 1572868
  28.1 9.8 %collective-permute-start.5 = (bf16[1280,128]{1,0:T(8,128)(2,1)S(1)}, bf16[1280,128]{1,0:T(8,128)(2,1)S(1)}, u32[]{:S(2)}, u32[]{:S(2)}) collective-permute-start(bf16[1280,128]{1,0:T(8,128)(2,1)S(1)} %get-tuple-element.30), channel_id=1, source_target_pairs={{0,13},{1,4},{2,15},{3,6},{4,1},{5,8},{6,3},{7,10},{8,5},{9,12},{1... | collective-permute-start | bytes 983048 | tf_op jit(solution)/shard_map/ppermute | solution.py:400
  28.2 14.4 %collective-permute-start.8 = (bf16[1280,128]{1,0:T(8,128)(2,1)S(1)}, bf16[1280,128]{1,0:T(8,128)(2,1)S(1)}, u32[]{:S(2)}, u32[]{:S(2)}) collective-permute-start(bf16[1280,128]{1,0:T(8,128)(2,1)S(1)} %get-tuple-element.36.sent_cross), channel_id=1, source_target_pairs={{0,15},{1,2},{2,1},{3,4},{4,3},{5,6},{6,5},{7,8},{8,7},{9,10},{10,... | collective-permute-start | bytes 983048 | tf_op jit(solution)/shard_map/ppermute | solution.py:400
  30.0 20.0 %collective-permute-start.9 = (bf16[2048,128]{1,0:T(8,128)(2,1)}, bf16[2048,128]{1,0:T(8,128)(2,1)S(1)}, u32[]{:S(2)}, u32[]{:S(2)}) collective-permute-start(bf16[2048,128]{1,0:T(8,128)(2,1)} %get-tuple-element.38), channel_id=1, source_target_pairs={{0,15},{1,2},{2,1},{3,4},{4,3},{5,6},{6,5},{7,8},{8,7},{9,10},{10,... | collective-permute-start | bytes 1572872 | tf_op jit(solution)/shard_map/ppermute | solution.py:400
  30.1 7.3 %collective-permute-start.6 = (bf16[640,128]{1,0:T(8,128)(2,1)S(1)}, bf16[640,128]{1,0:T(8,128)(2,1)S(1)}, u32[]{:S(2)}, u32[]{:S(2)}) collective-permute-start(bf16[640,128]{1,0:T(8,128)(2,1)S(1)} %get-tuple-element.31), channel_id=1, source_target_pairs={{0,1},{1,0},{2,3},{3,2},{4,5},{5,4},{6,7},{7,6},{8,9},{9,8},{10,11... | collective-permute-start | bytes 491528 | tf_op jit(solution)/shard_map/ppermute | solution.py:400
  36.4 1.4 %collective-permute-start.7 = (bf16[640,128]{1,0:T(8,128)(2,1)S(1)}, bf16[640,128]{1,0:T(8,128)(2,1)S(1)}, u32[]{:S(2)}, u32[]{:S(2)}) collective-permute-start(bf16[640,128]{1,0:T(8,128)(2,1)S(1)} %get-tuple-element.32), channel_id=1, source_target_pairs={{0,1},{1,0},{2,3},{3,2},{4,5},{5,4},{6,7},{7,6},{8,9},{9,8},{10,11... | collective-permute-start | bytes 491528 | tf_op jit(solution)/shard_map/ppermute | solution.py:400
  46.4 20.8 %collective-permute-start.13 = (bf16[512,512]{1,0:T(8,128)(2,1)S(1)}, bf16[512,512]{1,0:T(8,128)(2,1)S(1)}, u32[]{:S(2)}, u32[]{:S(2)}) collective-permute-start(bf16[512,512]{1,0:T(8,128)(2,1)S(1)} %get-tuple-element.37.own), channel_id=1, source_target_pairs={{0,15},{1,2},{2,1},{3,4},{4,3},{5,6},{6,5},{7,8},{8,7},{9,10},{10,... | collective-permute-start | bytes 1572872 | tf_op jit(solution)/shard_map/ppermute | solution.py:400
  50.0 17.2 %collective-permute-start.12 = (bf16[512,512]{1,0:T(8,128)(2,1)S(1)}, bf16[512,512]{1,0:T(8,128)(2,1)S(1)}, u32[]{:S(2)}, u32[]{:S(2)}) collective-permute-start(bf16[512,512]{1,0:T(8,128)(2,1)S(1)} %get-tuple-element.37.own), channel_id=1, source_target_pairs={{0,1},{1,0},{2,3},{3,2},{4,5},{5,4},{6,7},{7,6},{8,9},{9,8},{10,11... | collective-permute-start | bytes 1572872 | tf_op jit(solution)/shard_map/ppermute | solution.py:400
  51.4 19.9 %collective-permute-start.10 = (bf16[1280,128]{1,0:T(8,128)(2,1)S(1)}, bf16[1280,128]{1,0:T(8,128)(2,1)S(1)}, u32[]{:S(2)}, u32[]{:S(2)}) collective-permute-start(bf16[1280,128]{1,0:T(8,128)(2,1)S(1)} %get-tuple-element.41), channel_id=1, source_target_pairs={{0,15},{1,2},{2,1},{3,4},{4,3},{5,6},{6,5},{7,8},{8,7},{9,10},{10,... | collective-permute-start | bytes 983048 | tf_op jit(solution)/shard_map/ppermute | solution.py:400
  52.7 18.6 %collective-permute-start.11 = (bf16[1280,128]{1,0:T(8,128)(2,1)S(1)}, bf16[1280,128]{1,0:T(8,128)(2,1)S(1)}, u32[]{:S(2)}, u32[]{:S(2)}) collective-permute-start(bf16[1280,128]{1,0:T(8,128)(2,1)S(1)} %get-tuple-element.42), channel_id=1, source_target_pairs={{0,1},{1,0},{2,3},{3,2},{4,5},{5,4},{6,7},{7,6},{8,9},{9,8},{10,11... | collective-permute-start | bytes 983048 | tf_op jit(solution)/shard_map/ppermute | solution.py:400
  68.7 8.2 %collective-permute-start.16 = (bf16[1280,128]{1,0:T(8,128)(2,1)S(1)}, bf16[1280,128]{1,0:T(8,128)(2,1)S(1)}, u32[]{:S(2)}, u32[]{:S(2)}) collective-permute-start(bf16[1280,128]{1,0:T(8,128)(2,1)S(1)} %get-tuple-element.50), channel_id=1, source_target_pairs={{0,15},{1,2},{2,1},{3,4},{4,3},{5,6},{6,5},{7,8},{8,7},{9,10},{10,... | collective-permute-start | bytes 983048 | tf_op jit(solution)/shard_map/ppermute | solution.py:400
  71.2 5.6 %collective-permute-start.17 = (bf16[1280,128]{1,0:T(8,128)(2,1)S(1)}, bf16[1280,128]{1,0:T(8,128)(2,1)S(1)}, u32[]{:S(2)}, u32[]{:S(2)}) collective-permute-start(bf16[1280,128]{1,0:T(8,128)(2,1)S(1)} %get-tuple-element.51), channel_id=1, source_target_pairs={{0,1},{1,0},{2,3},{3,2},{4,5},{5,4},{6,7},{7,6},{8,9},{9,8},{10,11... | collective-permute-start | bytes 983048 | tf_op jit(solution)/shard_map/ppermute | solution.py:400
  73.5 10.3 %collective-permute-start.14 = (bf16[1280,128]{1,0:T(8,128)(2,1)S(1)}, bf16[1280,128]{1,0:T(8,128)(2,1)S(1)}, u32[]{:S(2)}, u32[]{:S(2)}) collective-permute-start(bf16[1280,128]{1,0:T(8,128)(2,1)S(1)} %get-tuple-element.48), channel_id=1, source_target_pairs={{0,15},{1,2},{2,1},{3,4},{4,3},{5,6},{6,5},{7,8},{8,7},{9,10},{10,... | collective-permute-start | bytes 983048 | tf_op jit(solution)/shard_map/ppermute | solution.py:400
  75.5 8.3 %collective-permute-start.15 = (bf16[1280,128]{1,0:T(8,128)(2,1)S(1)}, bf16[1280,128]{1,0:T(8,128)(2,1)S(1)}, u32[]{:S(2)}, u32[]{:S(2)}) collective-permute-start(bf16[1280,128]{1,0:T(8,128)(2,1)S(1)} %get-tuple-element.49), channel_id=1, source_target_pairs={{0,1},{1,0},{2,3},{3,2},{4,5},{5,4},{6,7},{7,6},{8,9},{9,8},{10,11... | collective-permute-start | bytes 983048 | tf_op jit(solution)/shard_map/ppermute | solution.py:400

commit v11 on v10

--- a/solution.py
+++ b/solution.py
@@ -34,6 +34,13 @@
     def clipped(self, row, col):
         lo, hi = self.inner(row, col)
         return max(lo, 0), min(hi, self.pairs)
+
+    def on_corner(self, row, col):
+        return max(row, col) < self.p or min(row, col) >= 2 * self.p
+
+    def corner_place(self, row, col):
+        r, c = (row, col) if row < self.p else (row - self.p, col - 2 * self.p)
+        return r, r + 1, c, c + 1
 
     def split(self, row, col):
         lo, hi = self.clipped(row, col)
@@ -167,7 +174,7 @@
         to_far[block(f, i, 0)] = jnp.where(odd, forth, back)
 
 
-def square_kernel(f, drop_ref, own, cross, mate, far_far, far_mate, far_mate_too, square, shifted, wide):
+def square_kernel(f, drop_ref, own, cross, mate, square, shifted, reach, here, partial, wide):
     h, p = f.h, f.p
     below, above = sides(f, drop_ref, plain(mate), plain(cross))
     for g, read in enumerate((below, plain(own), above)):
@@ -180,37 +187,83 @@
                     value = stored(read, r, offset, drop_ref[row], f.k)
                 else:
                     value = jnp.zeros((f.b, f.b), wide.dtype)
-                wide[block(f, row + h, col + h)] = value
+                wide[block(f, row, col + h)] = value
+    for i in range(h):
+        for g, row in enumerate((i, 2 * h + i)):
+            rows = pl.ds((g * h + i) * f.b, f.b)
+            source = pl.ds(row * f.b, f.b)
+            reach[rows, :] = wide[source, pl.ds(4 * g * f.group, f.group)]
+            here[rows, :] = wide[source, pl.ds((2 * g + 1) * f.group, f.group)]
+    unit = unit_tile(f)
+    for row, col in f.tiles(range(f.pairs)):
+        lo, hi = f.clipped(row, col)
+        total = dot(
+            wide[at(f, row, row + 1, lo + p, hi + p)], wide[at(f, lo, hi, col + p, col + p + 1)]
+        )
+        if f.on_corner(row, col):
+            partial[at(f, *f.corner_place(row, col))] = total
+            continue
+        total = masked(f, total, row, col, drop_ref)
+        place = banded(f, row, col, col + 1)
+        tile = wide[at(f, row, row + 1, col + p, col + p + 1)].astype(jnp.float32)
+        square[place] = total.astype(square.dtype)
+        shifted[place] = moved(total, tile, unit if row == col else None).astype(shifted.dtype)
+
+
+def unit_tile(f):
+    rows = lax.broadcasted_iota(jnp.int32, (f.t, f.t), 0)
+    return (rows == lax.broadcasted_iota(jnp.int32, (f.t, f.t), 1)).astype(jnp.float32)
+
+
+def moved(total, tile, unit):
+    value = 2.0 * total - 2.0 * tile
+    return value if unit is None else value + unit
+
+
+def corners_kernel(
+    f, drop_ref, far_far, far_mate, far_mate_too, reach, here, partial, square, shifted, low, high
+):
+    p = f.p
     far_mates = [indexed(f, far_mate), indexed(f, far_mate_too)]
     far_below, far_above = sides(f, drop_ref, lambda i: far_mates[i % 2](i // 2), indexed(f, far_far))
-    spread(f, wide, 0, h, far_below, under(h))
-    spread(f, wide, 4 * h, 3 * h, far_above, over(h))
-    unit = (
-        lax.broadcasted_iota(jnp.int32, (f.t, f.t), 0) == lax.broadcasted_iota(jnp.int32, (f.t, f.t), 1)
-    ).astype(jnp.float32)
+    spread(f, low, 0, 0, far_below, under(f.h))
+    spread(f, high, 0, 0, far_above, over(f.h))
+    unit = unit_tile(f)
     for row, col in f.tiles(range(f.pairs)):
-        lo, hi = f.inner(row, col)
-        lo, hi = lo + p, hi + p
-        total = dot(
-            wide[at(f, row + p, row + p + 1, lo, hi)], wide[at(f, lo, hi, col + p, col + p + 1)]
-        )
+        if not f.on_corner(row, col):
+            continue
+        place = at(f, *f.corner_place(row, col))
+        r, _, c, _ = f.corner_place(row, col)
+        total = partial[place]
+        if row < p:
+            a, z, far = max(row, col), p, low
+        else:
+            a, z, far = 0, min(row, col) - 2 * p + 1, high
+        if a < z:
+            total = total + dot(reach[at(f, r, r + 1, a, z)], far[at(f, a, z, c, c + 1)])
         total = masked(f, total, row, col, drop_ref)
-        here = wide[at(f, row + p, row + p + 1, col + p, col + p + 1)]
-        moved = 2.0 * total - 2.0 * here.astype(jnp.float32)
-        if row == col:
-            moved = moved + unit
-        place = banded(f, row, col, col + 1)
+        tile = here[place].astype(jnp.float32)
         square[place] = total.astype(square.dtype)
-        shifted[place] = moved.astype(shifted.dtype)
-
-
-def right_tile(f, left, right, row, col):
+        shifted[place] = moved(total, tile, unit if row == col else None).astype(shifted.dtype)
+
+
+def right_tile(f, left, corners, right, row, col):
     lo, hi = f.clipped(row, col)
-    return dot(left[banded(f, row, lo, hi)], right[at(f, lo, hi, col - f.p, col - f.p + 1)])
+    total = None
+    if row < f.p:
+        inside = corners[at(f, row, row + 1, lo, f.p)]
+        total = dot(inside, right[at(f, lo, f.p, col - f.p, col - f.p + 1)])
+        lo = f.p
+    elif row >= 2 * f.p:
+        inside = corners[at(f, row - f.p, row - f.p + 1, 0, hi - 2 * f.p)]
+        total = dot(inside, right[at(f, 2 * f.p, hi, col - f.p, col - f.p + 1)])
+        hi = 2 * f.p
+    rest = dot(left[banded(f, row, lo, hi)], right[at(f, lo, hi, col - f.p, col - f.p + 1)])
+    return rest if total is None else total + rest
 
 
 def first_sweep_kernel(
-    f, drop_ref, shifted, corner, sent_mate, sent_cross, mate, cross,
+    f, drop_ref, shifted, corners, corner, sent_mate, sent_cross, mate, cross,
     correction, fresh, partial, whole, before, after,
 ):
     h, p = f.h, f.p
@@ -222,7 +275,7 @@
     spread(f, before, 0, 0, down, over(h))
     spread(f, after, 0, 0, up, under(h))
     for row, col in f.tiles(f.own_pairs):
-        total = masked(f, right_tile(f, shifted, whole, row, col), row, col, drop_ref)
+        total = masked(f, right_tile(f, shifted, corners, whole, row, col), row, col, drop_ref)
         correction[at(f, row, row + 1, col - p, col - p + 1)] = total.astype(correction.dtype)
     for row, col in f.tiles(f.own_pairs):
         c = col - p
@@ -285,16 +338,16 @@
             whole[pl.ds(g * f.group + i * f.b, f.b), :] = source[pl.ds(i * f.b, f.b), :]
 
 
-def correction_kernel(f, drop_ref, shifted, low, own, high, correction, whole):
+def correction_kernel(f, drop_ref, shifted, corners, low, own, high, correction, whole):
     p = f.p
     gather(f, whole, low, own, high)
     for row, col in f.tiles(f.own_pairs):
-        total = masked(f, right_tile(f, shifted, whole, row, col), row, col, drop_ref)
+        total = masked(f, right_tile(f, shifted, corners, whole, row, col), row, col, drop_ref)
         correction[at(f, row, row + 1, col - p, col - p + 1)] = total.astype(correction.dtype)
 
 
 def second_edges_kernel(
-    f, drop_ref, mate, cross, correction, low, high, new_low, new_high, to_cross, to_mate
+    f, drop_ref, cross, mate, correction, low, high, new_low, new_high, to_cross, to_mate
 ):
     p = f.p
 
@@ -315,7 +368,7 @@
 
 
 def density_edges_kernel(
-    f, drop_ref, own, cross, mate, correction, new_low, new_high, square, whole, to_cross, to_mate,
+    f, drop_ref, own, cross, mate, correction, new_low, new_high, square, corners, whole, to_cross, to_mate,
     before, after, low, high,
 ):
     h, p = f.h, f.p
@@ -339,7 +392,7 @@
     for row, col in f.tiles(f.own_pairs):
         if row in f.own_pairs:
             continue
-        total = masked(f, right_tile(f, square, whole, row, col), row, col, drop_ref)
+        total = masked(f, right_tile(f, square, corners, whole, row, col), row, col, drop_ref)
         dest, local = (low, row) if row < p else (high, row - 2 * p)
         dest[at(f, local, local + 1, col - p, col - p + 1)] = total.astype(dest.dtype)
     pack_edges(f, drop_ref, low, high, to_cross, to_mate)
@@ -349,7 +402,7 @@
     p = f.p
     for row, col in f.tiles(f.own_pairs):
         if row in f.own_pairs:
-            total = masked(f, right_tile(f, square, whole, row, col), row, col, drop_ref)
+            total = masked(f, right_tile(f, square, None, whole, row, col), row, col, drop_ref)
             out[at(f, row - p, row - p + 1, col - p, col - p + 1)] = total.astype(out.dtype)
 
 
@@ -464,17 +517,24 @@
     cross_triangle = to_cross(triangle_cross)
     cross_corner = to_cross(corner_cross)
 
-    square, shifted = run(
+    both_corners = jax.ShapeDtypeStruct((2 * f.group, f.group), kind)
+    square, shifted, reach, here, partial = run(
         square_kernel,
-        [band, band],
-        [pltpu.VMEM((5 * f.group, 5 * f.group), kind)],
-        94, 28, drop, density, density_cross, density_mate, far_far, far_mate, far_mate_too, light=True,
+        [band, band, both_corners, both_corners, partial_sums],
+        [pltpu.VMEM((3 * f.group, 5 * f.group), kind)],
+        84, 26, drop, density, density_cross, density_mate,
+    )
+    square_corners, shifted_corners = run(
+        corners_kernel,
+        [both_corners, both_corners],
+        [group_scratch] * 2,
+        10, 16, drop, far_far, far_mate, far_mate_too, reach, here, partial, light=True,
     )
     correction, own, partial = run(
         first_sweep_kernel,
         [columns, square_group, partial_sums],
         [whole_scratch, group_scratch, group_scratch],
-        66, 24, drop, shifted, corner, slab_mate, triangle_cross, from_mate, cross_triangle, light=True,
+        66, 24, drop, shifted, shifted_corners, corner, slab_mate, triangle_cross, from_mate, cross_triangle, light=True,
     )
     corner_cross, corner_mate = to_cross(own), to_mate(own)
     low, high, edge_cross, edge_mate = run(
@@ -485,13 +545,13 @@
     )
     edge_cross, edge_mate = to_cross(edge_cross), to_mate(edge_mate)
     (correction,) = run(
-        correction_kernel, [columns], [whole_scratch], 38, 16, drop, shifted, low, own, high
+        correction_kernel, [columns], [whole_scratch], 38, 16, drop, shifted, shifted_corners, low, own, high
     )
     new_low, new_high, inverse_cross, inverse_mate = run(
         second_edges_kernel,
         [square_group, square_group, triangle, triangle],
         [],
-        20, 12, drop, corner_mate, corner_cross, correction, low, high,
+        20, 12, drop, corner_cross, corner_mate, correction, low, high,
     )
     inverse_cross, inverse_mate = to_cross(inverse_cross), to_mate(inverse_mate)
     whole, rim_cross, rim_mate = run(
@@ -499,6 +559,7 @@
         [columns, triangle, triangle],
         [group_scratch] * 4,
         38, 20, drop, own, edge_cross, edge_mate, correction, new_low, new_high, square,
+        square_corners,
     )
     rim_cross, rim_mate = to_cross(rim_cross), to_mate(rim_mate)
     (density_own,) = run(density_own_kernel, [square_group], [], 18, 12, drop, square, whole)

time: 85.8 us -> 85.7 us (level)
  waiting for transfers between devices: 32.7 us -> 30.8 us
  Pallas kernels: 23.2 us -> 24.2 us
    ppermute x18, waiting for transfers between devices: 32.7 us -> 30.8 us  [routed(): lax.ppermute(x, RING, [(i, (i + step(i)) % size) for i in range(size) if...]
    pallas_call x11 -> x12, Pallas kernels: 23.2 us -> 24.2 us  [call(): pl.pallas_call(kernel, out_shape=[*outs, *[jax.ShapeDtypeStruct(a.shape,...]
  transfers between devices with their start and end apart: 18 -> 18, of which waited for: 7 -> 3; matrix products, arithmetic and copies ran while one was open for 1% -> 1% of each run, Pallas kernels for 24% -> 25%
where the time goes in v11:
time: 85.7 us; the launch traced here: 85.5 us
  waiting for transfers between devices  30.8 us (36%)
  starting transfers between devices  26.6 us (31%)
  Pallas kernels  24.2 us (28%)
  local copies, waits for them, and re-layouts  2.04 us (2%)
  other arithmetic  1.04 us (1%)
    ppermute x18, waiting for transfers between devices, routed(): lax.ppermute(x, RING, [(i, (i + step(i)) % size) for i in range(size) if...  30.8 us
    ppermute x18, starting transfers between devices, routed(): lax.ppermute(x, RING, [(i, (i + step(i)) % size) for i in range(size) if...  26.6 us
    pallas_call x12, Pallas kernels, call(): pl.pallas_call(kernel, out_shape=[*outs, *[jax.ShapeDtypeStruct(a.shape,...  24.2 us
    unnamed x8, local copies, waits for them, and re-layouts  2.04 us
  transfers between devices with their start and end apart: 18, of which 3 were waited for; matrix products, arithmetic and copies ran while one was open for 1% of the time, Pallas kernels for 25%

profile of v11, /device:TPU:1, one launch (start us, length us, event | category | flops | bytes accessed | tf_op | source)
XLA Modules:
  0.0 85.5 jit_solution(18279609213841075938)
XLA Ops:
  0.6 2.7 %collective-permute-start.2 = (bf16[4,8,128,128]{3,2,1,0:T(8,128)(2,1)}, bf16[4,8,128,128]{3,2,1,0:T(8,128)(2,1)S(1)}, u32[]{:S(2)}, u32[]{:S(2)}) collective-permute-start(bf16[4,8,128,128]{3,2,1,0:T(8,128)(2,1)} %own.2), channel_id=1, source_target_pairs={{0,15},{1,2},{2,1},{3,4},{4,3},{5,6},{6,5},{7,8},{8,7},{9,10},{10,... | collective-permute-start | bytes 3145736 | tf_op jit(solution)/shard_map/ppermute | solution.py:453
  3.3 2.9 %collective-permute-start.3 = (bf16[4,8,128,128]{3,2,1,0:T(8,128)(2,1)}, bf16[4,8,128,128]{3,2,1,0:T(8,128)(2,1)S(1)}, u32[]{:S(2)}, u32[]{:S(2)}) collective-permute-start(bf16[4,8,128,128]{3,2,1,0:T(8,128)(2,1)} %own.2), channel_id=1, source_target_pairs={{0,1},{1,0},{2,3},{3,2},{4,5},{5,4},{6,7},{7,6},{8,9},{9,8},{10,11... | collective-permute-start | bytes 3145736 | tf_op jit(solution)/shard_map/ppermute | solution.py:453
  7.1 1.2 %copy-done = bf16[4,8,128,128]{3,2,1,0:T(8,128)(2,1)S(1)} copy-done((bf16[4,8,128,128]{3,2,1,0:T(8,128)(2,1)S(1)}, bf16[4,8,128,128]{3,2,1,0:T(8,128)(2,1)}, u32[]{:S(2)}) %copy-start) | copy-done | bytes 1048600
  8.4 2.1 %shard_map.51 = (bf16[2048,128]{1,0:T(8,128)(2,1)S(1)}, bf16[2048,128]{1,0:T(8,128)(2,1)}, bf16[3328,128]{1,0:T(8,128)(2,1)}, bf16[1280,128]{1,0:T(8,128)(2,1)S(1)}) custom-call(s32[5]{0:T(128)S(1)} %pad_add_fusion.1.drop_ref, bf16[4,8,128,128]{3,2,1,0:T(8,128)(2,1)S(1)} %copy-done), custom_call_target="tpu_custom_call" | custom-call | bytes 3276800 | tf_op jit(solution)/shard_map/pallas_call | solution.py:439
  12.0 15.3 %collective-permute-done = s32[4]{0:T(128)S(1)} collective-permute-done((s32[4]{0:T(128)S(1)}, s32[4]{0:T(128)S(1)}, u32[]{:S(2)}, u32[]{:S(2)}) %collective-permute-start) | collective-permute-done | bytes 48 | tf_op jit(solution)/shard_map/ppermute | solution.py:453
  28.2 1.8 %collective-permute-start.8 = (bf16[1280,128]{1,0:T(8,128)(2,1)S(1)}, bf16[1280,128]{1,0:T(8,128)(2,1)S(1)}, u32[]{:S(2)}, u32[]{:S(2)}) collective-permute-start(bf16[1280,128]{1,0:T(8,128)(2,1)S(1)} %get-tuple-element.45.sent_cross), channel_id=1, source_target_pairs={{0,15},{1,2},{2,1},{3,4},{4,3},{5,6},{6,5},{7,8},{8,7},{9,10},{10,... | collective-permute-start | bytes 983048 | tf_op jit(solution)/shard_map/ppermute | solution.py:453
  30.1 6.3 %collective-permute-start.6 = (bf16[640,128]{1,0:T(8,128)(2,1)S(1)}, bf16[640,128]{1,0:T(8,128)(2,1)S(1)}, u32[]{:S(2)}, u32[]{:S(2)}) collective-permute-start(bf16[640,128]{1,0:T(8,128)(2,1)S(1)} %get-tuple-element.38), channel_id=1, source_target_pairs={{0,1},{1,0},{2,3},{3,2},{4,5},{5,4},{6,7},{7,6},{8,9},{9,8},{10,11... | collective-permute-start | bytes 491528 | tf_op jit(solution)/shard_map/ppermute | solution.py:453
  36.4 4.3 %shard_map.50 = (bf16[1536,1280]{1,0:T(8,128)(2,1)S(1)}, bf16[1536,1280]{1,0:T(8,128)(2,1)S(1)}, bf16[1024,512]{1,0:T(8,128)(2,1)S(1)}, bf16[1024,512]{1,0:T(8,128)(2,1)S(1)}, f32[1024,512]{1,0:T(8,128)S(1)}) custom-call(s32[13]{0:T(128)S(1)} %pad_add_fusion.drop_ref, bf16[4,8,128,128]{3,2,1,0:T(8,128)(2,1)S(1)} %copy-done.3, ...), custom_call_target="tpu_custom_call" | custom-call | flops 2818572288 | bytes 15204352 | tf_op jit(solution)/shard_map/pallas_call | solution.py:439
  40.7 1.4 %shard_map.53 = (bf16[1024,512]{1,0:T(8,128)(2,1)S(1)}, bf16[1024,512]{1,0:T(8,128)(2,1)S(1)}) custom-call(s32[13]{0:T(128)S(1)} %pad_add_fusion.drop_ref, bf16[1280,128]{1,0:T(8,128)(2,1)S(1)} %collective-permute-done.5.far_far, bf16[640,128]{1,0:T(8,128)(2,1)S(1)} %collective-permute-done.6.far_mate, ...), custom_call_target="tpu_custom_call" | custom-call | tf_op jit(solution)/shard_map/pallas_call | solution.py:439
  42.1 3.8 %shard_map.54 = (bf16[1536,512]{1,0:T(8,128)(2,1)S(1)}, bf16[512,512]{1,0:T(8,128)(2,1)S(1)}, f32[1024,512]{1,0:T(8,128)S(1)}) custom-call(s32[13]{0:T(128)S(1)} %pad_add_fusion.drop_ref, bf16[1536,1280]{1,0:T(8,128)(2,1)S(1)} %get-tuple-element.33.shifted, bf16[1024,512]{1,0:T(8,128)(2,1)S(1)} %get-tuple-element.43.corners, ...), custom_call_target="tpu_custom_call" | custom-call | tf_op jit(solution)/shard_map/pallas_call | solution.py:439
  46.8 2.2 %collective-permute-start.13 = (bf16[512,512]{1,0:T(8,128)(2,1)S(1)}, bf16[512,512]{1,0:T(8,128)(2,1)S(1)}, u32[]{:S(2)}, u32[]{:S(2)}) collective-permute-start(bf16[512,512]{1,0:T(8,128)(2,1)S(1)} %get-tuple-element.46.own), channel_id=1, source_target_pairs={{0,1},{1,0},{2,3},{3,2},{4,5},{5,4},{6,7},{7,6},{8,9},{9,8},{10,11... | collective-permute-start | bytes 1572872 | tf_op jit(solution)/shard_map/ppermute | solution.py:453
  49.0 1.3 %shard_map.55 = (bf16[512,512]{1,0:T(8,128)(2,1)S(1)}, bf16[512,512]{1,0:T(8,128)(2,1)S(1)}, bf16[1280,128]{1,0:T(8,128)(2,1)S(1)}, bf16[1280,128]{1,0:T(8,128)(2,1)S(1)}) custom-call(s32[13]{0:T(128)S(1)} %pad_add_fusion.drop_ref, bf16[3328,128]{1,0:T(8,128)(2,1)S(1)} %collective-permute-done.4.refs_1_.mate, ...), custom_call_target="tpu_custom_call" | custom-call | flops 335544320 | bytes 6750208 | tf_op jit(solution)/shard_map/pallas_call | solution.py:439
  50.4 2.3 %collective-permute-start.10 = (bf16[1280,128]{1,0:T(8,128)(2,1)S(1)}, bf16[1280,128]{1,0:T(8,128)(2,1)S(1)}, u32[]{:S(2)}, u32[]{:S(2)}) collective-permute-start(bf16[1280,128]{1,0:T(8,128)(2,1)S(1)} %get-tuple-element.50), channel_id=1, source_target_pairs={{0,15},{1,2},{2,1},{3,4},{4,3},{5,6},{6,5},{7,8},{8,7},{9,10},{10,... | collective-permute-start | bytes 983048 | tf_op jit(solution)/shard_map/ppermute | solution.py:453
  52.7 2.1 %collective-permute-start.11 = (bf16[1280,128]{1,0:T(8,128)(2,1)S(1)}, bf16[1280,128]{1,0:T(8,128)(2,1)S(1)}, u32[]{:S(2)}, u32[]{:S(2)}) collective-permute-start(bf16[1280,128]{1,0:T(8,128)(2,1)S(1)} %get-tuple-element.51), channel_id=1, source_target_pairs={{0,1},{1,0},{2,3},{3,2},{4,5},{5,4},{6,7},{7,6},{8,9},{9,8},{10,11... | collective-permute-start | bytes 983048 | tf_op jit(solution)/shard_map/ppermute | solution.py:453
  54.8 2.0 %shard_map.56.correction = bf16[1536,512]{1,0:T(8,128)(2,1)S(1)} custom-call(s32[13]{0:T(128)S(1)} %pad_add_fusion.drop_ref, bf16[1536,1280]{1,0:T(8,128)(2,1)S(1)} %get-tuple-element.33.shifted, bf16[1024,512]{1,0:T(8,128)(2,1)S(1)} %get-tuple-element.43.corners, bf16[512,512]{1,0:T(8,128)(2,1)S(1)} %get-tuple-element.52.low, ...), custom_call_target="tpu_custom_call" | custom-call | flops 1275068416 | bytes 8126464 | tf_op jit(solution)/shard_map/pallas_call | solution.py:439
  56.8 10.2 %collective-permute-done.12.cross = bf16[512,512]{1,0:T(8,128)(2,1)S(1)} collective-permute-done((bf16[512,512]{1,0:T(8,128)(2,1)S(1)}, bf16[512,512]{1,0:T(8,128)(2,1)S(1)}, u32[]{:S(2)}, u32[]{:S(2)}) %collective-permute-start.12) | collective-permute-done | bytes 524320 | tf_op jit(solution)/shard_map/ppermute | solution.py:453
  67.0 1.5 %shard_map.57 = (bf16[512,512]{1,0:T(8,128)(2,1)S(1)}, bf16[512,512]{1,0:T(8,128)(2,1)S(1)}, bf16[1280,128]{1,0:T(8,128)(2,1)S(1)}, bf16[1280,128]{1,0:T(8,128)(2,1)S(1)}) custom-call(s32[13]{0:T(128)S(1)} %pad_add_fusion.drop_ref, bf16[512,512]{1,0:T(8,128)(2,1)S(1)} %collective-permute-done.12.cross, bf16[512,512]{1,0:T(8,128)(2,1)S(1)} %collective-permute-done.13.mate, ...), custom_call_target="tpu_custom_call" | custom-call | flops 671088640 | bytes 5373952 | tf_op jit(solution)/shard_map/pallas_call | solution.py:439
  68.5 2.5 %collective-permute-start.16 = (bf16[1280,128]{1,0:T(8,128)(2,1)S(1)}, bf16[1280,128]{1,0:T(8,128)(2,1)S(1)}, u32[]{:S(2)}, u32[]{:S(2)}) collective-permute-start(bf16[1280,128]{1,0:T(8,128)(2,1)S(1)} %get-tuple-element.60), channel_id=1, source_target_pairs={{0,15},{1,2},{2,1},{3,4},{4,3},{5,6},{6,5},{7,8},{8,7},{9,10},{10,... | collective-permute-start | bytes 983048 | tf_op jit(solution)/shard_map/ppermute | solution.py:453
  71.1 2.3 %shard_map.58 = (bf16[1536,512]{1,0:T(8,128)(2,1)S(1)}, bf16[1280,128]{1,0:T(8,128)(2,1)S(1)}, bf16[1280,128]{1,0:T(8,128)(2,1)S(1)}) custom-call(s32[13]{0:T(128)S(1)} %pad_add_fusion.drop_ref, bf16[512,512]{1,0:T(8,128)(2,1)S(1)} %get-tuple-element.46.own, bf16[1280,128]{1,0:T(8,128)(2,1)S(1)} %collective-permute-done.10.cross, ...), custom_call_target="tpu_custom_call" | custom-call | flops 1275068416 | bytes 11010048 | tf_op jit(solution)/shard_map/pallas_call | solution.py:439
  73.4 2.0 %collective-permute-start.14 = (bf16[1280,128]{1,0:T(8,128)(2,1)S(1)}, bf16[1280,128]{1,0:T(8,128)(2,1)S(1)}, u32[]{:S(2)}, u32[]{:S(2)}) collective-permute-start(bf16[1280,128]{1,0:T(8,128)(2,1)S(1)} %get-tuple-element.58), channel_id=1, source_target_pairs={{0,15},{1,2},{2,1},{3,4},{4,3},{5,6},{6,5},{7,8},{8,7},{9,10},{10,... | collective-permute-start | bytes 983048 | tf_op jit(solution)/shard_map/ppermute | solution.py:453
  75.4 1.3 %shard_map.59.own = bf16[512,512]{1,0:T(8,128)(2,1)S(1)} custom-call(s32[13]{0:T(128)S(1)} %pad_add_fusion.drop_ref, bf16[1536,1280]{1,0:T(8,128)(2,1)S(1)} %get-tuple-element.32.square, bf16[1536,512]{1,0:T(8,128)(2,1)S(1)} %get-tuple-element.57.whole.own), custom_call_target="tpu_custom_call" | custom-call | flops 603979776 | bytes 6029312 | tf_op jit(solution)/shard_map/pallas_call | solution.py:439
  76.7 1.8 %shard_map.61 = bf16[4,8,128,128]{3,2,1,0:T(8,128)(2,1)} custom-call(s32[13]{0:T(128)S(1)} %pad_add_fusion.drop_ref, bf16[1536,512]{1,0:T(8,128)(2,1)S(1)} %get-tuple-element.57.whole.own, bf16[1280,128]{1,0:T(8,128)(2,1)S(1)} %collective-permute-done.16.cross, bf16[1280,128]{1,0:T(8,128)(2,1)S(1)} %collective-permute-done.17.mate), custom_call_target="tpu_custom_call" | custom-call | bytes 3276800 | tf_op jit(solution)/shard_map/pallas_call | solution.py:439
  78.5 5.2 %collective-permute-done.14.cross = bf16[1280,128]{1,0:T(8,128)(2,1)S(1)} collective-permute-done((bf16[1280,128]{1,0:T(8,128)(2,1)S(1)}, bf16[1280,128]{1,0:T(8,128)(2,1)S(1)}, u32[]{:S(2)}, u32[]{:S(2)}) %collective-permute-start.14) | collective-permute-done | bytes 327712 | tf_op jit(solution)/shard_map/ppermute | solution.py:453
  83.7 1.8 %shard_map.60 = bf16[4,8,128,128]{3,2,1,0:T(8,128)(2,1)} custom-call(s32[13]{0:T(128)S(1)} %pad_add_fusion.drop_ref, bf16[512,512]{1,0:T(8,128)(2,1)S(1)} %shard_map.59.own, bf16[1280,128]{1,0:T(8,128)(2,1)S(1)} %collective-permute-done.14.cross, bf16[1280,128]{1,0:T(8,128)(2,1)S(1)} %collective-permute-done.15.mate), custom_call_target="tpu_custom_call" | custom-call | bytes 2228224 | tf_op jit(solution)/shard_map/pallas_call | solution.py:439
  (38 shorter events, 4.4 us)
Async XLA Ops:
  0.6 26.8 %collective-permute-start.2 = (bf16[4,8,128,128]{3,2,1,0:T(8,128)(2,1)}, bf16[4,8,128,128]{3,2,1,0:T(8,128)(2,1)S(1)}, u32[]{:S(2)}, u32[]{:S(2)}) collective-permute-start(bf16[4,8,128,128]{3,2,1,0:T(8,128)(2,1)} %own.2), channel_id=1, source_target_pairs={{0,15},{1,2},{2,1},{3,4},{4,3},{5,6},{6,5},{7,8},{8,7},{9,10},{10,... | collective-permute-start | bytes 3145736 | tf_op jit(solution)/shard_map/ppermute | solution.py:453
  3.3 24.1 %collective-permute-start.3 = (bf16[4,8,128,128]{3,2,1,0:T(8,128)(2,1)}, bf16[4,8,128,128]{3,2,1,0:T(8,128)(2,1)S(1)}, u32[]{:S(2)}, u32[]{:S(2)}) collective-permute-start(bf16[4,8,128,128]{3,2,1,0:T(8,128)(2,1)} %own.2), channel_id=1, source_target_pairs={{0,1},{1,0},{2,3},{3,2},{4,5},{5,4},{6,7},{7,6},{8,9},{9,8},{10,11... | collective-permute-start | bytes 3145736 | tf_op jit(solution)/shard_map/ppermute | solution.py:453
  7.1 1.2 %copy-start = (bf16[4,8,128,128]{3,2,1,0:T(8,128)(2,1)S(1)}, bf16[4,8,128,128]{3,2,1,0:T(8,128)(2,1)}, u32[]{:S(2)}) copy-start(bf16[4,8,128,128]{3,2,1,0:T(8,128)(2,1)} %own.3) | copy-start | bytes 3145732
  10.4 0.8 copy-start.1
  11.2 16.2 %collective-permute-start.4 = (bf16[3328,128]{1,0:T(8,128)(2,1)}, bf16[3328,128]{1,0:T(8,128)(2,1)S(1)}, u32[]{:S(2)}, u32[]{:S(2)}) collective-permute-start(bf16[3328,128]{1,0:T(8,128)(2,1)} %get-tuple-element.34.sent_mate), channel_id=1, source_target_pairs={{0,1},{1,0},{2,3},{3,2},{4,5},{5,4},{6,7},{7,6},{8,9},{9,8},{10,11... | collective-permute-start | bytes 2555912 | tf_op jit(solution)/shard_map/ppermute | solution.py:453
  11.2 16.1 %collective-permute-start = (s32[4]{0:T(128)S(1)}, s32[4]{0:T(128)S(1)}, u32[]{:S(2)}, u32[]{:S(2)}) collective-permute-start(s32[4]{0:T(128)S(1)} %broadcast_subtract_fusion), channel_id=1, source_target_pairs={{0,15},{1,2},{2,1},{3,4},{4,3},{5,6},{6,5},{7,8},{8,7},{9,10},{10,... | collective-permute-start | bytes 56 | tf_op jit(solution)/shard_map/ppermute | solution.py:453
  11.2 16.1 %collective-permute-start.1 = (s32[4]{0:T(128)S(1)}, s32[4]{0:T(128)S(1)}, u32[]{:S(2)}, u32[]{:S(2)}) collective-permute-start(s32[4]{0:T(128)S(1)} %broadcast_subtract_fusion), channel_id=1, source_target_pairs={{0,1},{1,0},{2,3},{3,2},{4,5},{5,4},{6,7},{7,6},{8,9},{9,8},{10,11... | collective-permute-start | bytes 56 | tf_op jit(solution)/shard_map/ppermute | solution.py:453
  12.0 24.4 %copy-start.3 = (bf16[4,8,128,128]{3,2,1,0:T(8,128)(2,1)S(1)}, bf16[4,8,128,128]{3,2,1,0:T(8,128)(2,1)}, u32[]{:S(2)}) copy-start(bf16[4,8,128,128]{3,2,1,0:T(8,128)(2,1)} %own.2) | copy-start | bytes 3145732
  28.1 12.5 %collective-permute-start.5 = (bf16[1280,128]{1,0:T(8,128)(2,1)S(1)}, bf16[1280,128]{1,0:T(8,128)(2,1)S(1)}, u32[]{:S(2)}, u32[]{:S(2)}) collective-permute-start(bf16[1280,128]{1,0:T(8,128)(2,1)S(1)} %get-tuple-element.37), channel_id=1, source_target_pairs={{0,13},{1,4},{2,15},{3,6},{4,1},{5,8},{6,3},{7,10},{8,5},{9,12},{1... | collective-permute-start | bytes 983048 | tf_op jit(solution)/shard_map/ppermute | solution.py:453
  28.2 13.9 %collective-permute-start.8 = (bf16[1280,128]{1,0:T(8,128)(2,1)S(1)}, bf16[1280,128]{1,0:T(8,128)(2,1)S(1)}, u32[]{:S(2)}, u32[]{:S(2)}) collective-permute-start(bf16[1280,128]{1,0:T(8,128)(2,1)S(1)} %get-tuple-element.45.sent_cross), channel_id=1, source_target_pairs={{0,15},{1,2},{2,1},{3,4},{4,3},{5,6},{6,5},{7,8},{8,7},{9,10},{10,... | collective-permute-start | bytes 983048 | tf_op jit(solution)/shard_map/ppermute | solution.py:453
  30.0 19.0 %collective-permute-start.9 = (bf16[2048,128]{1,0:T(8,128)(2,1)}, bf16[2048,128]{1,0:T(8,128)(2,1)S(1)}, u32[]{:S(2)}, u32[]{:S(2)}) collective-permute-start(bf16[2048,128]{1,0:T(8,128)(2,1)} %get-tuple-element.47), channel_id=1, source_target_pairs={{0,15},{1,2},{2,1},{3,4},{4,3},{5,6},{6,5},{7,8},{8,7},{9,10},{10,... | collective-permute-start | bytes 1572872 | tf_op jit(solution)/shard_map/ppermute | solution.py:453
  30.1 10.5 %collective-permute-start.6 = (bf16[640,128]{1,0:T(8,128)(2,1)S(1)}, bf16[640,128]{1,0:T(8,128)(2,1)S(1)}, u32[]{:S(2)}, u32[]{:S(2)}) collective-permute-start(bf16[640,128]{1,0:T(8,128)(2,1)S(1)} %get-tuple-element.38), channel_id=1, source_target_pairs={{0,1},{1,0},{2,3},{3,2},{4,5},{5,4},{6,7},{7,6},{8,9},{9,8},{10,11... | collective-permute-start | bytes 491528 | tf_op jit(solution)/shard_map/ppermute | solution.py:453
  36.4 4.3 %collective-permute-start.7 = (bf16[640,128]{1,0:T(8,128)(2,1)S(1)}, bf16[640,128]{1,0:T(8,128)(2,1)S(1)}, u32[]{:S(2)}, u32[]{:S(2)}) collective-permute-start(bf16[640,128]{1,0:T(8,128)(2,1)S(1)} %get-tuple-element.39), channel_id=1, source_target_pairs={{0,1},{1,0},{2,3},{3,2},{4,5},{5,4},{6,7},{7,6},{8,9},{9,8},{10,11... | collective-permute-start | bytes 491528 | tf_op jit(solution)/shard_map/ppermute | solution.py:453
  40.7 1.5 %copy-start.2 = (bf16[2048,128]{1,0:T(8,128)(2,1)S(1)}, bf16[2048,128]{1,0:T(8,128)(2,1)}, u32[]{:S(2)}) copy-start(bf16[2048,128]{1,0:T(8,128)(2,1)} %copy-done.1) | copy-start | bytes 1572868
  45.9 21.1 %collective-permute-start.12 = (bf16[512,512]{1,0:T(8,128)(2,1)S(1)}, bf16[512,512]{1,0:T(8,128)(2,1)S(1)}, u32[]{:S(2)}, u32[]{:S(2)}) collective-permute-start(bf16[512,512]{1,0:T(8,128)(2,1)S(1)} %get-tuple-element.46.own), channel_id=1, source_target_pairs={{0,15},{1,2},{2,1},{3,4},{4,3},{5,6},{6,5},{7,8},{8,7},{9,10},{10,... | collective-permute-start | bytes 1572872 | tf_op jit(solution)/shard_map/ppermute | solution.py:453
  46.8 20.2 %collective-permute-start.13 = (bf16[512,512]{1,0:T(8,128)(2,1)S(1)}, bf16[512,512]{1,0:T(8,128)(2,1)S(1)}, u32[]{:S(2)}, u32[]{:S(2)}) collective-permute-start(bf16[512,512]{1,0:T(8,128)(2,1)S(1)} %get-tuple-element.46.own), channel_id=1, source_target_pairs={{0,1},{1,0},{2,3},{3,2},{4,5},{5,4},{6,7},{7,6},{8,9},{9,8},{10,11... | collective-permute-start | bytes 1572872 | tf_op jit(solution)/shard_map/ppermute | solution.py:453
  50.4 20.7 %collective-permute-start.10 = (bf16[1280,128]{1,0:T(8,128)(2,1)S(1)}, bf16[1280,128]{1,0:T(8,128)(2,1)S(1)}, u32[]{:S(2)}, u32[]{:S(2)}) collective-permute-start(bf16[1280,128]{1,0:T(8,128)(2,1)S(1)} %get-tuple-element.50), channel_id=1, source_target_pairs={{0,15},{1,2},{2,1},{3,4},{4,3},{5,6},{6,5},{7,8},{8,7},{9,10},{10,... | collective-permute-start | bytes 983048 | tf_op jit(solution)/shard_map/ppermute | solution.py:453
  52.7 18.4 %collective-permute-start.11 = (bf16[1280,128]{1,0:T(8,128)(2,1)S(1)}, bf16[1280,128]{1,0:T(8,128)(2,1)S(1)}, u32[]{:S(2)}, u32[]{:S(2)}) collective-permute-start(bf16[1280,128]{1,0:T(8,128)(2,1)S(1)} %get-tuple-element.51), channel_id=1, source_target_pairs={{0,1},{1,0},{2,3},{3,2},{4,5},{5,4},{6,7},{7,6},{8,9},{9,8},{10,11... | collective-permute-start | bytes 983048 | tf_op jit(solution)/shard_map/ppermute | solution.py:453
  68.5 8.1 %collective-permute-start.16 = (bf16[1280,128]{1,0:T(8,128)(2,1)S(1)}, bf16[1280,128]{1,0:T(8,128)(2,1)S(1)}, u32[]{:S(2)}, u32[]{:S(2)}) collective-permute-start(bf16[1280,128]{1,0:T(8,128)(2,1)S(1)} %get-tuple-element.60), channel_id=1, source_target_pairs={{0,15},{1,2},{2,1},{3,4},{4,3},{5,6},{6,5},{7,8},{8,7},{9,10},{10,... | collective-permute-start | bytes 983048 | tf_op jit(solution)/shard_map/ppermute | solution.py:453
  71.1 5.6 %collective-permute-start.17 = (bf16[1280,128]{1,0:T(8,128)(2,1)S(1)}, bf16[1280,128]{1,0:T(8,128)(2,1)S(1)}, u32[]{:S(2)}, u32[]{:S(2)}) collective-permute-start(bf16[1280,128]{1,0:T(8,128)(2,1)S(1)} %get-tuple-element.61), channel_id=1, source_target_pairs={{0,1},{1,0},{2,3},{3,2},{4,5},{5,4},{6,7},{7,6},{8,9},{9,8},{10,11... | collective-permute-start | bytes 983048 | tf_op jit(solution)/shard_map/ppermute | solution.py:453
  73.4 10.3 %collective-permute-start.14 = (bf16[1280,128]{1,0:T(8,128)(2,1)S(1)}, bf16[1280,128]{1,0:T(8,128)(2,1)S(1)}, u32[]{:S(2)}, u32[]{:S(2)}) collective-permute-start(bf16[1280,128]{1,0:T(8,128)(2,1)S(1)} %get-tuple-element.58), channel_id=1, source_target_pairs={{0,15},{1,2},{2,1},{3,4},{4,3},{5,6},{6,5},{7,8},{8,7},{9,10},{10,... | collective-permute-start | bytes 983048 | tf_op jit(solution)/shard_map/ppermute | solution.py:453
  75.3 8.4 %collective-permute-start.15 = (bf16[1280,128]{1,0:T(8,128)(2,1)S(1)}, bf16[1280,128]{1,0:T(8,128)(2,1)S(1)}, u32[]{:S(2)}, u32[]{:S(2)}) collective-permute-start(bf16[1280,128]{1,0:T(8,128)(2,1)S(1)} %get-tuple-element.59), channel_id=1, source_target_pairs={{0,1},{1,0},{2,3},{3,2},{4,5},{5,4},{6,7},{7,6},{8,9},{9,8},{10,11... | collective-permute-start | bytes 983048 | tf_op jit(solution)/shard_map/ppermute | solution.py:453

commit v12 on v11

--- a/solution.py
+++ b/solution.py
@@ -144,7 +144,7 @@
         to_mate[block(f, i, 0)] = jnp.where(odd, back, forth)
 
 
-def slabs_kernel(f, drop_ref, own, corner, corner_again, to_mate, to_cross):
+def slabs_kernel(f, drop_ref, own, corner, corner_again, to_mate, to_cross, to_cross_again):
     h = f.h
     odd = drop_ref[h] == 1
     n = len(under(h))
@@ -153,7 +153,9 @@
         forth = stored(own, r, 2 * h + c - r, drop_ref[r])
         back = stored(own, s, d - s, drop_ref[s])
         to_mate[block(f, i, 0)] = jnp.where(odd, back, forth)
-        to_cross[block(f, i, 0)] = jnp.where(odd, forth, back)
+        across = jnp.where(odd, forth, back)
+        to_cross[block(f, i, 0)] = across
+        to_cross_again[block(f, i, 0)] = across
     for i, (r, c) in enumerate(full(h)):
         value = stored(own, r, c - r + h, drop_ref[r])
         corner[block(f, i, 0)] = value
@@ -221,7 +223,7 @@
 
 
 def corners_kernel(
-    f, drop_ref, far_far, far_mate, far_mate_too, reach, here, partial, square, shifted, low, high
+    f, drop_ref, far_far, far_mate, far_mate_too, reach, here, partial, unused, square, shifted, low, high
 ):
     p = f.p
     far_mates = [indexed(f, far_mate), indexed(f, far_mate_too)]
@@ -263,11 +265,17 @@
 
 
 def first_sweep_kernel(
-    f, drop_ref, shifted, corners, corner, sent_mate, sent_cross, mate, cross,
+    f, drop_ref, shifted, corners, corner, sent_mate, sent_cross, mate, direct, turned,
     correction, fresh, partial, whole, before, after,
 ):
     h, p = f.h, f.p
-    from_below, from_above = sides(f, drop_ref, indexed(f, mate), indexed(f, cross))
+    turning = drop_ref[3 * h + 1] == 1
+    direct_block, turned_block = indexed(f, direct), indexed(f, turned)
+
+    def cross(i):
+        return jnp.where(turning, turned_block(i), direct_block(i))
+
+    from_below, from_above = sides(f, drop_ref, indexed(f, mate), cross)
     down, up = sides(f, drop_ref, indexed(f, sent_mate), indexed(f, sent_cross))
     spread(f, whole, 0, 0, from_below, under(h))
     spread(f, whole, h, 0, indexed(f, corner), full(h))
@@ -347,7 +355,7 @@
 
 
 def second_edges_kernel(
-    f, drop_ref, cross, mate, correction, low, high, new_low, new_high, to_cross, to_mate
+    f, drop_ref, mate, cross, correction, low, high, new_low, new_high, to_cross, to_mate
 ):
     p = f.p
 
@@ -456,9 +464,9 @@
 def on_device(density, inverse_start, block_cols):
     rows, width, order, _ = density.shape
     half = width // 2
-    ring = lax.axis_size(RING)
+    ring, inner = lax.axis_size(RING), lax.axis_size(RING[1])
     total = rows * ring
-    assert rows == half and half % 2 == 0 and ring % 2 == 0
+    assert rows == half and half % 2 == 0 and inner % 2 == 0
     f = Frame(half, order)
     kind = density.dtype
     me = lax.axis_index(RING)
@@ -475,6 +483,9 @@
     def to_cross(x):
         return routed(x, cross_step)
 
+    def turns(i):
+        return i % inner in (0, inner - 1)
+
     positions = block_cols - (me * rows + jnp.arange(rows, dtype=jnp.int32))[:, None] + half
     positions = positions + jnp.where(positions < 0, total, jnp.where(positions >= total, -total, 0))
     own_drop = width * (width + 1) // 2 - jnp.sum(positions, axis=1)
@@ -482,10 +493,11 @@
     density_cross, density_mate = to_cross(density), to_mate(density)
     cross_drop, mate_drop = to_cross(own_drop), to_mate(own_drop)
     even = (me & 1) == 0
-    mark = jnp.reshape(me & 1, (1,))
-    start_drop = jnp.concatenate([own_drop, mark])
+    place = lax.axis_index(RING[1])
+    marks = jnp.stack([me & 1, ((place == 0) | (place == inner - 1)).astype(jnp.int32)])
+    start_drop = jnp.concatenate([own_drop, marks[:1]])
     drop = jnp.concatenate(
-        [jnp.where(even, cross_drop, mate_drop), own_drop, jnp.where(even, mate_drop, cross_drop), mark]
+        [jnp.where(even, cross_drop, mate_drop), own_drop, jnp.where(even, mate_drop, cross_drop), marks]
     )
 
     unit = 2 * f.t**3
@@ -504,17 +516,18 @@
     def run(kernel, outs, scratch, tiles, limit, *args, **kw):
         return call(functools.partial(kernel, f), outs, scratch, tiles * unit, limit, *args, **kw)
 
-    corner, corner_cross, slab_mate, triangle_cross = run(
-        slabs_kernel, [listed, listed, both, triangle], [], 0, 12, start_drop, inverse_start
+    corner, corner_cross, slab_mate, triangle_cross, triangle_turning = run(
+        slabs_kernel, [listed, listed, both, triangle, triangle], [], 0, 12, start_drop, inverse_start
     )
     from_mate = to_mate(slab_mate)
-    forward_mate, forward_mate_too, forward_far, triangle_cross, corner_cross = run(
+    direct_triangle = routed(triangle_cross, lambda i: 0 if turns(i) else cross_step(i))
+    forward_mate, forward_mate_too, forward_far, triangle_turning, corner_cross = run(
         forward_kernel, [half_triangle, half_triangle, triangle], [], 0, 12, drop, density_cross, density_mate, from_mate,
-        passed=(triangle_cross, corner_cross),
+        passed=(triangle_turning, corner_cross),
     )
     far_mate, far_mate_too = to_mate(forward_mate), to_mate(forward_mate_too)
     far_far = routed(forward_far, lambda i: 3 * cross_step(i))
-    cross_triangle = to_cross(triangle_cross)
+    turned_triangle = routed(triangle_turning, lambda i: cross_step(i) if turns(i) else 0)
     cross_corner = to_cross(corner_cross)
 
     both_corners = jax.ShapeDtypeStruct((2 * f.group, f.group), kind)
@@ -522,19 +535,21 @@
         square_kernel,
         [band, band, both_corners, both_corners, partial_sums],
         [pltpu.VMEM((3 * f.group, 5 * f.group), kind)],
-        84, 26, drop, density, density_cross, density_mate,
+        84, 26, drop, density, density_cross, density_mate, light=True,
     )
     square_corners, shifted_corners = run(
         corners_kernel,
         [both_corners, both_corners],
         [group_scratch] * 2,
-        10, 16, drop, far_far, far_mate, far_mate_too, reach, here, partial, light=True,
+        10, 16, drop, far_far, far_mate, far_mate_too, reach, here, partial,
+        direct_triangle, light=True,
     )
     correction, own, partial = run(
         first_sweep_kernel,
         [columns, square_group, partial_sums],
         [whole_scratch, group_scratch, group_scratch],
-        66, 24, drop, shifted, shifted_corners, corner, slab_mate, triangle_cross, from_mate, cross_triangle, light=True,
+        66, 24, drop, shifted, shifted_corners, corner, slab_mate, triangle_cross, from_mate,
+        direct_triangle, turned_triangle, light=True,
     )
     corner_cross, corner_mate = to_cross(own), to_mate(own)
     low, high, edge_cross, edge_mate = run(
@@ -551,7 +566,7 @@
         second_edges_kernel,
         [square_group, square_group, triangle, triangle],
         [],
-        20, 12, drop, corner_cross, corner_mate, correction, low, high,
+        20, 12, drop, corner_mate, corner_cross, correction, low, high,
     )
     inverse_cross, inverse_mate = to_cross(inverse_cross), to_mate(inverse_mate)
     whole, rim_cross, rim_mate = run(

time: 85.7 us -> 86.9 us (1.014)
    unnamed x8 -> x12, local copies, waits for them, and re-layouts: 2.04 us -> 2.78 us
    ppermute x18 -> x19, waiting for transfers between devices: 30.8 us -> 31.3 us  [routed(): lax.ppermute(x, RING, [(i, (i + step(i)) % size) for i in range(size) if...]
    ppermute x18 -> x19, starting transfers between devices: 26.6 us -> 26.6 us  [routed(): lax.ppermute(x, RING, [(i, (i + step(i)) % size) for i in range(size) if...]
  transfers between devices with their start and end apart: 18 -> 19, of which waited for: 3 -> 5; matrix products, arithmetic and copies ran while one was open for 1% -> 1% of each run, Pallas kernels for 25% -> 26%
where the time goes in v12:
time: 86.9 us; the launch traced here: 86.7 us
  waiting for transfers between devices  31.3 us (36%)
  starting transfers between devices  26.6 us (31%)
  Pallas kernels  24.1 us (28%)
  local copies, waits for them, and re-layouts  2.87 us (3%)
  other arithmetic  0.96 us (1%)
    ppermute x19, waiting for transfers between devices, routed(): lax.ppermute(x, RING, [(i, (i + step(i)) % size) for i in range(size) if...  31.3 us
    ppermute x19, starting transfers between devices, routed(): lax.ppermute(x, RING, [(i, (i + step(i)) % size) for i in range(size) if...  26.6 us
    pallas_call x12, Pallas kernels, call(): pl.pallas_call(kernel, out_shape=[*outs, *[jax.ShapeDtypeStruct(a.shape,...  24.1 us
    unnamed x12, local copies, waits for them, and re-layouts  2.78 us
  transfers between devices with their start and end apart: 19, of which 5 were waited for; matrix products, arithmetic and copies ran while one was open for 1% of the time, Pallas kernels for 26%

profile of v12, /device:TPU:1, one launch (start us, length us, event | category | flops | bytes accessed | tf_op | source)
XLA Modules:
  0.0 86.7 jit_solution(458462822217072196)
XLA Ops:
  0.6 2.7 %collective-permute-start.2 = (bf16[4,8,128,128]{3,2,1,0:T(8,128)(2,1)}, bf16[4,8,128,128]{3,2,1,0:T(8,128)(2,1)S(1)}, u32[]{:S(2)}, u32[]{:S(2)}) collective-permute-start(bf16[4,8,128,128]{3,2,1,0:T(8,128)(2,1)} %own.2), channel_id=1, source_target_pairs={{0,15},{1,2},{2,1},{3,4},{4,3},{5,6},{6,5},{7,8},{8,7},{9,10},{10,... | collective-permute-start | bytes 3145736 | tf_op jit(solution)/shard_map/ppermute | solution.py:461
  3.3 2.9 %collective-permute-start.3 = (bf16[4,8,128,128]{3,2,1,0:T(8,128)(2,1)}, bf16[4,8,128,128]{3,2,1,0:T(8,128)(2,1)S(1)}, u32[]{:S(2)}, u32[]{:S(2)}) collective-permute-start(bf16[4,8,128,128]{3,2,1,0:T(8,128)(2,1)} %own.2), channel_id=1, source_target_pairs={{0,1},{1,0},{2,3},{3,2},{4,5},{5,4},{6,7},{7,6},{8,9},{9,8},{10,11... | collective-permute-start | bytes 3145736 | tf_op jit(solution)/shard_map/ppermute | solution.py:461
  8.4 2.2 %shard_map.51 = (bf16[2048,128]{1,0:T(8,128)(2,1)S(1)}, bf16[2048,128]{1,0:T(8,128)(2,1)}, bf16[3328,128]{1,0:T(8,128)(2,1)}, bf16[1280,128]{1,0:T(8,128)(2,1)S(1)}, bf16[1280,128]{1,0:T(8,128)(2,1)}) custom-call(s32[5]{0:T(128)S(1)} %pad_add_fusion.drop_ref, bf16[4,8,128,128]{3,2,1,0:T(8,128)(2,1)S(1)} %copy-done), custom_call_target="tpu_custom_call" | custom-call | bytes 3604480 | tf_op jit(solution)/shard_map/pallas_call | solution.py:447
  12.6 1.5 %collective-permute-done.1 = s32[4]{0:T(128)S(1)} collective-permute-done((s32[4]{0:T(128)S(1)}, s32[4]{0:T(128)S(1)}, u32[]{:S(2)}, u32[]{:S(2)}) %collective-permute-start.1) | collective-permute-done | bytes 48 | tf_op jit(solution)/shard_map/ppermute | solution.py:461
  14.1 2.1 %collective-permute-start.8 = (bf16[1280,128]{1,0:T(8,128)(2,1)}, bf16[1280,128]{1,0:T(8,128)(2,1)S(1)}, u32[]{:S(2)}, u32[]{:S(2)}) collective-permute-start(bf16[1280,128]{1,0:T(8,128)(2,1)} %copy-done.4), channel_id=1, source_target_pairs={{1,2},{2,1},{5,6},{6,5},{9,10},{10,9},{13,14},{14,13},{17,18},{18,... | collective-permute-start | bytes 983048 | tf_op jit(solution)/shard_map/ppermute | solution.py:461
  16.3 11.0 %collective-permute-done = s32[4]{0:T(128)S(1)} collective-permute-done((s32[4]{0:T(128)S(1)}, s32[4]{0:T(128)S(1)}, u32[]{:S(2)}, u32[]{:S(2)}) %collective-permute-start) | collective-permute-done | bytes 48 | tf_op jit(solution)/shard_map/ppermute | solution.py:461
  28.9 1.8 %collective-permute-start.10 = (bf16[2048,128]{1,0:T(8,128)(2,1)}, bf16[2048,128]{1,0:T(8,128)(2,1)S(1)}, u32[]{:S(2)}, u32[]{:S(2)}) collective-permute-start(bf16[2048,128]{1,0:T(8,128)(2,1)} %get-tuple-element.49), channel_id=1, source_target_pairs={{0,15},{1,2},{2,1},{3,4},{4,3},{5,6},{6,5},{7,8},{8,7},{9,10},{10,... | collective-permute-start | bytes 1572872 | tf_op jit(solution)/shard_map/ppermute | solution.py:461
  30.7 7.6 %collective-permute-start.6 = (bf16[640,128]{1,0:T(8,128)(2,1)S(1)}, bf16[640,128]{1,0:T(8,128)(2,1)S(1)}, u32[]{:S(2)}, u32[]{:S(2)}) collective-permute-start(bf16[640,128]{1,0:T(8,128)(2,1)S(1)} %get-tuple-element.39), channel_id=1, source_target_pairs={{0,1},{1,0},{2,3},{3,2},{4,5},{5,4},{6,7},{7,6},{8,9},{9,8},{10,11... | collective-permute-start | bytes 491528 | tf_op jit(solution)/shard_map/ppermute | solution.py:461
  38.3 4.3 %shard_map.50 = (bf16[1536,1280]{1,0:T(8,128)(2,1)S(1)}, bf16[1536,1280]{1,0:T(8,128)(2,1)S(1)}, bf16[1024,512]{1,0:T(8,128)(2,1)S(1)}, bf16[1024,512]{1,0:T(8,128)(2,1)S(1)}, f32[1024,512]{1,0:T(8,128)S(1)}) custom-call(s32[14]{0:T(128)S(1)} %concatenate.6.drop_ref, bf16[4,8,128,128]{3,2,1,0:T(8,128)(2,1)S(1)} %copy-done.1, ...), custom_call_target="tpu_custom_call" | custom-call | tf_op jit(solution)/shard_map/pallas_call | solution.py:447
  42.7 1.4 %shard_map.53 = (bf16[1024,512]{1,0:T(8,128)(2,1)S(1)}, bf16[1024,512]{1,0:T(8,128)(2,1)S(1)}) custom-call(s32[14]{0:T(128)S(1)} %concatenate.6.drop_ref, bf16[1280,128]{1,0:T(8,128)(2,1)S(1)} %collective-permute-done.5.far_far, bf16[640,128]{1,0:T(8,128)(2,1)S(1)} %collective-permute-done.6.far_mate, ...), custom_call_target="tpu_custom_call" | custom-call | tf_op jit(solution)/shard_map/pallas_call | solution.py:447
  44.1 3.7 %shard_map.54 = (bf16[1536,512]{1,0:T(8,128)(2,1)S(1)}, bf16[512,512]{1,0:T(8,128)(2,1)S(1)}, f32[1024,512]{1,0:T(8,128)S(1)}) custom-call(s32[14]{0:T(128)S(1)} %concatenate.6.drop_ref, bf16[1536,1280]{1,0:T(8,128)(2,1)S(1)} %get-tuple-element.34.shifted, bf16[1024,512]{1,0:T(8,128)(2,1)S(1)} %get-tuple-element.45.corners, bf16[2048,128]{1,0:T(8,128)(2,1)S(1)} %copy-done.3, ...), custom_call_target="tpu_custom_call" | custom-call | tf_op jit(solution)/shard_map/pallas_call | solution.py:447
  47.9 1.9 %collective-permute-start.13 = (bf16[512,512]{1,0:T(8,128)(2,1)S(1)}, bf16[512,512]{1,0:T(8,128)(2,1)S(1)}, u32[]{:S(2)}, u32[]{:S(2)}) collective-permute-start(bf16[512,512]{1,0:T(8,128)(2,1)S(1)} %get-tuple-element.48.own), channel_id=1, source_target_pairs={{0,1},{1,0},{2,3},{3,2},{4,5},{5,4},{6,7},{7,6},{8,9},{9,8},{10,11... | collective-permute-start | bytes 1572872 | tf_op jit(solution)/shard_map/ppermute | solution.py:461
  49.8 1.3 %shard_map.55 = (bf16[512,512]{1,0:T(8,128)(2,1)S(1)}, bf16[512,512]{1,0:T(8,128)(2,1)S(1)}, bf16[1280,128]{1,0:T(8,128)(2,1)S(1)}, bf16[1280,128]{1,0:T(8,128)(2,1)S(1)}) custom-call(s32[14]{0:T(128)S(1)} %concatenate.6.drop_ref, bf16[3328,128]{1,0:T(8,128)(2,1)S(1)} %collective-permute-done.4.refs_1_.mate, ...), custom_call_target="tpu_custom_call" | custom-call | flops 335544320 | bytes 6750208 | tf_op jit(solution)/shard_map/pallas_call | solution.py:447
  51.2 3.5 %collective-permute-start.12 = (bf16[1280,128]{1,0:T(8,128)(2,1)S(1)}, bf16[1280,128]{1,0:T(8,128)(2,1)S(1)}, u32[]{:S(2)}, u32[]{:S(2)}) collective-permute-start(bf16[1280,128]{1,0:T(8,128)(2,1)S(1)} %get-tuple-element.53), channel_id=1, source_target_pairs={{0,1},{1,0},{2,3},{3,2},{4,5},{5,4},{6,7},{7,6},{8,9},{9,8},{10,11... | collective-permute-start | bytes 983048 | tf_op jit(solution)/shard_map/ppermute | solution.py:461
  54.7 2.0 %shard_map.56.correction = bf16[1536,512]{1,0:T(8,128)(2,1)S(1)} custom-call(s32[14]{0:T(128)S(1)} %concatenate.6.drop_ref, bf16[1536,1280]{1,0:T(8,128)(2,1)S(1)} %get-tuple-element.34.shifted, bf16[1024,512]{1,0:T(8,128)(2,1)S(1)} %get-tuple-element.45.corners, bf16[512,512]{1,0:T(8,128)(2,1)S(1)} %get-tuple-element.54.low, ...), custom_call_target="tpu_custom_call" | custom-call | flops 1275068416 | bytes 8126464 | tf_op jit(solution)/shard_map/pallas_call | solution.py:447
  56.7 10.0 %collective-permute-done.14.cross = bf16[512,512]{1,0:T(8,128)(2,1)S(1)} collective-permute-done((bf16[512,512]{1,0:T(8,128)(2,1)S(1)}, bf16[512,512]{1,0:T(8,128)(2,1)S(1)}, u32[]{:S(2)}, u32[]{:S(2)}) %collective-permute-start.14) | collective-permute-done | bytes 524320 | tf_op jit(solution)/shard_map/ppermute | solution.py:461
  66.7 1.5 %shard_map.57 = (bf16[512,512]{1,0:T(8,128)(2,1)S(1)}, bf16[512,512]{1,0:T(8,128)(2,1)S(1)}, bf16[1280,128]{1,0:T(8,128)(2,1)S(1)}, bf16[1280,128]{1,0:T(8,128)(2,1)S(1)}) custom-call(s32[14]{0:T(128)S(1)} %concatenate.6.drop_ref, bf16[512,512]{1,0:T(8,128)(2,1)S(1)} %collective-permute-done.13.mate, bf16[512,512]{1,0:T(8,128)(2,1)S(1)} %collective-permute-done.14.cross, ...), custom_call_target="tpu_custom_call" | custom-call | flops 671088640 | bytes 5373952 | tf_op jit(solution)/shard_map/pallas_call | solution.py:447
  68.1 2.5 %collective-permute-start.17 = (bf16[1280,128]{1,0:T(8,128)(2,1)S(1)}, bf16[1280,128]{1,0:T(8,128)(2,1)S(1)}, u32[]{:S(2)}, u32[]{:S(2)}) collective-permute-start(bf16[1280,128]{1,0:T(8,128)(2,1)S(1)} %get-tuple-element.62), channel_id=1, source_target_pairs={{0,15},{1,2},{2,1},{3,4},{4,3},{5,6},{6,5},{7,8},{8,7},{9,10},{10,... | collective-permute-start | bytes 983048 | tf_op jit(solution)/shard_map/ppermute | solution.py:461
  70.7 2.0 %collective-permute-done.11.cross = bf16[1280,128]{1,0:T(8,128)(2,1)S(1)} collective-permute-done((bf16[1280,128]{1,0:T(8,128)(2,1)S(1)}, bf16[1280,128]{1,0:T(8,128)(2,1)S(1)}, u32[]{:S(2)}, u32[]{:S(2)}) %collective-permute-start.11) | collective-permute-done | bytes 327712 | tf_op jit(solution)/shard_map/ppermute | solution.py:461
  72.6 2.2 %shard_map.58 = (bf16[1536,512]{1,0:T(8,128)(2,1)S(1)}, bf16[1280,128]{1,0:T(8,128)(2,1)S(1)}, bf16[1280,128]{1,0:T(8,128)(2,1)S(1)}) custom-call(s32[14]{0:T(128)S(1)} %concatenate.6.drop_ref, bf16[512,512]{1,0:T(8,128)(2,1)S(1)} %get-tuple-element.48.own, bf16[1280,128]{1,0:T(8,128)(2,1)S(1)} %collective-permute-done.11.cross, ...), custom_call_target="tpu_custom_call" | custom-call | flops 1275068416 | bytes 11010048 | tf_op jit(solution)/shard_map/pallas_call | solution.py:447
  75.0 1.3 %shard_map.59.own = bf16[512,512]{1,0:T(8,128)(2,1)S(1)} custom-call(s32[14]{0:T(128)S(1)} %concatenate.6.drop_ref, bf16[1536,1280]{1,0:T(8,128)(2,1)S(1)} %get-tuple-element.33.square, bf16[1536,512]{1,0:T(8,128)(2,1)S(1)} %get-tuple-element.59.whole.own), custom_call_target="tpu_custom_call" | custom-call | flops 603979776 | bytes 6029312 | tf_op jit(solution)/shard_map/pallas_call | solution.py:447
  76.3 1.8 %shard_map.61 = bf16[4,8,128,128]{3,2,1,0:T(8,128)(2,1)} custom-call(s32[14]{0:T(128)S(1)} %concatenate.6.drop_ref, bf16[1536,512]{1,0:T(8,128)(2,1)S(1)} %get-tuple-element.59.whole.own, bf16[1280,128]{1,0:T(8,128)(2,1)S(1)} %collective-permute-done.17.cross, bf16[1280,128]{1,0:T(8,128)(2,1)S(1)} %collective-permute-done.18.mate), custom_call_target="tpu_custom_call" | custom-call | bytes 3276800 | tf_op jit(solution)/shard_map/pallas_call | solution.py:447
  78.1 6.8 %collective-permute-done.15.cross = bf16[1280,128]{1,0:T(8,128)(2,1)S(1)} collective-permute-done((bf16[1280,128]{1,0:T(8,128)(2,1)S(1)}, bf16[1280,128]{1,0:T(8,128)(2,1)S(1)}, u32[]{:S(2)}, u32[]{:S(2)}) %collective-permute-start.15) | collective-permute-done | bytes 327712 | tf_op jit(solution)/shard_map/ppermute | solution.py:461
  84.9 1.8 %shard_map.60 = bf16[4,8,128,128]{3,2,1,0:T(8,128)(2,1)} custom-call(s32[14]{0:T(128)S(1)} %concatenate.6.drop_ref, bf16[512,512]{1,0:T(8,128)(2,1)S(1)} %shard_map.59.own, bf16[1280,128]{1,0:T(8,128)(2,1)S(1)} %collective-permute-done.15.cross, bf16[1280,128]{1,0:T(8,128)(2,1)S(1)} %collective-permute-done.16.mate), custom_call_target="tpu_custom_call" | custom-call | bytes 2228224 | tf_op jit(solution)/shard_map/pallas_call | solution.py:447
  (44 shorter events, 6.1 us)
Async XLA Ops:
  0.6 26.8 %collective-permute-start.2 = (bf16[4,8,128,128]{3,2,1,0:T(8,128)(2,1)}, bf16[4,8,128,128]{3,2,1,0:T(8,128)(2,1)S(1)}, u32[]{:S(2)}, u32[]{:S(2)}) collective-permute-start(bf16[4,8,128,128]{3,2,1,0:T(8,128)(2,1)} %own.2), channel_id=1, source_target_pairs={{0,15},{1,2},{2,1},{3,4},{4,3},{5,6},{6,5},{7,8},{8,7},{9,10},{10,... | collective-permute-start | bytes 3145736 | tf_op jit(solution)/shard_map/ppermute | solution.py:461
  3.3 24.1 %collective-permute-start.3 = (bf16[4,8,128,128]{3,2,1,0:T(8,128)(2,1)}, bf16[4,8,128,128]{3,2,1,0:T(8,128)(2,1)S(1)}, u32[]{:S(2)}, u32[]{:S(2)}) collective-permute-start(bf16[4,8,128,128]{3,2,1,0:T(8,128)(2,1)} %own.2), channel_id=1, source_target_pairs={{0,1},{1,0},{2,3},{3,2},{4,5},{5,4},{6,7},{7,6},{8,9},{9,8},{10,11... | collective-permute-start | bytes 3145736 | tf_op jit(solution)/shard_map/ppermute | solution.py:461
  7.1 1.2 %copy-start = (bf16[4,8,128,128]{3,2,1,0:T(8,128)(2,1)S(1)}, bf16[4,8,128,128]{3,2,1,0:T(8,128)(2,1)}, u32[]{:S(2)}) copy-start(bf16[4,8,128,128]{3,2,1,0:T(8,128)(2,1)} %own.3) | copy-start | bytes 3145732
  10.5 0.8 copy-start.2
  12.1 15.3 %collective-permute-start.4 = (bf16[3328,128]{1,0:T(8,128)(2,1)}, bf16[3328,128]{1,0:T(8,128)(2,1)S(1)}, u32[]{:S(2)}, u32[]{:S(2)}) collective-permute-start(bf16[3328,128]{1,0:T(8,128)(2,1)} %get-tuple-element.35.sent_mate), channel_id=1, source_target_pairs={{0,1},{1,0},{2,3},{3,2},{4,5},{5,4},{6,7},{7,6},{8,9},{9,8},{10,11... | collective-permute-start | bytes 2555912 | tf_op jit(solution)/shard_map/ppermute | solution.py:461
  12.1 2.0 %collective-permute-start.1 = (s32[4]{0:T(128)S(1)}, s32[4]{0:T(128)S(1)}, u32[]{:S(2)}, u32[]{:S(2)}) collective-permute-start(s32[4]{0:T(128)S(1)} %broadcast_subtract_fusion), channel_id=1, source_target_pairs={{0,1},{1,0},{2,3},{3,2},{4,5},{5,4},{6,7},{7,6},{8,9},{9,8},{10,11... | collective-permute-start | bytes 56 | tf_op jit(solution)/shard_map/ppermute | solution.py:461
  12.6 14.7 %collective-permute-start = (s32[4]{0:T(128)S(1)}, s32[4]{0:T(128)S(1)}, u32[]{:S(2)}, u32[]{:S(2)}) collective-permute-start(s32[4]{0:T(128)S(1)} %broadcast_subtract_fusion), channel_id=1, source_target_pairs={{0,15},{1,2},{2,1},{3,4},{4,3},{5,6},{6,5},{7,8},{8,7},{9,10},{10,... | collective-permute-start | bytes 56 | tf_op jit(solution)/shard_map/ppermute | solution.py:461
  14.1 24.2 %collective-permute-start.8 = (bf16[1280,128]{1,0:T(8,128)(2,1)}, bf16[1280,128]{1,0:T(8,128)(2,1)S(1)}, u32[]{:S(2)}, u32[]{:S(2)}) collective-permute-start(bf16[1280,128]{1,0:T(8,128)(2,1)} %copy-done.4), channel_id=1, source_target_pairs={{1,2},{2,1},{5,6},{6,5},{9,10},{10,9},{13,14},{14,13},{17,18},{18,... | collective-permute-start | bytes 983048 | tf_op jit(solution)/shard_map/ppermute | solution.py:461
  27.4 11.0 %copy-start.1 = (bf16[4,8,128,128]{3,2,1,0:T(8,128)(2,1)S(1)}, bf16[4,8,128,128]{3,2,1,0:T(8,128)(2,1)}, u32[]{:S(2)}) copy-start(bf16[4,8,128,128]{3,2,1,0:T(8,128)(2,1)} %own.2) | copy-start | bytes 3145732
  28.1 14.5 %collective-permute-start.5 = (bf16[1280,128]{1,0:T(8,128)(2,1)S(1)}, bf16[1280,128]{1,0:T(8,128)(2,1)S(1)}, u32[]{:S(2)}, u32[]{:S(2)}) collective-permute-start(bf16[1280,128]{1,0:T(8,128)(2,1)S(1)} %get-tuple-element.38), channel_id=1, source_target_pairs={{0,13},{1,4},{2,15},{3,6},{4,1},{5,8},{6,3},{7,10},{8,5},{9,12},{1... | collective-permute-start | bytes 983048 | tf_op jit(solution)/shard_map/ppermute | solution.py:461
  28.2 15.9 %collective-permute-start.9 = (bf16[1280,128]{1,0:T(8,128)(2,1)}, bf16[1280,128]{1,0:T(8,128)(2,1)S(1)}, u32[]{:S(2)}, u32[]{:S(2)}) collective-permute-start(bf16[1280,128]{1,0:T(8,128)(2,1)} %get-tuple-element.47), channel_id=1, source_target_pairs={{0,15},{3,4},{4,3},{7,8},{8,7},{11,12},{12,11},{15,0},{16,31},{19,... | collective-permute-start | bytes 983048 | tf_op jit(solution)/shard_map/ppermute | solution.py:461
  28.9 20.9 %collective-permute-start.10 = (bf16[2048,128]{1,0:T(8,128)(2,1)}, bf16[2048,128]{1,0:T(8,128)(2,1)S(1)}, u32[]{:S(2)}, u32[]{:S(2)}) collective-permute-start(bf16[2048,128]{1,0:T(8,128)(2,1)} %get-tuple-element.49), channel_id=1, source_target_pairs={{0,15},{1,2},{2,1},{3,4},{4,3},{5,6},{6,5},{7,8},{8,7},{9,10},{10,... | collective-permute-start | bytes 1572872 | tf_op jit(solution)/shard_map/ppermute | solution.py:461
  30.7 11.9 %collective-permute-start.6 = (bf16[640,128]{1,0:T(8,128)(2,1)S(1)}, bf16[640,128]{1,0:T(8,128)(2,1)S(1)}, u32[]{:S(2)}, u32[]{:S(2)}) collective-permute-start(bf16[640,128]{1,0:T(8,128)(2,1)S(1)} %get-tuple-element.39), channel_id=1, source_target_pairs={{0,1},{1,0},{2,3},{3,2},{4,5},{5,4},{6,7},{7,6},{8,9},{9,8},{10,11... | collective-permute-start | bytes 491528 | tf_op jit(solution)/shard_map/ppermute | solution.py:461
  38.3 4.3 %collective-permute-start.7 = (bf16[640,128]{1,0:T(8,128)(2,1)S(1)}, bf16[640,128]{1,0:T(8,128)(2,1)S(1)}, u32[]{:S(2)}, u32[]{:S(2)}) collective-permute-start(bf16[640,128]{1,0:T(8,128)(2,1)S(1)} %get-tuple-element.40), channel_id=1, source_target_pairs={{0,1},{1,0},{2,3},{3,2},{4,5},{5,4},{6,7},{7,6},{8,9},{9,8},{10,11... | collective-permute-start | bytes 491528 | tf_op jit(solution)/shard_map/ppermute | solution.py:461
  42.7 1.4 %copy-start.3 = (bf16[2048,128]{1,0:T(8,128)(2,1)S(1)}, bf16[2048,128]{1,0:T(8,128)(2,1)}, u32[]{:S(2)}) copy-start(bf16[2048,128]{1,0:T(8,128)(2,1)} %copy-done.2) | copy-start | bytes 1572868
  42.7 1.4 %copy-start.5 = (bf16[1280,128]{1,0:T(8,128)(2,1)S(1)}, bf16[1280,128]{1,0:T(8,128)(2,1)}, u32[]{:S(2)}) copy-start(bf16[1280,128]{1,0:T(8,128)(2,1)} %copy-done.4) | copy-start | bytes 983044
  47.8 18.8 %collective-permute-start.14 = (bf16[512,512]{1,0:T(8,128)(2,1)S(1)}, bf16[512,512]{1,0:T(8,128)(2,1)S(1)}, u32[]{:S(2)}, u32[]{:S(2)}) collective-permute-start(bf16[512,512]{1,0:T(8,128)(2,1)S(1)} %get-tuple-element.48.own), channel_id=1, source_target_pairs={{0,15},{1,2},{2,1},{3,4},{4,3},{5,6},{6,5},{7,8},{8,7},{9,10},{10,... | collective-permute-start | bytes 1572872 | tf_op jit(solution)/shard_map/ppermute | solution.py:461
  47.9 18.8 %collective-permute-start.13 = (bf16[512,512]{1,0:T(8,128)(2,1)S(1)}, bf16[512,512]{1,0:T(8,128)(2,1)S(1)}, u32[]{:S(2)}, u32[]{:S(2)}) collective-permute-start(bf16[512,512]{1,0:T(8,128)(2,1)S(1)} %get-tuple-element.48.own), channel_id=1, source_target_pairs={{0,1},{1,0},{2,3},{3,2},{4,5},{5,4},{6,7},{7,6},{8,9},{9,8},{10,11... | collective-permute-start | bytes 1572872 | tf_op jit(solution)/shard_map/ppermute | solution.py:461
  51.1 21.5 %collective-permute-start.11 = (bf16[1280,128]{1,0:T(8,128)(2,1)S(1)}, bf16[1280,128]{1,0:T(8,128)(2,1)S(1)}, u32[]{:S(2)}, u32[]{:S(2)}) collective-permute-start(bf16[1280,128]{1,0:T(8,128)(2,1)S(1)} %get-tuple-element.52), channel_id=1, source_target_pairs={{0,15},{1,2},{2,1},{3,4},{4,3},{5,6},{6,5},{7,8},{8,7},{9,10},{10,... | collective-permute-start | bytes 983048 | tf_op jit(solution)/shard_map/ppermute | solution.py:461
  51.2 21.5 %collective-permute-start.12 = (bf16[1280,128]{1,0:T(8,128)(2,1)S(1)}, bf16[1280,128]{1,0:T(8,128)(2,1)S(1)}, u32[]{:S(2)}, u32[]{:S(2)}) collective-permute-start(bf16[1280,128]{1,0:T(8,128)(2,1)S(1)} %get-tuple-element.53), channel_id=1, source_target_pairs={{0,1},{1,0},{2,3},{3,2},{4,5},{5,4},{6,7},{7,6},{8,9},{9,8},{10,11... | collective-permute-start | bytes 983048 | tf_op jit(solution)/shard_map/ppermute | solution.py:461
  68.1 8.2 %collective-permute-start.17 = (bf16[1280,128]{1,0:T(8,128)(2,1)S(1)}, bf16[1280,128]{1,0:T(8,128)(2,1)S(1)}, u32[]{:S(2)}, u32[]{:S(2)}) collective-permute-start(bf16[1280,128]{1,0:T(8,128)(2,1)S(1)} %get-tuple-element.62), channel_id=1, source_target_pairs={{0,15},{1,2},{2,1},{3,4},{4,3},{5,6},{6,5},{7,8},{8,7},{9,10},{10,... | collective-permute-start | bytes 983048 | tf_op jit(solution)/shard_map/ppermute | solution.py:461
  70.7 5.6 %collective-permute-start.18 = (bf16[1280,128]{1,0:T(8,128)(2,1)S(1)}, bf16[1280,128]{1,0:T(8,128)(2,1)S(1)}, u32[]{:S(2)}, u32[]{:S(2)}) collective-permute-start(bf16[1280,128]{1,0:T(8,128)(2,1)S(1)} %get-tuple-element.63), channel_id=1, source_target_pairs={{0,1},{1,0},{2,3},{3,2},{4,5},{5,4},{6,7},{7,6},{8,9},{9,8},{10,11... | collective-permute-start | bytes 983048 | tf_op jit(solution)/shard_map/ppermute | solution.py:461
  74.8 10.1 %collective-permute-start.15 = (bf16[1280,128]{1,0:T(8,128)(2,1)S(1)}, bf16[1280,128]{1,0:T(8,128)(2,1)S(1)}, u32[]{:S(2)}, u32[]{:S(2)}) collective-permute-start(bf16[1280,128]{1,0:T(8,128)(2,1)S(1)} %get-tuple-element.60), channel_id=1, source_target_pairs={{0,15},{1,2},{2,1},{3,4},{4,3},{5,6},{6,5},{7,8},{8,7},{9,10},{10,... | collective-permute-start | bytes 983048 | tf_op jit(solution)/shard_map/ppermute | solution.py:461
  74.9 10.0 %collective-permute-start.16 = (bf16[1280,128]{1,0:T(8,128)(2,1)S(1)}, bf16[1280,128]{1,0:T(8,128)(2,1)S(1)}, u32[]{:S(2)}, u32[]{:S(2)}) collective-permute-start(bf16[1280,128]{1,0:T(8,128)(2,1)S(1)} %get-tuple-element.61), channel_id=1, source_target_pairs={{0,1},{1,0},{2,3},{3,2},{4,5},{5,4},{6,7},{7,6},{8,9},{9,8},{10,11... | collective-permute-start | bytes 983048 | tf_op jit(solution)/shard_map/ppermute | solution.py:461
  (1 other events, 0.7 us)

commit v13 on v12

--- a/solution.py
+++ b/solution.py
@@ -166,13 +166,12 @@
 def forward_kernel(f, drop_ref, cross, *refs):
     h = f.h
     odd = odd_place(f, drop_ref)
-    to_mate, to_far = refs[-5:-3], refs[-3]
+    to_mate, to_far = refs[-4:-2]
     for i, (lower, upper) in enumerate(zip(under(h), over(h))):
         (r, c), (s, d) = lower, upper
         forth = stored(cross, r, 2 * h + c - r, jnp.where(odd, drop_ref[2 * h + r], drop_ref[r]))
         back = stored(cross, s, d - s, jnp.where(odd, drop_ref[2 * h + s], drop_ref[s]))
-        part, place = i % 2, i // 2
-        to_mate[part][block(f, place, 0)] = jnp.where(odd, back, forth)
+        to_mate[block(f, i, 0)] = jnp.where(odd, back, forth)
         to_far[block(f, i, 0)] = jnp.where(odd, forth, back)
 
 
@@ -223,11 +222,10 @@
 
 
 def corners_kernel(
-    f, drop_ref, far_far, far_mate, far_mate_too, reach, here, partial, unused, square, shifted, low, high
+    f, drop_ref, far_far, far_mate, reach, here, partial, unused, square, shifted, low, high
 ):
     p = f.p
-    far_mates = [indexed(f, far_mate), indexed(f, far_mate_too)]
-    far_below, far_above = sides(f, drop_ref, lambda i: far_mates[i % 2](i // 2), indexed(f, far_far))
+    far_below, far_above = sides(f, drop_ref, indexed(f, far_mate), indexed(f, far_far))
     spread(f, low, 0, 0, far_below, under(f.h))
     spread(f, high, 0, 0, far_above, over(f.h))
     unit = unit_tile(f)
@@ -506,7 +504,6 @@
     columns = jax.ShapeDtypeStruct((3 * f.group, f.group), kind)
     band = jax.ShapeDtypeStruct((3 * f.group, (2 * f.p + 1) * f.t), kind)
     triangle = jax.ShapeDtypeStruct((count * order, order), kind)
-    half_triangle = jax.ShapeDtypeStruct((count // 2 * order, order), kind)
     listed = jax.ShapeDtypeStruct((half * half * order, order), kind)
     both = jax.ShapeDtypeStruct(((count + half * half) * order, order), kind)
     partial_sums = jax.ShapeDtypeStruct((2 * f.group, f.group), jnp.float32)
@@ -521,11 +518,11 @@
     )
     from_mate = to_mate(slab_mate)
     direct_triangle = routed(triangle_cross, lambda i: 0 if turns(i) else cross_step(i))
-    forward_mate, forward_mate_too, forward_far, triangle_turning, corner_cross = run(
-        forward_kernel, [half_triangle, half_triangle, triangle], [], 0, 12, drop, density_cross, density_mate, from_mate,
+    forward_mate, forward_far, triangle_turning, corner_cross = run(
+        forward_kernel, [triangle, triangle], [], 0, 12, drop, density_cross, density_mate, from_mate,
         passed=(triangle_turning, corner_cross),
     )
-    far_mate, far_mate_too = to_mate(forward_mate), to_mate(forward_mate_too)
+    far_mate = to_mate(forward_mate)
     far_far = routed(forward_far, lambda i: 3 * cross_step(i))
     turned_triangle = routed(triangle_turning, lambda i: cross_step(i) if turns(i) else 0)
     cross_corner = to_cross(corner_cross)
@@ -541,7 +538,7 @@
         corners_kernel,
         [both_corners, both_corners],
         [group_scratch] * 2,
-        10, 16, drop, far_far, far_mate, far_mate_too, reach, here, partial,
+        10, 16, drop, far_far, far_mate, reach, here, partial,
         direct_triangle, light=True,
     )
     correction, own, partial = run(

time: 86.9 us -> 86.7 us (level)
  starting transfers between devices: 26.6 us -> 24.8 us
  waiting for transfers between devices: 31.3 us -> 32.8 us
    ppermute x19 -> x18, starting transfers between devices: 26.6 us -> 24.8 us  [routed(): lax.ppermute(x, RING, [(i, (i + step(i)) % size) for i in range(size) if...]
    ppermute x19 -> x18, waiting for transfers between devices: 31.3 us -> 32.8 us  [routed(): lax.ppermute(x, RING, [(i, (i + step(i)) % size) for i in range(size) if...]
  transfers between devices with their start and end apart: 19 -> 18, of which waited for: 5 -> 7; matrix products, arithmetic and copies ran while one was open for 1% -> 1% of each run, Pallas kernels for 26% -> 26%
where the time goes in v13:
time: 86.7 us; the launch traced here: 86.4 us
  waiting for transfers between devices  32.8 us (38%)
  starting transfers between devices  24.8 us (29%)
  Pallas kernels  24.1 us (28%)
  local copies, waits for them, and re-layouts  2.88 us (3%)
  other arithmetic  0.96 us (1%)
    ppermute x18, waiting for transfers between devices, routed(): lax.ppermute(x, RING, [(i, (i + step(i)) % size) for i in range(size) if...  32.8 us
    ppermute x18, starting transfers between devices, routed(): lax.ppermute(x, RING, [(i, (i + step(i)) % size) for i in range(size) if...  24.8 us
    pallas_call x12, Pallas kernels, call(): pl.pallas_call(kernel, out_shape=[*outs, *[jax.ShapeDtypeStruct(a.shape,...  24.1 us
    unnamed x12, local copies, waits for them, and re-layouts  2.8 us
  transfers between devices with their start and end apart: 18, of which 7 were waited for; matrix products, arithmetic and copies ran while one was open for 1% of the time, Pallas kernels for 26%

profile of v13, /device:TPU:1, one launch (start us, length us, event | category | flops | bytes accessed | tf_op | source)
XLA Modules:
  0.0 86.4 jit_solution(7688698780692715778)
XLA Ops:
  0.6 2.7 %collective-permute-start.2 = (bf16[4,8,128,128]{3,2,1,0:T(8,128)(2,1)}, bf16[4,8,128,128]{3,2,1,0:T(8,128)(2,1)S(1)}, u32[]{:S(2)}, u32[]{:S(2)}) collective-permute-start(bf16[4,8,128,128]{3,2,1,0:T(8,128)(2,1)} %own.2), channel_id=1, source_target_pairs={{0,15},{1,2},{2,1},{3,4},{4,3},{5,6},{6,5},{7,8},{8,7},{9,10},{10,... | collective-permute-start | bytes 3145736 | tf_op jit(solution)/shard_map/ppermute | solution.py:459
  3.3 2.9 %collective-permute-start.3 = (bf16[4,8,128,128]{3,2,1,0:T(8,128)(2,1)}, bf16[4,8,128,128]{3,2,1,0:T(8,128)(2,1)S(1)}, u32[]{:S(2)}, u32[]{:S(2)}) collective-permute-start(bf16[4,8,128,128]{3,2,1,0:T(8,128)(2,1)} %own.2), channel_id=1, source_target_pairs={{0,1},{1,0},{2,3},{3,2},{4,5},{5,4},{6,7},{7,6},{8,9},{9,8},{10,11... | collective-permute-start | bytes 3145736 | tf_op jit(solution)/shard_map/ppermute | solution.py:459
  8.4 2.2 %shard_map.51 = (bf16[2048,128]{1,0:T(8,128)(2,1)S(1)}, bf16[2048,128]{1,0:T(8,128)(2,1)}, bf16[3328,128]{1,0:T(8,128)(2,1)}, bf16[1280,128]{1,0:T(8,128)(2,1)S(1)}, bf16[1280,128]{1,0:T(8,128)(2,1)}) custom-call(s32[5]{0:T(128)S(1)} %pad_add_fusion.drop_ref, bf16[4,8,128,128]{3,2,1,0:T(8,128)(2,1)S(1)} %copy-done), custom_call_target="tpu_custom_call" | custom-call | bytes 3604480 | tf_op jit(solution)/shard_map/pallas_call | solution.py:445
  12.6 1.5 %collective-permute-done.1 = s32[4]{0:T(128)S(1)} collective-permute-done((s32[4]{0:T(128)S(1)}, s32[4]{0:T(128)S(1)}, u32[]{:S(2)}, u32[]{:S(2)}) %collective-permute-start.1) | collective-permute-done | bytes 48 | tf_op jit(solution)/shard_map/ppermute | solution.py:459
  14.1 2.1 %collective-permute-start.7 = (bf16[1280,128]{1,0:T(8,128)(2,1)}, bf16[1280,128]{1,0:T(8,128)(2,1)S(1)}, u32[]{:S(2)}, u32[]{:S(2)}) collective-permute-start(bf16[1280,128]{1,0:T(8,128)(2,1)} %copy-done.4), channel_id=1, source_target_pairs={{1,2},{2,1},{5,6},{6,5},{9,10},{10,9},{13,14},{14,13},{17,18},{18,... | collective-permute-start | bytes 983048 | tf_op jit(solution)/shard_map/ppermute | solution.py:459
  16.3 11.0 %collective-permute-done = s32[4]{0:T(128)S(1)} collective-permute-done((s32[4]{0:T(128)S(1)}, s32[4]{0:T(128)S(1)}, u32[]{:S(2)}, u32[]{:S(2)}) %collective-permute-start) | collective-permute-done | bytes 48 | tf_op jit(solution)/shard_map/ppermute | solution.py:459
  28.2 3.7 %collective-permute-start.6 = (bf16[1280,128]{1,0:T(8,128)(2,1)S(1)}, bf16[1280,128]{1,0:T(8,128)(2,1)S(1)}, u32[]{:S(2)}, u32[]{:S(2)}) collective-permute-start(bf16[1280,128]{1,0:T(8,128)(2,1)S(1)} %get-tuple-element.38), channel_id=1, source_target_pairs={{0,1},{1,0},{2,3},{3,2},{4,5},{5,4},{6,7},{7,6},{8,9},{9,8},{10,11... | collective-permute-start | bytes 983048 | tf_op jit(solution)/shard_map/ppermute | solution.py:459
  32.7 4.3 %shard_map.50 = (bf16[1536,1280]{1,0:T(8,128)(2,1)S(1)}, bf16[1536,1280]{1,0:T(8,128)(2,1)S(1)}, bf16[1024,512]{1,0:T(8,128)(2,1)S(1)}, bf16[1024,512]{1,0:T(8,128)(2,1)S(1)}, f32[1024,512]{1,0:T(8,128)S(1)}) custom-call(s32[14]{0:T(128)S(1)} %concatenate.6.drop_ref, bf16[4,8,128,128]{3,2,1,0:T(8,128)(2,1)S(1)} %copy-done.1, ...), custom_call_target="tpu_custom_call" | custom-call | tf_op jit(solution)/shard_map/pallas_call | solution.py:445
  37.9 1.4 %shard_map.53 = (bf16[1024,512]{1,0:T(8,128)(2,1)S(1)}, bf16[1024,512]{1,0:T(8,128)(2,1)S(1)}) custom-call(s32[14]{0:T(128)S(1)} %concatenate.6.drop_ref, bf16[1280,128]{1,0:T(8,128)(2,1)S(1)} %collective-permute-done.5.far_far, bf16[1280,128]{1,0:T(8,128)(2,1)S(1)} %collective-permute-done.6.far_mate, bf16[1024,512]{1,0:T(8,128)(2,1)S(1)} %get-tuple-element.39.reach, ...), custom_call_target="tpu_custom_call" | custom-call | tf_op jit(solution)/shard_map/pallas_call | solution.py:445
  39.4 3.7 %shard_map.54 = (bf16[1536,512]{1,0:T(8,128)(2,1)S(1)}, bf16[512,512]{1,0:T(8,128)(2,1)S(1)}, f32[1024,512]{1,0:T(8,128)S(1)}) custom-call(s32[14]{0:T(128)S(1)} %concatenate.6.drop_ref, bf16[1536,1280]{1,0:T(8,128)(2,1)S(1)} %get-tuple-element.33.shifted, bf16[1024,512]{1,0:T(8,128)(2,1)S(1)} %get-tuple-element.43.corners, bf16[2048,128]{1,0:T(8,128)(2,1)S(1)} %copy-done.3, ...), custom_call_target="tpu_custom_call" | custom-call | tf_op jit(solution)/shard_map/pallas_call | solution.py:445
  43.1 3.6 %collective-permute-start.13 = (bf16[512,512]{1,0:T(8,128)(2,1)S(1)}, bf16[512,512]{1,0:T(8,128)(2,1)S(1)}, u32[]{:S(2)}, u32[]{:S(2)}) collective-permute-start(bf16[512,512]{1,0:T(8,128)(2,1)S(1)} %get-tuple-element.46.own), channel_id=1, source_target_pairs={{0,15},{1,2},{2,1},{3,4},{4,3},{5,6},{6,5},{7,8},{8,7},{9,10},{10,... | collective-permute-start | bytes 1572872 | tf_op jit(solution)/shard_map/ppermute | solution.py:459
  46.7 2.8 %collective-permute-start.12 = (bf16[512,512]{1,0:T(8,128)(2,1)S(1)}, bf16[512,512]{1,0:T(8,128)(2,1)S(1)}, u32[]{:S(2)}, u32[]{:S(2)}) collective-permute-start(bf16[512,512]{1,0:T(8,128)(2,1)S(1)} %get-tuple-element.46.own), channel_id=1, source_target_pairs={{0,1},{1,0},{2,3},{3,2},{4,5},{5,4},{6,7},{7,6},{8,9},{9,8},{10,11... | collective-permute-start | bytes 1572872 | tf_op jit(solution)/shard_map/ppermute | solution.py:459
  50.6 1.3 %shard_map.55 = (bf16[512,512]{1,0:T(8,128)(2,1)S(1)}, bf16[512,512]{1,0:T(8,128)(2,1)S(1)}, bf16[1280,128]{1,0:T(8,128)(2,1)S(1)}, bf16[1280,128]{1,0:T(8,128)(2,1)S(1)}) custom-call(s32[14]{0:T(128)S(1)} %concatenate.6.drop_ref, bf16[3328,128]{1,0:T(8,128)(2,1)S(1)} %collective-permute-done.4.refs_1_.mate, ...), custom_call_target="tpu_custom_call" | custom-call | flops 335544320 | bytes 6750208 | tf_op jit(solution)/shard_map/pallas_call | solution.py:445
  52.0 2.8 %collective-permute-start.11 = (bf16[1280,128]{1,0:T(8,128)(2,1)S(1)}, bf16[1280,128]{1,0:T(8,128)(2,1)S(1)}, u32[]{:S(2)}, u32[]{:S(2)}) collective-permute-start(bf16[1280,128]{1,0:T(8,128)(2,1)S(1)} %get-tuple-element.51), channel_id=1, source_target_pairs={{0,1},{1,0},{2,3},{3,2},{4,5},{5,4},{6,7},{7,6},{8,9},{9,8},{10,11... | collective-permute-start | bytes 983048 | tf_op jit(solution)/shard_map/ppermute | solution.py:459
  54.8 2.0 %shard_map.56.correction = bf16[1536,512]{1,0:T(8,128)(2,1)S(1)} custom-call(s32[14]{0:T(128)S(1)} %concatenate.6.drop_ref, bf16[1536,1280]{1,0:T(8,128)(2,1)S(1)} %get-tuple-element.33.shifted, bf16[1024,512]{1,0:T(8,128)(2,1)S(1)} %get-tuple-element.43.corners, bf16[512,512]{1,0:T(8,128)(2,1)S(1)} %get-tuple-element.52.low, ...), custom_call_target="tpu_custom_call" | custom-call | flops 1275068416 | bytes 8126464 | tf_op jit(solution)/shard_map/pallas_call | solution.py:445
  56.8 9.6 %collective-permute-done.13.cross = bf16[512,512]{1,0:T(8,128)(2,1)S(1)} collective-permute-done((bf16[512,512]{1,0:T(8,128)(2,1)S(1)}, bf16[512,512]{1,0:T(8,128)(2,1)S(1)}, u32[]{:S(2)}, u32[]{:S(2)}) %collective-permute-start.13) | collective-permute-done | bytes 524320 | tf_op jit(solution)/shard_map/ppermute | solution.py:459
  66.4 1.5 %shard_map.57 = (bf16[512,512]{1,0:T(8,128)(2,1)S(1)}, bf16[512,512]{1,0:T(8,128)(2,1)S(1)}, bf16[1280,128]{1,0:T(8,128)(2,1)S(1)}, bf16[1280,128]{1,0:T(8,128)(2,1)S(1)}) custom-call(s32[14]{0:T(128)S(1)} %concatenate.6.drop_ref, bf16[512,512]{1,0:T(8,128)(2,1)S(1)} %collective-permute-done.12.mate, bf16[512,512]{1,0:T(8,128)(2,1)S(1)} %collective-permute-done.13.cross, ...), custom_call_target="tpu_custom_call" | custom-call | flops 671088640 | bytes 5373952 | tf_op jit(solution)/shard_map/pallas_call | solution.py:445
  67.9 2.5 %collective-permute-start.16 = (bf16[1280,128]{1,0:T(8,128)(2,1)S(1)}, bf16[1280,128]{1,0:T(8,128)(2,1)S(1)}, u32[]{:S(2)}, u32[]{:S(2)}) collective-permute-start(bf16[1280,128]{1,0:T(8,128)(2,1)S(1)} %get-tuple-element.60), channel_id=1, source_target_pairs={{0,15},{1,2},{2,1},{3,4},{4,3},{5,6},{6,5},{7,8},{8,7},{9,10},{10,... | collective-permute-start | bytes 983048 | tf_op jit(solution)/shard_map/ppermute | solution.py:459
  70.4 2.0 %collective-permute-done.10.cross = bf16[1280,128]{1,0:T(8,128)(2,1)S(1)} collective-permute-done((bf16[1280,128]{1,0:T(8,128)(2,1)S(1)}, bf16[1280,128]{1,0:T(8,128)(2,1)S(1)}, u32[]{:S(2)}, u32[]{:S(2)}) %collective-permute-start.10) | collective-permute-done | bytes 327712 | tf_op jit(solution)/shard_map/ppermute | solution.py:459
  72.4 2.2 %shard_map.58 = (bf16[1536,512]{1,0:T(8,128)(2,1)S(1)}, bf16[1280,128]{1,0:T(8,128)(2,1)S(1)}, bf16[1280,128]{1,0:T(8,128)(2,1)S(1)}) custom-call(s32[14]{0:T(128)S(1)} %concatenate.6.drop_ref, bf16[512,512]{1,0:T(8,128)(2,1)S(1)} %get-tuple-element.46.own, bf16[1280,128]{1,0:T(8,128)(2,1)S(1)} %collective-permute-done.10.cross, ...), custom_call_target="tpu_custom_call" | custom-call | flops 1275068416 | bytes 11010048 | tf_op jit(solution)/shard_map/pallas_call | solution.py:445
  74.8 1.3 %shard_map.59.own = bf16[512,512]{1,0:T(8,128)(2,1)S(1)} custom-call(s32[14]{0:T(128)S(1)} %concatenate.6.drop_ref, bf16[1536,1280]{1,0:T(8,128)(2,1)S(1)} %get-tuple-element.32.square, bf16[1536,512]{1,0:T(8,128)(2,1)S(1)} %get-tuple-element.57.whole.own), custom_call_target="tpu_custom_call" | custom-call | flops 603979776 | bytes 6029312 | tf_op jit(solution)/shard_map/pallas_call | solution.py:445
  76.2 1.8 %shard_map.61 = bf16[4,8,128,128]{3,2,1,0:T(8,128)(2,1)} custom-call(s32[14]{0:T(128)S(1)} %concatenate.6.drop_ref, bf16[1536,512]{1,0:T(8,128)(2,1)S(1)} %get-tuple-element.57.whole.own, bf16[1280,128]{1,0:T(8,128)(2,1)S(1)} %collective-permute-done.16.cross, bf16[1280,128]{1,0:T(8,128)(2,1)S(1)} %collective-permute-done.17.mate), custom_call_target="tpu_custom_call" | custom-call | bytes 3276800 | tf_op jit(solution)/shard_map/pallas_call | solution.py:445
  77.9 6.7 %collective-permute-done.14.cross = bf16[1280,128]{1,0:T(8,128)(2,1)S(1)} collective-permute-done((bf16[1280,128]{1,0:T(8,128)(2,1)S(1)}, bf16[1280,128]{1,0:T(8,128)(2,1)S(1)}, u32[]{:S(2)}, u32[]{:S(2)}) %collective-permute-start.14) | collective-permute-done | bytes 327712 | tf_op jit(solution)/shard_map/ppermute | solution.py:459
  84.6 1.8 %shard_map.60 = bf16[4,8,128,128]{3,2,1,0:T(8,128)(2,1)} custom-call(s32[14]{0:T(128)S(1)} %concatenate.6.drop_ref, bf16[512,512]{1,0:T(8,128)(2,1)S(1)} %shard_map.59.own, bf16[1280,128]{1,0:T(8,128)(2,1)S(1)} %collective-permute-done.14.cross, bf16[1280,128]{1,0:T(8,128)(2,1)S(1)} %collective-permute-done.15.mate), custom_call_target="tpu_custom_call" | custom-call | bytes 2228224 | tf_op jit(solution)/shard_map/pallas_call | solution.py:445
  (42 shorter events, 8.3 us)
Async XLA Ops:
  0.6 26.8 %collective-permute-start.2 = (bf16[4,8,128,128]{3,2,1,0:T(8,128)(2,1)}, bf16[4,8,128,128]{3,2,1,0:T(8,128)(2,1)S(1)}, u32[]{:S(2)}, u32[]{:S(2)}) collective-permute-start(bf16[4,8,128,128]{3,2,1,0:T(8,128)(2,1)} %own.2), channel_id=1, source_target_pairs={{0,15},{1,2},{2,1},{3,4},{4,3},{5,6},{6,5},{7,8},{8,7},{9,10},{10,... | collective-permute-start | bytes 3145736 | tf_op jit(solution)/shard_map/ppermute | solution.py:459
  3.3 24.1 %collective-permute-start.3 = (bf16[4,8,128,128]{3,2,1,0:T(8,128)(2,1)}, bf16[4,8,128,128]{3,2,1,0:T(8,128)(2,1)S(1)}, u32[]{:S(2)}, u32[]{:S(2)}) collective-permute-start(bf16[4,8,128,128]{3,2,1,0:T(8,128)(2,1)} %own.2), channel_id=1, source_target_pairs={{0,1},{1,0},{2,3},{3,2},{4,5},{5,4},{6,7},{7,6},{8,9},{9,8},{10,11... | collective-permute-start | bytes 3145736 | tf_op jit(solution)/shard_map/ppermute | solution.py:459
  7.1 1.2 %copy-start = (bf16[4,8,128,128]{3,2,1,0:T(8,128)(2,1)S(1)}, bf16[4,8,128,128]{3,2,1,0:T(8,128)(2,1)}, u32[]{:S(2)}) copy-start(bf16[4,8,128,128]{3,2,1,0:T(8,128)(2,1)} %own.3) | copy-start | bytes 3145732
  10.5 0.8 copy-start.2
  11.4 0.7 copy-start.4
  12.1 15.3 %collective-permute-start.4 = (bf16[3328,128]{1,0:T(8,128)(2,1)}, bf16[3328,128]{1,0:T(8,128)(2,1)S(1)}, u32[]{:S(2)}, u32[]{:S(2)}) collective-permute-start(bf16[3328,128]{1,0:T(8,128)(2,1)} %get-tuple-element.34.sent_mate), channel_id=1, source_target_pairs={{0,1},{1,0},{2,3},{3,2},{4,5},{5,4},{6,7},{7,6},{8,9},{9,8},{10,11... | collective-permute-start | bytes 2555912 | tf_op jit(solution)/shard_map/ppermute | solution.py:459
  12.1 2.0 %collective-permute-start.1 = (s32[4]{0:T(128)S(1)}, s32[4]{0:T(128)S(1)}, u32[]{:S(2)}, u32[]{:S(2)}) collective-permute-start(s32[4]{0:T(128)S(1)} %broadcast_subtract_fusion), channel_id=1, source_target_pairs={{0,1},{1,0},{2,3},{3,2},{4,5},{5,4},{6,7},{7,6},{8,9},{9,8},{10,11... | collective-permute-start | bytes 56 | tf_op jit(solution)/shard_map/ppermute | solution.py:459
  12.6 14.7 %collective-permute-start = (s32[4]{0:T(128)S(1)}, s32[4]{0:T(128)S(1)}, u32[]{:S(2)}, u32[]{:S(2)}) collective-permute-start(s32[4]{0:T(128)S(1)} %broadcast_subtract_fusion), channel_id=1, source_target_pairs={{0,15},{1,2},{2,1},{3,4},{4,3},{5,6},{6,5},{7,8},{8,7},{9,10},{10,... | collective-permute-start | bytes 56 | tf_op jit(solution)/shard_map/ppermute | solution.py:459
  14.1 22.9 %collective-permute-start.7 = (bf16[1280,128]{1,0:T(8,128)(2,1)}, bf16[1280,128]{1,0:T(8,128)(2,1)S(1)}, u32[]{:S(2)}, u32[]{:S(2)}) collective-permute-start(bf16[1280,128]{1,0:T(8,128)(2,1)} %copy-done.4), channel_id=1, source_target_pairs={{1,2},{2,1},{5,6},{6,5},{9,10},{10,9},{13,14},{14,13},{17,18},{18,... | collective-permute-start | bytes 983048 | tf_op jit(solution)/shard_map/ppermute | solution.py:459
  27.4 5.3 %copy-start.1 = (bf16[4,8,128,128]{3,2,1,0:T(8,128)(2,1)S(1)}, bf16[4,8,128,128]{3,2,1,0:T(8,128)(2,1)}, u32[]{:S(2)}) copy-start(bf16[4,8,128,128]{3,2,1,0:T(8,128)(2,1)} %own.2) | copy-start | bytes 3145732
  28.1 9.8 %collective-permute-start.5 = (bf16[1280,128]{1,0:T(8,128)(2,1)S(1)}, bf16[1280,128]{1,0:T(8,128)(2,1)S(1)}, u32[]{:S(2)}, u32[]{:S(2)}) collective-permute-start(bf16[1280,128]{1,0:T(8,128)(2,1)S(1)} %get-tuple-element.37), channel_id=1, source_target_pairs={{0,13},{1,4},{2,15},{3,6},{4,1},{5,8},{6,3},{7,10},{8,5},{9,12},{1... | collective-permute-start | bytes 983048 | tf_op jit(solution)/shard_map/ppermute | solution.py:459
  28.2 9.7 %collective-permute-start.6 = (bf16[1280,128]{1,0:T(8,128)(2,1)S(1)}, bf16[1280,128]{1,0:T(8,128)(2,1)S(1)}, u32[]{:S(2)}, u32[]{:S(2)}) collective-permute-start(bf16[1280,128]{1,0:T(8,128)(2,1)S(1)} %get-tuple-element.38), channel_id=1, source_target_pairs={{0,1},{1,0},{2,3},{3,2},{4,5},{5,4},{6,7},{7,6},{8,9},{9,8},{10,11... | collective-permute-start | bytes 983048 | tf_op jit(solution)/shard_map/ppermute | solution.py:459
  31.9 7.4 %collective-permute-start.8 = (bf16[1280,128]{1,0:T(8,128)(2,1)}, bf16[1280,128]{1,0:T(8,128)(2,1)S(1)}, u32[]{:S(2)}, u32[]{:S(2)}) collective-permute-start(bf16[1280,128]{1,0:T(8,128)(2,1)} %get-tuple-element.45), channel_id=1, source_target_pairs={{0,15},{3,4},{4,3},{7,8},{8,7},{11,12},{12,11},{15,0},{16,31},{19,... | collective-permute-start | bytes 983048 | tf_op jit(solution)/shard_map/ppermute | solution.py:459
  32.6 18.0 %collective-permute-start.9 = (bf16[2048,128]{1,0:T(8,128)(2,1)}, bf16[2048,128]{1,0:T(8,128)(2,1)S(1)}, u32[]{:S(2)}, u32[]{:S(2)}) collective-permute-start(bf16[2048,128]{1,0:T(8,128)(2,1)} %get-tuple-element.47), channel_id=1, source_target_pairs={{0,15},{1,2},{2,1},{3,4},{4,3},{5,6},{6,5},{7,8},{8,7},{9,10},{10,... | collective-permute-start | bytes 1572872 | tf_op jit(solution)/shard_map/ppermute | solution.py:459
  37.9 1.4 %copy-start.3 = (bf16[2048,128]{1,0:T(8,128)(2,1)S(1)}, bf16[2048,128]{1,0:T(8,128)(2,1)}, u32[]{:S(2)}) copy-start(bf16[2048,128]{1,0:T(8,128)(2,1)} %copy-done.2) | copy-start | bytes 1572868
  37.9 1.4 %copy-start.5 = (bf16[1280,128]{1,0:T(8,128)(2,1)S(1)}, bf16[1280,128]{1,0:T(8,128)(2,1)}, u32[]{:S(2)}) copy-start(bf16[1280,128]{1,0:T(8,128)(2,1)} %copy-done.4) | copy-start | bytes 983044
  43.1 23.3 %collective-permute-start.13 = (bf16[512,512]{1,0:T(8,128)(2,1)S(1)}, bf16[512,512]{1,0:T(8,128)(2,1)S(1)}, u32[]{:S(2)}, u32[]{:S(2)}) collective-permute-start(bf16[512,512]{1,0:T(8,128)(2,1)S(1)} %get-tuple-element.46.own), channel_id=1, source_target_pairs={{0,15},{1,2},{2,1},{3,4},{4,3},{5,6},{6,5},{7,8},{8,7},{9,10},{10,... | collective-permute-start | bytes 1572872 | tf_op jit(solution)/shard_map/ppermute | solution.py:459
  46.7 19.7 %collective-permute-start.12 = (bf16[512,512]{1,0:T(8,128)(2,1)S(1)}, bf16[512,512]{1,0:T(8,128)(2,1)S(1)}, u32[]{:S(2)}, u32[]{:S(2)}) collective-permute-start(bf16[512,512]{1,0:T(8,128)(2,1)S(1)} %get-tuple-element.46.own), channel_id=1, source_target_pairs={{0,1},{1,0},{2,3},{3,2},{4,5},{5,4},{6,7},{7,6},{8,9},{9,8},{10,11... | collective-permute-start | bytes 1572872 | tf_op jit(solution)/shard_map/ppermute | solution.py:459
  51.9 20.5 %collective-permute-start.10 = (bf16[1280,128]{1,0:T(8,128)(2,1)S(1)}, bf16[1280,128]{1,0:T(8,128)(2,1)S(1)}, u32[]{:S(2)}, u32[]{:S(2)}) collective-permute-start(bf16[1280,128]{1,0:T(8,128)(2,1)S(1)} %get-tuple-element.50), channel_id=1, source_target_pairs={{0,15},{1,2},{2,1},{3,4},{4,3},{5,6},{6,5},{7,8},{8,7},{9,10},{10,... | collective-permute-start | bytes 983048 | tf_op jit(solution)/shard_map/ppermute | solution.py:459
  52.0 20.4 %collective-permute-start.11 = (bf16[1280,128]{1,0:T(8,128)(2,1)S(1)}, bf16[1280,128]{1,0:T(8,128)(2,1)S(1)}, u32[]{:S(2)}, u32[]{:S(2)}) collective-permute-start(bf16[1280,128]{1,0:T(8,128)(2,1)S(1)} %get-tuple-element.51), channel_id=1, source_target_pairs={{0,1},{1,0},{2,3},{3,2},{4,5},{5,4},{6,7},{7,6},{8,9},{9,8},{10,11... | collective-permute-start | bytes 983048 | tf_op jit(solution)/shard_map/ppermute | solution.py:459
  67.9 8.3 %collective-permute-start.16 = (bf16[1280,128]{1,0:T(8,128)(2,1)S(1)}, bf16[1280,128]{1,0:T(8,128)(2,1)S(1)}, u32[]{:S(2)}, u32[]{:S(2)}) collective-permute-start(bf16[1280,128]{1,0:T(8,128)(2,1)S(1)} %get-tuple-element.60), channel_id=1, source_target_pairs={{0,15},{1,2},{2,1},{3,4},{4,3},{5,6},{6,5},{7,8},{8,7},{9,10},{10,... | collective-permute-start | bytes 983048 | tf_op jit(solution)/shard_map/ppermute | solution.py:459
  70.4 5.7 %collective-permute-start.17 = (bf16[1280,128]{1,0:T(8,128)(2,1)S(1)}, bf16[1280,128]{1,0:T(8,128)(2,1)S(1)}, u32[]{:S(2)}, u32[]{:S(2)}) collective-permute-start(bf16[1280,128]{1,0:T(8,128)(2,1)S(1)} %get-tuple-element.61), channel_id=1, source_target_pairs={{0,1},{1,0},{2,3},{3,2},{4,5},{5,4},{6,7},{7,6},{8,9},{9,8},{10,11... | collective-permute-start | bytes 983048 | tf_op jit(solution)/shard_map/ppermute | solution.py:459
  74.6 10.1 %collective-permute-start.14 = (bf16[1280,128]{1,0:T(8,128)(2,1)S(1)}, bf16[1280,128]{1,0:T(8,128)(2,1)S(1)}, u32[]{:S(2)}, u32[]{:S(2)}) collective-permute-start(bf16[1280,128]{1,0:T(8,128)(2,1)S(1)} %get-tuple-element.58), channel_id=1, source_target_pairs={{0,15},{1,2},{2,1},{3,4},{4,3},{5,6},{6,5},{7,8},{8,7},{9,10},{10,... | collective-permute-start | bytes 983048 | tf_op jit(solution)/shard_map/ppermute | solution.py:459
  74.6 10.0 %collective-permute-start.15 = (bf16[1280,128]{1,0:T(8,128)(2,1)S(1)}, bf16[1280,128]{1,0:T(8,128)(2,1)S(1)}, u32[]{:S(2)}, u32[]{:S(2)}) collective-permute-start(bf16[1280,128]{1,0:T(8,128)(2,1)S(1)} %get-tuple-element.59), channel_id=1, source_target_pairs={{0,1},{1,0},{2,3},{3,2},{4,5},{5,4},{6,7},{7,6},{8,9},{9,8},{10,11... | collective-permute-start | bytes 983048 | tf_op jit(solution)/shard_map/ppermute | solution.py:459

commit v14 on v11

--- a/solution.py
+++ b/solution.py
@@ -406,9 +406,9 @@
             out[at(f, row - p, row - p + 1, col - p, col - p + 1)] = total.astype(out.dtype)
 
 
-def rows_kernel(f, first, drop_ref, own, cross, mate, out):
+def slots_kernel(f, first, drop_ref, own, mate, out):
     h = f.h
-    below, above = sides(f, drop_ref, indexed(f, mate), indexed(f, cross))
+    mate_block = indexed(f, mate)
     over_index = {place: i for i, place in enumerate(over(h))}
     under_index = {place: i for i, place in enumerate(under(h))}
     for r in range(h):
@@ -417,13 +417,51 @@
         def at_offset(offset, r=r):
             col = r + offset
             if col < h:
-                return below(over_index[r, col])
+                return mate_block(over_index[r, col])
             if col < 2 * h:
                 return own[block(f, first + r, col - h)]
-            return above(under_index[r, col - 2 * h])
+            return mate_block(under_index[r, col - 2 * h])
 
         for s in range(f.k):
             out[r, s] = jnp.where(dropped <= s, at_offset(s + 1), at_offset(s))
+
+
+def last_slots_kernel(f, drop_ref, slots, cross, out, sides_ref, sems):
+    h, k = f.h, f.k
+    odd = odd_place(f, drop_ref)
+    cross_block = indexed(f, cross)
+    over_index = {place: i for i, place in enumerate(over(h))}
+    under_index = {place: i for i, place in enumerate(under(h))}
+    copies = []
+
+    def copy(source, r, lo, hi):
+        there = pltpu.make_async_copy(
+            source.at[r, pl.ds(lo, hi - lo)], out.at[r, pl.ds(lo, hi - lo)], sems.at[len(copies)]
+        )
+        there.start()
+        copies.append(there)
+
+    for r in range(h):
+        copy(slots, r, h - r, k - 1 - r)
+    for r in range(h):
+        dropped = drop_ref[h + r]
+        for lo, hi, mine in ((0, h - r, jnp.logical_not(odd)), (k - 1 - r, k, odd)):
+            for s in range(lo, hi):
+                here = slots[r, s]
+
+                def at_offset(offset, r=r, low=lo == 0, here=here):
+                    col = r + offset
+                    if low and col < h:
+                        return cross_block(over_index[r, col])
+                    if not low and col >= 2 * h:
+                        return cross_block(under_index[r, col - 2 * h])
+                    return here
+
+                value = jnp.where(dropped <= s, at_offset(s + 1), at_offset(s))
+                sides_ref[r, s] = jnp.where(mine, value, here)
+            copy(sides_ref, r, lo, hi)
+    for there in copies:
+        there.wait()
 
 
 VMEM = pl.BlockSpec(memory_space=pltpu.VMEM)
@@ -431,7 +469,7 @@
 ANY = pl.BlockSpec(memory_space=pl.ANY)
 
 
-def call(kernel, outs, scratch, flops, limit, drop, *args, passed=(), light=False):
+def call(kernel, outs, scratch, flops, limit, drop, *args, passed=(), light=False, off=False):
     moved = sum(a.size * a.dtype.itemsize for a in args) + sum(s.size * s.dtype.itemsize for s in outs)
     if light:
         flops = moved = 0
@@ -440,7 +478,7 @@
         kernel,
         out_shape=[*outs, *[jax.ShapeDtypeStruct(a.shape, a.dtype) for a in passed]],
         in_specs=[SMEM] + [VMEM] * n + [ANY] * len(passed),
-        out_specs=[VMEM] * len(outs) + [ANY] * len(passed),
+        out_specs=[ANY if off else VMEM] * len(outs) + [ANY] * len(passed),
         scratch_shapes=scratch,
         input_output_aliases={1 + n + i: len(outs) + i for i in range(len(passed))},
         compiler_params=pltpu.CompilerParams(vmem_limit_bytes=limit * MIB),
@@ -566,7 +604,11 @@
     out = jax.ShapeDtypeStruct(density.shape, kind)
 
     def assembled(own, first, cross, mate):
-        return call(functools.partial(rows_kernel, f, first), [out], [], 0, 8, drop, own, cross, mate)[0]
+        (slots,) = call(functools.partial(slots_kernel, f, first), [out], [], 0, 8, drop, own, mate)
+        scratch = [pltpu.VMEM(out.shape, kind), pltpu.SemaphoreType.DMA((3 * half,))]
+        return call(
+            functools.partial(last_slots_kernel, f), [out], scratch, 0, 8, drop, slots, cross, off=True
+        )[0]
 
     inverse_next = assembled(whole, half, inverse_cross, inverse_mate)
     density_next = assembled(density_own, 0, rim_cross, rim_mate)

time: 85.7 us -> 85.3 us (level)
  waiting for transfers between devices: 30.8 us -> 29.4 us
  Pallas kernels: 24.2 us -> 25.4 us
    ppermute x18, waiting for transfers between devices: 30.8 us -> 29.4 us  [routed(): lax.ppermute(x, RING, [(i, (i + step(i)) % size) for i in range(size) if...]
    pallas_call x12 -> x14, Pallas kernels: 24.2 us -> 25.4 us  [call(): pl.pallas_call(kernel, out_shape=[*outs, *[jax.ShapeDtypeStruct(a.shape,...]
  transfers between devices with their start and end apart: 18 -> 18, of which waited for: 3 -> 5; matrix products, arithmetic and copies ran while one was open for 1% -> 1% of each run, Pallas kernels for 25% -> 27%
where the time goes in v14:
time: 85.3 us; the launch traced here: 85.1 us
  waiting for transfers between devices  29.4 us (34%)
  starting transfers between devices  26.4 us (31%)
  Pallas kernels  25.4 us (30%)
  local copies, waits for them, and re-layouts  2.04 us (2%)
  other arithmetic  1.04 us (1%)
    ppermute x18, waiting for transfers between devices, routed(): lax.ppermute(x, RING, [(i, (i + step(i)) % size) for i in range(size) if...  29.4 us
    ppermute x18, starting transfers between devices, routed(): lax.ppermute(x, RING, [(i, (i + step(i)) % size) for i in range(size) if...  26.4 us
    pallas_call x14, Pallas kernels, call(): pl.pallas_call(kernel, out_shape=[*outs, *[jax.ShapeDtypeStruct(a.shape,...  25.4 us
    unnamed x8, local copies, waits for them, and re-layouts  2.04 us
  transfers between devices with their start and end apart: 18, of which 5 were waited for; matrix products, arithmetic and copies ran while one was open for 1% of the time, Pallas kernels for 27%

profile of v14, /device:TPU:1, one launch (start us, length us, event | category | flops | bytes accessed | tf_op | source)
XLA Modules:
  0.0 85.1 jit_solution(2600349334104769609)
XLA Ops:
  0.6 2.7 %collective-permute-start.2 = (bf16[4,8,128,128]{3,2,1,0:T(8,128)(2,1)}, bf16[4,8,128,128]{3,2,1,0:T(8,128)(2,1)S(1)}, u32[]{:S(2)}, u32[]{:S(2)}) collective-permute-start(bf16[4,8,128,128]{3,2,1,0:T(8,128)(2,1)} %own.2), channel_id=1, source_target_pairs={{0,15},{1,2},{2,1},{3,4},{4,3},{5,6},{6,5},{7,8},{8,7},{9,10},{10,... | collective-permute-start | bytes 3145736 | tf_op jit(solution)/shard_map/ppermute | solution.py:491
  3.3 2.9 %collective-permute-start.3 = (bf16[4,8,128,128]{3,2,1,0:T(8,128)(2,1)}, bf16[4,8,128,128]{3,2,1,0:T(8,128)(2,1)S(1)}, u32[]{:S(2)}, u32[]{:S(2)}) collective-permute-start(bf16[4,8,128,128]{3,2,1,0:T(8,128)(2,1)} %own.2), channel_id=1, source_target_pairs={{0,1},{1,0},{2,3},{3,2},{4,5},{5,4},{6,7},{7,6},{8,9},{9,8},{10,11... | collective-permute-start | bytes 3145736 | tf_op jit(solution)/shard_map/ppermute | solution.py:491
  8.4 2.1 %shard_map.51 = (bf16[2048,128]{1,0:T(8,128)(2,1)S(1)}, bf16[2048,128]{1,0:T(8,128)(2,1)}, bf16[3328,128]{1,0:T(8,128)(2,1)}, bf16[1280,128]{1,0:T(8,128)(2,1)S(1)}) custom-call(s32[5]{0:T(128)S(1)} %pad_add_fusion.1.drop_ref, bf16[4,8,128,128]{3,2,1,0:T(8,128)(2,1)S(1)} %copy-done), custom_call_target="tpu_custom_call" | custom-call | bytes 3276800 | tf_op jit(solution)/shard_map/pallas_call | solution.py:477
  12.0 15.3 %collective-permute-done = s32[4]{0:T(128)S(1)} collective-permute-done((s32[4]{0:T(128)S(1)}, s32[4]{0:T(128)S(1)}, u32[]{:S(2)}, u32[]{:S(2)}) %collective-permute-start) | collective-permute-done | bytes 48 | tf_op jit(solution)/shard_map/ppermute | solution.py:491
  28.2 1.8 %collective-permute-start.8 = (bf16[1280,128]{1,0:T(8,128)(2,1)S(1)}, bf16[1280,128]{1,0:T(8,128)(2,1)S(1)}, u32[]{:S(2)}, u32[]{:S(2)}) collective-permute-start(bf16[1280,128]{1,0:T(8,128)(2,1)S(1)} %get-tuple-element.45.sent_cross), channel_id=1, source_target_pairs={{0,15},{1,2},{2,1},{3,4},{4,3},{5,6},{6,5},{7,8},{8,7},{9,10},{10,... | collective-permute-start | bytes 983048 | tf_op jit(solution)/shard_map/ppermute | solution.py:491
  30.1 6.3 %collective-permute-start.6 = (bf16[640,128]{1,0:T(8,128)(2,1)S(1)}, bf16[640,128]{1,0:T(8,128)(2,1)S(1)}, u32[]{:S(2)}, u32[]{:S(2)}) collective-permute-start(bf16[640,128]{1,0:T(8,128)(2,1)S(1)} %get-tuple-element.38), channel_id=1, source_target_pairs={{0,1},{1,0},{2,3},{3,2},{4,5},{5,4},{6,7},{7,6},{8,9},{9,8},{10,11... | collective-permute-start | bytes 491528 | tf_op jit(solution)/shard_map/ppermute | solution.py:491
  36.4 4.3 %shard_map.50 = (bf16[1536,1280]{1,0:T(8,128)(2,1)S(1)}, bf16[1536,1280]{1,0:T(8,128)(2,1)S(1)}, bf16[1024,512]{1,0:T(8,128)(2,1)S(1)}, bf16[1024,512]{1,0:T(8,128)(2,1)S(1)}, f32[1024,512]{1,0:T(8,128)S(1)}) custom-call(s32[13]{0:T(128)S(1)} %pad_add_fusion.drop_ref, bf16[4,8,128,128]{3,2,1,0:T(8,128)(2,1)S(1)} %copy-done.3, ...), custom_call_target="tpu_custom_call" | custom-call | flops 2818572288 | bytes 15204352 | tf_op jit(solution)/shard_map/pallas_call | solution.py:477
  40.7 1.4 %shard_map.53 = (bf16[1024,512]{1,0:T(8,128)(2,1)S(1)}, bf16[1024,512]{1,0:T(8,128)(2,1)S(1)}) custom-call(s32[13]{0:T(128)S(1)} %pad_add_fusion.drop_ref, bf16[1280,128]{1,0:T(8,128)(2,1)S(1)} %collective-permute-done.5.far_far, bf16[640,128]{1,0:T(8,128)(2,1)S(1)} %collective-permute-done.6.far_mate, ...), custom_call_target="tpu_custom_call" | custom-call | tf_op jit(solution)/shard_map/pallas_call | solution.py:477
  42.1 3.8 %shard_map.54 = (bf16[1536,512]{1,0:T(8,128)(2,1)S(1)}, bf16[512,512]{1,0:T(8,128)(2,1)S(1)}, f32[1024,512]{1,0:T(8,128)S(1)}) custom-call(s32[13]{0:T(128)S(1)} %pad_add_fusion.drop_ref, bf16[1536,1280]{1,0:T(8,128)(2,1)S(1)} %get-tuple-element.33.shifted, bf16[1024,512]{1,0:T(8,128)(2,1)S(1)} %get-tuple-element.43.corners, ...), custom_call_target="tpu_custom_call" | custom-call | tf_op jit(solution)/shard_map/pallas_call | solution.py:477
  46.8 2.2 %collective-permute-start.13 = (bf16[512,512]{1,0:T(8,128)(2,1)S(1)}, bf16[512,512]{1,0:T(8,128)(2,1)S(1)}, u32[]{:S(2)}, u32[]{:S(2)}) collective-permute-start(bf16[512,512]{1,0:T(8,128)(2,1)S(1)} %get-tuple-element.46.own), channel_id=1, source_target_pairs={{0,1},{1,0},{2,3},{3,2},{4,5},{5,4},{6,7},{7,6},{8,9},{9,8},{10,11... | collective-permute-start | bytes 1572872 | tf_op jit(solution)/shard_map/ppermute | solution.py:491
  49.0 1.3 %shard_map.55 = (bf16[512,512]{1,0:T(8,128)(2,1)S(1)}, bf16[512,512]{1,0:T(8,128)(2,1)S(1)}, bf16[1280,128]{1,0:T(8,128)(2,1)S(1)}, bf16[1280,128]{1,0:T(8,128)(2,1)S(1)}) custom-call(s32[13]{0:T(128)S(1)} %pad_add_fusion.drop_ref, bf16[3328,128]{1,0:T(8,128)(2,1)S(1)} %collective-permute-done.4.refs_1_.mate, ...), custom_call_target="tpu_custom_call" | custom-call | flops 335544320 | bytes 6750208 | tf_op jit(solution)/shard_map/pallas_call | solution.py:477
  50.4 2.3 %collective-permute-start.10 = (bf16[1280,128]{1,0:T(8,128)(2,1)S(1)}, bf16[1280,128]{1,0:T(8,128)(2,1)S(1)}, u32[]{:S(2)}, u32[]{:S(2)}) collective-permute-start(bf16[1280,128]{1,0:T(8,128)(2,1)S(1)} %get-tuple-element.50), channel_id=1, source_target_pairs={{0,15},{1,2},{2,1},{3,4},{4,3},{5,6},{6,5},{7,8},{8,7},{9,10},{10,... | collective-permute-start | bytes 983048 | tf_op jit(solution)/shard_map/ppermute | solution.py:491
  52.7 2.1 %collective-permute-start.11 = (bf16[1280,128]{1,0:T(8,128)(2,1)S(1)}, bf16[1280,128]{1,0:T(8,128)(2,1)S(1)}, u32[]{:S(2)}, u32[]{:S(2)}) collective-permute-start(bf16[1280,128]{1,0:T(8,128)(2,1)S(1)} %get-tuple-element.51), channel_id=1, source_target_pairs={{0,1},{1,0},{2,3},{3,2},{4,5},{5,4},{6,7},{7,6},{8,9},{9,8},{10,11... | collective-permute-start | bytes 983048 | tf_op jit(solution)/shard_map/ppermute | solution.py:491
  54.8 2.0 %shard_map.56.correction = bf16[1536,512]{1,0:T(8,128)(2,1)S(1)} custom-call(s32[13]{0:T(128)S(1)} %pad_add_fusion.drop_ref, bf16[1536,1280]{1,0:T(8,128)(2,1)S(1)} %get-tuple-element.33.shifted, bf16[1024,512]{1,0:T(8,128)(2,1)S(1)} %get-tuple-element.43.corners, bf16[512,512]{1,0:T(8,128)(2,1)S(1)} %get-tuple-element.52.low, ...), custom_call_target="tpu_custom_call" | custom-call | flops 1275068416 | bytes 8126464 | tf_op jit(solution)/shard_map/pallas_call | solution.py:477
  56.8 8.0 %collective-permute-done.12.cross = bf16[512,512]{1,0:T(8,128)(2,1)S(1)} collective-permute-done((bf16[512,512]{1,0:T(8,128)(2,1)S(1)}, bf16[512,512]{1,0:T(8,128)(2,1)S(1)}, u32[]{:S(2)}, u32[]{:S(2)}) %collective-permute-start.12) | collective-permute-done | bytes 524320 | tf_op jit(solution)/shard_map/ppermute | solution.py:491
  64.8 1.5 %shard_map.57 = (bf16[512,512]{1,0:T(8,128)(2,1)S(1)}, bf16[512,512]{1,0:T(8,128)(2,1)S(1)}, bf16[1280,128]{1,0:T(8,128)(2,1)S(1)}, bf16[1280,128]{1,0:T(8,128)(2,1)S(1)}) custom-call(s32[13]{0:T(128)S(1)} %pad_add_fusion.drop_ref, bf16[512,512]{1,0:T(8,128)(2,1)S(1)} %collective-permute-done.12.cross, bf16[512,512]{1,0:T(8,128)(2,1)S(1)} %collective-permute-done.13.mate, ...), custom_call_target="tpu_custom_call" | custom-call | flops 671088640 | bytes 5373952 | tf_op jit(solution)/shard_map/pallas_call | solution.py:477
  66.3 1.3 %collective-permute-start.17 = (bf16[1280,128]{1,0:T(8,128)(2,1)S(1)}, bf16[1280,128]{1,0:T(8,128)(2,1)S(1)}, u32[]{:S(2)}, u32[]{:S(2)}) collective-permute-start(bf16[1280,128]{1,0:T(8,128)(2,1)S(1)} %get-tuple-element.61), channel_id=1, source_target_pairs={{0,15},{1,2},{2,1},{3,4},{4,3},{5,6},{6,5},{7,8},{8,7},{9,10},{10,... | collective-permute-start | bytes 983048 | tf_op jit(solution)/shard_map/ppermute | solution.py:491
  68.3 2.3 %shard_map.58 = (bf16[1536,512]{1,0:T(8,128)(2,1)S(1)}, bf16[1280,128]{1,0:T(8,128)(2,1)S(1)}, bf16[1280,128]{1,0:T(8,128)(2,1)S(1)}) custom-call(s32[13]{0:T(128)S(1)} %pad_add_fusion.drop_ref, bf16[512,512]{1,0:T(8,128)(2,1)S(1)} %get-tuple-element.46.own, bf16[1280,128]{1,0:T(8,128)(2,1)S(1)} %collective-permute-done.10.cross, ...), custom_call_target="tpu_custom_call" | custom-call | flops 1275068416 | bytes 11010048 | tf_op jit(solution)/shard_map/pallas_call | solution.py:477
  70.5 2.9 %collective-permute-start.14 = (bf16[1280,128]{1,0:T(8,128)(2,1)S(1)}, bf16[1280,128]{1,0:T(8,128)(2,1)S(1)}, u32[]{:S(2)}, u32[]{:S(2)}) collective-permute-start(bf16[1280,128]{1,0:T(8,128)(2,1)S(1)} %get-tuple-element.58), channel_id=1, source_target_pairs={{0,1},{1,0},{2,3},{3,2},{4,5},{5,4},{6,7},{7,6},{8,9},{9,8},{10,11... | collective-permute-start | bytes 983048 | tf_op jit(solution)/shard_map/ppermute | solution.py:491
  73.5 1.3 %shard_map.59.own = bf16[512,512]{1,0:T(8,128)(2,1)S(1)} custom-call(s32[13]{0:T(128)S(1)} %pad_add_fusion.drop_ref, bf16[1536,1280]{1,0:T(8,128)(2,1)S(1)} %get-tuple-element.32.square, bf16[1536,512]{1,0:T(8,128)(2,1)S(1)} %get-tuple-element.57.whole.own), custom_call_target="tpu_custom_call" | custom-call | flops 603979776 | bytes 6029312 | tf_op jit(solution)/shard_map/pallas_call | solution.py:477
  75.5 3.1 %collective-permute-done.17.cross = bf16[1280,128]{1,0:T(8,128)(2,1)S(1)} collective-permute-done((bf16[1280,128]{1,0:T(8,128)(2,1)S(1)}, bf16[1280,128]{1,0:T(8,128)(2,1)S(1)}, u32[]{:S(2)}, u32[]{:S(2)}) %collective-permute-start.17) | collective-permute-done | bytes 327712 | tf_op jit(solution)/shard_map/ppermute | solution.py:491
  78.7 1.6 %shard_map.63 = bf16[4,8,128,128]{3,2,1,0:T(8,128)(2,1)} custom-call(s32[13]{0:T(128)S(1)} %pad_add_fusion.drop_ref, bf16[4,8,128,128]{3,2,1,0:T(8,128)(2,1)S(1)} %shard_map.62.slots, bf16[1280,128]{1,0:T(8,128)(2,1)S(1)} %collective-permute-done.17.cross), custom_call_target="tpu_custom_call" | custom-call | bytes 2424832 | tf_op jit(solution)/shard_map/pallas_call | solution.py:477
  81.1 2.4 %collective-permute-done.15.cross = bf16[1280,128]{1,0:T(8,128)(2,1)S(1)} collective-permute-done((bf16[1280,128]{1,0:T(8,128)(2,1)S(1)}, bf16[1280,128]{1,0:T(8,128)(2,1)S(1)}, u32[]{:S(2)}, u32[]{:S(2)}) %collective-permute-start.15) | collective-permute-done | bytes 327712 | tf_op jit(solution)/shard_map/ppermute | solution.py:491
  83.5 1.6 %shard_map.61 = bf16[4,8,128,128]{3,2,1,0:T(8,128)(2,1)} custom-call(s32[13]{0:T(128)S(1)} %pad_add_fusion.drop_ref, bf16[4,8,128,128]{3,2,1,0:T(8,128)(2,1)S(1)} %shard_map.60.slots, bf16[1280,128]{1,0:T(8,128)(2,1)S(1)} %collective-permute-done.15.cross), custom_call_target="tpu_custom_call" | custom-call | bytes 2424832 | tf_op jit(solution)/shard_map/pallas_call | solution.py:477
  (40 shorter events, 7.8 us)
Async XLA Ops:
  0.6 26.8 %collective-permute-start.2 = (bf16[4,8,128,128]{3,2,1,0:T(8,128)(2,1)}, bf16[4,8,128,128]{3,2,1,0:T(8,128)(2,1)S(1)}, u32[]{:S(2)}, u32[]{:S(2)}) collective-permute-start(bf16[4,8,128,128]{3,2,1,0:T(8,128)(2,1)} %own.2), channel_id=1, source_target_pairs={{0,15},{1,2},{2,1},{3,4},{4,3},{5,6},{6,5},{7,8},{8,7},{9,10},{10,... | collective-permute-start | bytes 3145736 | tf_op jit(solution)/shard_map/ppermute | solution.py:491
  3.3 24.1 %collective-permute-start.3 = (bf16[4,8,128,128]{3,2,1,0:T(8,128)(2,1)}, bf16[4,8,128,128]{3,2,1,0:T(8,128)(2,1)S(1)}, u32[]{:S(2)}, u32[]{:S(2)}) collective-permute-start(bf16[4,8,128,128]{3,2,1,0:T(8,128)(2,1)} %own.2), channel_id=1, source_target_pairs={{0,1},{1,0},{2,3},{3,2},{4,5},{5,4},{6,7},{7,6},{8,9},{9,8},{10,11... | collective-permute-start | bytes 3145736 | tf_op jit(solution)/shard_map/ppermute | solution.py:491
  7.1 1.2 %copy-start = (bf16[4,8,128,128]{3,2,1,0:T(8,128)(2,1)S(1)}, bf16[4,8,128,128]{3,2,1,0:T(8,128)(2,1)}, u32[]{:S(2)}) copy-start(bf16[4,8,128,128]{3,2,1,0:T(8,128)(2,1)} %own.3) | copy-start | bytes 3145732
  10.4 0.8 copy-start.1
  11.2 16.2 %collective-permute-start.4 = (bf16[3328,128]{1,0:T(8,128)(2,1)}, bf16[3328,128]{1,0:T(8,128)(2,1)S(1)}, u32[]{:S(2)}, u32[]{:S(2)}) collective-permute-start(bf16[3328,128]{1,0:T(8,128)(2,1)} %get-tuple-element.34.sent_mate), channel_id=1, source_target_pairs={{0,1},{1,0},{2,3},{3,2},{4,5},{5,4},{6,7},{7,6},{8,9},{9,8},{10,11... | collective-permute-start | bytes 2555912 | tf_op jit(solution)/shard_map/ppermute | solution.py:491
  11.2 16.1 %collective-permute-start = (s32[4]{0:T(128)S(1)}, s32[4]{0:T(128)S(1)}, u32[]{:S(2)}, u32[]{:S(2)}) collective-permute-start(s32[4]{0:T(128)S(1)} %broadcast_subtract_fusion), channel_id=1, source_target_pairs={{0,15},{1,2},{2,1},{3,4},{4,3},{5,6},{6,5},{7,8},{8,7},{9,10},{10,... | collective-permute-start | bytes 56 | tf_op jit(solution)/shard_map/ppermute | solution.py:491
  11.2 16.1 %collective-permute-start.1 = (s32[4]{0:T(128)S(1)}, s32[4]{0:T(128)S(1)}, u32[]{:S(2)}, u32[]{:S(2)}) collective-permute-start(s32[4]{0:T(128)S(1)} %broadcast_subtract_fusion), channel_id=1, source_target_pairs={{0,1},{1,0},{2,3},{3,2},{4,5},{5,4},{6,7},{7,6},{8,9},{9,8},{10,11... | collective-permute-start | bytes 56 | tf_op jit(solution)/shard_map/ppermute | solution.py:491
  12.0 24.4 %copy-start.3 = (bf16[4,8,128,128]{3,2,1,0:T(8,128)(2,1)S(1)}, bf16[4,8,128,128]{3,2,1,0:T(8,128)(2,1)}, u32[]{:S(2)}) copy-start(bf16[4,8,128,128]{3,2,1,0:T(8,128)(2,1)} %own.2) | copy-start | bytes 3145732
  28.1 12.5 %collective-permute-start.5 = (bf16[1280,128]{1,0:T(8,128)(2,1)S(1)}, bf16[1280,128]{1,0:T(8,128)(2,1)S(1)}, u32[]{:S(2)}, u32[]{:S(2)}) collective-permute-start(bf16[1280,128]{1,0:T(8,128)(2,1)S(1)} %get-tuple-element.37), channel_id=1, source_target_pairs={{0,13},{1,4},{2,15},{3,6},{4,1},{5,8},{6,3},{7,10},{8,5},{9,12},{1... | collective-permute-start | bytes 983048 | tf_op jit(solution)/shard_map/ppermute | solution.py:491
  28.2 13.9 %collective-permute-start.8 = (bf16[1280,128]{1,0:T(8,128)(2,1)S(1)}, bf16[1280,128]{1,0:T(8,128)(2,1)S(1)}, u32[]{:S(2)}, u32[]{:S(2)}) collective-permute-start(bf16[1280,128]{1,0:T(8,128)(2,1)S(1)} %get-tuple-element.45.sent_cross), channel_id=1, source_target_pairs={{0,15},{1,2},{2,1},{3,4},{4,3},{5,6},{6,5},{7,8},{8,7},{9,10},{10,... | collective-permute-start | bytes 983048 | tf_op jit(solution)/shard_map/ppermute | solution.py:491
  30.0 19.0 %collective-permute-start.9 = (bf16[2048,128]{1,0:T(8,128)(2,1)}, bf16[2048,128]{1,0:T(8,128)(2,1)S(1)}, u32[]{:S(2)}, u32[]{:S(2)}) collective-permute-start(bf16[2048,128]{1,0:T(8,128)(2,1)} %get-tuple-element.47), channel_id=1, source_target_pairs={{0,15},{1,2},{2,1},{3,4},{4,3},{5,6},{6,5},{7,8},{8,7},{9,10},{10,... | collective-permute-start | bytes 1572872 | tf_op jit(solution)/shard_map/ppermute | solution.py:491
  30.1 10.5 %collective-permute-start.6 = (bf16[640,128]{1,0:T(8,128)(2,1)S(1)}, bf16[640,128]{1,0:T(8,128)(2,1)S(1)}, u32[]{:S(2)}, u32[]{:S(2)}) collective-permute-start(bf16[640,128]{1,0:T(8,128)(2,1)S(1)} %get-tuple-element.38), channel_id=1, source_target_pairs={{0,1},{1,0},{2,3},{3,2},{4,5},{5,4},{6,7},{7,6},{8,9},{9,8},{10,11... | collective-permute-start | bytes 491528 | tf_op jit(solution)/shard_map/ppermute | solution.py:491
  36.4 4.3 %collective-permute-start.7 = (bf16[640,128]{1,0:T(8,128)(2,1)S(1)}, bf16[640,128]{1,0:T(8,128)(2,1)S(1)}, u32[]{:S(2)}, u32[]{:S(2)}) collective-permute-start(bf16[640,128]{1,0:T(8,128)(2,1)S(1)} %get-tuple-element.39), channel_id=1, source_target_pairs={{0,1},{1,0},{2,3},{3,2},{4,5},{5,4},{6,7},{7,6},{8,9},{9,8},{10,11... | collective-permute-start | bytes 491528 | tf_op jit(solution)/shard_map/ppermute | solution.py:491
  40.7 1.5 %copy-start.2 = (bf16[2048,128]{1,0:T(8,128)(2,1)S(1)}, bf16[2048,128]{1,0:T(8,128)(2,1)}, u32[]{:S(2)}) copy-start(bf16[2048,128]{1,0:T(8,128)(2,1)} %copy-done.1) | copy-start | bytes 1572868
  45.9 18.8 %collective-permute-start.12 = (bf16[512,512]{1,0:T(8,128)(2,1)S(1)}, bf16[512,512]{1,0:T(8,128)(2,1)S(1)}, u32[]{:S(2)}, u32[]{:S(2)}) collective-permute-start(bf16[512,512]{1,0:T(8,128)(2,1)S(1)} %get-tuple-element.46.own), channel_id=1, source_target_pairs={{0,15},{1,2},{2,1},{3,4},{4,3},{5,6},{6,5},{7,8},{8,7},{9,10},{10,... | collective-permute-start | bytes 1572872 | tf_op jit(solution)/shard_map/ppermute | solution.py:491
  46.8 18.0 %collective-permute-start.13 = (bf16[512,512]{1,0:T(8,128)(2,1)S(1)}, bf16[512,512]{1,0:T(8,128)(2,1)S(1)}, u32[]{:S(2)}, u32[]{:S(2)}) collective-permute-start(bf16[512,512]{1,0:T(8,128)(2,1)S(1)} %get-tuple-element.46.own), channel_id=1, source_target_pairs={{0,1},{1,0},{2,3},{3,2},{4,5},{5,4},{6,7},{7,6},{8,9},{9,8},{10,11... | collective-permute-start | bytes 1572872 | tf_op jit(solution)/shard_map/ppermute | solution.py:491
  50.4 17.9 %collective-permute-start.10 = (bf16[1280,128]{1,0:T(8,128)(2,1)S(1)}, bf16[1280,128]{1,0:T(8,128)(2,1)S(1)}, u32[]{:S(2)}, u32[]{:S(2)}) collective-permute-start(bf16[1280,128]{1,0:T(8,128)(2,1)S(1)} %get-tuple-element.50), channel_id=1, source_target_pairs={{0,15},{1,2},{2,1},{3,4},{4,3},{5,6},{6,5},{7,8},{8,7},{9,10},{10,... | collective-permute-start | bytes 983048 | tf_op jit(solution)/shard_map/ppermute | solution.py:491
  52.7 15.6 %collective-permute-start.11 = (bf16[1280,128]{1,0:T(8,128)(2,1)S(1)}, bf16[1280,128]{1,0:T(8,128)(2,1)S(1)}, u32[]{:S(2)}, u32[]{:S(2)}) collective-permute-start(bf16[1280,128]{1,0:T(8,128)(2,1)S(1)} %get-tuple-element.51), channel_id=1, source_target_pairs={{0,1},{1,0},{2,3},{3,2},{4,5},{5,4},{6,7},{7,6},{8,9},{9,8},{10,11... | collective-permute-start | bytes 983048 | tf_op jit(solution)/shard_map/ppermute | solution.py:491
  66.3 8.5 %collective-permute-start.16 = (bf16[1280,128]{1,0:T(8,128)(2,1)S(1)}, bf16[1280,128]{1,0:T(8,128)(2,1)S(1)}, u32[]{:S(2)}, u32[]{:S(2)}) collective-permute-start(bf16[1280,128]{1,0:T(8,128)(2,1)S(1)} %get-tuple-element.60), channel_id=1, source_target_pairs={{0,1},{1,0},{2,3},{3,2},{4,5},{5,4},{6,7},{7,6},{8,9},{9,8},{10,11... | collective-permute-start | bytes 983048 | tf_op jit(solution)/shard_map/ppermute | solution.py:491
  66.3 12.4 %collective-permute-start.17 = (bf16[1280,128]{1,0:T(8,128)(2,1)S(1)}, bf16[1280,128]{1,0:T(8,128)(2,1)S(1)}, u32[]{:S(2)}, u32[]{:S(2)}) collective-permute-start(bf16[1280,128]{1,0:T(8,128)(2,1)S(1)} %get-tuple-element.61), channel_id=1, source_target_pairs={{0,15},{1,2},{2,1},{3,4},{4,3},{5,6},{6,5},{7,8},{8,7},{9,10},{10,... | collective-permute-start | bytes 983048 | tf_op jit(solution)/shard_map/ppermute | solution.py:491
  70.5 9.8 %collective-permute-start.14 = (bf16[1280,128]{1,0:T(8,128)(2,1)S(1)}, bf16[1280,128]{1,0:T(8,128)(2,1)S(1)}, u32[]{:S(2)}, u32[]{:S(2)}) collective-permute-start(bf16[1280,128]{1,0:T(8,128)(2,1)S(1)} %get-tuple-element.58), channel_id=1, source_target_pairs={{0,1},{1,0},{2,3},{3,2},{4,5},{5,4},{6,7},{7,6},{8,9},{9,8},{10,11... | collective-permute-start | bytes 983048 | tf_op jit(solution)/shard_map/ppermute | solution.py:491
  73.5 10.0 %collective-permute-start.15 = (bf16[1280,128]{1,0:T(8,128)(2,1)S(1)}, bf16[1280,128]{1,0:T(8,128)(2,1)S(1)}, u32[]{:S(2)}, u32[]{:S(2)}) collective-permute-start(bf16[1280,128]{1,0:T(8,128)(2,1)S(1)} %get-tuple-element.59), channel_id=1, source_target_pairs={{0,15},{1,2},{2,1},{3,4},{4,3},{5,6},{6,5},{7,8},{8,7},{9,10},{10,... | collective-permute-start | bytes 983048 | tf_op jit(solution)/shard_map/ppermute | solution.py:491

commit v15 on v11

--- a/solution.py
+++ b/solution.py
@@ -136,12 +136,13 @@
             dest[block(f, row + r, col + c)] = jnp.zeros((f.b, f.b), dest.dtype) if i is None else read(i)
 
 
-def pack_edges(f, drop_ref, low, high, to_cross, to_mate):
+def pack_edges(f, drop_ref, low, high, to_cross, *to_mate):
     odd = odd_place(f, drop_ref)
+    parts = len(to_mate)
     for i, (lower, upper) in enumerate(zip(under(f.h), over(f.h))):
         back, forth = low[block(f, *lower)], high[block(f, *upper)]
         to_cross[block(f, i, 0)] = jnp.where(odd, forth, back)
-        to_mate[block(f, i, 0)] = jnp.where(odd, back, forth)
+        to_mate[i % parts][block(f, i // parts, 0)] = jnp.where(odd, back, forth)
 
 
 def slabs_kernel(f, drop_ref, own, corner, corner_again, to_mate, to_cross):
@@ -369,7 +370,7 @@
 
 def density_edges_kernel(
     f, drop_ref, own, cross, mate, correction, new_low, new_high, square, corners, whole, to_cross, to_mate,
-    before, after, low, high,
+    to_mate_too, before, after, low, high,
 ):
     h, p = f.h, f.p
     below, above = sides(f, drop_ref, indexed(f, mate), indexed(f, cross))
@@ -395,7 +396,7 @@
         total = masked(f, right_tile(f, square, corners, whole, row, col), row, col, drop_ref)
         dest, local = (low, row) if row < p else (high, row - 2 * p)
         dest[at(f, local, local + 1, col - p, col - p + 1)] = total.astype(dest.dtype)
-    pack_edges(f, drop_ref, low, high, to_cross, to_mate)
+    pack_edges(f, drop_ref, low, high, to_cross, to_mate, to_mate_too)
 
 
 def density_own_kernel(f, drop_ref, square, whole, out):
@@ -406,24 +407,72 @@
             out[at(f, row - p, row - p + 1, col - p, col - p + 1)] = total.astype(out.dtype)
 
 
-def rows_kernel(f, first, drop_ref, own, cross, mate, out):
+def slots_kernel(f, first, parts, drop_ref, own, *refs):
     h = f.h
-    below, above = sides(f, drop_ref, indexed(f, mate), indexed(f, cross))
+    mates = [indexed(f, ref) for ref in refs[:parts]]
+    slots, out, sem = refs[parts:]
     over_index = {place: i for i, place in enumerate(over(h))}
     under_index = {place: i for i, place in enumerate(under(h))}
+
+    def mate_block(i):
+        return mates[i % parts](i // parts)
+
     for r in range(h):
         dropped = drop_ref[h + r]
 
         def at_offset(offset, r=r):
             col = r + offset
             if col < h:
-                return below(over_index[r, col])
+                return mate_block(over_index[r, col])
             if col < 2 * h:
                 return own[block(f, first + r, col - h)]
-            return above(under_index[r, col - 2 * h])
+            return mate_block(under_index[r, col - 2 * h])
 
         for s in range(f.k):
-            out[r, s] = jnp.where(dropped <= s, at_offset(s + 1), at_offset(s))
+            slots[r, s] = jnp.where(dropped <= s, at_offset(s + 1), at_offset(s))
+    copy = pltpu.make_async_copy(slots, out, sem)
+    copy.start()
+    copy.wait()
+
+
+def last_slots_kernel(f, drop_ref, slots, cross, unused, out, side, sems):
+    h, k = f.h, f.k
+    odd = odd_place(f, drop_ref)
+    cross_block = indexed(f, cross)
+    over_index = {place: i for i, place in enumerate(over(h))}
+    under_index = {place: i for i, place in enumerate(under(h))}
+
+    def fill(low):
+        copies = []
+        for r in range(h):
+            dropped = drop_ref[h + r]
+            lo, hi = (0, h - r) if low else (k - 1 - r, k)
+            for s in range(lo, hi):
+
+                def at_offset(offset, r=r, s=s):
+                    col = r + offset
+                    if low and col < h:
+                        return cross_block(over_index[r, col])
+                    if not low and col >= 2 * h:
+                        return cross_block(under_index[r, col - 2 * h])
+                    return slots[r, s]
+
+                side[r, s] = jnp.where(dropped <= s, at_offset(s + 1), at_offset(s))
+            copy = pltpu.make_async_copy(
+                side.at[r, pl.ds(lo, hi - lo)], out.at[r, pl.ds(lo, hi - lo)], sems.at[r]
+            )
+            copy.start()
+            copies.append(copy)
+        for copy in copies:
+            copy.wait()
+
+    @pl.when(odd)
+    def _():
+        fill(False)
+
+    @pl.when(jnp.logical_not(odd))
+    def _():
+        fill(True)
 
 
 VMEM = pl.BlockSpec(memory_space=pltpu.VMEM)
@@ -431,7 +480,7 @@
 ANY = pl.BlockSpec(memory_space=pl.ANY)
 
 
-def call(kernel, outs, scratch, flops, limit, drop, *args, passed=(), light=False):
+def call(kernel, outs, scratch, flops, limit, drop, *args, passed=(), light=False, off=0):
     moved = sum(a.size * a.dtype.itemsize for a in args) + sum(s.size * s.dtype.itemsize for s in outs)
     if light:
         flops = moved = 0
@@ -440,7 +489,7 @@
         kernel,
         out_shape=[*outs, *[jax.ShapeDtypeStruct(a.shape, a.dtype) for a in passed]],
         in_specs=[SMEM] + [VMEM] * n + [ANY] * len(passed),
-        out_specs=[VMEM] * len(outs) + [ANY] * len(passed),
+        out_specs=[VMEM] * (len(outs) - off) + [ANY] * (off + len(passed)),
         scratch_shapes=scratch,
         input_output_aliases={1 + n + i: len(outs) + i for i in range(len(passed))},
         compiler_params=pltpu.CompilerParams(vmem_limit_bytes=limit * MIB),
@@ -554,22 +603,27 @@
         20, 12, drop, corner_cross, corner_mate, correction, low, high,
     )
     inverse_cross, inverse_mate = to_cross(inverse_cross), to_mate(inverse_mate)
-    whole, rim_cross, rim_mate = run(
+    whole, rim_cross, rim_mate, rim_mate_too = run(
         density_edges_kernel,
-        [columns, triangle, triangle],
+        [columns, triangle, half_triangle, half_triangle],
         [group_scratch] * 4,
         38, 20, drop, own, edge_cross, edge_mate, correction, new_low, new_high, square,
         square_corners,
     )
-    rim_cross, rim_mate = to_cross(rim_cross), to_mate(rim_mate)
+    rim_cross, rim_mates = to_cross(rim_cross), [to_mate(rim_mate), to_mate(rim_mate_too)]
     (density_own,) = run(density_own_kernel, [square_group], [], 18, 12, drop, square, whole)
     out = jax.ShapeDtypeStruct(density.shape, kind)
 
-    def assembled(own, first, cross, mate):
-        return call(functools.partial(rows_kernel, f, first), [out], [], 0, 8, drop, own, cross, mate)[0]
-
-    inverse_next = assembled(whole, half, inverse_cross, inverse_mate)
-    density_next = assembled(density_own, 0, rim_cross, rim_mate)
+    def assembled(own, first, cross, mates):
+        kernel = functools.partial(slots_kernel, f, first, len(mates))
+        scratch = [pltpu.SemaphoreType.DMA(())]
+        slots, early = call(kernel, [out, out], scratch, 0, 8, drop, own, *mates, light=True, off=1)
+        scratch = [pltpu.VMEM(out.shape, kind), pltpu.SemaphoreType.DMA((half,))]
+        kernel = functools.partial(last_slots_kernel, f)
+        return call(kernel, [], scratch, 0, 8, drop, slots, cross, passed=(early,), light=True)[0]
+
+    inverse_next = assembled(whole, half, inverse_cross, [inverse_mate])
+    density_next = assembled(density_own, 0, rim_cross, rim_mates)
     return density_next, inverse_next
 
 

time: 85.7 us -> 85 us (level)
  waiting for transfers between devices: 30.8 us -> 27.6 us
  Pallas kernels: 24.2 us -> 26.7 us
    ppermute x18 -> x19, waiting for transfers between devices: 30.8 us -> 27.6 us  [routed(): lax.ppermute(x, RING, [(i, (i + step(i)) % size) for i in range(size) if...]
    pallas_call x12 -> x14, Pallas kernels: 24.2 us -> 26.7 us  [call(): pl.pallas_call(kernel, out_shape=[*outs, *[jax.ShapeDtypeStruct(a.shape,...]
    ppermute x18 -> x19, starting transfers between devices: 26.6 us -> 26.5 us  [routed(): lax.ppermute(x, RING, [(i, (i + step(i)) % size) for i in range(size) if...]
  transfers between devices with their start and end apart: 18 -> 19, of which waited for: 3 -> 5; matrix products, arithmetic and copies ran while one was open for 1% -> 1% of each run, Pallas kernels for 25% -> 29%
where the time goes in v15:
time: 85 us; the launch traced here: 84.8 us
  waiting for transfers between devices  27.6 us (32%)
  Pallas kernels  26.7 us (31%)
  starting transfers between devices  26.5 us (31%)
  local copies, waits for them, and re-layouts  2.04 us (2%)
  other arithmetic  1.04 us (1%)
    ppermute x19, waiting for transfers between devices, routed(): lax.ppermute(x, RING, [(i, (i + step(i)) % size) for i in range(size) if...  27.6 us
    pallas_call x14, Pallas kernels, call(): pl.pallas_call(kernel, out_shape=[*outs, *[jax.ShapeDtypeStruct(a.shape,...  26.7 us
    ppermute x19, starting transfers between devices, routed(): lax.ppermute(x, RING, [(i, (i + step(i)) % size) for i in range(size) if...  26.5 us
    unnamed x8, local copies, waits for them, and re-layouts  2.04 us
  transfers between devices with their start and end apart: 19, of which 5 were waited for; matrix products, arithmetic and copies ran while one was open for 1% of the time, Pallas kernels for 29%

profile of v15, /device:TPU:1, one launch (start us, length us, event | category | flops | bytes accessed | tf_op | source)
XLA Modules:
  0.0 84.8 jit_solution(18382090977156281271)
XLA Ops:
  0.6 2.7 %collective-permute-start.2 = (bf16[4,8,128,128]{3,2,1,0:T(8,128)(2,1)}, bf16[4,8,128,128]{3,2,1,0:T(8,128)(2,1)S(1)}, u32[]{:S(2)}, u32[]{:S(2)}) collective-permute-start(bf16[4,8,128,128]{3,2,1,0:T(8,128)(2,1)} %own.2), channel_id=1, source_target_pairs={{0,15},{1,2},{2,1},{3,4},{4,3},{5,6},{6,5},{7,8},{8,7},{9,10},{10,... | collective-permute-start | bytes 3145736 | tf_op jit(solution)/shard_map/ppermute | solution.py:502
  3.3 2.9 %collective-permute-start.3 = (bf16[4,8,128,128]{3,2,1,0:T(8,128)(2,1)}, bf16[4,8,128,128]{3,2,1,0:T(8,128)(2,1)S(1)}, u32[]{:S(2)}, u32[]{:S(2)}) collective-permute-start(bf16[4,8,128,128]{3,2,1,0:T(8,128)(2,1)} %own.2), channel_id=1, source_target_pairs={{0,1},{1,0},{2,3},{3,2},{4,5},{5,4},{6,7},{7,6},{8,9},{9,8},{10,11... | collective-permute-start | bytes 3145736 | tf_op jit(solution)/shard_map/ppermute | solution.py:502
  8.4 2.1 %shard_map.51 = (bf16[2048,128]{1,0:T(8,128)(2,1)S(1)}, bf16[2048,128]{1,0:T(8,128)(2,1)}, bf16[3328,128]{1,0:T(8,128)(2,1)}, bf16[1280,128]{1,0:T(8,128)(2,1)S(1)}) custom-call(s32[5]{0:T(128)S(1)} %pad_add_fusion.1.drop_ref, bf16[4,8,128,128]{3,2,1,0:T(8,128)(2,1)S(1)} %copy-done), custom_call_target="tpu_custom_call" | custom-call | bytes 3276800 | tf_op jit(solution)/shard_map/pallas_call | solution.py:488
  12.0 15.3 %collective-permute-done = s32[4]{0:T(128)S(1)} collective-permute-done((s32[4]{0:T(128)S(1)}, s32[4]{0:T(128)S(1)}, u32[]{:S(2)}, u32[]{:S(2)}) %collective-permute-start) | collective-permute-done | bytes 48 | tf_op jit(solution)/shard_map/ppermute | solution.py:502
  28.2 1.8 %collective-permute-start.8 = (bf16[1280,128]{1,0:T(8,128)(2,1)S(1)}, bf16[1280,128]{1,0:T(8,128)(2,1)S(1)}, u32[]{:S(2)}, u32[]{:S(2)}) collective-permute-start(bf16[1280,128]{1,0:T(8,128)(2,1)S(1)} %get-tuple-element.50.sent_cross), channel_id=1, source_target_pairs={{0,15},{1,2},{2,1},{3,4},{4,3},{5,6},{6,5},{7,8},{8,7},{9,10},{10,... | collective-permute-start | bytes 983048 | tf_op jit(solution)/shard_map/ppermute | solution.py:502
  30.1 6.3 %collective-permute-start.6 = (bf16[640,128]{1,0:T(8,128)(2,1)S(1)}, bf16[640,128]{1,0:T(8,128)(2,1)S(1)}, u32[]{:S(2)}, u32[]{:S(2)}) collective-permute-start(bf16[640,128]{1,0:T(8,128)(2,1)S(1)} %get-tuple-element.43), channel_id=1, source_target_pairs={{0,1},{1,0},{2,3},{3,2},{4,5},{5,4},{6,7},{7,6},{8,9},{9,8},{10,11... | collective-permute-start | bytes 491528 | tf_op jit(solution)/shard_map/ppermute | solution.py:502
  36.4 4.3 %shard_map.50 = (bf16[1536,1280]{1,0:T(8,128)(2,1)S(1)}, bf16[1536,1280]{1,0:T(8,128)(2,1)S(1)}, bf16[1024,512]{1,0:T(8,128)(2,1)S(1)}, bf16[1024,512]{1,0:T(8,128)(2,1)S(1)}, f32[1024,512]{1,0:T(8,128)S(1)}) custom-call(s32[13]{0:T(128)S(1)} %pad_add_fusion.drop_ref, bf16[4,8,128,128]{3,2,1,0:T(8,128)(2,1)S(1)} %copy-done.3, ...), custom_call_target="tpu_custom_call" | custom-call | flops 2818572288 | bytes 15204352 | tf_op jit(solution)/shard_map/pallas_call | solution.py:488
  40.7 1.4 %shard_map.53 = (bf16[1024,512]{1,0:T(8,128)(2,1)S(1)}, bf16[1024,512]{1,0:T(8,128)(2,1)S(1)}) custom-call(s32[13]{0:T(128)S(1)} %pad_add_fusion.drop_ref, bf16[1280,128]{1,0:T(8,128)(2,1)S(1)} %collective-permute-done.5.far_far, bf16[640,128]{1,0:T(8,128)(2,1)S(1)} %collective-permute-done.6.far_mate, ...), custom_call_target="tpu_custom_call" | custom-call | tf_op jit(solution)/shard_map/pallas_call | solution.py:488
  42.1 3.8 %shard_map.54 = (bf16[1536,512]{1,0:T(8,128)(2,1)S(1)}, bf16[512,512]{1,0:T(8,128)(2,1)S(1)}, f32[1024,512]{1,0:T(8,128)S(1)}) custom-call(s32[13]{0:T(128)S(1)} %pad_add_fusion.drop_ref, bf16[1536,1280]{1,0:T(8,128)(2,1)S(1)} %get-tuple-element.38.shifted, bf16[1024,512]{1,0:T(8,128)(2,1)S(1)} %get-tuple-element.48.corners, ...), custom_call_target="tpu_custom_call" | custom-call | tf_op jit(solution)/shard_map/pallas_call | solution.py:488
  46.8 2.2 %collective-permute-start.13 = (bf16[512,512]{1,0:T(8,128)(2,1)S(1)}, bf16[512,512]{1,0:T(8,128)(2,1)S(1)}, u32[]{:S(2)}, u32[]{:S(2)}) collective-permute-start(bf16[512,512]{1,0:T(8,128)(2,1)S(1)} %get-tuple-element.51.own), channel_id=1, source_target_pairs={{0,1},{1,0},{2,3},{3,2},{4,5},{5,4},{6,7},{7,6},{8,9},{9,8},{10,11... | collective-permute-start | bytes 1572872 | tf_op jit(solution)/shard_map/ppermute | solution.py:502
  49.0 1.3 %shard_map.55 = (bf16[512,512]{1,0:T(8,128)(2,1)S(1)}, bf16[512,512]{1,0:T(8,128)(2,1)S(1)}, bf16[1280,128]{1,0:T(8,128)(2,1)S(1)}, bf16[1280,128]{1,0:T(8,128)(2,1)S(1)}) custom-call(s32[13]{0:T(128)S(1)} %pad_add_fusion.drop_ref, bf16[3328,128]{1,0:T(8,128)(2,1)S(1)} %collective-permute-done.4.refs_1_.mate, ...), custom_call_target="tpu_custom_call" | custom-call | flops 335544320 | bytes 6750208 | tf_op jit(solution)/shard_map/pallas_call | solution.py:488
  50.4 2.3 %collective-permute-start.10 = (bf16[1280,128]{1,0:T(8,128)(2,1)S(1)}, bf16[1280,128]{1,0:T(8,128)(2,1)S(1)}, u32[]{:S(2)}, u32[]{:S(2)}) collective-permute-start(bf16[1280,128]{1,0:T(8,128)(2,1)S(1)} %get-tuple-element.55), channel_id=1, source_target_pairs={{0,15},{1,2},{2,1},{3,4},{4,3},{5,6},{6,5},{7,8},{8,7},{9,10},{10,... | collective-permute-start | bytes 983048 | tf_op jit(solution)/shard_map/ppermute | solution.py:502
  52.7 2.1 %collective-permute-start.11 = (bf16[1280,128]{1,0:T(8,128)(2,1)S(1)}, bf16[1280,128]{1,0:T(8,128)(2,1)S(1)}, u32[]{:S(2)}, u32[]{:S(2)}) collective-permute-start(bf16[1280,128]{1,0:T(8,128)(2,1)S(1)} %get-tuple-element.56), channel_id=1, source_target_pairs={{0,1},{1,0},{2,3},{3,2},{4,5},{5,4},{6,7},{7,6},{8,9},{9,8},{10,11... | collective-permute-start | bytes 983048 | tf_op jit(solution)/shard_map/ppermute | solution.py:502
  54.8 2.0 %shard_map.56.correction = bf16[1536,512]{1,0:T(8,128)(2,1)S(1)} custom-call(s32[13]{0:T(128)S(1)} %pad_add_fusion.drop_ref, bf16[1536,1280]{1,0:T(8,128)(2,1)S(1)} %get-tuple-element.38.shifted, bf16[1024,512]{1,0:T(8,128)(2,1)S(1)} %get-tuple-element.48.corners, bf16[512,512]{1,0:T(8,128)(2,1)S(1)} %get-tuple-element.57.low, ...), custom_call_target="tpu_custom_call" | custom-call | flops 1275068416 | bytes 8126464 | tf_op jit(solution)/shard_map/pallas_call | solution.py:488
  56.8 8.0 %collective-permute-done.12.cross = bf16[512,512]{1,0:T(8,128)(2,1)S(1)} collective-permute-done((bf16[512,512]{1,0:T(8,128)(2,1)S(1)}, bf16[512,512]{1,0:T(8,128)(2,1)S(1)}, u32[]{:S(2)}, u32[]{:S(2)}) %collective-permute-start.12) | collective-permute-done | bytes 524320 | tf_op jit(solution)/shard_map/ppermute | solution.py:502
  64.8 1.5 %shard_map.57 = (bf16[512,512]{1,0:T(8,128)(2,1)S(1)}, bf16[512,512]{1,0:T(8,128)(2,1)S(1)}, bf16[1280,128]{1,0:T(8,128)(2,1)S(1)}, bf16[1280,128]{1,0:T(8,128)(2,1)S(1)}) custom-call(s32[13]{0:T(128)S(1)} %pad_add_fusion.drop_ref, bf16[512,512]{1,0:T(8,128)(2,1)S(1)} %collective-permute-done.12.cross, bf16[512,512]{1,0:T(8,128)(2,1)S(1)} %collective-permute-done.13.mate, ...), custom_call_target="tpu_custom_call" | custom-call | flops 671088640 | bytes 5373952 | tf_op jit(solution)/shard_map/pallas_call | solution.py:488
  68.3 2.2 %shard_map.58 = (bf16[1536,512]{1,0:T(8,128)(2,1)S(1)}, bf16[1280,128]{1,0:T(8,128)(2,1)S(1)}, bf16[640,128]{1,0:T(8,128)(2,1)S(1)}, bf16[640,128]{1,0:T(8,128)(2,1)S(1)}) custom-call(s32[13]{0:T(128)S(1)} %pad_add_fusion.drop_ref, bf16[512,512]{1,0:T(8,128)(2,1)S(1)} %get-tuple-element.51.own, bf16[1280,128]{1,0:T(8,128)(2,1)S(1)} %collective-permute-done.10.cross, ...), custom_call_target="tpu_custom_call" | custom-call | flops 1275068416 | bytes 11010048 | tf_op jit(solution)/shard_map/pallas_call | solution.py:488
  70.5 1.3 %collective-permute-start.16 = (bf16[1280,128]{1,0:T(8,128)(2,1)S(1)}, bf16[1280,128]{1,0:T(8,128)(2,1)S(1)}, u32[]{:S(2)}, u32[]{:S(2)}) collective-permute-start(bf16[1280,128]{1,0:T(8,128)(2,1)S(1)} %get-tuple-element.66), channel_id=1, source_target_pairs={{0,15},{1,2},{2,1},{3,4},{4,3},{5,6},{6,5},{7,8},{8,7},{9,10},{10,... | collective-permute-start | bytes 983048 | tf_op jit(solution)/shard_map/ppermute | solution.py:502
  71.8 1.8 %collective-permute-start.14 = (bf16[640,128]{1,0:T(8,128)(2,1)S(1)}, bf16[640,128]{1,0:T(8,128)(2,1)S(1)}, u32[]{:S(2)}, u32[]{:S(2)}) collective-permute-start(bf16[640,128]{1,0:T(8,128)(2,1)S(1)} %get-tuple-element.63), channel_id=1, source_target_pairs={{0,1},{1,0},{2,3},{3,2},{4,5},{5,4},{6,7},{7,6},{8,9},{9,8},{10,11... | collective-permute-start | bytes 491528 | tf_op jit(solution)/shard_map/ppermute | solution.py:502
  73.6 1.3 %shard_map.59.own = bf16[512,512]{1,0:T(8,128)(2,1)S(1)} custom-call(s32[13]{0:T(128)S(1)} %pad_add_fusion.drop_ref, bf16[1536,1280]{1,0:T(8,128)(2,1)S(1)} %get-tuple-element.37.square, bf16[1536,512]{1,0:T(8,128)(2,1)S(1)} %get-tuple-element.62.whole.own), custom_call_target="tpu_custom_call" | custom-call | flops 603979776 | bytes 6029312 | tf_op jit(solution)/shard_map/pallas_call | solution.py:488
  75.0 1.7 %shard_map.60 = (bf16[4,8,128,128]{3,2,1,0:T(8,128)(2,1)S(1)}, bf16[4,8,128,128]{3,2,1,0:T(8,128)(2,1)}) custom-call(s32[13]{0:T(128)S(1)} %pad_add_fusion.drop_ref, bf16[512,512]{1,0:T(8,128)(2,1)S(1)} %shard_map.59.own, bf16[640,128]{1,0:T(8,128)(2,1)S(1)} %collective-permute-done.14.refs_0_, bf16[640,128]{1,0:T(8,128)(2,1)S(1)} %collective-permute-done.15.refs_1_), custom_call_target="tpu_custom_call" | custom-call | tf_op jit(solution)/shard_map/pallas_call | solution.py:488
  76.7 1.7 %shard_map.62 = (bf16[4,8,128,128]{3,2,1,0:T(8,128)(2,1)S(1)}, bf16[4,8,128,128]{3,2,1,0:T(8,128)(2,1)}) custom-call(s32[13]{0:T(128)S(1)} %pad_add_fusion.drop_ref, bf16[1536,512]{1,0:T(8,128)(2,1)S(1)} %get-tuple-element.62.whole.own, bf16[1280,128]{1,0:T(8,128)(2,1)S(1)} %collective-permute-done.17.refs_0_), custom_call_target="tpu_custom_call" | custom-call | tf_op jit(solution)/shard_map/pallas_call | solution.py:488
  80.0 3.4 %collective-permute-done.16.cross = bf16[1280,128]{1,0:T(8,128)(2,1)S(1)} collective-permute-done((bf16[1280,128]{1,0:T(8,128)(2,1)S(1)}, bf16[1280,128]{1,0:T(8,128)(2,1)S(1)}, u32[]{:S(2)}, u32[]{:S(2)}) %collective-permute-start.16) | collective-permute-done | bytes 327712 | tf_op jit(solution)/shard_map/ppermute | solution.py:502
  83.4 1.3 %shard_map.61 = bf16[4,8,128,128]{3,2,1,0:T(8,128)(2,1)} custom-call(s32[13]{0:T(128)S(1)} %pad_add_fusion.drop_ref, bf16[4,8,128,128]{3,2,1,0:T(8,128)(2,1)S(1)} %get-tuple-element.65.slots, bf16[1280,128]{1,0:T(8,128)(2,1)S(1)} %collective-permute-done.16.cross, bf16[4,8,128,128]{3,2,1,0:T(8,128)(2,1)} %get-tuple-element.67.unused), custom_call_target="tpu_custom_call", output_to_operand_aliasing={{}: (3, {})} | custom-call | tf_op jit(solution)/shard_map/pallas_call | solution.py:488
  (42 shorter events, 9.2 us)
Async XLA Ops:
  0.6 26.8 %collective-permute-start.2 = (bf16[4,8,128,128]{3,2,1,0:T(8,128)(2,1)}, bf16[4,8,128,128]{3,2,1,0:T(8,128)(2,1)S(1)}, u32[]{:S(2)}, u32[]{:S(2)}) collective-permute-start(bf16[4,8,128,128]{3,2,1,0:T(8,128)(2,1)} %own.2), channel_id=1, source_target_pairs={{0,15},{1,2},{2,1},{3,4},{4,3},{5,6},{6,5},{7,8},{8,7},{9,10},{10,... | collective-permute-start | bytes 3145736 | tf_op jit(solution)/shard_map/ppermute | solution.py:502
  3.3 24.1 %collective-permute-start.3 = (bf16[4,8,128,128]{3,2,1,0:T(8,128)(2,1)}, bf16[4,8,128,128]{3,2,1,0:T(8,128)(2,1)S(1)}, u32[]{:S(2)}, u32[]{:S(2)}) collective-permute-start(bf16[4,8,128,128]{3,2,1,0:T(8,128)(2,1)} %own.2), channel_id=1, source_target_pairs={{0,1},{1,0},{2,3},{3,2},{4,5},{5,4},{6,7},{7,6},{8,9},{9,8},{10,11... | collective-permute-start | bytes 3145736 | tf_op jit(solution)/shard_map/ppermute | solution.py:502
  7.1 1.2 %copy-start = (bf16[4,8,128,128]{3,2,1,0:T(8,128)(2,1)S(1)}, bf16[4,8,128,128]{3,2,1,0:T(8,128)(2,1)}, u32[]{:S(2)}) copy-start(bf16[4,8,128,128]{3,2,1,0:T(8,128)(2,1)} %own.3) | copy-start | bytes 3145732
  10.4 0.8 copy-start.1
  11.2 16.2 %collective-permute-start.4 = (bf16[3328,128]{1,0:T(8,128)(2,1)}, bf16[3328,128]{1,0:T(8,128)(2,1)S(1)}, u32[]{:S(2)}, u32[]{:S(2)}) collective-permute-start(bf16[3328,128]{1,0:T(8,128)(2,1)} %get-tuple-element.39.sent_mate), channel_id=1, source_target_pairs={{0,1},{1,0},{2,3},{3,2},{4,5},{5,4},{6,7},{7,6},{8,9},{9,8},{10,11... | collective-permute-start | bytes 2555912 | tf_op jit(solution)/shard_map/ppermute | solution.py:502
  11.2 16.1 %collective-permute-start = (s32[4]{0:T(128)S(1)}, s32[4]{0:T(128)S(1)}, u32[]{:S(2)}, u32[]{:S(2)}) collective-permute-start(s32[4]{0:T(128)S(1)} %broadcast_subtract_fusion), channel_id=1, source_target_pairs={{0,15},{1,2},{2,1},{3,4},{4,3},{5,6},{6,5},{7,8},{8,7},{9,10},{10,... | collective-permute-start | bytes 56 | tf_op jit(solution)/shard_map/ppermute | solution.py:502
  11.2 16.1 %collective-permute-start.1 = (s32[4]{0:T(128)S(1)}, s32[4]{0:T(128)S(1)}, u32[]{:S(2)}, u32[]{:S(2)}) collective-permute-start(s32[4]{0:T(128)S(1)} %broadcast_subtract_fusion), channel_id=1, source_target_pairs={{0,1},{1,0},{2,3},{3,2},{4,5},{5,4},{6,7},{7,6},{8,9},{9,8},{10,11... | collective-permute-start | bytes 56 | tf_op jit(solution)/shard_map/ppermute | solution.py:502
  12.0 24.4 %copy-start.3 = (bf16[4,8,128,128]{3,2,1,0:T(8,128)(2,1)S(1)}, bf16[4,8,128,128]{3,2,1,0:T(8,128)(2,1)}, u32[]{:S(2)}) copy-start(bf16[4,8,128,128]{3,2,1,0:T(8,128)(2,1)} %own.2) | copy-start | bytes 3145732
  28.1 12.5 %collective-permute-start.5 = (bf16[1280,128]{1,0:T(8,128)(2,1)S(1)}, bf16[1280,128]{1,0:T(8,128)(2,1)S(1)}, u32[]{:S(2)}, u32[]{:S(2)}) collective-permute-start(bf16[1280,128]{1,0:T(8,128)(2,1)S(1)} %get-tuple-element.42), channel_id=1, source_target_pairs={{0,13},{1,4},{2,15},{3,6},{4,1},{5,8},{6,3},{7,10},{8,5},{9,12},{1... | collective-permute-start | bytes 983048 | tf_op jit(solution)/shard_map/ppermute | solution.py:502
  28.2 13.9 %collective-permute-start.8 = (bf16[1280,128]{1,0:T(8,128)(2,1)S(1)}, bf16[1280,128]{1,0:T(8,128)(2,1)S(1)}, u32[]{:S(2)}, u32[]{:S(2)}) collective-permute-start(bf16[1280,128]{1,0:T(8,128)(2,1)S(1)} %get-tuple-element.50.sent_cross), channel_id=1, source_target_pairs={{0,15},{1,2},{2,1},{3,4},{4,3},{5,6},{6,5},{7,8},{8,7},{9,10},{10,... | collective-permute-start | bytes 983048 | tf_op jit(solution)/shard_map/ppermute | solution.py:502
  30.0 19.0 %collective-permute-start.9 = (bf16[2048,128]{1,0:T(8,128)(2,1)}, bf16[2048,128]{1,0:T(8,128)(2,1)S(1)}, u32[]{:S(2)}, u32[]{:S(2)}) collective-permute-start(bf16[2048,128]{1,0:T(8,128)(2,1)} %get-tuple-element.52), channel_id=1, source_target_pairs={{0,15},{1,2},{2,1},{3,4},{4,3},{5,6},{6,5},{7,8},{8,7},{9,10},{10,... | collective-permute-start | bytes 1572872 | tf_op jit(solution)/shard_map/ppermute | solution.py:502
  30.1 10.5 %collective-permute-start.6 = (bf16[640,128]{1,0:T(8,128)(2,1)S(1)}, bf16[640,128]{1,0:T(8,128)(2,1)S(1)}, u32[]{:S(2)}, u32[]{:S(2)}) collective-permute-start(bf16[640,128]{1,0:T(8,128)(2,1)S(1)} %get-tuple-element.43), channel_id=1, source_target_pairs={{0,1},{1,0},{2,3},{3,2},{4,5},{5,4},{6,7},{7,6},{8,9},{9,8},{10,11... | collective-permute-start | bytes 491528 | tf_op jit(solution)/shard_map/ppermute | solution.py:502
  36.4 4.3 %collective-permute-start.7 = (bf16[640,128]{1,0:T(8,128)(2,1)S(1)}, bf16[640,128]{1,0:T(8,128)(2,1)S(1)}, u32[]{:S(2)}, u32[]{:S(2)}) collective-permute-start(bf16[640,128]{1,0:T(8,128)(2,1)S(1)} %get-tuple-element.44), channel_id=1, source_target_pairs={{0,1},{1,0},{2,3},{3,2},{4,5},{5,4},{6,7},{7,6},{8,9},{9,8},{10,11... | collective-permute-start | bytes 491528 | tf_op jit(solution)/shard_map/ppermute | solution.py:502
  40.7 1.5 %copy-start.2 = (bf16[2048,128]{1,0:T(8,128)(2,1)S(1)}, bf16[2048,128]{1,0:T(8,128)(2,1)}, u32[]{:S(2)}) copy-start(bf16[2048,128]{1,0:T(8,128)(2,1)} %copy-done.1) | copy-start | bytes 1572868
  45.9 18.8 %collective-permute-start.12 = (bf16[512,512]{1,0:T(8,128)(2,1)S(1)}, bf16[512,512]{1,0:T(8,128)(2,1)S(1)}, u32[]{:S(2)}, u32[]{:S(2)}) collective-permute-start(bf16[512,512]{1,0:T(8,128)(2,1)S(1)} %get-tuple-element.51.own), channel_id=1, source_target_pairs={{0,15},{1,2},{2,1},{3,4},{4,3},{5,6},{6,5},{7,8},{8,7},{9,10},{10,... | collective-permute-start | bytes 1572872 | tf_op jit(solution)/shard_map/ppermute | solution.py:502
  46.8 18.0 %collective-permute-start.13 = (bf16[512,512]{1,0:T(8,128)(2,1)S(1)}, bf16[512,512]{1,0:T(8,128)(2,1)S(1)}, u32[]{:S(2)}, u32[]{:S(2)}) collective-permute-start(bf16[512,512]{1,0:T(8,128)(2,1)S(1)} %get-tuple-element.51.own), channel_id=1, source_target_pairs={{0,1},{1,0},{2,3},{3,2},{4,5},{5,4},{6,7},{7,6},{8,9},{9,8},{10,11... | collective-permute-start | bytes 1572872 | tf_op jit(solution)/shard_map/ppermute | solution.py:502
  50.4 17.9 %collective-permute-start.10 = (bf16[1280,128]{1,0:T(8,128)(2,1)S(1)}, bf16[1280,128]{1,0:T(8,128)(2,1)S(1)}, u32[]{:S(2)}, u32[]{:S(2)}) collective-permute-start(bf16[1280,128]{1,0:T(8,128)(2,1)S(1)} %get-tuple-element.55), channel_id=1, source_target_pairs={{0,15},{1,2},{2,1},{3,4},{4,3},{5,6},{6,5},{7,8},{8,7},{9,10},{10,... | collective-permute-start | bytes 983048 | tf_op jit(solution)/shard_map/ppermute | solution.py:502
  52.7 15.6 %collective-permute-start.11 = (bf16[1280,128]{1,0:T(8,128)(2,1)S(1)}, bf16[1280,128]{1,0:T(8,128)(2,1)S(1)}, u32[]{:S(2)}, u32[]{:S(2)}) collective-permute-start(bf16[1280,128]{1,0:T(8,128)(2,1)S(1)} %get-tuple-element.56), channel_id=1, source_target_pairs={{0,1},{1,0},{2,3},{3,2},{4,5},{5,4},{6,7},{7,6},{8,9},{9,8},{10,11... | collective-permute-start | bytes 983048 | tf_op jit(solution)/shard_map/ppermute | solution.py:502
  66.3 10.5 %collective-permute-start.17 = (bf16[1280,128]{1,0:T(8,128)(2,1)S(1)}, bf16[1280,128]{1,0:T(8,128)(2,1)S(1)}, u32[]{:S(2)}, u32[]{:S(2)}) collective-permute-start(bf16[1280,128]{1,0:T(8,128)(2,1)S(1)} %get-tuple-element.68), channel_id=1, source_target_pairs={{0,1},{1,0},{2,3},{3,2},{4,5},{5,4},{6,7},{7,6},{8,9},{9,8},{10,11... | collective-permute-start | bytes 983048 | tf_op jit(solution)/shard_map/ppermute | solution.py:502
  66.3 12.4 %collective-permute-start.18 = (bf16[1280,128]{1,0:T(8,128)(2,1)S(1)}, bf16[1280,128]{1,0:T(8,128)(2,1)S(1)}, u32[]{:S(2)}, u32[]{:S(2)}) collective-permute-start(bf16[1280,128]{1,0:T(8,128)(2,1)S(1)} %get-tuple-element.70), channel_id=1, source_target_pairs={{0,15},{1,2},{2,1},{3,4},{4,3},{5,6},{6,5},{7,8},{8,7},{9,10},{10,... | collective-permute-start | bytes 983048 | tf_op jit(solution)/shard_map/ppermute | solution.py:502
  70.5 12.9 %collective-permute-start.16 = (bf16[1280,128]{1,0:T(8,128)(2,1)S(1)}, bf16[1280,128]{1,0:T(8,128)(2,1)S(1)}, u32[]{:S(2)}, u32[]{:S(2)}) collective-permute-start(bf16[1280,128]{1,0:T(8,128)(2,1)S(1)} %get-tuple-element.66), channel_id=1, source_target_pairs={{0,15},{1,2},{2,1},{3,4},{4,3},{5,6},{6,5},{7,8},{8,7},{9,10},{10,... | collective-permute-start | bytes 983048 | tf_op jit(solution)/shard_map/ppermute | solution.py:502
  71.8 3.1 %collective-permute-start.14 = (bf16[640,128]{1,0:T(8,128)(2,1)S(1)}, bf16[640,128]{1,0:T(8,128)(2,1)S(1)}, u32[]{:S(2)}, u32[]{:S(2)}) collective-permute-start(bf16[640,128]{1,0:T(8,128)(2,1)S(1)} %get-tuple-element.63), channel_id=1, source_target_pairs={{0,1},{1,0},{2,3},{3,2},{4,5},{5,4},{6,7},{7,6},{8,9},{9,8},{10,11... | collective-permute-start | bytes 491528 | tf_op jit(solution)/shard_map/ppermute | solution.py:502
  73.6 1.4 %collective-permute-start.15 = (bf16[640,128]{1,0:T(8,128)(2,1)S(1)}, bf16[640,128]{1,0:T(8,128)(2,1)S(1)}, u32[]{:S(2)}, u32[]{:S(2)}) collective-permute-start(bf16[640,128]{1,0:T(8,128)(2,1)S(1)} %get-tuple-element.64), channel_id=1, source_target_pairs={{0,1},{1,0},{2,3},{3,2},{4,5},{5,4},{6,7},{7,6},{8,9},{9,8},{10,11... | collective-permute-start | bytes 491528 | tf_op jit(solution)/shard_map/ppermute | solution.py:502

commit v16 on v15

--- a/solution.py
+++ b/solution.py
@@ -145,7 +145,7 @@
         to_mate[i % parts][block(f, i // parts, 0)] = jnp.where(odd, back, forth)
 
 
-def slabs_kernel(f, drop_ref, own, corner, corner_again, to_mate, to_cross):
+def slabs_kernel(f, drop_ref, own, corner, corner_again, to_mate, to_cross, to_cross_again):
     h = f.h
     odd = drop_ref[h] == 1
     n = len(under(h))
@@ -154,7 +154,9 @@
         forth = stored(own, r, 2 * h + c - r, drop_ref[r])
         back = stored(own, s, d - s, drop_ref[s])
         to_mate[block(f, i, 0)] = jnp.where(odd, back, forth)
-        to_cross[block(f, i, 0)] = jnp.where(odd, forth, back)
+        across = jnp.where(odd, forth, back)
+        to_cross[block(f, i, 0)] = across
+        to_cross_again[block(f, i, 0)] = across
     for i, (r, c) in enumerate(full(h)):
         value = stored(own, r, c - r + h, drop_ref[r])
         corner[block(f, i, 0)] = value
@@ -165,13 +167,12 @@
 def forward_kernel(f, drop_ref, cross, *refs):
     h = f.h
     odd = odd_place(f, drop_ref)
-    to_mate, to_far = refs[-5:-3], refs[-3]
+    to_mate, to_far = refs[-4:-2]
     for i, (lower, upper) in enumerate(zip(under(h), over(h))):
         (r, c), (s, d) = lower, upper
         forth = stored(cross, r, 2 * h + c - r, jnp.where(odd, drop_ref[2 * h + r], drop_ref[r]))
         back = stored(cross, s, d - s, jnp.where(odd, drop_ref[2 * h + s], drop_ref[s]))
-        part, place = i % 2, i // 2
-        to_mate[part][block(f, place, 0)] = jnp.where(odd, back, forth)
+        to_mate[block(f, i, 0)] = jnp.where(odd, back, forth)
         to_far[block(f, i, 0)] = jnp.where(odd, forth, back)
 
 
@@ -222,11 +223,10 @@
 
 
 def corners_kernel(
-    f, drop_ref, far_far, far_mate, far_mate_too, reach, here, partial, square, shifted, low, high
+    f, drop_ref, far_far, far_mate, reach, here, partial, unused, square, shifted, low, high
 ):
     p = f.p
-    far_mates = [indexed(f, far_mate), indexed(f, far_mate_too)]
-    far_below, far_above = sides(f, drop_ref, lambda i: far_mates[i % 2](i // 2), indexed(f, far_far))
+    far_below, far_above = sides(f, drop_ref, indexed(f, far_mate), indexed(f, far_far))
     spread(f, low, 0, 0, far_below, under(f.h))
     spread(f, high, 0, 0, far_above, over(f.h))
     unit = unit_tile(f)
@@ -264,11 +264,17 @@
 
 
 def first_sweep_kernel(
-    f, drop_ref, shifted, corners, corner, sent_mate, sent_cross, mate, cross,
+    f, drop_ref, shifted, corners, corner, sent_mate, sent_cross, mate, direct, turned,
     correction, fresh, partial, whole, before, after,
 ):
     h, p = f.h, f.p
-    from_below, from_above = sides(f, drop_ref, indexed(f, mate), indexed(f, cross))
+    turning = drop_ref[3 * h + 1] == 1
+    direct_block, turned_block = indexed(f, direct), indexed(f, turned)
+
+    def cross(i):
+        return jnp.where(turning, turned_block(i), direct_block(i))
+
+    from_below, from_above = sides(f, drop_ref, indexed(f, mate), cross)
     down, up = sides(f, drop_ref, indexed(f, sent_mate), indexed(f, sent_cross))
     spread(f, whole, 0, 0, from_below, under(h))
     spread(f, whole, h, 0, indexed(f, corner), full(h))
@@ -348,7 +354,7 @@
 
 
 def second_edges_kernel(
-    f, drop_ref, cross, mate, correction, low, high, new_low, new_high, to_cross, to_mate
+    f, drop_ref, mate, cross, correction, low, high, new_low, new_high, to_cross, to_mate
 ):
     p = f.p
 
@@ -505,9 +511,9 @@
 def on_device(density, inverse_start, block_cols):
     rows, width, order, _ = density.shape
     half = width // 2
-    ring = lax.axis_size(RING)
+    ring, inner = lax.axis_size(RING), lax.axis_size(RING[1])
     total = rows * ring
-    assert rows == half and half % 2 == 0 and ring % 2 == 0
+    assert rows == half and half % 2 == 0 and inner % 2 == 0
     f = Frame(half, order)
     kind = density.dtype
     me = lax.axis_index(RING)
@@ -524,6 +530,9 @@
     def to_cross(x):
         return routed(x, cross_step)
 
+    def turns(i):
+        return i % inner in (0, inner - 1)
+
     positions = block_cols - (me * rows + jnp.arange(rows, dtype=jnp.int32))[:, None] + half
     positions = positions + jnp.where(positions < 0, total, jnp.where(positions >= total, -total, 0))
     own_drop = width * (width + 1) // 2 - jnp.sum(positions, axis=1)
@@ -531,10 +540,11 @@
     density_cross, density_mate = to_cross(density), to_mate(density)
     cross_drop, mate_drop = to_cross(own_drop), to_mate(own_drop)
     even = (me & 1) == 0
-    mark = jnp.reshape(me & 1, (1,))
-    start_drop = jnp.concatenate([own_drop, mark])
+    place = lax.axis_index(RING[1])
+    marks = jnp.stack([me & 1, ((place == 0) | (place == inner - 1)).astype(jnp.int32)])
+    start_drop = jnp.concatenate([own_drop, marks[:1]])
     drop = jnp.concatenate(
-        [jnp.where(even, cross_drop, mate_drop), own_drop, jnp.where(even, mate_drop, cross_drop), mark]
+        [jnp.where(even, cross_drop, mate_drop), own_drop, jnp.where(even, mate_drop, cross_drop), marks]
     )
 
     unit = 2 * f.t**3
@@ -553,17 +563,18 @@
     def run(kernel, outs, scratch, tiles, limit, *args, **kw):
         return call(functools.partial(kernel, f), outs, scratch, tiles * unit, limit, *args, **kw)
 
-    corner, corner_cross, slab_mate, triangle_cross = run(
-        slabs_kernel, [listed, listed, both, triangle], [], 0, 12, start_drop, inverse_start
+    corner, corner_cross, slab_mate, triangle_cross, triangle_turning = run(
+        slabs_kernel, [listed, listed, both, triangle, triangle], [], 0, 12, start_drop, inverse_start
     )
     from_mate = to_mate(slab_mate)
-    forward_mate, forward_mate_too, forward_far, triangle_cross, corner_cross = run(
-        forward_kernel, [half_triangle, half_triangle, triangle], [], 0, 12, drop, density_cross, density_mate, from_mate,
-        passed=(triangle_cross, corner_cross),
-    )
-    far_mate, far_mate_too = to_mate(forward_mate), to_mate(forward_mate_too)
+    direct_triangle = routed(triangle_cross, lambda i: 0 if turns(i) else cross_step(i))
+    forward_mate, forward_far, triangle_turning, corner_cross = run(
+        forward_kernel, [triangle, triangle], [], 0, 12, drop, density_cross, density_mate, from_mate,
+        passed=(triangle_turning, corner_cross),
+    )
+    far_mate = to_mate(forward_mate)
     far_far = routed(forward_far, lambda i: 3 * cross_step(i))
-    cross_triangle = to_cross(triangle_cross)
+    turned_triangle = routed(triangle_turning, lambda i: cross_step(i) if turns(i) else 0)
     cross_corner = to_cross(corner_cross)
 
     both_corners = jax.ShapeDtypeStruct((2 * f.group, f.group), kind)
@@ -571,19 +582,20 @@
         square_kernel,
         [band, band, both_corners, both_corners, partial_sums],
         [pltpu.VMEM((3 * f.group, 5 * f.group), kind)],
-        84, 26, drop, density, density_cross, density_mate,
+        84, 26, drop, density, density_cross, density_mate, light=True,
     )
     square_corners, shifted_corners = run(
         corners_kernel,
         [both_corners, both_corners],
         [group_scratch] * 2,
-        10, 16, drop, far_far, far_mate, far_mate_too, reach, here, partial, light=True,
+        10, 16, drop, far_far, far_mate, reach, here, partial, direct_triangle, light=True,
     )
     correction, own, partial = run(
         first_sweep_kernel,
         [columns, square_group, partial_sums],
         [whole_scratch, group_scratch, group_scratch],
-        66, 24, drop, shifted, shifted_corners, corner, slab_mate, triangle_cross, from_mate, cross_triangle, light=True,
+        66, 24, drop, shifted, shifted_corners, corner, slab_mate, triangle_cross, from_mate,
+        direct_triangle, turned_triangle, light=True,
     )
     corner_cross, corner_mate = to_cross(own), to_mate(own)
     low, high, edge_cross, edge_mate = run(
@@ -600,7 +612,7 @@
         second_edges_kernel,
         [square_group, square_group, triangle, triangle],
         [],
-        20, 12, drop, corner_cross, corner_mate, correction, low, high,
+        20, 12, drop, corner_mate, corner_cross, correction, low, high,
     )
     inverse_cross, inverse_mate = to_cross(inverse_cross), to_mate(inverse_mate)
     whole, rim_cross, rim_mate, rim_mate_too = run(

time: 85 us -> 85.6 us (level)
  starting transfers between devices: 26.5 us -> 25.2 us
  waiting for transfers between devices: 27.6 us -> 28.8 us
    ppermute x19, starting transfers between devices: 26.5 us -> 25.2 us  [routed(): lax.ppermute(x, RING, [(i, (i + step(i)) % size) for i in range(size) if...]
    ppermute x19, waiting for transfers between devices: 27.6 us -> 28.8 us  [routed(): lax.ppermute(x, RING, [(i, (i + step(i)) % size) for i in range(size) if...]
    unnamed x8 -> x12, local copies, waits for them, and re-layouts: 2.04 us -> 2.74 us
  transfers between devices with their start and end apart: 19 -> 19, of which waited for: 5 -> 9; matrix products, arithmetic and copies ran while one was open for 1% -> 1% of each run, Pallas kernels for 29% -> 30%
where the time goes in v16:
time: 85.6 us; the launch traced here: 85.3 us
  waiting for transfers between devices  28.8 us (34%)
  Pallas kernels  26.6 us (31%)
  starting transfers between devices  25.2 us (29%)
  local copies, waits for them, and re-layouts  2.83 us (3%)
  other arithmetic  0.96 us (1%)
  between operations  0.86 us (1%)
    ppermute x19, waiting for transfers between devices, routed(): lax.ppermute(x, RING, [(i, (i + step(i)) % size) for i in range(size) if...  28.8 us
    pallas_call x14, Pallas kernels, call(): pl.pallas_call(kernel, out_shape=[*outs, *[jax.ShapeDtypeStruct(a.shape,...  26.6 us
    ppermute x19, starting transfers between devices, routed(): lax.ppermute(x, RING, [(i, (i + step(i)) % size) for i in range(size) if...  25.2 us
    unnamed x12, local copies, waits for them, and re-layouts  2.74 us
  transfers between devices with their start and end apart: 19, of which 9 were waited for; matrix products, arithmetic and copies ran while one was open for 1% of the time, Pallas kernels for 30%

profile of v16, /device:TPU:1, one launch (start us, length us, event | category | flops | bytes accessed | tf_op | source)
XLA Modules:
  0.0 85.3 jit_solution(14090682202304806909)
XLA Ops:
  0.6 2.7 %collective-permute-start.2 = (bf16[4,8,128,128]{3,2,1,0:T(8,128)(2,1)}, bf16[4,8,128,128]{3,2,1,0:T(8,128)(2,1)S(1)}, u32[]{:S(2)}, u32[]{:S(2)}) collective-permute-start(bf16[4,8,128,128]{3,2,1,0:T(8,128)(2,1)} %own.2), channel_id=1, source_target_pairs={{0,15},{1,2},{2,1},{3,4},{4,3},{5,6},{6,5},{7,8},{8,7},{9,10},{10,... | collective-permute-start | bytes 3145736 | tf_op jit(solution)/shard_map/ppermute | solution.py:508
  3.3 2.9 %collective-permute-start.3 = (bf16[4,8,128,128]{3,2,1,0:T(8,128)(2,1)}, bf16[4,8,128,128]{3,2,1,0:T(8,128)(2,1)S(1)}, u32[]{:S(2)}, u32[]{:S(2)}) collective-permute-start(bf16[4,8,128,128]{3,2,1,0:T(8,128)(2,1)} %own.2), channel_id=1, source_target_pairs={{0,1},{1,0},{2,3},{3,2},{4,5},{5,4},{6,7},{7,6},{8,9},{9,8},{10,11... | collective-permute-start | bytes 3145736 | tf_op jit(solution)/shard_map/ppermute | solution.py:508
  8.4 2.2 %shard_map.51 = (bf16[2048,128]{1,0:T(8,128)(2,1)S(1)}, bf16[2048,128]{1,0:T(8,128)(2,1)}, bf16[3328,128]{1,0:T(8,128)(2,1)}, bf16[1280,128]{1,0:T(8,128)(2,1)S(1)}, bf16[1280,128]{1,0:T(8,128)(2,1)}) custom-call(s32[5]{0:T(128)S(1)} %pad_add_fusion.drop_ref, bf16[4,8,128,128]{3,2,1,0:T(8,128)(2,1)S(1)} %copy-done), custom_call_target="tpu_custom_call" | custom-call | bytes 3604480 | tf_op jit(solution)/shard_map/pallas_call | solution.py:494
  12.6 1.5 %collective-permute-done.1 = s32[4]{0:T(128)S(1)} collective-permute-done((s32[4]{0:T(128)S(1)}, s32[4]{0:T(128)S(1)}, u32[]{:S(2)}, u32[]{:S(2)}) %collective-permute-start.1) | collective-permute-done | bytes 48 | tf_op jit(solution)/shard_map/ppermute | solution.py:508
  14.1 2.1 %collective-permute-start.7 = (bf16[1280,128]{1,0:T(8,128)(2,1)}, bf16[1280,128]{1,0:T(8,128)(2,1)S(1)}, u32[]{:S(2)}, u32[]{:S(2)}) collective-permute-start(bf16[1280,128]{1,0:T(8,128)(2,1)} %copy-done.4), channel_id=1, source_target_pairs={{1,2},{2,1},{5,6},{6,5},{9,10},{10,9},{13,14},{14,13},{17,18},{18,... | collective-permute-start | bytes 983048 | tf_op jit(solution)/shard_map/ppermute | solution.py:508
  16.2 11.1 %collective-permute-done = s32[4]{0:T(128)S(1)} collective-permute-done((s32[4]{0:T(128)S(1)}, s32[4]{0:T(128)S(1)}, u32[]{:S(2)}, u32[]{:S(2)}) %collective-permute-start) | collective-permute-done | bytes 48 | tf_op jit(solution)/shard_map/ppermute | solution.py:508
  28.2 3.7 %collective-permute-start.6 = (bf16[1280,128]{1,0:T(8,128)(2,1)S(1)}, bf16[1280,128]{1,0:T(8,128)(2,1)S(1)}, u32[]{:S(2)}, u32[]{:S(2)}) collective-permute-start(bf16[1280,128]{1,0:T(8,128)(2,1)S(1)} %get-tuple-element.43), channel_id=1, source_target_pairs={{0,1},{1,0},{2,3},{3,2},{4,5},{5,4},{6,7},{7,6},{8,9},{9,8},{10,11... | collective-permute-start | bytes 983048 | tf_op jit(solution)/shard_map/ppermute | solution.py:508
  32.7 4.3 %shard_map.50 = (bf16[1536,1280]{1,0:T(8,128)(2,1)S(1)}, bf16[1536,1280]{1,0:T(8,128)(2,1)S(1)}, bf16[1024,512]{1,0:T(8,128)(2,1)S(1)}, bf16[1024,512]{1,0:T(8,128)(2,1)S(1)}, f32[1024,512]{1,0:T(8,128)S(1)}) custom-call(s32[14]{0:T(128)S(1)} %concatenate.6.drop_ref, bf16[4,8,128,128]{3,2,1,0:T(8,128)(2,1)S(1)} %copy-done.1, ...), custom_call_target="tpu_custom_call" | custom-call | tf_op jit(solution)/shard_map/pallas_call | solution.py:494
  37.9 1.4 %shard_map.53 = (bf16[1024,512]{1,0:T(8,128)(2,1)S(1)}, bf16[1024,512]{1,0:T(8,128)(2,1)S(1)}) custom-call(s32[14]{0:T(128)S(1)} %concatenate.6.drop_ref, bf16[1280,128]{1,0:T(8,128)(2,1)S(1)} %collective-permute-done.5.far_far, bf16[1280,128]{1,0:T(8,128)(2,1)S(1)} %collective-permute-done.6.far_mate, bf16[1024,512]{1,0:T(8,128)(2,1)S(1)} %get-tuple-element.44.reach, ...), custom_call_target="tpu_custom_call" | custom-call | tf_op jit(solution)/shard_map/pallas_call | solution.py:494
  39.4 3.7 %shard_map.54 = (bf16[1536,512]{1,0:T(8,128)(2,1)S(1)}, bf16[512,512]{1,0:T(8,128)(2,1)S(1)}, f32[1024,512]{1,0:T(8,128)S(1)}) custom-call(s32[14]{0:T(128)S(1)} %concatenate.6.drop_ref, bf16[1536,1280]{1,0:T(8,128)(2,1)S(1)} %get-tuple-element.38.shifted, bf16[1024,512]{1,0:T(8,128)(2,1)S(1)} %get-tuple-element.48.corners, bf16[2048,128]{1,0:T(8,128)(2,1)S(1)} %copy-done.3, ...), custom_call_target="tpu_custom_call" | custom-call | tf_op jit(solution)/shard_map/pallas_call | solution.py:494
  43.1 3.6 %collective-permute-start.13 = (bf16[512,512]{1,0:T(8,128)(2,1)S(1)}, bf16[512,512]{1,0:T(8,128)(2,1)S(1)}, u32[]{:S(2)}, u32[]{:S(2)}) collective-permute-start(bf16[512,512]{1,0:T(8,128)(2,1)S(1)} %get-tuple-element.51.own), channel_id=1, source_target_pairs={{0,15},{1,2},{2,1},{3,4},{4,3},{5,6},{6,5},{7,8},{8,7},{9,10},{10,... | collective-permute-start | bytes 1572872 | tf_op jit(solution)/shard_map/ppermute | solution.py:508
  46.7 2.8 %collective-permute-start.12 = (bf16[512,512]{1,0:T(8,128)(2,1)S(1)}, bf16[512,512]{1,0:T(8,128)(2,1)S(1)}, u32[]{:S(2)}, u32[]{:S(2)}) collective-permute-start(bf16[512,512]{1,0:T(8,128)(2,1)S(1)} %get-tuple-element.51.own), channel_id=1, source_target_pairs={{0,1},{1,0},{2,3},{3,2},{4,5},{5,4},{6,7},{7,6},{8,9},{9,8},{10,11... | collective-permute-start | bytes 1572872 | tf_op jit(solution)/shard_map/ppermute | solution.py:508
  52.0 2.8 %collective-permute-start.11 = (bf16[1280,128]{1,0:T(8,128)(2,1)S(1)}, bf16[1280,128]{1,0:T(8,128)(2,1)S(1)}, u32[]{:S(2)}, u32[]{:S(2)}) collective-permute-start(bf16[1280,128]{1,0:T(8,128)(2,1)S(1)} %get-tuple-element.56), channel_id=1, source_target_pairs={{0,1},{1,0},{2,3},{3,2},{4,5},{5,4},{6,7},{7,6},{8,9},{9,8},{10,11... | collective-permute-start | bytes 983048 | tf_op jit(solution)/shard_map/ppermute | solution.py:508
  54.8 2.0 %shard_map.56.correction = bf16[1536,512]{1,0:T(8,128)(2,1)S(1)} custom-call(s32[14]{0:T(128)S(1)} %concatenate.6.drop_ref, bf16[1536,1280]{1,0:T(8,128)(2,1)S(1)} %get-tuple-element.38.shifted, bf16[1024,512]{1,0:T(8,128)(2,1)S(1)} %get-tuple-element.48.corners, bf16[512,512]{1,0:T(8,128)(2,1)S(1)} %get-tuple-element.57.low, ...), custom_call_target="tpu_custom_call" | custom-call | flops 1275068416 | bytes 8126464 | tf_op jit(solution)/shard_map/pallas_call | solution.py:494
  56.8 8.6 %collective-permute-done.13.cross = bf16[512,512]{1,0:T(8,128)(2,1)S(1)} collective-permute-done((bf16[512,512]{1,0:T(8,128)(2,1)S(1)}, bf16[512,512]{1,0:T(8,128)(2,1)S(1)}, u32[]{:S(2)}, u32[]{:S(2)}) %collective-permute-start.13) | collective-permute-done | bytes 524320 | tf_op jit(solution)/shard_map/ppermute | solution.py:508
  65.4 1.5 %shard_map.57 = (bf16[512,512]{1,0:T(8,128)(2,1)S(1)}, bf16[512,512]{1,0:T(8,128)(2,1)S(1)}, bf16[1280,128]{1,0:T(8,128)(2,1)S(1)}, bf16[1280,128]{1,0:T(8,128)(2,1)S(1)}) custom-call(s32[14]{0:T(128)S(1)} %concatenate.6.drop_ref, bf16[512,512]{1,0:T(8,128)(2,1)S(1)} %collective-permute-done.12.mate, bf16[512,512]{1,0:T(8,128)(2,1)S(1)} %collective-permute-done.13.cross, ...), custom_call_target="tpu_custom_call" | custom-call | flops 671088640 | bytes 5373952 | tf_op jit(solution)/shard_map/pallas_call | solution.py:494
  67.0 1.9 %collective-permute-done.10.cross = bf16[1280,128]{1,0:T(8,128)(2,1)S(1)} collective-permute-done((bf16[1280,128]{1,0:T(8,128)(2,1)S(1)}, bf16[1280,128]{1,0:T(8,128)(2,1)S(1)}, u32[]{:S(2)}, u32[]{:S(2)}) %collective-permute-start.10) | collective-permute-done | bytes 327712 | tf_op jit(solution)/shard_map/ppermute | solution.py:508
  68.9 2.2 %shard_map.58 = (bf16[1536,512]{1,0:T(8,128)(2,1)S(1)}, bf16[1280,128]{1,0:T(8,128)(2,1)S(1)}, bf16[640,128]{1,0:T(8,128)(2,1)S(1)}, bf16[640,128]{1,0:T(8,128)(2,1)S(1)}) custom-call(s32[14]{0:T(128)S(1)} %concatenate.6.drop_ref, bf16[512,512]{1,0:T(8,128)(2,1)S(1)} %get-tuple-element.51.own, bf16[1280,128]{1,0:T(8,128)(2,1)S(1)} %collective-permute-done.10.cross, ...), custom_call_target="tpu_custom_call" | custom-call | flops 1275068416 | bytes 11010048 | tf_op jit(solution)/shard_map/pallas_call | solution.py:494
  71.1 3.0 %collective-permute-start.14 = (bf16[640,128]{1,0:T(8,128)(2,1)S(1)}, bf16[640,128]{1,0:T(8,128)(2,1)S(1)}, u32[]{:S(2)}, u32[]{:S(2)}) collective-permute-start(bf16[640,128]{1,0:T(8,128)(2,1)S(1)} %get-tuple-element.63), channel_id=1, source_target_pairs={{0,1},{1,0},{2,3},{3,2},{4,5},{5,4},{6,7},{7,6},{8,9},{9,8},{10,11... | collective-permute-start | bytes 491528 | tf_op jit(solution)/shard_map/ppermute | solution.py:508
  74.1 1.3 %shard_map.59.own = bf16[512,512]{1,0:T(8,128)(2,1)S(1)} custom-call(s32[14]{0:T(128)S(1)} %concatenate.6.drop_ref, bf16[1536,1280]{1,0:T(8,128)(2,1)S(1)} %get-tuple-element.37.square, bf16[1536,512]{1,0:T(8,128)(2,1)S(1)} %get-tuple-element.62.whole.own), custom_call_target="tpu_custom_call" | custom-call | flops 603979776 | bytes 6029312 | tf_op jit(solution)/shard_map/pallas_call | solution.py:494
  75.5 1.7 %shard_map.60 = (bf16[4,8,128,128]{3,2,1,0:T(8,128)(2,1)S(1)}, bf16[4,8,128,128]{3,2,1,0:T(8,128)(2,1)}) custom-call(s32[14]{0:T(128)S(1)} %concatenate.6.drop_ref, bf16[512,512]{1,0:T(8,128)(2,1)S(1)} %shard_map.59.own, bf16[640,128]{1,0:T(8,128)(2,1)S(1)} %collective-permute-done.14.refs_0_, bf16[640,128]{1,0:T(8,128)(2,1)S(1)} %collective-permute-done.15.refs_1_), custom_call_target="tpu_custom_call" | custom-call | tf_op jit(solution)/shard_map/pallas_call | solution.py:494
  77.2 1.7 %shard_map.62 = (bf16[4,8,128,128]{3,2,1,0:T(8,128)(2,1)S(1)}, bf16[4,8,128,128]{3,2,1,0:T(8,128)(2,1)}) custom-call(s32[14]{0:T(128)S(1)} %concatenate.6.drop_ref, bf16[1536,512]{1,0:T(8,128)(2,1)S(1)} %get-tuple-element.62.whole.own, bf16[1280,128]{1,0:T(8,128)(2,1)S(1)} %collective-permute-done.17.refs_0_), custom_call_target="tpu_custom_call" | custom-call | tf_op jit(solution)/shard_map/pallas_call | solution.py:494
  79.0 1.5 %collective-permute-done.18.cross = bf16[1280,128]{1,0:T(8,128)(2,1)S(1)} collective-permute-done((bf16[1280,128]{1,0:T(8,128)(2,1)S(1)}, bf16[1280,128]{1,0:T(8,128)(2,1)S(1)}, u32[]{:S(2)}, u32[]{:S(2)}) %collective-permute-start.18) | collective-permute-done | bytes 327712 | tf_op jit(solution)/shard_map/ppermute | solution.py:508
  81.8 2.2 %collective-permute-done.16.cross = bf16[1280,128]{1,0:T(8,128)(2,1)S(1)} collective-permute-done((bf16[1280,128]{1,0:T(8,128)(2,1)S(1)}, bf16[1280,128]{1,0:T(8,128)(2,1)S(1)}, u32[]{:S(2)}, u32[]{:S(2)}) %collective-permute-start.16) | collective-permute-done | bytes 327712 | tf_op jit(solution)/shard_map/ppermute | solution.py:508
  (46 shorter events, 12.2 us)
Async XLA Ops:
  0.6 26.8 %collective-permute-start.2 = (bf16[4,8,128,128]{3,2,1,0:T(8,128)(2,1)}, bf16[4,8,128,128]{3,2,1,0:T(8,128)(2,1)S(1)}, u32[]{:S(2)}, u32[]{:S(2)}) collective-permute-start(bf16[4,8,128,128]{3,2,1,0:T(8,128)(2,1)} %own.2), channel_id=1, source_target_pairs={{0,15},{1,2},{2,1},{3,4},{4,3},{5,6},{6,5},{7,8},{8,7},{9,10},{10,... | collective-permute-start | bytes 3145736 | tf_op jit(solution)/shard_map/ppermute | solution.py:508
  3.3 24.1 %collective-permute-start.3 = (bf16[4,8,128,128]{3,2,1,0:T(8,128)(2,1)}, bf16[4,8,128,128]{3,2,1,0:T(8,128)(2,1)S(1)}, u32[]{:S(2)}, u32[]{:S(2)}) collective-permute-start(bf16[4,8,128,128]{3,2,1,0:T(8,128)(2,1)} %own.2), channel_id=1, source_target_pairs={{0,1},{1,0},{2,3},{3,2},{4,5},{5,4},{6,7},{7,6},{8,9},{9,8},{10,11... | collective-permute-start | bytes 3145736 | tf_op jit(solution)/shard_map/ppermute | solution.py:508
  7.1 1.2 %copy-start = (bf16[4,8,128,128]{3,2,1,0:T(8,128)(2,1)S(1)}, bf16[4,8,128,128]{3,2,1,0:T(8,128)(2,1)}, u32[]{:S(2)}) copy-start(bf16[4,8,128,128]{3,2,1,0:T(8,128)(2,1)} %own.3) | copy-start | bytes 3145732
  10.5 0.8 copy-start.2
  12.0 15.3 %collective-permute-start.4 = (bf16[3328,128]{1,0:T(8,128)(2,1)}, bf16[3328,128]{1,0:T(8,128)(2,1)S(1)}, u32[]{:S(2)}, u32[]{:S(2)}) collective-permute-start(bf16[3328,128]{1,0:T(8,128)(2,1)} %get-tuple-element.39.sent_mate), channel_id=1, source_target_pairs={{0,1},{1,0},{2,3},{3,2},{4,5},{5,4},{6,7},{7,6},{8,9},{9,8},{10,11... | collective-permute-start | bytes 2555912 | tf_op jit(solution)/shard_map/ppermute | solution.py:508
  12.0 2.0 %collective-permute-start.1 = (s32[4]{0:T(128)S(1)}, s32[4]{0:T(128)S(1)}, u32[]{:S(2)}, u32[]{:S(2)}) collective-permute-start(s32[4]{0:T(128)S(1)} %broadcast_subtract_fusion), channel_id=1, source_target_pairs={{0,1},{1,0},{2,3},{3,2},{4,5},{5,4},{6,7},{7,6},{8,9},{9,8},{10,11... | collective-permute-start | bytes 56 | tf_op jit(solution)/shard_map/ppermute | solution.py:508
  12.6 14.7 %collective-permute-start = (s32[4]{0:T(128)S(1)}, s32[4]{0:T(128)S(1)}, u32[]{:S(2)}, u32[]{:S(2)}) collective-permute-start(s32[4]{0:T(128)S(1)} %broadcast_subtract_fusion), channel_id=1, source_target_pairs={{0,15},{1,2},{2,1},{3,4},{4,3},{5,6},{6,5},{7,8},{8,7},{9,10},{10,... | collective-permute-start | bytes 56 | tf_op jit(solution)/shard_map/ppermute | solution.py:508
  14.1 22.9 %collective-permute-start.7 = (bf16[1280,128]{1,0:T(8,128)(2,1)}, bf16[1280,128]{1,0:T(8,128)(2,1)S(1)}, u32[]{:S(2)}, u32[]{:S(2)}) collective-permute-start(bf16[1280,128]{1,0:T(8,128)(2,1)} %copy-done.4), channel_id=1, source_target_pairs={{1,2},{2,1},{5,6},{6,5},{9,10},{10,9},{13,14},{14,13},{17,18},{18,... | collective-permute-start | bytes 983048 | tf_op jit(solution)/shard_map/ppermute | solution.py:508
  27.4 5.3 %copy-start.1 = (bf16[4,8,128,128]{3,2,1,0:T(8,128)(2,1)S(1)}, bf16[4,8,128,128]{3,2,1,0:T(8,128)(2,1)}, u32[]{:S(2)}) copy-start(bf16[4,8,128,128]{3,2,1,0:T(8,128)(2,1)} %own.2) | copy-start | bytes 3145732
  28.1 9.8 %collective-permute-start.5 = (bf16[1280,128]{1,0:T(8,128)(2,1)S(1)}, bf16[1280,128]{1,0:T(8,128)(2,1)S(1)}, u32[]{:S(2)}, u32[]{:S(2)}) collective-permute-start(bf16[1280,128]{1,0:T(8,128)(2,1)S(1)} %get-tuple-element.42), channel_id=1, source_target_pairs={{0,13},{1,4},{2,15},{3,6},{4,1},{5,8},{6,3},{7,10},{8,5},{9,12},{1... | collective-permute-start | bytes 983048 | tf_op jit(solution)/shard_map/ppermute | solution.py:508
  28.2 9.7 %collective-permute-start.6 = (bf16[1280,128]{1,0:T(8,128)(2,1)S(1)}, bf16[1280,128]{1,0:T(8,128)(2,1)S(1)}, u32[]{:S(2)}, u32[]{:S(2)}) collective-permute-start(bf16[1280,128]{1,0:T(8,128)(2,1)S(1)} %get-tuple-element.43), channel_id=1, source_target_pairs={{0,1},{1,0},{2,3},{3,2},{4,5},{5,4},{6,7},{7,6},{8,9},{9,8},{10,11... | collective-permute-start | bytes 983048 | tf_op jit(solution)/shard_map/ppermute | solution.py:508
  31.9 7.4 %collective-permute-start.8 = (bf16[1280,128]{1,0:T(8,128)(2,1)}, bf16[1280,128]{1,0:T(8,128)(2,1)S(1)}, u32[]{:S(2)}, u32[]{:S(2)}) collective-permute-start(bf16[1280,128]{1,0:T(8,128)(2,1)} %get-tuple-element.50), channel_id=1, source_target_pairs={{0,15},{3,4},{4,3},{7,8},{8,7},{11,12},{12,11},{15,0},{16,31},{19,... | collective-permute-start | bytes 983048 | tf_op jit(solution)/shard_map/ppermute | solution.py:508
  32.6 18.0 %collective-permute-start.9 = (bf16[2048,128]{1,0:T(8,128)(2,1)}, bf16[2048,128]{1,0:T(8,128)(2,1)S(1)}, u32[]{:S(2)}, u32[]{:S(2)}) collective-permute-start(bf16[2048,128]{1,0:T(8,128)(2,1)} %get-tuple-element.52), channel_id=1, source_target_pairs={{0,15},{1,2},{2,1},{3,4},{4,3},{5,6},{6,5},{7,8},{8,7},{9,10},{10,... | collective-permute-start | bytes 1572872 | tf_op jit(solution)/shard_map/ppermute | solution.py:508
  37.9 1.4 %copy-start.3 = (bf16[2048,128]{1,0:T(8,128)(2,1)S(1)}, bf16[2048,128]{1,0:T(8,128)(2,1)}, u32[]{:S(2)}) copy-start(bf16[2048,128]{1,0:T(8,128)(2,1)} %copy-done.2) | copy-start | bytes 1572868
  37.9 1.4 %copy-start.5 = (bf16[1280,128]{1,0:T(8,128)(2,1)S(1)}, bf16[1280,128]{1,0:T(8,128)(2,1)}, u32[]{:S(2)}) copy-start(bf16[1280,128]{1,0:T(8,128)(2,1)} %copy-done.4) | copy-start | bytes 983044
  43.1 22.3 %collective-permute-start.13 = (bf16[512,512]{1,0:T(8,128)(2,1)S(1)}, bf16[512,512]{1,0:T(8,128)(2,1)S(1)}, u32[]{:S(2)}, u32[]{:S(2)}) collective-permute-start(bf16[512,512]{1,0:T(8,128)(2,1)S(1)} %get-tuple-element.51.own), channel_id=1, source_target_pairs={{0,15},{1,2},{2,1},{3,4},{4,3},{5,6},{6,5},{7,8},{8,7},{9,10},{10,... | collective-permute-start | bytes 1572872 | tf_op jit(solution)/shard_map/ppermute | solution.py:508
  46.7 18.7 %collective-permute-start.12 = (bf16[512,512]{1,0:T(8,128)(2,1)S(1)}, bf16[512,512]{1,0:T(8,128)(2,1)S(1)}, u32[]{:S(2)}, u32[]{:S(2)}) collective-permute-start(bf16[512,512]{1,0:T(8,128)(2,1)S(1)} %get-tuple-element.51.own), channel_id=1, source_target_pairs={{0,1},{1,0},{2,3},{3,2},{4,5},{5,4},{6,7},{7,6},{8,9},{9,8},{10,11... | collective-permute-start | bytes 1572872 | tf_op jit(solution)/shard_map/ppermute | solution.py:508
  51.9 16.9 %collective-permute-start.10 = (bf16[1280,128]{1,0:T(8,128)(2,1)S(1)}, bf16[1280,128]{1,0:T(8,128)(2,1)S(1)}, u32[]{:S(2)}, u32[]{:S(2)}) collective-permute-start(bf16[1280,128]{1,0:T(8,128)(2,1)S(1)} %get-tuple-element.55), channel_id=1, source_target_pairs={{0,15},{1,2},{2,1},{3,4},{4,3},{5,6},{6,5},{7,8},{8,7},{9,10},{10,... | collective-permute-start | bytes 983048 | tf_op jit(solution)/shard_map/ppermute | solution.py:508
  52.0 16.9 %collective-permute-start.11 = (bf16[1280,128]{1,0:T(8,128)(2,1)S(1)}, bf16[1280,128]{1,0:T(8,128)(2,1)S(1)}, u32[]{:S(2)}, u32[]{:S(2)}) collective-permute-start(bf16[1280,128]{1,0:T(8,128)(2,1)S(1)} %get-tuple-element.56), channel_id=1, source_target_pairs={{0,1},{1,0},{2,3},{3,2},{4,5},{5,4},{6,7},{7,6},{8,9},{9,8},{10,11... | collective-permute-start | bytes 983048 | tf_op jit(solution)/shard_map/ppermute | solution.py:508
  66.8 10.4 %collective-permute-start.17 = (bf16[1280,128]{1,0:T(8,128)(2,1)S(1)}, bf16[1280,128]{1,0:T(8,128)(2,1)S(1)}, u32[]{:S(2)}, u32[]{:S(2)}) collective-permute-start(bf16[1280,128]{1,0:T(8,128)(2,1)S(1)} %get-tuple-element.68), channel_id=1, source_target_pairs={{0,1},{1,0},{2,3},{3,2},{4,5},{5,4},{6,7},{7,6},{8,9},{9,8},{10,11... | collective-permute-start | bytes 983048 | tf_op jit(solution)/shard_map/ppermute | solution.py:508
  66.9 13.6 %collective-permute-start.18 = (bf16[1280,128]{1,0:T(8,128)(2,1)S(1)}, bf16[1280,128]{1,0:T(8,128)(2,1)S(1)}, u32[]{:S(2)}, u32[]{:S(2)}) collective-permute-start(bf16[1280,128]{1,0:T(8,128)(2,1)S(1)} %get-tuple-element.70), channel_id=1, source_target_pairs={{0,15},{1,2},{2,1},{3,4},{4,3},{5,6},{6,5},{7,8},{8,7},{9,10},{10,... | collective-permute-start | bytes 983048 | tf_op jit(solution)/shard_map/ppermute | solution.py:508
  71.0 13.0 %collective-permute-start.16 = (bf16[1280,128]{1,0:T(8,128)(2,1)S(1)}, bf16[1280,128]{1,0:T(8,128)(2,1)S(1)}, u32[]{:S(2)}, u32[]{:S(2)}) collective-permute-start(bf16[1280,128]{1,0:T(8,128)(2,1)S(1)} %get-tuple-element.66), channel_id=1, source_target_pairs={{0,15},{1,2},{2,1},{3,4},{4,3},{5,6},{6,5},{7,8},{8,7},{9,10},{10,... | collective-permute-start | bytes 983048 | tf_op jit(solution)/shard_map/ppermute | solution.py:508
  71.1 4.3 %collective-permute-start.14 = (bf16[640,128]{1,0:T(8,128)(2,1)S(1)}, bf16[640,128]{1,0:T(8,128)(2,1)S(1)}, u32[]{:S(2)}, u32[]{:S(2)}) collective-permute-start(bf16[640,128]{1,0:T(8,128)(2,1)S(1)} %get-tuple-element.63), channel_id=1, source_target_pairs={{0,1},{1,0},{2,3},{3,2},{4,5},{5,4},{6,7},{7,6},{8,9},{9,8},{10,11... | collective-permute-start | bytes 491528 | tf_op jit(solution)/shard_map/ppermute | solution.py:508
  74.1 1.4 %collective-permute-start.15 = (bf16[640,128]{1,0:T(8,128)(2,1)S(1)}, bf16[640,128]{1,0:T(8,128)(2,1)S(1)}, u32[]{:S(2)}, u32[]{:S(2)}) collective-permute-start(bf16[640,128]{1,0:T(8,128)(2,1)S(1)} %get-tuple-element.64), channel_id=1, source_target_pairs={{0,1},{1,0},{2,3},{3,2},{4,5},{5,4},{6,7},{7,6},{8,9},{9,8},{10,11... | collective-permute-start | bytes 491528 | tf_op jit(solution)/shard_map/ppermute | solution.py:508
  (1 other events, 0.7 us)

commit v17 on v15

--- a/solution.py
+++ b/solution.py
@@ -369,7 +369,7 @@
 
 
 def density_edges_kernel(
-    f, drop_ref, own, cross, mate, correction, new_low, new_high, square, corners, whole, to_cross, to_mate,
+    f, drop_ref, own, mate, cross, correction, new_low, new_high, square, corners, whole, to_cross, to_mate,
     to_mate_too, before, after, low, high,
 ):
     h, p = f.h, f.p
@@ -607,7 +607,7 @@
         density_edges_kernel,
         [columns, triangle, half_triangle, half_triangle],
         [group_scratch] * 4,
-        38, 20, drop, own, edge_cross, edge_mate, correction, new_low, new_high, square,
+        38, 20, drop, own, edge_mate, edge_cross, correction, new_low, new_high, square,
         square_corners,
     )
     rim_cross, rim_mates = to_cross(rim_cross), [to_mate(rim_mate), to_mate(rim_mate_too)]

time: 85 us -> 85 us (level)
  starting transfers between devices: 26.5 us -> 24.5 us
  waiting for transfers between devices: 27.6 us -> 29.6 us
    ppermute x19, starting transfers between devices: 26.5 us -> 24.5 us  [routed(): lax.ppermute(x, RING, [(i, (i + step(i)) % size) for i in range(size) if...]
    ppermute x19, waiting for transfers between devices: 27.6 us -> 29.6 us  [routed(): lax.ppermute(x, RING, [(i, (i + step(i)) % size) for i in range(size) if...]
where the time goes in v17:
time: 85 us; the launch traced here: 84.8 us
  waiting for transfers between devices  29.6 us (35%)
  Pallas kernels  26.7 us (31%)
  starting transfers between devices  24.5 us (29%)
  local copies, waits for them, and re-layouts  2.04 us (2%)
  other arithmetic  1.04 us (1%)
    ppermute x19, waiting for transfers between devices, routed(): lax.ppermute(x, RING, [(i, (i + step(i)) % size) for i in range(size) if...  29.6 us
    pallas_call x14, Pallas kernels, call(): pl.pallas_call(kernel, out_shape=[*outs, *[jax.ShapeDtypeStruct(a.shape,...  26.7 us
    ppermute x19, starting transfers between devices, routed(): lax.ppermute(x, RING, [(i, (i + step(i)) % size) for i in range(size) if...  24.5 us
    unnamed x8, local copies, waits for them, and re-layouts  2.04 us
  transfers between devices with their start and end apart: 19, of which 5 were waited for; matrix products, arithmetic and copies ran while one was open for 1% of the time, Pallas kernels for 29%

profile of v17, /device:TPU:1, one launch (start us, length us, event | category | flops | bytes accessed | tf_op | source)
XLA Modules:
  0.0 84.8 jit_solution(10316287282254354169)
XLA Ops:
  0.6 2.7 %collective-permute-start.2 = (bf16[4,8,128,128]{3,2,1,0:T(8,128)(2,1)}, bf16[4,8,128,128]{3,2,1,0:T(8,128)(2,1)S(1)}, u32[]{:S(2)}, u32[]{:S(2)}) collective-permute-start(bf16[4,8,128,128]{3,2,1,0:T(8,128)(2,1)} %own.2), channel_id=1, source_target_pairs={{0,15},{1,2},{2,1},{3,4},{4,3},{5,6},{6,5},{7,8},{8,7},{9,10},{10,... | collective-permute-start | bytes 3145736 | tf_op jit(solution)/shard_map/ppermute | solution.py:502
  3.3 2.9 %collective-permute-start.3 = (bf16[4,8,128,128]{3,2,1,0:T(8,128)(2,1)}, bf16[4,8,128,128]{3,2,1,0:T(8,128)(2,1)S(1)}, u32[]{:S(2)}, u32[]{:S(2)}) collective-permute-start(bf16[4,8,128,128]{3,2,1,0:T(8,128)(2,1)} %own.2), channel_id=1, source_target_pairs={{0,1},{1,0},{2,3},{3,2},{4,5},{5,4},{6,7},{7,6},{8,9},{9,8},{10,11... | collective-permute-start | bytes 3145736 | tf_op jit(solution)/shard_map/ppermute | solution.py:502
  8.4 2.1 %shard_map.51 = (bf16[2048,128]{1,0:T(8,128)(2,1)S(1)}, bf16[2048,128]{1,0:T(8,128)(2,1)}, bf16[3328,128]{1,0:T(8,128)(2,1)}, bf16[1280,128]{1,0:T(8,128)(2,1)S(1)}) custom-call(s32[5]{0:T(128)S(1)} %pad_add_fusion.1.drop_ref, bf16[4,8,128,128]{3,2,1,0:T(8,128)(2,1)S(1)} %copy-done), custom_call_target="tpu_custom_call" | custom-call | bytes 3276800 | tf_op jit(solution)/shard_map/pallas_call | solution.py:488
  12.0 15.3 %collective-permute-done = s32[4]{0:T(128)S(1)} collective-permute-done((s32[4]{0:T(128)S(1)}, s32[4]{0:T(128)S(1)}, u32[]{:S(2)}, u32[]{:S(2)}) %collective-permute-start) | collective-permute-done | bytes 48 | tf_op jit(solution)/shard_map/ppermute | solution.py:502
  28.2 1.8 %collective-permute-start.8 = (bf16[1280,128]{1,0:T(8,128)(2,1)S(1)}, bf16[1280,128]{1,0:T(8,128)(2,1)S(1)}, u32[]{:S(2)}, u32[]{:S(2)}) collective-permute-start(bf16[1280,128]{1,0:T(8,128)(2,1)S(1)} %get-tuple-element.50.sent_cross), channel_id=1, source_target_pairs={{0,15},{1,2},{2,1},{3,4},{4,3},{5,6},{6,5},{7,8},{8,7},{9,10},{10,... | collective-permute-start | bytes 983048 | tf_op jit(solution)/shard_map/ppermute | solution.py:502
  30.1 6.3 %collective-permute-start.6 = (bf16[640,128]{1,0:T(8,128)(2,1)S(1)}, bf16[640,128]{1,0:T(8,128)(2,1)S(1)}, u32[]{:S(2)}, u32[]{:S(2)}) collective-permute-start(bf16[640,128]{1,0:T(8,128)(2,1)S(1)} %get-tuple-element.43), channel_id=1, source_target_pairs={{0,1},{1,0},{2,3},{3,2},{4,5},{5,4},{6,7},{7,6},{8,9},{9,8},{10,11... | collective-permute-start | bytes 491528 | tf_op jit(solution)/shard_map/ppermute | solution.py:502
  36.4 4.3 %shard_map.50 = (bf16[1536,1280]{1,0:T(8,128)(2,1)S(1)}, bf16[1536,1280]{1,0:T(8,128)(2,1)S(1)}, bf16[1024,512]{1,0:T(8,128)(2,1)S(1)}, bf16[1024,512]{1,0:T(8,128)(2,1)S(1)}, f32[1024,512]{1,0:T(8,128)S(1)}) custom-call(s32[13]{0:T(128)S(1)} %pad_add_fusion.drop_ref, bf16[4,8,128,128]{3,2,1,0:T(8,128)(2,1)S(1)} %copy-done.3, ...), custom_call_target="tpu_custom_call" | custom-call | flops 2818572288 | bytes 15204352 | tf_op jit(solution)/shard_map/pallas_call | solution.py:488
  40.7 1.4 %shard_map.53 = (bf16[1024,512]{1,0:T(8,128)(2,1)S(1)}, bf16[1024,512]{1,0:T(8,128)(2,1)S(1)}) custom-call(s32[13]{0:T(128)S(1)} %pad_add_fusion.drop_ref, bf16[1280,128]{1,0:T(8,128)(2,1)S(1)} %collective-permute-done.5.far_far, bf16[640,128]{1,0:T(8,128)(2,1)S(1)} %collective-permute-done.6.far_mate, ...), custom_call_target="tpu_custom_call" | custom-call | tf_op jit(solution)/shard_map/pallas_call | solution.py:488
  42.1 3.8 %shard_map.54 = (bf16[1536,512]{1,0:T(8,128)(2,1)S(1)}, bf16[512,512]{1,0:T(8,128)(2,1)S(1)}, f32[1024,512]{1,0:T(8,128)S(1)}) custom-call(s32[13]{0:T(128)S(1)} %pad_add_fusion.drop_ref, bf16[1536,1280]{1,0:T(8,128)(2,1)S(1)} %get-tuple-element.38.shifted, bf16[1024,512]{1,0:T(8,128)(2,1)S(1)} %get-tuple-element.48.corners, ...), custom_call_target="tpu_custom_call" | custom-call | tf_op jit(solution)/shard_map/pallas_call | solution.py:488
  46.8 2.2 %collective-permute-start.13 = (bf16[512,512]{1,0:T(8,128)(2,1)S(1)}, bf16[512,512]{1,0:T(8,128)(2,1)S(1)}, u32[]{:S(2)}, u32[]{:S(2)}) collective-permute-start(bf16[512,512]{1,0:T(8,128)(2,1)S(1)} %get-tuple-element.51.own), channel_id=1, source_target_pairs={{0,1},{1,0},{2,3},{3,2},{4,5},{5,4},{6,7},{7,6},{8,9},{9,8},{10,11... | collective-permute-start | bytes 1572872 | tf_op jit(solution)/shard_map/ppermute | solution.py:502
  49.0 1.3 %shard_map.55 = (bf16[512,512]{1,0:T(8,128)(2,1)S(1)}, bf16[512,512]{1,0:T(8,128)(2,1)S(1)}, bf16[1280,128]{1,0:T(8,128)(2,1)S(1)}, bf16[1280,128]{1,0:T(8,128)(2,1)S(1)}) custom-call(s32[13]{0:T(128)S(1)} %pad_add_fusion.drop_ref, bf16[3328,128]{1,0:T(8,128)(2,1)S(1)} %collective-permute-done.4.refs_1_.mate, ...), custom_call_target="tpu_custom_call" | custom-call | flops 335544320 | bytes 6750208 | tf_op jit(solution)/shard_map/pallas_call | solution.py:488
  50.4 1.9 %collective-permute-start.10 = (bf16[1280,128]{1,0:T(8,128)(2,1)S(1)}, bf16[1280,128]{1,0:T(8,128)(2,1)S(1)}, u32[]{:S(2)}, u32[]{:S(2)}) collective-permute-start(bf16[1280,128]{1,0:T(8,128)(2,1)S(1)} %get-tuple-element.55), channel_id=1, source_target_pairs={{0,1},{1,0},{2,3},{3,2},{4,5},{5,4},{6,7},{7,6},{8,9},{9,8},{10,11... | collective-permute-start | bytes 983048 | tf_op jit(solution)/shard_map/ppermute | solution.py:502
  52.7 2.0 %shard_map.56.correction = bf16[1536,512]{1,0:T(8,128)(2,1)S(1)} custom-call(s32[13]{0:T(128)S(1)} %pad_add_fusion.drop_ref, bf16[1536,1280]{1,0:T(8,128)(2,1)S(1)} %get-tuple-element.38.shifted, bf16[1024,512]{1,0:T(8,128)(2,1)S(1)} %get-tuple-element.48.corners, bf16[512,512]{1,0:T(8,128)(2,1)S(1)} %get-tuple-element.57.low, ...), custom_call_target="tpu_custom_call" | custom-call | flops 1275068416 | bytes 8126464 | tf_op jit(solution)/shard_map/pallas_call | solution.py:488
  54.7 10.0 %collective-permute-done.12.cross = bf16[512,512]{1,0:T(8,128)(2,1)S(1)} collective-permute-done((bf16[512,512]{1,0:T(8,128)(2,1)S(1)}, bf16[512,512]{1,0:T(8,128)(2,1)S(1)}, u32[]{:S(2)}, u32[]{:S(2)}) %collective-permute-start.12) | collective-permute-done | bytes 524320 | tf_op jit(solution)/shard_map/ppermute | solution.py:502
  64.8 1.5 %shard_map.57 = (bf16[512,512]{1,0:T(8,128)(2,1)S(1)}, bf16[512,512]{1,0:T(8,128)(2,1)S(1)}, bf16[1280,128]{1,0:T(8,128)(2,1)S(1)}, bf16[1280,128]{1,0:T(8,128)(2,1)S(1)}) custom-call(s32[13]{0:T(128)S(1)} %pad_add_fusion.drop_ref, bf16[512,512]{1,0:T(8,128)(2,1)S(1)} %collective-permute-done.12.cross, bf16[512,512]{1,0:T(8,128)(2,1)S(1)} %collective-permute-done.13.mate, ...), custom_call_target="tpu_custom_call" | custom-call | flops 671088640 | bytes 5373952 | tf_op jit(solution)/shard_map/pallas_call | solution.py:488
  66.3 1.3 %collective-permute-start.18 = (bf16[1280,128]{1,0:T(8,128)(2,1)S(1)}, bf16[1280,128]{1,0:T(8,128)(2,1)S(1)}, u32[]{:S(2)}, u32[]{:S(2)}) collective-permute-start(bf16[1280,128]{1,0:T(8,128)(2,1)S(1)} %get-tuple-element.70), channel_id=1, source_target_pairs={{0,15},{1,2},{2,1},{3,4},{4,3},{5,6},{6,5},{7,8},{8,7},{9,10},{10,... | collective-permute-start | bytes 983048 | tf_op jit(solution)/shard_map/ppermute | solution.py:502
  68.3 2.3 %shard_map.58 = (bf16[1536,512]{1,0:T(8,128)(2,1)S(1)}, bf16[1280,128]{1,0:T(8,128)(2,1)S(1)}, bf16[640,128]{1,0:T(8,128)(2,1)S(1)}, bf16[640,128]{1,0:T(8,128)(2,1)S(1)}) custom-call(s32[13]{0:T(128)S(1)} %pad_add_fusion.drop_ref, bf16[512,512]{1,0:T(8,128)(2,1)S(1)} %get-tuple-element.51.own, bf16[1280,128]{1,0:T(8,128)(2,1)S(1)} %collective-permute-done.10.mate, ...), custom_call_target="tpu_custom_call" | custom-call | flops 1275068416 | bytes 11010048 | tf_op jit(solution)/shard_map/pallas_call | solution.py:488
  71.8 1.8 %collective-permute-start.14 = (bf16[640,128]{1,0:T(8,128)(2,1)S(1)}, bf16[640,128]{1,0:T(8,128)(2,1)S(1)}, u32[]{:S(2)}, u32[]{:S(2)}) collective-permute-start(bf16[640,128]{1,0:T(8,128)(2,1)S(1)} %get-tuple-element.63), channel_id=1, source_target_pairs={{0,1},{1,0},{2,3},{3,2},{4,5},{5,4},{6,7},{7,6},{8,9},{9,8},{10,11... | collective-permute-start | bytes 491528 | tf_op jit(solution)/shard_map/ppermute | solution.py:502
  73.6 1.3 %shard_map.59.own = bf16[512,512]{1,0:T(8,128)(2,1)S(1)} custom-call(s32[13]{0:T(128)S(1)} %pad_add_fusion.drop_ref, bf16[1536,1280]{1,0:T(8,128)(2,1)S(1)} %get-tuple-element.37.square, bf16[1536,512]{1,0:T(8,128)(2,1)S(1)} %get-tuple-element.62.whole.own), custom_call_target="tpu_custom_call" | custom-call | flops 603979776 | bytes 6029312 | tf_op jit(solution)/shard_map/pallas_call | solution.py:488
  75.0 1.7 %shard_map.60 = (bf16[4,8,128,128]{3,2,1,0:T(8,128)(2,1)S(1)}, bf16[4,8,128,128]{3,2,1,0:T(8,128)(2,1)}) custom-call(s32[13]{0:T(128)S(1)} %pad_add_fusion.drop_ref, bf16[512,512]{1,0:T(8,128)(2,1)S(1)} %shard_map.59.own, bf16[640,128]{1,0:T(8,128)(2,1)S(1)} %collective-permute-done.14.refs_0_, bf16[640,128]{1,0:T(8,128)(2,1)S(1)} %collective-permute-done.15.refs_1_), custom_call_target="tpu_custom_call" | custom-call | tf_op jit(solution)/shard_map/pallas_call | solution.py:488
  76.7 1.7 %shard_map.62 = (bf16[4,8,128,128]{3,2,1,0:T(8,128)(2,1)S(1)}, bf16[4,8,128,128]{3,2,1,0:T(8,128)(2,1)}) custom-call(s32[13]{0:T(128)S(1)} %pad_add_fusion.drop_ref, bf16[1536,512]{1,0:T(8,128)(2,1)S(1)} %get-tuple-element.62.whole.own, bf16[1280,128]{1,0:T(8,128)(2,1)S(1)} %collective-permute-done.17.refs_0_), custom_call_target="tpu_custom_call" | custom-call | tf_op jit(solution)/shard_map/pallas_call | solution.py:488
  78.7 1.3 %shard_map.63 = bf16[4,8,128,128]{3,2,1,0:T(8,128)(2,1)} custom-call(s32[13]{0:T(128)S(1)} %pad_add_fusion.drop_ref, bf16[4,8,128,128]{3,2,1,0:T(8,128)(2,1)S(1)} %get-tuple-element.69.slots, bf16[1280,128]{1,0:T(8,128)(2,1)S(1)} %collective-permute-done.18.cross, bf16[4,8,128,128]{3,2,1,0:T(8,128)(2,1)} %get-tuple-element.71.unused), custom_call_target="tpu_custom_call", output_to_operand_aliasing={{}: (3, {})} | custom-call | tf_op jit(solution)/shard_map/pallas_call | solution.py:488
  80.0 3.4 %collective-permute-done.16.cross = bf16[1280,128]{1,0:T(8,128)(2,1)S(1)} collective-permute-done((bf16[1280,128]{1,0:T(8,128)(2,1)S(1)}, bf16[1280,128]{1,0:T(8,128)(2,1)S(1)}, u32[]{:S(2)}, u32[]{:S(2)}) %collective-permute-start.16) | collective-permute-done | bytes 327712 | tf_op jit(solution)/shard_map/ppermute | solution.py:502
  83.4 1.3 %shard_map.61 = bf16[4,8,128,128]{3,2,1,0:T(8,128)(2,1)} custom-call(s32[13]{0:T(128)S(1)} %pad_add_fusion.drop_ref, bf16[4,8,128,128]{3,2,1,0:T(8,128)(2,1)S(1)} %get-tuple-element.65.slots, bf16[1280,128]{1,0:T(8,128)(2,1)S(1)} %collective-permute-done.16.cross, bf16[4,8,128,128]{3,2,1,0:T(8,128)(2,1)} %get-tuple-element.67.unused), custom_call_target="tpu_custom_call", output_to_operand_aliasing={{}: (3, {})} | custom-call | tf_op jit(solution)/shard_map/pallas_call | solution.py:488
  (42 shorter events, 8.4 us)
Async XLA Ops:
  0.6 26.8 %collective-permute-start.2 = (bf16[4,8,128,128]{3,2,1,0:T(8,128)(2,1)}, bf16[4,8,128,128]{3,2,1,0:T(8,128)(2,1)S(1)}, u32[]{:S(2)}, u32[]{:S(2)}) collective-permute-start(bf16[4,8,128,128]{3,2,1,0:T(8,128)(2,1)} %own.2), channel_id=1, source_target_pairs={{0,15},{1,2},{2,1},{3,4},{4,3},{5,6},{6,5},{7,8},{8,7},{9,10},{10,... | collective-permute-start | bytes 3145736 | tf_op jit(solution)/shard_map/ppermute | solution.py:502
  3.3 24.1 %collective-permute-start.3 = (bf16[4,8,128,128]{3,2,1,0:T(8,128)(2,1)}, bf16[4,8,128,128]{3,2,1,0:T(8,128)(2,1)S(1)}, u32[]{:S(2)}, u32[]{:S(2)}) collective-permute-start(bf16[4,8,128,128]{3,2,1,0:T(8,128)(2,1)} %own.2), channel_id=1, source_target_pairs={{0,1},{1,0},{2,3},{3,2},{4,5},{5,4},{6,7},{7,6},{8,9},{9,8},{10,11... | collective-permute-start | bytes 3145736 | tf_op jit(solution)/shard_map/ppermute | solution.py:502
  7.1 1.2 %copy-start = (bf16[4,8,128,128]{3,2,1,0:T(8,128)(2,1)S(1)}, bf16[4,8,128,128]{3,2,1,0:T(8,128)(2,1)}, u32[]{:S(2)}) copy-start(bf16[4,8,128,128]{3,2,1,0:T(8,128)(2,1)} %own.3) | copy-start | bytes 3145732
  10.4 0.8 copy-start.1
  11.2 16.2 %collective-permute-start.4 = (bf16[3328,128]{1,0:T(8,128)(2,1)}, bf16[3328,128]{1,0:T(8,128)(2,1)S(1)}, u32[]{:S(2)}, u32[]{:S(2)}) collective-permute-start(bf16[3328,128]{1,0:T(8,128)(2,1)} %get-tuple-element.39.sent_mate), channel_id=1, source_target_pairs={{0,1},{1,0},{2,3},{3,2},{4,5},{5,4},{6,7},{7,6},{8,9},{9,8},{10,11... | collective-permute-start | bytes 2555912 | tf_op jit(solution)/shard_map/ppermute | solution.py:502
  11.2 16.1 %collective-permute-start = (s32[4]{0:T(128)S(1)}, s32[4]{0:T(128)S(1)}, u32[]{:S(2)}, u32[]{:S(2)}) collective-permute-start(s32[4]{0:T(128)S(1)} %broadcast_subtract_fusion), channel_id=1, source_target_pairs={{0,15},{1,2},{2,1},{3,4},{4,3},{5,6},{6,5},{7,8},{8,7},{9,10},{10,... | collective-permute-start | bytes 56 | tf_op jit(solution)/shard_map/ppermute | solution.py:502
  11.2 16.1 %collective-permute-start.1 = (s32[4]{0:T(128)S(1)}, s32[4]{0:T(128)S(1)}, u32[]{:S(2)}, u32[]{:S(2)}) collective-permute-start(s32[4]{0:T(128)S(1)} %broadcast_subtract_fusion), channel_id=1, source_target_pairs={{0,1},{1,0},{2,3},{3,2},{4,5},{5,4},{6,7},{7,6},{8,9},{9,8},{10,11... | collective-permute-start | bytes 56 | tf_op jit(solution)/shard_map/ppermute | solution.py:502
  12.0 24.4 %copy-start.3 = (bf16[4,8,128,128]{3,2,1,0:T(8,128)(2,1)S(1)}, bf16[4,8,128,128]{3,2,1,0:T(8,128)(2,1)}, u32[]{:S(2)}) copy-start(bf16[4,8,128,128]{3,2,1,0:T(8,128)(2,1)} %own.2) | copy-start | bytes 3145732
  28.1 12.5 %collective-permute-start.5 = (bf16[1280,128]{1,0:T(8,128)(2,1)S(1)}, bf16[1280,128]{1,0:T(8,128)(2,1)S(1)}, u32[]{:S(2)}, u32[]{:S(2)}) collective-permute-start(bf16[1280,128]{1,0:T(8,128)(2,1)S(1)} %get-tuple-element.42), channel_id=1, source_target_pairs={{0,13},{1,4},{2,15},{3,6},{4,1},{5,8},{6,3},{7,10},{8,5},{9,12},{1... | collective-permute-start | bytes 983048 | tf_op jit(solution)/shard_map/ppermute | solution.py:502
  28.2 13.9 %collective-permute-start.8 = (bf16[1280,128]{1,0:T(8,128)(2,1)S(1)}, bf16[1280,128]{1,0:T(8,128)(2,1)S(1)}, u32[]{:S(2)}, u32[]{:S(2)}) collective-permute-start(bf16[1280,128]{1,0:T(8,128)(2,1)S(1)} %get-tuple-element.50.sent_cross), channel_id=1, source_target_pairs={{0,15},{1,2},{2,1},{3,4},{4,3},{5,6},{6,5},{7,8},{8,7},{9,10},{10,... | collective-permute-start | bytes 983048 | tf_op jit(solution)/shard_map/ppermute | solution.py:502
  30.0 19.0 %collective-permute-start.9 = (bf16[2048,128]{1,0:T(8,128)(2,1)}, bf16[2048,128]{1,0:T(8,128)(2,1)S(1)}, u32[]{:S(2)}, u32[]{:S(2)}) collective-permute-start(bf16[2048,128]{1,0:T(8,128)(2,1)} %get-tuple-element.52), channel_id=1, source_target_pairs={{0,15},{1,2},{2,1},{3,4},{4,3},{5,6},{6,5},{7,8},{8,7},{9,10},{10,... | collective-permute-start | bytes 1572872 | tf_op jit(solution)/shard_map/ppermute | solution.py:502
  30.1 10.5 %collective-permute-start.6 = (bf16[640,128]{1,0:T(8,128)(2,1)S(1)}, bf16[640,128]{1,0:T(8,128)(2,1)S(1)}, u32[]{:S(2)}, u32[]{:S(2)}) collective-permute-start(bf16[640,128]{1,0:T(8,128)(2,1)S(1)} %get-tuple-element.43), channel_id=1, source_target_pairs={{0,1},{1,0},{2,3},{3,2},{4,5},{5,4},{6,7},{7,6},{8,9},{9,8},{10,11... | collective-permute-start | bytes 491528 | tf_op jit(solution)/shard_map/ppermute | solution.py:502
  36.4 4.3 %collective-permute-start.7 = (bf16[640,128]{1,0:T(8,128)(2,1)S(1)}, bf16[640,128]{1,0:T(8,128)(2,1)S(1)}, u32[]{:S(2)}, u32[]{:S(2)}) collective-permute-start(bf16[640,128]{1,0:T(8,128)(2,1)S(1)} %get-tuple-element.44), channel_id=1, source_target_pairs={{0,1},{1,0},{2,3},{3,2},{4,5},{5,4},{6,7},{7,6},{8,9},{9,8},{10,11... | collective-permute-start | bytes 491528 | tf_op jit(solution)/shard_map/ppermute | solution.py:502
  40.7 1.5 %copy-start.2 = (bf16[2048,128]{1,0:T(8,128)(2,1)S(1)}, bf16[2048,128]{1,0:T(8,128)(2,1)}, u32[]{:S(2)}) copy-start(bf16[2048,128]{1,0:T(8,128)(2,1)} %copy-done.1) | copy-start | bytes 1572868
  45.9 18.8 %collective-permute-start.12 = (bf16[512,512]{1,0:T(8,128)(2,1)S(1)}, bf16[512,512]{1,0:T(8,128)(2,1)S(1)}, u32[]{:S(2)}, u32[]{:S(2)}) collective-permute-start(bf16[512,512]{1,0:T(8,128)(2,1)S(1)} %get-tuple-element.51.own), channel_id=1, source_target_pairs={{0,15},{1,2},{2,1},{3,4},{4,3},{5,6},{6,5},{7,8},{8,7},{9,10},{10,... | collective-permute-start | bytes 1572872 | tf_op jit(solution)/shard_map/ppermute | solution.py:502
  46.8 18.0 %collective-permute-start.13 = (bf16[512,512]{1,0:T(8,128)(2,1)S(1)}, bf16[512,512]{1,0:T(8,128)(2,1)S(1)}, u32[]{:S(2)}, u32[]{:S(2)}) collective-permute-start(bf16[512,512]{1,0:T(8,128)(2,1)S(1)} %get-tuple-element.51.own), channel_id=1, source_target_pairs={{0,1},{1,0},{2,3},{3,2},{4,5},{5,4},{6,7},{7,6},{8,9},{9,8},{10,11... | collective-permute-start | bytes 1572872 | tf_op jit(solution)/shard_map/ppermute | solution.py:502
  50.4 17.3 %collective-permute-start.10 = (bf16[1280,128]{1,0:T(8,128)(2,1)S(1)}, bf16[1280,128]{1,0:T(8,128)(2,1)S(1)}, u32[]{:S(2)}, u32[]{:S(2)}) collective-permute-start(bf16[1280,128]{1,0:T(8,128)(2,1)S(1)} %get-tuple-element.55), channel_id=1, source_target_pairs={{0,1},{1,0},{2,3},{3,2},{4,5},{5,4},{6,7},{7,6},{8,9},{9,8},{10,11... | collective-permute-start | bytes 983048 | tf_op jit(solution)/shard_map/ppermute | solution.py:502
  52.2 16.0 %collective-permute-start.11 = (bf16[1280,128]{1,0:T(8,128)(2,1)S(1)}, bf16[1280,128]{1,0:T(8,128)(2,1)S(1)}, u32[]{:S(2)}, u32[]{:S(2)}) collective-permute-start(bf16[1280,128]{1,0:T(8,128)(2,1)S(1)} %get-tuple-element.56), channel_id=1, source_target_pairs={{0,15},{1,2},{2,1},{3,4},{4,3},{5,6},{6,5},{7,8},{8,7},{9,10},{10,... | collective-permute-start | bytes 983048 | tf_op jit(solution)/shard_map/ppermute | solution.py:502
  66.3 10.5 %collective-permute-start.17 = (bf16[1280,128]{1,0:T(8,128)(2,1)S(1)}, bf16[1280,128]{1,0:T(8,128)(2,1)S(1)}, u32[]{:S(2)}, u32[]{:S(2)}) collective-permute-start(bf16[1280,128]{1,0:T(8,128)(2,1)S(1)} %get-tuple-element.68), channel_id=1, source_target_pairs={{0,1},{1,0},{2,3},{3,2},{4,5},{5,4},{6,7},{7,6},{8,9},{9,8},{10,11... | collective-permute-start | bytes 983048 | tf_op jit(solution)/shard_map/ppermute | solution.py:502
  66.3 12.4 %collective-permute-start.18 = (bf16[1280,128]{1,0:T(8,128)(2,1)S(1)}, bf16[1280,128]{1,0:T(8,128)(2,1)S(1)}, u32[]{:S(2)}, u32[]{:S(2)}) collective-permute-start(bf16[1280,128]{1,0:T(8,128)(2,1)S(1)} %get-tuple-element.70), channel_id=1, source_target_pairs={{0,15},{1,2},{2,1},{3,4},{4,3},{5,6},{6,5},{7,8},{8,7},{9,10},{10,... | collective-permute-start | bytes 983048 | tf_op jit(solution)/shard_map/ppermute | solution.py:502
  70.5 12.9 %collective-permute-start.16 = (bf16[1280,128]{1,0:T(8,128)(2,1)S(1)}, bf16[1280,128]{1,0:T(8,128)(2,1)S(1)}, u32[]{:S(2)}, u32[]{:S(2)}) collective-permute-start(bf16[1280,128]{1,0:T(8,128)(2,1)S(1)} %get-tuple-element.66), channel_id=1, source_target_pairs={{0,15},{1,2},{2,1},{3,4},{4,3},{5,6},{6,5},{7,8},{8,7},{9,10},{10,... | collective-permute-start | bytes 983048 | tf_op jit(solution)/shard_map/ppermute | solution.py:502
  71.8 3.1 %collective-permute-start.14 = (bf16[640,128]{1,0:T(8,128)(2,1)S(1)}, bf16[640,128]{1,0:T(8,128)(2,1)S(1)}, u32[]{:S(2)}, u32[]{:S(2)}) collective-permute-start(bf16[640,128]{1,0:T(8,128)(2,1)S(1)} %get-tuple-element.63), channel_id=1, source_target_pairs={{0,1},{1,0},{2,3},{3,2},{4,5},{5,4},{6,7},{7,6},{8,9},{9,8},{10,11... | collective-permute-start | bytes 491528 | tf_op jit(solution)/shard_map/ppermute | solution.py:502
  73.6 1.4 %collective-permute-start.15 = (bf16[640,128]{1,0:T(8,128)(2,1)S(1)}, bf16[640,128]{1,0:T(8,128)(2,1)S(1)}, u32[]{:S(2)}, u32[]{:S(2)}) collective-permute-start(bf16[640,128]{1,0:T(8,128)(2,1)S(1)} %get-tuple-element.64), channel_id=1, source_target_pairs={{0,1},{1,0},{2,3},{3,2},{4,5},{5,4},{6,7},{7,6},{8,9},{9,8},{10,11... | collective-permute-start | bytes 491528 | tf_op jit(solution)/shard_map/ppermute | solution.py:502

commit v18 on v16

--- a/solution.py
+++ b/solution.py
@@ -375,7 +375,7 @@
 
 
 def density_edges_kernel(
-    f, drop_ref, own, cross, mate, correction, new_low, new_high, square, corners, whole, to_cross, to_mate,
+    f, drop_ref, own, mate, cross, correction, new_low, new_high, square, corners, whole, to_cross, to_mate,
     to_mate_too, before, after, low, high,
 ):
     h, p = f.h, f.p
@@ -619,7 +619,7 @@
         density_edges_kernel,
         [columns, triangle, half_triangle, half_triangle],
         [group_scratch] * 4,
-        38, 20, drop, own, edge_cross, edge_mate, correction, new_low, new_high, square,
+        38, 20, drop, own, edge_mate, edge_cross, correction, new_low, new_high, square,
         square_corners,
     )
     rim_cross, rim_mates = to_cross(rim_cross), [to_mate(rim_mate), to_mate(rim_mate_too)]

time: 85.6 us -> 85.6 us (level)
  starting transfers between devices: 25.2 us -> 22.6 us
  waiting for transfers between devices: 28.8 us -> 31.4 us
    ppermute x19, waiting for transfers between devices: 28.8 us -> 31.4 us  [routed(): lax.ppermute(x, RING, [(i, (i + step(i)) % size) for i in range(size) if...]
    ppermute x19, starting transfers between devices: 25.2 us -> 22.6 us  [routed(): lax.ppermute(x, RING, [(i, (i + step(i)) % size) for i in range(size) if...]
where the time goes in v18:
time: 85.6 us; the launch traced here: 85.3 us
  waiting for transfers between devices  31.4 us (37%)
  Pallas kernels  26.6 us (31%)
  starting transfers between devices  22.6 us (26%)
  local copies, waits for them, and re-layouts  2.83 us (3%)
  other arithmetic  0.96 us (1%)
  between operations  0.86 us (1%)
    ppermute x19, waiting for transfers between devices, routed(): lax.ppermute(x, RING, [(i, (i + step(i)) % size) for i in range(size) if...  31.4 us
    pallas_call x14, Pallas kernels, call(): pl.pallas_call(kernel, out_shape=[*outs, *[jax.ShapeDtypeStruct(a.shape,...  26.6 us
    ppermute x19, starting transfers between devices, routed(): lax.ppermute(x, RING, [(i, (i + step(i)) % size) for i in range(size) if...  22.6 us
    unnamed x12, local copies, waits for them, and re-layouts  2.74 us
  transfers between devices with their start and end apart: 19, of which 9 were waited for; matrix products, arithmetic and copies ran while one was open for 1% of the time, Pallas kernels for 30%

profile of v18, /device:TPU:1, one launch (start us, length us, event | category | flops | bytes accessed | tf_op | source)
XLA Modules:
  0.0 85.3 jit_solution(16326886279583863649)
XLA Ops:
  0.6 2.7 %collective-permute-start.2 = (bf16[4,8,128,128]{3,2,1,0:T(8,128)(2,1)}, bf16[4,8,128,128]{3,2,1,0:T(8,128)(2,1)S(1)}, u32[]{:S(2)}, u32[]{:S(2)}) collective-permute-start(bf16[4,8,128,128]{3,2,1,0:T(8,128)(2,1)} %own.2), channel_id=1, source_target_pairs={{0,15},{1,2},{2,1},{3,4},{4,3},{5,6},{6,5},{7,8},{8,7},{9,10},{10,... | collective-permute-start | bytes 3145736 | tf_op jit(solution)/shard_map/ppermute | solution.py:508
  3.3 2.9 %collective-permute-start.3 = (bf16[4,8,128,128]{3,2,1,0:T(8,128)(2,1)}, bf16[4,8,128,128]{3,2,1,0:T(8,128)(2,1)S(1)}, u32[]{:S(2)}, u32[]{:S(2)}) collective-permute-start(bf16[4,8,128,128]{3,2,1,0:T(8,128)(2,1)} %own.2), channel_id=1, source_target_pairs={{0,1},{1,0},{2,3},{3,2},{4,5},{5,4},{6,7},{7,6},{8,9},{9,8},{10,11... | collective-permute-start | bytes 3145736 | tf_op jit(solution)/shard_map/ppermute | solution.py:508
  8.4 2.2 %shard_map.51 = (bf16[2048,128]{1,0:T(8,128)(2,1)S(1)}, bf16[2048,128]{1,0:T(8,128)(2,1)}, bf16[3328,128]{1,0:T(8,128)(2,1)}, bf16[1280,128]{1,0:T(8,128)(2,1)S(1)}, bf16[1280,128]{1,0:T(8,128)(2,1)}) custom-call(s32[5]{0:T(128)S(1)} %pad_add_fusion.drop_ref, bf16[4,8,128,128]{3,2,1,0:T(8,128)(2,1)S(1)} %copy-done), custom_call_target="tpu_custom_call" | custom-call | bytes 3604480 | tf_op jit(solution)/shard_map/pallas_call | solution.py:494
  12.6 1.5 %collective-permute-done.1 = s32[4]{0:T(128)S(1)} collective-permute-done((s32[4]{0:T(128)S(1)}, s32[4]{0:T(128)S(1)}, u32[]{:S(2)}, u32[]{:S(2)}) %collective-permute-start.1) | collective-permute-done | bytes 48 | tf_op jit(solution)/shard_map/ppermute | solution.py:508
  14.1 2.1 %collective-permute-start.7 = (bf16[1280,128]{1,0:T(8,128)(2,1)}, bf16[1280,128]{1,0:T(8,128)(2,1)S(1)}, u32[]{:S(2)}, u32[]{:S(2)}) collective-permute-start(bf16[1280,128]{1,0:T(8,128)(2,1)} %copy-done.4), channel_id=1, source_target_pairs={{1,2},{2,1},{5,6},{6,5},{9,10},{10,9},{13,14},{14,13},{17,18},{18,... | collective-permute-start | bytes 983048 | tf_op jit(solution)/shard_map/ppermute | solution.py:508
  16.2 11.1 %collective-permute-done = s32[4]{0:T(128)S(1)} collective-permute-done((s32[4]{0:T(128)S(1)}, s32[4]{0:T(128)S(1)}, u32[]{:S(2)}, u32[]{:S(2)}) %collective-permute-start) | collective-permute-done | bytes 48 | tf_op jit(solution)/shard_map/ppermute | solution.py:508
  28.2 3.7 %collective-permute-start.6 = (bf16[1280,128]{1,0:T(8,128)(2,1)S(1)}, bf16[1280,128]{1,0:T(8,128)(2,1)S(1)}, u32[]{:S(2)}, u32[]{:S(2)}) collective-permute-start(bf16[1280,128]{1,0:T(8,128)(2,1)S(1)} %get-tuple-element.43), channel_id=1, source_target_pairs={{0,1},{1,0},{2,3},{3,2},{4,5},{5,4},{6,7},{7,6},{8,9},{9,8},{10,11... | collective-permute-start | bytes 983048 | tf_op jit(solution)/shard_map/ppermute | solution.py:508
  32.7 4.3 %shard_map.50 = (bf16[1536,1280]{1,0:T(8,128)(2,1)S(1)}, bf16[1536,1280]{1,0:T(8,128)(2,1)S(1)}, bf16[1024,512]{1,0:T(8,128)(2,1)S(1)}, bf16[1024,512]{1,0:T(8,128)(2,1)S(1)}, f32[1024,512]{1,0:T(8,128)S(1)}) custom-call(s32[14]{0:T(128)S(1)} %concatenate.6.drop_ref, bf16[4,8,128,128]{3,2,1,0:T(8,128)(2,1)S(1)} %copy-done.1, ...), custom_call_target="tpu_custom_call" | custom-call | tf_op jit(solution)/shard_map/pallas_call | solution.py:494
  37.9 1.4 %shard_map.53 = (bf16[1024,512]{1,0:T(8,128)(2,1)S(1)}, bf16[1024,512]{1,0:T(8,128)(2,1)S(1)}) custom-call(s32[14]{0:T(128)S(1)} %concatenate.6.drop_ref, bf16[1280,128]{1,0:T(8,128)(2,1)S(1)} %collective-permute-done.5.far_far, bf16[1280,128]{1,0:T(8,128)(2,1)S(1)} %collective-permute-done.6.far_mate, bf16[1024,512]{1,0:T(8,128)(2,1)S(1)} %get-tuple-element.44.reach, ...), custom_call_target="tpu_custom_call" | custom-call | tf_op jit(solution)/shard_map/pallas_call | solution.py:494
  39.4 3.7 %shard_map.54 = (bf16[1536,512]{1,0:T(8,128)(2,1)S(1)}, bf16[512,512]{1,0:T(8,128)(2,1)S(1)}, f32[1024,512]{1,0:T(8,128)S(1)}) custom-call(s32[14]{0:T(128)S(1)} %concatenate.6.drop_ref, bf16[1536,1280]{1,0:T(8,128)(2,1)S(1)} %get-tuple-element.38.shifted, bf16[1024,512]{1,0:T(8,128)(2,1)S(1)} %get-tuple-element.48.corners, bf16[2048,128]{1,0:T(8,128)(2,1)S(1)} %copy-done.3, ...), custom_call_target="tpu_custom_call" | custom-call | tf_op jit(solution)/shard_map/pallas_call | solution.py:494
  43.1 3.6 %collective-permute-start.13 = (bf16[512,512]{1,0:T(8,128)(2,1)S(1)}, bf16[512,512]{1,0:T(8,128)(2,1)S(1)}, u32[]{:S(2)}, u32[]{:S(2)}) collective-permute-start(bf16[512,512]{1,0:T(8,128)(2,1)S(1)} %get-tuple-element.51.own), channel_id=1, source_target_pairs={{0,15},{1,2},{2,1},{3,4},{4,3},{5,6},{6,5},{7,8},{8,7},{9,10},{10,... | collective-permute-start | bytes 1572872 | tf_op jit(solution)/shard_map/ppermute | solution.py:508
  46.7 2.8 %collective-permute-start.12 = (bf16[512,512]{1,0:T(8,128)(2,1)S(1)}, bf16[512,512]{1,0:T(8,128)(2,1)S(1)}, u32[]{:S(2)}, u32[]{:S(2)}) collective-permute-start(bf16[512,512]{1,0:T(8,128)(2,1)S(1)} %get-tuple-element.51.own), channel_id=1, source_target_pairs={{0,1},{1,0},{2,3},{3,2},{4,5},{5,4},{6,7},{7,6},{8,9},{9,8},{10,11... | collective-permute-start | bytes 1572872 | tf_op jit(solution)/shard_map/ppermute | solution.py:508
  52.2 2.0 %shard_map.56.correction = bf16[1536,512]{1,0:T(8,128)(2,1)S(1)} custom-call(s32[14]{0:T(128)S(1)} %concatenate.6.drop_ref, bf16[1536,1280]{1,0:T(8,128)(2,1)S(1)} %get-tuple-element.38.shifted, bf16[1024,512]{1,0:T(8,128)(2,1)S(1)} %get-tuple-element.48.corners, bf16[512,512]{1,0:T(8,128)(2,1)S(1)} %get-tuple-element.57.low, ...), custom_call_target="tpu_custom_call" | custom-call | flops 1275068416 | bytes 8126464 | tf_op jit(solution)/shard_map/pallas_call | solution.py:494
  54.2 11.2 %collective-permute-done.13.cross = bf16[512,512]{1,0:T(8,128)(2,1)S(1)} collective-permute-done((bf16[512,512]{1,0:T(8,128)(2,1)S(1)}, bf16[512,512]{1,0:T(8,128)(2,1)S(1)}, u32[]{:S(2)}, u32[]{:S(2)}) %collective-permute-start.13) | collective-permute-done | bytes 524320 | tf_op jit(solution)/shard_map/ppermute | solution.py:508
  65.4 1.5 %shard_map.57 = (bf16[512,512]{1,0:T(8,128)(2,1)S(1)}, bf16[512,512]{1,0:T(8,128)(2,1)S(1)}, bf16[1280,128]{1,0:T(8,128)(2,1)S(1)}, bf16[1280,128]{1,0:T(8,128)(2,1)S(1)}) custom-call(s32[14]{0:T(128)S(1)} %concatenate.6.drop_ref, bf16[512,512]{1,0:T(8,128)(2,1)S(1)} %collective-permute-done.12.mate, bf16[512,512]{1,0:T(8,128)(2,1)S(1)} %collective-permute-done.13.cross, ...), custom_call_target="tpu_custom_call" | custom-call | flops 671088640 | bytes 5373952 | tf_op jit(solution)/shard_map/pallas_call | solution.py:494
  67.0 1.9 %collective-permute-done.11.cross = bf16[1280,128]{1,0:T(8,128)(2,1)S(1)} collective-permute-done((bf16[1280,128]{1,0:T(8,128)(2,1)S(1)}, bf16[1280,128]{1,0:T(8,128)(2,1)S(1)}, u32[]{:S(2)}, u32[]{:S(2)}) %collective-permute-start.11) | collective-permute-done | bytes 327712 | tf_op jit(solution)/shard_map/ppermute | solution.py:508
  68.9 2.2 %shard_map.58 = (bf16[1536,512]{1,0:T(8,128)(2,1)S(1)}, bf16[1280,128]{1,0:T(8,128)(2,1)S(1)}, bf16[640,128]{1,0:T(8,128)(2,1)S(1)}, bf16[640,128]{1,0:T(8,128)(2,1)S(1)}) custom-call(s32[14]{0:T(128)S(1)} %concatenate.6.drop_ref, bf16[512,512]{1,0:T(8,128)(2,1)S(1)} %get-tuple-element.51.own, bf16[1280,128]{1,0:T(8,128)(2,1)S(1)} %collective-permute-done.10.mate, ...), custom_call_target="tpu_custom_call" | custom-call | flops 1275068416 | bytes 11010048 | tf_op jit(solution)/shard_map/pallas_call | solution.py:494
  71.1 3.0 %collective-permute-start.14 = (bf16[640,128]{1,0:T(8,128)(2,1)S(1)}, bf16[640,128]{1,0:T(8,128)(2,1)S(1)}, u32[]{:S(2)}, u32[]{:S(2)}) collective-permute-start(bf16[640,128]{1,0:T(8,128)(2,1)S(1)} %get-tuple-element.63), channel_id=1, source_target_pairs={{0,1},{1,0},{2,3},{3,2},{4,5},{5,4},{6,7},{7,6},{8,9},{9,8},{10,11... | collective-permute-start | bytes 491528 | tf_op jit(solution)/shard_map/ppermute | solution.py:508
  74.1 1.3 %shard_map.59.own = bf16[512,512]{1,0:T(8,128)(2,1)S(1)} custom-call(s32[14]{0:T(128)S(1)} %concatenate.6.drop_ref, bf16[1536,1280]{1,0:T(8,128)(2,1)S(1)} %get-tuple-element.37.square, bf16[1536,512]{1,0:T(8,128)(2,1)S(1)} %get-tuple-element.62.whole.own), custom_call_target="tpu_custom_call" | custom-call | flops 603979776 | bytes 6029312 | tf_op jit(solution)/shard_map/pallas_call | solution.py:494
  75.5 1.7 %shard_map.60 = (bf16[4,8,128,128]{3,2,1,0:T(8,128)(2,1)S(1)}, bf16[4,8,128,128]{3,2,1,0:T(8,128)(2,1)}) custom-call(s32[14]{0:T(128)S(1)} %concatenate.6.drop_ref, bf16[512,512]{1,0:T(8,128)(2,1)S(1)} %shard_map.59.own, bf16[640,128]{1,0:T(8,128)(2,1)S(1)} %collective-permute-done.14.refs_0_, bf16[640,128]{1,0:T(8,128)(2,1)S(1)} %collective-permute-done.15.refs_1_), custom_call_target="tpu_custom_call" | custom-call | tf_op jit(solution)/shard_map/pallas_call | solution.py:494
  77.2 1.7 %shard_map.62 = (bf16[4,8,128,128]{3,2,1,0:T(8,128)(2,1)S(1)}, bf16[4,8,128,128]{3,2,1,0:T(8,128)(2,1)}) custom-call(s32[14]{0:T(128)S(1)} %concatenate.6.drop_ref, bf16[1536,512]{1,0:T(8,128)(2,1)S(1)} %get-tuple-element.62.whole.own, bf16[1280,128]{1,0:T(8,128)(2,1)S(1)} %collective-permute-done.17.refs_0_), custom_call_target="tpu_custom_call" | custom-call | tf_op jit(solution)/shard_map/pallas_call | solution.py:494
  79.0 1.5 %collective-permute-done.18.cross = bf16[1280,128]{1,0:T(8,128)(2,1)S(1)} collective-permute-done((bf16[1280,128]{1,0:T(8,128)(2,1)S(1)}, bf16[1280,128]{1,0:T(8,128)(2,1)S(1)}, u32[]{:S(2)}, u32[]{:S(2)}) %collective-permute-start.18) | collective-permute-done | bytes 327712 | tf_op jit(solution)/shard_map/ppermute | solution.py:508
  81.8 2.2 %collective-permute-done.16.cross = bf16[1280,128]{1,0:T(8,128)(2,1)S(1)} collective-permute-done((bf16[1280,128]{1,0:T(8,128)(2,1)S(1)}, bf16[1280,128]{1,0:T(8,128)(2,1)S(1)}, u32[]{:S(2)}, u32[]{:S(2)}) %collective-permute-start.16) | collective-permute-done | bytes 327712 | tf_op jit(solution)/shard_map/ppermute | solution.py:508
  84.0 1.3 %shard_map.61 = bf16[4,8,128,128]{3,2,1,0:T(8,128)(2,1)} custom-call(s32[14]{0:T(128)S(1)} %concatenate.6.drop_ref, bf16[4,8,128,128]{3,2,1,0:T(8,128)(2,1)S(1)} %get-tuple-element.65.slots, bf16[1280,128]{1,0:T(8,128)(2,1)S(1)} %collective-permute-done.16.cross, bf16[4,8,128,128]{3,2,1,0:T(8,128)(2,1)} %get-tuple-element.67.unused), custom_call_target="tpu_custom_call", output_to_operand_aliasing={{}: (3, {})} | custom-call | tf_op jit(solution)/shard_map/pallas_call | solution.py:494
  (46 shorter events, 11.0 us)
Async XLA Ops:
  0.6 26.8 %collective-permute-start.2 = (bf16[4,8,128,128]{3,2,1,0:T(8,128)(2,1)}, bf16[4,8,128,128]{3,2,1,0:T(8,128)(2,1)S(1)}, u32[]{:S(2)}, u32[]{:S(2)}) collective-permute-start(bf16[4,8,128,128]{3,2,1,0:T(8,128)(2,1)} %own.2), channel_id=1, source_target_pairs={{0,15},{1,2},{2,1},{3,4},{4,3},{5,6},{6,5},{7,8},{8,7},{9,10},{10,... | collective-permute-start | bytes 3145736 | tf_op jit(solution)/shard_map/ppermute | solution.py:508
  3.3 24.1 %collective-permute-start.3 = (bf16[4,8,128,128]{3,2,1,0:T(8,128)(2,1)}, bf16[4,8,128,128]{3,2,1,0:T(8,128)(2,1)S(1)}, u32[]{:S(2)}, u32[]{:S(2)}) collective-permute-start(bf16[4,8,128,128]{3,2,1,0:T(8,128)(2,1)} %own.2), channel_id=1, source_target_pairs={{0,1},{1,0},{2,3},{3,2},{4,5},{5,4},{6,7},{7,6},{8,9},{9,8},{10,11... | collective-permute-start | bytes 3145736 | tf_op jit(solution)/shard_map/ppermute | solution.py:508
  7.1 1.2 %copy-start = (bf16[4,8,128,128]{3,2,1,0:T(8,128)(2,1)S(1)}, bf16[4,8,128,128]{3,2,1,0:T(8,128)(2,1)}, u32[]{:S(2)}) copy-start(bf16[4,8,128,128]{3,2,1,0:T(8,128)(2,1)} %own.3) | copy-start | bytes 3145732
  10.5 0.8 copy-start.2
  12.0 15.3 %collective-permute-start.4 = (bf16[3328,128]{1,0:T(8,128)(2,1)}, bf16[3328,128]{1,0:T(8,128)(2,1)S(1)}, u32[]{:S(2)}, u32[]{:S(2)}) collective-permute-start(bf16[3328,128]{1,0:T(8,128)(2,1)} %get-tuple-element.39.sent_mate), channel_id=1, source_target_pairs={{0,1},{1,0},{2,3},{3,2},{4,5},{5,4},{6,7},{7,6},{8,9},{9,8},{10,11... | collective-permute-start | bytes 2555912 | tf_op jit(solution)/shard_map/ppermute | solution.py:508
  12.0 2.0 %collective-permute-start.1 = (s32[4]{0:T(128)S(1)}, s32[4]{0:T(128)S(1)}, u32[]{:S(2)}, u32[]{:S(2)}) collective-permute-start(s32[4]{0:T(128)S(1)} %broadcast_subtract_fusion), channel_id=1, source_target_pairs={{0,1},{1,0},{2,3},{3,2},{4,5},{5,4},{6,7},{7,6},{8,9},{9,8},{10,11... | collective-permute-start | bytes 56 | tf_op jit(solution)/shard_map/ppermute | solution.py:508
  12.6 14.7 %collective-permute-start = (s32[4]{0:T(128)S(1)}, s32[4]{0:T(128)S(1)}, u32[]{:S(2)}, u32[]{:S(2)}) collective-permute-start(s32[4]{0:T(128)S(1)} %broadcast_subtract_fusion), channel_id=1, source_target_pairs={{0,15},{1,2},{2,1},{3,4},{4,3},{5,6},{6,5},{7,8},{8,7},{9,10},{10,... | collective-permute-start | bytes 56 | tf_op jit(solution)/shard_map/ppermute | solution.py:508
  14.1 22.9 %collective-permute-start.7 = (bf16[1280,128]{1,0:T(8,128)(2,1)}, bf16[1280,128]{1,0:T(8,128)(2,1)S(1)}, u32[]{:S(2)}, u32[]{:S(2)}) collective-permute-start(bf16[1280,128]{1,0:T(8,128)(2,1)} %copy-done.4), channel_id=1, source_target_pairs={{1,2},{2,1},{5,6},{6,5},{9,10},{10,9},{13,14},{14,13},{17,18},{18,... | collective-permute-start | bytes 983048 | tf_op jit(solution)/shard_map/ppermute | solution.py:508
  27.4 5.3 %copy-start.1 = (bf16[4,8,128,128]{3,2,1,0:T(8,128)(2,1)S(1)}, bf16[4,8,128,128]{3,2,1,0:T(8,128)(2,1)}, u32[]{:S(2)}) copy-start(bf16[4,8,128,128]{3,2,1,0:T(8,128)(2,1)} %own.2) | copy-start | bytes 3145732
  28.1 9.8 %collective-permute-start.5 = (bf16[1280,128]{1,0:T(8,128)(2,1)S(1)}, bf16[1280,128]{1,0:T(8,128)(2,1)S(1)}, u32[]{:S(2)}, u32[]{:S(2)}) collective-permute-start(bf16[1280,128]{1,0:T(8,128)(2,1)S(1)} %get-tuple-element.42), channel_id=1, source_target_pairs={{0,13},{1,4},{2,15},{3,6},{4,1},{5,8},{6,3},{7,10},{8,5},{9,12},{1... | collective-permute-start | bytes 983048 | tf_op jit(solution)/shard_map/ppermute | solution.py:508
  28.2 9.7 %collective-permute-start.6 = (bf16[1280,128]{1,0:T(8,128)(2,1)S(1)}, bf16[1280,128]{1,0:T(8,128)(2,1)S(1)}, u32[]{:S(2)}, u32[]{:S(2)}) collective-permute-start(bf16[1280,128]{1,0:T(8,128)(2,1)S(1)} %get-tuple-element.43), channel_id=1, source_target_pairs={{0,1},{1,0},{2,3},{3,2},{4,5},{5,4},{6,7},{7,6},{8,9},{9,8},{10,11... | collective-permute-start | bytes 983048 | tf_op jit(solution)/shard_map/ppermute | solution.py:508
  31.9 7.4 %collective-permute-start.8 = (bf16[1280,128]{1,0:T(8,128)(2,1)}, bf16[1280,128]{1,0:T(8,128)(2,1)S(1)}, u32[]{:S(2)}, u32[]{:S(2)}) collective-permute-start(bf16[1280,128]{1,0:T(8,128)(2,1)} %get-tuple-element.50), channel_id=1, source_target_pairs={{0,15},{3,4},{4,3},{7,8},{8,7},{11,12},{12,11},{15,0},{16,31},{19,... | collective-permute-start | bytes 983048 | tf_op jit(solution)/shard_map/ppermute | solution.py:508
  32.6 18.0 %collective-permute-start.9 = (bf16[2048,128]{1,0:T(8,128)(2,1)}, bf16[2048,128]{1,0:T(8,128)(2,1)S(1)}, u32[]{:S(2)}, u32[]{:S(2)}) collective-permute-start(bf16[2048,128]{1,0:T(8,128)(2,1)} %get-tuple-element.52), channel_id=1, source_target_pairs={{0,15},{1,2},{2,1},{3,4},{4,3},{5,6},{6,5},{7,8},{8,7},{9,10},{10,... | collective-permute-start | bytes 1572872 | tf_op jit(solution)/shard_map/ppermute | solution.py:508
  37.9 1.4 %copy-start.3 = (bf16[2048,128]{1,0:T(8,128)(2,1)S(1)}, bf16[2048,128]{1,0:T(8,128)(2,1)}, u32[]{:S(2)}) copy-start(bf16[2048,128]{1,0:T(8,128)(2,1)} %copy-done.2) | copy-start | bytes 1572868
  37.9 1.4 %copy-start.5 = (bf16[1280,128]{1,0:T(8,128)(2,1)S(1)}, bf16[1280,128]{1,0:T(8,128)(2,1)}, u32[]{:S(2)}) copy-start(bf16[1280,128]{1,0:T(8,128)(2,1)} %copy-done.4) | copy-start | bytes 983044
  43.1 22.3 %collective-permute-start.13 = (bf16[512,512]{1,0:T(8,128)(2,1)S(1)}, bf16[512,512]{1,0:T(8,128)(2,1)S(1)}, u32[]{:S(2)}, u32[]{:S(2)}) collective-permute-start(bf16[512,512]{1,0:T(8,128)(2,1)S(1)} %get-tuple-element.51.own), channel_id=1, source_target_pairs={{0,15},{1,2},{2,1},{3,4},{4,3},{5,6},{6,5},{7,8},{8,7},{9,10},{10,... | collective-permute-start | bytes 1572872 | tf_op jit(solution)/shard_map/ppermute | solution.py:508
  46.7 18.7 %collective-permute-start.12 = (bf16[512,512]{1,0:T(8,128)(2,1)S(1)}, bf16[512,512]{1,0:T(8,128)(2,1)S(1)}, u32[]{:S(2)}, u32[]{:S(2)}) collective-permute-start(bf16[512,512]{1,0:T(8,128)(2,1)S(1)} %get-tuple-element.51.own), channel_id=1, source_target_pairs={{0,1},{1,0},{2,3},{3,2},{4,5},{5,4},{6,7},{7,6},{8,9},{9,8},{10,11... | collective-permute-start | bytes 1572872 | tf_op jit(solution)/shard_map/ppermute | solution.py:508
  51.9 15.1 %collective-permute-start.10 = (bf16[1280,128]{1,0:T(8,128)(2,1)S(1)}, bf16[1280,128]{1,0:T(8,128)(2,1)S(1)}, u32[]{:S(2)}, u32[]{:S(2)}) collective-permute-start(bf16[1280,128]{1,0:T(8,128)(2,1)S(1)} %get-tuple-element.55), channel_id=1, source_target_pairs={{0,1},{1,0},{2,3},{3,2},{4,5},{5,4},{6,7},{7,6},{8,9},{9,8},{10,11... | collective-permute-start | bytes 983048 | tf_op jit(solution)/shard_map/ppermute | solution.py:508
  52.2 16.7 %collective-permute-start.11 = (bf16[1280,128]{1,0:T(8,128)(2,1)S(1)}, bf16[1280,128]{1,0:T(8,128)(2,1)S(1)}, u32[]{:S(2)}, u32[]{:S(2)}) collective-permute-start(bf16[1280,128]{1,0:T(8,128)(2,1)S(1)} %get-tuple-element.56), channel_id=1, source_target_pairs={{0,15},{1,2},{2,1},{3,4},{4,3},{5,6},{6,5},{7,8},{8,7},{9,10},{10,... | collective-permute-start | bytes 983048 | tf_op jit(solution)/shard_map/ppermute | solution.py:508
  66.8 10.4 %collective-permute-start.17 = (bf16[1280,128]{1,0:T(8,128)(2,1)S(1)}, bf16[1280,128]{1,0:T(8,128)(2,1)S(1)}, u32[]{:S(2)}, u32[]{:S(2)}) collective-permute-start(bf16[1280,128]{1,0:T(8,128)(2,1)S(1)} %get-tuple-element.68), channel_id=1, source_target_pairs={{0,1},{1,0},{2,3},{3,2},{4,5},{5,4},{6,7},{7,6},{8,9},{9,8},{10,11... | collective-permute-start | bytes 983048 | tf_op jit(solution)/shard_map/ppermute | solution.py:508
  66.9 13.6 %collective-permute-start.18 = (bf16[1280,128]{1,0:T(8,128)(2,1)S(1)}, bf16[1280,128]{1,0:T(8,128)(2,1)S(1)}, u32[]{:S(2)}, u32[]{:S(2)}) collective-permute-start(bf16[1280,128]{1,0:T(8,128)(2,1)S(1)} %get-tuple-element.70), channel_id=1, source_target_pairs={{0,15},{1,2},{2,1},{3,4},{4,3},{5,6},{6,5},{7,8},{8,7},{9,10},{10,... | collective-permute-start | bytes 983048 | tf_op jit(solution)/shard_map/ppermute | solution.py:508
  71.0 13.0 %collective-permute-start.16 = (bf16[1280,128]{1,0:T(8,128)(2,1)S(1)}, bf16[1280,128]{1,0:T(8,128)(2,1)S(1)}, u32[]{:S(2)}, u32[]{:S(2)}) collective-permute-start(bf16[1280,128]{1,0:T(8,128)(2,1)S(1)} %get-tuple-element.66), channel_id=1, source_target_pairs={{0,15},{1,2},{2,1},{3,4},{4,3},{5,6},{6,5},{7,8},{8,7},{9,10},{10,... | collective-permute-start | bytes 983048 | tf_op jit(solution)/shard_map/ppermute | solution.py:508
  71.1 4.3 %collective-permute-start.14 = (bf16[640,128]{1,0:T(8,128)(2,1)S(1)}, bf16[640,128]{1,0:T(8,128)(2,1)S(1)}, u32[]{:S(2)}, u32[]{:S(2)}) collective-permute-start(bf16[640,128]{1,0:T(8,128)(2,1)S(1)} %get-tuple-element.63), channel_id=1, source_target_pairs={{0,1},{1,0},{2,3},{3,2},{4,5},{5,4},{6,7},{7,6},{8,9},{9,8},{10,11... | collective-permute-start | bytes 491528 | tf_op jit(solution)/shard_map/ppermute | solution.py:508
  74.1 1.4 %collective-permute-start.15 = (bf16[640,128]{1,0:T(8,128)(2,1)S(1)}, bf16[640,128]{1,0:T(8,128)(2,1)S(1)}, u32[]{:S(2)}, u32[]{:S(2)}) collective-permute-start(bf16[640,128]{1,0:T(8,128)(2,1)S(1)} %get-tuple-element.64), channel_id=1, source_target_pairs={{0,1},{1,0},{2,3},{3,2},{4,5},{5,4},{6,7},{7,6},{8,9},{9,8},{10,11... | collective-permute-start | bytes 491528 | tf_op jit(solution)/shard_map/ppermute | solution.py:508
  (1 other events, 0.7 us)

commit v19 on v18

--- a/solution.py
+++ b/solution.py
@@ -263,10 +263,7 @@
     return rest if total is None else total + rest
 
 
-def first_sweep_kernel(
-    f, drop_ref, shifted, corners, corner, sent_mate, sent_cross, mate, direct, turned,
-    correction, fresh, partial, whole, before, after,
-):
+def early_sweep_kernel(f, drop_ref, shifted, corner, mate, direct, turned, whole, early):
     h, p = f.h, f.p
     turning = drop_ref[3 * h + 1] == 1
     direct_block, turned_block = indexed(f, direct), indexed(f, turned)
@@ -275,33 +272,48 @@
         return jnp.where(turning, turned_block(i), direct_block(i))
 
     from_below, from_above = sides(f, drop_ref, indexed(f, mate), cross)
-    down, up = sides(f, drop_ref, indexed(f, sent_mate), indexed(f, sent_cross))
     spread(f, whole, 0, 0, from_below, under(h))
     spread(f, whole, h, 0, indexed(f, corner), full(h))
     spread(f, whole, 2 * h, 0, from_above, over(h))
+    for row, col in f.tiles(f.own_pairs):
+        lo, hi = f.clipped(row, col)
+        lo = p if row < p else lo
+        hi = 2 * p if row >= 2 * p else hi
+        c = col - p
+        early[at(f, row, row + 1, c, c + 1)] = dot(
+            shifted[banded(f, row, lo, hi)], whole[at(f, lo, hi, c, c + 1)]
+        )
+
+
+def first_sweep_kernel(
+    f, drop_ref, corners, early, whole, sent_mate, sent_cross, correction, fresh, before, after
+):
+    h, p = f.h, f.p
+    down, up = sides(f, drop_ref, indexed(f, sent_mate), indexed(f, sent_cross))
     spread(f, before, 0, 0, down, over(h))
     spread(f, after, 0, 0, up, under(h))
     for row, col in f.tiles(f.own_pairs):
-        total = masked(f, right_tile(f, shifted, corners, whole, row, col), row, col, drop_ref)
-        correction[at(f, row, row + 1, col - p, col - p + 1)] = total.astype(correction.dtype)
-    for row, col in f.tiles(f.own_pairs):
+        lo, hi = f.clipped(row, col)
         c = col - p
-        own_row = row in f.own_pairs
+        total = early[at(f, row, row + 1, c, c + 1)]
+        if row < p:
+            total = total + dot(corners[at(f, row, row + 1, lo, p)], whole[at(f, lo, p, c, c + 1)])
+        elif row >= 2 * p:
+            total = total + dot(
+                corners[at(f, row - p, row - p + 1, 0, hi - 2 * p)], whole[at(f, 2 * p, hi, c, c + 1)]
+            )
+        total = masked(f, total, row, col, drop_ref)
+        correction[at(f, row, row + 1, c, c + 1)] = total.astype(correction.dtype)
+    for row, col in f.tiles(f.own_pairs):
+        if row not in f.own_pairs:
+            continue
+        c, local = col - p, row - p
         total = 2.0 * whole[at(f, row, row + 1, c, c + 1)].astype(jnp.float32)
         for g, a, z in f.split(row, col):
-            if g == 1:
-                left = whole[at(f, row, row + 1, a, z)]
-            elif own_row:
-                left = (before, None, after)[g][at(f, row - p, row - p + 1, a, z)]
-            else:
-                continue
+            left = whole[at(f, row, row + 1, a, z)] if g == 1 else (before, None, after)[g][at(f, local, local + 1, a, z)]
             total = total - dot(left, correction[at(f, g * p + a, g * p + z, c, c + 1)])
-        if own_row:
-            total = masked(f, total, row, col, drop_ref)
-            fresh[at(f, row - p, row - p + 1, c, c + 1)] = total.astype(fresh.dtype)
-        else:
-            place = row if row < p else row - p
-            partial[at(f, place, place + 1, c, c + 1)] = total
+        total = masked(f, total, row, col, drop_ref)
+        fresh[at(f, local, local + 1, c, c + 1)] = total.astype(fresh.dtype)
 
 
 def edges(f, drop_ref, corner_below, corner_above, correction, start, low, high):
@@ -324,7 +336,7 @@
 
 
 def first_edges_kernel(
-    f, drop_ref, mate, cross, correction, partial, low, high, to_cross, to_mate, before, after
+    f, drop_ref, mate, cross, correction, whole, low, high, to_cross, to_mate, before, after
 ):
     p = f.p
     below, above = sides(f, drop_ref, indexed(f, mate, len(under(f.h))), indexed(f, cross))
@@ -332,8 +344,14 @@
     spread(f, after, 0, 0, above, full(f.h))
 
     def start(row, col):
-        place = row if row < p else row - p
-        return partial[at(f, place, place + 1, col - p, col - p + 1)]
+        c = col - p
+        total = 2.0 * whole[at(f, row, row + 1, c, c + 1)].astype(jnp.float32)
+        for g, a, z in f.split(row, col):
+            if g == 1:
+                total = total - dot(
+                    whole[at(f, row, row + 1, a, z)], correction[at(f, p + a, p + z, c, c + 1)]
+                )
+        return total
 
     edges(f, drop_ref, plain(before), plain(after), correction, start, low, high)
     pack_edges(f, drop_ref, low, high, to_cross, to_mate)
@@ -584,25 +602,31 @@
         [pltpu.VMEM((3 * f.group, 5 * f.group), kind)],
         84, 26, drop, density, density_cross, density_mate, light=True,
     )
+    early_sums = jax.ShapeDtypeStruct((3 * f.group, f.group), jnp.float32)
+    columns_start, early = run(
+        early_sweep_kernel,
+        [columns, early_sums],
+        [],
+        28, 16, drop, shifted, corner, from_mate, direct_triangle, turned_triangle, light=True,
+    )
     square_corners, shifted_corners = run(
         corners_kernel,
         [both_corners, both_corners],
         [group_scratch] * 2,
-        10, 16, drop, far_far, far_mate, reach, here, partial, direct_triangle, light=True,
-    )
-    correction, own, partial = run(
+        10, 16, drop, far_far, far_mate, reach, here, partial, early, light=True,
+    )
+    correction, own = run(
         first_sweep_kernel,
-        [columns, square_group, partial_sums],
-        [whole_scratch, group_scratch, group_scratch],
-        66, 24, drop, shifted, shifted_corners, corner, slab_mate, triangle_cross, from_mate,
-        direct_triangle, turned_triangle, light=True,
+        [columns, square_group],
+        [group_scratch, group_scratch],
+        28, 20, drop, shifted_corners, early, columns_start, slab_mate, triangle_cross, light=True,
     )
     corner_cross, corner_mate = to_cross(own), to_mate(own)
     low, high, edge_cross, edge_mate = run(
         first_edges_kernel,
         [square_group, square_group, triangle, triangle],
         [group_scratch] * 2,
-        10, 16, drop, from_mate, cross_corner, correction, partial,
+        20, 16, drop, from_mate, cross_corner, correction, columns_start,
     )
     edge_cross, edge_mate = to_cross(edge_cross), to_mate(edge_mate)
     (correction,) = run(

time: 85.6 us -> 87.2 us (1.019)
  the two profiles are of different devices: /device:TPU:1 before, /device:TPU:17 now
where the time goes in v19:
time: 87.2 us; the launch traced here: 86.9 us
  waiting for transfers between devices  35.6 us (41%)
  Pallas kernels  27.7 us (32%)
  starting transfers between devices  19.7 us (23%)
  local copies, waits for them, and re-layouts  2.04 us (2%)
  other arithmetic  0.96 us (1%)
    ppermute x19, waiting for transfers between devices, routed(): lax.ppermute(x, RING, [(i, (i + step(i)) % size) for i in range(size) if...  35.6 us
    pallas_call x15, Pallas kernels, call(): pl.pallas_call(kernel, out_shape=[*outs, *[jax.ShapeDtypeStruct(a.shape,...  27.7 us
    ppermute x19, starting transfers between devices, routed(): lax.ppermute(x, RING, [(i, (i + step(i)) % size) for i in range(size) if...  19.7 us
    unnamed x8, local copies, waits for them, and re-layouts  1.95 us
  transfers between devices with their start and end apart: 19, of which 8 were waited for; matrix products, arithmetic and copies ran while one was open for 1% of the time, Pallas kernels for 30%

profile of v19, /device:TPU:17, one launch (start us, length us, event | category | flops | bytes accessed | tf_op | source)
XLA Modules:
  0.0 86.9 jit_solution(12326931286610294976)
XLA Ops:
  0.6 1.8 %collective-permute-start.2 = (bf16[4,8,128,128]{3,2,1,0:T(8,128)(2,1)}, bf16[4,8,128,128]{3,2,1,0:T(8,128)(2,1)S(1)}, u32[]{:S(2)}, u32[]{:S(2)}) collective-permute-start(bf16[4,8,128,128]{3,2,1,0:T(8,128)(2,1)} %own.2), channel_id=1, source_target_pairs={{0,15},{1,2},{2,1},{3,4},{4,3},{5,6},{6,5},{7,8},{8,7},{9,10},{10,... | collective-permute-start | bytes 3145736 | tf_op jit(solution)/shard_map/ppermute | solution.py:526
  4.7 2.2 %shard_map.51 = (bf16[2048,128]{1,0:T(8,128)(2,1)S(1)}, bf16[2048,128]{1,0:T(8,128)(2,1)}, bf16[3328,128]{1,0:T(8,128)(2,1)}, bf16[1280,128]{1,0:T(8,128)(2,1)S(1)}, bf16[1280,128]{1,0:T(8,128)(2,1)}) custom-call(s32[5]{0:T(128)S(1)} %pad_add_fusion.drop_ref, bf16[4,8,128,128]{3,2,1,0:T(8,128)(2,1)S(1)} %copy-done), custom_call_target="tpu_custom_call" | custom-call | bytes 3604480 | tf_op jit(solution)/shard_map/pallas_call | solution.py:512
  8.1 1.7 %collective-permute-start = (s32[4]{0:T(128)S(1)}, s32[4]{0:T(128)S(1)}, u32[]{:S(2)}, u32[]{:S(2)}) collective-permute-start(s32[4]{0:T(128)S(1)} %broadcast_subtract_fusion), channel_id=1, source_target_pairs={{0,15},{1,2},{2,1},{3,4},{4,3},{5,6},{6,5},{7,8},{8,7},{9,10},{10,... | collective-permute-start | bytes 56 | tf_op jit(solution)/shard_map/ppermute | solution.py:526
  9.9 3.2 %collective-permute-start.7 = (bf16[1280,128]{1,0:T(8,128)(2,1)}, bf16[1280,128]{1,0:T(8,128)(2,1)}, u32[]{:S(2)}, u32[]{:S(2)}) collective-permute-start(bf16[1280,128]{1,0:T(8,128)(2,1)} %copy-done.2), channel_id=1, source_target_pairs={{1,2},{2,1},{5,6},{6,5},{9,10},{10,9},{13,14},{14,13},{17,18},{18,... | collective-permute-start | bytes 983048 | tf_op jit(solution)/shard_map/ppermute | solution.py:526
  13.1 16.8 %collective-permute-done = s32[4]{0:T(128)S(1)} collective-permute-done((s32[4]{0:T(128)S(1)}, s32[4]{0:T(128)S(1)}, u32[]{:S(2)}, u32[]{:S(2)}) %collective-permute-start) | collective-permute-done | bytes 48 | tf_op jit(solution)/shard_map/ppermute | solution.py:526
  32.1 1.3 %collective-permute-start.9 = (bf16[2048,128]{1,0:T(8,128)(2,1)}, bf16[2048,128]{1,0:T(8,128)(2,1)S(1)}, u32[]{:S(2)}, u32[]{:S(2)}) collective-permute-start(bf16[2048,128]{1,0:T(8,128)(2,1)} %get-tuple-element.55), channel_id=1, source_target_pairs={{0,15},{1,2},{2,1},{3,4},{4,3},{5,6},{6,5},{7,8},{8,7},{9,10},{10,... | collective-permute-start | bytes 1572872 | tf_op jit(solution)/shard_map/ppermute | solution.py:526
  33.5 4.3 %shard_map.50 = (bf16[1536,1280]{1,0:T(8,128)(2,1)S(1)}, bf16[1536,1280]{1,0:T(8,128)(2,1)S(1)}, bf16[1024,512]{1,0:T(8,128)(2,1)S(1)}, bf16[1024,512]{1,0:T(8,128)(2,1)S(1)}, f32[1024,512]{1,0:T(8,128)S(1)}) custom-call(s32[14]{0:T(128)S(1)} %concatenate.6.drop_ref, bf16[4,8,128,128]{3,2,1,0:T(8,128)(2,1)S(1)} %copy-done.1, ...), custom_call_target="tpu_custom_call" | custom-call | tf_op jit(solution)/shard_map/pallas_call | solution.py:512
  37.8 2.2 %shard_map.53 = (bf16[1536,512]{1,0:T(8,128)(2,1)S(1)}, f32[1536,512]{1,0:T(8,128)S(1)}) custom-call(s32[14]{0:T(128)S(1)} %concatenate.6.drop_ref, bf16[1536,1280]{1,0:T(8,128)(2,1)S(1)} %get-tuple-element.47.shifted, bf16[2048,128]{1,0:T(8,128)(2,1)S(1)} %get-tuple-element.48.corner, bf16[3328,128]{1,0:T(8,128)(2,1)S(1)} %collective-permute-done.4.refs_1_.mate, ...), custom_call_target="tpu_custom_call" | custom-call | tf_op jit(solution)/shard_map/pallas_call | solution.py:512
  40.8 1.4 %shard_map.54 = (bf16[1024,512]{1,0:T(8,128)(2,1)S(1)}, bf16[1024,512]{1,0:T(8,128)(2,1)S(1)}) custom-call(s32[14]{0:T(128)S(1)} %concatenate.6.drop_ref, bf16[1280,128]{1,0:T(8,128)(2,1)S(1)} %collective-permute-done.5.far_far, bf16[1280,128]{1,0:T(8,128)(2,1)S(1)} %collective-permute-done.6.far_mate, bf16[1024,512]{1,0:T(8,128)(2,1)S(1)} %get-tuple-element.44.reach, ...), custom_call_target="tpu_custom_call" | custom-call | tf_op jit(solution)/shard_map/pallas_call | solution.py:512
  42.3 2.4 %shard_map.55 = (bf16[1536,512]{1,0:T(8,128)(2,1)S(1)}, bf16[512,512]{1,0:T(8,128)(2,1)S(1)}) custom-call(s32[14]{0:T(128)S(1)} %concatenate.6.drop_ref, bf16[1024,512]{1,0:T(8,128)(2,1)S(1)} %get-tuple-element.52.corners, f32[1536,512]{1,0:T(8,128)S(1)} %get-tuple-element.51.unused.early, bf16[1536,512]{1,0:T(8,128)(2,1)S(1)} %get-tuple-element.53.whole, ...), custom_call_target="tpu_custom_call" | custom-call | tf_op jit(solution)/shard_map/pallas_call | solution.py:512
  44.7 6.3 %collective-permute-start.13 = (bf16[512,512]{1,0:T(8,128)(2,1)S(1)}, bf16[512,512]{1,0:T(8,128)(2,1)S(1)}, u32[]{:S(2)}, u32[]{:S(2)}) collective-permute-start(bf16[512,512]{1,0:T(8,128)(2,1)S(1)} %get-tuple-element.54.own), channel_id=1, source_target_pairs={{0,15},{1,2},{2,1},{3,4},{4,3},{5,6},{6,5},{7,8},{8,7},{9,10},{10,... | collective-permute-start | bytes 1572872 | tf_op jit(solution)/shard_map/ppermute | solution.py:526
  50.9 2.0 %collective-permute-start.12 = (bf16[512,512]{1,0:T(8,128)(2,1)S(1)}, bf16[512,512]{1,0:T(8,128)(2,1)S(1)}, u32[]{:S(2)}, u32[]{:S(2)}) collective-permute-start(bf16[512,512]{1,0:T(8,128)(2,1)S(1)} %get-tuple-element.54.own), channel_id=1, source_target_pairs={{0,1},{1,0},{2,3},{3,2},{4,5},{5,4},{6,7},{7,6},{8,9},{9,8},{10,11... | collective-permute-start | bytes 1572872 | tf_op jit(solution)/shard_map/ppermute | solution.py:526
  53.0 1.5 %shard_map.56 = (bf16[512,512]{1,0:T(8,128)(2,1)S(1)}, bf16[512,512]{1,0:T(8,128)(2,1)S(1)}, bf16[1280,128]{1,0:T(8,128)(2,1)S(1)}, bf16[1280,128]{1,0:T(8,128)(2,1)S(1)}) custom-call(s32[14]{0:T(128)S(1)} %concatenate.6.drop_ref, bf16[3328,128]{1,0:T(8,128)(2,1)S(1)} %collective-permute-done.4.refs_1_.mate, ...), custom_call_target="tpu_custom_call" | custom-call | flops 671088640 | bytes 6225920 | tf_op jit(solution)/shard_map/pallas_call | solution.py:512
  54.6 2.0 %shard_map.57.correction = bf16[1536,512]{1,0:T(8,128)(2,1)S(1)} custom-call(s32[14]{0:T(128)S(1)} %concatenate.6.drop_ref, bf16[1536,1280]{1,0:T(8,128)(2,1)S(1)} %get-tuple-element.47.shifted, bf16[1024,512]{1,0:T(8,128)(2,1)S(1)} %get-tuple-element.52.corners, bf16[512,512]{1,0:T(8,128)(2,1)S(1)} %get-tuple-element.59.low, ...), custom_call_target="tpu_custom_call" | custom-call | flops 1275068416 | bytes 8126464 | tf_op jit(solution)/shard_map/pallas_call | solution.py:512
  56.6 10.3 %collective-permute-done.13.cross = bf16[512,512]{1,0:T(8,128)(2,1)S(1)} collective-permute-done((bf16[512,512]{1,0:T(8,128)(2,1)S(1)}, bf16[512,512]{1,0:T(8,128)(2,1)S(1)}, u32[]{:S(2)}, u32[]{:S(2)}) %collective-permute-start.13) | collective-permute-done | bytes 524320 | tf_op jit(solution)/shard_map/ppermute | solution.py:526
  66.9 1.5 %shard_map.58 = (bf16[512,512]{1,0:T(8,128)(2,1)S(1)}, bf16[512,512]{1,0:T(8,128)(2,1)S(1)}, bf16[1280,128]{1,0:T(8,128)(2,1)S(1)}, bf16[1280,128]{1,0:T(8,128)(2,1)S(1)}) custom-call(s32[14]{0:T(128)S(1)} %concatenate.6.drop_ref, bf16[512,512]{1,0:T(8,128)(2,1)S(1)} %collective-permute-done.12.mate, bf16[512,512]{1,0:T(8,128)(2,1)S(1)} %collective-permute-done.13.cross, ...), custom_call_target="tpu_custom_call" | custom-call | flops 671088640 | bytes 5373952 | tf_op jit(solution)/shard_map/pallas_call | solution.py:512
  68.6 1.9 %collective-permute-done.11.cross = bf16[1280,128]{1,0:T(8,128)(2,1)S(1)} collective-permute-done((bf16[1280,128]{1,0:T(8,128)(2,1)S(1)}, bf16[1280,128]{1,0:T(8,128)(2,1)S(1)}, u32[]{:S(2)}, u32[]{:S(2)}) %collective-permute-start.11) | collective-permute-done | bytes 327712 | tf_op jit(solution)/shard_map/ppermute | solution.py:526
  70.4 2.2 %shard_map.59 = (bf16[1536,512]{1,0:T(8,128)(2,1)S(1)}, bf16[1280,128]{1,0:T(8,128)(2,1)S(1)}, bf16[640,128]{1,0:T(8,128)(2,1)S(1)}, bf16[640,128]{1,0:T(8,128)(2,1)S(1)}) custom-call(s32[14]{0:T(128)S(1)} %concatenate.6.drop_ref, bf16[512,512]{1,0:T(8,128)(2,1)S(1)} %get-tuple-element.54.own, bf16[1280,128]{1,0:T(8,128)(2,1)S(1)} %collective-permute-done.10.mate, ...), custom_call_target="tpu_custom_call" | custom-call | flops 1275068416 | bytes 11010048 | tf_op jit(solution)/shard_map/pallas_call | solution.py:512
  73.9 1.3 %shard_map.60.own = bf16[512,512]{1,0:T(8,128)(2,1)S(1)} custom-call(s32[14]{0:T(128)S(1)} %concatenate.6.drop_ref, bf16[1536,1280]{1,0:T(8,128)(2,1)S(1)} %get-tuple-element.38.square, bf16[1536,512]{1,0:T(8,128)(2,1)S(1)} %get-tuple-element.64.whole.own), custom_call_target="tpu_custom_call" | custom-call | flops 603979776 | bytes 6029312 | tf_op jit(solution)/shard_map/pallas_call | solution.py:512
  75.3 1.7 %shard_map.61 = (bf16[4,8,128,128]{3,2,1,0:T(8,128)(2,1)S(1)}, bf16[4,8,128,128]{3,2,1,0:T(8,128)(2,1)}) custom-call(s32[14]{0:T(128)S(1)} %concatenate.6.drop_ref, bf16[512,512]{1,0:T(8,128)(2,1)S(1)} %shard_map.60.own, bf16[640,128]{1,0:T(8,128)(2,1)S(1)} %collective-permute-done.14.refs_0_, bf16[640,128]{1,0:T(8,128)(2,1)S(1)} %collective-permute-done.15.refs_1_), custom_call_target="tpu_custom_call" | custom-call | tf_op jit(solution)/shard_map/pallas_call | solution.py:512
  77.0 1.7 %shard_map.63 = (bf16[4,8,128,128]{3,2,1,0:T(8,128)(2,1)S(1)}, bf16[4,8,128,128]{3,2,1,0:T(8,128)(2,1)}) custom-call(s32[14]{0:T(128)S(1)} %concatenate.6.drop_ref, bf16[1536,512]{1,0:T(8,128)(2,1)S(1)} %get-tuple-element.64.whole.own, bf16[1280,128]{1,0:T(8,128)(2,1)S(1)} %collective-permute-done.17.refs_0_), custom_call_target="tpu_custom_call" | custom-call | tf_op jit(solution)/shard_map/pallas_call | solution.py:512
  78.7 3.3 %collective-permute-done.18.cross = bf16[1280,128]{1,0:T(8,128)(2,1)S(1)} collective-permute-done((bf16[1280,128]{1,0:T(8,128)(2,1)S(1)}, bf16[1280,128]{1,0:T(8,128)(2,1)S(1)}, u32[]{:S(2)}, u32[]{:S(2)}) %collective-permute-start.18) | collective-permute-done | bytes 327712 | tf_op jit(solution)/shard_map/ppermute | solution.py:526
  82.1 1.3 %shard_map.64 = bf16[4,8,128,128]{3,2,1,0:T(8,128)(2,1)} custom-call(s32[14]{0:T(128)S(1)} %concatenate.6.drop_ref, bf16[4,8,128,128]{3,2,1,0:T(8,128)(2,1)S(1)} %get-tuple-element.71.slots, bf16[1280,128]{1,0:T(8,128)(2,1)S(1)} %collective-permute-done.18.cross, bf16[4,8,128,128]{3,2,1,0:T(8,128)(2,1)} %get-tuple-element.73.unused), custom_call_target="tpu_custom_call", output_to_operand_aliasing={{}: (3, {})} | custom-call | tf_op jit(solution)/shard_map/pallas_call | solution.py:512
  83.4 2.2 %collective-permute-done.16.cross = bf16[1280,128]{1,0:T(8,128)(2,1)S(1)} collective-permute-done((bf16[1280,128]{1,0:T(8,128)(2,1)S(1)}, bf16[1280,128]{1,0:T(8,128)(2,1)S(1)}, u32[]{:S(2)}, u32[]{:S(2)}) %collective-permute-start.16) | collective-permute-done | bytes 327712 | tf_op jit(solution)/shard_map/ppermute | solution.py:526
  (43 shorter events, 9.5 us)
Async XLA Ops:
  0.6 29.4 %collective-permute-start.2 = (bf16[4,8,128,128]{3,2,1,0:T(8,128)(2,1)}, bf16[4,8,128,128]{3,2,1,0:T(8,128)(2,1)S(1)}, u32[]{:S(2)}, u32[]{:S(2)}) collective-permute-start(bf16[4,8,128,128]{3,2,1,0:T(8,128)(2,1)} %own.2), channel_id=1, source_target_pairs={{0,15},{1,2},{2,1},{3,4},{4,3},{5,6},{6,5},{7,8},{8,7},{9,10},{10,... | collective-permute-start | bytes 3145736 | tf_op jit(solution)/shard_map/ppermute | solution.py:526
  2.5 27.6 %collective-permute-start.3 = (bf16[4,8,128,128]{3,2,1,0:T(8,128)(2,1)}, bf16[4,8,128,128]{3,2,1,0:T(8,128)(2,1)S(1)}, u32[]{:S(2)}, u32[]{:S(2)}) collective-permute-start(bf16[4,8,128,128]{3,2,1,0:T(8,128)(2,1)} %own.2), channel_id=1, source_target_pairs={{0,1},{1,0},{2,3},{3,2},{4,5},{5,4},{6,7},{7,6},{8,9},{9,8},{10,11... | collective-permute-start | bytes 3145736 | tf_op jit(solution)/shard_map/ppermute | solution.py:526
  3.4 1.2 %copy-start = (bf16[4,8,128,128]{3,2,1,0:T(8,128)(2,1)S(1)}, bf16[4,8,128,128]{3,2,1,0:T(8,128)(2,1)}, u32[]{:S(2)}) copy-start(bf16[4,8,128,128]{3,2,1,0:T(8,128)(2,1)} %own.3) | copy-start | bytes 3145732
  6.8 0.7 copy-start.2
  7.6 22.5 %collective-permute-start.4 = (bf16[3328,128]{1,0:T(8,128)(2,1)}, bf16[3328,128]{1,0:T(8,128)(2,1)S(1)}, u32[]{:S(2)}, u32[]{:S(2)}) collective-permute-start(bf16[3328,128]{1,0:T(8,128)(2,1)} %get-tuple-element.39.sent_mate), channel_id=1, source_target_pairs={{0,1},{1,0},{2,3},{3,2},{4,5},{5,4},{6,7},{7,6},{8,9},{9,8},{10,11... | collective-permute-start | bytes 2555912 | tf_op jit(solution)/shard_map/ppermute | solution.py:526
  8.1 1.8 %collective-permute-start.1 = (s32[4]{0:T(128)S(1)}, s32[4]{0:T(128)S(1)}, u32[]{:S(2)}, u32[]{:S(2)}) collective-permute-start(s32[4]{0:T(128)S(1)} %broadcast_subtract_fusion), channel_id=1, source_target_pairs={{0,1},{1,0},{2,3},{3,2},{4,5},{5,4},{6,7},{7,6},{8,9},{9,8},{10,11... | collective-permute-start | bytes 56 | tf_op jit(solution)/shard_map/ppermute | solution.py:526
  8.1 21.9 %collective-permute-start = (s32[4]{0:T(128)S(1)}, s32[4]{0:T(128)S(1)}, u32[]{:S(2)}, u32[]{:S(2)}) collective-permute-start(s32[4]{0:T(128)S(1)} %broadcast_subtract_fusion), channel_id=1, source_target_pairs={{0,15},{1,2},{2,1},{3,4},{4,3},{5,6},{6,5},{7,8},{8,7},{9,10},{10,... | collective-permute-start | bytes 56 | tf_op jit(solution)/shard_map/ppermute | solution.py:526
  9.9 27.9 %collective-permute-start.7 = (bf16[1280,128]{1,0:T(8,128)(2,1)}, bf16[1280,128]{1,0:T(8,128)(2,1)}, u32[]{:S(2)}, u32[]{:S(2)}) collective-permute-start(bf16[1280,128]{1,0:T(8,128)(2,1)} %copy-done.2), channel_id=1, source_target_pairs={{1,2},{2,1},{5,6},{6,5},{9,10},{10,9},{13,14},{14,13},{17,18},{18,... | collective-permute-start | bytes 983048 | tf_op jit(solution)/shard_map/ppermute | solution.py:526
  30.1 3.4 %copy-start.1 = (bf16[4,8,128,128]{3,2,1,0:T(8,128)(2,1)S(1)}, bf16[4,8,128,128]{3,2,1,0:T(8,128)(2,1)}, u32[]{:S(2)}) copy-start(bf16[4,8,128,128]{3,2,1,0:T(8,128)(2,1)} %own.2) | copy-start | bytes 3145732
  30.8 6.9 %collective-permute-start.8 = (bf16[1280,128]{1,0:T(8,128)(2,1)}, bf16[1280,128]{1,0:T(8,128)(2,1)S(1)}, u32[]{:S(2)}, u32[]{:S(2)}) collective-permute-start(bf16[1280,128]{1,0:T(8,128)(2,1)} %get-tuple-element.50), channel_id=1, source_target_pairs={{0,15},{3,4},{4,3},{7,8},{8,7},{11,12},{12,11},{15,0},{16,31},{19,... | collective-permute-start | bytes 983048 | tf_op jit(solution)/shard_map/ppermute | solution.py:526
  31.5 9.3 %collective-permute-start.5 = (bf16[1280,128]{1,0:T(8,128)(2,1)S(1)}, bf16[1280,128]{1,0:T(8,128)(2,1)S(1)}, u32[]{:S(2)}, u32[]{:S(2)}) collective-permute-start(bf16[1280,128]{1,0:T(8,128)(2,1)S(1)} %get-tuple-element.42), channel_id=1, source_target_pairs={{0,13},{1,4},{2,15},{3,6},{4,1},{5,8},{6,3},{7,10},{8,5},{9,12},{1... | collective-permute-start | bytes 983048 | tf_op jit(solution)/shard_map/ppermute | solution.py:526
  31.6 9.3 %collective-permute-start.6 = (bf16[1280,128]{1,0:T(8,128)(2,1)S(1)}, bf16[1280,128]{1,0:T(8,128)(2,1)S(1)}, u32[]{:S(2)}, u32[]{:S(2)}) collective-permute-start(bf16[1280,128]{1,0:T(8,128)(2,1)S(1)} %get-tuple-element.43), channel_id=1, source_target_pairs={{0,1},{1,0},{2,3},{3,2},{4,5},{5,4},{6,7},{7,6},{8,9},{9,8},{10,11... | collective-permute-start | bytes 983048 | tf_op jit(solution)/shard_map/ppermute | solution.py:526
  32.1 20.8 %collective-permute-start.9 = (bf16[2048,128]{1,0:T(8,128)(2,1)}, bf16[2048,128]{1,0:T(8,128)(2,1)S(1)}, u32[]{:S(2)}, u32[]{:S(2)}) collective-permute-start(bf16[2048,128]{1,0:T(8,128)(2,1)} %get-tuple-element.55), channel_id=1, source_target_pairs={{0,15},{1,2},{2,1},{3,4},{4,3},{5,6},{6,5},{7,8},{8,7},{9,10},{10,... | collective-permute-start | bytes 1572872 | tf_op jit(solution)/shard_map/ppermute | solution.py:526
  40.8 1.4 %copy-start.3 = (bf16[1280,128]{1,0:T(8,128)(2,1)S(1)}, bf16[1280,128]{1,0:T(8,128)(2,1)}, u32[]{:S(2)}) copy-start(bf16[1280,128]{1,0:T(8,128)(2,1)} %copy-done.2) | copy-start | bytes 983044
  44.7 22.3 %collective-permute-start.13 = (bf16[512,512]{1,0:T(8,128)(2,1)S(1)}, bf16[512,512]{1,0:T(8,128)(2,1)S(1)}, u32[]{:S(2)}, u32[]{:S(2)}) collective-permute-start(bf16[512,512]{1,0:T(8,128)(2,1)S(1)} %get-tuple-element.54.own), channel_id=1, source_target_pairs={{0,15},{1,2},{2,1},{3,4},{4,3},{5,6},{6,5},{7,8},{8,7},{9,10},{10,... | collective-permute-start | bytes 1572872 | tf_op jit(solution)/shard_map/ppermute | solution.py:526
  50.9 16.0 %collective-permute-start.12 = (bf16[512,512]{1,0:T(8,128)(2,1)S(1)}, bf16[512,512]{1,0:T(8,128)(2,1)S(1)}, u32[]{:S(2)}, u32[]{:S(2)}) collective-permute-start(bf16[512,512]{1,0:T(8,128)(2,1)S(1)} %get-tuple-element.54.own), channel_id=1, source_target_pairs={{0,1},{1,0},{2,3},{3,2},{4,5},{5,4},{6,7},{7,6},{8,9},{9,8},{10,11... | collective-permute-start | bytes 1572872 | tf_op jit(solution)/shard_map/ppermute | solution.py:526
  54.5 14.1 %collective-permute-start.10 = (bf16[1280,128]{1,0:T(8,128)(2,1)S(1)}, bf16[1280,128]{1,0:T(8,128)(2,1)S(1)}, u32[]{:S(2)}, u32[]{:S(2)}) collective-permute-start(bf16[1280,128]{1,0:T(8,128)(2,1)S(1)} %get-tuple-element.57), channel_id=1, source_target_pairs={{0,1},{1,0},{2,3},{3,2},{4,5},{5,4},{6,7},{7,6},{8,9},{9,8},{10,11... | collective-permute-start | bytes 983048 | tf_op jit(solution)/shard_map/ppermute | solution.py:526
  54.6 15.9 %collective-permute-start.11 = (bf16[1280,128]{1,0:T(8,128)(2,1)S(1)}, bf16[1280,128]{1,0:T(8,128)(2,1)S(1)}, u32[]{:S(2)}, u32[]{:S(2)}) collective-permute-start(bf16[1280,128]{1,0:T(8,128)(2,1)S(1)} %get-tuple-element.58), channel_id=1, source_target_pairs={{0,15},{1,2},{2,1},{3,4},{4,3},{5,6},{6,5},{7,8},{8,7},{9,10},{10,... | collective-permute-start | bytes 983048 | tf_op jit(solution)/shard_map/ppermute | solution.py:526
  68.4 8.6 %collective-permute-start.17 = (bf16[1280,128]{1,0:T(8,128)(2,1)S(1)}, bf16[1280,128]{1,0:T(8,128)(2,1)S(1)}, u32[]{:S(2)}, u32[]{:S(2)}) collective-permute-start(bf16[1280,128]{1,0:T(8,128)(2,1)S(1)} %get-tuple-element.70), channel_id=1, source_target_pairs={{0,1},{1,0},{2,3},{3,2},{4,5},{5,4},{6,7},{7,6},{8,9},{9,8},{10,11... | collective-permute-start | bytes 983048 | tf_op jit(solution)/shard_map/ppermute | solution.py:526
  68.5 13.6 %collective-permute-start.18 = (bf16[1280,128]{1,0:T(8,128)(2,1)S(1)}, bf16[1280,128]{1,0:T(8,128)(2,1)S(1)}, u32[]{:S(2)}, u32[]{:S(2)}) collective-permute-start(bf16[1280,128]{1,0:T(8,128)(2,1)S(1)} %get-tuple-element.72), channel_id=1, source_target_pairs={{0,15},{1,2},{2,1},{3,4},{4,3},{5,6},{6,5},{7,8},{8,7},{9,10},{10,... | collective-permute-start | bytes 983048 | tf_op jit(solution)/shard_map/ppermute | solution.py:526
  72.6 13.0 %collective-permute-start.16 = (bf16[1280,128]{1,0:T(8,128)(2,1)S(1)}, bf16[1280,128]{1,0:T(8,128)(2,1)S(1)}, u32[]{:S(2)}, u32[]{:S(2)}) collective-permute-start(bf16[1280,128]{1,0:T(8,128)(2,1)S(1)} %get-tuple-element.68), channel_id=1, source_target_pairs={{0,15},{1,2},{2,1},{3,4},{4,3},{5,6},{6,5},{7,8},{8,7},{9,10},{10,... | collective-permute-start | bytes 983048 | tf_op jit(solution)/shard_map/ppermute | solution.py:526
  72.7 2.5 %collective-permute-start.14 = (bf16[640,128]{1,0:T(8,128)(2,1)S(1)}, bf16[640,128]{1,0:T(8,128)(2,1)S(1)}, u32[]{:S(2)}, u32[]{:S(2)}) collective-permute-start(bf16[640,128]{1,0:T(8,128)(2,1)S(1)} %get-tuple-element.65), channel_id=1, source_target_pairs={{0,1},{1,0},{2,3},{3,2},{4,5},{5,4},{6,7},{7,6},{8,9},{9,8},{10,11... | collective-permute-start | bytes 491528 | tf_op jit(solution)/shard_map/ppermute | solution.py:526
  73.9 1.4 %collective-permute-start.15 = (bf16[640,128]{1,0:T(8,128)(2,1)S(1)}, bf16[640,128]{1,0:T(8,128)(2,1)S(1)}, u32[]{:S(2)}, u32[]{:S(2)}) collective-permute-start(bf16[640,128]{1,0:T(8,128)(2,1)S(1)} %get-tuple-element.66), channel_id=1, source_target_pairs={{0,1},{1,0},{2,3},{3,2},{4,5},{5,4},{6,7},{7,6},{8,9},{9,8},{10,11... | collective-permute-start | bytes 491528 | tf_op jit(solution)/shard_map/ppermute | solution.py:526

commit v20 on v18

--- a/solution.py
+++ b/solution.py
@@ -265,7 +265,7 @@
 
 def first_sweep_kernel(
     f, drop_ref, shifted, corners, corner, sent_mate, sent_cross, mate, direct, turned,
-    correction, fresh, partial, whole, before, after,
+    correction, fresh, whole, before, after,
 ):
     h, p = f.h, f.p
     turning = drop_ref[3 * h + 1] == 1
@@ -285,23 +285,16 @@
         total = masked(f, right_tile(f, shifted, corners, whole, row, col), row, col, drop_ref)
         correction[at(f, row, row + 1, col - p, col - p + 1)] = total.astype(correction.dtype)
     for row, col in f.tiles(f.own_pairs):
-        c = col - p
-        own_row = row in f.own_pairs
+        if row not in f.own_pairs:
+            continue
+        c, local = col - p, row - p
         total = 2.0 * whole[at(f, row, row + 1, c, c + 1)].astype(jnp.float32)
         for g, a, z in f.split(row, col):
-            if g == 1:
-                left = whole[at(f, row, row + 1, a, z)]
-            elif own_row:
-                left = (before, None, after)[g][at(f, row - p, row - p + 1, a, z)]
-            else:
-                continue
+            source, first = (before, local) if g == 0 else (whole, row) if g == 1 else (after, local)
+            left = source[at(f, first, first + 1, a, z)]
             total = total - dot(left, correction[at(f, g * p + a, g * p + z, c, c + 1)])
-        if own_row:
-            total = masked(f, total, row, col, drop_ref)
-            fresh[at(f, row - p, row - p + 1, c, c + 1)] = total.astype(fresh.dtype)
-        else:
-            place = row if row < p else row - p
-            partial[at(f, place, place + 1, c, c + 1)] = total
+        total = masked(f, total, row, col, drop_ref)
+        fresh[at(f, local, local + 1, c, c + 1)] = total.astype(fresh.dtype)
 
 
 def edges(f, drop_ref, corner_below, corner_above, correction, start, low, high):
@@ -324,7 +317,7 @@
 
 
 def first_edges_kernel(
-    f, drop_ref, mate, cross, correction, partial, low, high, to_cross, to_mate, before, after
+    f, drop_ref, mate, cross, correction, whole, low, high, to_cross, to_mate, before, after
 ):
     p = f.p
     below, above = sides(f, drop_ref, indexed(f, mate, len(under(f.h))), indexed(f, cross))
@@ -332,8 +325,14 @@
     spread(f, after, 0, 0, above, full(f.h))
 
     def start(row, col):
-        place = row if row < p else row - p
-        return partial[at(f, place, place + 1, col - p, col - p + 1)]
+        c = col - p
+        total = 2.0 * whole[at(f, row, row + 1, c, c + 1)].astype(jnp.float32)
+        for g, a, z in f.split(row, col):
+            if g == 1:
+                total = total - dot(
+                    whole[at(f, row, row + 1, a, z)], correction[at(f, p + a, p + z, c, c + 1)]
+                )
+        return total
 
     edges(f, drop_ref, plain(before), plain(after), correction, start, low, high)
     pack_edges(f, drop_ref, low, high, to_cross, to_mate)
@@ -590,11 +589,11 @@
         [group_scratch] * 2,
         10, 16, drop, far_far, far_mate, reach, here, partial, direct_triangle, light=True,
     )
-    correction, own, partial = run(
+    correction, own, columns_start = run(
         first_sweep_kernel,
-        [columns, square_group, partial_sums],
-        [whole_scratch, group_scratch, group_scratch],
-        66, 24, drop, shifted, shifted_corners, corner, slab_mate, triangle_cross, from_mate,
+        [columns, square_group, columns],
+        [group_scratch, group_scratch],
+        56, 24, drop, shifted, shifted_corners, corner, slab_mate, triangle_cross, from_mate,
         direct_triangle, turned_triangle, light=True,
     )
     corner_cross, corner_mate = to_cross(own), to_mate(own)
@@ -602,7 +601,7 @@
         first_edges_kernel,
         [square_group, square_group, triangle, triangle],
         [group_scratch] * 2,
-        10, 16, drop, from_mate, cross_corner, correction, partial,
+        20, 16, drop, from_mate, cross_corner, correction, columns_start,
     )
     edge_cross, edge_mate = to_cross(edge_cross), to_mate(edge_mate)
     (correction,) = run(

time: 85.6 us -> 85.6 us (level)
  no operation moved by 1% of the time
where the time goes in v20:
time: 85.6 us; the launch traced here: 85.3 us
  waiting for transfers between devices  31.5 us (37%)
  Pallas kernels  26.6 us (31%)
  starting transfers between devices  22.6 us (26%)
  local copies, waits for them, and re-layouts  2.83 us (3%)
  other arithmetic  0.96 us (1%)
  between operations  0.86 us (1%)
    ppermute x19, waiting for transfers between devices, routed(): lax.ppermute(x, RING, [(i, (i + step(i)) % size) for i in range(size) if...  31.5 us
    pallas_call x14, Pallas kernels, call(): pl.pallas_call(kernel, out_shape=[*outs, *[jax.ShapeDtypeStruct(a.shape,...  26.6 us
    ppermute x19, starting transfers between devices, routed(): lax.ppermute(x, RING, [(i, (i + step(i)) % size) for i in range(size) if...  22.6 us
    unnamed x12, local copies, waits for them, and re-layouts  2.75 us
  transfers between devices with their start and end apart: 19, of which 9 were waited for; matrix products, arithmetic and copies ran while one was open for 1% of the time, Pallas kernels for 30%

profile of v20, /device:TPU:1, one launch (start us, length us, event | category | flops | bytes accessed | tf_op | source)
XLA Modules:
  0.0 85.3 jit_solution(15084912515934737950)
XLA Ops:
  0.6 2.7 %collective-permute-start.2 = (bf16[4,8,128,128]{3,2,1,0:T(8,128)(2,1)}, bf16[4,8,128,128]{3,2,1,0:T(8,128)(2,1)S(1)}, u32[]{:S(2)}, u32[]{:S(2)}) collective-permute-start(bf16[4,8,128,128]{3,2,1,0:T(8,128)(2,1)} %own.2), channel_id=1, source_target_pairs={{0,15},{1,2},{2,1},{3,4},{4,3},{5,6},{6,5},{7,8},{8,7},{9,10},{10,... | collective-permute-start | bytes 3145736 | tf_op jit(solution)/shard_map/ppermute | solution.py:507
  3.3 2.9 %collective-permute-start.3 = (bf16[4,8,128,128]{3,2,1,0:T(8,128)(2,1)}, bf16[4,8,128,128]{3,2,1,0:T(8,128)(2,1)S(1)}, u32[]{:S(2)}, u32[]{:S(2)}) collective-permute-start(bf16[4,8,128,128]{3,2,1,0:T(8,128)(2,1)} %own.2), channel_id=1, source_target_pairs={{0,1},{1,0},{2,3},{3,2},{4,5},{5,4},{6,7},{7,6},{8,9},{9,8},{10,11... | collective-permute-start | bytes 3145736 | tf_op jit(solution)/shard_map/ppermute | solution.py:507
  8.4 2.2 %shard_map.51 = (bf16[2048,128]{1,0:T(8,128)(2,1)S(1)}, bf16[2048,128]{1,0:T(8,128)(2,1)}, bf16[3328,128]{1,0:T(8,128)(2,1)}, bf16[1280,128]{1,0:T(8,128)(2,1)S(1)}, bf16[1280,128]{1,0:T(8,128)(2,1)}) custom-call(s32[5]{0:T(128)S(1)} %pad_add_fusion.drop_ref, bf16[4,8,128,128]{3,2,1,0:T(8,128)(2,1)S(1)} %copy-done), custom_call_target="tpu_custom_call" | custom-call | bytes 3604480 | tf_op jit(solution)/shard_map/pallas_call | solution.py:493
  12.6 1.5 %collective-permute-done.1 = s32[4]{0:T(128)S(1)} collective-permute-done((s32[4]{0:T(128)S(1)}, s32[4]{0:T(128)S(1)}, u32[]{:S(2)}, u32[]{:S(2)}) %collective-permute-start.1) | collective-permute-done | bytes 48 | tf_op jit(solution)/shard_map/ppermute | solution.py:507
  14.1 2.1 %collective-permute-start.7 = (bf16[1280,128]{1,0:T(8,128)(2,1)}, bf16[1280,128]{1,0:T(8,128)(2,1)S(1)}, u32[]{:S(2)}, u32[]{:S(2)}) collective-permute-start(bf16[1280,128]{1,0:T(8,128)(2,1)} %copy-done.4), channel_id=1, source_target_pairs={{1,2},{2,1},{5,6},{6,5},{9,10},{10,9},{13,14},{14,13},{17,18},{18,... | collective-permute-start | bytes 983048 | tf_op jit(solution)/shard_map/ppermute | solution.py:507
  16.2 11.1 %collective-permute-done = s32[4]{0:T(128)S(1)} collective-permute-done((s32[4]{0:T(128)S(1)}, s32[4]{0:T(128)S(1)}, u32[]{:S(2)}, u32[]{:S(2)}) %collective-permute-start) | collective-permute-done | bytes 48 | tf_op jit(solution)/shard_map/ppermute | solution.py:507
  28.2 3.7 %collective-permute-start.6 = (bf16[1280,128]{1,0:T(8,128)(2,1)S(1)}, bf16[1280,128]{1,0:T(8,128)(2,1)S(1)}, u32[]{:S(2)}, u32[]{:S(2)}) collective-permute-start(bf16[1280,128]{1,0:T(8,128)(2,1)S(1)} %get-tuple-element.43), channel_id=1, source_target_pairs={{0,1},{1,0},{2,3},{3,2},{4,5},{5,4},{6,7},{7,6},{8,9},{9,8},{10,11... | collective-permute-start | bytes 983048 | tf_op jit(solution)/shard_map/ppermute | solution.py:507
  32.7 4.3 %shard_map.50 = (bf16[1536,1280]{1,0:T(8,128)(2,1)S(1)}, bf16[1536,1280]{1,0:T(8,128)(2,1)S(1)}, bf16[1024,512]{1,0:T(8,128)(2,1)S(1)}, bf16[1024,512]{1,0:T(8,128)(2,1)S(1)}, f32[1024,512]{1,0:T(8,128)S(1)}) custom-call(s32[14]{0:T(128)S(1)} %concatenate.6.drop_ref, bf16[4,8,128,128]{3,2,1,0:T(8,128)(2,1)S(1)} %copy-done.1, ...), custom_call_target="tpu_custom_call" | custom-call | tf_op jit(solution)/shard_map/pallas_call | solution.py:493
  37.9 1.4 %shard_map.53 = (bf16[1024,512]{1,0:T(8,128)(2,1)S(1)}, bf16[1024,512]{1,0:T(8,128)(2,1)S(1)}) custom-call(s32[14]{0:T(128)S(1)} %concatenate.6.drop_ref, bf16[1280,128]{1,0:T(8,128)(2,1)S(1)} %collective-permute-done.5.far_far, bf16[1280,128]{1,0:T(8,128)(2,1)S(1)} %collective-permute-done.6.far_mate, bf16[1024,512]{1,0:T(8,128)(2,1)S(1)} %get-tuple-element.44.reach, ...), custom_call_target="tpu_custom_call" | custom-call | tf_op jit(solution)/shard_map/pallas_call | solution.py:493
  39.4 3.4 %shard_map.54 = (bf16[1536,512]{1,0:T(8,128)(2,1)S(1)}, bf16[512,512]{1,0:T(8,128)(2,1)S(1)}, bf16[1536,512]{1,0:T(8,128)(2,1)S(1)}) custom-call(s32[14]{0:T(128)S(1)} %concatenate.6.drop_ref, bf16[1536,1280]{1,0:T(8,128)(2,1)S(1)} %get-tuple-element.38.shifted, bf16[1024,512]{1,0:T(8,128)(2,1)S(1)} %get-tuple-element.48.corners, ...), custom_call_target="tpu_custom_call" | custom-call | tf_op jit(solution)/shard_map/pallas_call | solution.py:493
  42.8 3.6 %collective-permute-start.13 = (bf16[512,512]{1,0:T(8,128)(2,1)S(1)}, bf16[512,512]{1,0:T(8,128)(2,1)S(1)}, u32[]{:S(2)}, u32[]{:S(2)}) collective-permute-start(bf16[512,512]{1,0:T(8,128)(2,1)S(1)} %get-tuple-element.51.own), channel_id=1, source_target_pairs={{0,15},{1,2},{2,1},{3,4},{4,3},{5,6},{6,5},{7,8},{8,7},{9,10},{10,... | collective-permute-start | bytes 1572872 | tf_op jit(solution)/shard_map/ppermute | solution.py:507
  46.4 2.8 %collective-permute-start.12 = (bf16[512,512]{1,0:T(8,128)(2,1)S(1)}, bf16[512,512]{1,0:T(8,128)(2,1)S(1)}, u32[]{:S(2)}, u32[]{:S(2)}) collective-permute-start(bf16[512,512]{1,0:T(8,128)(2,1)S(1)} %get-tuple-element.51.own), channel_id=1, source_target_pairs={{0,1},{1,0},{2,3},{3,2},{4,5},{5,4},{6,7},{7,6},{8,9},{9,8},{10,11... | collective-permute-start | bytes 1572872 | tf_op jit(solution)/shard_map/ppermute | solution.py:507
  49.2 1.4 %collective-permute-done.9.cross = bf16[2048,128]{1,0:T(8,128)(2,1)S(1)} collective-permute-done((bf16[2048,128]{1,0:T(8,128)(2,1)}, bf16[2048,128]{1,0:T(8,128)(2,1)S(1)}, u32[]{:S(2)}, u32[]{:S(2)}) %collective-permute-start.9) | collective-permute-done | bytes 524320 | tf_op jit(solution)/shard_map/ppermute | solution.py:507
  50.6 1.5 %shard_map.55 = (bf16[512,512]{1,0:T(8,128)(2,1)S(1)}, bf16[512,512]{1,0:T(8,128)(2,1)S(1)}, bf16[1280,128]{1,0:T(8,128)(2,1)S(1)}, bf16[1280,128]{1,0:T(8,128)(2,1)S(1)}) custom-call(s32[14]{0:T(128)S(1)} %concatenate.6.drop_ref, bf16[3328,128]{1,0:T(8,128)(2,1)S(1)} %collective-permute-done.4.refs_1_.mate, ...), custom_call_target="tpu_custom_call" | custom-call | flops 671088640 | bytes 6225920 | tf_op jit(solution)/shard_map/pallas_call | solution.py:493
  52.4 2.0 %shard_map.56.correction = bf16[1536,512]{1,0:T(8,128)(2,1)S(1)} custom-call(s32[14]{0:T(128)S(1)} %concatenate.6.drop_ref, bf16[1536,1280]{1,0:T(8,128)(2,1)S(1)} %get-tuple-element.38.shifted, bf16[1024,512]{1,0:T(8,128)(2,1)S(1)} %get-tuple-element.48.corners, bf16[512,512]{1,0:T(8,128)(2,1)S(1)} %get-tuple-element.57.low, ...), custom_call_target="tpu_custom_call" | custom-call | flops 1275068416 | bytes 8126464 | tf_op jit(solution)/shard_map/pallas_call | solution.py:493
  54.4 10.9 %collective-permute-done.13.cross = bf16[512,512]{1,0:T(8,128)(2,1)S(1)} collective-permute-done((bf16[512,512]{1,0:T(8,128)(2,1)S(1)}, bf16[512,512]{1,0:T(8,128)(2,1)S(1)}, u32[]{:S(2)}, u32[]{:S(2)}) %collective-permute-start.13) | collective-permute-done | bytes 524320 | tf_op jit(solution)/shard_map/ppermute | solution.py:507
  65.4 1.5 %shard_map.57 = (bf16[512,512]{1,0:T(8,128)(2,1)S(1)}, bf16[512,512]{1,0:T(8,128)(2,1)S(1)}, bf16[1280,128]{1,0:T(8,128)(2,1)S(1)}, bf16[1280,128]{1,0:T(8,128)(2,1)S(1)}) custom-call(s32[14]{0:T(128)S(1)} %concatenate.6.drop_ref, bf16[512,512]{1,0:T(8,128)(2,1)S(1)} %collective-permute-done.12.mate, bf16[512,512]{1,0:T(8,128)(2,1)S(1)} %collective-permute-done.13.cross, ...), custom_call_target="tpu_custom_call" | custom-call | flops 671088640 | bytes 5373952 | tf_op jit(solution)/shard_map/pallas_call | solution.py:493
  67.0 1.9 %collective-permute-done.11.cross = bf16[1280,128]{1,0:T(8,128)(2,1)S(1)} collective-permute-done((bf16[1280,128]{1,0:T(8,128)(2,1)S(1)}, bf16[1280,128]{1,0:T(8,128)(2,1)S(1)}, u32[]{:S(2)}, u32[]{:S(2)}) %collective-permute-start.11) | collective-permute-done | bytes 327712 | tf_op jit(solution)/shard_map/ppermute | solution.py:507
  68.9 2.2 %shard_map.58 = (bf16[1536,512]{1,0:T(8,128)(2,1)S(1)}, bf16[1280,128]{1,0:T(8,128)(2,1)S(1)}, bf16[640,128]{1,0:T(8,128)(2,1)S(1)}, bf16[640,128]{1,0:T(8,128)(2,1)S(1)}) custom-call(s32[14]{0:T(128)S(1)} %concatenate.6.drop_ref, bf16[512,512]{1,0:T(8,128)(2,1)S(1)} %get-tuple-element.51.own, bf16[1280,128]{1,0:T(8,128)(2,1)S(1)} %collective-permute-done.10.mate, ...), custom_call_target="tpu_custom_call" | custom-call | flops 1275068416 | bytes 11010048 | tf_op jit(solution)/shard_map/pallas_call | solution.py:493
  71.1 3.0 %collective-permute-start.14 = (bf16[640,128]{1,0:T(8,128)(2,1)S(1)}, bf16[640,128]{1,0:T(8,128)(2,1)S(1)}, u32[]{:S(2)}, u32[]{:S(2)}) collective-permute-start(bf16[640,128]{1,0:T(8,128)(2,1)S(1)} %get-tuple-element.63), channel_id=1, source_target_pairs={{0,1},{1,0},{2,3},{3,2},{4,5},{5,4},{6,7},{7,6},{8,9},{9,8},{10,11... | collective-permute-start | bytes 491528 | tf_op jit(solution)/shard_map/ppermute | solution.py:507
  75.5 1.7 %shard_map.60 = (bf16[4,8,128,128]{3,2,1,0:T(8,128)(2,1)S(1)}, bf16[4,8,128,128]{3,2,1,0:T(8,128)(2,1)}) custom-call(s32[14]{0:T(128)S(1)} %concatenate.6.drop_ref, bf16[512,512]{1,0:T(8,128)(2,1)S(1)} %shard_map.59.own, bf16[640,128]{1,0:T(8,128)(2,1)S(1)} %collective-permute-done.14.refs_0_, bf16[640,128]{1,0:T(8,128)(2,1)S(1)} %collective-permute-done.15.refs_1_), custom_call_target="tpu_custom_call" | custom-call | tf_op jit(solution)/shard_map/pallas_call | solution.py:493
  77.3 1.7 %shard_map.62 = (bf16[4,8,128,128]{3,2,1,0:T(8,128)(2,1)S(1)}, bf16[4,8,128,128]{3,2,1,0:T(8,128)(2,1)}) custom-call(s32[14]{0:T(128)S(1)} %concatenate.6.drop_ref, bf16[1536,512]{1,0:T(8,128)(2,1)S(1)} %get-tuple-element.62.whole.own, bf16[1280,128]{1,0:T(8,128)(2,1)S(1)} %collective-permute-done.17.refs_0_), custom_call_target="tpu_custom_call" | custom-call | tf_op jit(solution)/shard_map/pallas_call | solution.py:493
  79.0 1.5 %collective-permute-done.18.cross = bf16[1280,128]{1,0:T(8,128)(2,1)S(1)} collective-permute-done((bf16[1280,128]{1,0:T(8,128)(2,1)S(1)}, bf16[1280,128]{1,0:T(8,128)(2,1)S(1)}, u32[]{:S(2)}, u32[]{:S(2)}) %collective-permute-start.18) | collective-permute-done | bytes 327712 | tf_op jit(solution)/shard_map/ppermute | solution.py:507
  81.8 2.2 %collective-permute-done.16.cross = bf16[1280,128]{1,0:T(8,128)(2,1)S(1)} collective-permute-done((bf16[1280,128]{1,0:T(8,128)(2,1)S(1)}, bf16[1280,128]{1,0:T(8,128)(2,1)S(1)}, u32[]{:S(2)}, u32[]{:S(2)}) %collective-permute-start.16) | collective-permute-done | bytes 327712 | tf_op jit(solution)/shard_map/ppermute | solution.py:507
  (46 shorter events, 11.3 us)
Async XLA Ops:
  0.6 26.8 %collective-permute-start.2 = (bf16[4,8,128,128]{3,2,1,0:T(8,128)(2,1)}, bf16[4,8,128,128]{3,2,1,0:T(8,128)(2,1)S(1)}, u32[]{:S(2)}, u32[]{:S(2)}) collective-permute-start(bf16[4,8,128,128]{3,2,1,0:T(8,128)(2,1)} %own.2), channel_id=1, source_target_pairs={{0,15},{1,2},{2,1},{3,4},{4,3},{5,6},{6,5},{7,8},{8,7},{9,10},{10,... | collective-permute-start | bytes 3145736 | tf_op jit(solution)/shard_map/ppermute | solution.py:507
  3.3 24.1 %collective-permute-start.3 = (bf16[4,8,128,128]{3,2,1,0:T(8,128)(2,1)}, bf16[4,8,128,128]{3,2,1,0:T(8,128)(2,1)S(1)}, u32[]{:S(2)}, u32[]{:S(2)}) collective-permute-start(bf16[4,8,128,128]{3,2,1,0:T(8,128)(2,1)} %own.2), channel_id=1, source_target_pairs={{0,1},{1,0},{2,3},{3,2},{4,5},{5,4},{6,7},{7,6},{8,9},{9,8},{10,11... | collective-permute-start | bytes 3145736 | tf_op jit(solution)/shard_map/ppermute | solution.py:507
  7.1 1.2 %copy-start = (bf16[4,8,128,128]{3,2,1,0:T(8,128)(2,1)S(1)}, bf16[4,8,128,128]{3,2,1,0:T(8,128)(2,1)}, u32[]{:S(2)}) copy-start(bf16[4,8,128,128]{3,2,1,0:T(8,128)(2,1)} %own.3) | copy-start | bytes 3145732
  10.5 0.8 copy-start.2
  12.0 15.3 %collective-permute-start.4 = (bf16[3328,128]{1,0:T(8,128)(2,1)}, bf16[3328,128]{1,0:T(8,128)(2,1)S(1)}, u32[]{:S(2)}, u32[]{:S(2)}) collective-permute-start(bf16[3328,128]{1,0:T(8,128)(2,1)} %get-tuple-element.39.sent_mate), channel_id=1, source_target_pairs={{0,1},{1,0},{2,3},{3,2},{4,5},{5,4},{6,7},{7,6},{8,9},{9,8},{10,11... | collective-permute-start | bytes 2555912 | tf_op jit(solution)/shard_map/ppermute | solution.py:507
  12.0 2.0 %collective-permute-start.1 = (s32[4]{0:T(128)S(1)}, s32[4]{0:T(128)S(1)}, u32[]{:S(2)}, u32[]{:S(2)}) collective-permute-start(s32[4]{0:T(128)S(1)} %broadcast_subtract_fusion), channel_id=1, source_target_pairs={{0,1},{1,0},{2,3},{3,2},{4,5},{5,4},{6,7},{7,6},{8,9},{9,8},{10,11... | collective-permute-start | bytes 56 | tf_op jit(solution)/shard_map/ppermute | solution.py:507
  12.6 14.7 %collective-permute-start = (s32[4]{0:T(128)S(1)}, s32[4]{0:T(128)S(1)}, u32[]{:S(2)}, u32[]{:S(2)}) collective-permute-start(s32[4]{0:T(128)S(1)} %broadcast_subtract_fusion), channel_id=1, source_target_pairs={{0,15},{1,2},{2,1},{3,4},{4,3},{5,6},{6,5},{7,8},{8,7},{9,10},{10,... | collective-permute-start | bytes 56 | tf_op jit(solution)/shard_map/ppermute | solution.py:507
  14.1 22.9 %collective-permute-start.7 = (bf16[1280,128]{1,0:T(8,128)(2,1)}, bf16[1280,128]{1,0:T(8,128)(2,1)S(1)}, u32[]{:S(2)}, u32[]{:S(2)}) collective-permute-start(bf16[1280,128]{1,0:T(8,128)(2,1)} %copy-done.4), channel_id=1, source_target_pairs={{1,2},{2,1},{5,6},{6,5},{9,10},{10,9},{13,14},{14,13},{17,18},{18,... | collective-permute-start | bytes 983048 | tf_op jit(solution)/shard_map/ppermute | solution.py:507
  27.4 5.3 %copy-start.1 = (bf16[4,8,128,128]{3,2,1,0:T(8,128)(2,1)S(1)}, bf16[4,8,128,128]{3,2,1,0:T(8,128)(2,1)}, u32[]{:S(2)}) copy-start(bf16[4,8,128,128]{3,2,1,0:T(8,128)(2,1)} %own.2) | copy-start | bytes 3145732
  28.1 9.8 %collective-permute-start.5 = (bf16[1280,128]{1,0:T(8,128)(2,1)S(1)}, bf16[1280,128]{1,0:T(8,128)(2,1)S(1)}, u32[]{:S(2)}, u32[]{:S(2)}) collective-permute-start(bf16[1280,128]{1,0:T(8,128)(2,1)S(1)} %get-tuple-element.42), channel_id=1, source_target_pairs={{0,13},{1,4},{2,15},{3,6},{4,1},{5,8},{6,3},{7,10},{8,5},{9,12},{1... | collective-permute-start | bytes 983048 | tf_op jit(solution)/shard_map/ppermute | solution.py:507
  28.2 9.7 %collective-permute-start.6 = (bf16[1280,128]{1,0:T(8,128)(2,1)S(1)}, bf16[1280,128]{1,0:T(8,128)(2,1)S(1)}, u32[]{:S(2)}, u32[]{:S(2)}) collective-permute-start(bf16[1280,128]{1,0:T(8,128)(2,1)S(1)} %get-tuple-element.43), channel_id=1, source_target_pairs={{0,1},{1,0},{2,3},{3,2},{4,5},{5,4},{6,7},{7,6},{8,9},{9,8},{10,11... | collective-permute-start | bytes 983048 | tf_op jit(solution)/shard_map/ppermute | solution.py:507
  31.9 7.4 %collective-permute-start.8 = (bf16[1280,128]{1,0:T(8,128)(2,1)}, bf16[1280,128]{1,0:T(8,128)(2,1)S(1)}, u32[]{:S(2)}, u32[]{:S(2)}) collective-permute-start(bf16[1280,128]{1,0:T(8,128)(2,1)} %get-tuple-element.50), channel_id=1, source_target_pairs={{0,15},{3,4},{4,3},{7,8},{8,7},{11,12},{12,11},{15,0},{16,31},{19,... | collective-permute-start | bytes 983048 | tf_op jit(solution)/shard_map/ppermute | solution.py:507
  32.6 18.0 %collective-permute-start.9 = (bf16[2048,128]{1,0:T(8,128)(2,1)}, bf16[2048,128]{1,0:T(8,128)(2,1)S(1)}, u32[]{:S(2)}, u32[]{:S(2)}) collective-permute-start(bf16[2048,128]{1,0:T(8,128)(2,1)} %get-tuple-element.52), channel_id=1, source_target_pairs={{0,15},{1,2},{2,1},{3,4},{4,3},{5,6},{6,5},{7,8},{8,7},{9,10},{10,... | collective-permute-start | bytes 1572872 | tf_op jit(solution)/shard_map/ppermute | solution.py:507
  37.9 1.4 %copy-start.3 = (bf16[2048,128]{1,0:T(8,128)(2,1)S(1)}, bf16[2048,128]{1,0:T(8,128)(2,1)}, u32[]{:S(2)}) copy-start(bf16[2048,128]{1,0:T(8,128)(2,1)} %copy-done.2) | copy-start | bytes 1572868
  37.9 1.4 %copy-start.5 = (bf16[1280,128]{1,0:T(8,128)(2,1)S(1)}, bf16[1280,128]{1,0:T(8,128)(2,1)}, u32[]{:S(2)}) copy-start(bf16[1280,128]{1,0:T(8,128)(2,1)} %copy-done.4) | copy-start | bytes 983044
  42.8 22.6 %collective-permute-start.13 = (bf16[512,512]{1,0:T(8,128)(2,1)S(1)}, bf16[512,512]{1,0:T(8,128)(2,1)S(1)}, u32[]{:S(2)}, u32[]{:S(2)}) collective-permute-start(bf16[512,512]{1,0:T(8,128)(2,1)S(1)} %get-tuple-element.51.own), channel_id=1, source_target_pairs={{0,15},{1,2},{2,1},{3,4},{4,3},{5,6},{6,5},{7,8},{8,7},{9,10},{10,... | collective-permute-start | bytes 1572872 | tf_op jit(solution)/shard_map/ppermute | solution.py:507
  46.4 18.9 %collective-permute-start.12 = (bf16[512,512]{1,0:T(8,128)(2,1)S(1)}, bf16[512,512]{1,0:T(8,128)(2,1)S(1)}, u32[]{:S(2)}, u32[]{:S(2)}) collective-permute-start(bf16[512,512]{1,0:T(8,128)(2,1)S(1)} %get-tuple-element.51.own), channel_id=1, source_target_pairs={{0,1},{1,0},{2,3},{3,2},{4,5},{5,4},{6,7},{7,6},{8,9},{9,8},{10,11... | collective-permute-start | bytes 1572872 | tf_op jit(solution)/shard_map/ppermute | solution.py:507
  52.1 14.9 %collective-permute-start.10 = (bf16[1280,128]{1,0:T(8,128)(2,1)S(1)}, bf16[1280,128]{1,0:T(8,128)(2,1)S(1)}, u32[]{:S(2)}, u32[]{:S(2)}) collective-permute-start(bf16[1280,128]{1,0:T(8,128)(2,1)S(1)} %get-tuple-element.55), channel_id=1, source_target_pairs={{0,1},{1,0},{2,3},{3,2},{4,5},{5,4},{6,7},{7,6},{8,9},{9,8},{10,11... | collective-permute-start | bytes 983048 | tf_op jit(solution)/shard_map/ppermute | solution.py:507
  52.4 16.5 %collective-permute-start.11 = (bf16[1280,128]{1,0:T(8,128)(2,1)S(1)}, bf16[1280,128]{1,0:T(8,128)(2,1)S(1)}, u32[]{:S(2)}, u32[]{:S(2)}) collective-permute-start(bf16[1280,128]{1,0:T(8,128)(2,1)S(1)} %get-tuple-element.56), channel_id=1, source_target_pairs={{0,15},{1,2},{2,1},{3,4},{4,3},{5,6},{6,5},{7,8},{8,7},{9,10},{10,... | collective-permute-start | bytes 983048 | tf_op jit(solution)/shard_map/ppermute | solution.py:507
  66.8 10.4 %collective-permute-start.17 = (bf16[1280,128]{1,0:T(8,128)(2,1)S(1)}, bf16[1280,128]{1,0:T(8,128)(2,1)S(1)}, u32[]{:S(2)}, u32[]{:S(2)}) collective-permute-start(bf16[1280,128]{1,0:T(8,128)(2,1)S(1)} %get-tuple-element.68), channel_id=1, source_target_pairs={{0,1},{1,0},{2,3},{3,2},{4,5},{5,4},{6,7},{7,6},{8,9},{9,8},{10,11... | collective-permute-start | bytes 983048 | tf_op jit(solution)/shard_map/ppermute | solution.py:507
  66.9 13.6 %collective-permute-start.18 = (bf16[1280,128]{1,0:T(8,128)(2,1)S(1)}, bf16[1280,128]{1,0:T(8,128)(2,1)S(1)}, u32[]{:S(2)}, u32[]{:S(2)}) collective-permute-start(bf16[1280,128]{1,0:T(8,128)(2,1)S(1)} %get-tuple-element.70), channel_id=1, source_target_pairs={{0,15},{1,2},{2,1},{3,4},{4,3},{5,6},{6,5},{7,8},{8,7},{9,10},{10,... | collective-permute-start | bytes 983048 | tf_op jit(solution)/shard_map/ppermute | solution.py:507
  71.0 13.0 %collective-permute-start.16 = (bf16[1280,128]{1,0:T(8,128)(2,1)S(1)}, bf16[1280,128]{1,0:T(8,128)(2,1)S(1)}, u32[]{:S(2)}, u32[]{:S(2)}) collective-permute-start(bf16[1280,128]{1,0:T(8,128)(2,1)S(1)} %get-tuple-element.66), channel_id=1, source_target_pairs={{0,15},{1,2},{2,1},{3,4},{4,3},{5,6},{6,5},{7,8},{8,7},{9,10},{10,... | collective-permute-start | bytes 983048 | tf_op jit(solution)/shard_map/ppermute | solution.py:507
  71.1 4.3 %collective-permute-start.14 = (bf16[640,128]{1,0:T(8,128)(2,1)S(1)}, bf16[640,128]{1,0:T(8,128)(2,1)S(1)}, u32[]{:S(2)}, u32[]{:S(2)}) collective-permute-start(bf16[640,128]{1,0:T(8,128)(2,1)S(1)} %get-tuple-element.63), channel_id=1, source_target_pairs={{0,1},{1,0},{2,3},{3,2},{4,5},{5,4},{6,7},{7,6},{8,9},{9,8},{10,11... | collective-permute-start | bytes 491528 | tf_op jit(solution)/shard_map/ppermute | solution.py:507
  74.1 1.4 %collective-permute-start.15 = (bf16[640,128]{1,0:T(8,128)(2,1)S(1)}, bf16[640,128]{1,0:T(8,128)(2,1)S(1)}, u32[]{:S(2)}, u32[]{:S(2)}) collective-permute-start(bf16[640,128]{1,0:T(8,128)(2,1)S(1)} %get-tuple-element.64), channel_id=1, source_target_pairs={{0,1},{1,0},{2,3},{3,2},{4,5},{5,4},{6,7},{7,6},{8,9},{9,8},{10,11... | collective-permute-start | bytes 491528 | tf_op jit(solution)/shard_map/ppermute | solution.py:507
  (1 other events, 0.7 us)

commit v21 on v15

--- a/solution.py
+++ b/solution.py
@@ -265,7 +265,7 @@
 
 def first_sweep_kernel(
     f, drop_ref, shifted, corners, corner, sent_mate, sent_cross, mate, cross,
-    correction, fresh, partial, whole, before, after,
+    correction, fresh, whole, before, after,
 ):
     h, p = f.h, f.p
     from_below, from_above = sides(f, drop_ref, indexed(f, mate), indexed(f, cross))
@@ -279,23 +279,16 @@
         total = masked(f, right_tile(f, shifted, corners, whole, row, col), row, col, drop_ref)
         correction[at(f, row, row + 1, col - p, col - p + 1)] = total.astype(correction.dtype)
     for row, col in f.tiles(f.own_pairs):
-        c = col - p
-        own_row = row in f.own_pairs
+        if row not in f.own_pairs:
+            continue
+        c, local = col - p, row - p
         total = 2.0 * whole[at(f, row, row + 1, c, c + 1)].astype(jnp.float32)
         for g, a, z in f.split(row, col):
-            if g == 1:
-                left = whole[at(f, row, row + 1, a, z)]
-            elif own_row:
-                left = (before, None, after)[g][at(f, row - p, row - p + 1, a, z)]
-            else:
-                continue
+            source, first = (before, local) if g == 0 else (whole, row) if g == 1 else (after, local)
+            left = source[at(f, first, first + 1, a, z)]
             total = total - dot(left, correction[at(f, g * p + a, g * p + z, c, c + 1)])
-        if own_row:
-            total = masked(f, total, row, col, drop_ref)
-            fresh[at(f, row - p, row - p + 1, c, c + 1)] = total.astype(fresh.dtype)
-        else:
-            place = row if row < p else row - p
-            partial[at(f, place, place + 1, c, c + 1)] = total
+        total = masked(f, total, row, col, drop_ref)
+        fresh[at(f, local, local + 1, c, c + 1)] = total.astype(fresh.dtype)
 
 
 def edges(f, drop_ref, corner_below, corner_above, correction, start, low, high):
@@ -318,7 +311,7 @@
 
 
 def first_edges_kernel(
-    f, drop_ref, mate, cross, correction, partial, low, high, to_cross, to_mate, before, after
+    f, drop_ref, mate, cross, correction, whole, low, high, to_cross, to_mate, before, after
 ):
     p = f.p
     below, above = sides(f, drop_ref, indexed(f, mate, len(under(f.h))), indexed(f, cross))
@@ -326,8 +319,14 @@
     spread(f, after, 0, 0, above, full(f.h))
 
     def start(row, col):
-        place = row if row < p else row - p
-        return partial[at(f, place, place + 1, col - p, col - p + 1)]
+        c = col - p
+        total = 2.0 * whole[at(f, row, row + 1, c, c + 1)].astype(jnp.float32)
+        for g, a, z in f.split(row, col):
+            if g == 1:
+                total = total - dot(
+                    whole[at(f, row, row + 1, a, z)], correction[at(f, p + a, p + z, c, c + 1)]
+                )
+        return total
 
     edges(f, drop_ref, plain(before), plain(after), correction, start, low, high)
     pack_edges(f, drop_ref, low, high, to_cross, to_mate)
@@ -579,18 +578,18 @@
         [group_scratch] * 2,
         10, 16, drop, far_far, far_mate, far_mate_too, reach, here, partial, light=True,
     )
-    correction, own, partial = run(
+    correction, own, columns_start = run(
         first_sweep_kernel,
-        [columns, square_group, partial_sums],
-        [whole_scratch, group_scratch, group_scratch],
-        66, 24, drop, shifted, shifted_corners, corner, slab_mate, triangle_cross, from_mate, cross_triangle, light=True,
+        [columns, square_group, columns],
+        [group_scratch, group_scratch],
+        56, 24, drop, shifted, shifted_corners, corner, slab_mate, triangle_cross, from_mate, cross_triangle, light=True,
     )
     corner_cross, corner_mate = to_cross(own), to_mate(own)
     low, high, edge_cross, edge_mate = run(
         first_edges_kernel,
         [square_group, square_group, triangle, triangle],
         [group_scratch] * 2,
-        10, 16, drop, from_mate, cross_corner, correction, partial,
+        20, 16, drop, from_mate, cross_corner, correction, columns_start,
     )
     edge_cross, edge_mate = to_cross(edge_cross), to_mate(edge_mate)
     (correction,) = run(

time: 85 us -> 85 us (level)
  starting transfers between devices: 26.5 us -> 33.6 us
  waiting for transfers between devices: 27.6 us -> 20.5 us
    ppermute x19, waiting for transfers between devices: 27.6 us -> 20.5 us  [routed(): lax.ppermute(x, RING, [(i, (i + step(i)) % size) for i in range(size) if...]
    ppermute x19, starting transfers between devices: 26.5 us -> 33.6 us  [routed(): lax.ppermute(x, RING, [(i, (i + step(i)) % size) for i in range(size) if...]
  transfers between devices with their start and end apart: 19 -> 19, of which waited for: 5 -> 6; matrix products, arithmetic and copies ran while one was open for 1% -> 1% of each run, Pallas kernels for 29% -> 29%
where the time goes in v21:
time: 85 us; the launch traced here: 84.8 us
  starting transfers between devices  33.6 us (40%)
  Pallas kernels  26.8 us (32%)
  waiting for transfers between devices  20.5 us (24%)
  local copies, waits for them, and re-layouts  2.05 us (2%)
  other arithmetic  1.04 us (1%)
    ppermute x19, starting transfers between devices, routed(): lax.ppermute(x, RING, [(i, (i + step(i)) % size) for i in range(size) if...  33.6 us
    pallas_call x14, Pallas kernels, call(): pl.pallas_call(kernel, out_shape=[*outs, *[jax.ShapeDtypeStruct(a.shape,...  26.8 us
    ppermute x19, waiting for transfers between devices, routed(): lax.ppermute(x, RING, [(i, (i + step(i)) % size) for i in range(size) if...  20.5 us
    unnamed x8, local copies, waits for them, and re-layouts  2.05 us
  transfers between devices with their start and end apart: 19, of which 6 were waited for; matrix products, arithmetic and copies ran while one was open for 1% of the time, Pallas kernels for 29%

profile of v21, /device:TPU:1, one launch (start us, length us, event | category | flops | bytes accessed | tf_op | source)
XLA Modules:
  0.0 84.8 jit_solution(447937505963176291)
XLA Ops:
  0.6 2.7 %collective-permute-start.2 = (bf16[4,8,128,128]{3,2,1,0:T(8,128)(2,1)}, bf16[4,8,128,128]{3,2,1,0:T(8,128)(2,1)S(1)}, u32[]{:S(2)}, u32[]{:S(2)}) collective-permute-start(bf16[4,8,128,128]{3,2,1,0:T(8,128)(2,1)} %own.2), channel_id=1, source_target_pairs={{0,15},{1,2},{2,1},{3,4},{4,3},{5,6},{6,5},{7,8},{8,7},{9,10},{10,... | collective-permute-start | bytes 3145736 | tf_op jit(solution)/shard_map/ppermute | solution.py:501
  3.3 2.9 %collective-permute-start.3 = (bf16[4,8,128,128]{3,2,1,0:T(8,128)(2,1)}, bf16[4,8,128,128]{3,2,1,0:T(8,128)(2,1)S(1)}, u32[]{:S(2)}, u32[]{:S(2)}) collective-permute-start(bf16[4,8,128,128]{3,2,1,0:T(8,128)(2,1)} %own.2), channel_id=1, source_target_pairs={{0,1},{1,0},{2,3},{3,2},{4,5},{5,4},{6,7},{7,6},{8,9},{9,8},{10,11... | collective-permute-start | bytes 3145736 | tf_op jit(solution)/shard_map/ppermute | solution.py:501
  8.4 2.1 %shard_map.51 = (bf16[2048,128]{1,0:T(8,128)(2,1)S(1)}, bf16[2048,128]{1,0:T(8,128)(2,1)}, bf16[3328,128]{1,0:T(8,128)(2,1)}, bf16[1280,128]{1,0:T(8,128)(2,1)S(1)}) custom-call(s32[5]{0:T(128)S(1)} %pad_add_fusion.1.drop_ref, bf16[4,8,128,128]{3,2,1,0:T(8,128)(2,1)S(1)} %copy-done), custom_call_target="tpu_custom_call" | custom-call | bytes 3276800 | tf_op jit(solution)/shard_map/pallas_call | solution.py:487
  12.0 15.3 %collective-permute-done = s32[4]{0:T(128)S(1)} collective-permute-done((s32[4]{0:T(128)S(1)}, s32[4]{0:T(128)S(1)}, u32[]{:S(2)}, u32[]{:S(2)}) %collective-permute-start) | collective-permute-done | bytes 48 | tf_op jit(solution)/shard_map/ppermute | solution.py:501
  28.2 1.8 %collective-permute-start.8 = (bf16[1280,128]{1,0:T(8,128)(2,1)S(1)}, bf16[1280,128]{1,0:T(8,128)(2,1)S(1)}, u32[]{:S(2)}, u32[]{:S(2)}) collective-permute-start(bf16[1280,128]{1,0:T(8,128)(2,1)S(1)} %get-tuple-element.50.sent_cross), channel_id=1, source_target_pairs={{0,15},{1,2},{2,1},{3,4},{4,3},{5,6},{6,5},{7,8},{8,7},{9,10},{10,... | collective-permute-start | bytes 983048 | tf_op jit(solution)/shard_map/ppermute | solution.py:501
  30.1 6.3 %collective-permute-start.6 = (bf16[640,128]{1,0:T(8,128)(2,1)S(1)}, bf16[640,128]{1,0:T(8,128)(2,1)S(1)}, u32[]{:S(2)}, u32[]{:S(2)}) collective-permute-start(bf16[640,128]{1,0:T(8,128)(2,1)S(1)} %get-tuple-element.43), channel_id=1, source_target_pairs={{0,1},{1,0},{2,3},{3,2},{4,5},{5,4},{6,7},{7,6},{8,9},{9,8},{10,11... | collective-permute-start | bytes 491528 | tf_op jit(solution)/shard_map/ppermute | solution.py:501
  36.4 4.3 %shard_map.50 = (bf16[1536,1280]{1,0:T(8,128)(2,1)S(1)}, bf16[1536,1280]{1,0:T(8,128)(2,1)S(1)}, bf16[1024,512]{1,0:T(8,128)(2,1)S(1)}, bf16[1024,512]{1,0:T(8,128)(2,1)S(1)}, f32[1024,512]{1,0:T(8,128)S(1)}) custom-call(s32[13]{0:T(128)S(1)} %pad_add_fusion.drop_ref, bf16[4,8,128,128]{3,2,1,0:T(8,128)(2,1)S(1)} %copy-done.3, ...), custom_call_target="tpu_custom_call" | custom-call | flops 2818572288 | bytes 15204352 | tf_op jit(solution)/shard_map/pallas_call | solution.py:487
  40.7 1.4 %shard_map.53 = (bf16[1024,512]{1,0:T(8,128)(2,1)S(1)}, bf16[1024,512]{1,0:T(8,128)(2,1)S(1)}) custom-call(s32[13]{0:T(128)S(1)} %pad_add_fusion.drop_ref, bf16[1280,128]{1,0:T(8,128)(2,1)S(1)} %collective-permute-done.5.far_far, bf16[640,128]{1,0:T(8,128)(2,1)S(1)} %collective-permute-done.6.far_mate, ...), custom_call_target="tpu_custom_call" | custom-call | tf_op jit(solution)/shard_map/pallas_call | solution.py:487
  42.2 3.5 %shard_map.54 = (bf16[1536,512]{1,0:T(8,128)(2,1)S(1)}, bf16[512,512]{1,0:T(8,128)(2,1)S(1)}, bf16[1536,512]{1,0:T(8,128)(2,1)S(1)}) custom-call(s32[13]{0:T(128)S(1)} %pad_add_fusion.drop_ref, bf16[1536,1280]{1,0:T(8,128)(2,1)S(1)} %get-tuple-element.38.shifted, bf16[1024,512]{1,0:T(8,128)(2,1)S(1)} %get-tuple-element.48.corners, ...), custom_call_target="tpu_custom_call" | custom-call | tf_op jit(solution)/shard_map/pallas_call | solution.py:487
  46.5 2.2 %collective-permute-start.13 = (bf16[512,512]{1,0:T(8,128)(2,1)S(1)}, bf16[512,512]{1,0:T(8,128)(2,1)S(1)}, u32[]{:S(2)}, u32[]{:S(2)}) collective-permute-start(bf16[512,512]{1,0:T(8,128)(2,1)S(1)} %get-tuple-element.51.own), channel_id=1, source_target_pairs={{0,1},{1,0},{2,3},{3,2},{4,5},{5,4},{6,7},{7,6},{8,9},{9,8},{10,11... | collective-permute-start | bytes 1572872 | tf_op jit(solution)/shard_map/ppermute | solution.py:501
  48.9 1.6 %shard_map.55 = (bf16[512,512]{1,0:T(8,128)(2,1)S(1)}, bf16[512,512]{1,0:T(8,128)(2,1)S(1)}, bf16[1280,128]{1,0:T(8,128)(2,1)S(1)}, bf16[1280,128]{1,0:T(8,128)(2,1)S(1)}) custom-call(s32[13]{0:T(128)S(1)} %pad_add_fusion.drop_ref, bf16[3328,128]{1,0:T(8,128)(2,1)S(1)} %collective-permute-done.4.refs_1_.mate, ...), custom_call_target="tpu_custom_call" | custom-call | flops 671088640 | bytes 6225920 | tf_op jit(solution)/shard_map/pallas_call | solution.py:487
  50.6 11.5 %collective-permute-start.10 = (bf16[1280,128]{1,0:T(8,128)(2,1)S(1)}, bf16[1280,128]{1,0:T(8,128)(2,1)S(1)}, u32[]{:S(2)}, u32[]{:S(2)}) collective-permute-start(bf16[1280,128]{1,0:T(8,128)(2,1)S(1)} %get-tuple-element.55), channel_id=1, source_target_pairs={{0,15},{1,2},{2,1},{3,4},{4,3},{5,6},{6,5},{7,8},{8,7},{9,10},{10,... | collective-permute-start | bytes 983048 | tf_op jit(solution)/shard_map/ppermute | solution.py:501
  62.1 2.0 %shard_map.56.correction = bf16[1536,512]{1,0:T(8,128)(2,1)S(1)} custom-call(s32[13]{0:T(128)S(1)} %pad_add_fusion.drop_ref, bf16[1536,1280]{1,0:T(8,128)(2,1)S(1)} %get-tuple-element.38.shifted, bf16[1024,512]{1,0:T(8,128)(2,1)S(1)} %get-tuple-element.48.corners, bf16[512,512]{1,0:T(8,128)(2,1)S(1)} %get-tuple-element.57.low, ...), custom_call_target="tpu_custom_call" | custom-call | flops 1275068416 | bytes 8126464 | tf_op jit(solution)/shard_map/pallas_call | solution.py:487
  64.8 1.5 %shard_map.57 = (bf16[512,512]{1,0:T(8,128)(2,1)S(1)}, bf16[512,512]{1,0:T(8,128)(2,1)S(1)}, bf16[1280,128]{1,0:T(8,128)(2,1)S(1)}, bf16[1280,128]{1,0:T(8,128)(2,1)S(1)}) custom-call(s32[13]{0:T(128)S(1)} %pad_add_fusion.drop_ref, bf16[512,512]{1,0:T(8,128)(2,1)S(1)} %collective-permute-done.12.cross, bf16[512,512]{1,0:T(8,128)(2,1)S(1)} %collective-permute-done.13.mate, ...), custom_call_target="tpu_custom_call" | custom-call | flops 671088640 | bytes 5373952 | tf_op jit(solution)/shard_map/pallas_call | solution.py:487
  66.3 1.3 %collective-permute-start.18 = (bf16[1280,128]{1,0:T(8,128)(2,1)S(1)}, bf16[1280,128]{1,0:T(8,128)(2,1)S(1)}, u32[]{:S(2)}, u32[]{:S(2)}) collective-permute-start(bf16[1280,128]{1,0:T(8,128)(2,1)S(1)} %get-tuple-element.70), channel_id=1, source_target_pairs={{0,15},{1,2},{2,1},{3,4},{4,3},{5,6},{6,5},{7,8},{8,7},{9,10},{10,... | collective-permute-start | bytes 983048 | tf_op jit(solution)/shard_map/ppermute | solution.py:501
  68.3 2.3 %shard_map.58 = (bf16[1536,512]{1,0:T(8,128)(2,1)S(1)}, bf16[1280,128]{1,0:T(8,128)(2,1)S(1)}, bf16[640,128]{1,0:T(8,128)(2,1)S(1)}, bf16[640,128]{1,0:T(8,128)(2,1)S(1)}) custom-call(s32[13]{0:T(128)S(1)} %pad_add_fusion.drop_ref, bf16[512,512]{1,0:T(8,128)(2,1)S(1)} %get-tuple-element.51.own, bf16[1280,128]{1,0:T(8,128)(2,1)S(1)} %collective-permute-done.10.cross, ...), custom_call_target="tpu_custom_call" | custom-call | flops 1275068416 | bytes 11010048 | tf_op jit(solution)/shard_map/pallas_call | solution.py:487
  70.5 1.3 %collective-permute-start.16 = (bf16[1280,128]{1,0:T(8,128)(2,1)S(1)}, bf16[1280,128]{1,0:T(8,128)(2,1)S(1)}, u32[]{:S(2)}, u32[]{:S(2)}) collective-permute-start(bf16[1280,128]{1,0:T(8,128)(2,1)S(1)} %get-tuple-element.66), channel_id=1, source_target_pairs={{0,15},{1,2},{2,1},{3,4},{4,3},{5,6},{6,5},{7,8},{8,7},{9,10},{10,... | collective-permute-start | bytes 983048 | tf_op jit(solution)/shard_map/ppermute | solution.py:501
  71.9 1.8 %collective-permute-start.14 = (bf16[640,128]{1,0:T(8,128)(2,1)S(1)}, bf16[640,128]{1,0:T(8,128)(2,1)S(1)}, u32[]{:S(2)}, u32[]{:S(2)}) collective-permute-start(bf16[640,128]{1,0:T(8,128)(2,1)S(1)} %get-tuple-element.63), channel_id=1, source_target_pairs={{0,1},{1,0},{2,3},{3,2},{4,5},{5,4},{6,7},{7,6},{8,9},{9,8},{10,11... | collective-permute-start | bytes 491528 | tf_op jit(solution)/shard_map/ppermute | solution.py:501
  73.6 1.3 %shard_map.59.own = bf16[512,512]{1,0:T(8,128)(2,1)S(1)} custom-call(s32[13]{0:T(128)S(1)} %pad_add_fusion.drop_ref, bf16[1536,1280]{1,0:T(8,128)(2,1)S(1)} %get-tuple-element.37.square, bf16[1536,512]{1,0:T(8,128)(2,1)S(1)} %get-tuple-element.62.whole.own), custom_call_target="tpu_custom_call" | custom-call | flops 603979776 | bytes 6029312 | tf_op jit(solution)/shard_map/pallas_call | solution.py:487
  75.0 1.7 %shard_map.60 = (bf16[4,8,128,128]{3,2,1,0:T(8,128)(2,1)S(1)}, bf16[4,8,128,128]{3,2,1,0:T(8,128)(2,1)}) custom-call(s32[13]{0:T(128)S(1)} %pad_add_fusion.drop_ref, bf16[512,512]{1,0:T(8,128)(2,1)S(1)} %shard_map.59.own, bf16[640,128]{1,0:T(8,128)(2,1)S(1)} %collective-permute-done.14.refs_0_, bf16[640,128]{1,0:T(8,128)(2,1)S(1)} %collective-permute-done.15.refs_1_), custom_call_target="tpu_custom_call" | custom-call | tf_op jit(solution)/shard_map/pallas_call | solution.py:487
  76.8 1.7 %shard_map.62 = (bf16[4,8,128,128]{3,2,1,0:T(8,128)(2,1)S(1)}, bf16[4,8,128,128]{3,2,1,0:T(8,128)(2,1)}) custom-call(s32[13]{0:T(128)S(1)} %pad_add_fusion.drop_ref, bf16[1536,512]{1,0:T(8,128)(2,1)S(1)} %get-tuple-element.62.whole.own, bf16[1280,128]{1,0:T(8,128)(2,1)S(1)} %collective-permute-done.17.refs_0_), custom_call_target="tpu_custom_call" | custom-call | tf_op jit(solution)/shard_map/pallas_call | solution.py:487
  78.7 1.3 %shard_map.63 = bf16[4,8,128,128]{3,2,1,0:T(8,128)(2,1)} custom-call(s32[13]{0:T(128)S(1)} %pad_add_fusion.drop_ref, bf16[4,8,128,128]{3,2,1,0:T(8,128)(2,1)S(1)} %get-tuple-element.69.slots, bf16[1280,128]{1,0:T(8,128)(2,1)S(1)} %collective-permute-done.18.cross, bf16[4,8,128,128]{3,2,1,0:T(8,128)(2,1)} %get-tuple-element.71.unused), custom_call_target="tpu_custom_call", output_to_operand_aliasing={{}: (3, {})} | custom-call | tf_op jit(solution)/shard_map/pallas_call | solution.py:487
  80.0 3.4 %collective-permute-done.16.cross = bf16[1280,128]{1,0:T(8,128)(2,1)S(1)} collective-permute-done((bf16[1280,128]{1,0:T(8,128)(2,1)S(1)}, bf16[1280,128]{1,0:T(8,128)(2,1)S(1)}, u32[]{:S(2)}, u32[]{:S(2)}) %collective-permute-start.16) | collective-permute-done | bytes 327712 | tf_op jit(solution)/shard_map/ppermute | solution.py:501
  83.4 1.3 %shard_map.61 = bf16[4,8,128,128]{3,2,1,0:T(8,128)(2,1)} custom-call(s32[13]{0:T(128)S(1)} %pad_add_fusion.drop_ref, bf16[4,8,128,128]{3,2,1,0:T(8,128)(2,1)S(1)} %get-tuple-element.65.slots, bf16[1280,128]{1,0:T(8,128)(2,1)S(1)} %collective-permute-done.16.cross, bf16[4,8,128,128]{3,2,1,0:T(8,128)(2,1)} %get-tuple-element.67.unused), custom_call_target="tpu_custom_call", output_to_operand_aliasing={{}: (3, {})} | custom-call | tf_op jit(solution)/shard_map/pallas_call | solution.py:487
  (42 shorter events, 7.4 us)
Async XLA Ops:
  0.6 26.8 %collective-permute-start.2 = (bf16[4,8,128,128]{3,2,1,0:T(8,128)(2,1)}, bf16[4,8,128,128]{3,2,1,0:T(8,128)(2,1)S(1)}, u32[]{:S(2)}, u32[]{:S(2)}) collective-permute-start(bf16[4,8,128,128]{3,2,1,0:T(8,128)(2,1)} %own.2), channel_id=1, source_target_pairs={{0,15},{1,2},{2,1},{3,4},{4,3},{5,6},{6,5},{7,8},{8,7},{9,10},{10,... | collective-permute-start | bytes 3145736 | tf_op jit(solution)/shard_map/ppermute | solution.py:501
  3.3 24.1 %collective-permute-start.3 = (bf16[4,8,128,128]{3,2,1,0:T(8,128)(2,1)}, bf16[4,8,128,128]{3,2,1,0:T(8,128)(2,1)S(1)}, u32[]{:S(2)}, u32[]{:S(2)}) collective-permute-start(bf16[4,8,128,128]{3,2,1,0:T(8,128)(2,1)} %own.2), channel_id=1, source_target_pairs={{0,1},{1,0},{2,3},{3,2},{4,5},{5,4},{6,7},{7,6},{8,9},{9,8},{10,11... | collective-permute-start | bytes 3145736 | tf_op jit(solution)/shard_map/ppermute | solution.py:501
  7.1 1.2 %copy-start = (bf16[4,8,128,128]{3,2,1,0:T(8,128)(2,1)S(1)}, bf16[4,8,128,128]{3,2,1,0:T(8,128)(2,1)}, u32[]{:S(2)}) copy-start(bf16[4,8,128,128]{3,2,1,0:T(8,128)(2,1)} %own.3) | copy-start | bytes 3145732
  10.4 0.8 copy-start.1
  11.2 16.2 %collective-permute-start.4 = (bf16[3328,128]{1,0:T(8,128)(2,1)}, bf16[3328,128]{1,0:T(8,128)(2,1)S(1)}, u32[]{:S(2)}, u32[]{:S(2)}) collective-permute-start(bf16[3328,128]{1,0:T(8,128)(2,1)} %get-tuple-element.39.sent_mate), channel_id=1, source_target_pairs={{0,1},{1,0},{2,3},{3,2},{4,5},{5,4},{6,7},{7,6},{8,9},{9,8},{10,11... | collective-permute-start | bytes 2555912 | tf_op jit(solution)/shard_map/ppermute | solution.py:501
  11.2 16.1 %collective-permute-start = (s32[4]{0:T(128)S(1)}, s32[4]{0:T(128)S(1)}, u32[]{:S(2)}, u32[]{:S(2)}) collective-permute-start(s32[4]{0:T(128)S(1)} %broadcast_subtract_fusion), channel_id=1, source_target_pairs={{0,15},{1,2},{2,1},{3,4},{4,3},{5,6},{6,5},{7,8},{8,7},{9,10},{10,... | collective-permute-start | bytes 56 | tf_op jit(solution)/shard_map/ppermute | solution.py:501
  11.2 16.1 %collective-permute-start.1 = (s32[4]{0:T(128)S(1)}, s32[4]{0:T(128)S(1)}, u32[]{:S(2)}, u32[]{:S(2)}) collective-permute-start(s32[4]{0:T(128)S(1)} %broadcast_subtract_fusion), channel_id=1, source_target_pairs={{0,1},{1,0},{2,3},{3,2},{4,5},{5,4},{6,7},{7,6},{8,9},{9,8},{10,11... | collective-permute-start | bytes 56 | tf_op jit(solution)/shard_map/ppermute | solution.py:501
  27.4 9.0 %copy-start.3 = (bf16[4,8,128,128]{3,2,1,0:T(8,128)(2,1)S(1)}, bf16[4,8,128,128]{3,2,1,0:T(8,128)(2,1)}, u32[]{:S(2)}) copy-start(bf16[4,8,128,128]{3,2,1,0:T(8,128)(2,1)} %own.2) | copy-start | bytes 3145732
  28.1 12.5 %collective-permute-start.5 = (bf16[1280,128]{1,0:T(8,128)(2,1)S(1)}, bf16[1280,128]{1,0:T(8,128)(2,1)S(1)}, u32[]{:S(2)}, u32[]{:S(2)}) collective-permute-start(bf16[1280,128]{1,0:T(8,128)(2,1)S(1)} %get-tuple-element.42), channel_id=1, source_target_pairs={{0,13},{1,4},{2,15},{3,6},{4,1},{5,8},{6,3},{7,10},{8,5},{9,12},{1... | collective-permute-start | bytes 983048 | tf_op jit(solution)/shard_map/ppermute | solution.py:501
  28.2 13.9 %collective-permute-start.8 = (bf16[1280,128]{1,0:T(8,128)(2,1)S(1)}, bf16[1280,128]{1,0:T(8,128)(2,1)S(1)}, u32[]{:S(2)}, u32[]{:S(2)}) collective-permute-start(bf16[1280,128]{1,0:T(8,128)(2,1)S(1)} %get-tuple-element.50.sent_cross), channel_id=1, source_target_pairs={{0,15},{1,2},{2,1},{3,4},{4,3},{5,6},{6,5},{7,8},{8,7},{9,10},{10,... | collective-permute-start | bytes 983048 | tf_op jit(solution)/shard_map/ppermute | solution.py:501
  30.0 18.9 %collective-permute-start.9 = (bf16[2048,128]{1,0:T(8,128)(2,1)}, bf16[2048,128]{1,0:T(8,128)(2,1)S(1)}, u32[]{:S(2)}, u32[]{:S(2)}) collective-permute-start(bf16[2048,128]{1,0:T(8,128)(2,1)} %get-tuple-element.52), channel_id=1, source_target_pairs={{0,15},{1,2},{2,1},{3,4},{4,3},{5,6},{6,5},{7,8},{8,7},{9,10},{10,... | collective-permute-start | bytes 1572872 | tf_op jit(solution)/shard_map/ppermute | solution.py:501
  30.1 10.5 %collective-permute-start.6 = (bf16[640,128]{1,0:T(8,128)(2,1)S(1)}, bf16[640,128]{1,0:T(8,128)(2,1)S(1)}, u32[]{:S(2)}, u32[]{:S(2)}) collective-permute-start(bf16[640,128]{1,0:T(8,128)(2,1)S(1)} %get-tuple-element.43), channel_id=1, source_target_pairs={{0,1},{1,0},{2,3},{3,2},{4,5},{5,4},{6,7},{7,6},{8,9},{9,8},{10,11... | collective-permute-start | bytes 491528 | tf_op jit(solution)/shard_map/ppermute | solution.py:501
  36.4 4.3 %collective-permute-start.7 = (bf16[640,128]{1,0:T(8,128)(2,1)S(1)}, bf16[640,128]{1,0:T(8,128)(2,1)S(1)}, u32[]{:S(2)}, u32[]{:S(2)}) collective-permute-start(bf16[640,128]{1,0:T(8,128)(2,1)S(1)} %get-tuple-element.44), channel_id=1, source_target_pairs={{0,1},{1,0},{2,3},{3,2},{4,5},{5,4},{6,7},{7,6},{8,9},{9,8},{10,11... | collective-permute-start | bytes 491528 | tf_op jit(solution)/shard_map/ppermute | solution.py:501
  40.7 1.5 %copy-start.2 = (bf16[2048,128]{1,0:T(8,128)(2,1)S(1)}, bf16[2048,128]{1,0:T(8,128)(2,1)}, u32[]{:S(2)}) copy-start(bf16[2048,128]{1,0:T(8,128)(2,1)} %copy-done.1) | copy-start | bytes 1572868
  45.7 19.1 %collective-permute-start.12 = (bf16[512,512]{1,0:T(8,128)(2,1)S(1)}, bf16[512,512]{1,0:T(8,128)(2,1)S(1)}, u32[]{:S(2)}, u32[]{:S(2)}) collective-permute-start(bf16[512,512]{1,0:T(8,128)(2,1)S(1)} %get-tuple-element.51.own), channel_id=1, source_target_pairs={{0,15},{1,2},{2,1},{3,4},{4,3},{5,6},{6,5},{7,8},{8,7},{9,10},{10,... | collective-permute-start | bytes 1572872 | tf_op jit(solution)/shard_map/ppermute | solution.py:501
  46.5 18.2 %collective-permute-start.13 = (bf16[512,512]{1,0:T(8,128)(2,1)S(1)}, bf16[512,512]{1,0:T(8,128)(2,1)S(1)}, u32[]{:S(2)}, u32[]{:S(2)}) collective-permute-start(bf16[512,512]{1,0:T(8,128)(2,1)S(1)} %get-tuple-element.51.own), channel_id=1, source_target_pairs={{0,1},{1,0},{2,3},{3,2},{4,5},{5,4},{6,7},{7,6},{8,9},{9,8},{10,11... | collective-permute-start | bytes 1572872 | tf_op jit(solution)/shard_map/ppermute | solution.py:501
  50.6 17.7 %collective-permute-start.10 = (bf16[1280,128]{1,0:T(8,128)(2,1)S(1)}, bf16[1280,128]{1,0:T(8,128)(2,1)S(1)}, u32[]{:S(2)}, u32[]{:S(2)}) collective-permute-start(bf16[1280,128]{1,0:T(8,128)(2,1)S(1)} %get-tuple-element.55), channel_id=1, source_target_pairs={{0,15},{1,2},{2,1},{3,4},{4,3},{5,6},{6,5},{7,8},{8,7},{9,10},{10,... | collective-permute-start | bytes 983048 | tf_op jit(solution)/shard_map/ppermute | solution.py:501
  62.1 6.2 %collective-permute-start.11 = (bf16[1280,128]{1,0:T(8,128)(2,1)S(1)}, bf16[1280,128]{1,0:T(8,128)(2,1)S(1)}, u32[]{:S(2)}, u32[]{:S(2)}) collective-permute-start(bf16[1280,128]{1,0:T(8,128)(2,1)S(1)} %get-tuple-element.56), channel_id=1, source_target_pairs={{0,1},{1,0},{2,3},{3,2},{4,5},{5,4},{6,7},{7,6},{8,9},{9,8},{10,11... | collective-permute-start | bytes 983048 | tf_op jit(solution)/shard_map/ppermute | solution.py:501
  66.3 10.5 %collective-permute-start.17 = (bf16[1280,128]{1,0:T(8,128)(2,1)S(1)}, bf16[1280,128]{1,0:T(8,128)(2,1)S(1)}, u32[]{:S(2)}, u32[]{:S(2)}) collective-permute-start(bf16[1280,128]{1,0:T(8,128)(2,1)S(1)} %get-tuple-element.68), channel_id=1, source_target_pairs={{0,1},{1,0},{2,3},{3,2},{4,5},{5,4},{6,7},{7,6},{8,9},{9,8},{10,11... | collective-permute-start | bytes 983048 | tf_op jit(solution)/shard_map/ppermute | solution.py:501
  66.3 12.4 %collective-permute-start.18 = (bf16[1280,128]{1,0:T(8,128)(2,1)S(1)}, bf16[1280,128]{1,0:T(8,128)(2,1)S(1)}, u32[]{:S(2)}, u32[]{:S(2)}) collective-permute-start(bf16[1280,128]{1,0:T(8,128)(2,1)S(1)} %get-tuple-element.70), channel_id=1, source_target_pairs={{0,15},{1,2},{2,1},{3,4},{4,3},{5,6},{6,5},{7,8},{8,7},{9,10},{10,... | collective-permute-start | bytes 983048 | tf_op jit(solution)/shard_map/ppermute | solution.py:501
  70.5 12.9 %collective-permute-start.16 = (bf16[1280,128]{1,0:T(8,128)(2,1)S(1)}, bf16[1280,128]{1,0:T(8,128)(2,1)S(1)}, u32[]{:S(2)}, u32[]{:S(2)}) collective-permute-start(bf16[1280,128]{1,0:T(8,128)(2,1)S(1)} %get-tuple-element.66), channel_id=1, source_target_pairs={{0,15},{1,2},{2,1},{3,4},{4,3},{5,6},{6,5},{7,8},{8,7},{9,10},{10,... | collective-permute-start | bytes 983048 | tf_op jit(solution)/shard_map/ppermute | solution.py:501
  71.9 3.1 %collective-permute-start.14 = (bf16[640,128]{1,0:T(8,128)(2,1)S(1)}, bf16[640,128]{1,0:T(8,128)(2,1)S(1)}, u32[]{:S(2)}, u32[]{:S(2)}) collective-permute-start(bf16[640,128]{1,0:T(8,128)(2,1)S(1)} %get-tuple-element.63), channel_id=1, source_target_pairs={{0,1},{1,0},{2,3},{3,2},{4,5},{5,4},{6,7},{7,6},{8,9},{9,8},{10,11... | collective-permute-start | bytes 491528 | tf_op jit(solution)/shard_map/ppermute | solution.py:501
  73.6 1.4 %collective-permute-start.15 = (bf16[640,128]{1,0:T(8,128)(2,1)S(1)}, bf16[640,128]{1,0:T(8,128)(2,1)S(1)}, u32[]{:S(2)}, u32[]{:S(2)}) collective-permute-start(bf16[640,128]{1,0:T(8,128)(2,1)S(1)} %get-tuple-element.64), channel_id=1, source_target_pairs={{0,1},{1,0},{2,3},{3,2},{4,5},{5,4},{6,7},{7,6},{8,9},{9,8},{10,11... | collective-permute-start | bytes 491528 | tf_op jit(solution)/shard_map/ppermute | solution.py:501

commit v22 on v15

--- a/solution.py
+++ b/solution.py
@@ -444,7 +444,7 @@
 
     def fill(low):
         copies = []
-        for r in range(h):
+        for r in range(h) if low else reversed(range(h)):
             dropped = drop_ref[h + r]
             lo, hi = (0, h - r) if low else (k - 1 - r, k)
             for s in range(lo, hi):

time: 85 us -> 85 us (level)
  no operation moved by 1% of the time
where the time goes in v22:
time: 85 us; the launch traced here: 84.8 us
  waiting for transfers between devices  27.6 us (32%)
  Pallas kernels  26.7 us (31%)
  starting transfers between devices  26.5 us (31%)
  local copies, waits for them, and re-layouts  2.04 us (2%)
  other arithmetic  1.04 us (1%)
    ppermute x19, waiting for transfers between devices, routed(): lax.ppermute(x, RING, [(i, (i + step(i)) % size) for i in range(size) if...  27.6 us
    pallas_call x14, Pallas kernels, call(): pl.pallas_call(kernel, out_shape=[*outs, *[jax.ShapeDtypeStruct(a.shape,...  26.7 us
    ppermute x19, starting transfers between devices, routed(): lax.ppermute(x, RING, [(i, (i + step(i)) % size) for i in range(size) if...  26.5 us
    unnamed x8, local copies, waits for them, and re-layouts  2.04 us
  transfers between devices with their start and end apart: 19, of which 5 were waited for; matrix products, arithmetic and copies ran while one was open for 1% of the time, Pallas kernels for 29%

profile of v22, /device:TPU:1, one launch (start us, length us, event | category | flops | bytes accessed | tf_op | source)
XLA Modules:
  0.0 84.8 jit_solution(638706569985995708)
XLA Ops:
  0.6 2.7 %collective-permute-start.2 = (bf16[4,8,128,128]{3,2,1,0:T(8,128)(2,1)}, bf16[4,8,128,128]{3,2,1,0:T(8,128)(2,1)S(1)}, u32[]{:S(2)}, u32[]{:S(2)}) collective-permute-start(bf16[4,8,128,128]{3,2,1,0:T(8,128)(2,1)} %own.2), channel_id=1, source_target_pairs={{0,15},{1,2},{2,1},{3,4},{4,3},{5,6},{6,5},{7,8},{8,7},{9,10},{10,... | collective-permute-start | bytes 3145736 | tf_op jit(solution)/shard_map/ppermute | solution.py:502
  3.3 2.9 %collective-permute-start.3 = (bf16[4,8,128,128]{3,2,1,0:T(8,128)(2,1)}, bf16[4,8,128,128]{3,2,1,0:T(8,128)(2,1)S(1)}, u32[]{:S(2)}, u32[]{:S(2)}) collective-permute-start(bf16[4,8,128,128]{3,2,1,0:T(8,128)(2,1)} %own.2), channel_id=1, source_target_pairs={{0,1},{1,0},{2,3},{3,2},{4,5},{5,4},{6,7},{7,6},{8,9},{9,8},{10,11... | collective-permute-start | bytes 3145736 | tf_op jit(solution)/shard_map/ppermute | solution.py:502
  8.4 2.1 %shard_map.51 = (bf16[2048,128]{1,0:T(8,128)(2,1)S(1)}, bf16[2048,128]{1,0:T(8,128)(2,1)}, bf16[3328,128]{1,0:T(8,128)(2,1)}, bf16[1280,128]{1,0:T(8,128)(2,1)S(1)}) custom-call(s32[5]{0:T(128)S(1)} %pad_add_fusion.1.drop_ref, bf16[4,8,128,128]{3,2,1,0:T(8,128)(2,1)S(1)} %copy-done), custom_call_target="tpu_custom_call" | custom-call | bytes 3276800 | tf_op jit(solution)/shard_map/pallas_call | solution.py:488
  12.0 15.3 %collective-permute-done = s32[4]{0:T(128)S(1)} collective-permute-done((s32[4]{0:T(128)S(1)}, s32[4]{0:T(128)S(1)}, u32[]{:S(2)}, u32[]{:S(2)}) %collective-permute-start) | collective-permute-done | bytes 48 | tf_op jit(solution)/shard_map/ppermute | solution.py:502
  28.2 1.8 %collective-permute-start.8 = (bf16[1280,128]{1,0:T(8,128)(2,1)S(1)}, bf16[1280,128]{1,0:T(8,128)(2,1)S(1)}, u32[]{:S(2)}, u32[]{:S(2)}) collective-permute-start(bf16[1280,128]{1,0:T(8,128)(2,1)S(1)} %get-tuple-element.50.sent_cross), channel_id=1, source_target_pairs={{0,15},{1,2},{2,1},{3,4},{4,3},{5,6},{6,5},{7,8},{8,7},{9,10},{10,... | collective-permute-start | bytes 983048 | tf_op jit(solution)/shard_map/ppermute | solution.py:502
  30.1 6.3 %collective-permute-start.6 = (bf16[640,128]{1,0:T(8,128)(2,1)S(1)}, bf16[640,128]{1,0:T(8,128)(2,1)S(1)}, u32[]{:S(2)}, u32[]{:S(2)}) collective-permute-start(bf16[640,128]{1,0:T(8,128)(2,1)S(1)} %get-tuple-element.43), channel_id=1, source_target_pairs={{0,1},{1,0},{2,3},{3,2},{4,5},{5,4},{6,7},{7,6},{8,9},{9,8},{10,11... | collective-permute-start | bytes 491528 | tf_op jit(solution)/shard_map/ppermute | solution.py:502
  36.4 4.3 %shard_map.50 = (bf16[1536,1280]{1,0:T(8,128)(2,1)S(1)}, bf16[1536,1280]{1,0:T(8,128)(2,1)S(1)}, bf16[1024,512]{1,0:T(8,128)(2,1)S(1)}, bf16[1024,512]{1,0:T(8,128)(2,1)S(1)}, f32[1024,512]{1,0:T(8,128)S(1)}) custom-call(s32[13]{0:T(128)S(1)} %pad_add_fusion.drop_ref, bf16[4,8,128,128]{3,2,1,0:T(8,128)(2,1)S(1)} %copy-done.3, ...), custom_call_target="tpu_custom_call" | custom-call | flops 2818572288 | bytes 15204352 | tf_op jit(solution)/shard_map/pallas_call | solution.py:488
  40.7 1.4 %shard_map.53 = (bf16[1024,512]{1,0:T(8,128)(2,1)S(1)}, bf16[1024,512]{1,0:T(8,128)(2,1)S(1)}) custom-call(s32[13]{0:T(128)S(1)} %pad_add_fusion.drop_ref, bf16[1280,128]{1,0:T(8,128)(2,1)S(1)} %collective-permute-done.5.far_far, bf16[640,128]{1,0:T(8,128)(2,1)S(1)} %collective-permute-done.6.far_mate, ...), custom_call_target="tpu_custom_call" | custom-call | tf_op jit(solution)/shard_map/pallas_call | solution.py:488
  42.1 3.8 %shard_map.54 = (bf16[1536,512]{1,0:T(8,128)(2,1)S(1)}, bf16[512,512]{1,0:T(8,128)(2,1)S(1)}, f32[1024,512]{1,0:T(8,128)S(1)}) custom-call(s32[13]{0:T(128)S(1)} %pad_add_fusion.drop_ref, bf16[1536,1280]{1,0:T(8,128)(2,1)S(1)} %get-tuple-element.38.shifted, bf16[1024,512]{1,0:T(8,128)(2,1)S(1)} %get-tuple-element.48.corners, ...), custom_call_target="tpu_custom_call" | custom-call | tf_op jit(solution)/shard_map/pallas_call | solution.py:488
  46.8 2.2 %collective-permute-start.13 = (bf16[512,512]{1,0:T(8,128)(2,1)S(1)}, bf16[512,512]{1,0:T(8,128)(2,1)S(1)}, u32[]{:S(2)}, u32[]{:S(2)}) collective-permute-start(bf16[512,512]{1,0:T(8,128)(2,1)S(1)} %get-tuple-element.51.own), channel_id=1, source_target_pairs={{0,1},{1,0},{2,3},{3,2},{4,5},{5,4},{6,7},{7,6},{8,9},{9,8},{10,11... | collective-permute-start | bytes 1572872 | tf_op jit(solution)/shard_map/ppermute | solution.py:502
  49.0 1.3 %shard_map.55 = (bf16[512,512]{1,0:T(8,128)(2,1)S(1)}, bf16[512,512]{1,0:T(8,128)(2,1)S(1)}, bf16[1280,128]{1,0:T(8,128)(2,1)S(1)}, bf16[1280,128]{1,0:T(8,128)(2,1)S(1)}) custom-call(s32[13]{0:T(128)S(1)} %pad_add_fusion.drop_ref, bf16[3328,128]{1,0:T(8,128)(2,1)S(1)} %collective-permute-done.4.refs_1_.mate, ...), custom_call_target="tpu_custom_call" | custom-call | flops 335544320 | bytes 6750208 | tf_op jit(solution)/shard_map/pallas_call | solution.py:488
  50.4 2.3 %collective-permute-start.10 = (bf16[1280,128]{1,0:T(8,128)(2,1)S(1)}, bf16[1280,128]{1,0:T(8,128)(2,1)S(1)}, u32[]{:S(2)}, u32[]{:S(2)}) collective-permute-start(bf16[1280,128]{1,0:T(8,128)(2,1)S(1)} %get-tuple-element.55), channel_id=1, source_target_pairs={{0,15},{1,2},{2,1},{3,4},{4,3},{5,6},{6,5},{7,8},{8,7},{9,10},{10,... | collective-permute-start | bytes 983048 | tf_op jit(solution)/shard_map/ppermute | solution.py:502
  52.7 2.1 %collective-permute-start.11 = (bf16[1280,128]{1,0:T(8,128)(2,1)S(1)}, bf16[1280,128]{1,0:T(8,128)(2,1)S(1)}, u32[]{:S(2)}, u32[]{:S(2)}) collective-permute-start(bf16[1280,128]{1,0:T(8,128)(2,1)S(1)} %get-tuple-element.56), channel_id=1, source_target_pairs={{0,1},{1,0},{2,3},{3,2},{4,5},{5,4},{6,7},{7,6},{8,9},{9,8},{10,11... | collective-permute-start | bytes 983048 | tf_op jit(solution)/shard_map/ppermute | solution.py:502
  54.8 2.0 %shard_map.56.correction = bf16[1536,512]{1,0:T(8,128)(2,1)S(1)} custom-call(s32[13]{0:T(128)S(1)} %pad_add_fusion.drop_ref, bf16[1536,1280]{1,0:T(8,128)(2,1)S(1)} %get-tuple-element.38.shifted, bf16[1024,512]{1,0:T(8,128)(2,1)S(1)} %get-tuple-element.48.corners, bf16[512,512]{1,0:T(8,128)(2,1)S(1)} %get-tuple-element.57.low, ...), custom_call_target="tpu_custom_call" | custom-call | flops 1275068416 | bytes 8126464 | tf_op jit(solution)/shard_map/pallas_call | solution.py:488
  56.8 8.0 %collective-permute-done.12.cross = bf16[512,512]{1,0:T(8,128)(2,1)S(1)} collective-permute-done((bf16[512,512]{1,0:T(8,128)(2,1)S(1)}, bf16[512,512]{1,0:T(8,128)(2,1)S(1)}, u32[]{:S(2)}, u32[]{:S(2)}) %collective-permute-start.12) | collective-permute-done | bytes 524320 | tf_op jit(solution)/shard_map/ppermute | solution.py:502
  64.8 1.5 %shard_map.57 = (bf16[512,512]{1,0:T(8,128)(2,1)S(1)}, bf16[512,512]{1,0:T(8,128)(2,1)S(1)}, bf16[1280,128]{1,0:T(8,128)(2,1)S(1)}, bf16[1280,128]{1,0:T(8,128)(2,1)S(1)}) custom-call(s32[13]{0:T(128)S(1)} %pad_add_fusion.drop_ref, bf16[512,512]{1,0:T(8,128)(2,1)S(1)} %collective-permute-done.12.cross, bf16[512,512]{1,0:T(8,128)(2,1)S(1)} %collective-permute-done.13.mate, ...), custom_call_target="tpu_custom_call" | custom-call | flops 671088640 | bytes 5373952 | tf_op jit(solution)/shard_map/pallas_call | solution.py:488
  68.3 2.2 %shard_map.58 = (bf16[1536,512]{1,0:T(8,128)(2,1)S(1)}, bf16[1280,128]{1,0:T(8,128)(2,1)S(1)}, bf16[640,128]{1,0:T(8,128)(2,1)S(1)}, bf16[640,128]{1,0:T(8,128)(2,1)S(1)}) custom-call(s32[13]{0:T(128)S(1)} %pad_add_fusion.drop_ref, bf16[512,512]{1,0:T(8,128)(2,1)S(1)} %get-tuple-element.51.own, bf16[1280,128]{1,0:T(8,128)(2,1)S(1)} %collective-permute-done.10.cross, ...), custom_call_target="tpu_custom_call" | custom-call | flops 1275068416 | bytes 11010048 | tf_op jit(solution)/shard_map/pallas_call | solution.py:488
  71.8 1.8 %collective-permute-start.14 = (bf16[640,128]{1,0:T(8,128)(2,1)S(1)}, bf16[640,128]{1,0:T(8,128)(2,1)S(1)}, u32[]{:S(2)}, u32[]{:S(2)}) collective-permute-start(bf16[640,128]{1,0:T(8,128)(2,1)S(1)} %get-tuple-element.63), channel_id=1, source_target_pairs={{0,1},{1,0},{2,3},{3,2},{4,5},{5,4},{6,7},{7,6},{8,9},{9,8},{10,11... | collective-permute-start | bytes 491528 | tf_op jit(solution)/shard_map/ppermute | solution.py:502
  73.6 1.3 %shard_map.59.own = bf16[512,512]{1,0:T(8,128)(2,1)S(1)} custom-call(s32[13]{0:T(128)S(1)} %pad_add_fusion.drop_ref, bf16[1536,1280]{1,0:T(8,128)(2,1)S(1)} %get-tuple-element.37.square, bf16[1536,512]{1,0:T(8,128)(2,1)S(1)} %get-tuple-element.62.whole.own), custom_call_target="tpu_custom_call" | custom-call | flops 603979776 | bytes 6029312 | tf_op jit(solution)/shard_map/pallas_call | solution.py:488
  75.0 1.7 %shard_map.60 = (bf16[4,8,128,128]{3,2,1,0:T(8,128)(2,1)S(1)}, bf16[4,8,128,128]{3,2,1,0:T(8,128)(2,1)}) custom-call(s32[13]{0:T(128)S(1)} %pad_add_fusion.drop_ref, bf16[512,512]{1,0:T(8,128)(2,1)S(1)} %shard_map.59.own, bf16[640,128]{1,0:T(8,128)(2,1)S(1)} %collective-permute-done.14.refs_0_, bf16[640,128]{1,0:T(8,128)(2,1)S(1)} %collective-permute-done.15.refs_1_), custom_call_target="tpu_custom_call" | custom-call | tf_op jit(solution)/shard_map/pallas_call | solution.py:488
  76.7 1.7 %shard_map.62 = (bf16[4,8,128,128]{3,2,1,0:T(8,128)(2,1)S(1)}, bf16[4,8,128,128]{3,2,1,0:T(8,128)(2,1)}) custom-call(s32[13]{0:T(128)S(1)} %pad_add_fusion.drop_ref, bf16[1536,512]{1,0:T(8,128)(2,1)S(1)} %get-tuple-element.62.whole.own, bf16[1280,128]{1,0:T(8,128)(2,1)S(1)} %collective-permute-done.17.refs_0_), custom_call_target="tpu_custom_call" | custom-call | tf_op jit(solution)/shard_map/pallas_call | solution.py:488
  78.7 1.3 %shard_map.63 = bf16[4,8,128,128]{3,2,1,0:T(8,128)(2,1)} custom-call(s32[13]{0:T(128)S(1)} %pad_add_fusion.drop_ref, bf16[4,8,128,128]{3,2,1,0:T(8,128)(2,1)S(1)} %get-tuple-element.69.slots, bf16[1280,128]{1,0:T(8,128)(2,1)S(1)} %collective-permute-done.18.cross, bf16[4,8,128,128]{3,2,1,0:T(8,128)(2,1)} %get-tuple-element.71.unused), custom_call_target="tpu_custom_call", output_to_operand_aliasing={{}: (3, {})} | custom-call | tf_op jit(solution)/shard_map/pallas_call | solution.py:488
  80.0 3.4 %collective-permute-done.16.cross = bf16[1280,128]{1,0:T(8,128)(2,1)S(1)} collective-permute-done((bf16[1280,128]{1,0:T(8,128)(2,1)S(1)}, bf16[1280,128]{1,0:T(8,128)(2,1)S(1)}, u32[]{:S(2)}, u32[]{:S(2)}) %collective-permute-start.16) | collective-permute-done | bytes 327712 | tf_op jit(solution)/shard_map/ppermute | solution.py:502
  83.4 1.3 %shard_map.61 = bf16[4,8,128,128]{3,2,1,0:T(8,128)(2,1)} custom-call(s32[13]{0:T(128)S(1)} %pad_add_fusion.drop_ref, bf16[4,8,128,128]{3,2,1,0:T(8,128)(2,1)S(1)} %get-tuple-element.65.slots, bf16[1280,128]{1,0:T(8,128)(2,1)S(1)} %collective-permute-done.16.cross, bf16[4,8,128,128]{3,2,1,0:T(8,128)(2,1)} %get-tuple-element.67.unused), custom_call_target="tpu_custom_call", output_to_operand_aliasing={{}: (3, {})} | custom-call | tf_op jit(solution)/shard_map/pallas_call | solution.py:488
  (42 shorter events, 9.2 us)
Async XLA Ops:
  0.6 26.8 %collective-permute-start.2 = (bf16[4,8,128,128]{3,2,1,0:T(8,128)(2,1)}, bf16[4,8,128,128]{3,2,1,0:T(8,128)(2,1)S(1)}, u32[]{:S(2)}, u32[]{:S(2)}) collective-permute-start(bf16[4,8,128,128]{3,2,1,0:T(8,128)(2,1)} %own.2), channel_id=1, source_target_pairs={{0,15},{1,2},{2,1},{3,4},{4,3},{5,6},{6,5},{7,8},{8,7},{9,10},{10,... | collective-permute-start | bytes 3145736 | tf_op jit(solution)/shard_map/ppermute | solution.py:502
  3.3 24.1 %collective-permute-start.3 = (bf16[4,8,128,128]{3,2,1,0:T(8,128)(2,1)}, bf16[4,8,128,128]{3,2,1,0:T(8,128)(2,1)S(1)}, u32[]{:S(2)}, u32[]{:S(2)}) collective-permute-start(bf16[4,8,128,128]{3,2,1,0:T(8,128)(2,1)} %own.2), channel_id=1, source_target_pairs={{0,1},{1,0},{2,3},{3,2},{4,5},{5,4},{6,7},{7,6},{8,9},{9,8},{10,11... | collective-permute-start | bytes 3145736 | tf_op jit(solution)/shard_map/ppermute | solution.py:502
  7.1 1.2 %copy-start = (bf16[4,8,128,128]{3,2,1,0:T(8,128)(2,1)S(1)}, bf16[4,8,128,128]{3,2,1,0:T(8,128)(2,1)}, u32[]{:S(2)}) copy-start(bf16[4,8,128,128]{3,2,1,0:T(8,128)(2,1)} %own.3) | copy-start | bytes 3145732
  10.4 0.8 copy-start.1
  11.2 16.2 %collective-permute-start.4 = (bf16[3328,128]{1,0:T(8,128)(2,1)}, bf16[3328,128]{1,0:T(8,128)(2,1)S(1)}, u32[]{:S(2)}, u32[]{:S(2)}) collective-permute-start(bf16[3328,128]{1,0:T(8,128)(2,1)} %get-tuple-element.39.sent_mate), channel_id=1, source_target_pairs={{0,1},{1,0},{2,3},{3,2},{4,5},{5,4},{6,7},{7,6},{8,9},{9,8},{10,11... | collective-permute-start | bytes 2555912 | tf_op jit(solution)/shard_map/ppermute | solution.py:502
  11.2 16.1 %collective-permute-start = (s32[4]{0:T(128)S(1)}, s32[4]{0:T(128)S(1)}, u32[]{:S(2)}, u32[]{:S(2)}) collective-permute-start(s32[4]{0:T(128)S(1)} %broadcast_subtract_fusion), channel_id=1, source_target_pairs={{0,15},{1,2},{2,1},{3,4},{4,3},{5,6},{6,5},{7,8},{8,7},{9,10},{10,... | collective-permute-start | bytes 56 | tf_op jit(solution)/shard_map/ppermute | solution.py:502
  11.2 16.1 %collective-permute-start.1 = (s32[4]{0:T(128)S(1)}, s32[4]{0:T(128)S(1)}, u32[]{:S(2)}, u32[]{:S(2)}) collective-permute-start(s32[4]{0:T(128)S(1)} %broadcast_subtract_fusion), channel_id=1, source_target_pairs={{0,1},{1,0},{2,3},{3,2},{4,5},{5,4},{6,7},{7,6},{8,9},{9,8},{10,11... | collective-permute-start | bytes 56 | tf_op jit(solution)/shard_map/ppermute | solution.py:502
  12.0 24.4 %copy-start.3 = (bf16[4,8,128,128]{3,2,1,0:T(8,128)(2,1)S(1)}, bf16[4,8,128,128]{3,2,1,0:T(8,128)(2,1)}, u32[]{:S(2)}) copy-start(bf16[4,8,128,128]{3,2,1,0:T(8,128)(2,1)} %own.2) | copy-start | bytes 3145732
  28.1 12.5 %collective-permute-start.5 = (bf16[1280,128]{1,0:T(8,128)(2,1)S(1)}, bf16[1280,128]{1,0:T(8,128)(2,1)S(1)}, u32[]{:S(2)}, u32[]{:S(2)}) collective-permute-start(bf16[1280,128]{1,0:T(8,128)(2,1)S(1)} %get-tuple-element.42), channel_id=1, source_target_pairs={{0,13},{1,4},{2,15},{3,6},{4,1},{5,8},{6,3},{7,10},{8,5},{9,12},{1... | collective-permute-start | bytes 983048 | tf_op jit(solution)/shard_map/ppermute | solution.py:502
  28.2 13.9 %collective-permute-start.8 = (bf16[1280,128]{1,0:T(8,128)(2,1)S(1)}, bf16[1280,128]{1,0:T(8,128)(2,1)S(1)}, u32[]{:S(2)}, u32[]{:S(2)}) collective-permute-start(bf16[1280,128]{1,0:T(8,128)(2,1)S(1)} %get-tuple-element.50.sent_cross), channel_id=1, source_target_pairs={{0,15},{1,2},{2,1},{3,4},{4,3},{5,6},{6,5},{7,8},{8,7},{9,10},{10,... | collective-permute-start | bytes 983048 | tf_op jit(solution)/shard_map/ppermute | solution.py:502
  30.0 19.0 %collective-permute-start.9 = (bf16[2048,128]{1,0:T(8,128)(2,1)}, bf16[2048,128]{1,0:T(8,128)(2,1)S(1)}, u32[]{:S(2)}, u32[]{:S(2)}) collective-permute-start(bf16[2048,128]{1,0:T(8,128)(2,1)} %get-tuple-element.52), channel_id=1, source_target_pairs={{0,15},{1,2},{2,1},{3,4},{4,3},{5,6},{6,5},{7,8},{8,7},{9,10},{10,... | collective-permute-start | bytes 1572872 | tf_op jit(solution)/shard_map/ppermute | solution.py:502
  30.1 10.5 %collective-permute-start.6 = (bf16[640,128]{1,0:T(8,128)(2,1)S(1)}, bf16[640,128]{1,0:T(8,128)(2,1)S(1)}, u32[]{:S(2)}, u32[]{:S(2)}) collective-permute-start(bf16[640,128]{1,0:T(8,128)(2,1)S(1)} %get-tuple-element.43), channel_id=1, source_target_pairs={{0,1},{1,0},{2,3},{3,2},{4,5},{5,4},{6,7},{7,6},{8,9},{9,8},{10,11... | collective-permute-start | bytes 491528 | tf_op jit(solution)/shard_map/ppermute | solution.py:502
  36.4 4.3 %collective-permute-start.7 = (bf16[640,128]{1,0:T(8,128)(2,1)S(1)}, bf16[640,128]{1,0:T(8,128)(2,1)S(1)}, u32[]{:S(2)}, u32[]{:S(2)}) collective-permute-start(bf16[640,128]{1,0:T(8,128)(2,1)S(1)} %get-tuple-element.44), channel_id=1, source_target_pairs={{0,1},{1,0},{2,3},{3,2},{4,5},{5,4},{6,7},{7,6},{8,9},{9,8},{10,11... | collective-permute-start | bytes 491528 | tf_op jit(solution)/shard_map/ppermute | solution.py:502
  40.7 1.5 %copy-start.2 = (bf16[2048,128]{1,0:T(8,128)(2,1)S(1)}, bf16[2048,128]{1,0:T(8,128)(2,1)}, u32[]{:S(2)}) copy-start(bf16[2048,128]{1,0:T(8,128)(2,1)} %copy-done.1) | copy-start | bytes 1572868
  45.9 18.8 %collective-permute-start.12 = (bf16[512,512]{1,0:T(8,128)(2,1)S(1)}, bf16[512,512]{1,0:T(8,128)(2,1)S(1)}, u32[]{:S(2)}, u32[]{:S(2)}) collective-permute-start(bf16[512,512]{1,0:T(8,128)(2,1)S(1)} %get-tuple-element.51.own), channel_id=1, source_target_pairs={{0,15},{1,2},{2,1},{3,4},{4,3},{5,6},{6,5},{7,8},{8,7},{9,10},{10,... | collective-permute-start | bytes 1572872 | tf_op jit(solution)/shard_map/ppermute | solution.py:502
  46.8 18.0 %collective-permute-start.13 = (bf16[512,512]{1,0:T(8,128)(2,1)S(1)}, bf16[512,512]{1,0:T(8,128)(2,1)S(1)}, u32[]{:S(2)}, u32[]{:S(2)}) collective-permute-start(bf16[512,512]{1,0:T(8,128)(2,1)S(1)} %get-tuple-element.51.own), channel_id=1, source_target_pairs={{0,1},{1,0},{2,3},{3,2},{4,5},{5,4},{6,7},{7,6},{8,9},{9,8},{10,11... | collective-permute-start | bytes 1572872 | tf_op jit(solution)/shard_map/ppermute | solution.py:502
  50.4 17.9 %collective-permute-start.10 = (bf16[1280,128]{1,0:T(8,128)(2,1)S(1)}, bf16[1280,128]{1,0:T(8,128)(2,1)S(1)}, u32[]{:S(2)}, u32[]{:S(2)}) collective-permute-start(bf16[1280,128]{1,0:T(8,128)(2,1)S(1)} %get-tuple-element.55), channel_id=1, source_target_pairs={{0,15},{1,2},{2,1},{3,4},{4,3},{5,6},{6,5},{7,8},{8,7},{9,10},{10,... | collective-permute-start | bytes 983048 | tf_op jit(solution)/shard_map/ppermute | solution.py:502
  52.7 15.6 %collective-permute-start.11 = (bf16[1280,128]{1,0:T(8,128)(2,1)S(1)}, bf16[1280,128]{1,0:T(8,128)(2,1)S(1)}, u32[]{:S(2)}, u32[]{:S(2)}) collective-permute-start(bf16[1280,128]{1,0:T(8,128)(2,1)S(1)} %get-tuple-element.56), channel_id=1, source_target_pairs={{0,1},{1,0},{2,3},{3,2},{4,5},{5,4},{6,7},{7,6},{8,9},{9,8},{10,11... | collective-permute-start | bytes 983048 | tf_op jit(solution)/shard_map/ppermute | solution.py:502
  66.3 10.5 %collective-permute-start.17 = (bf16[1280,128]{1,0:T(8,128)(2,1)S(1)}, bf16[1280,128]{1,0:T(8,128)(2,1)S(1)}, u32[]{:S(2)}, u32[]{:S(2)}) collective-permute-start(bf16[1280,128]{1,0:T(8,128)(2,1)S(1)} %get-tuple-element.68), channel_id=1, source_target_pairs={{0,1},{1,0},{2,3},{3,2},{4,5},{5,4},{6,7},{7,6},{8,9},{9,8},{10,11... | collective-permute-start | bytes 983048 | tf_op jit(solution)/shard_map/ppermute | solution.py:502
  66.3 12.4 %collective-permute-start.18 = (bf16[1280,128]{1,0:T(8,128)(2,1)S(1)}, bf16[1280,128]{1,0:T(8,128)(2,1)S(1)}, u32[]{:S(2)}, u32[]{:S(2)}) collective-permute-start(bf16[1280,128]{1,0:T(8,128)(2,1)S(1)} %get-tuple-element.70), channel_id=1, source_target_pairs={{0,15},{1,2},{2,1},{3,4},{4,3},{5,6},{6,5},{7,8},{8,7},{9,10},{10,... | collective-permute-start | bytes 983048 | tf_op jit(solution)/shard_map/ppermute | solution.py:502
  70.5 12.9 %collective-permute-start.16 = (bf16[1280,128]{1,0:T(8,128)(2,1)S(1)}, bf16[1280,128]{1,0:T(8,128)(2,1)S(1)}, u32[]{:S(2)}, u32[]{:S(2)}) collective-permute-start(bf16[1280,128]{1,0:T(8,128)(2,1)S(1)} %get-tuple-element.66), channel_id=1, source_target_pairs={{0,15},{1,2},{2,1},{3,4},{4,3},{5,6},{6,5},{7,8},{8,7},{9,10},{10,... | collective-permute-start | bytes 983048 | tf_op jit(solution)/shard_map/ppermute | solution.py:502
  71.8 3.1 %collective-permute-start.14 = (bf16[640,128]{1,0:T(8,128)(2,1)S(1)}, bf16[640,128]{1,0:T(8,128)(2,1)S(1)}, u32[]{:S(2)}, u32[]{:S(2)}) collective-permute-start(bf16[640,128]{1,0:T(8,128)(2,1)S(1)} %get-tuple-element.63), channel_id=1, source_target_pairs={{0,1},{1,0},{2,3},{3,2},{4,5},{5,4},{6,7},{7,6},{8,9},{9,8},{10,11... | collective-permute-start | bytes 491528 | tf_op jit(solution)/shard_map/ppermute | solution.py:502
  73.6 1.4 %collective-permute-start.15 = (bf16[640,128]{1,0:T(8,128)(2,1)S(1)}, bf16[640,128]{1,0:T(8,128)(2,1)S(1)}, u32[]{:S(2)}, u32[]{:S(2)}) collective-permute-start(bf16[640,128]{1,0:T(8,128)(2,1)S(1)} %get-tuple-element.64), channel_id=1, source_target_pairs={{0,1},{1,0},{2,3},{3,2},{4,5},{5,4},{6,7},{7,6},{8,9},{9,8},{10,11... | collective-permute-start | bytes 491528 | tf_op jit(solution)/shard_map/ppermute | solution.py:502

commit v23 on v21

--- a/solution.py
+++ b/solution.py
@@ -368,7 +368,7 @@
 
 
 def density_edges_kernel(
-    f, drop_ref, own, cross, mate, correction, new_low, new_high, square, corners, whole, to_cross, to_mate,
+    f, drop_ref, own, mate, cross, correction, new_low, new_high, square, corners, whole, to_cross, to_mate,
     to_mate_too, before, after, low, high,
 ):
     h, p = f.h, f.p
@@ -606,7 +606,7 @@
         density_edges_kernel,
         [columns, triangle, half_triangle, half_triangle],
         [group_scratch] * 4,
-        38, 20, drop, own, edge_cross, edge_mate, correction, new_low, new_high, square,
+        38, 20, drop, own, edge_mate, edge_cross, correction, new_low, new_high, square,
         square_corners,
     )
     rim_cross, rim_mates = to_cross(rim_cross), [to_mate(rim_mate), to_mate(rim_mate_too)]

time: 85 us -> 85 us (level)
  starting transfers between devices: 33.6 us -> 28.9 us
  waiting for transfers between devices: 20.5 us -> 25.1 us
    ppermute x19, starting transfers between devices: 33.6 us -> 28.9 us  [routed(): lax.ppermute(x, RING, [(i, (i + step(i)) % size) for i in range(size) if...]
    ppermute x19, waiting for transfers between devices: 20.5 us -> 25.1 us  [routed(): lax.ppermute(x, RING, [(i, (i + step(i)) % size) for i in range(size) if...]
where the time goes in v23:
time: 85 us; the launch traced here: 84.8 us
  starting transfers between devices  28.9 us (34%)
  Pallas kernels  26.8 us (32%)
  waiting for transfers between devices  25.1 us (30%)
  local copies, waits for them, and re-layouts  2.05 us (2%)
  other arithmetic  1.04 us (1%)
    ppermute x19, starting transfers between devices, routed(): lax.ppermute(x, RING, [(i, (i + step(i)) % size) for i in range(size) if...  28.9 us
    pallas_call x14, Pallas kernels, call(): pl.pallas_call(kernel, out_shape=[*outs, *[jax.ShapeDtypeStruct(a.shape,...  26.8 us
    ppermute x19, waiting for transfers between devices, routed(): lax.ppermute(x, RING, [(i, (i + step(i)) % size) for i in range(size) if...  25.1 us
    unnamed x8, local copies, waits for them, and re-layouts  2.05 us
  transfers between devices with their start and end apart: 19, of which 6 were waited for; matrix products, arithmetic and copies ran while one was open for 1% of the time, Pallas kernels for 29%

profile of v23, /device:TPU:1, one launch (start us, length us, event | category | flops | bytes accessed | tf_op | source)
XLA Modules:
  0.0 84.8 jit_solution(9603513848897034973)
XLA Ops:
  0.6 2.7 %collective-permute-start.2 = (bf16[4,8,128,128]{3,2,1,0:T(8,128)(2,1)}, bf16[4,8,128,128]{3,2,1,0:T(8,128)(2,1)S(1)}, u32[]{:S(2)}, u32[]{:S(2)}) collective-permute-start(bf16[4,8,128,128]{3,2,1,0:T(8,128)(2,1)} %own.2), channel_id=1, source_target_pairs={{0,15},{1,2},{2,1},{3,4},{4,3},{5,6},{6,5},{7,8},{8,7},{9,10},{10,... | collective-permute-start | bytes 3145736 | tf_op jit(solution)/shard_map/ppermute | solution.py:501
  3.3 2.9 %collective-permute-start.3 = (bf16[4,8,128,128]{3,2,1,0:T(8,128)(2,1)}, bf16[4,8,128,128]{3,2,1,0:T(8,128)(2,1)S(1)}, u32[]{:S(2)}, u32[]{:S(2)}) collective-permute-start(bf16[4,8,128,128]{3,2,1,0:T(8,128)(2,1)} %own.2), channel_id=1, source_target_pairs={{0,1},{1,0},{2,3},{3,2},{4,5},{5,4},{6,7},{7,6},{8,9},{9,8},{10,11... | collective-permute-start | bytes 3145736 | tf_op jit(solution)/shard_map/ppermute | solution.py:501
  8.4 2.1 %shard_map.51 = (bf16[2048,128]{1,0:T(8,128)(2,1)S(1)}, bf16[2048,128]{1,0:T(8,128)(2,1)}, bf16[3328,128]{1,0:T(8,128)(2,1)}, bf16[1280,128]{1,0:T(8,128)(2,1)S(1)}) custom-call(s32[5]{0:T(128)S(1)} %pad_add_fusion.1.drop_ref, bf16[4,8,128,128]{3,2,1,0:T(8,128)(2,1)S(1)} %copy-done), custom_call_target="tpu_custom_call" | custom-call | bytes 3276800 | tf_op jit(solution)/shard_map/pallas_call | solution.py:487
  12.0 15.3 %collective-permute-done = s32[4]{0:T(128)S(1)} collective-permute-done((s32[4]{0:T(128)S(1)}, s32[4]{0:T(128)S(1)}, u32[]{:S(2)}, u32[]{:S(2)}) %collective-permute-start) | collective-permute-done | bytes 48 | tf_op jit(solution)/shard_map/ppermute | solution.py:501
  28.2 1.8 %collective-permute-start.8 = (bf16[1280,128]{1,0:T(8,128)(2,1)S(1)}, bf16[1280,128]{1,0:T(8,128)(2,1)S(1)}, u32[]{:S(2)}, u32[]{:S(2)}) collective-permute-start(bf16[1280,128]{1,0:T(8,128)(2,1)S(1)} %get-tuple-element.50.sent_cross), channel_id=1, source_target_pairs={{0,15},{1,2},{2,1},{3,4},{4,3},{5,6},{6,5},{7,8},{8,7},{9,10},{10,... | collective-permute-start | bytes 983048 | tf_op jit(solution)/shard_map/ppermute | solution.py:501
  30.1 6.3 %collective-permute-start.6 = (bf16[640,128]{1,0:T(8,128)(2,1)S(1)}, bf16[640,128]{1,0:T(8,128)(2,1)S(1)}, u32[]{:S(2)}, u32[]{:S(2)}) collective-permute-start(bf16[640,128]{1,0:T(8,128)(2,1)S(1)} %get-tuple-element.43), channel_id=1, source_target_pairs={{0,1},{1,0},{2,3},{3,2},{4,5},{5,4},{6,7},{7,6},{8,9},{9,8},{10,11... | collective-permute-start | bytes 491528 | tf_op jit(solution)/shard_map/ppermute | solution.py:501
  36.4 4.3 %shard_map.50 = (bf16[1536,1280]{1,0:T(8,128)(2,1)S(1)}, bf16[1536,1280]{1,0:T(8,128)(2,1)S(1)}, bf16[1024,512]{1,0:T(8,128)(2,1)S(1)}, bf16[1024,512]{1,0:T(8,128)(2,1)S(1)}, f32[1024,512]{1,0:T(8,128)S(1)}) custom-call(s32[13]{0:T(128)S(1)} %pad_add_fusion.drop_ref, bf16[4,8,128,128]{3,2,1,0:T(8,128)(2,1)S(1)} %copy-done.3, ...), custom_call_target="tpu_custom_call" | custom-call | flops 2818572288 | bytes 15204352 | tf_op jit(solution)/shard_map/pallas_call | solution.py:487
  40.7 1.4 %shard_map.53 = (bf16[1024,512]{1,0:T(8,128)(2,1)S(1)}, bf16[1024,512]{1,0:T(8,128)(2,1)S(1)}) custom-call(s32[13]{0:T(128)S(1)} %pad_add_fusion.drop_ref, bf16[1280,128]{1,0:T(8,128)(2,1)S(1)} %collective-permute-done.5.far_far, bf16[640,128]{1,0:T(8,128)(2,1)S(1)} %collective-permute-done.6.far_mate, ...), custom_call_target="tpu_custom_call" | custom-call | tf_op jit(solution)/shard_map/pallas_call | solution.py:487
  42.2 3.5 %shard_map.54 = (bf16[1536,512]{1,0:T(8,128)(2,1)S(1)}, bf16[512,512]{1,0:T(8,128)(2,1)S(1)}, bf16[1536,512]{1,0:T(8,128)(2,1)S(1)}) custom-call(s32[13]{0:T(128)S(1)} %pad_add_fusion.drop_ref, bf16[1536,1280]{1,0:T(8,128)(2,1)S(1)} %get-tuple-element.38.shifted, bf16[1024,512]{1,0:T(8,128)(2,1)S(1)} %get-tuple-element.48.corners, ...), custom_call_target="tpu_custom_call" | custom-call | tf_op jit(solution)/shard_map/pallas_call | solution.py:487
  46.5 2.2 %collective-permute-start.13 = (bf16[512,512]{1,0:T(8,128)(2,1)S(1)}, bf16[512,512]{1,0:T(8,128)(2,1)S(1)}, u32[]{:S(2)}, u32[]{:S(2)}) collective-permute-start(bf16[512,512]{1,0:T(8,128)(2,1)S(1)} %get-tuple-element.51.own), channel_id=1, source_target_pairs={{0,1},{1,0},{2,3},{3,2},{4,5},{5,4},{6,7},{7,6},{8,9},{9,8},{10,11... | collective-permute-start | bytes 1572872 | tf_op jit(solution)/shard_map/ppermute | solution.py:501
  48.9 1.6 %shard_map.55 = (bf16[512,512]{1,0:T(8,128)(2,1)S(1)}, bf16[512,512]{1,0:T(8,128)(2,1)S(1)}, bf16[1280,128]{1,0:T(8,128)(2,1)S(1)}, bf16[1280,128]{1,0:T(8,128)(2,1)S(1)}) custom-call(s32[13]{0:T(128)S(1)} %pad_add_fusion.drop_ref, bf16[3328,128]{1,0:T(8,128)(2,1)S(1)} %collective-permute-done.4.refs_1_.mate, ...), custom_call_target="tpu_custom_call" | custom-call | flops 671088640 | bytes 6225920 | tf_op jit(solution)/shard_map/pallas_call | solution.py:487
  50.6 1.9 %collective-permute-start.10 = (bf16[1280,128]{1,0:T(8,128)(2,1)S(1)}, bf16[1280,128]{1,0:T(8,128)(2,1)S(1)}, u32[]{:S(2)}, u32[]{:S(2)}) collective-permute-start(bf16[1280,128]{1,0:T(8,128)(2,1)S(1)} %get-tuple-element.55), channel_id=1, source_target_pairs={{0,1},{1,0},{2,3},{3,2},{4,5},{5,4},{6,7},{7,6},{8,9},{9,8},{10,11... | collective-permute-start | bytes 983048 | tf_op jit(solution)/shard_map/ppermute | solution.py:501
  52.5 6.1 %collective-permute-start.11 = (bf16[1280,128]{1,0:T(8,128)(2,1)S(1)}, bf16[1280,128]{1,0:T(8,128)(2,1)S(1)}, u32[]{:S(2)}, u32[]{:S(2)}) collective-permute-start(bf16[1280,128]{1,0:T(8,128)(2,1)S(1)} %get-tuple-element.56), channel_id=1, source_target_pairs={{0,15},{1,2},{2,1},{3,4},{4,3},{5,6},{6,5},{7,8},{8,7},{9,10},{10,... | collective-permute-start | bytes 983048 | tf_op jit(solution)/shard_map/ppermute | solution.py:501
  58.7 2.0 %shard_map.56.correction = bf16[1536,512]{1,0:T(8,128)(2,1)S(1)} custom-call(s32[13]{0:T(128)S(1)} %pad_add_fusion.drop_ref, bf16[1536,1280]{1,0:T(8,128)(2,1)S(1)} %get-tuple-element.38.shifted, bf16[1024,512]{1,0:T(8,128)(2,1)S(1)} %get-tuple-element.48.corners, bf16[512,512]{1,0:T(8,128)(2,1)S(1)} %get-tuple-element.57.low, ...), custom_call_target="tpu_custom_call" | custom-call | flops 1275068416 | bytes 8126464 | tf_op jit(solution)/shard_map/pallas_call | solution.py:487
  60.7 4.1 %collective-permute-done.12.cross = bf16[512,512]{1,0:T(8,128)(2,1)S(1)} collective-permute-done((bf16[512,512]{1,0:T(8,128)(2,1)S(1)}, bf16[512,512]{1,0:T(8,128)(2,1)S(1)}, u32[]{:S(2)}, u32[]{:S(2)}) %collective-permute-start.12) | collective-permute-done | bytes 524320 | tf_op jit(solution)/shard_map/ppermute | solution.py:501
  64.8 1.5 %shard_map.57 = (bf16[512,512]{1,0:T(8,128)(2,1)S(1)}, bf16[512,512]{1,0:T(8,128)(2,1)S(1)}, bf16[1280,128]{1,0:T(8,128)(2,1)S(1)}, bf16[1280,128]{1,0:T(8,128)(2,1)S(1)}) custom-call(s32[13]{0:T(128)S(1)} %pad_add_fusion.drop_ref, bf16[512,512]{1,0:T(8,128)(2,1)S(1)} %collective-permute-done.12.cross, bf16[512,512]{1,0:T(8,128)(2,1)S(1)} %collective-permute-done.13.mate, ...), custom_call_target="tpu_custom_call" | custom-call | flops 671088640 | bytes 5373952 | tf_op jit(solution)/shard_map/pallas_call | solution.py:487
  66.4 1.8 %collective-permute-done.11.cross = bf16[1280,128]{1,0:T(8,128)(2,1)S(1)} collective-permute-done((bf16[1280,128]{1,0:T(8,128)(2,1)S(1)}, bf16[1280,128]{1,0:T(8,128)(2,1)S(1)}, u32[]{:S(2)}, u32[]{:S(2)}) %collective-permute-start.11) | collective-permute-done | bytes 327712 | tf_op jit(solution)/shard_map/ppermute | solution.py:501
  68.3 2.3 %shard_map.58 = (bf16[1536,512]{1,0:T(8,128)(2,1)S(1)}, bf16[1280,128]{1,0:T(8,128)(2,1)S(1)}, bf16[640,128]{1,0:T(8,128)(2,1)S(1)}, bf16[640,128]{1,0:T(8,128)(2,1)S(1)}) custom-call(s32[13]{0:T(128)S(1)} %pad_add_fusion.drop_ref, bf16[512,512]{1,0:T(8,128)(2,1)S(1)} %get-tuple-element.51.own, bf16[1280,128]{1,0:T(8,128)(2,1)S(1)} %collective-permute-done.10.mate, ...), custom_call_target="tpu_custom_call" | custom-call | flops 1275068416 | bytes 11010048 | tf_op jit(solution)/shard_map/pallas_call | solution.py:487
  71.8 1.8 %collective-permute-start.14 = (bf16[640,128]{1,0:T(8,128)(2,1)S(1)}, bf16[640,128]{1,0:T(8,128)(2,1)S(1)}, u32[]{:S(2)}, u32[]{:S(2)}) collective-permute-start(bf16[640,128]{1,0:T(8,128)(2,1)S(1)} %get-tuple-element.63), channel_id=1, source_target_pairs={{0,1},{1,0},{2,3},{3,2},{4,5},{5,4},{6,7},{7,6},{8,9},{9,8},{10,11... | collective-permute-start | bytes 491528 | tf_op jit(solution)/shard_map/ppermute | solution.py:501
  73.6 1.3 %shard_map.59.own = bf16[512,512]{1,0:T(8,128)(2,1)S(1)} custom-call(s32[13]{0:T(128)S(1)} %pad_add_fusion.drop_ref, bf16[1536,1280]{1,0:T(8,128)(2,1)S(1)} %get-tuple-element.37.square, bf16[1536,512]{1,0:T(8,128)(2,1)S(1)} %get-tuple-element.62.whole.own), custom_call_target="tpu_custom_call" | custom-call | flops 603979776 | bytes 6029312 | tf_op jit(solution)/shard_map/pallas_call | solution.py:487
  75.0 1.7 %shard_map.60 = (bf16[4,8,128,128]{3,2,1,0:T(8,128)(2,1)S(1)}, bf16[4,8,128,128]{3,2,1,0:T(8,128)(2,1)}) custom-call(s32[13]{0:T(128)S(1)} %pad_add_fusion.drop_ref, bf16[512,512]{1,0:T(8,128)(2,1)S(1)} %shard_map.59.own, bf16[640,128]{1,0:T(8,128)(2,1)S(1)} %collective-permute-done.14.refs_0_, bf16[640,128]{1,0:T(8,128)(2,1)S(1)} %collective-permute-done.15.refs_1_), custom_call_target="tpu_custom_call" | custom-call | tf_op jit(solution)/shard_map/pallas_call | solution.py:487
  76.8 1.7 %shard_map.62 = (bf16[4,8,128,128]{3,2,1,0:T(8,128)(2,1)S(1)}, bf16[4,8,128,128]{3,2,1,0:T(8,128)(2,1)}) custom-call(s32[13]{0:T(128)S(1)} %pad_add_fusion.drop_ref, bf16[1536,512]{1,0:T(8,128)(2,1)S(1)} %get-tuple-element.62.whole.own, bf16[1280,128]{1,0:T(8,128)(2,1)S(1)} %collective-permute-done.17.refs_0_), custom_call_target="tpu_custom_call" | custom-call | tf_op jit(solution)/shard_map/pallas_call | solution.py:487
  78.5 1.5 %collective-permute-done.18.cross = bf16[1280,128]{1,0:T(8,128)(2,1)S(1)} collective-permute-done((bf16[1280,128]{1,0:T(8,128)(2,1)S(1)}, bf16[1280,128]{1,0:T(8,128)(2,1)S(1)}, u32[]{:S(2)}, u32[]{:S(2)}) %collective-permute-start.18) | collective-permute-done | bytes 327712 | tf_op jit(solution)/shard_map/ppermute | solution.py:501
  81.3 2.2 %collective-permute-done.16.cross = bf16[1280,128]{1,0:T(8,128)(2,1)S(1)} collective-permute-done((bf16[1280,128]{1,0:T(8,128)(2,1)S(1)}, bf16[1280,128]{1,0:T(8,128)(2,1)S(1)}, u32[]{:S(2)}, u32[]{:S(2)}) %collective-permute-start.16) | collective-permute-done | bytes 327712 | tf_op jit(solution)/shard_map/ppermute | solution.py:501
  (42 shorter events, 9.9 us)
Async XLA Ops:
  0.6 26.8 %collective-permute-start.2 = (bf16[4,8,128,128]{3,2,1,0:T(8,128)(2,1)}, bf16[4,8,128,128]{3,2,1,0:T(8,128)(2,1)S(1)}, u32[]{:S(2)}, u32[]{:S(2)}) collective-permute-start(bf16[4,8,128,128]{3,2,1,0:T(8,128)(2,1)} %own.2), channel_id=1, source_target_pairs={{0,15},{1,2},{2,1},{3,4},{4,3},{5,6},{6,5},{7,8},{8,7},{9,10},{10,... | collective-permute-start | bytes 3145736 | tf_op jit(solution)/shard_map/ppermute | solution.py:501
  3.3 24.1 %collective-permute-start.3 = (bf16[4,8,128,128]{3,2,1,0:T(8,128)(2,1)}, bf16[4,8,128,128]{3,2,1,0:T(8,128)(2,1)S(1)}, u32[]{:S(2)}, u32[]{:S(2)}) collective-permute-start(bf16[4,8,128,128]{3,2,1,0:T(8,128)(2,1)} %own.2), channel_id=1, source_target_pairs={{0,1},{1,0},{2,3},{3,2},{4,5},{5,4},{6,7},{7,6},{8,9},{9,8},{10,11... | collective-permute-start | bytes 3145736 | tf_op jit(solution)/shard_map/ppermute | solution.py:501
  7.1 1.2 %copy-start = (bf16[4,8,128,128]{3,2,1,0:T(8,128)(2,1)S(1)}, bf16[4,8,128,128]{3,2,1,0:T(8,128)(2,1)}, u32[]{:S(2)}) copy-start(bf16[4,8,128,128]{3,2,1,0:T(8,128)(2,1)} %own.3) | copy-start | bytes 3145732
  10.4 0.8 copy-start.1
  11.2 16.2 %collective-permute-start.4 = (bf16[3328,128]{1,0:T(8,128)(2,1)}, bf16[3328,128]{1,0:T(8,128)(2,1)S(1)}, u32[]{:S(2)}, u32[]{:S(2)}) collective-permute-start(bf16[3328,128]{1,0:T(8,128)(2,1)} %get-tuple-element.39.sent_mate), channel_id=1, source_target_pairs={{0,1},{1,0},{2,3},{3,2},{4,5},{5,4},{6,7},{7,6},{8,9},{9,8},{10,11... | collective-permute-start | bytes 2555912 | tf_op jit(solution)/shard_map/ppermute | solution.py:501
  11.2 16.1 %collective-permute-start = (s32[4]{0:T(128)S(1)}, s32[4]{0:T(128)S(1)}, u32[]{:S(2)}, u32[]{:S(2)}) collective-permute-start(s32[4]{0:T(128)S(1)} %broadcast_subtract_fusion), channel_id=1, source_target_pairs={{0,15},{1,2},{2,1},{3,4},{4,3},{5,6},{6,5},{7,8},{8,7},{9,10},{10,... | collective-permute-start | bytes 56 | tf_op jit(solution)/shard_map/ppermute | solution.py:501
  11.2 16.1 %collective-permute-start.1 = (s32[4]{0:T(128)S(1)}, s32[4]{0:T(128)S(1)}, u32[]{:S(2)}, u32[]{:S(2)}) collective-permute-start(s32[4]{0:T(128)S(1)} %broadcast_subtract_fusion), channel_id=1, source_target_pairs={{0,1},{1,0},{2,3},{3,2},{4,5},{5,4},{6,7},{7,6},{8,9},{9,8},{10,11... | collective-permute-start | bytes 56 | tf_op jit(solution)/shard_map/ppermute | solution.py:501
  27.4 9.0 %copy-start.3 = (bf16[4,8,128,128]{3,2,1,0:T(8,128)(2,1)S(1)}, bf16[4,8,128,128]{3,2,1,0:T(8,128)(2,1)}, u32[]{:S(2)}) copy-start(bf16[4,8,128,128]{3,2,1,0:T(8,128)(2,1)} %own.2) | copy-start | bytes 3145732
  28.1 12.5 %collective-permute-start.5 = (bf16[1280,128]{1,0:T(8,128)(2,1)S(1)}, bf16[1280,128]{1,0:T(8,128)(2,1)S(1)}, u32[]{:S(2)}, u32[]{:S(2)}) collective-permute-start(bf16[1280,128]{1,0:T(8,128)(2,1)S(1)} %get-tuple-element.42), channel_id=1, source_target_pairs={{0,13},{1,4},{2,15},{3,6},{4,1},{5,8},{6,3},{7,10},{8,5},{9,12},{1... | collective-permute-start | bytes 983048 | tf_op jit(solution)/shard_map/ppermute | solution.py:501
  28.2 13.9 %collective-permute-start.8 = (bf16[1280,128]{1,0:T(8,128)(2,1)S(1)}, bf16[1280,128]{1,0:T(8,128)(2,1)S(1)}, u32[]{:S(2)}, u32[]{:S(2)}) collective-permute-start(bf16[1280,128]{1,0:T(8,128)(2,1)S(1)} %get-tuple-element.50.sent_cross), channel_id=1, source_target_pairs={{0,15},{1,2},{2,1},{3,4},{4,3},{5,6},{6,5},{7,8},{8,7},{9,10},{10,... | collective-permute-start | bytes 983048 | tf_op jit(solution)/shard_map/ppermute | solution.py:501
  30.0 18.9 %collective-permute-start.9 = (bf16[2048,128]{1,0:T(8,128)(2,1)}, bf16[2048,128]{1,0:T(8,128)(2,1)S(1)}, u32[]{:S(2)}, u32[]{:S(2)}) collective-permute-start(bf16[2048,128]{1,0:T(8,128)(2,1)} %get-tuple-element.52), channel_id=1, source_target_pairs={{0,15},{1,2},{2,1},{3,4},{4,3},{5,6},{6,5},{7,8},{8,7},{9,10},{10,... | collective-permute-start | bytes 1572872 | tf_op jit(solution)/shard_map/ppermute | solution.py:501
  30.1 10.5 %collective-permute-start.6 = (bf16[640,128]{1,0:T(8,128)(2,1)S(1)}, bf16[640,128]{1,0:T(8,128)(2,1)S(1)}, u32[]{:S(2)}, u32[]{:S(2)}) collective-permute-start(bf16[640,128]{1,0:T(8,128)(2,1)S(1)} %get-tuple-element.43), channel_id=1, source_target_pairs={{0,1},{1,0},{2,3},{3,2},{4,5},{5,4},{6,7},{7,6},{8,9},{9,8},{10,11... | collective-permute-start | bytes 491528 | tf_op jit(solution)/shard_map/ppermute | solution.py:501
  36.4 4.3 %collective-permute-start.7 = (bf16[640,128]{1,0:T(8,128)(2,1)S(1)}, bf16[640,128]{1,0:T(8,128)(2,1)S(1)}, u32[]{:S(2)}, u32[]{:S(2)}) collective-permute-start(bf16[640,128]{1,0:T(8,128)(2,1)S(1)} %get-tuple-element.44), channel_id=1, source_target_pairs={{0,1},{1,0},{2,3},{3,2},{4,5},{5,4},{6,7},{7,6},{8,9},{9,8},{10,11... | collective-permute-start | bytes 491528 | tf_op jit(solution)/shard_map/ppermute | solution.py:501
  40.7 1.5 %copy-start.2 = (bf16[2048,128]{1,0:T(8,128)(2,1)S(1)}, bf16[2048,128]{1,0:T(8,128)(2,1)}, u32[]{:S(2)}) copy-start(bf16[2048,128]{1,0:T(8,128)(2,1)} %copy-done.1) | copy-start | bytes 1572868
  45.7 19.1 %collective-permute-start.12 = (bf16[512,512]{1,0:T(8,128)(2,1)S(1)}, bf16[512,512]{1,0:T(8,128)(2,1)S(1)}, u32[]{:S(2)}, u32[]{:S(2)}) collective-permute-start(bf16[512,512]{1,0:T(8,128)(2,1)S(1)} %get-tuple-element.51.own), channel_id=1, source_target_pairs={{0,15},{1,2},{2,1},{3,4},{4,3},{5,6},{6,5},{7,8},{8,7},{9,10},{10,... | collective-permute-start | bytes 1572872 | tf_op jit(solution)/shard_map/ppermute | solution.py:501
  46.5 18.2 %collective-permute-start.13 = (bf16[512,512]{1,0:T(8,128)(2,1)S(1)}, bf16[512,512]{1,0:T(8,128)(2,1)S(1)}, u32[]{:S(2)}, u32[]{:S(2)}) collective-permute-start(bf16[512,512]{1,0:T(8,128)(2,1)S(1)} %get-tuple-element.51.own), channel_id=1, source_target_pairs={{0,1},{1,0},{2,3},{3,2},{4,5},{5,4},{6,7},{7,6},{8,9},{9,8},{10,11... | collective-permute-start | bytes 1572872 | tf_op jit(solution)/shard_map/ppermute | solution.py:501
  50.6 15.8 %collective-permute-start.10 = (bf16[1280,128]{1,0:T(8,128)(2,1)S(1)}, bf16[1280,128]{1,0:T(8,128)(2,1)S(1)}, u32[]{:S(2)}, u32[]{:S(2)}) collective-permute-start(bf16[1280,128]{1,0:T(8,128)(2,1)S(1)} %get-tuple-element.55), channel_id=1, source_target_pairs={{0,1},{1,0},{2,3},{3,2},{4,5},{5,4},{6,7},{7,6},{8,9},{9,8},{10,11... | collective-permute-start | bytes 983048 | tf_op jit(solution)/shard_map/ppermute | solution.py:501
  52.5 15.8 %collective-permute-start.11 = (bf16[1280,128]{1,0:T(8,128)(2,1)S(1)}, bf16[1280,128]{1,0:T(8,128)(2,1)S(1)}, u32[]{:S(2)}, u32[]{:S(2)}) collective-permute-start(bf16[1280,128]{1,0:T(8,128)(2,1)S(1)} %get-tuple-element.56), channel_id=1, source_target_pairs={{0,15},{1,2},{2,1},{3,4},{4,3},{5,6},{6,5},{7,8},{8,7},{9,10},{10,... | collective-permute-start | bytes 983048 | tf_op jit(solution)/shard_map/ppermute | solution.py:501
  66.3 10.5 %collective-permute-start.17 = (bf16[1280,128]{1,0:T(8,128)(2,1)S(1)}, bf16[1280,128]{1,0:T(8,128)(2,1)S(1)}, u32[]{:S(2)}, u32[]{:S(2)}) collective-permute-start(bf16[1280,128]{1,0:T(8,128)(2,1)S(1)} %get-tuple-element.68), channel_id=1, source_target_pairs={{0,1},{1,0},{2,3},{3,2},{4,5},{5,4},{6,7},{7,6},{8,9},{9,8},{10,11... | collective-permute-start | bytes 983048 | tf_op jit(solution)/shard_map/ppermute | solution.py:501
  66.3 13.6 %collective-permute-start.18 = (bf16[1280,128]{1,0:T(8,128)(2,1)S(1)}, bf16[1280,128]{1,0:T(8,128)(2,1)S(1)}, u32[]{:S(2)}, u32[]{:S(2)}) collective-permute-start(bf16[1280,128]{1,0:T(8,128)(2,1)S(1)} %get-tuple-element.70), channel_id=1, source_target_pairs={{0,15},{1,2},{2,1},{3,4},{4,3},{5,6},{6,5},{7,8},{8,7},{9,10},{10,... | collective-permute-start | bytes 983048 | tf_op jit(solution)/shard_map/ppermute | solution.py:501
  70.5 12.9 %collective-permute-start.16 = (bf16[1280,128]{1,0:T(8,128)(2,1)S(1)}, bf16[1280,128]{1,0:T(8,128)(2,1)S(1)}, u32[]{:S(2)}, u32[]{:S(2)}) collective-permute-start(bf16[1280,128]{1,0:T(8,128)(2,1)S(1)} %get-tuple-element.66), channel_id=1, source_target_pairs={{0,15},{1,2},{2,1},{3,4},{4,3},{5,6},{6,5},{7,8},{8,7},{9,10},{10,... | collective-permute-start | bytes 983048 | tf_op jit(solution)/shard_map/ppermute | solution.py:501
  71.8 3.1 %collective-permute-start.14 = (bf16[640,128]{1,0:T(8,128)(2,1)S(1)}, bf16[640,128]{1,0:T(8,128)(2,1)S(1)}, u32[]{:S(2)}, u32[]{:S(2)}) collective-permute-start(bf16[640,128]{1,0:T(8,128)(2,1)S(1)} %get-tuple-element.63), channel_id=1, source_target_pairs={{0,1},{1,0},{2,3},{3,2},{4,5},{5,4},{6,7},{7,6},{8,9},{9,8},{10,11... | collective-permute-start | bytes 491528 | tf_op jit(solution)/shard_map/ppermute | solution.py:501
  73.6 1.4 %collective-permute-start.15 = (bf16[640,128]{1,0:T(8,128)(2,1)S(1)}, bf16[640,128]{1,0:T(8,128)(2,1)S(1)}, u32[]{:S(2)}, u32[]{:S(2)}) collective-permute-start(bf16[640,128]{1,0:T(8,128)(2,1)S(1)} %get-tuple-element.64), channel_id=1, source_target_pairs={{0,1},{1,0},{2,3},{3,2},{4,5},{5,4},{6,7},{7,6},{8,9},{9,8},{10,11... | collective-permute-start | bytes 491528 | tf_op jit(solution)/shard_map/ppermute | solution.py:501
